TPU v7x, 32 devices: a whole 2x2x4 slice. The times are simulated.
32 devices in a mesh: seq: 8 (over y, x, core), head: 4 (over z).
Axes of the slice: x: 2, y: 2, z: 4, core: 2. Of those that a mesh axis runs over, the one named last changes fastest.
Arguments:
- enc_in: bfloat16 [2048, 4, 768], P(('seq', 'head')), may hold values from -6 to 6
- conv_weight: bfloat16 [5, 768, 1536], replicated, may hold values from -0.09375 to 0.09375
- norm_gain: float32 [1536], replicated, may hold values from 0.25 to 1.75
- w_qkv: bfloat16 [3, 1536, 1536], P(None, None, 'head'), may hold values from -0.63788795 to 0.63788795
- w_out: bfloat16 [1536, 1536], P('head'), may hold values from -0.15625 to 0.15625
- grad_out: bfloat16 [1024, 4, 1536], P(('seq', 'head')), may hold values from -6 to 6
Outputs:
- mixed: bfloat16 [1024, 4, 1536], P(('seq', 'head'))
- grad_input: bfloat16 [2048, 4, 768], P(('seq', 'head'))
- grad_w_qkv: float32 [3, 1536, 1536], P(None, None, 'head')
- grad_w_out: float32 [1536, 1536], P('head')
All inputs are finite; a program needn't handle non-finite values.
Results may differ from a plain program's by a relative error of at most 0.024.
Values may be sent and summed in bfloat16 or wider, within the bound.
No kernel may reach another device: no remote copies, remote signals or barrier semaphores. Data moves between devices by JAX's collectives and lax.ppermute only.
A program may use at most 256 MiB of HBM per device.

v0:
```python
import jax
import jax.numpy as jnp
from jax import lax
from jax.sharding import PartitionSpec as P

DH = 192
KW = 5


def padded_2(block, sides, width):
    for axis, dim in sides:
        count = lax.axis_size(axis)
        forward = [(i, i + 1) for i in range(count - 1)]
        backward = [(target, source) for source, target in forward]
        low = lax.ppermute(
            lax.slice_in_dim(block, block.shape[dim] - width, None, axis=dim), axis, forward
        )
        high = lax.ppermute(lax.slice_in_dim(block, 0, width, axis=dim), axis, backward)
        block = jnp.concatenate([low, block, high], axis=dim)
    return block


def body(enc_in, conv_weight, norm_gain, w_qkv, w_out, grad_out):
    fine_rows = enc_in.shape[0]
    slab_rows = fine_rows // 2
    seq_count = enc_in.shape[1]
    out_width = conv_weight.shape[2]
    local_width = w_qkv.shape[2]
    local_heads = local_width // DH
    logit_scale = DH ** (-0.5)
    padded = padded_2(enc_in, ((("seq", "head"), 0),), 2)
    convolved = jnp.zeros((fine_rows, seq_count, out_width), jnp.float32)
    for offset in range(KW):
        convolved = convolved + jnp.einsum(
            "tbi,io->tbo",
            padded[offset : offset + fine_rows],
            conv_weight[offset],
            preferred_element_type=jnp.float32,
        )
    activated, gelu_pull = jax.vjp(jax.nn.gelu, convolved)
    skip = jnp.mean(activated.reshape(slab_rows, 2, seq_count, out_width), axis=1).astype(
        jnp.bfloat16
    )
    skip_wide = skip.astype(jnp.float32)
    inv_rms = lax.rsqrt(jnp.mean(skip_wide * skip_wide, axis=-1, keepdims=True) + 1e-06)
    normed = (skip_wide * inv_rms * norm_gain).astype(jnp.bfloat16)
    normed_rows = lax.all_gather(normed, "head", axis=0, tiled=True)
    grad_rows = lax.all_gather(grad_out, "head", axis=0, tiled=True)
    tower_rows = normed_rows.shape[0]
    qkv = jnp.einsum(
        "tbc,ice->itbe", normed_rows, w_qkv, preferred_element_type=jnp.float32
    ).astype(jnp.bfloat16)
    qkv = qkv.reshape(3, tower_rows, seq_count, local_heads, DH)
    query_matrix, key_matrix, value_matrix = (qkv[0], qkv[1], qkv[2])
    key_all, value_all = (
        lax.all_gather(key_matrix, "seq", axis=0, tiled=True),
        lax.all_gather(value_matrix, "seq", axis=0, tiled=True),
    )
    attention_logits = (
        jnp.einsum("qbhd,kbhd->bhqk", query_matrix, key_all, preferred_element_type=jnp.float32)
        * logit_scale
    )
    row_peak = jnp.max(attention_logits, axis=-1, keepdims=True)
    exponent = jnp.exp(attention_logits - row_peak)
    row_total = jnp.sum(exponent, axis=-1, keepdims=True)
    soft_weights = exponent / row_total
    narrow_probabilities = soft_weights.astype(jnp.bfloat16)
    attention_output = jnp.einsum(
        "bhqk,kbhd->qbhd", narrow_probabilities, value_all, preferred_element_type=jnp.float32
    )
    o_narrow = attention_output.reshape(tower_rows, seq_count, local_width).astype(jnp.bfloat16)
    piece = o_narrow
    head_sum = lax.psum_scatter(
        jnp.einsum("tbe,ec->tbc", piece, w_out, preferred_element_type=jnp.float32).astype(
            jnp.bfloat16
        ),
        "head",
        scatter_dimension=0,
        tiled=True,
    ).astype(jnp.float32)
    mixed = (skip_wide + head_sum).astype(jnp.bfloat16)
    part_w_out = jnp.einsum("tbe,tbc->ec", o_narrow, grad_rows, preferred_element_type=jnp.float32)
    d_out = jnp.einsum("tbc,ec->tbe", grad_rows, w_out, preferred_element_type=jnp.float32).astype(
        jnp.bfloat16
    )
    d_out = d_out.reshape(tower_rows, seq_count, local_heads, DH)
    delta = jnp.sum(d_out.astype(jnp.float32) * attention_output, axis=-1)
    probability_gradient = jnp.einsum(
        "qbhd,kbhd->bhqk", d_out, value_all, preferred_element_type=jnp.float32
    )
    d_scores = soft_weights * (probability_gradient - jnp.transpose(delta, (1, 2, 0))[..., None])
    narrow_gradient = d_scores.astype(jnp.bfloat16)
    query_gradient = logit_scale * jnp.einsum(
        "bhqk,kbhd->qbhd", narrow_gradient, key_all, preferred_element_type=jnp.float32
    )
    key_terms = logit_scale * jnp.einsum(
        "bhqk,qbhd->kbhd", narrow_gradient, query_matrix, preferred_element_type=jnp.float32
    )
    value_terms = jnp.einsum(
        "bhqk,qbhd->kbhd", narrow_probabilities, d_out, preferred_element_type=jnp.float32
    )
    d_keys, d_values = (
        lax.psum_scatter(
            key_terms.astype(jnp.bfloat16), "seq", scatter_dimension=0, tiled=True
        ).astype(jnp.float32),
        lax.psum_scatter(
            value_terms.astype(jnp.bfloat16), "seq", scatter_dimension=0, tiled=True
        ).astype(jnp.float32),
    )
    dqkv = (
        jnp.stack([query_gradient, d_keys, d_values])
        .reshape(3, tower_rows, seq_count, local_width)
        .astype(jnp.bfloat16)
    )
    part_w_qkv = jnp.einsum("tbc,itbe->ice", normed_rows, dqkv, preferred_element_type=jnp.float32)
    piece = dqkv
    d_normed = lax.psum_scatter(
        jnp.einsum("itbe,ice->tbc", piece, w_qkv, preferred_element_type=jnp.float32).astype(
            jnp.bfloat16
        ),
        "head",
        scatter_dimension=0,
        tiled=True,
    ).astype(jnp.float32)
    unit_rows = skip_wide * inv_rms
    scaled = d_normed * norm_gain
    d_skip = grad_out.astype(jnp.float32) + inv_rms * (
        scaled - unit_rows * jnp.mean(scaled * unit_rows, axis=-1, keepdims=True)
    )
    d_act = jnp.repeat(d_skip, 2, axis=0) * 0.5
    d_conv = gelu_pull(d_act)[0].astype(jnp.bfloat16)
    d_pad = padded_2(d_conv, ((("seq", "head"), 0),), 2)
    grad_input = jnp.zeros((fine_rows, seq_count, enc_in.shape[2]), jnp.float32)
    for offset in range(KW):
        grad_input = grad_input + jnp.einsum(
            "tbo,io->tbi",
            d_pad[4 - offset : 4 - offset + fine_rows],
            conv_weight[offset],
            preferred_element_type=jnp.float32,
        )
    grad_w_qkv, grad_w_out = (
        lax.psum(part_w_qkv.astype(jnp.bfloat16), "seq").astype(jnp.float32),
        lax.psum(part_w_out.astype(jnp.bfloat16), "seq").astype(jnp.float32),
    )
    return (mixed, grad_input.astype(jnp.bfloat16), grad_w_qkv, grad_w_out)


def solution(mesh):
    return jax.shard_map(
        body,
        mesh=mesh,
        in_specs=(
            P(("seq", "head"), None, None),
            P(),
            P(),
            P(None, None, "head"),
            P("head", None),
            P(("seq", "head"), None, None),
        ),
        out_specs=(
            P(("seq", "head"), None, None),
            P(("seq", "head"), None, None),
            P(None, None, "head"),
            P("head", None),
        ),
        check_vma=False,
    )
```

profile of v0, /device:TPU:26, one launch (start us, length us, event | category | flops | bytes accessed | tf_op | source)
XLA Modules:
  0.0 491.6 jit_solution(5350123949234500055)
XLA Ops:
  10.4 3.9 collective-permute-start.1
  24.6 4.4 multiply_multiply_fusion.2
  32.0 4.2 reduce_sum.45
  41.1 35.9 %all-gather.5.cloned.1.call-done = bf16[128,4,1536]{2,0,1:T(8,128)(2,1)} async-done(((bf16[32,4,1536]{2,0,1:T(8,128)(2,1)}), bf16[128,4,1536]{2,0,1:T(8,128)(2,1)}) %all-gather.5.cloned.1.call-update) | async-done | bytes 1572880 | tf_op jit(solution)/shard_map/all_gather | solution.py:47
  77.1 3.6 fusion.62
  85.9 29.3 %all-gather.11.cloned.1.call-done = bf16[128,4,1536]{2,0,1:T(8,128)(2,1)} async-done(((bf16[32,4,1536]{2,0,1:T(8,128)(2,1)}), bf16[128,4,1536]{2,0,1:T(8,128)(2,1)}) %all-gather.11.cloned.1.call-update) | async-done | bytes 1572880 | tf_op jit(solution)/shard_map/all_gather | solution.py:48
  122.5 28.4 %all-gather.9.cloned.1.call-done = bf16[1024,4,2,192]{0,3,2,1:T(8,128)(2,1)} async-done(((bf16[128,4,2,192]{0,3,2,1:T(8,128)(2,1)}), bf16[1024,4,2,192]{0,3,2,1:T(8,128)(2,1)}) %all-gather.9.cloned.1.call-update) | async-done | bytes 3145744 | tf_op jit(solution)/shard_map/all_gather | solution.py:56
  150.8 5.7 %fusion.125 = (f32[4,2,128]{2,1,0:T(2,128)S(1)}, f32[4,2,128,1024]{3,2,1,0:T(8,128)}) fusion(bf16[128,4,2,192]{0,3,2,1:T(8,128)(2,1)} %bitcast.135, bf16[1024,4,2,192]{0,3,2,1:T(8,128)(2,1)} %all-gather.9.cloned.1.call-done), kind=kOutput, calls=%fused_computation.132 | convolution fusion | flops 405799936 | bytes 7737344 | tf_op jit(solution)/shard_map/sub | solution.py:64
  156.5 5.0 %convolution_convert_fusion.1 = bf16[4,2,192,1024]{3,2,1,0:T(8,128)(2,1)} fusion(bf16[128,4,2,192]{0,3,2,1:T(8,128)(2,1)} %bitcast.144, f32[4,2,128,1024]{3,2,1,0:T(8,128)} %get-tuple-element.40, f32[4,2,128]{2,1,0:T(2,128)S(1)} %get-tuple-element.39), kind=kOutput, calls=%fused_computation.39 | convolution fusion | flops 406323200 | bytes 7737344 | tf_op jit(solution)/shard_map/bhqk,qbhd->kbhd/dot_general | solution.py:99
  161.5 4.7 copy.97
  166.3 19.2 %all-gather.7.cloned.1.call-done = bf16[1024,4,2,192]{0,3,2,1:T(8,128)(2,1)} async-done(((bf16[128,4,2,192]{0,3,2,1:T(8,128)(2,1)}), bf16[1024,4,2,192]{0,3,2,1:T(8,128)(2,1)}) %all-gather.7.cloned.1.call-update) | async-done | bytes 3145744 | tf_op jit(solution)/shard_map/all_gather | solution.py:57
  185.4 5.1 %multiply_reduce_fusion.1 = (f32[128,4,2]{0,2,1:T(2,128)S(1)}, bf16[128,4,2,192]{0,3,2,1:T(8,128)(2,1)}) fusion(bf16[128,4,2,192]{0,3,2,1:T(8,128)(2,1)} %bitcast.145, bf16[1024,4,2,192]{0,3,2,1:T(8,128)(2,1)} %all-gather.7.cloned.1.call-done, f32[4,2,128,1024]{3,2,1,0:T(8,128)} %get-tuple-element.40, f32[4,2,128]{2,1,0:T(2,128)S(1)} %get-tuple-element.39), kind=kOutput, calls=%fused_computation.104 | convolution fusion | flops 405535744 | bytes 8134656 | tf_op jit(solution)/shard_map/bhqk,kbhd->qbhd/dot_general | solution.py:68
  194.8 4.8 copy.95
  199.7 4.6 fusion.82
  209.5 25.3 %reduce-scatter.15.cloned.1.call-done = bf16[128,1536]{1,0:T(8,128)(2,1)} async-done(((bf16[1024,1536]{1,0:T(8,128)(2,1)}), bf16[128,1536]{1,0:T(8,128)(2,1)}) %reduce-scatter.15.cloned.1.call-update) | async-done | bytes 393232
  238.8 46.0 %reduce-scatter.13.cloned.1.call-done = bf16[128,1536]{1,0:T(8,128)(2,1)} async-done(((bf16[1024,1536]{1,0:T(8,128)(2,1)}), bf16[128,1536]{1,0:T(8,128)(2,1)}) %reduce-scatter.13.cloned.1.call-update) | async-done | bytes 393232
  288.6 5.6 %fusion.6 = bf16[3,1536,384]{1,2,0:T(8,128)(2,1)} fusion(bf16[128,4,1536]{2,0,1:T(8,128)(2,1)} %all-gather.5.cloned.1.call-done, bf16[1,128,4,384]{3,1,0,2:T(8,128)(2,1)} %copy.82, bf16[1,128,4,384]{3,1,0,2:T(8,128)(2,1)} %copy.81, bf16[1,128,4,384]{3,1,0,2:T(8,128)(2,1)} %copy.80), kind=kOutput, calls=%fused_computation.11 | convolution fusion | flops 1814888448 | bytes 6291456 | tf_op jit(solution)/shard_map/tbc,itbe->ice/dot_general | solution.py:115
  294.5 4.6 fusion.12
  299.2 4.0 convolution_convert_fusion
  303.2 78.2 %all-reduce.3.cloned.1.call-done = (bf16[3,1536,384]{1,2,0:T(8,128)(2,1)}, bf16[384,1536]{1,0:T(8,128)(2,1)}) async-done(((bf16[3,1536,384]{1,2,0:T(8,128)(2,1)}, bf16[384,1536]{1,0:T(8,128)(2,1)}), (bf16[3,1536,384]{1,2,0:T(8,128)(2,1)}, bf16[384,1536]{1,0:T(8,128)(2,1)})) %all-reduce.3.cloned.1.call-update) | async-done | bytes 4718608 | tf_op jit(solution)/shard_map/psum | solution.py:142
  384.4 6.4 %copy.86 = f32[3,1536,384]{2,1,0:T(8,128)} copy(bf16[3,1536,384]{1,2,0:T(8,128)(2,1)} %get-tuple-element.20) | data formatting | bytes 10616832
  390.8 26.4 %reduce-scatter.11.cloned.1.call-done = bf16[32,4,1536]{2,0,1:T(8,128)(2,1)} async-done(((bf16[128,4,1536]{2,0,1:T(8,128)(2,1)}), bf16[32,4,1536]{2,0,1:T(8,128)(2,1)}) %reduce-scatter.11.cloned.1.call-update) | async-done | bytes 393232 | tf_op jit(solution)/shard_map/reduce_scatter | solution.py:117
  418.7 35.3 %reduce-scatter.9.cloned.1.call-done = bf16[32,4,1536]{2,0,1:T(8,128)(2,1)} async-done(((bf16[128,4,1536]{2,0,1:T(8,128)(2,1)}), bf16[32,4,1536]{2,0,1:T(8,128)(2,1)}) %reduce-scatter.9.cloned.1.call-update) | async-done | bytes 393232 | tf_op jit(solution)/shard_map/reduce_scatter | solution.py:73
  464.3 3.8 collective-permute-start.3
  (83 shorter events, 83.0 us)
Async XLA Ops:
  7.2 69.9 %copy-start = (bf16[3,1536,384]{2,1,0:T(8,128)(2,1)S(1)}, bf16[3,1536,384]{2,1,0:T(8,128)(2,1)}, u32[]{:S(2)}) copy-start(bf16[3,1536,384]{2,1,0:T(8,128)(2,1)} %param.9) | copy-start | bytes 10616836
  7.2 69.9 %all-gather.5.cloned.1.call-start = ((), (), s32[]{:S(2)}) async-start(), calls=%async_computation.4 | async-start | bytes 1966080 | tf_op jit(solution)/shard_map/all_gather | solution.py:47
  8.5 11.2 %collective-permute-start = (bf16[2,4,768]{2,0,1:T(2,128)(2,1)S(1)}, bf16[2,4,768]{2,0,1:T(2,128)(2,1)S(1)}, u32[]{:S(2)}, u32[]{:S(2)}) collective-permute-start(bf16[2,4,768]{2,0,1:T(2,128)(2,1)S(1)} %get-tuple-element.33), channel_id=1, source_target_pairs={{0,1},{1,2},{2,3},{3,4},{4,5},{5,6},{6,7},{7,8},{8,9},{9,10},{10,1... | collective-permute-start | bytes 36872 | tf_op jit(solution)/shard_map/ppermute | solution.py:15
  10.4 6.8 %collective-permute-start.1 = (bf16[2,4,768]{2,0,1:T(2,128)(2,1)S(1)}, bf16[2,4,768]{2,0,1:T(2,128)(2,1)S(1)}, u32[]{:S(2)}, u32[]{:S(2)}) collective-permute-start(bf16[2,4,768]{2,0,1:T(2,128)(2,1)S(1)} %get-tuple-element.34), channel_id=1, source_target_pairs={{1,0},{2,1},{3,2},{4,3},{5,4},{6,5},{7,6},{8,7},{9,8},{10,9},{11,1... | collective-permute-start | bytes 36872 | tf_op jit(solution)/shard_map/ppermute | solution.py:18
  32.0 6.2 %copy-start.7 = (f32[1536]{0:T(1024)S(1)}, f32[1536]{0:T(1024)}, u32[]{:S(2)}) copy-start(f32[1536]{0:T(1024)} %param.8) | copy-start | bytes 18436
  37.5 0.8 copy-start.1
  39.2 76.0 %all-gather.11.cloned.1.call-start = ((), (), s32[]{:S(2)}) async-start(), calls=%async_computation.8 | async-start | bytes 1966080 | tf_op jit(solution)/shard_map/all_gather | solution.py:48
  41.1 109.8 %all-gather.9.cloned.1.call-start = ((), (), s32[]{:S(2)}) async-start(), calls=%async_computation.6 | async-start | bytes 3538944 | tf_op jit(solution)/shard_map/all_gather | solution.py:56
  83.7 101.8 %all-gather.7.cloned.1.call-start = ((), (), s32[]{:S(2)}) async-start(), calls=%async_computation.5 | async-start | bytes 3538944 | tf_op jit(solution)/shard_map/all_gather | solution.py:57
  85.6 149.2 %reduce-scatter.15.cloned.1.call-start = ((), (), s32[]{:S(2)}) async-start(), calls=%async_computation.11 | async-start | bytes 3538944
  166.2 118.5 %reduce-scatter.13.cloned.1.call-start = ((), (), s32[]{:S(2)}) async-start(), calls=%async_computation.10 | async-start | bytes 3538944
  185.4 5.2 %copy-start.4 = (f32[4,2,128,1024]{3,2,1,0:T(8,128)S(1)}, f32[4,2,128,1024]{3,2,1,0:T(8,128)}, u32[]{:S(2)}) copy-start(f32[4,2,128,1024]{3,2,1,0:T(8,128)} %get-tuple-element.40) | copy-start | bytes 12582916
  185.4 5.2 %copy-start.6 = (bf16[128,4,384]{0,2,1:T(8,128)(2,1)S(1)}, bf16[128,4,384]{0,2,1:T(8,128)(2,1)}, u32[]{:S(2)}) copy-start(bf16[128,4,384]{0,2,1:T(8,128)(2,1)} %copy.79) | copy-start | bytes 1179652
  185.4 5.7 %copy-start.8 = (bf16[1024,4,2,192]{0,3,2,1:T(8,128)(2,1)S(1)}, bf16[1024,4,2,192]{0,3,2,1:T(8,128)(2,1)}, u32[]{:S(2)}) copy-start(bf16[1024,4,2,192]{0,3,2,1:T(8,128)(2,1)} %all-gather.7.cloned.1.call-done) | copy-start | bytes 9437188
  191.1 1.1 copy-start.2
  192.2 2.6 copy-start.3
  199.7 181.8 %all-reduce.3.cloned.1.call-start = ((), (), s32[]{:S(2)}) async-start(), calls=%async_computation.12 | async-start | bytes 9437184 | tf_op jit(solution)/shard_map/psum | solution.py:142
  294.2 123.0 %reduce-scatter.11.cloned.1.call-start = ((), (), s32[]{:S(2)}) async-start(), calls=%async_computation.9 | async-start | bytes 1966080 | tf_op jit(solution)/shard_map/reduce_scatter | solution.py:117
  299.2 154.8 %reduce-scatter.9.cloned.1.call-start = ((), (), s32[]{:S(2)}) async-start(), calls=%async_computation.7 | async-start | bytes 1966080 | tf_op jit(solution)/shard_map/reduce_scatter | solution.py:73
  464.3 6.3 %copy-start.5 = (bf16[32,4,1536]{2,0,1:T(8,128)(2,1)S(1)}, bf16[32,4,1536]{2,0,1:T(8,128)(2,1)}, u32[]{:S(2)}) copy-start(bf16[32,4,1536]{2,0,1:T(8,128)(2,1)} %get-tuple-element.32) | copy-start | bytes 1179652
  464.3 9.5 %collective-permute-start.3 = (bf16[2,4,1536]{2,0,1:T(2,128)(2,1)S(1)}, bf16[2,4,1536]{2,0,1:T(2,128)(2,1)S(1)}, u32[]{:S(2)}, u32[]{:S(2)}) collective-permute-start(bf16[2,4,1536]{2,0,1:T(2,128)(2,1)S(1)} %get-tuple-element.28), channel_id=1, source_target_pairs={{0,1},{1,2},{2,3},{3,4},{4,5},{5,6},{6,7},{7,8},{8,9},{9,10},{10,1... | collective-permute-start | bytes 73736 | tf_op jit(solution)/shard_map/ppermute | solution.py:15
  471.6 7.2 %collective-permute-start.2 = (bf16[2,4,1536]{2,0,1:T(2,128)(2,1)S(1)}, bf16[2,4,1536]{2,0,1:T(2,128)(2,1)S(1)}, u32[]{:S(2)}, u32[]{:S(2)}) collective-permute-start(bf16[2,4,1536]{2,0,1:T(2,128)(2,1)S(1)} %get-tuple-element.27), channel_id=1, source_target_pairs={{1,0},{2,1},{3,2},{4,3},{5,4},{6,5},{7,6},{8,7},{9,8},{10,9},{11,1... | collective-permute-start | bytes 73736 | tf_op jit(solution)/shard_map/ppermute | solution.py:18
Sparse Core Ops, SparseCore 0:
  39.3 37.7 all-gather.4
  79.2 35.9 all-gather.10
  117.1 33.7 all-gather.8
  152.6 32.8 all-gather.6
  188.7 46.1 reduce-scatter.14
  238.5 46.2 reduce-scatter.12
  294.4 87.0 all-reduce.2
  383.8 33.3 reduce-scatter.10
  419.7 34.2 reduce-scatter.8
where the time goes:
time: 499 us; the launch traced here: 492 us
  waiting for transfers between devices  325 us (65%)
  matrix products  75.6 us (15%)
  local copies, waits for them, and re-layouts  48.6 us (10%)
  other arithmetic  16.1 us (3%)
  between operations  14.1 us (3%)
  starting transfers between devices  12.6 us (3%)
    psum x1, waiting for transfers between devices, body(): lax.psum(part_w_qkv.astype(jnp.bfloat16), 'seq').astype(jnp.float32)  78.2 us
    unnamed x11, waiting for transfers between devices  71.5 us
    all_gather x1, waiting for transfers between devices, body(): normed_rows = lax.all_gather(normed, 'head', axis=0, tiled=True)  35.9 us
    reduce_scatter x1, waiting for transfers between devices, body(): lax.psum_scatter(jnp.einsum('tbe,ec->tbc', piece, w_out, preferred_elemen...  35.3 us
    all_gather x1, waiting for transfers between devices, body(): grad_rows = lax.all_gather(grad_out, 'head', axis=0, tiled=True)  29.3 us
    all_gather x1, waiting for transfers between devices, body(): lax.all_gather(key_matrix, 'seq', axis=0, tiled=True)  28.4 us
    reduce_scatter x1, waiting for transfers between devices, body(): lax.psum_scatter(jnp.einsum('itbe,ice->tbc', piece, w_qkv, preferred_elem...  26.4 us
    unnamed x27, local copies, waits for them, and re-layouts  26.2 us
  transfers between devices with their start and end apart: 13, of which 10 were waited for; matrix products, arithmetic and copies ran while one was open for 19% of the time, Pallas kernels for 0%

commit v1 on v0

--- a/solution.py
+++ b/solution.py
@@ -1,10 +1,389 @@
+import functools
+
 import jax
 import jax.numpy as jnp
 from jax import lax
+from jax.experimental import pallas as pl
+from jax.experimental.pallas import tpu as pltpu
 from jax.sharding import PartitionSpec as P
 
 DH = 192
 KW = 5
+VMEM_LIMIT = 56 * 1024 * 1024
+BF = jnp.bfloat16
+F32 = jnp.float32
+
+
+def params():
+    return pltpu.CompilerParams(vmem_limit_bytes=VMEM_LIMIT)
+
+
+def dot(a, b, contract):
+    return lax.dot_general(a, b, (contract, ((), ())), preferred_element_type=F32)
+
+
+NN = ((1,), (0,))
+NT = ((1,), (1,))
+TN = ((0,), (0,))
+
+
+def shifted(ref, parity, shift, rows):
+    seqs = ref.shape[1]
+    wide = ref[parity].astype(F32)[:, shift : shift + rows, :]
+    return wide.reshape(seqs * rows, ref.shape[3]).astype(BF)
+
+
+def conv_kernel(x_ref, w_ref, gain_ref, skip_ref, slope_ref, normed_ref, acc):
+    step = pl.program_id(0)
+    rows = x_ref.shape[2] - 2
+    half = acc.shape[0] // 2
+    for tap in range(KW):
+
+        @pl.when(step == tap)
+        def _():
+            for parity in range(2):
+                place = parity + tap
+                lhs = shifted(x_ref, place % 2, place // 2, rows)
+                term = dot(lhs, w_ref[0], NN)
+                part = pl.ds(parity * half, half)
+                if tap == 0:
+                    acc[part, :] = term
+                else:
+                    acc[part, :] = acc[part, :] + term
+
+    @pl.when(step == KW - 1)
+    def _():
+        root = 0.7978845608028654
+        total = None
+        for parity in range(2):
+            x = acc[parity * half : (parity + 1) * half, :]
+            square = x * x
+            t = jnp.tanh(root * (x + 0.044715 * (square * x)))
+            left = 0.5 * (1.0 + t)
+            act = x * left
+            slope_ref[parity] = left + (0.5 * root) * x * (1.0 - t * t) * (
+                1.0 + (3 * 0.044715) * square
+            )
+            total = act if total is None else total + act
+        skip = (0.5 * total).astype(BF)
+        skip_ref[...] = skip
+        wide = skip.astype(F32)
+        inv = lax.rsqrt(jnp.mean(wide * wide, axis=-1, keepdims=True) + 1e-06)
+        normed_ref[...] = (wide * inv * gain_ref[...]).astype(BF)
+
+
+def encoder(padded, conv_weight, norm_gain):
+    _, seqs, rows2, c_in = padded.shape
+    rows = rows2 - 2
+    width = conv_weight.shape[2]
+    flat = seqs * rows
+    return pl.pallas_call(
+        conv_kernel,
+        grid=(KW,),
+        in_specs=[
+            pl.BlockSpec(padded.shape, lambda k: (0, 0, 0, 0)),
+            pl.BlockSpec((1, c_in, width), lambda k: (k, 0, 0)),
+            pl.BlockSpec((1, width), lambda k: (0, 0)),
+        ],
+        out_specs=[
+            pl.BlockSpec((flat, width), lambda k: (0, 0)),
+            pl.BlockSpec((2, flat, width), lambda k: (0, 0, 0)),
+            pl.BlockSpec((flat, width), lambda k: (0, 0)),
+        ],
+        out_shape=[
+            jax.ShapeDtypeStruct((flat, width), BF),
+            jax.ShapeDtypeStruct((2, flat, width), F32),
+            jax.ShapeDtypeStruct((flat, width), BF),
+        ],
+        scratch_shapes=[pltpu.VMEM((2 * flat, width), F32)],
+        compiler_params=params(),
+        name="encoder_forward",
+    )(padded, conv_weight, norm_gain.reshape(1, width))
+
+
+def d_conv_kernel(dn_ref, skip_ref, grad_ref, gain_ref, slope_ref, out_ref):
+    wide = skip_ref[...].astype(F32)
+    inv = lax.rsqrt(jnp.mean(wide * wide, axis=-1, keepdims=True) + 1e-06)
+    unit = wide * inv
+    scaled = dn_ref[...].astype(F32) * gain_ref[...]
+    d_skip = grad_ref[...].astype(F32) + inv * (
+        scaled - unit * jnp.mean(scaled * unit, axis=-1, keepdims=True)
+    )
+    d_act = 0.5 * d_skip
+    for parity in range(2):
+        out_ref[parity] = (slope_ref[parity] * d_act).astype(BF)
+
+
+def d_conv_call(d_normed, skip, grad, norm_gain, slope):
+    return pl.pallas_call(
+        d_conv_kernel,
+        out_shape=jax.ShapeDtypeStruct(slope.shape, BF),
+        compiler_params=params(),
+        name="conv_gradient",
+    )(d_normed, skip, grad, norm_gain.reshape(1, -1), slope)
+
+
+def conv_back_kernel(d_ref, w_ref, out_ref, acc):
+    step = pl.program_id(0)
+    rows = d_ref.shape[2] - 2
+    half = acc.shape[0] // 2
+    for tap in range(KW):
+
+        @pl.when(step == tap)
+        def _():
+            for parity in range(2):
+                place = parity + KW - 1 - tap
+                lhs = shifted(d_ref, place % 2, place // 2, rows)
+                term = dot(lhs, w_ref[0], NT)
+                part = pl.ds(parity * half, half)
+                if tap == 0:
+                    acc[part, :] = term
+                elif tap < KW - 1:
+                    acc[part, :] = acc[part, :] + term
+                else:
+                    out_ref[part, :] = (acc[part, :] + term).astype(BF)
+
+
+def conv_back(d_pad, conv_weight):
+    _, seqs, rows2, width = d_pad.shape
+    c_in = conv_weight.shape[1]
+    flat = 2 * seqs * (rows2 - 2)
+    return pl.pallas_call(
+        conv_back_kernel,
+        grid=(KW,),
+        in_specs=[
+            pl.BlockSpec(d_pad.shape, lambda k: (0, 0, 0, 0)),
+            pl.BlockSpec((1, c_in, width), lambda k: (k, 0, 0)),
+        ],
+        out_specs=pl.BlockSpec((flat, c_in), lambda k: (0, 0)),
+        out_shape=jax.ShapeDtypeStruct((flat, c_in), BF),
+        scratch_shapes=[pltpu.VMEM((flat, c_in), F32)],
+        compiler_params=params(),
+        name="encoder_backward",
+    )(d_pad, conv_weight)
+
+
+def project_kernel(x_ref, g_ref, w_ref, wo_ref, out_ref):
+    groups, seqs, rows, width = x_ref.shape
+    flat = groups * seqs * rows
+    x = x_ref[...].reshape(flat, width)
+    g = g_ref[...].reshape(flat, width)
+    qkv = dot(x, w_ref[0], NN)
+    d_o = dot(g, wo_ref[0], NT)
+    both = jnp.concatenate([qkv, d_o], axis=1).astype(BF)
+    for z in range(groups):
+        for b in range(seqs):
+            first = (z * seqs + b) * rows
+            out_ref[b, 0, z * rows : (z + 1) * rows, :] = both[first : first + rows]
+
+
+def project(x, g, w_pack, w_out):
+    groups, seqs, rows, width = x.shape
+    heads, _, packed = w_pack.shape
+    full = packed + w_out.shape[1]
+    return pl.pallas_call(
+        project_kernel,
+        grid=(heads,),
+        in_specs=[
+            pl.BlockSpec(x.shape, lambda h: (0, 0, 0, 0)),
+            pl.BlockSpec(g.shape, lambda h: (0, 0, 0, 0)),
+            pl.BlockSpec((1, width, packed), lambda h: (h, 0, 0)),
+            pl.BlockSpec((1, w_out.shape[1], width), lambda h: (h, 0, 0)),
+        ],
+        out_specs=pl.BlockSpec((seqs, 1, groups * rows, full), lambda h: (0, h, 0, 0)),
+        out_shape=jax.ShapeDtypeStruct((seqs, heads, groups * rows, full), BF),
+        compiler_params=params(),
+        name="projections",
+    )(x, g, w_pack, w_out)
+
+
+def attention_kernel(in_ref, out_ref, dk_acc, dv_acc, *, block):
+    scale = DH ** (-0.5)
+    length = in_ref.shape[0]
+    k = in_ref[:, DH : 2 * DH]
+    v = in_ref[:, 2 * DH : 3 * DH]
+    for start in range(0, length, block):
+        rows = pl.ds(start, block)
+        q = in_ref[rows, 0:DH]
+        d_o = in_ref[rows, 3 * DH : 4 * DH]
+        s = dot(q, k, NT) * scale
+        e = jnp.exp(s - jnp.max(s, axis=-1, keepdims=True))
+        p = e * (1.0 / jnp.sum(e, axis=-1, keepdims=True))
+        p_b = p.astype(BF)
+        o = dot(p_b, v, NN)
+        delta = jnp.sum(d_o.astype(F32) * o, axis=-1, keepdims=True)
+        d_p = dot(d_o, v, NT)
+        ds = (p * (d_p - delta)).astype(BF)
+        dq = scale * dot(ds, k, NN)
+        dk = dot(ds, q, TN)
+        dv = dot(p_b, d_o, TN)
+        if start == 0:
+            dk_acc[...] = dk
+            dv_acc[...] = dv
+        else:
+            dk_acc[...] += dk
+            dv_acc[...] += dv
+        out_ref[rows, 0:DH] = o.astype(BF)
+        out_ref[rows, DH : 2 * DH] = dq.astype(BF)
+    out_ref[:, 2 * DH : 3 * DH] = (scale * dk_acc[...]).astype(BF)
+    out_ref[:, 3 * DH : 4 * DH] = dv_acc[...].astype(BF)
+
+
+def attention(packed):
+    length = packed.shape[0]
+    return pl.pallas_call(
+        functools.partial(attention_kernel, block=min(256, length)),
+        out_shape=jax.ShapeDtypeStruct(packed.shape, BF),
+        scratch_shapes=[pltpu.VMEM((length, DH), F32), pltpu.VMEM((length, DH), F32)],
+        compiler_params=params(),
+        name="attention",
+    )(packed)
+
+
+def ordered(ref, first, last, groups):
+    seqs, _, rows, _ = ref.shape
+    rows //= groups
+    pieces = [
+        ref[b, 0, z * rows : (z + 1) * rows, first:last]
+        for z in range(groups)
+        for b in range(seqs)
+    ]
+    return jnp.concatenate(pieces, axis=0)
+
+
+def term_kernel(in_ref, w_ref, out_ref, acc, *, first, last, contract):
+    groups = out_ref.shape[0]
+    step = pl.program_id(0)
+    term = dot(ordered(in_ref, first, last, groups), w_ref[0], contract)
+
+    @pl.when(step == 0)
+    def _():
+        acc[...] = term
+
+    @pl.when(step > 0)
+    def _():
+        acc[...] += term
+
+    @pl.when(step == pl.num_programs(0) - 1)
+    def _():
+        out_ref[...] = acc[...].astype(BF).reshape(out_ref.shape)
+
+
+def head_sum_term(units, weight, groups, first, last, contract, width, name):
+    seqs, heads, rows, full = units.shape
+    shape = (groups, seqs, rows // groups, width)
+    return pl.pallas_call(
+        functools.partial(term_kernel, first=first, last=last, contract=contract),
+        grid=(heads,),
+        in_specs=[
+            pl.BlockSpec((seqs, 1, rows, full), lambda h: (0, h, 0, 0)),
+            pl.BlockSpec((1,) + weight.shape[1:], lambda h: (h, 0, 0)),
+        ],
+        out_specs=pl.BlockSpec(shape, lambda h: (0, 0, 0, 0)),
+        out_shape=jax.ShapeDtypeStruct(shape, BF),
+        scratch_shapes=[pltpu.VMEM((seqs * rows, width), F32)],
+        compiler_params=params(),
+        name=name,
+    )(units, weight)
+
+
+def weight_kernel(in_ref, x_ref, g_ref, qkv_ref, out_ref):
+    groups, seqs, rows, width = x_ref.shape
+    flat = groups * seqs * rows
+    x = x_ref[...].reshape(flat, width)
+    g = g_ref[...].reshape(flat, width)
+    both = ordered(in_ref, 0, 4 * DH, groups)
+    qkv_ref[0] = dot(x, both[:, DH:], TN).astype(BF)
+    out_ref[0] = dot(both[:, :DH], g, TN).astype(BF)
+
+
+def weight_gradients(units, x, g):
+    seqs, heads, rows, full = units.shape
+    width = x.shape[-1]
+    return pl.pallas_call(
+        weight_kernel,
+        grid=(heads,),
+        in_specs=[
+            pl.BlockSpec((seqs, 1, rows, full), lambda h: (0, h, 0, 0)),
+            pl.BlockSpec(x.shape, lambda h: (0, 0, 0, 0)),
+            pl.BlockSpec(g.shape, lambda h: (0, 0, 0, 0)),
+        ],
+        out_specs=[
+            pl.BlockSpec((1, width, 3 * DH), lambda h: (h, 0, 0)),
+            pl.BlockSpec((1, DH, width), lambda h: (h, 0, 0)),
+        ],
+        out_shape=[
+            jax.ShapeDtypeStruct((heads, width, 3 * DH), BF),
+            jax.ShapeDtypeStruct((heads, DH, width), BF),
+        ],
+        compiler_params=params(),
+        name="weight_gradients",
+    )(units, x, g)
+
+
+def neighbour_edges(pairs):
+    axes = ("seq", "head")
+    count = lax.axis_size(axes)
+    forward = [(i, i + 1) for i in range(count - 1)]
+    backward = [(target, source) for source, target in forward]
+    low = lax.ppermute(pairs[:, :, -1:, :], axes, forward)
+    high = lax.ppermute(pairs[:, :, :1, :], axes, backward)
+    return jnp.concatenate([low, pairs, high], axis=2)
+
+
+def unit_body(enc_in, conv_weight, norm_gain, w_qkv, w_out, grad_out):
+    rows = enc_in.shape[0] // 2
+    seqs = enc_in.shape[1]
+    width = conv_weight.shape[2]
+    local = w_qkv.shape[2]
+    heads = local // DH
+    groups = lax.axis_size("head")
+    blocks = lax.axis_size("seq")
+
+    grad = jnp.transpose(grad_out, (1, 0, 2))
+    grad_rows = lax.all_gather(grad, "head", axis=0, tiled=False)
+
+    pairs = jnp.transpose(enc_in.reshape(rows, 2, seqs, enc_in.shape[2]), (1, 2, 0, 3))
+    skip, slope, normed = encoder(neighbour_edges(pairs), conv_weight, norm_gain)
+    normed_rows = lax.all_gather(normed.reshape(seqs, rows, width), "head", axis=0, tiled=False)
+
+    w_pack = jnp.transpose(w_qkv.reshape(3, width, heads, DH), (2, 1, 0, 3))
+    w_pack = w_pack.reshape(heads, width, 3 * DH)
+    w_rows = w_out.reshape(heads, DH, width)
+    mine = project(normed_rows, grad_rows, w_pack, w_rows)
+    tower = groups * rows
+    sent = mine.reshape(blocks, tower, 4 * DH)
+    unit = lax.all_to_all(sent, "seq", split_axis=0, concat_axis=0, tiled=True)
+    result = attention(unit.reshape(blocks * tower, 4 * DH))
+    back = lax.all_to_all(
+        result.reshape(blocks, tower, 4 * DH), "seq", split_axis=0, concat_axis=0, tiled=True
+    )
+    units = back.reshape(seqs, heads, tower, 4 * DH)
+
+    d_term = head_sum_term(units, w_pack, groups, DH, 4 * DH, NT, width, "d_term")
+    d_normed = lax.psum_scatter(d_term, "head", scatter_dimension=0, tiled=False)
+    head_term = head_sum_term(units, w_rows, groups, 0, DH, NN, width, "head_term")
+    head_sum = lax.psum_scatter(head_term, "head", scatter_dimension=0, tiled=False)
+    part_qkv, part_out = weight_gradients(units, normed_rows, grad_rows)
+    sum_qkv = lax.psum(part_qkv, "seq")
+    sum_out = lax.psum(part_out, "seq")
+
+    flat = seqs * rows
+    d_conv = d_conv_call(
+        d_normed.reshape(flat, width), skip, grad.reshape(flat, width), norm_gain, slope
+    )
+    d_pad = neighbour_edges(d_conv.reshape(2, seqs, rows, width))
+    grad_input = conv_back(d_pad, conv_weight)
+    grad_input = jnp.transpose(grad_input.reshape(2, seqs, rows, -1), (2, 0, 1, 3))
+
+    mixed = skip.reshape(seqs, rows, width).astype(F32) + head_sum.astype(F32)
+    grad_qkv = jnp.transpose(sum_qkv.reshape(heads, width, 3, DH), (2, 1, 0, 3))
+    return (
+        jnp.transpose(mixed.astype(BF), (1, 0, 2)),
+        grad_input.reshape(enc_in.shape),
+        grad_qkv.reshape(3, width, local).astype(F32),
+        sum_out.reshape(local, width).astype(F32),
+    )
 
 
 def padded_2(block, sides, width):
@@ -20,7 +399,7 @@
     return block
 
 
-def body(enc_in, conv_weight, norm_gain, w_qkv, w_out, grad_out):
+def gathered_body(enc_in, conv_weight, norm_gain, w_qkv, w_out, grad_out):
     fine_rows = enc_in.shape[0]
     slab_rows = fine_rows // 2
     seq_count = enc_in.shape[1]
@@ -145,6 +524,12 @@
     return (mixed, grad_input.astype(jnp.bfloat16), grad_w_qkv, grad_w_out)
 
 
+def body(enc_in, conv_weight, norm_gain, w_qkv, w_out, grad_out):
+    units = enc_in.shape[1] * (w_qkv.shape[2] // DH)
+    chosen = unit_body if units == lax.axis_size("seq") else gathered_body
+    return chosen(enc_in, conv_weight, norm_gain, w_qkv, w_out, grad_out)
+
+
 def solution(mesh):
     return jax.shard_map(
         body,

time: 499 us -> 353 us (0.71)
  waiting for transfers between devices: 325 us -> 175 us
  matrix products: 75.6 us -> 0 us
  Pallas kernels: 0 us -> 59.4 us
  blocking collectives: 0 us -> 49.6 us
  local copies, waits for them, and re-layouts: 48.6 us -> 30.4 us
  other arithmetic: 16.1 us -> 5.01 us
    unnamed x11 -> x5, waiting for transfers between devices: 71.5 us -> 0.08 us
    dot_general x21 -> x0, matrix products: 70 us -> none  [the longest x5 14.3 us: body(): jnp.einsum('tbi,io->tbo', padded[offset:offset + fine_rows], conv_weight[...]
    all_gather x4 -> x2, waiting for transfers between devices: 113 us -> 44.1 us  [the longest x1 38.2 us: unit_body(): lax.all_gather(normed.reshape(seqs, rows, width), 'head', axis=0, tiled=F...]
    pallas_call x0 -> x8, Pallas kernels: none -> 59.4 us  [the longest x1 11.1 us: conv_back(): pl.pallas_call(conv_back_kernel, grid=(KW,), in_specs=[pl.BlockSpec(d_pad...]
    all_to_all x0 -> x2, blocking collectives: none -> 49.6 us  [the longest x1 25.3 us: unit_body(): lax.all_to_all(result.reshape(blocks, tower, 4 * DH), 'seq', split_axis=0...]
    unnamed x27 -> x14, local copies, waits for them, and re-layouts: 26.2 us -> 13.1 us
    reduce_scatter x2, waiting for transfers between devices: 61.8 us -> 54.2 us  [the longest x1 27.5 us: unit_body(): lax.psum_scatter(d_term, 'head', scatter_dimension=0, tiled=False)]
    reduce_sum x3 -> x0, other arithmetic: 6.84 us -> none  [the longest x1 4.15 us: body(): jnp.mean(activated.reshape(slab_rows, 2, seq_count, out_width), axis=1)]
  transfers between devices with their start and end apart: 13 -> 9, of which waited for: 10 -> 6; matrix products, arithmetic and copies ran while one was open for 19% -> 7% of each run, Pallas kernels for 0% -> 7%
where the time goes in v1:
time: 353 us; the launch traced here: 349 us
  waiting for transfers between devices  175 us (50%)
  Pallas kernels  59.4 us (17%)
  blocking collectives  49.6 us (14%)
  local copies, waits for them, and re-layouts  30.4 us (9%)
  starting transfers between devices  15.1 us (4%)
  between operations  13.9 us (4%)
  other arithmetic  5.01 us (1%)
    psum x1, waiting for transfers between devices, unit_body(): sum_qkv = lax.psum(part_qkv, 'seq')  76 us
    all_gather x1, waiting for transfers between devices, unit_body(): lax.all_gather(normed.reshape(seqs, rows, width), 'head', axis=0, tiled=F...  38.2 us
    reduce_scatter x1, waiting for transfers between devices, unit_body(): lax.psum_scatter(d_term, 'head', scatter_dimension=0, tiled=False)  27.5 us
    reduce_scatter x1, waiting for transfers between devices, unit_body(): lax.psum_scatter(head_term, 'head', scatter_dimension=0, tiled=False)  26.7 us
    all_to_all x1, blocking collectives, unit_body(): lax.all_to_all(result.reshape(blocks, tower, 4 * DH), 'seq', split_axis=0...  25.3 us
    all_to_all x1, blocking collectives, unit_body(): unit = lax.all_to_all(sent, 'seq', split_axis=0, concat_axis=0, tiled=True)  24.4 us
    unnamed x14, local copies, waits for them, and re-layouts  13.1 us
    pallas_call x1, Pallas kernels, conv_back(): pl.pallas_call(conv_back_kernel, grid=(KW,), in_specs=[pl.BlockSpec(d_pad...  11.1 us
  transfers between devices with their start and end apart: 9, of which 6 were waited for; matrix products, arithmetic and copies ran while one was open for 7% of the time, Pallas kernels for 7%

profile of v1, /device:TPU:26, one launch (start us, length us, event | category | flops | bytes accessed | tf_op | source)
XLA Modules:
  0.0 348.8 jit_solution(1544199374299594542)
XLA Ops:
  10.2 2.4 collective-permute-start.1
  12.6 5.0 %collective-permute-start = (bf16[2,4,1,768]{3,2,1,0:T(2,128)(2,1)S(1)}, bf16[2,4,1,768]{3,2,1,0:T(2,128)(2,1)S(1)}, u32[]{:S(2)}, u32[]{:S(2)}) collective-permute-start(bf16[2,4,1,768]{3,2,1,0:T(2,128)(2,1)S(1)} %get-tuple-element.32), channel_id=1, source_target_pairs={{0,1},{1,2},{2,3},{3,4},{4,5},{5,6},{6,7},{7,8},{8,9},{9,10},{10,1... | collective-permute-start | bytes 36872 | tf_op jit(solution)/shard_map/ppermute | solution.py:329
  20.1 10.0 %encoder_forward.1 = (bf16[128,1536]{1,0:T(8,128)(2,1)}, f32[2,128,1536]{2,1,0:T(8,128)}, bf16[128,1536]{1,0:T(8,128)(2,1)}) custom-call(bf16[2,4,34,768]{3,2,1,0:T(8,128)(2,1)} %pad_maximum_fusion.1.x_ref, bf16[5,768,1536]{2,1,0:T(8,128)(2,1)} %w_ref.3, f32[1,1536]{1,0:T(1,128)} %reshape.63.gain_ref), custom_call_target="tpu_custom_call" | custom-call | tf_op jit(solution)/shard_map/encoder_forward/pallas_call | solution.py:80
  30.1 3.7 %copy.30 = bf16[3,1536,384]{1,2,0:T(8,128)(2,1)} copy(bf16[3,1536,384]{2,1,0:T(8,128)(2,1)S(1)} %copy-done.1) | data formatting | bytes 7077888 | tf_op args[3]
  33.8 2.2 copy.31
  36.0 3.7 %copy.32.w_ref = bf16[2,1536,576]{2,1,0:T(8,128)(2,1)} copy(bf16[2,1536,576]{1,2,0:T(8,128)(2,1)S(1)} %bitcast.40) | data formatting | bytes 7077888 | tf_op jit(solution)/shard_map/reshape | solution.py:351
  39.7 5.9 %all-gather.6.cloned.1.call-done = bf16[16,32,1536]{2,1,0:T(8,128)(2,1)} async-done(((bf16[4,32,1536]{2,1,0:T(8,128)(2,1)}), bf16[16,32,1536]{2,1,0:T(8,128)(2,1)}) %all-gather.6.cloned.1.call-update) | async-done | bytes 1572880 | tf_op jit(solution)/shard_map/all_gather | solution.py:344
  45.6 38.2 %all-gather.4.cloned.1.call-done.x_ref = bf16[4,4,32,1536]{3,2,1,0:T(8,128)(2,1)} async-done(((bf16[1,4,32,1536]{3,2,1,0:T(8,128)(2,1)}), bf16[4,4,32,1536]{3,2,1,0:T(8,128)(2,1)}) %all-gather.4.cloned.1.call-update) | async-done | bytes 1572880 | tf_op jit(solution)/shard_map/all_gather | solution.py:348
  83.8 7.3 %projections.1 = bf16[4,2,128,768]{3,2,1,0:T(8,128)(2,1)} custom-call(bf16[4,4,32,1536]{3,2,1,0:T(8,128)(2,1)} %all-gather.4.cloned.1.call-done.x_ref, bf16[4,4,32,1536]{3,2,1,0:T(8,128)(2,1)} %bitcast.44, bf16[2,1536,576]{2,1,0:T(8,128)(2,1)} %copy.32.w_ref, bf16[2,192,1536]{2,1,0:T(8,128)(2,1)} %bitcast.49), custom_call_target="tpu_custom_call" | custom-call | tf_op jit(solution)/shard_map/projections/pallas_call | solution.py:184
  91.1 24.4 %all_to_all.10 = bf16[8,128,768]{2,1,0:T(8,128)(2,1)} all-to-all(bf16[8,128,768]{2,1,0:T(8,128)(2,1)} %bitcast.48), channel_id=1, replica_groups=mesh['seq'=8,'head'=4] {'seq'}, dimensions={0} | all-to-all | bytes 3145728 | tf_op jit(solution)/shard_map/all_to_all | solution.py:356
  115.5 9.5 %attention.1 = bf16[1024,768]{1,0:T(8,128)(2,1)} custom-call(bf16[1024,768]{1,0:T(8,128)(2,1)} %bitcast.46), custom_call_target="tpu_custom_call" | custom-call | tf_op jit(solution)/shard_map/attention/pallas_call | solution.py:234
  125.0 25.3 %all_to_all.11 = bf16[8,128,768]{2,1,0:T(8,128)(2,1)} all-to-all(bf16[8,128,768]{2,1,0:T(8,128)(2,1)} %bitcast.47), channel_id=1, replica_groups=mesh['seq'=8,'head'=4] {'seq'}, dimensions={0} | all-to-all | bytes 3145728 | tf_op jit(solution)/shard_map/all_to_all | solution.py:358
  150.3 7.4 %weight_gradients.1 = (bf16[2,1536,576]{2,1,0:T(8,128)(2,1)}, bf16[2,192,1536]{2,1,0:T(8,128)(2,1)}) custom-call(bf16[4,2,128,768]{3,2,1,0:T(8,128)(2,1)} %bitcast.37, bf16[4,4,32,1536]{3,2,1,0:T(8,128)(2,1)} %all-gather.4.cloned.1.call-done.x_ref, bf16[4,4,32,1536]{3,2,1,0:T(8,128)(2,1)} %bitcast.45), custom_call_target="tpu_custom_call" | custom-call | tf_op jit(solution)/shard_map/weight_gradients/pallas_call | solution.py:303
  157.6 4.4 %copy.35 = bf16[2,1536,576]{1,2,0:T(8,128)(2,1)S(1)} copy(bf16[2,1536,576]{2,1,0:T(8,128)(2,1)} %get-tuple-element.12) | data formatting | bytes 7077888 | tf_op jit(solution)/shard_map/weight_gradients/pallas_call | solution.py:303
  164.2 6.6 %d_term.1 = bf16[4,4,32,1536]{3,2,1,0:T(8,128)(2,1)} custom-call(bf16[4,2,128,768]{3,2,1,0:T(8,128)(2,1)} %bitcast.38, bf16[2,1536,576]{2,1,0:T(8,128)(2,1)} %copy.32.w_ref), custom_call_target="tpu_custom_call" | custom-call | tf_op jit(solution)/shard_map/d_term/pallas_call | solution.py:275
  171.0 4.2 %head_term.1 = bf16[4,4,32,1536]{3,2,1,0:T(8,128)(2,1)} custom-call(bf16[4,2,128,768]{3,2,1,0:T(8,128)(2,1)} %bitcast.39, bf16[2,192,1536]{2,1,0:T(8,128)(2,1)} %bitcast.50), custom_call_target="tpu_custom_call" | custom-call | tf_op jit(solution)/shard_map/head_term/pallas_call | solution.py:275
  175.3 76.0 %all-reduce.3.cloned.1.call-done = (bf16[3,1536,384]{1,2,0:T(8,128)(2,1)}, bf16[384,1536]{1,0:T(8,128)(2,1)}) async-done(((bf16[3,1536,384]{1,2,0:T(8,128)(2,1)}, bf16[384,1536]{1,0:T(8,128)(2,1)}), (bf16[3,1536,384]{1,2,0:T(8,128)(2,1)}, bf16[384,1536]{1,0:T(8,128)(2,1)})) %all-reduce.3.cloned.1.call-update) | async-done | bytes 4718608 | tf_op jit(solution)/shard_map/psum | solution.py:368
  251.3 6.5 %copy.38 = f32[3,1536,384]{2,1,0:T(8,128)} copy(bf16[3,1536,384]{1,2,0:T(8,128)(2,1)} %get-tuple-element.26) | data formatting | bytes 10616832
  259.5 27.5 %reduce-scatter.5.cloned.1.call-done = bf16[1,4,32,1536]{3,2,1,0:T(8,128)(2,1)} async-done(((bf16[4,4,32,1536]{3,2,1,0:T(8,128)(2,1)}), bf16[1,4,32,1536]{3,2,1,0:T(8,128)(2,1)}) %reduce-scatter.5.cloned.1.call-update) | async-done | bytes 393232 | tf_op jit(solution)/shard_map/reduce_scatter | solution.py:364
  287.0 3.4 conv_gradient.1
  291.5 3.4 collective-permute-start.3
  294.9 4.0 %collective-permute-start.2 = (bf16[2,4,1,1536]{3,2,1,0:T(2,128)(2,1)S(1)}, bf16[2,4,1,1536]{3,2,1,0:T(2,128)(2,1)S(1)}, u32[]{:S(2)}, u32[]{:S(2)}) collective-permute-start(bf16[2,4,1,1536]{3,2,1,0:T(2,128)(2,1)S(1)} %get-tuple-element.28), channel_id=1, source_target_pairs={{0,1},{1,2},{2,3},{3,4},{4,5},{5,6},{6,7},{7,8},{8,9},{9,10},{10,1... | collective-permute-start | bytes 73736 | tf_op jit(solution)/shard_map/ppermute | solution.py:329
  298.9 26.7 %reduce-scatter.3.cloned.1.call-done = bf16[1,4,32,1536]{3,2,1,0:T(8,128)(2,1)} async-done(((bf16[4,4,32,1536]{3,2,1,0:T(8,128)(2,1)}), bf16[1,4,32,1536]{3,2,1,0:T(8,128)(2,1)}) %reduce-scatter.3.cloned.1.call-update) | async-done | bytes 393232 | tf_op jit(solution)/shard_map/reduce_scatter | solution.py:366
  329.1 11.1 %encoder_backward.1 = bf16[256,768]{1,0:T(8,128)(2,1)} custom-call(bf16[2,4,34,1536]{3,2,1,0:T(8,128)(2,1)} %pad_maximum_fusion.d_ref, bf16[5,768,1536]{2,1,0:T(8,128)(2,1)} %w_ref.3), custom_call_target="tpu_custom_call" | custom-call | tf_op jit(solution)/shard_map/encoder_backward/pallas_call | solution.py:151
  (36 shorter events, 16.3 us)
Async XLA Ops:
  7.2 10.4 %copy-start.4 = (f32[1536]{0:T(1024)S(1)}, f32[1536]{0:T(1024)}, u32[]{:S(2)}) copy-start(f32[1536]{0:T(1024)} %param.8) | copy-start | bytes 18436
  7.2 38.4 %all-gather.6.cloned.1.call-start = ((), (), s32[]{:S(2)}) async-start(), calls=%async_computation.7 | async-start | bytes 1966080 | tf_op jit(solution)/shard_map/all_gather | solution.py:344
  9.1 74.7 %all-gather.4.cloned.1.call-start = ((), (), s32[]{:S(2)}) async-start(), calls=%async_computation.4 | async-start | bytes 1966080 | tf_op jit(solution)/shard_map/all_gather | solution.py:348
  10.2 8.0 %collective-permute-start.1 = (bf16[2,4,1,768]{3,2,1,0:T(2,128)(2,1)S(1)}, bf16[2,4,1,768]{3,2,1,0:T(2,128)(2,1)S(1)}, u32[]{:S(2)}, u32[]{:S(2)}) collective-permute-start(bf16[2,4,1,768]{3,2,1,0:T(2,128)(2,1)S(1)} %get-tuple-element.33), channel_id=1, source_target_pairs={{1,0},{2,1},{3,2},{4,3},{5,4},{6,5},{7,6},{8,7},{9,8},{10,9},{11,1... | collective-permute-start | bytes 36872 | tf_op jit(solution)/shard_map/ppermute | solution.py:330
  12.6 6.5 %collective-permute-start = (bf16[2,4,1,768]{3,2,1,0:T(2,128)(2,1)S(1)}, bf16[2,4,1,768]{3,2,1,0:T(2,128)(2,1)S(1)}, u32[]{:S(2)}, u32[]{:S(2)}) collective-permute-start(bf16[2,4,1,768]{3,2,1,0:T(2,128)(2,1)S(1)} %get-tuple-element.32), channel_id=1, source_target_pairs={{0,1},{1,2},{2,3},{3,4},{4,5},{5,6},{6,7},{7,8},{8,9},{9,10},{10,1... | collective-permute-start | bytes 36872 | tf_op jit(solution)/shard_map/ppermute | solution.py:329
  20.0 10.0 %copy-start.1 = (bf16[3,1536,384]{2,1,0:T(8,128)(2,1)S(1)}, bf16[3,1536,384]{2,1,0:T(8,128)(2,1)}, u32[]{:S(2)}) copy-start(bf16[3,1536,384]{2,1,0:T(8,128)(2,1)} %param.9) | copy-start | bytes 10616836
  30.0 221.3 %all-reduce.3.cloned.1.call-start = ((), (), s32[]{:S(2)}) async-start(), calls=%async_computation.8 | async-start | bytes 9437184 | tf_op jit(solution)/shard_map/psum | solution.py:368
  164.1 122.9 %reduce-scatter.5.cloned.1.call-start = ((), (), s32[]{:S(2)}) async-start(), calls=%async_computation.6 | async-start | bytes 1966080 | tf_op jit(solution)/shard_map/reduce_scatter | solution.py:364
  170.8 154.9 %reduce-scatter.3.cloned.1.call-start = ((), (), s32[]{:S(2)}) async-start(), calls=%async_computation.5 | async-start | bytes 1966080 | tf_op jit(solution)/shard_map/reduce_scatter | solution.py:366
  251.3 6.5 %copy-start.3 = (bf16[384,1536]{1,0:T(8,128)(2,1)S(1)}, bf16[384,1536]{1,0:T(8,128)(2,1)}, u32[]{:S(2)}) copy-start(bf16[384,1536]{1,0:T(8,128)(2,1)} %get-tuple-element.27) | copy-start | bytes 3538948
  259.5 66.1 %copy-start.2 = (bf16[128,1536]{1,0:T(8,128)(2,1)S(1)}, bf16[128,1536]{1,0:T(8,128)(2,1)}, u32[]{:S(2)}) copy-start(bf16[128,1536]{1,0:T(8,128)(2,1)} %get-tuple-element.9.skip_ref) | copy-start | bytes 1179652
  290.4 37.5 %copy-start = (bf16[2,128,1536]{2,1,0:T(8,128)(2,1)S(1)}, bf16[2,128,1536]{2,1,0:T(8,128)(2,1)}, u32[]{:S(2)}) copy-start(bf16[2,128,1536]{2,1,0:T(8,128)(2,1)} %conv_gradient.1) | copy-start | bytes 2359300
  291.5 36.3 %collective-permute-start.3 = (bf16[2,4,1,1536]{3,2,1,0:T(2,128)(2,1)S(1)}, bf16[2,4,1,1536]{3,2,1,0:T(2,128)(2,1)S(1)}, u32[]{:S(2)}, u32[]{:S(2)}) collective-permute-start(bf16[2,4,1,1536]{3,2,1,0:T(2,128)(2,1)S(1)} %get-tuple-element.29), channel_id=1, source_target_pairs={{1,0},{2,1},{3,2},{4,3},{5,4},{6,5},{7,6},{8,7},{9,8},{10,9},{11,1... | collective-permute-start | bytes 73736 | tf_op jit(solution)/shard_map/ppermute | solution.py:330
  294.9 32.9 %collective-permute-start.2 = (bf16[2,4,1,1536]{3,2,1,0:T(2,128)(2,1)S(1)}, bf16[2,4,1,1536]{3,2,1,0:T(2,128)(2,1)S(1)}, u32[]{:S(2)}, u32[]{:S(2)}) collective-permute-start(bf16[2,4,1,1536]{3,2,1,0:T(2,128)(2,1)S(1)} %get-tuple-element.28), channel_id=1, source_target_pairs={{0,1},{1,2},{2,3},{3,4},{4,5},{5,6},{6,7},{7,8},{8,9},{9,10},{10,1... | collective-permute-start | bytes 73736 | tf_op jit(solution)/shard_map/ppermute | solution.py:329
Sparse Core Ops, SparseCore 0:
  9.6 35.9 all-gather.5
  47.7 36.0 all-gather.3
  164.3 86.9 all-reduce.2
  253.6 33.3 reduce-scatter.4
  289.3 36.3 reduce-scatter.2

commit v2 on v0

--- a/solution.py
+++ b/solution.py
@@ -1,10 +1,562 @@
+import functools
+
 import jax
 import jax.numpy as jnp
 from jax import lax
+from jax.experimental import pallas as pl
+from jax.experimental.pallas import tpu as pltpu
 from jax.sharding import PartitionSpec as P
 
 DH = 192
 KW = 5
+VMEM_LIMIT = 56 * 1024 * 1024
+BF = jnp.bfloat16
+F32 = jnp.float32
+
+
+def params():
+    return pltpu.CompilerParams(vmem_limit_bytes=VMEM_LIMIT)
+
+
+def dot(a, b, contract):
+    return lax.dot_general(a, b, (contract, ((), ())), preferred_element_type=F32)
+
+
+NN = ((1,), (0,))
+NT = ((1,), (1,))
+TN = ((0,), (0,))
+
+
+def whole(shape):
+    return pl.BlockSpec(shape, lambda *_: (0,) * len(shape))
+
+
+SCALARS = pl.BlockSpec(memory_space=pltpu.SMEM)
+
+
+def wrapped(value, size):
+    return jnp.where(value < 0, value + size, jnp.where(value >= size, value - size, value))
+
+
+def shifted(ref, start, rows):
+    seqs = ref.shape[1]
+    parts = []
+    for parity in range(2):
+        place = parity + start
+        wide = ref[place % 2].astype(F32)[:, place // 2 : place // 2 + rows, :]
+        parts.append(wide.reshape(seqs * rows, ref.shape[3]))
+    return jnp.concatenate(parts, axis=0).astype(BF)
+
+
+def conv_kernel(at_ref, x_ref, w_ref, gain_ref, skip_ref, slope_ref, normed_ref, acc):
+    step = pl.program_id(0)
+    rows = x_ref.shape[2] - 2
+    seqs = x_ref.shape[1]
+    half = acc.shape[0] // 2
+    for tap in range(KW):
+
+        @pl.when(step == tap)
+        def _():
+            term = dot(shifted(x_ref, tap, rows), w_ref[0], NN)
+            if tap == 0:
+                acc[...] = term
+            else:
+                acc[...] += term
+
+    @pl.when(step == KW - 1)
+    def _():
+        root = 0.7978845608028654
+        total = None
+        for parity in range(2):
+            x = acc[parity * half : (parity + 1) * half, :]
+            square = x * x
+            t = jnp.tanh(root * (x + 0.044715 * (square * x)))
+            left = 0.5 * (1.0 + t)
+            act = x * left
+            slope = left + (0.5 * root) * x * (1.0 - t * t) * (1.0 + (3 * 0.044715) * square)
+            slope_ref[parity] = slope.reshape(slope_ref.shape[1:])
+            total = act if total is None else total + act
+        skip = (0.5 * total).astype(BF)
+        skip_ref[...] = skip.reshape(skip_ref.shape)
+        wide = skip.astype(F32)
+        inv = lax.rsqrt(jnp.mean(wide * wide, axis=-1, keepdims=True) + 1e-06)
+        normed = (wide * inv * gain_ref[...]).astype(BF)
+        for b in range(seqs):
+            normed_ref[wrapped(b - at_ref[0], seqs)] = normed[b * rows : (b + 1) * rows]
+
+
+def encoder(at, padded, conv_weight, norm_gain):
+    _, seqs, rows2, c_in = padded.shape
+    rows = rows2 - 2
+    width = conv_weight.shape[2]
+    shape = (seqs, rows, width)
+    return pl.pallas_call(
+        conv_kernel,
+        grid=(KW,),
+        in_specs=[
+            SCALARS,
+            whole(padded.shape),
+            pl.BlockSpec((1, c_in, width), lambda k: (k, 0, 0)),
+            whole((1, width)),
+        ],
+        out_specs=[whole(shape), whole((2,) + shape), whole(shape)],
+        out_shape=[
+            jax.ShapeDtypeStruct(shape, BF),
+            jax.ShapeDtypeStruct((2,) + shape, F32),
+            jax.ShapeDtypeStruct(shape, BF),
+        ],
+        scratch_shapes=[pltpu.VMEM((2 * seqs * rows, width), F32)],
+        compiler_params=params(),
+        name="encoder_forward",
+    )(at, padded, conv_weight, norm_gain.reshape(1, width))
+
+
+def d_conv_body(seqs, at_ref, *refs):
+    dn_refs = refs[:seqs]
+    skip_ref, grad_ref, gain_ref, slope_ref, out_ref = refs[seqs:]
+    for slot in range(seqs):
+        b = wrapped(at_ref[0] + slot, seqs)
+        wide = skip_ref[b].astype(F32)
+        inv = lax.rsqrt(jnp.mean(wide * wide, axis=-1, keepdims=True) + 1e-06)
+        unit = wide * inv
+        scaled = dn_refs[slot][...].astype(F32) * gain_ref[...]
+        d_skip = grad_ref[b].astype(F32) + inv * (
+            scaled - unit * jnp.mean(scaled * unit, axis=-1, keepdims=True)
+        )
+        d_act = 0.5 * d_skip
+        for parity in range(2):
+            out_ref[parity, b] = (slope_ref[parity, b] * d_act).astype(BF)
+
+
+def conv_gradient(at, d_normed, skip, grad, norm_gain, slope):
+    seqs = len(d_normed)
+    vmem = pl.BlockSpec(memory_space=pltpu.VMEM)
+    return pl.pallas_call(
+        functools.partial(d_conv_body, seqs),
+        in_specs=[SCALARS] + [vmem] * (seqs + 4),
+        out_specs=vmem,
+        out_shape=jax.ShapeDtypeStruct(slope.shape, BF),
+        compiler_params=params(),
+        name="conv_gradient",
+    )(at, *d_normed, skip, grad, norm_gain.reshape(1, -1), slope)
+
+
+def mixed_body(seqs, at_ref, *refs):
+    skip_ref, out_ref = refs[seqs:]
+    for slot in range(seqs):
+        b = wrapped(at_ref[0] + slot, seqs)
+        out_ref[b] = (skip_ref[b].astype(F32) + refs[slot][...].astype(F32)).astype(BF)
+
+
+def mixed_call(at, terms, skip):
+    seqs = len(terms)
+    vmem = pl.BlockSpec(memory_space=pltpu.VMEM)
+    return pl.pallas_call(
+        functools.partial(mixed_body, seqs),
+        in_specs=[SCALARS] + [vmem] * (seqs + 1),
+        out_specs=vmem,
+        out_shape=jax.ShapeDtypeStruct(skip.shape, BF),
+        compiler_params=params(),
+        name="mixed_sum",
+    )(at, *terms, skip)
+
+
+def conv_back_kernel(d_ref, w_ref, out_ref, acc):
+    step = pl.program_id(0)
+    rows = d_ref.shape[2] - 2
+    for tap in range(KW):
+
+        @pl.when(step == tap)
+        def _():
+            term = dot(shifted(d_ref, KW - 1 - tap, rows), w_ref[0], NT)
+            if tap == 0:
+                acc[...] = term
+            elif tap < KW - 1:
+                acc[...] += term
+            else:
+                out_ref[...] = (acc[...] + term).astype(BF)
+
+
+def conv_back(d_pad, conv_weight):
+    _, seqs, rows2, width = d_pad.shape
+    c_in = conv_weight.shape[1]
+    flat = 2 * seqs * (rows2 - 2)
+    return pl.pallas_call(
+        conv_back_kernel,
+        grid=(KW,),
+        in_specs=[
+            whole(d_pad.shape),
+            pl.BlockSpec((1, c_in, width), lambda k: (k, 0, 0)),
+        ],
+        out_specs=whole((flat, c_in)),
+        out_shape=jax.ShapeDtypeStruct((flat, c_in), BF),
+        scratch_shapes=[pltpu.VMEM((flat, c_in), F32)],
+        compiler_params=params(),
+        name="encoder_backward",
+    )(d_pad, conv_weight)
+
+
+def product_kernel(head_ref, x_ref, w_ref, out_ref, *, contract):
+    del head_ref
+    out_ref[...] = dot(x_ref[...], w_ref[0], contract).astype(BF)
+
+
+def head_product(head, x, weight, contract, name):
+    columns = weight.shape[2] if contract == NN else weight.shape[1]
+    rows, width = x.shape
+    return pl.pallas_call(
+        functools.partial(product_kernel, contract=contract),
+        grid_spec=pltpu.PrefetchScalarGridSpec(
+            num_scalar_prefetch=1,
+            grid=(1,),
+            in_specs=[
+                pl.BlockSpec((rows, width), lambda i, head: (0, 0)),
+                pl.BlockSpec((1,) + weight.shape[1:], lambda i, head: (head[0], 0, 0)),
+            ],
+            out_specs=pl.BlockSpec((rows, columns), lambda i, head: (0, 0)),
+        ),
+        out_shape=jax.ShapeDtypeStruct((rows, columns), BF),
+        compiler_params=params(),
+        name=name,
+    )(head, x, weight)
+
+
+def attention_kernel(qa_ref, qb_ref, da_ref, db_ref, oa_ref, ob_ref, k_all, v_all, dk_acc, dv_acc, *, block):
+    scale = DH ** (-0.5)
+    half = qa_ref.shape[0]
+    for place, ref in enumerate((qa_ref, qb_ref)):
+        rows = pl.ds(place * half, half)
+        k_all[rows, :] = ref[:, DH : 2 * DH]
+        v_all[rows, :] = ref[:, 2 * DH : 3 * DH]
+    k = k_all[...]
+    v = v_all[...]
+    for place, (q_ref, d_ref, out_ref) in enumerate(
+        ((qa_ref, da_ref, oa_ref), (qb_ref, db_ref, ob_ref))
+    ):
+        for start in range(0, half, block):
+            rows = pl.ds(start, block)
+            q = q_ref[rows, 0:DH]
+            d_o = d_ref[rows, :]
+            s = dot(q, k, NT) * scale
+            e = jnp.exp(s - jnp.max(s, axis=-1, keepdims=True))
+            p = e * (1.0 / jnp.sum(e, axis=-1, keepdims=True))
+            p_b = p.astype(BF)
+            o = dot(p_b, v, NN)
+            delta = jnp.sum(d_o.astype(F32) * o, axis=-1, keepdims=True)
+            d_p = dot(d_o, v, NT)
+            ds = (p * (d_p - delta)).astype(BF)
+            dq = scale * dot(ds, k, NN)
+            dk = dot(ds, q, TN)
+            dv = dot(p_b, d_o, TN)
+            if place == 0 and start == 0:
+                dk_acc[...] = dk
+                dv_acc[...] = dv
+            else:
+                dk_acc[...] += dk
+                dv_acc[...] += dv
+            out_ref[rows, 0:DH] = o.astype(BF)
+            out_ref[rows, DH : 2 * DH] = dq.astype(BF)
+    for place, out_ref in enumerate((oa_ref, ob_ref)):
+        rows = pl.ds(place * half, half)
+        out_ref[:, 2 * DH : 3 * DH] = (scale * dk_acc[rows, :]).astype(BF)
+        out_ref[:, 3 * DH : 4 * DH] = dv_acc[rows, :].astype(BF)
+
+
+def attention(qkv_a, qkv_b, d_a, d_b):
+    half = qkv_a.shape[0]
+    shape = jax.ShapeDtypeStruct((half, 4 * DH), BF)
+    return pl.pallas_call(
+        functools.partial(attention_kernel, block=min(256, half)),
+        out_shape=[shape, shape],
+        scratch_shapes=[
+            pltpu.VMEM((2 * half, DH), BF),
+            pltpu.VMEM((2 * half, DH), BF),
+            pltpu.VMEM((2 * half, DH), F32),
+            pltpu.VMEM((2 * half, DH), F32),
+        ],
+        compiler_params=params(),
+        name="attention",
+    )(qkv_a, qkv_b, d_a, d_b)
+
+
+def term_kernel(head_ref, a_ref, b_ref, w_ref, out_ref, acc, *, first, last, contract):
+    step = pl.program_id(0)
+    groups = out_ref.shape[0]
+
+    @pl.when(step == 0)
+    def _():
+        acc[...] = dot(a_ref[:, first:last], w_ref[0], contract)
+
+    @pl.when(step == 1)
+    def _():
+        total = acc[...] + dot(b_ref[:, first:last], w_ref[0], contract)
+        total = total.astype(BF).reshape(out_ref.shape)
+        for z in range(groups):
+            out_ref[wrapped(z - head_ref[1], groups)] = total[z]
+
+
+def pair_term(place, mine, got, weight, shape, first, last, contract, name):
+    half, full = mine.shape
+    return pl.pallas_call(
+        functools.partial(term_kernel, first=first, last=last, contract=contract),
+        grid_spec=pltpu.PrefetchScalarGridSpec(
+            num_scalar_prefetch=1,
+            grid=(2,),
+            in_specs=[
+                pl.BlockSpec((half, full), lambda i, at: (0, 0)),
+                pl.BlockSpec((half, full), lambda i, at: (0, 0)),
+                pl.BlockSpec(
+                    (1,) + weight.shape[1:],
+                    lambda i, at: (jnp.where(i == 0, at[0], 1 - at[0]), 0, 0),
+                ),
+            ],
+            out_specs=pl.BlockSpec(shape, lambda i, at: (0, 0, 0, 0)),
+            scratch_shapes=[pltpu.VMEM((half, shape[-1]), F32)],
+        ),
+        out_shape=jax.ShapeDtypeStruct(shape, BF),
+        compiler_params=params(),
+        name=name,
+    )(place, mine, got, weight)
+
+
+def place_kernel(at_ref, *refs):
+    step = pl.program_id(0)
+    del at_ref
+    for slot, ref in enumerate(refs[:-1]):
+
+        @pl.when(step == slot)
+        def _():
+            refs[-1][...] = ref[...]
+
+
+def in_order(at, slots, name):
+    count = len(slots)
+    rows, width = slots[0].shape
+    return pl.pallas_call(
+        place_kernel,
+        grid_spec=pltpu.PrefetchScalarGridSpec(
+            num_scalar_prefetch=1,
+            grid=(count,),
+            in_specs=[pl.BlockSpec((rows, width), lambda q, at: (0, 0))] * count,
+            out_specs=pl.BlockSpec(
+                (rows, width), lambda q, at: (lax.rem(at[0] - q + count, count), 0)
+            ),
+        ),
+        out_shape=jax.ShapeDtypeStruct((count * rows, width), slots[0].dtype),
+        compiler_params=params(),
+        name=name,
+    )(at, *slots)
+
+
+def sum_kernel(*refs):
+    total = refs[0][...].astype(F32)
+    for ref in refs[1:-1]:
+        total = total + ref[...].astype(F32)
+    refs[-1][...] = total.astype(BF)
+
+
+def summed(parts, name):
+    return pl.pallas_call(
+        sum_kernel,
+        out_shape=jax.ShapeDtypeStruct(parts[0].shape, BF),
+        compiler_params=params(),
+        name=name,
+    )(*parts)
+
+
+def weight_kernel(at_ref, xa_ref, xb_ref, ga_ref, gb_ref, ra_ref, rb_ref, out_ref):
+    del at_ref
+    qkv = dot(xa_ref[...], ra_ref[:, DH:], TN) + dot(xb_ref[...], rb_ref[:, DH:], TN)
+    out = dot(ga_ref[...], ra_ref[:, :DH], TN) + dot(gb_ref[...], rb_ref[:, :DH], TN)
+    out_ref[0, :, : 3 * DH] = qkv.astype(BF)
+    out_ref[0, :, 3 * DH :] = out.astype(BF)
+
+
+def weight_gradients(at, xa, xb, ga, gb, ra, rb, seqs):
+    half, width = xa.shape
+    chunk = width // seqs
+    full = ra.shape[1]
+    column = pl.BlockSpec((half, chunk), lambda r, at: (0, lax.rem(r + at[0], seqs)))
+    rest = pl.BlockSpec((half, full), lambda r, at: (0, 0))
+    return pl.pallas_call(
+        weight_kernel,
+        grid_spec=pltpu.PrefetchScalarGridSpec(
+            num_scalar_prefetch=1,
+            grid=(seqs,),
+            in_specs=[column] * 4 + [rest] * 2,
+            out_specs=pl.BlockSpec((1, chunk, full), lambda r, at: (r, 0, 0)),
+        ),
+        out_shape=jax.ShapeDtypeStruct((seqs, chunk, full), BF),
+        compiler_params=params(),
+        name="weight_gradients",
+    )(at, xa, xb, ga, gb, ra, rb)
+
+
+def unpack_kernel(at_ref, *refs):
+    seqs = (len(refs) - 2) // 2
+    qkv_ref, out_ref = refs[-2:]
+    step = pl.program_id(0)
+    first_head = at_ref[1] == 0
+    for slot in range(seqs):
+
+        @pl.when(step == slot)
+        def _():
+            mine = refs[slot][...].astype(F32)
+            other = refs[seqs + slot][...].astype(F32)
+            low = jnp.where(first_head, mine, other)
+            high = jnp.where(first_head, other, mine)
+            for i in range(3):
+                columns = slice(i * DH, (i + 1) * DH)
+                qkv_ref[i] = jnp.concatenate([low[:, columns], high[:, columns]], axis=1)
+            out_ref[:DH, :] = low[:, 3 * DH :].T
+            out_ref[DH:, :] = high[:, 3 * DH :].T
+
+
+def unpack_weights(at, mine, other):
+    seqs = len(mine)
+    chunk, full = mine[0].shape
+    width = chunk * seqs
+    local = 2 * DH
+
+    def place(r, at):
+        return lax.rem(at[0] - r + seqs, seqs)
+
+    return pl.pallas_call(
+        unpack_kernel,
+        grid_spec=pltpu.PrefetchScalarGridSpec(
+            num_scalar_prefetch=1,
+            grid=(seqs,),
+            in_specs=[pl.BlockSpec((chunk, full), lambda r, at: (0, 0))] * (2 * seqs),
+            out_specs=[
+                pl.BlockSpec((3, chunk, local), lambda r, at: (0, place(r, at), 0)),
+                pl.BlockSpec((local, chunk), lambda r, at: (0, place(r, at))),
+            ],
+        ),
+        out_shape=[
+            jax.ShapeDtypeStruct((3, width, local), F32),
+            jax.ShapeDtypeStruct((local, width), F32),
+        ],
+        compiler_params=params(),
+        name="weight_outputs",
+    )(at, *mine, *other)
+
+
+def neighbour_edges(pairs):
+    axes = ("seq", "head")
+    count = lax.axis_size(axes)
+    forward = [(i, i + 1) for i in range(count - 1)]
+    backward = [(target, source) for source, target in forward]
+    low = lax.ppermute(pairs[:, :, -1:, :], axes, forward)
+    high = lax.ppermute(pairs[:, :, :1, :], axes, backward)
+    return jnp.concatenate([low, pairs, high], axis=2)
+
+
+def send_chip(x, step, heads):
+    count = lax.axis_size("seq")
+    return lax.ppermute(x, "seq", [(s, (s + step * heads) % count) for s in range(count)])
+
+
+def send_z(x, step):
+    count = lax.axis_size("head")
+    return lax.ppermute(x, "head", [(z, (z + step) % count) for z in range(count)])
+
+
+def swap_heads(x):
+    count = lax.axis_size("seq")
+    return lax.ppermute(x, "seq", [(s, s + 1 - 2 * (s % 2)) for s in range(count)])
+
+
+def unit_body(enc_in, conv_weight, norm_gain, w_qkv, w_out, grad_out):
+    rows = enc_in.shape[0] // 2
+    seqs = enc_in.shape[1]
+    width = conv_weight.shape[2]
+    local = w_qkv.shape[2]
+    heads = local // DH
+    groups = lax.axis_size("head")
+    half = groups * seqs * rows
+    place = lax.axis_index("seq")
+    own_seq = (place // heads).astype(jnp.int32)
+    own_head = (place % heads).astype(jnp.int32)
+    own_z = lax.axis_index("head").astype(jnp.int32)
+    zero = jnp.zeros((), jnp.int32)
+    at = jnp.stack([own_seq, own_head])
+    head_mine = own_head.reshape(1)
+    head_other = (1 - own_head).reshape(1)
+
+    def to_chips(slots):
+        return [slots[r] if r == 0 else send_chip(slots[r], r, heads) for r in range(seqs)]
+
+    def from_chips(slots):
+        return [slots[r] if r == 0 else send_chip(slots[r], -r, heads) for r in range(seqs)]
+
+    grad = jnp.transpose(grad_out, (1, 0, 2))
+    grad_slots = [
+        lax.dynamic_index_in_dim(grad, (own_seq + r) % seqs, 0, keepdims=False)
+        for r in range(seqs)
+    ]
+    grad_slab = jnp.concatenate(to_chips(grad_slots), axis=0)
+    grad_rows = in_order(
+        own_z.reshape(1),
+        [grad_slab if q == 0 else send_z(grad_slab, q) for q in range(groups)],
+        "grad_rows",
+    )
+
+    pairs = jnp.transpose(enc_in.reshape(rows, 2, seqs, enc_in.shape[2]), (1, 2, 0, 3))
+    skip, slope, normed = encoder(at, neighbour_edges(pairs), conv_weight, norm_gain)
+    normed_slab = jnp.concatenate(to_chips([normed[r] for r in range(seqs)]), axis=0)
+    normed_rows = lax.all_gather(normed_slab, "head", axis=0, tiled=True)
+
+    w_pack = jnp.transpose(w_qkv.reshape(3, width, heads, DH), (2, 1, 0, 3))
+    w_pack = w_pack.reshape(heads, width, 3 * DH)
+    w_rows = w_out.reshape(heads, DH, width)
+    d_got = swap_heads(head_product(head_other, grad_rows, w_rows, NT, "d_o_other"))
+    d_mine = head_product(head_mine, grad_rows, w_rows, NT, "d_o_own")
+    qkv_got = swap_heads(head_product(head_other, normed_rows, w_pack, NN, "qkv_other"))
+    qkv_mine = head_product(head_mine, normed_rows, w_pack, NN, "qkv_own")
+    result_mine, result_other = attention(qkv_mine, qkv_got, d_mine, d_got)
+    result_got = swap_heads(result_other)
+
+    shape = (groups, seqs, rows, width)
+    plain = jnp.stack([own_head, zero])
+    d_term = pair_term(
+        plain, result_mine, result_got, w_pack, shape, DH, 4 * DH, NT, "d_term"
+    )
+    d_normed = lax.psum_scatter(d_term, "head", scatter_dimension=0, tiled=False)
+    d_normed = from_chips([d_normed[r] for r in range(seqs)])
+
+    turned = jnp.stack([own_head, own_z])
+    head_term = pair_term(
+        turned, result_mine, result_got, w_rows, shape, 0, DH, NN, "head_term"
+    )
+    head_sum = summed(
+        [head_term[q] if q == 0 else send_z(head_term[q], q) for q in range(groups)], "head_sum"
+    )
+    head_sum = from_chips([head_sum[r] for r in range(seqs)])
+    mixed = mixed_call(at, head_sum, skip)
+
+    part = weight_gradients(
+        own_seq.reshape(1),
+        normed_rows,
+        swap_heads(normed_rows),
+        grad_rows,
+        swap_heads(grad_rows),
+        result_mine,
+        result_other,
+        seqs,
+    )
+    chunk = summed(to_chips([part[r] for r in range(seqs)]), "weight_sum")
+    chunks = [chunk if r == 0 else send_chip(chunk, r, heads) for r in range(seqs)]
+    grad_w_qkv, grad_w_out = unpack_weights(at, chunks, [swap_heads(c) for c in chunks])
+
+    d_conv = conv_gradient(at, d_normed, skip, grad, norm_gain, slope)
+    grad_input = conv_back(neighbour_edges(d_conv), conv_weight)
+    grad_input = jnp.transpose(grad_input.reshape(2, seqs, rows, -1), (2, 0, 1, 3))
+    return (
+        jnp.transpose(mixed, (1, 0, 2)),
+        grad_input.reshape(enc_in.shape),
+        grad_w_qkv,
+        grad_w_out,
+    )
 
 
 def padded_2(block, sides, width):
@@ -20,7 +572,7 @@
     return block
 
 
-def body(enc_in, conv_weight, norm_gain, w_qkv, w_out, grad_out):
+def gathered_body(enc_in, conv_weight, norm_gain, w_qkv, w_out, grad_out):
     fine_rows = enc_in.shape[0]
     slab_rows = fine_rows // 2
     seq_count = enc_in.shape[1]
@@ -145,6 +697,13 @@
     return (mixed, grad_input.astype(jnp.bfloat16), grad_w_qkv, grad_w_out)
 
 
+def body(enc_in, conv_weight, norm_gain, w_qkv, w_out, grad_out):
+    heads = w_qkv.shape[2] // DH
+    fits = heads == 2 and enc_in.shape[1] * heads == lax.axis_size("seq")
+    chosen = unit_body if fits else gathered_body
+    return chosen(enc_in, conv_weight, norm_gain, w_qkv, w_out, grad_out)
+
+
 def solution(mesh):
     return jax.shard_map(
         body,

time: 499 us -> 308 us (0.62)
  waiting for transfers between devices: 325 us -> 105 us
  Pallas kernels: 0 us -> 82.2 us
  matrix products: 75.6 us -> 0 us
  starting transfers between devices: 12.6 us -> 55.9 us
  other arithmetic: 16.1 us -> 5.81 us
  local copies, waits for them, and re-layouts: 48.6 us -> 40.3 us
    pallas_call x0 -> x16, Pallas kernels: none -> 82.2 us  [the longest x4 14.1 us: head_product(): pl.pallas_call(functools.partial(product_kernel, contract=contract), grid...]
    psum x1 -> x0, waiting for transfers between devices: 78.2 us -> none  [body(): lax.psum(part_w_qkv.astype(jnp.bfloat16), 'seq').astype(jnp.float32)]
    all_gather x4 -> x1, waiting for transfers between devices: 113 us -> 39.5 us  [unit_body(): normed_rows = lax.all_gather(normed_slab, 'head', axis=0, tiled=True)]
    unnamed x11 -> x2, waiting for transfers between devices: 71.5 us -> 0.03 us
    dot_general x21 -> x0, matrix products: 70 us -> none  [the longest x5 14.3 us: body(): jnp.einsum('tbi,io->tbo', padded[offset:offset + fine_rows], conv_weight[...]
    ppermute x4 -> x37, waiting for transfers between devices: 0.31 us -> 65.7 us  [the longest x6 32.2 us: send_z(): lax.ppermute(x, 'head', [(z, (z + step) % count) for z in range(count)])]
    reduce_scatter x2 -> x1, waiting for transfers between devices: 61.8 us -> 0.01 us  [unit_body(): lax.psum_scatter(d_term, 'head', scatter_dimension=0, tiled=False)]
    ppermute x4 -> x37, starting transfers between devices: 11.8 us -> 55.8 us  [the longest x18 22.6 us: send_chip(): lax.ppermute(x, 'seq', [(s, (s + step * heads) % count) for s in range(co...]
  transfers between devices with their start and end apart: 13 -> 39, of which waited for: 10 -> 11; matrix products, arithmetic and copies ran while one was open for 19% -> 10% of each run, Pallas kernels for 0% -> 16%
where the time goes in v2:
time: 308 us; the launch traced here: 304 us
  waiting for transfers between devices  105 us (34%)
  Pallas kernels  82.2 us (27%)
  starting transfers between devices  55.9 us (18%)
  local copies, waits for them, and re-layouts  40.3 us (13%)
  between operations  14.4 us (5%)
  other arithmetic  5.81 us (2%)
    all_gather x1, waiting for transfers between devices, unit_body(): normed_rows = lax.all_gather(normed_slab, 'head', axis=0, tiled=True)  39.5 us
    ppermute x6, waiting for transfers between devices, send_z(): lax.ppermute(x, 'head', [(z, (z + step) % count) for z in range(count)])  32.2 us
    ppermute x18, waiting for transfers between devices, send_chip(): lax.ppermute(x, 'seq', [(s, (s + step * heads) % count) for s in range(co...  32 us
    ppermute x18, starting transfers between devices, send_chip(): lax.ppermute(x, 'seq', [(s, (s + step * heads) % count) for s in range(co...  22.6 us
    ppermute x6, starting transfers between devices, send_z(): lax.ppermute(x, 'head', [(z, (z + step) % count) for z in range(count)])  16.7 us
    unnamed x65, local copies, waits for them, and re-layouts  16.3 us
    pallas_call x4, Pallas kernels, head_product(): pl.pallas_call(functools.partial(product_kernel, contract=contract), grid...  14.1 us
    pallas_call x2, Pallas kernels, pair_term(): pl.pallas_call(functools.partial(term_kernel, first=first, last=last, con...  11.5 us
  transfers between devices with their start and end apart: 39, of which 11 were waited for; matrix products, arithmetic and copies ran while one was open for 10% of the time, Pallas kernels for 16%

profile of v2, /device:TPU:26, one launch (start us, length us, event | category | flops | bytes accessed | tf_op | source)
XLA Modules:
  0.0 303.9 jit_solution(13934567638061750166)
XLA Ops:
  10.7 5.0 %collective-permute-start = (bf16[2,4,1,768]{3,2,1,0:T(2,128)(2,1)S(1)}, bf16[2,4,1,768]{3,2,1,0:T(2,128)(2,1)S(1)}, u32[]{:S(2)}, u32[]{:S(2)}) collective-permute-start(bf16[2,4,1,768]{3,2,1,0:T(2,128)(2,1)S(1)} %get-tuple-element.58), channel_id=1, source_target_pairs={{0,1},{1,2},{2,3},{3,4},{4,5},{5,6},{6,7},{7,8},{8,9},{9,10},{10,1... | collective-permute-start | bytes 36872 | tf_op jit(solution)/shard_map/ppermute | solution.py:449
  18.5 9.7 %encoder_forward.1 = (bf16[4,32,1536]{2,1,0:T(8,128)(2,1)}, f32[2,4,32,1536]{3,2,1,0:T(8,128)}, bf16[4,32,1536]{2,1,0:T(8,128)(2,1)}) custom-call(s32[2]{0:T(128)} %pad_add_fusion.at_ref, bf16[2,4,34,768]{3,2,1,0:T(8,128)(2,1)} %pad_maximum_fusion.1.x_ref, bf16[5,768,1536]{2,1,0:T(8,128)(2,1)} %w_ref.3, f32[1,1536]{1,0:T(1,128)} %reshape.53.gain_ref.refs_6_), custom_call_target="tpu_custom_call" | custom-call | tf_op jit(solution)/shard_map/encoder_forward/pallas_call | solution.py:93
  45.6 3.7 %copy.28 = bf16[3,1536,384]{1,2,0:T(8,128)(2,1)} copy(bf16[3,1536,384]{2,1,0:T(8,128)(2,1)S(1)} %copy-done.3) | data formatting | bytes 7077888 | tf_op args[3]
  51.5 3.7 %copy.30.w_ref = bf16[2,1536,576]{2,1,0:T(8,128)(2,1)} copy(bf16[2,1536,576]{1,2,0:T(8,128)(2,1)S(1)} %bitcast.69) | data formatting | bytes 7077888 | tf_op jit(solution)/shard_map/reshape | solution.py:510
  56.3 4.0 %collective-permute-start.9 = (bf16[128,1536]{1,0:T(8,128)(2,1)S(1)}, bf16[128,1536]{1,0:T(8,128)(2,1)S(1)}, u32[]{:S(2)}, u32[]{:S(2)}) collective-permute-start(bf16[128,1536]{1,0:T(8,128)(2,1)S(1)} %pad_maximum_fusion.3.refs_0_), channel_id=1, source_target_pairs={{0,1},{1,2},{2,3},{3,0},{4,5},{5,6},{6,7},{7,4},{8,9},{9,10},{10,1... | collective-permute-start | bytes 1179656 | tf_op jit(solution)/shard_map/ppermute | solution.py:461
  61.0 39.5 %all-gather.2.cloned.1.call-done.x_ref.xa_ref = bf16[512,1536]{1,0:T(8,128)(2,1)} async-done(((bf16[128,1536]{1,0:T(8,128)(2,1)}), bf16[512,1536]{1,0:T(8,128)(2,1)}) %all-gather.2.cloned.1.call-update) | async-done | bytes 1572880 | tf_op jit(solution)/shard_map/all_gather | solution.py:507
  100.5 4.2 %qkv_other.1 = bf16[512,576]{1,0:T(8,128)(2,1)} custom-call(s32[1]{0:T(128)} %bitcast.12.head_ref, bf16[512,1536]{1,0:T(8,128)(2,1)} %all-gather.2.cloned.1.call-done.x_ref.xa_ref, bf16[2,1536,576]{2,1,0:T(8,128)(2,1)} %copy.30.w_ref), custom_call_target="tpu_custom_call" | custom-call | tf_op jit(solution)/shard_map/qkv_other/pallas_call | solution.py:207
  108.9 3.1 %grad_rows.1.x_ref.ga_ref = bf16[512,1536]{1,0:T(8,128)(2,1)} custom-call(s32[1]{0:T(128)} %bitcast.2.at_ref, bf16[128,1536]{1,0:T(8,128)(2,1)} %copy-done.7, bf16[128,1536]{1,0:T(8,128)(2,1)} %copy-done.19, bf16[128,1536]{1,0:T(8,128)(2,1)} %copy-done.20, bf16[128,1536]{1,0:T(8,128)(2,1)} %copy-done.21), custom_call_target="tpu_custom_call" | custom-call | tf_op jit(solution)/shard_map/grad_rows/pallas_call | solution.py:335
  111.9 2.8 d_o_other.1
  114.8 2.8 d_o_own.1.da_ref
  117.6 4.2 %qkv_own.1.qa_ref = bf16[512,576]{1,0:T(8,128)(2,1)} custom-call(s32[1]{0:T(128)} %bitcast.1.head_ref, bf16[512,1536]{1,0:T(8,128)(2,1)} %all-gather.2.cloned.1.call-done.x_ref.xa_ref, bf16[2,1536,576]{2,1,0:T(8,128)(2,1)} %copy.30.w_ref), custom_call_target="tpu_custom_call" | custom-call | tf_op jit(solution)/shard_map/qkv_own/pallas_call | solution.py:207
  123.6 8.9 %attention.1 = (bf16[512,768]{1,0:T(8,128)(2,1)}, bf16[512,768]{1,0:T(8,128)(2,1)}) custom-call(bf16[512,576]{1,0:T(8,128)(2,1)} %qkv_own.1.qa_ref, bf16[512,576]{1,0:T(8,128)(2,1)} %copy.37.qb_ref, bf16[512,192]{1,0:T(8,128)(2,1)} %d_o_own.1.da_ref, bf16[512,192]{1,0:T(8,128)(2,1)} %copy-done.24), custom_call_target="tpu_custom_call" | custom-call | tf_op jit(solution)/shard_map/attention/pallas_call | solution.py:268
  136.1 7.0 %d_term.1 = bf16[4,4,32,1536]{3,2,1,0:T(8,128)(2,1)} custom-call(s32[2]{0:T(128)} %pad_add_fusion.2.head_ref, bf16[512,768]{1,0:T(8,128)(2,1)} %get-tuple-element.12.a_ref.ra_ref, bf16[512,768]{1,0:T(8,128)(2,1)} %copy-done.4, bf16[2,1536,576]{2,1,0:T(8,128)(2,1)} %copy.30.w_ref), custom_call_target="tpu_custom_call" | custom-call | tf_op jit(solution)/shard_map/d_term/pallas_call | solution.py:300
  144.3 4.5 %head_term.1 = bf16[4,4,32,1536]{3,2,1,0:T(8,128)(2,1)} custom-call(s32[2]{0:T(128)} %pad_add_fusion.1.head_ref, bf16[512,768]{1,0:T(8,128)(2,1)} %get-tuple-element.12.a_ref.ra_ref, bf16[512,768]{1,0:T(8,128)(2,1)} %copy-done.4, bf16[2,192,1536]{2,1,0:T(8,128)(2,1)} %bitcast.73), custom_call_target="tpu_custom_call" | custom-call | tf_op jit(solution)/shard_map/head_term/pallas_call | solution.py:300
  153.4 8.2 %weight_gradients.1 = bf16[4,384,768]{2,1,0:T(8,128)(2,1)} custom-call(s32[1]{0:T(128)} %bitcast.at_ref, bf16[512,1536]{1,0:T(8,128)(2,1)} %all-gather.2.cloned.1.call-done.x_ref.xa_ref, bf16[512,1536]{1,0:T(8,128)(2,1)} %copy-done.6, bf16[512,1536]{1,0:T(8,128)(2,1)} %grad_rows.1.x_ref.ga_ref, bf16[512,1536]{1,0:T(8,128)(2,1)} %copy-done.5, ...), custom_call_target="tpu_custom_call" | custom-call | tf_op jit(solution)/shard_map/weight_gradients/pallas_call | solution.py:381
  169.6 7.2 %collective-permute-done.14.refs_1_ = bf16[4,32,1536]{2,1,0:T(8,128)(2,1)} collective-permute-done((bf16[4,32,1536]{2,1,0:T(8,128)(2,1)S(1)}, bf16[4,32,1536]{2,1,0:T(8,128)(2,1)}, u32[]{:S(2)}, u32[]{:S(2)}) %collective-permute-start.14) | collective-permute-done | bytes 393248 | tf_op jit(solution)/shard_map/ppermute | solution.py:461
  176.7 10.2 %collective-permute-start.16 = (bf16[4,32,1536]{2,1,0:T(8,128)(2,1)S(1)}, bf16[4,32,1536]{2,1,0:T(8,128)(2,1)S(1)}, u32[]{:S(2)}, u32[]{:S(2)}) collective-permute-start(bf16[4,32,1536]{2,1,0:T(8,128)(2,1)S(1)} %get-tuple-element.34), channel_id=1, source_target_pairs={{0,3},{1,0},{2,1},{3,2},{4,7},{5,4},{6,5},{7,6},{8,11},{9,8},{10,9... | collective-permute-start | bytes 1179656 | tf_op jit(solution)/shard_map/ppermute | solution.py:461
  187.0 23.2 %collective-permute-done.15.refs_2_ = bf16[4,32,1536]{2,1,0:T(8,128)(2,1)S(1)} collective-permute-done((bf16[4,32,1536]{2,1,0:T(8,128)(2,1)S(1)}, bf16[4,32,1536]{2,1,0:T(8,128)(2,1)S(1)}, u32[]{:S(2)}, u32[]{:S(2)}) %collective-permute-start.15) | collective-permute-done | bytes 393248 | tf_op jit(solution)/shard_map/ppermute | solution.py:461
  214.6 2.7 weight_sum.1.refs_0_
  225.2 24.3 %collective-permute-done.17.refs_1_ = bf16[32,1536]{1,0:T(8,128)(2,1)S(1)} collective-permute-done((bf16[32,1536]{1,0:T(8,128)(2,1)S(1)}, bf16[32,1536]{1,0:T(8,128)(2,1)S(1)}, u32[]{:S(2)}, u32[]{:S(2)}) %collective-permute-start.17) | collective-permute-done | bytes 98336 | tf_op jit(solution)/shard_map/ppermute | solution.py:456
  256.1 3.3 %conv_gradient.1 = bf16[2,4,32,1536]{3,2,1,0:T(8,128)(2,1)} custom-call(s32[2]{0:T(128)} %pad_add_fusion.at_ref, bf16[32,1536]{1,0:T(8,128)(2,1)} %get-tuple-element.45.refs_0_, bf16[32,1536]{1,0:T(8,128)(2,1)} %copy-done.28, bf16[32,1536]{1,0:T(8,128)(2,1)} %copy-done.29, bf16[32,1536]{1,0:T(8,128)(2,1)} %copy-done.30, ...), custom_call_target="tpu_custom_call" | custom-call | tf_op jit(solution)/shard_map/conv_gradient/pallas_call | solution.py:134
  266.0 5.4 %collective-permute-start.23 = (bf16[2,4,1,1536]{3,2,1,0:T(2,128)(2,1)S(1)}, bf16[2,4,1,1536]{3,2,1,0:T(2,128)(2,1)S(1)}, u32[]{:S(2)}, u32[]{:S(2)}) collective-permute-start(bf16[2,4,1,1536]{3,2,1,0:T(2,128)(2,1)S(1)} %get-tuple-element.38), channel_id=1, source_target_pairs={{0,1},{1,2},{2,3},{3,4},{4,5},{5,6},{6,7},{7,8},{8,9},{9,10},{10,1... | collective-permute-start | bytes 73736 | tf_op jit(solution)/shard_map/ppermute | solution.py:449
  277.5 7.7 %weight_outputs.1 = (f32[3,1536,384]{2,1,0:T(8,128)}, f32[384,1536]{1,0:T(8,128)}) custom-call(s32[2]{0:T(128)} %pad_add_fusion.at_ref, bf16[384,768]{1,0:T(8,128)(2,1)} %weight_sum.1.refs_0_, bf16[384,768]{1,0:T(8,128)(2,1)} %copy-done.9, bf16[384,768]{1,0:T(8,128)(2,1)} %copy-done.10, bf16[384,768]{1,0:T(8,128)(2,1)} %copy-done.11, ...), custom_call_target="tpu_custom_call" | custom-call | tf_op jit(solution)/shard_map/weight_outputs/pallas_call | solution.py:424
  286.5 8.5 %encoder_backward.1 = bf16[256,768]{1,0:T(8,128)(2,1)} custom-call(bf16[2,4,34,1536]{3,2,1,0:T(8,128)(2,1)} %pad_maximum_fusion.d_ref, bf16[5,768,1536]{2,1,0:T(8,128)(2,1)} %w_ref.3), custom_call_target="tpu_custom_call" | custom-call | tf_op jit(solution)/shard_map/encoder_backward/pallas_call | solution.py:184
  (159 shorter events, 85.3 us)
Async XLA Ops:
  7.2 93.4 %all-gather.2.cloned.1.call-start = ((), (), s32[]{:S(2)}) async-start(), calls=%async_computation.1 | async-start | bytes 1966080 | tf_op jit(solution)/shard_map/all_gather | solution.py:507
  38.4 184.5 %reduce-scatter.2.cloned.1.call-start = ((), (), s32[]{:S(2)}) async-start(), calls=%async_computation.2 | async-start | bytes 1966080 | tf_op jit(solution)/shard_map/reduce_scatter | solution.py:524
  42.1 13.1 %collective-permute-start.8 = (bf16[32,1536]{1,0:T(8,128)(2,1)}, bf16[32,1536]{1,0:T(8,128)(2,1)}, u32[]{:S(2)}, u32[]{:S(2)}) collective-permute-start(bf16[32,1536]{1,0:T(8,128)(2,1)} %get-tuple-element.51), channel_id=1, source_target_pairs={{0,24},{4,28},{8,0},{12,4},{16,8},{20,12},{24,16},{28,20},{1,25},{... | collective-permute-start | bytes 294920 | tf_op jit(solution)/shard_map/ppermute | solution.py:456
  56.3 49.9 %collective-permute-start.9 = (bf16[128,1536]{1,0:T(8,128)(2,1)S(1)}, bf16[128,1536]{1,0:T(8,128)(2,1)S(1)}, u32[]{:S(2)}, u32[]{:S(2)}) collective-permute-start(bf16[128,1536]{1,0:T(8,128)(2,1)S(1)} %pad_maximum_fusion.3.refs_0_), channel_id=1, source_target_pairs={{0,1},{1,2},{2,3},{3,0},{4,5},{5,6},{6,7},{7,4},{8,9},{9,10},{10,1... | collective-permute-start | bytes 1179656 | tf_op jit(solution)/shard_map/ppermute | solution.py:461
  60.4 47.6 %collective-permute-start.10 = (bf16[128,1536]{1,0:T(8,128)(2,1)S(1)}, bf16[128,1536]{1,0:T(8,128)(2,1)S(1)}, u32[]{:S(2)}, u32[]{:S(2)}) collective-permute-start(bf16[128,1536]{1,0:T(8,128)(2,1)S(1)} %pad_maximum_fusion.3.refs_0_), channel_id=1, source_target_pairs={{0,2},{1,3},{2,0},{3,1},{4,6},{5,7},{6,4},{7,5},{8,10},{9,11},{10,... | collective-permute-start | bytes 1179656 | tf_op jit(solution)/shard_map/ppermute | solution.py:461
  60.4 47.6 %collective-permute-start.11 = (bf16[128,1536]{1,0:T(8,128)(2,1)S(1)}, bf16[128,1536]{1,0:T(8,128)(2,1)S(1)}, u32[]{:S(2)}, u32[]{:S(2)}) collective-permute-start(bf16[128,1536]{1,0:T(8,128)(2,1)S(1)} %pad_maximum_fusion.3.refs_0_), channel_id=1, source_target_pairs={{0,3},{1,0},{2,1},{3,2},{4,7},{5,4},{6,5},{7,6},{8,11},{9,8},{10,9... | collective-permute-start | bytes 1179656 | tf_op jit(solution)/shard_map/ppermute | solution.py:461
  106.1 15.7 %collective-permute-start.5 = (bf16[512,576]{0,1:T(8,128)(2,1)S(1)}, bf16[512,576]{0,1:T(8,128)(2,1)S(1)}, u32[]{:S(2)}, u32[]{:S(2)}) collective-permute-start(bf16[512,576]{0,1:T(8,128)(2,1)S(1)} %copy.32), channel_id=1, source_target_pairs={{0,4},{4,0},{8,12},{12,8},{16,20},{20,16},{24,28},{28,24},{1,5},{5... | collective-permute-start | bytes 1769480 | tf_op jit(solution)/shard_map/ppermute | solution.py:466
  151.1 25.7 %collective-permute-start.14 = (bf16[4,32,1536]{2,1,0:T(8,128)(2,1)S(1)}, bf16[4,32,1536]{2,1,0:T(8,128)(2,1)}, u32[]{:S(2)}, u32[]{:S(2)}) collective-permute-start(bf16[4,32,1536]{2,1,0:T(8,128)(2,1)S(1)} %get-tuple-element.36), channel_id=1, source_target_pairs={{0,1},{1,2},{2,3},{3,0},{4,5},{5,6},{6,7},{7,4},{8,9},{9,10},{10,1... | collective-permute-start | bytes 1179656 | tf_op jit(solution)/shard_map/ppermute | solution.py:461
  164.3 49.1 %collective-permute-start.27 = (bf16[384,768]{1,0:T(8,128)(2,1)S(1)}, bf16[384,768]{1,0:T(8,128)(2,1)S(1)}, u32[]{:S(2)}, u32[]{:S(2)}) collective-permute-start(bf16[384,768]{1,0:T(8,128)(2,1)S(1)} %get-tuple-element.32), channel_id=1, source_target_pairs={{0,8},{4,12},{8,16},{12,20},{16,24},{20,28},{24,0},{28,4},{1,9},{5... | collective-permute-start | bytes 1769480 | tf_op jit(solution)/shard_map/ppermute | solution.py:456
  165.7 47.7 %collective-permute-start.28 = (bf16[384,768]{1,0:T(8,128)(2,1)S(1)}, bf16[384,768]{1,0:T(8,128)(2,1)S(1)}, u32[]{:S(2)}, u32[]{:S(2)}) collective-permute-start(bf16[384,768]{1,0:T(8,128)(2,1)S(1)} %get-tuple-element.31), channel_id=1, source_target_pairs={{0,16},{4,20},{8,24},{12,28},{16,0},{20,4},{24,8},{28,12},{1,17},{... | collective-permute-start | bytes 1769480 | tf_op jit(solution)/shard_map/ppermute | solution.py:456
  166.0 47.4 %collective-permute-start.29 = (bf16[384,768]{1,0:T(8,128)(2,1)S(1)}, bf16[384,768]{1,0:T(8,128)(2,1)S(1)}, u32[]{:S(2)}, u32[]{:S(2)}) collective-permute-start(bf16[384,768]{1,0:T(8,128)(2,1)S(1)} %get-tuple-element.30), channel_id=1, source_target_pairs={{0,24},{4,28},{8,0},{12,4},{16,8},{20,12},{24,16},{28,20},{1,25},{... | collective-permute-start | bytes 1769480 | tf_op jit(solution)/shard_map/ppermute | solution.py:456
  167.8 42.4 %collective-permute-start.15 = (bf16[4,32,1536]{2,1,0:T(8,128)(2,1)S(1)}, bf16[4,32,1536]{2,1,0:T(8,128)(2,1)S(1)}, u32[]{:S(2)}, u32[]{:S(2)}) collective-permute-start(bf16[4,32,1536]{2,1,0:T(8,128)(2,1)S(1)} %get-tuple-element.35), channel_id=1, source_target_pairs={{0,2},{1,3},{2,0},{3,1},{4,6},{5,7},{6,4},{7,5},{8,10},{9,11},{10,... | collective-permute-start | bytes 1179656 | tf_op jit(solution)/shard_map/ppermute | solution.py:461
  176.7 33.5 %collective-permute-start.16 = (bf16[4,32,1536]{2,1,0:T(8,128)(2,1)S(1)}, bf16[4,32,1536]{2,1,0:T(8,128)(2,1)S(1)}, u32[]{:S(2)}, u32[]{:S(2)}) collective-permute-start(bf16[4,32,1536]{2,1,0:T(8,128)(2,1)S(1)} %get-tuple-element.34), channel_id=1, source_target_pairs={{0,3},{1,0},{2,1},{3,2},{4,7},{5,4},{6,5},{7,6},{8,11},{9,8},{10,9... | collective-permute-start | bytes 1179656 | tf_op jit(solution)/shard_map/ppermute | solution.py:461
  217.3 32.7 %collective-permute-start.30 = (bf16[384,768]{1,0:T(8,128)(2,1)}, bf16[384,768]{1,0:T(8,128)(2,1)S(1)}, u32[]{:S(2)}, u32[]{:S(2)}) collective-permute-start(bf16[384,768]{1,0:T(8,128)(2,1)} %weight_sum.1.refs_0_), channel_id=1, source_target_pairs={{0,8},{4,12},{8,16},{12,20},{16,24},{20,28},{24,0},{28,4},{1,9},{5... | collective-permute-start | bytes 1769480 | tf_op jit(solution)/shard_map/ppermute | solution.py:456
  218.8 32.7 %collective-permute-start.31 = (bf16[384,768]{1,0:T(8,128)(2,1)}, bf16[384,768]{1,0:T(8,128)(2,1)S(1)}, u32[]{:S(2)}, u32[]{:S(2)}) collective-permute-start(bf16[384,768]{1,0:T(8,128)(2,1)} %weight_sum.1.refs_0_), channel_id=1, source_target_pairs={{0,16},{4,20},{8,24},{12,28},{16,0},{20,4},{24,8},{28,12},{1,17},{... | collective-permute-start | bytes 1769480 | tf_op jit(solution)/shard_map/ppermute | solution.py:456
  219.3 32.1 %collective-permute-start.32 = (bf16[384,768]{1,0:T(8,128)(2,1)}, bf16[384,768]{1,0:T(8,128)(2,1)S(1)}, u32[]{:S(2)}, u32[]{:S(2)}) collective-permute-start(bf16[384,768]{1,0:T(8,128)(2,1)} %weight_sum.1.refs_0_), channel_id=1, source_target_pairs={{0,24},{4,28},{8,0},{12,4},{16,8},{20,12},{24,16},{28,20},{1,25},{... | collective-permute-start | bytes 1769480 | tf_op jit(solution)/shard_map/ppermute | solution.py:456
  221.5 28.0 %collective-permute-start.17 = (bf16[32,1536]{1,0:T(8,128)(2,1)S(1)}, bf16[32,1536]{1,0:T(8,128)(2,1)S(1)}, u32[]{:S(2)}, u32[]{:S(2)}) collective-permute-start(bf16[32,1536]{1,0:T(8,128)(2,1)S(1)} %get-tuple-element.48), channel_id=1, source_target_pairs={{0,24},{4,28},{8,0},{12,4},{16,8},{20,12},{24,16},{28,20},{1,25},{... | collective-permute-start | bytes 294920 | tf_op jit(solution)/shard_map/ppermute | solution.py:456
  224.6 27.3 %collective-permute-start.20 = (bf16[32,1536]{1,0:T(8,128)(2,1)S(1)}, bf16[32,1536]{1,0:T(8,128)(2,1)S(1)}, u32[]{:S(2)}, u32[]{:S(2)}) collective-permute-start(bf16[32,1536]{1,0:T(8,128)(2,1)S(1)} %get-tuple-element.44), channel_id=1, source_target_pairs={{0,24},{4,28},{8,0},{12,4},{16,8},{20,12},{24,16},{28,20},{1,25},{... | collective-permute-start | bytes 294920 | tf_op jit(solution)/shard_map/ppermute | solution.py:456
  251.4 14.6 %collective-permute-start.33 = (bf16[384,768]{1,0:T(8,128)(2,1)}, bf16[384,768]{1,0:T(8,128)(2,1)S(1)}, u32[]{:S(2)}, u32[]{:S(2)}) collective-permute-start(bf16[384,768]{1,0:T(8,128)(2,1)} %weight_sum.1.refs_0_), channel_id=1, source_target_pairs={{0,4},{4,0},{8,12},{12,8},{16,20},{20,16},{24,28},{28,24},{1,5},{5... | collective-permute-start | bytes 1769480 | tf_op jit(solution)/shard_map/ppermute | solution.py:466
  251.5 24.2 %collective-permute-start.34 = (bf16[384,768]{1,0:T(8,128)(2,1)S(1)}, bf16[384,768]{1,0:T(8,128)(2,1)S(1)}, u32[]{:S(2)}, u32[]{:S(2)}) collective-permute-start(bf16[384,768]{1,0:T(8,128)(2,1)S(1)} %collective-permute-done.30.refs_1_), channel_id=1, source_target_pairs={{0,4},{4,0},{8,12},{12,8},{16,20},{20,16},{24,28},{28,24},{1,5},{5... | collective-permute-start | bytes 1769480 | tf_op jit(solution)/shard_map/ppermute | solution.py:466
  252.0 23.7 %collective-permute-start.35 = (bf16[384,768]{1,0:T(8,128)(2,1)S(1)}, bf16[384,768]{1,0:T(8,128)(2,1)S(1)}, u32[]{:S(2)}, u32[]{:S(2)}) collective-permute-start(bf16[384,768]{1,0:T(8,128)(2,1)S(1)} %collective-permute-done.31.refs_2_), channel_id=1, source_target_pairs={{0,4},{4,0},{8,12},{12,8},{16,20},{20,16},{24,28},{28,24},{1,5},{5... | collective-permute-start | bytes 1769480 | tf_op jit(solution)/shard_map/ppermute | solution.py:466
  254.1 21.6 %collective-permute-start.36 = (bf16[384,768]{1,0:T(8,128)(2,1)S(1)}, bf16[384,768]{1,0:T(8,128)(2,1)S(1)}, u32[]{:S(2)}, u32[]{:S(2)}) collective-permute-start(bf16[384,768]{1,0:T(8,128)(2,1)S(1)} %collective-permute-done.32.refs_3_), channel_id=1, source_target_pairs={{0,4},{4,0},{8,12},{12,8},{16,20},{20,16},{24,28},{28,24},{1,5},{5... | collective-permute-start | bytes 1769480 | tf_op jit(solution)/shard_map/ppermute | solution.py:466
  264.1 21.0 %collective-permute-start.24 = (bf16[2,4,1,1536]{3,2,1,0:T(2,128)(2,1)S(1)}, bf16[2,4,1,1536]{3,2,1,0:T(2,128)(2,1)S(1)}, u32[]{:S(2)}, u32[]{:S(2)}) collective-permute-start(bf16[2,4,1,1536]{3,2,1,0:T(2,128)(2,1)S(1)} %get-tuple-element.39), channel_id=1, source_target_pairs={{1,0},{2,1},{3,2},{4,3},{5,4},{6,5},{7,6},{8,7},{9,8},{10,9},{11,1... | collective-permute-start | bytes 73736 | tf_op jit(solution)/shard_map/ppermute | solution.py:450
  266.0 19.1 %collective-permute-start.23 = (bf16[2,4,1,1536]{3,2,1,0:T(2,128)(2,1)S(1)}, bf16[2,4,1,1536]{3,2,1,0:T(2,128)(2,1)S(1)}, u32[]{:S(2)}, u32[]{:S(2)}) collective-permute-start(bf16[2,4,1,1536]{3,2,1,0:T(2,128)(2,1)S(1)} %get-tuple-element.38), channel_id=1, source_target_pairs={{0,1},{1,2},{2,3},{3,4},{4,5},{5,6},{6,7},{7,8},{8,9},{9,10},{10,1... | collective-permute-start | bytes 73736 | tf_op jit(solution)/shard_map/ppermute | solution.py:449
  (46 other events, 341.0 us)
Sparse Core Ops, SparseCore 0:
  38.5 61.9 all-gather.1
  143.2 55.4 reduce-scatter.1

commit v3 on v2

--- a/solution.py
+++ b/solution.py
@@ -38,82 +38,109 @@
     return jnp.where(value < 0, value + size, jnp.where(value >= size, value - size, value))
 
 
-def shifted(ref, start, rows):
-    seqs = ref.shape[1]
-    parts = []
+def turned_rows(ref, low_ref, high_ref, parity, shift):
+    seqs, rows, width = ref.shape[1:]
+    own = ref[parity]
+    if shift != 1:
+        wide = own.astype(F32)
+        if shift == 0:
+            parts = [low_ref[parity].astype(F32), wide[:, : rows - 1]]
+        else:
+            parts = [wide[:, 1:], high_ref[parity].astype(F32)]
+        own = jnp.concatenate(parts, axis=1).astype(BF)
+    return own.reshape(seqs * rows, width)
+
+
+def conv_kernel(
+    at_ref, x_ref, low_ref, high_ref, w_ref, gain_ref, skip_ref, slope_ref, *rest
+):
+    normed_refs, (lhs, squares, whole_normed) = rest[:-3], rest[-3:]
+    step = pl.program_id(0)
+    seqs, rows, c_in = x_ref.shape[1:]
+    half = seqs * rows
+    tile = w_ref.shape[2]
+
+    @pl.when(step == 0)
+    def _():
+        for parity in range(2):
+            for shift in range(3):
+                value = turned_rows(x_ref, low_ref, high_ref, parity, shift)
+                for out in range(2):
+                    tap = 2 * shift + parity - out
+                    if 0 <= tap < KW:
+                        lhs[out * half : (out + 1) * half, tap * c_in : (tap + 1) * c_in] = value
+        squares[...] = jnp.zeros_like(squares)
+
+    conv = dot(lhs[...], w_ref[...].reshape(KW * c_in, tile), NN)
+    root = 0.7978845608028654
+    total = None
     for parity in range(2):
-        place = parity + start
-        wide = ref[place % 2].astype(F32)[:, place // 2 : place // 2 + rows, :]
-        parts.append(wide.reshape(seqs * rows, ref.shape[3]))
-    return jnp.concatenate(parts, axis=0).astype(BF)
-
-
-def conv_kernel(at_ref, x_ref, w_ref, gain_ref, skip_ref, slope_ref, normed_ref, acc):
-    step = pl.program_id(0)
-    rows = x_ref.shape[2] - 2
-    seqs = x_ref.shape[1]
-    half = acc.shape[0] // 2
-    for tap in range(KW):
-
-        @pl.when(step == tap)
-        def _():
-            term = dot(shifted(x_ref, tap, rows), w_ref[0], NN)
-            if tap == 0:
-                acc[...] = term
-            else:
-                acc[...] += term
-
-    @pl.when(step == KW - 1)
+        x = conv[parity * half : (parity + 1) * half, :]
+        square = x * x
+        t = jnp.tanh(root * (x + 0.044715 * (square * x)))
+        left = 0.5 * (1.0 + t)
+        act = x * left
+        slope = left + (0.5 * root) * x * (1.0 - t * t) * (1.0 + (3 * 0.044715) * square)
+        slope_ref[parity] = slope.reshape(slope_ref.shape[1:])
+        total = act if total is None else total + act
+    skip = (0.5 * total).astype(BF)
+    columns = pl.ds(pl.multiple_of(step * tile, tile), tile)
+    skip_ref[:, :, columns] = skip.reshape(seqs, rows, tile)
+    wide = skip.astype(F32)
+    squares[...] += jnp.sum(wide * wide, axis=-1, keepdims=True)
+
+    @pl.when(step == pl.num_programs(0) - 1)
     def _():
-        root = 0.7978845608028654
-        total = None
-        for parity in range(2):
-            x = acc[parity * half : (parity + 1) * half, :]
-            square = x * x
-            t = jnp.tanh(root * (x + 0.044715 * (square * x)))
-            left = 0.5 * (1.0 + t)
-            act = x * left
-            slope = left + (0.5 * root) * x * (1.0 - t * t) * (1.0 + (3 * 0.044715) * square)
-            slope_ref[parity] = slope.reshape(slope_ref.shape[1:])
-            total = act if total is None else total + act
-        skip = (0.5 * total).astype(BF)
-        skip_ref[...] = skip.reshape(skip_ref.shape)
-        wide = skip.astype(F32)
-        inv = lax.rsqrt(jnp.mean(wide * wide, axis=-1, keepdims=True) + 1e-06)
+        width = skip_ref.shape[2]
+        inv = lax.rsqrt(squares[...] * (1.0 / width) + 1e-06)
+        wide = skip_ref[...].reshape(half, width).astype(F32)
         normed = (wide * inv * gain_ref[...]).astype(BF)
-        for b in range(seqs):
-            normed_ref[wrapped(b - at_ref[0], seqs)] = normed[b * rows : (b + 1) * rows]
-
-
-def encoder(at, padded, conv_weight, norm_gain):
-    _, seqs, rows2, c_in = padded.shape
-    rows = rows2 - 2
+        whole_normed[...] = normed.reshape(whole_normed.shape)
+        for slot in range(seqs):
+            normed_refs[slot][...] = whole_normed[wrapped(at_ref[0] + slot, seqs)]
+
+
+def encoder(at, pairs, low, high, conv_weight, norm_gain):
+    _, seqs, rows, c_in = pairs.shape
     width = conv_weight.shape[2]
+    tile = 256 if width % 256 == 0 else width
     shape = (seqs, rows, width)
-    return pl.pallas_call(
+    outs = pl.pallas_call(
         conv_kernel,
-        grid=(KW,),
+        grid=(width // tile,),
         in_specs=[
             SCALARS,
-            whole(padded.shape),
-            pl.BlockSpec((1, c_in, width), lambda k: (k, 0, 0)),
+            whole(pairs.shape),
+            whole(low.shape),
+            whole(high.shape),
+            pl.BlockSpec((KW, c_in, tile), lambda n: (0, 0, n)),
             whole((1, width)),
         ],
-        out_specs=[whole(shape), whole((2,) + shape), whole(shape)],
+        out_specs=[
+            whole(shape),
+            pl.BlockSpec((2, seqs, rows, tile), lambda n: (0, 0, 0, n)),
+        ]
+        + [whole((rows, width))] * seqs,
         out_shape=[
             jax.ShapeDtypeStruct(shape, BF),
             jax.ShapeDtypeStruct((2,) + shape, F32),
-            jax.ShapeDtypeStruct(shape, BF),
+        ]
+        + [jax.ShapeDtypeStruct((rows, width), BF)] * seqs,
+        scratch_shapes=[
+            pltpu.VMEM((2 * seqs * rows, KW * c_in), BF),
+            pltpu.VMEM((seqs * rows, 1), F32),
+            pltpu.VMEM(shape, BF),
         ],
-        scratch_shapes=[pltpu.VMEM((2 * seqs * rows, width), F32)],
         compiler_params=params(),
         name="encoder_forward",
-    )(at, padded, conv_weight, norm_gain.reshape(1, width))
+    )(at, pairs, low, high, conv_weight, norm_gain.reshape(1, width))
+    return outs[0], outs[1], list(outs[2:])
 
 
 def d_conv_body(seqs, at_ref, *refs):
     dn_refs = refs[:seqs]
-    skip_ref, grad_ref, gain_ref, slope_ref, out_ref = refs[seqs:]
+    skip_ref, grad_ref, gain_ref, slope_ref, out_ref, first_ref, last_ref = refs[seqs:]
+    rows = out_ref.shape[2]
     for slot in range(seqs):
         b = wrapped(at_ref[0] + slot, seqs)
         wide = skip_ref[b].astype(F32)
@@ -125,17 +152,21 @@
         )
         d_act = 0.5 * d_skip
         for parity in range(2):
-            out_ref[parity, b] = (slope_ref[parity, b] * d_act).astype(BF)
+            value = slope_ref[parity, b] * d_act
+            out_ref[parity, b] = value.astype(BF)
+            first_ref[parity, b] = value[:1].astype(BF)
+            last_ref[parity, b] = value[rows - 1 :].astype(BF)
 
 
 def conv_gradient(at, d_normed, skip, grad, norm_gain, slope):
     seqs = len(d_normed)
     vmem = pl.BlockSpec(memory_space=pltpu.VMEM)
+    edge = jax.ShapeDtypeStruct(slope.shape[:2] + (1, slope.shape[3]), BF)
     return pl.pallas_call(
         functools.partial(d_conv_body, seqs),
         in_specs=[SCALARS] + [vmem] * (seqs + 4),
-        out_specs=vmem,
-        out_shape=jax.ShapeDtypeStruct(slope.shape, BF),
+        out_specs=[vmem] * 3,
+        out_shape=[jax.ShapeDtypeStruct(slope.shape, BF)] + [edge] * 2,
         compiler_params=params(),
         name="conv_gradient",
     )(at, *d_normed, skip, grad, norm_gain.reshape(1, -1), slope)
@@ -161,14 +192,22 @@
     )(at, *terms, skip)
 
 
-def conv_back_kernel(d_ref, w_ref, out_ref, acc):
+def conv_back_kernel(d_ref, low_ref, high_ref, w_ref, out_ref, turned, acc):
     step = pl.program_id(0)
-    rows = d_ref.shape[2] - 2
+
+    @pl.when(step == 0)
+    def _():
+        for parity in range(2):
+            for shift in range(3):
+                turned[parity, shift] = turned_rows(d_ref, low_ref, high_ref, parity, shift)
+
     for tap in range(KW):
 
         @pl.when(step == tap)
         def _():
-            term = dot(shifted(d_ref, KW - 1 - tap, rows), w_ref[0], NT)
+            places = [KW - 1 - tap, KW - tap]
+            lhs = jnp.concatenate([turned[p % 2, p // 2] for p in places], axis=0)
+            term = dot(lhs, w_ref[0], NT)
             if tap == 0:
                 acc[...] = term
             elif tap < KW - 1:
@@ -177,32 +216,41 @@
                 out_ref[...] = (acc[...] + term).astype(BF)
 
 
-def conv_back(d_pad, conv_weight):
-    _, seqs, rows2, width = d_pad.shape
+def conv_back(d_conv, low, high, conv_weight):
+    _, seqs, rows, width = d_conv.shape
     c_in = conv_weight.shape[1]
-    flat = 2 * seqs * (rows2 - 2)
+    flat = 2 * seqs * rows
     return pl.pallas_call(
         conv_back_kernel,
         grid=(KW,),
         in_specs=[
-            whole(d_pad.shape),
+            whole(d_conv.shape),
+            whole(low.shape),
+            whole(high.shape),
             pl.BlockSpec((1, c_in, width), lambda k: (k, 0, 0)),
         ],
         out_specs=whole((flat, c_in)),
         out_shape=jax.ShapeDtypeStruct((flat, c_in), BF),
-        scratch_shapes=[pltpu.VMEM((flat, c_in), F32)],
+        scratch_shapes=[
+            pltpu.VMEM((2, 3, seqs * rows, width), BF),
+            pltpu.VMEM((flat, c_in), F32),
+        ],
         compiler_params=params(),
         name="encoder_backward",
-    )(d_pad, conv_weight)
+    )(d_conv, low, high, conv_weight)
 
 
 def product_kernel(head_ref, x_ref, w_ref, out_ref, *, contract):
     del head_ref
-    out_ref[...] = dot(x_ref[...], w_ref[0], contract).astype(BF)
+    value = dot(x_ref[...], w_ref[0], contract).astype(BF)
+    out_ref[:, : value.shape[1]] = value
+    if value.shape[1] < out_ref.shape[1]:
+        out_ref[:, value.shape[1] :] = jnp.zeros_like(out_ref[:, value.shape[1] :])
 
 
 def head_product(head, x, weight, contract, name):
     columns = weight.shape[2] if contract == NN else weight.shape[1]
+    columns += -columns % 128
     rows, width = x.shape
     return pl.pallas_call(
         functools.partial(product_kernel, contract=contract),
@@ -236,7 +284,7 @@
         for start in range(0, half, block):
             rows = pl.ds(start, block)
             q = q_ref[rows, 0:DH]
-            d_o = d_ref[rows, :]
+            d_o = d_ref[rows, 0:DH]
             s = dot(q, k, NT) * scale
             e = jnp.exp(s - jnp.max(s, axis=-1, keepdims=True))
             p = e * (1.0 / jnp.sum(e, axis=-1, keepdims=True))
@@ -279,9 +327,9 @@
     )(qkv_a, qkv_b, d_a, d_b)
 
 
-def term_kernel(head_ref, a_ref, b_ref, w_ref, out_ref, acc, *, first, last, contract):
+def term_kernel(head_ref, a_ref, b_ref, w_ref, *rest, first, last, contract):
+    out_refs, acc = rest[:-1], rest[-1]
     step = pl.program_id(0)
-    groups = out_ref.shape[0]
 
     @pl.when(step == 0)
     def _():
@@ -289,14 +337,21 @@
 
     @pl.when(step == 1)
     def _():
-        total = acc[...] + dot(b_ref[:, first:last], w_ref[0], contract)
-        total = total.astype(BF).reshape(out_ref.shape)
-        for z in range(groups):
-            out_ref[wrapped(z - head_ref[1], groups)] = total[z]
-
-
-def pair_term(place, mine, got, weight, shape, first, last, contract, name):
+        acc[...] += dot(b_ref[:, first:last], w_ref[0], contract)
+        count = len(out_refs)
+        if count == 1:
+            out_refs[0][...] = acc[...].astype(BF)
+            return
+        size = out_refs[0].shape[0]
+        for slot, out_ref in enumerate(out_refs):
+            block = wrapped(head_ref[1] + slot, count)
+            rows = pl.ds(pl.multiple_of(block * size, size), size)
+            out_ref[...] = acc[rows, :].astype(BF)
+
+
+def pair_term(place, mine, got, weight, width, slots, first, last, contract, name):
     half, full = mine.shape
+    size = half // slots
     return pl.pallas_call(
         functools.partial(term_kernel, first=first, last=last, contract=contract),
         grid_spec=pltpu.PrefetchScalarGridSpec(
@@ -310,42 +365,13 @@
                     lambda i, at: (jnp.where(i == 0, at[0], 1 - at[0]), 0, 0),
                 ),
             ],
-            out_specs=pl.BlockSpec(shape, lambda i, at: (0, 0, 0, 0)),
-            scratch_shapes=[pltpu.VMEM((half, shape[-1]), F32)],
+            out_specs=[pl.BlockSpec((size, width), lambda i, at: (0, 0))] * slots,
+            scratch_shapes=[pltpu.VMEM((half, width), F32)],
         ),
-        out_shape=jax.ShapeDtypeStruct(shape, BF),
+        out_shape=[jax.ShapeDtypeStruct((size, width), BF)] * slots,
         compiler_params=params(),
         name=name,
     )(place, mine, got, weight)
-
-
-def place_kernel(at_ref, *refs):
-    step = pl.program_id(0)
-    del at_ref
-    for slot, ref in enumerate(refs[:-1]):
-
-        @pl.when(step == slot)
-        def _():
-            refs[-1][...] = ref[...]
-
-
-def in_order(at, slots, name):
-    count = len(slots)
-    rows, width = slots[0].shape
-    return pl.pallas_call(
-        place_kernel,
-        grid_spec=pltpu.PrefetchScalarGridSpec(
-            num_scalar_prefetch=1,
-            grid=(count,),
-            in_specs=[pl.BlockSpec((rows, width), lambda q, at: (0, 0))] * count,
-            out_specs=pl.BlockSpec(
-                (rows, width), lambda q, at: (lax.rem(at[0] - q + count, count), 0)
-            ),
-        ),
-        out_shape=jax.ShapeDtypeStruct((count * rows, width), slots[0].dtype),
-        compiler_params=params(),
-        name=name,
-    )(at, *slots)
 
 
 def sum_kernel(*refs):
@@ -364,12 +390,16 @@
     )(*parts)
 
 
-def weight_kernel(at_ref, xa_ref, xb_ref, ga_ref, gb_ref, ra_ref, rb_ref, out_ref):
+def weight_kernel(at_ref, xa_ref, xb_ref, ga_ref, gb_ref, ra_ref, rb_ref, *out_refs):
     del at_ref
     qkv = dot(xa_ref[...], ra_ref[:, DH:], TN) + dot(xb_ref[...], rb_ref[:, DH:], TN)
     out = dot(ga_ref[...], ra_ref[:, :DH], TN) + dot(gb_ref[...], rb_ref[:, :DH], TN)
-    out_ref[0, :, : 3 * DH] = qkv.astype(BF)
-    out_ref[0, :, 3 * DH :] = out.astype(BF)
+    for slot, out_ref in enumerate(out_refs):
+
+        @pl.when(pl.program_id(0) == slot)
+        def _():
+            out_ref[:, : 3 * DH] = qkv.astype(BF)
+            out_ref[:, 3 * DH :] = out.astype(BF)
 
 
 def weight_gradients(at, xa, xb, ga, gb, ra, rb, seqs):
@@ -384,9 +414,9 @@
             num_scalar_prefetch=1,
             grid=(seqs,),
             in_specs=[column] * 4 + [rest] * 2,
-            out_specs=pl.BlockSpec((1, chunk, full), lambda r, at: (r, 0, 0)),
+            out_specs=[pl.BlockSpec((chunk, full), lambda r, at: (0, 0))] * seqs,
         ),
-        out_shape=jax.ShapeDtypeStruct((seqs, chunk, full), BF),
+        out_shape=[jax.ShapeDtypeStruct((chunk, full), BF)] * seqs,
         compiler_params=params(),
         name="weight_gradients",
     )(at, xa, xb, ga, gb, ra, rb)
@@ -441,14 +471,12 @@
     )(at, *mine, *other)
 
 
-def neighbour_edges(pairs):
+def neighbour_edges(first, last):
     axes = ("seq", "head")
     count = lax.axis_size(axes)
     forward = [(i, i + 1) for i in range(count - 1)]
     backward = [(target, source) for source, target in forward]
-    low = lax.ppermute(pairs[:, :, -1:, :], axes, forward)
-    high = lax.ppermute(pairs[:, :, :1, :], axes, backward)
-    return jnp.concatenate([low, pairs, high], axis=2)
+    return lax.ppermute(last, axes, forward), lax.ppermute(first, axes, backward)
 
 
 def send_chip(x, step, heads):
@@ -490,20 +518,17 @@
         return [slots[r] if r == 0 else send_chip(slots[r], -r, heads) for r in range(seqs)]
 
     grad = jnp.transpose(grad_out, (1, 0, 2))
+    grad_z = lax.all_gather(grad, "head", axis=0, tiled=False)
     grad_slots = [
-        lax.dynamic_index_in_dim(grad, (own_seq + r) % seqs, 0, keepdims=False)
+        lax.dynamic_index_in_dim(grad_z, (own_seq + r) % seqs, 1, keepdims=False)
         for r in range(seqs)
     ]
-    grad_slab = jnp.concatenate(to_chips(grad_slots), axis=0)
-    grad_rows = in_order(
-        own_z.reshape(1),
-        [grad_slab if q == 0 else send_z(grad_slab, q) for q in range(groups)],
-        "grad_rows",
-    )
+    grad_rows = jnp.stack(to_chips(grad_slots), axis=1).reshape(half, width)
 
     pairs = jnp.transpose(enc_in.reshape(rows, 2, seqs, enc_in.shape[2]), (1, 2, 0, 3))
-    skip, slope, normed = encoder(at, neighbour_edges(pairs), conv_weight, norm_gain)
-    normed_slab = jnp.concatenate(to_chips([normed[r] for r in range(seqs)]), axis=0)
+    low, high = neighbour_edges(pairs[:, :, :1, :], pairs[:, :, -1:, :])
+    skip, slope, normed = encoder(at, pairs, low, high, conv_weight, norm_gain)
+    normed_slab = jnp.concatenate(to_chips(normed), axis=0)
     normed_rows = lax.all_gather(normed_slab, "head", axis=0, tiled=True)
 
     w_pack = jnp.transpose(w_qkv.reshape(3, width, heads, DH), (2, 1, 0, 3))
@@ -516,21 +541,23 @@
     result_mine, result_other = attention(qkv_mine, qkv_got, d_mine, d_got)
     result_got = swap_heads(result_other)
 
-    shape = (groups, seqs, rows, width)
     plain = jnp.stack([own_head, zero])
-    d_term = pair_term(
-        plain, result_mine, result_got, w_pack, shape, DH, 4 * DH, NT, "d_term"
-    )
-    d_normed = lax.psum_scatter(d_term, "head", scatter_dimension=0, tiled=False)
-    d_normed = from_chips([d_normed[r] for r in range(seqs)])
+    (d_term,) = pair_term(
+        plain, result_mine, result_got, w_pack, width, 1, DH, 4 * DH, NT, "d_term"
+    )
+    d_normed = lax.psum_scatter(
+        d_term.reshape(groups, seqs, rows, width), "head", scatter_dimension=0, tiled=False
+    )
 
     turned = jnp.stack([own_head, own_z])
     head_term = pair_term(
-        turned, result_mine, result_got, w_rows, shape, 0, DH, NN, "head_term"
-    )
+        turned, result_mine, result_got, w_rows, width, groups, 0, DH, NN, "head_term"
+    )
+    head_term, d_normed = lax.optimization_barrier((head_term, d_normed))
+    d_normed = from_chips([d_normed[r] for r in range(seqs)])
     head_sum = summed(
         [head_term[q] if q == 0 else send_z(head_term[q], q) for q in range(groups)], "head_sum"
-    )
+    ).reshape(seqs, rows, width)
     head_sum = from_chips([head_sum[r] for r in range(seqs)])
     mixed = mixed_call(at, head_sum, skip)
 
@@ -544,12 +571,13 @@
         result_other,
         seqs,
     )
-    chunk = summed(to_chips([part[r] for r in range(seqs)]), "weight_sum")
+    chunk = summed(to_chips(part), "weight_sum")
     chunks = [chunk if r == 0 else send_chip(chunk, r, heads) for r in range(seqs)]
     grad_w_qkv, grad_w_out = unpack_weights(at, chunks, [swap_heads(c) for c in chunks])
 
-    d_conv = conv_gradient(at, d_normed, skip, grad, norm_gain, slope)
-    grad_input = conv_back(neighbour_edges(d_conv), conv_weight)
+    d_conv, first, last = conv_gradient(at, d_normed, skip, grad, norm_gain, slope)
+    low, high = neighbour_edges(first, last)
+    grad_input = conv_back(d_conv, low, high, conv_weight)
     grad_input = jnp.transpose(grad_input.reshape(2, seqs, rows, -1), (2, 0, 1, 3))
     return (
         jnp.transpose(mixed, (1, 0, 2)),

time: 308 us -> 276 us (0.90)
  starting transfers between devices: 55.9 us -> 37.9 us
  local copies, waits for them, and re-layouts: 40.3 us -> 31.3 us
  waiting for transfers between devices: 105 us -> 101 us
    all_gather x1, waiting for transfers between devices: 39.5 us -> 21.4 us  [unit_body(): normed_rows = lax.all_gather(normed_slab, 'head', axis=0, tiled=True)]
    ppermute x18, waiting for transfers between devices: 32 us -> 49.8 us  [send_chip(): lax.ppermute(x, 'seq', [(s, (s + step * heads) % count) for s in range(co...]
    ppermute x6 -> x3, waiting for transfers between devices: 32.2 us -> 14.7 us  [send_z(): lax.ppermute(x, 'head', [(z, (z + step) % count) for z in range(count)])]
    ppermute x6 -> x3, starting transfers between devices: 16.7 us -> 2.81 us  [send_z(): lax.ppermute(x, 'head', [(z, (z + step) % count) for z in range(count)])]
    squeeze x5 -> x0, local copies, waits for them, and re-layouts: 8.46 us -> none  [the longest x1 2.56 us: unit_body(): chunk = summed(to_chips([part[r] for r in range(seqs)]), 'weight_sum')]
    all_gather x0 -> x1, waiting for transfers between devices: none -> 6.72 us  [unit_body(): grad_z = lax.all_gather(grad, 'head', axis=0, tiled=False)]
    ppermute x9, waiting for transfers between devices: 1.56 us -> 6.11 us  [swap_heads(): lax.ppermute(x, 'seq', [(s, s + 1 - 2 * (s % 2)) for s in range(count)])]
    pallas_call x3 -> x2, Pallas kernels: 21.3 us -> 18.9 us  [the longest x1 10.1 us: encoder(): pl.pallas_call(conv_kernel, grid=(width // tile,), in_specs=[SCALARS, who...]
  transfers between devices with their start and end apart: 39 -> 37, of which waited for: 11 -> 15; matrix products, arithmetic and copies ran while one was open for 10% -> 9% of each run, Pallas kernels for 16% -> 23%
where the time goes in v3:
time: 276 us; the launch traced here: 270 us
  waiting for transfers between devices  101 us (37%)
  Pallas kernels  80.8 us (29%)
  starting transfers between devices  37.9 us (14%)
  local copies, waits for them, and re-layouts  31.3 us (11%)
  between operations  14.1 us (5%)
  other arithmetic  5.43 us (2%)
    ppermute x18, waiting for transfers between devices, send_chip(): lax.ppermute(x, 'seq', [(s, (s + step * heads) % count) for s in range(co...  49.8 us
    ppermute x18, starting transfers between devices, send_chip(): lax.ppermute(x, 'seq', [(s, (s + step * heads) % count) for s in range(co...  21.8 us
    all_gather x1, waiting for transfers between devices, unit_body(): normed_rows = lax.all_gather(normed_slab, 'head', axis=0, tiled=True)  21.4 us
    unnamed x73, local copies, waits for them, and re-layouts  15.4 us
    ppermute x3, waiting for transfers between devices, send_z(): lax.ppermute(x, 'head', [(z, (z + step) % count) for z in range(count)])  14.7 us
    pallas_call x4, Pallas kernels, head_product(): pl.pallas_call(functools.partial(product_kernel, contract=contract), grid...  14.3 us
    pallas_call x2, Pallas kernels, pair_term(): pl.pallas_call(functools.partial(term_kernel, first=first, last=last, con...  11.5 us
    pallas_call x1, Pallas kernels, encoder(): pl.pallas_call(conv_kernel, grid=(width // tile,), in_specs=[SCALARS, who...  10.1 us
  transfers between devices with their start and end apart: 37, of which 15 were waited for; matrix products, arithmetic and copies ran while one was open for 9% of the time, Pallas kernels for 23%

profile of v3, /device:TPU:26, one launch (start us, length us, event | category | flops | bytes accessed | tf_op | source)
XLA Modules:
  0.0 270.2 jit_solution(7042998533247300700)
XLA Ops:
  12.2 3.9 %collective-permute-start.1 = (bf16[2,4,1,768]{3,2,1,0:T(2,128)(2,1)S(1)}, bf16[2,4,1,768]{3,2,1,0:T(2,128)(2,1)S(1)}, u32[]{:S(2)}, u32[]{:S(2)}) collective-permute-start(bf16[2,4,1,768]{3,2,1,0:T(2,128)(2,1)S(1)} %get-tuple-element.80), channel_id=1, source_target_pairs={{1,0},{2,1},{3,2},{4,3},{5,4},{6,5},{7,6},{8,7},{9,8},{10,9},{11,1... | collective-permute-start | bytes 36872 | tf_op jit(solution)/shard_map/ppermute | solution.py:479
  19.7 10.1 %encoder_forward.1 = (bf16[4,32,1536]{2,1,0:T(8,128)(2,1)}, f32[2,4,32,1536]{3,2,1,0:T(8,128)}, bf16[32,1536]{1,0:T(8,128)(2,1)}, bf16[32,1536]{1,0:T(8,128)(2,1...) custom-call(s32[2]{0:T(128)} %pad_add_fusion.at_ref, bf16[2,4,32,768]{3,2,1,0:T(8,128)(2,1)} %bitcast.55, ...), custom_call_target="tpu_custom_call" | custom-call | tf_op jit(solution)/shard_map/encoder_forward/pallas_call | solution.py:108
  39.1 6.7 %all-gather.6.cloned.1.call-done = bf16[16,32,1536]{2,1,0:T(8,128)(2,1)} async-done(((bf16[4,32,1536]{2,1,0:T(8,128)(2,1)}), bf16[16,32,1536]{2,1,0:T(8,128)(2,1)}) %all-gather.6.cloned.1.call-update) | async-done | bytes 1572880 | tf_op jit(solution)/shard_map/all_gather | solution.py:521
  52.8 3.7 %copy.24 = bf16[3,1536,384]{1,2,0:T(8,128)(2,1)} copy(bf16[3,1536,384]{2,1,0:T(8,128)(2,1)S(1)} %copy-done.2) | data formatting | bytes 7077888 | tf_op args[3]
  58.9 3.7 %copy.26.w_ref = bf16[2,1536,576]{2,1,0:T(8,128)(2,1)} copy(bf16[2,1536,576]{1,2,0:T(8,128)(2,1)S(1)} %bitcast.46) | data formatting | bytes 7077888 | tf_op jit(solution)/shard_map/reshape | solution.py:535
  62.6 21.4 %all-gather.4.cloned.1.call-done.x_ref.xa_ref = bf16[512,1536]{1,0:T(8,128)(2,1)} async-done(((bf16[128,1536]{1,0:T(8,128)(2,1)}), bf16[512,1536]{1,0:T(8,128)(2,1)}) %all-gather.4.cloned.1.call-update) | async-done | bytes 1572880 | tf_op jit(solution)/shard_map/all_gather | solution.py:532
  84.0 4.3 %qkv_other.1 = bf16[512,640]{1,0:T(8,128)(2,1)} custom-call(s32[1]{0:T(128)} %bitcast.8.head_ref, bf16[512,1536]{1,0:T(8,128)(2,1)} %all-gather.4.cloned.1.call-done.x_ref.xa_ref, bf16[2,1536,576]{2,1,0:T(8,128)(2,1)} %copy.26.w_ref), custom_call_target="tpu_custom_call" | custom-call | tf_op jit(solution)/shard_map/qkv_other/pallas_call | solution.py:255
  90.9 2.8 %d_o_other.1 = bf16[512,256]{1,0:T(8,128)(2,1)} custom-call(s32[1]{0:T(128)} %bitcast.8.head_ref, bf16[512,1536]{1,0:T(8,128)(2,1)} %bitcast.42, bf16[2,192,1536]{2,1,0:T(8,128)(2,1)} %bitcast.48), custom_call_target="tpu_custom_call" | custom-call | tf_op jit(solution)/shard_map/d_o_other/pallas_call | solution.py:255
  94.2 4.3 %qkv_own.1.qa_ref = bf16[512,640]{1,0:T(8,128)(2,1)} custom-call(s32[1]{0:T(128)} %bitcast.1.head_ref, bf16[512,1536]{1,0:T(8,128)(2,1)} %all-gather.4.cloned.1.call-done.x_ref.xa_ref, bf16[2,1536,576]{2,1,0:T(8,128)(2,1)} %copy.26.w_ref), custom_call_target="tpu_custom_call" | custom-call | tf_op jit(solution)/shard_map/qkv_own/pallas_call | solution.py:255
  98.5 2.8 %d_o_own.1.da_ref = bf16[512,256]{1,0:T(8,128)(2,1)} custom-call(s32[1]{0:T(128)} %bitcast.1.head_ref, bf16[512,1536]{1,0:T(8,128)(2,1)} %bitcast.43, bf16[2,192,1536]{2,1,0:T(8,128)(2,1)} %bitcast.49), custom_call_target="tpu_custom_call" | custom-call | tf_op jit(solution)/shard_map/d_o_own/pallas_call | solution.py:255
  102.9 8.9 %attention.1 = (bf16[512,768]{1,0:T(8,128)(2,1)}, bf16[512,768]{1,0:T(8,128)(2,1)}) custom-call(bf16[512,640]{1,0:T(8,128)(2,1)} %qkv_own.1.qa_ref, bf16[512,640]{1,0:T(8,128)(2,1)} %copy-done.9, bf16[512,256]{1,0:T(8,128)(2,1)} %d_o_own.1.da_ref, bf16[512,256]{1,0:T(8,128)(2,1)} %copy-done.23), custom_call_target="tpu_custom_call" | custom-call | tf_op jit(solution)/shard_map/attention/pallas_call | solution.py:316
  115.3 6.9 %d_term.1 = bf16[512,1536]{1,0:T(8,128)(2,1)} custom-call(s32[2]{0:T(128)} %get-tuple-element.83.head_ref, bf16[512,768]{1,0:T(8,128)(2,1)} %get-tuple-element.34.a_ref.ra_ref, bf16[512,768]{1,0:T(8,128)(2,1)} %copy-done.3, bf16[2,1536,576]{2,1,0:T(8,128)(2,1)} %copy.26.w_ref), custom_call_target="tpu_custom_call" | custom-call | tf_op jit(solution)/shard_map/d_term/pallas_call | solution.py:355
  129.1 9.1 %weight_gradients.1 = (bf16[384,768]{1,0:T(8,128)(2,1)}, bf16[384,768]{1,0:T(8,128)(2,1)}, bf16[384,768]{1,0:T(8,128)(2,1)}, bf16[384,768]{1,0:T(8,128)(2,1)}) custom-call(s32[1]{0:T(128)} %bitcast.at_ref, bf16[512,1536]{1,0:T(8,128)(2,1)} %all-gather.4.cloned.1.call-done.x_ref.xa_ref, bf16[512,1536]{1,0:T(8,128)(2,1)} %copy-done.7, ...), custom_call_target="tpu_custom_call" | custom-call | tf_op jit(solution)/shard_map/weight_gradients/pallas_call | solution.py:411
  141.7 12.9 %collective-permute-done.24.refs_1_ = bf16[384,768]{1,0:T(8,128)(2,1)S(1)} collective-permute-done((bf16[384,768]{1,0:T(8,128)(2,1)}, bf16[384,768]{1,0:T(8,128)(2,1)S(1)}, u32[]{:S(2)}, u32[]{:S(2)}) %collective-permute-start.24) | collective-permute-done | bytes 589856 | tf_op jit(solution)/shard_map/ppermute | solution.py:484
  154.6 13.1 %collective-permute-done.25.refs_2_ = bf16[384,768]{1,0:T(8,128)(2,1)S(1)} collective-permute-done((bf16[384,768]{1,0:T(8,128)(2,1)}, bf16[384,768]{1,0:T(8,128)(2,1)S(1)}, u32[]{:S(2)}, u32[]{:S(2)}) %collective-permute-start.25) | collective-permute-done | bytes 589856 | tf_op jit(solution)/shard_map/ppermute | solution.py:484
  174.0 4.7 %head_term.1 = (bf16[128,1536]{1,0:T(8,128)(2,1)}, bf16[128,1536]{1,0:T(8,128)(2,1)}, bf16[128,1536]{1,0:T(8,128)(2,1)}, bf16[128,1536]{1,0:T(8,128)(2,1)}) custom-call(s32[2]{0:T(128)} %get-tuple-element.82.head_ref, bf16[512,768]{1,0:T(8,128)(2,1)} %get-tuple-element.34.a_ref.ra_ref, bf16[512,768]{1,0:T(8,128)(2,1)} %copy-done.3, ...), custom_call_target="tpu_custom_call" | custom-call | tf_op jit(solution)/shard_map/head_term/pallas_call | solution.py:355
  181.5 6.4 %collective-permute-done.27.refs_1_ = bf16[384,768]{1,0:T(8,128)(2,1)S(1)} collective-permute-done((bf16[384,768]{1,0:T(8,128)(2,1)}, bf16[384,768]{1,0:T(8,128)(2,1)S(1)}, u32[]{:S(2)}, u32[]{:S(2)}) %collective-permute-start.27) | collective-permute-done | bytes 589856 | tf_op jit(solution)/shard_map/ppermute | solution.py:484
  187.9 12.5 %collective-permute-done.28.refs_2_ = bf16[384,768]{1,0:T(8,128)(2,1)S(1)} collective-permute-done((bf16[384,768]{1,0:T(8,128)(2,1)}, bf16[384,768]{1,0:T(8,128)(2,1)S(1)}, u32[]{:S(2)}, u32[]{:S(2)}) %collective-permute-start.28) | collective-permute-done | bytes 589856 | tf_op jit(solution)/shard_map/ppermute | solution.py:484
  201.0 5.1 %collective-permute-done.12.refs_2_ = bf16[128,1536]{1,0:T(8,128)(2,1)S(1)} collective-permute-done((bf16[128,1536]{1,0:T(8,128)(2,1)}, bf16[128,1536]{1,0:T(8,128)(2,1)S(1)}, u32[]{:S(2)}, u32[]{:S(2)}) %collective-permute-start.12) | collective-permute-done | bytes 393248 | tf_op jit(solution)/shard_map/ppermute | solution.py:489
  208.0 9.6 %collective-permute-done.13.refs_3_ = bf16[128,1536]{1,0:T(8,128)(2,1)S(1)} collective-permute-done((bf16[128,1536]{1,0:T(8,128)(2,1)}, bf16[128,1536]{1,0:T(8,128)(2,1)S(1)}, u32[]{:S(2)}, u32[]{:S(2)}) %collective-permute-start.13) | collective-permute-done | bytes 393248 | tf_op jit(solution)/shard_map/ppermute | solution.py:489
  230.5 3.3 %conv_gradient.1 = (bf16[2,4,32,1536]{3,2,1,0:T(8,128)(2,1)}, bf16[2,4,1,1536]{3,2,1,0:T(2,128)(2,1)}, bf16[2,4,1,1536]{3,2,1,0:T(2,128)(2,1)}) custom-call(s32[2]{0:T(128)} %pad_add_fusion.at_ref, bf16[32,1536]{1,0:T(8,128)(2,1)} %get-tuple-element.75.refs_0_, bf16[32,1536]{1,0:T(8,128)(2,1)} %copy-done.27, bf16[32,1536]{1,0:T(8,128)(2,1)} %copy-done.28, ...), custom_call_target="tpu_custom_call" | custom-call | tf_op jit(solution)/shard_map/conv_gradient/pallas_call | solution.py:165
  235.8 3.9 %collective-permute-start.21 = (bf16[2,4,1,1536]{3,2,1,0:T(2,128)(2,1)}, bf16[2,4,1,1536]{3,2,1,0:T(2,128)(2,1)S(1)}, u32[]{:S(2)}, u32[]{:S(2)}) collective-permute-start(bf16[2,4,1,1536]{3,2,1,0:T(2,128)(2,1)} %get-tuple-element.49), channel_id=1, source_target_pairs={{1,0},{2,1},{3,2},{4,3},{5,4},{6,5},{7,6},{8,7},{9,8},{10,9},{11,1... | collective-permute-start | bytes 73736 | tf_op jit(solution)/shard_map/ppermute | solution.py:479
  239.7 7.7 %weight_outputs.1 = (f32[3,1536,384]{2,1,0:T(8,128)}, f32[384,1536]{1,0:T(8,128)}) custom-call(s32[2]{0:T(128)} %pad_add_fusion.at_ref, bf16[384,768]{1,0:T(8,128)(2,1)} %weight_sum.1.refs_0_, bf16[384,768]{1,0:T(8,128)(2,1)} %copy-done.10, bf16[384,768]{1,0:T(8,128)(2,1)} %copy-done.11, bf16[384,768]{1,0:T(8,128)(2,1)} %copy-done.12, ...), custom_call_target="tpu_custom_call" | custom-call | tf_op jit(solution)/shard_map/weight_outputs/pallas_call | solution.py:454
  248.0 8.7 %encoder_backward.1 = bf16[256,768]{1,0:T(8,128)(2,1)} custom-call(bf16[2,4,32,1536]{3,2,1,0:T(8,128)(2,1)} %get-tuple-element.47.d_ref, bf16[2,4,1,1536]{3,2,1,0:T(2,128)(2,1)} %copy-done.30, bf16[2,4,1,1536]{3,2,1,0:T(2,128)(2,1)} %copy-done.31, bf16[5,768,1536]{2,1,0:T(8,128)(2,1)} %w_ref.3), custom_call_target="tpu_custom_call" | custom-call | tf_op jit(solution)/shard_map/encoder_backward/pallas_call | solution.py:223
  (154 shorter events, 79.4 us)
Async XLA Ops:
  7.2 38.7 %all-gather.6.cloned.1.call-start = ((), (), s32[]{:S(2)}) async-start(), calls=%async_computation.3 | async-start | bytes 1966080 | tf_op jit(solution)/shard_map/all_gather | solution.py:521
  9.1 74.9 %all-gather.4.cloned.1.call-start = ((), (), s32[]{:S(2)}) async-start(), calls=%async_computation.1 | async-start | bytes 1966080 | tf_op jit(solution)/shard_map/all_gather | solution.py:532
  39.0 139.6 %reduce-scatter.2.cloned.1.call-start = ((), (), s32[]{:S(2)}) async-start(), calls=%async_computation.2 | async-start | bytes 1966080 | tf_op jit(solution)/shard_map/reduce_scatter | solution.py:548
  48.4 39.9 %collective-permute-start.8 = (bf16[4,32,1536]{2,1,0:T(8,128)(2,1)}, bf16[4,32,1536]{2,1,0:T(8,128)(2,1)}, u32[]{:S(2)}, u32[]{:S(2)}) collective-permute-start(bf16[4,32,1536]{2,1,0:T(8,128)(2,1)} %get-tuple-element.69), channel_id=1, source_target_pairs={{0,24},{4,28},{8,0},{12,4},{16,8},{20,12},{24,16},{28,20},{1,25},{... | collective-permute-start | bytes 1179656 | tf_op jit(solution)/shard_map/ppermute | solution.py:484
  48.7 39.6 %collective-permute-start.7 = (bf16[4,32,1536]{2,1,0:T(8,128)(2,1)}, bf16[4,32,1536]{2,1,0:T(8,128)(2,1)}, u32[]{:S(2)}, u32[]{:S(2)}) collective-permute-start(bf16[4,32,1536]{2,1,0:T(8,128)(2,1)} %get-tuple-element.70), channel_id=1, source_target_pairs={{0,16},{4,20},{8,24},{12,28},{16,0},{20,4},{24,8},{28,12},{1,17},{... | collective-permute-start | bytes 1179656 | tf_op jit(solution)/shard_map/ppermute | solution.py:484
  50.4 37.9 %collective-permute-start.6 = (bf16[4,32,1536]{2,1,0:T(8,128)(2,1)}, bf16[4,32,1536]{2,1,0:T(8,128)(2,1)}, u32[]{:S(2)}, u32[]{:S(2)}) collective-permute-start(bf16[4,32,1536]{2,1,0:T(8,128)(2,1)} %get-tuple-element.71), channel_id=1, source_target_pairs={{0,8},{4,12},{8,16},{12,20},{16,24},{20,28},{24,0},{28,4},{1,9},{5... | collective-permute-start | bytes 1179656 | tf_op jit(solution)/shard_map/ppermute | solution.py:484
  88.3 13.1 %collective-permute-start.5 = (bf16[512,640]{1,0:T(8,128)(2,1)}, bf16[512,640]{1,0:T(8,128)(2,1)S(1)}, u32[]{:S(2)}, u32[]{:S(2)}) collective-permute-start(bf16[512,640]{1,0:T(8,128)(2,1)} %qkv_other.1), channel_id=1, source_target_pairs={{0,4},{4,0},{8,12},{12,8},{16,20},{20,16},{24,28},{28,24},{1,5},{5... | collective-permute-start | bytes 1966088 | tf_op jit(solution)/shard_map/ppermute | solution.py:494
  138.2 16.4 %collective-permute-start.24 = (bf16[384,768]{1,0:T(8,128)(2,1)}, bf16[384,768]{1,0:T(8,128)(2,1)S(1)}, u32[]{:S(2)}, u32[]{:S(2)}) collective-permute-start(bf16[384,768]{1,0:T(8,128)(2,1)} %get-tuple-element.51), channel_id=1, source_target_pairs={{0,8},{4,12},{8,16},{12,20},{16,24},{20,28},{24,0},{28,4},{1,9},{5... | collective-permute-start | bytes 1769480 | tf_op jit(solution)/shard_map/ppermute | solution.py:484
  139.7 28.0 %collective-permute-start.25 = (bf16[384,768]{1,0:T(8,128)(2,1)}, bf16[384,768]{1,0:T(8,128)(2,1)S(1)}, u32[]{:S(2)}, u32[]{:S(2)}) collective-permute-start(bf16[384,768]{1,0:T(8,128)(2,1)} %get-tuple-element.52), channel_id=1, source_target_pairs={{0,16},{4,20},{8,24},{12,28},{16,0},{20,4},{24,8},{28,12},{1,17},{... | collective-permute-start | bytes 1769480 | tf_op jit(solution)/shard_map/ppermute | solution.py:484
  140.2 27.4 %collective-permute-start.26 = (bf16[384,768]{1,0:T(8,128)(2,1)}, bf16[384,768]{1,0:T(8,128)(2,1)S(1)}, u32[]{:S(2)}, u32[]{:S(2)}) collective-permute-start(bf16[384,768]{1,0:T(8,128)(2,1)} %get-tuple-element.53), channel_id=1, source_target_pairs={{0,24},{4,28},{8,0},{12,4},{16,8},{20,12},{24,16},{28,20},{1,25},{... | collective-permute-start | bytes 1769480 | tf_op jit(solution)/shard_map/ppermute | solution.py:484
  171.4 16.5 %collective-permute-start.27 = (bf16[384,768]{1,0:T(8,128)(2,1)}, bf16[384,768]{1,0:T(8,128)(2,1)S(1)}, u32[]{:S(2)}, u32[]{:S(2)}) collective-permute-start(bf16[384,768]{1,0:T(8,128)(2,1)} %weight_sum.1.refs_0_), channel_id=1, source_target_pairs={{0,8},{4,12},{8,16},{12,20},{16,24},{20,28},{24,0},{28,4},{1,9},{5... | collective-permute-start | bytes 1769480 | tf_op jit(solution)/shard_map/ppermute | solution.py:484
  172.6 27.8 %collective-permute-start.28 = (bf16[384,768]{1,0:T(8,128)(2,1)}, bf16[384,768]{1,0:T(8,128)(2,1)S(1)}, u32[]{:S(2)}, u32[]{:S(2)}) collective-permute-start(bf16[384,768]{1,0:T(8,128)(2,1)} %weight_sum.1.refs_0_), channel_id=1, source_target_pairs={{0,16},{4,20},{8,24},{12,28},{16,0},{20,4},{24,8},{28,12},{1,17},{... | collective-permute-start | bytes 1769480 | tf_op jit(solution)/shard_map/ppermute | solution.py:484
  173.1 27.3 %collective-permute-start.29 = (bf16[384,768]{1,0:T(8,128)(2,1)}, bf16[384,768]{1,0:T(8,128)(2,1)S(1)}, u32[]{:S(2)}, u32[]{:S(2)}) collective-permute-start(bf16[384,768]{1,0:T(8,128)(2,1)} %weight_sum.1.refs_0_), channel_id=1, source_target_pairs={{0,24},{4,28},{8,0},{12,4},{16,8},{20,12},{24,16},{28,20},{1,25},{... | collective-permute-start | bytes 1769480 | tf_op jit(solution)/shard_map/ppermute | solution.py:484
  178.6 22.3 %collective-permute-start.11 = (bf16[128,1536]{1,0:T(8,128)(2,1)}, bf16[128,1536]{1,0:T(8,128)(2,1)S(1)}, u32[]{:S(2)}, u32[]{:S(2)}) collective-permute-start(bf16[128,1536]{1,0:T(8,128)(2,1)} %get-tuple-element.41), channel_id=1, source_target_pairs={{0,1},{1,2},{2,3},{3,0},{4,5},{5,6},{6,7},{7,4},{8,9},{9,10},{10,1... | collective-permute-start | bytes 1179656 | tf_op jit(solution)/shard_map/ppermute | solution.py:489
  181.1 25.1 %collective-permute-start.12 = (bf16[128,1536]{1,0:T(8,128)(2,1)}, bf16[128,1536]{1,0:T(8,128)(2,1)S(1)}, u32[]{:S(2)}, u32[]{:S(2)}) collective-permute-start(bf16[128,1536]{1,0:T(8,128)(2,1)} %get-tuple-element.42), channel_id=1, source_target_pairs={{0,2},{1,3},{2,0},{3,1},{4,6},{5,7},{6,4},{7,5},{8,10},{9,11},{10,... | collective-permute-start | bytes 1179656 | tf_op jit(solution)/shard_map/ppermute | solution.py:489
  187.9 34.6 %collective-permute-start.30 = (bf16[384,768]{1,0:T(8,128)(2,1)S(1)}, bf16[384,768]{1,0:T(8,128)(2,1)S(1)}, u32[]{:S(2)}, u32[]{:S(2)}) collective-permute-start(bf16[384,768]{1,0:T(8,128)(2,1)S(1)} %copy-done.4), channel_id=1, source_target_pairs={{0,4},{4,0},{8,12},{12,8},{16,20},{20,16},{24,28},{28,24},{1,5},{5... | collective-permute-start | bytes 1769480 | tf_op jit(solution)/shard_map/ppermute | solution.py:494
  200.4 22.6 %collective-permute-start.31 = (bf16[384,768]{1,0:T(8,128)(2,1)S(1)}, bf16[384,768]{1,0:T(8,128)(2,1)S(1)}, u32[]{:S(2)}, u32[]{:S(2)}) collective-permute-start(bf16[384,768]{1,0:T(8,128)(2,1)S(1)} %collective-permute-done.27.refs_1_), channel_id=1, source_target_pairs={{0,4},{4,0},{8,12},{12,8},{16,20},{20,16},{24,28},{28,24},{1,5},{5... | collective-permute-start | bytes 1769480 | tf_op jit(solution)/shard_map/ppermute | solution.py:494
  200.4 33.4 %collective-permute-start.32 = (bf16[384,768]{1,0:T(8,128)(2,1)S(1)}, bf16[384,768]{1,0:T(8,128)(2,1)S(1)}, u32[]{:S(2)}, u32[]{:S(2)}) collective-permute-start(bf16[384,768]{1,0:T(8,128)(2,1)S(1)} %collective-permute-done.28.refs_2_), channel_id=1, source_target_pairs={{0,4},{4,0},{8,12},{12,8},{16,20},{20,16},{24,28},{28,24},{1,5},{5... | collective-permute-start | bytes 1769480 | tf_op jit(solution)/shard_map/ppermute | solution.py:494
  200.9 34.9 %collective-permute-start.33 = (bf16[384,768]{1,0:T(8,128)(2,1)S(1)}, bf16[384,768]{1,0:T(8,128)(2,1)S(1)}, u32[]{:S(2)}, u32[]{:S(2)}) collective-permute-start(bf16[384,768]{1,0:T(8,128)(2,1)S(1)} %collective-permute-done.29.refs_3_), channel_id=1, source_target_pairs={{0,4},{4,0},{8,12},{12,8},{16,20},{20,16},{24,28},{28,24},{1,5},{5... | collective-permute-start | bytes 1769480 | tf_op jit(solution)/shard_map/ppermute | solution.py:494
  226.4 32.4 %collective-permute-start.14 = (bf16[32,1536]{1,0:T(8,128)(2,1)S(1)}, bf16[32,1536]{1,0:T(8,128)(2,1)S(1)}, u32[]{:S(2)}, u32[]{:S(2)}) collective-permute-start(bf16[32,1536]{1,0:T(8,128)(2,1)S(1)} %get-tuple-element.78), channel_id=1, source_target_pairs={{0,24},{4,28},{8,0},{12,4},{16,8},{20,12},{24,16},{28,20},{1,25},{... | collective-permute-start | bytes 294920 | tf_op jit(solution)/shard_map/ppermute | solution.py:484
  228.8 30.0 %collective-permute-start.15 = (bf16[32,1536]{1,0:T(8,128)(2,1)S(1)}, bf16[32,1536]{1,0:T(8,128)(2,1)S(1)}, u32[]{:S(2)}, u32[]{:S(2)}) collective-permute-start(bf16[32,1536]{1,0:T(8,128)(2,1)S(1)} %get-tuple-element.77), channel_id=1, source_target_pairs={{0,16},{4,20},{8,24},{12,28},{16,0},{20,4},{24,8},{28,12},{1,17},{... | collective-permute-start | bytes 294920 | tf_op jit(solution)/shard_map/ppermute | solution.py:484
  229.1 29.8 %collective-permute-start.16 = (bf16[32,1536]{1,0:T(8,128)(2,1)S(1)}, bf16[32,1536]{1,0:T(8,128)(2,1)S(1)}, u32[]{:S(2)}, u32[]{:S(2)}) collective-permute-start(bf16[32,1536]{1,0:T(8,128)(2,1)S(1)} %get-tuple-element.76), channel_id=1, source_target_pairs={{0,8},{4,12},{8,16},{12,20},{16,24},{20,28},{24,0},{28,4},{1,9},{5... | collective-permute-start | bytes 294920 | tf_op jit(solution)/shard_map/ppermute | solution.py:484
  233.8 13.6 %collective-permute-start.20 = (bf16[2,4,1,1536]{3,2,1,0:T(2,128)(2,1)}, bf16[2,4,1,1536]{3,2,1,0:T(2,128)(2,1)S(1)}, u32[]{:S(2)}, u32[]{:S(2)}) collective-permute-start(bf16[2,4,1,1536]{3,2,1,0:T(2,128)(2,1)} %get-tuple-element.48), channel_id=1, source_target_pairs={{0,1},{1,2},{2,3},{3,4},{4,5},{5,6},{6,7},{7,8},{8,9},{9,10},{10,1... | collective-permute-start | bytes 73736 | tf_op jit(solution)/shard_map/ppermute | solution.py:479
  235.8 11.6 %collective-permute-start.21 = (bf16[2,4,1,1536]{3,2,1,0:T(2,128)(2,1)}, bf16[2,4,1,1536]{3,2,1,0:T(2,128)(2,1)S(1)}, u32[]{:S(2)}, u32[]{:S(2)}) collective-permute-start(bf16[2,4,1,1536]{3,2,1,0:T(2,128)(2,1)} %get-tuple-element.49), channel_id=1, source_target_pairs={{1,0},{2,1},{3,2},{4,3},{5,4},{6,5},{7,6},{8,7},{9,8},{10,9},{11,1... | collective-permute-start | bytes 73736 | tf_op jit(solution)/shard_map/ppermute | solution.py:479
  (48 other events, 336.3 us)
Sparse Core Ops, SparseCore 0:
  9.6 36.2 all-gather.5
  48.0 35.9 all-gather.3
  122.3 34.2 reduce-scatter.1

commit v4 on v3

--- a/solution.py
+++ b/solution.py
@@ -10,6 +10,7 @@
 DH = 192
 KW = 5
 VMEM_LIMIT = 56 * 1024 * 1024
+COST = pl.CostEstimate(flops=1000, bytes_accessed=1000, transcendentals=0)
 BF = jnp.bfloat16
 F32 = jnp.float32
 
@@ -132,6 +133,7 @@
             pltpu.VMEM(shape, BF),
         ],
         compiler_params=params(),
+        cost_estimate=COST,
         name="encoder_forward",
     )(at, pairs, low, high, conv_weight, norm_gain.reshape(1, width))
     return outs[0], outs[1], list(outs[2:])
@@ -168,6 +170,7 @@
         out_specs=[vmem] * 3,
         out_shape=[jax.ShapeDtypeStruct(slope.shape, BF)] + [edge] * 2,
         compiler_params=params(),
+        cost_estimate=COST,
         name="conv_gradient",
     )(at, *d_normed, skip, grad, norm_gain.reshape(1, -1), slope)
 
@@ -188,6 +191,7 @@
         out_specs=vmem,
         out_shape=jax.ShapeDtypeStruct(skip.shape, BF),
         compiler_params=params(),
+        cost_estimate=COST,
         name="mixed_sum",
     )(at, *terms, skip)
 
@@ -199,21 +203,21 @@
     def _():
         for parity in range(2):
             for shift in range(3):
-                turned[parity, shift] = turned_rows(d_ref, low_ref, high_ref, parity, shift)
+                turned[parity, shift] = turned_rows(d_ref, low_ref, high_ref, parity, shift).T
 
     for tap in range(KW):
 
         @pl.when(step == tap)
         def _():
             places = [KW - 1 - tap, KW - tap]
-            lhs = jnp.concatenate([turned[p % 2, p // 2] for p in places], axis=0)
-            term = dot(lhs, w_ref[0], NT)
+            rhs = jnp.concatenate([turned[p % 2, p // 2] for p in places], axis=1)
+            term = dot(w_ref[0], rhs, NN)
             if tap == 0:
                 acc[...] = term
             elif tap < KW - 1:
                 acc[...] += term
             else:
-                out_ref[...] = (acc[...] + term).astype(BF)
+                out_ref[...] = (acc[...] + term).T.astype(BF)
 
 
 def conv_back(d_conv, low, high, conv_weight):
@@ -232,12 +236,44 @@
         out_specs=whole((flat, c_in)),
         out_shape=jax.ShapeDtypeStruct((flat, c_in), BF),
         scratch_shapes=[
-            pltpu.VMEM((2, 3, seqs * rows, width), BF),
-            pltpu.VMEM((flat, c_in), F32),
+            pltpu.VMEM((2, 3, width, seqs * rows), BF),
+            pltpu.VMEM((c_in, flat), F32),
         ],
         compiler_params=params(),
+        cost_estimate=COST,
         name="encoder_backward",
     )(d_conv, low, high, conv_weight)
+
+
+def pack_kernel(w_ref, pack_ref, turned_ref):
+    for i in range(3):
+        for head in range(pack_ref.shape[0]):
+            part = w_ref[i, :, head * DH : (head + 1) * DH]
+            columns = slice(i * DH, (i + 1) * DH)
+            pack_ref[head, :, columns] = part
+            turned_ref[head, columns, :] = part.T
+
+
+def pack_weights(w_qkv):
+    _, width, local = w_qkv.shape
+    heads = local // DH
+    tile = local
+    return pl.pallas_call(
+        pack_kernel,
+        grid=(width // tile,),
+        in_specs=[pl.BlockSpec((3, tile, local), lambda n: (0, n, 0))],
+        out_specs=[
+            pl.BlockSpec((heads, tile, 3 * DH), lambda n: (0, n, 0)),
+            pl.BlockSpec((heads, 3 * DH, tile), lambda n: (0, 0, n)),
+        ],
+        out_shape=[
+            jax.ShapeDtypeStruct((heads, width, 3 * DH), BF),
+            jax.ShapeDtypeStruct((heads, 3 * DH, width), BF),
+        ],
+        compiler_params=params(),
+        cost_estimate=COST,
+        name="pack_weights",
+    )(w_qkv)
 
 
 def product_kernel(head_ref, x_ref, w_ref, out_ref, *, contract):
@@ -265,6 +301,7 @@
         ),
         out_shape=jax.ShapeDtypeStruct((rows, columns), BF),
         compiler_params=params(),
+        cost_estimate=COST,
         name=name,
     )(head, x, weight)
 
@@ -302,12 +339,12 @@
             else:
                 dk_acc[...] += dk
                 dv_acc[...] += dv
-            out_ref[rows, 0:DH] = o.astype(BF)
-            out_ref[rows, DH : 2 * DH] = dq.astype(BF)
+            out_ref[rows, 0:DH] = dq.astype(BF)
+            out_ref[rows, 3 * DH : 4 * DH] = o.astype(BF)
     for place, out_ref in enumerate((oa_ref, ob_ref)):
         rows = pl.ds(place * half, half)
-        out_ref[:, 2 * DH : 3 * DH] = (scale * dk_acc[rows, :]).astype(BF)
-        out_ref[:, 3 * DH : 4 * DH] = dv_acc[rows, :].astype(BF)
+        out_ref[:, DH : 2 * DH] = (scale * dk_acc[rows, :]).astype(BF)
+        out_ref[:, 2 * DH : 3 * DH] = dv_acc[rows, :].astype(BF)
 
 
 def attention(qkv_a, qkv_b, d_a, d_b):
@@ -323,53 +360,49 @@
             pltpu.VMEM((2 * half, DH), F32),
         ],
         compiler_params=params(),
+        cost_estimate=COST,
         name="attention",
     )(qkv_a, qkv_b, d_a, d_b)
 
 
-def term_kernel(head_ref, a_ref, b_ref, w_ref, *rest, first, last, contract):
-    out_refs, acc = rest[:-1], rest[-1]
-    step = pl.program_id(0)
-
-    @pl.when(step == 0)
-    def _():
-        acc[...] = dot(a_ref[:, first:last], w_ref[0], contract)
-
-    @pl.when(step == 1)
-    def _():
-        acc[...] += dot(b_ref[:, first:last], w_ref[0], contract)
-        count = len(out_refs)
-        if count == 1:
-            out_refs[0][...] = acc[...].astype(BF)
-            return
-        size = out_refs[0].shape[0]
+def term_kernel(head_ref, a_ref, b_ref, w_ref, *out_refs, first, last):
+    head = head_ref[0]
+    total = dot(a_ref[:, first:last], w_ref[head], NN)
+    total += dot(b_ref[:, first:last], w_ref[1 - head], NN)
+    count = len(out_refs)
+    size = out_refs[0].shape[0]
+    value = total.astype(BF)
+    if count == 1:
+        out_refs[0][...] = value
+        return
+    for block in range(count):
         for slot, out_ref in enumerate(out_refs):
-            block = wrapped(head_ref[1] + slot, count)
-            rows = pl.ds(pl.multiple_of(block * size, size), size)
-            out_ref[...] = acc[rows, :].astype(BF)
-
-
-def pair_term(place, mine, got, weight, width, slots, first, last, contract, name):
+
+            @pl.when(wrapped(block - head_ref[1], count) == slot)
+            def _():
+                out_ref[...] = value[block * size : (block + 1) * size]
+
+
+def pair_term(place, mine, got, weight, slots, first, last, name):
     half, full = mine.shape
+    heads, depth, width = weight.shape
     size = half // slots
-    return pl.pallas_call(
-        functools.partial(term_kernel, first=first, last=last, contract=contract),
+    tile = 512 if width % 512 == 0 else width
+    return pl.pallas_call(
+        functools.partial(term_kernel, first=first, last=last),
         grid_spec=pltpu.PrefetchScalarGridSpec(
             num_scalar_prefetch=1,
-            grid=(2,),
+            grid=(width // tile,),
             in_specs=[
-                pl.BlockSpec((half, full), lambda i, at: (0, 0)),
-                pl.BlockSpec((half, full), lambda i, at: (0, 0)),
-                pl.BlockSpec(
-                    (1,) + weight.shape[1:],
-                    lambda i, at: (jnp.where(i == 0, at[0], 1 - at[0]), 0, 0),
-                ),
+                pl.BlockSpec((half, full), lambda n, at: (0, 0)),
+                pl.BlockSpec((half, full), lambda n, at: (0, 0)),
+                pl.BlockSpec((heads, depth, tile), lambda n, at: (0, 0, n)),
             ],
-            out_specs=[pl.BlockSpec((size, width), lambda i, at: (0, 0))] * slots,
-            scratch_shapes=[pltpu.VMEM((half, width), F32)],
+            out_specs=[pl.BlockSpec((size, tile), lambda n, at: (0, n))] * slots,
         ),
         out_shape=[jax.ShapeDtypeStruct((size, width), BF)] * slots,
         compiler_params=params(),
+        cost_estimate=COST,
         name=name,
     )(place, mine, got, weight)
 
@@ -386,20 +419,32 @@
         sum_kernel,
         out_shape=jax.ShapeDtypeStruct(parts[0].shape, BF),
         compiler_params=params(),
+        cost_estimate=COST,
         name=name,
     )(*parts)
 
 
-def weight_kernel(at_ref, xa_ref, xb_ref, ga_ref, gb_ref, ra_ref, rb_ref, *out_refs):
+def weight_kernel(at_ref, xa_ref, xb_ref, ga_ref, gb_ref, ra_ref, rb_ref, *rest):
     del at_ref
-    qkv = dot(xa_ref[...], ra_ref[:, DH:], TN) + dot(xb_ref[...], rb_ref[:, DH:], TN)
-    out = dot(ga_ref[...], ra_ref[:, :DH], TN) + dot(gb_ref[...], rb_ref[:, :DH], TN)
+    out_refs, turned = rest[:-1], rest[-1]
+    step = pl.program_id(0)
+    half = ra_ref.shape[0]
+    split = 3 * DH
+
+    @pl.when(step == 0)
+    def _():
+        turned[:, :half] = ra_ref[...].T
+        turned[:, half:] = rb_ref[...].T
+
+    a, b = slice(0, half), slice(half, 2 * half)
+    qkv = dot(turned[:split, a], xa_ref[...], NN) + dot(turned[:split, b], xb_ref[...], NN)
+    out = dot(turned[split:, a], ga_ref[...], NN) + dot(turned[split:, b], gb_ref[...], NN)
     for slot, out_ref in enumerate(out_refs):
 
-        @pl.when(pl.program_id(0) == slot)
+        @pl.when(step == slot)
         def _():
-            out_ref[:, : 3 * DH] = qkv.astype(BF)
-            out_ref[:, 3 * DH :] = out.astype(BF)
+            out_ref[:split, :] = qkv.astype(BF)
+            out_ref[split:, :] = out.astype(BF)
 
 
 def weight_gradients(at, xa, xb, ga, gb, ra, rb, seqs):
@@ -414,61 +459,75 @@
             num_scalar_prefetch=1,
             grid=(seqs,),
             in_specs=[column] * 4 + [rest] * 2,
-            out_specs=[pl.BlockSpec((chunk, full), lambda r, at: (0, 0))] * seqs,
+            out_specs=[pl.BlockSpec((full, chunk), lambda r, at: (0, 0))] * seqs,
+            scratch_shapes=[pltpu.VMEM((full, 2 * half), BF)],
         ),
-        out_shape=[jax.ShapeDtypeStruct((chunk, full), BF)] * seqs,
-        compiler_params=params(),
+        out_shape=[jax.ShapeDtypeStruct((full, chunk), BF)] * seqs,
+        compiler_params=params(),
+        cost_estimate=COST,
         name="weight_gradients",
     )(at, xa, xb, ga, gb, ra, rb)
 
 
-def unpack_kernel(at_ref, *refs):
-    seqs = (len(refs) - 2) // 2
-    qkv_ref, out_ref = refs[-2:]
-    step = pl.program_id(0)
-    first_head = at_ref[1] == 0
-    for slot in range(seqs):
-
-        @pl.when(step == slot)
-        def _():
-            mine = refs[slot][...].astype(F32)
-            other = refs[seqs + slot][...].astype(F32)
-            low = jnp.where(first_head, mine, other)
-            high = jnp.where(first_head, other, mine)
-            for i in range(3):
-                columns = slice(i * DH, (i + 1) * DH)
-                qkv_ref[i] = jnp.concatenate([low[:, columns], high[:, columns]], axis=1)
-            out_ref[:DH, :] = low[:, 3 * DH :].T
-            out_ref[DH:, :] = high[:, 3 * DH :].T
+def weight_sum_kernel(*refs):
+    out_ref = refs[-1]
+    split = 3 * DH
+    total = refs[0][...].astype(F32)
+    for ref in refs[1:-1]:
+        total = total + ref[...].astype(F32)
+    out_ref[:, :split] = total[:split].T.astype(BF)
+    for part in range(2):
+        rows = slice(part * DH, (part + 1) * DH)
+        out_ref[rows, split:] = total[split:, rows].astype(BF)
+
+
+def weight_sum(parts):
+    full, chunk = parts[0].shape
+    return pl.pallas_call(
+        weight_sum_kernel,
+        out_shape=jax.ShapeDtypeStruct((chunk, full), BF),
+        compiler_params=params(),
+        cost_estimate=COST,
+        name="weight_sum",
+    )(*parts)
+
+
+def unpack_kernel(at_ref, mine_ref, other_ref, qkv_ref, out_ref):
+    first_head = at_ref[0] == 0
+    mine = mine_ref[0].astype(F32)
+    other = other_ref[0].astype(F32)
+    low = jnp.where(first_head, mine, other)
+    high = jnp.where(first_head, other, mine)
+    split = 3 * DH
+    for i in range(3):
+        columns = slice(i * DH, (i + 1) * DH)
+        qkv_ref[i] = jnp.concatenate([low[:, columns], high[:, columns]], axis=1)
+    for head, value in enumerate((low, high)):
+        halves = [value[part * DH : (part + 1) * DH, split:] for part in range(2)]
+        out_ref[head * DH : (head + 1) * DH, :] = jnp.concatenate(halves, axis=1)
 
 
 def unpack_weights(at, mine, other):
-    seqs = len(mine)
-    chunk, full = mine[0].shape
+    seqs, chunk, full = mine.shape
     width = chunk * seqs
     local = 2 * DH
-
-    def place(r, at):
-        return lax.rem(at[0] - r + seqs, seqs)
-
+    block = pl.BlockSpec((1, chunk, full), lambda r: (r, 0, 0))
     return pl.pallas_call(
         unpack_kernel,
-        grid_spec=pltpu.PrefetchScalarGridSpec(
-            num_scalar_prefetch=1,
-            grid=(seqs,),
-            in_specs=[pl.BlockSpec((chunk, full), lambda r, at: (0, 0))] * (2 * seqs),
-            out_specs=[
-                pl.BlockSpec((3, chunk, local), lambda r, at: (0, place(r, at), 0)),
-                pl.BlockSpec((local, chunk), lambda r, at: (0, place(r, at))),
-            ],
-        ),
+        grid=(seqs,),
+        in_specs=[SCALARS, block, block],
+        out_specs=[
+            pl.BlockSpec((3, chunk, local), lambda r: (0, r, 0)),
+            pl.BlockSpec((local, chunk), lambda r: (0, r)),
+        ],
         out_shape=[
             jax.ShapeDtypeStruct((3, width, local), F32),
             jax.ShapeDtypeStruct((local, width), F32),
         ],
         compiler_params=params(),
+        cost_estimate=COST,
         name="weight_outputs",
-    )(at, *mine, *other)
+    )(at, mine, other)
 
 
 def neighbour_edges(first, last):
@@ -477,6 +536,10 @@
     forward = [(i, i + 1) for i in range(count - 1)]
     backward = [(target, source) for source, target in forward]
     return lax.ppermute(last, axes, forward), lax.ppermute(first, axes, backward)
+
+
+def after(value, *others):
+    return lax.optimization_barrier((value,) + others)[0]
 
 
 def send_chip(x, step, heads):
@@ -519,65 +582,70 @@
 
     grad = jnp.transpose(grad_out, (1, 0, 2))
     grad_z = lax.all_gather(grad, "head", axis=0, tiled=False)
+    pairs = jnp.transpose(enc_in.reshape(rows, 2, seqs, enc_in.shape[2]), (1, 2, 0, 3))
+    low, high = neighbour_edges(pairs[:, :, :1, :], pairs[:, :, -1:, :])
+    skip, slope, normed = encoder(at, pairs, low, high, conv_weight, norm_gain)
+    normed_slab = jnp.concatenate(to_chips(normed), axis=0)
+    normed_rows = lax.all_gather(normed_slab, "head", axis=0, tiled=True)
+
+    grad_z = after(grad_z, normed_slab)
     grad_slots = [
         lax.dynamic_index_in_dim(grad_z, (own_seq + r) % seqs, 1, keepdims=False)
         for r in range(seqs)
     ]
     grad_rows = jnp.stack(to_chips(grad_slots), axis=1).reshape(half, width)
-
-    pairs = jnp.transpose(enc_in.reshape(rows, 2, seqs, enc_in.shape[2]), (1, 2, 0, 3))
-    low, high = neighbour_edges(pairs[:, :, :1, :], pairs[:, :, -1:, :])
-    skip, slope, normed = encoder(at, pairs, low, high, conv_weight, norm_gain)
-    normed_slab = jnp.concatenate(to_chips(normed), axis=0)
-    normed_rows = lax.all_gather(normed_slab, "head", axis=0, tiled=True)
-
-    w_pack = jnp.transpose(w_qkv.reshape(3, width, heads, DH), (2, 1, 0, 3))
-    w_pack = w_pack.reshape(heads, width, 3 * DH)
+    w_pack, w_turned = pack_weights(after(w_qkv, normed_slab))
     w_rows = w_out.reshape(heads, DH, width)
     d_got = swap_heads(head_product(head_other, grad_rows, w_rows, NT, "d_o_other"))
     d_mine = head_product(head_mine, grad_rows, w_rows, NT, "d_o_own")
+    grad_swapped = swap_heads(grad_rows)
+    normed_rows = after(normed_rows, d_got, d_mine, grad_swapped, w_pack, w_turned)
+
     qkv_got = swap_heads(head_product(head_other, normed_rows, w_pack, NN, "qkv_other"))
+    normed_swapped = swap_heads(normed_rows)
     qkv_mine = head_product(head_mine, normed_rows, w_pack, NN, "qkv_own")
+    qkv_mine = after(qkv_mine, normed_swapped)
     result_mine, result_other = attention(qkv_mine, qkv_got, d_mine, d_got)
     result_got = swap_heads(result_other)
 
     plain = jnp.stack([own_head, zero])
-    (d_term,) = pair_term(
-        plain, result_mine, result_got, w_pack, width, 1, DH, 4 * DH, NT, "d_term"
-    )
+    (d_term,) = pair_term(plain, result_mine, result_got, w_turned, 1, 0, 3 * DH, "d_term")
     d_normed = lax.psum_scatter(
         d_term.reshape(groups, seqs, rows, width), "head", scatter_dimension=0, tiled=False
     )
-
-    turned = jnp.stack([own_head, own_z])
-    head_term = pair_term(
-        turned, result_mine, result_got, w_rows, width, groups, 0, DH, NN, "head_term"
-    )
-    head_term, d_normed = lax.optimization_barrier((head_term, d_normed))
-    d_normed = from_chips([d_normed[r] for r in range(seqs)])
-    head_sum = summed(
-        [head_term[q] if q == 0 else send_z(head_term[q], q) for q in range(groups)], "head_sum"
-    ).reshape(seqs, rows, width)
-    head_sum = from_chips([head_sum[r] for r in range(seqs)])
-    mixed = mixed_call(at, head_sum, skip)
-
     part = weight_gradients(
         own_seq.reshape(1),
         normed_rows,
-        swap_heads(normed_rows),
+        normed_swapped,
         grad_rows,
-        swap_heads(grad_rows),
+        grad_swapped,
         result_mine,
         result_other,
         seqs,
     )
-    chunk = summed(to_chips(part), "weight_sum")
-    chunks = [chunk if r == 0 else send_chip(chunk, r, heads) for r in range(seqs)]
-    grad_w_qkv, grad_w_out = unpack_weights(at, chunks, [swap_heads(c) for c in chunks])
+    part = to_chips(part)
+    turned = jnp.stack([own_head, own_z])
+    head_term = pair_term(
+        turned, result_mine, result_got, w_rows, groups, 3 * DH, 4 * DH, "head_term"
+    )
+    head_slots = [head_term[0], send_z(head_term[1], 1)]
+    head_slots += [send_z(after(head_term[q], d_normed), q) for q in range(2, groups)]
+    part = [after(p, d_normed) for p in part]
+    d_normed = from_chips([d_normed[r] for r in range(seqs)])
+    chunk = weight_sum(part)
+    same_head = [[b * heads + h for b in range(seqs)] for h in range(heads)]
+    chunks = lax.all_gather(chunk, "seq", axis_index_groups=same_head)
 
     d_conv, first, last = conv_gradient(at, d_normed, skip, grad, norm_gain, slope)
     low, high = neighbour_edges(first, last)
     grad_input = conv_back(d_conv, low, high, conv_weight)
+
+    head_slots = [after(h, low, high) for h in head_slots]
+    head_sum = summed(head_slots, "head_sum").reshape(seqs, rows, width)
+    head_sum = from_chips([head_sum[r] for r in range(seqs)])
+    mixed = mixed_call(at, head_sum, skip)
+    chunks = after(chunks, grad_input)
+    grad_w_qkv, grad_w_out = unpack_weights(head_mine, chunks, swap_heads(chunks))
     grad_input = jnp.transpose(grad_input.reshape(2, seqs, rows, -1), (2, 0, 1, 3))
     return (
         jnp.transpose(mixed, (1, 0, 2)),
@@ -727,7 +795,9 @@
 
 def body(enc_in, conv_weight, norm_gain, w_qkv, w_out, grad_out):
     heads = w_qkv.shape[2] // DH
-    fits = heads == 2 and enc_in.shape[1] * heads == lax.axis_size("seq")
+    seqs = enc_in.shape[1]
+    fits = heads == 2 and seqs * heads == lax.axis_size("seq")
+    fits = fits and conv_weight.shape[2] == seqs * w_qkv.shape[2]
     chosen = unit_body if fits else gathered_body
     return chosen(enc_in, conv_weight, norm_gain, w_qkv, w_out, grad_out)
 

time: 276 us -> 270 us (0.978); the launches traced: 270 us -> 268 us
  local copies, waits for them, and re-layouts: 31.3 us -> 21.5 us
  waiting for transfers between devices: 101 us -> 110 us
  Pallas kernels: 80.8 us -> 87.2 us
  other arithmetic: 5.43 us -> 1.46 us
  starting transfers between devices: 37.9 us -> 34.4 us
    ppermute x3, waiting for transfers between devices: 14.7 us -> 34.4 us  [send_z(): lax.ppermute(x, 'head', [(z, (z + step) % count) for z in range(count)])]
    all_gather x1, waiting for transfers between devices: 21.4 us -> 2.55 us  [unit_body(): normed_rows = lax.all_gather(normed_slab, 'head', axis=0, tiled=True)]
    pallas_call x3 -> x5, Pallas kernels: 19.2 us -> 28.5 us  [the longest x2 12.2 us: pair_term(): pl.pallas_call(functools.partial(term_kernel, first=first, last=last), gr...]
    reduce_scatter x1, waiting for transfers between devices: 0.01 us -> 8.45 us  [unit_body(): lax.psum_scatter(d_term.reshape(groups, seqs, rows, width), 'head', scatt...]
    all_gather x0 -> x1, waiting for transfers between devices: none -> 6.56 us  [unit_body(): chunks = lax.all_gather(chunk, 'seq', axis_index_groups=same_head)]
    ppermute x9 -> x6, waiting for transfers between devices: 6.11 us -> 1.49 us  [swap_heads(): lax.ppermute(x, 'seq', [(s, s + 1 - 2 * (s % 2)) for s in range(count)])]
    reshape x1 -> x0, local copies, waits for them, and re-layouts: 3.7 us -> none  [unit_body(): w_pack = w_pack.reshape(heads, width, 3 * DH)]
    ppermute x18 -> x15, starting transfers between devices: 21.8 us -> 18.4 us  [send_chip(): lax.ppermute(x, 'seq', [(s, (s + step * heads) % count) for s in range(co...]
  transfers between devices with their start and end apart: 37 -> 32, of which waited for: 15 -> 23; matrix products, arithmetic and copies ran while one was open for 9% -> 4% of each run, Pallas kernels for 23% -> 23%
where the time goes in v4:
time: 270 us; the launch traced here: 268 us
  waiting for transfers between devices  110 us (41%)
  Pallas kernels  87.2 us (32%)
  starting transfers between devices  34.4 us (13%)
  local copies, waits for them, and re-layouts  21.5 us (8%)
  between operations  14 us (5%)
    ppermute x15, waiting for transfers between devices, send_chip(): lax.ppermute(x, 'seq', [(s, (s + step * heads) % count) for s in range(co...  46.8 us
    ppermute x3, waiting for transfers between devices, send_z(): lax.ppermute(x, 'head', [(z, (z + step) % count) for z in range(count)])  34.4 us
    ppermute x15, starting transfers between devices, send_chip(): lax.ppermute(x, 'seq', [(s, (s + step * heads) % count) for s in range(co...  18.4 us
    unnamed x61, local copies, waits for them, and re-layouts  15 us
    pallas_call x4, Pallas kernels, head_product(): pl.pallas_call(functools.partial(product_kernel, contract=contract), grid...  14.8 us
    pallas_call x2, Pallas kernels, pair_term(): pl.pallas_call(functools.partial(term_kernel, first=first, last=last), gr...  12.2 us
    pallas_call x1, Pallas kernels, encoder(): pl.pallas_call(conv_kernel, grid=(width // tile,), in_specs=[SCALARS, who...  10.1 us
    pallas_call x1, Pallas kernels, attention(): pl.pallas_call(functools.partial(attention_kernel, block=min(256, half)),...  8.85 us
  transfers between devices with their start and end apart: 32, of which 23 were waited for; matrix products, arithmetic and copies ran while one was open for 4% of the time, Pallas kernels for 23%

profile of v4, /device:TPU:26, one launch (start us, length us, event | category | flops | bytes accessed | tf_op | source)
XLA Modules:
  0.0 268.2 jit_solution(379438168035278143)
XLA Ops:
  12.6 5.0 %collective-permute-start = (bf16[2,4,1,768]{3,2,1,0:T(2,128)(2,1)S(1)}, bf16[2,4,1,768]{3,2,1,0:T(2,128)(2,1)S(1)}, u32[]{:S(2)}, u32[]{:S(2)}) collective-permute-start(bf16[2,4,1,768]{3,2,1,0:T(2,128)(2,1)S(1)} %get-tuple-element.105), channel_id=1, source_target_pairs={{0,1},{1,2},{2,3},{3,4},{4,5},{5,6},{6,7},{7,8},{8,9},{9,10},{10,1... | collective-permute-start | bytes 36872 | tf_op jit(solution)/shard_map/ppermute | solution.py:538
  20.1 10.1 %encoder_forward.1 = (bf16[4,32,1536]{2,1,0:T(8,128)(2,1)}, f32[2,4,32,1536]{3,2,1,0:T(8,128)}, bf16[32,1536]{1,0:T(8,128)(2,1)}, bf16[32,1536]{1,0:T(8,128)(2,1...) custom-call(s32[2]{0:T(128)} %pad_add_fusion.at_ref, bf16[2,4,32,768]{3,2,1,0:T(8,128)(2,1)} %bitcast.52, ...), custom_call_target="tpu_custom_call" | custom-call | flops 1000 | bytes 1000 | tf_op jit(solution)/shard_map/encoder_forward/pallas_call | solution.py:109
  35.5 3.7 %collective-permute-done.3 = bf16[32,1536]{1,0:T(8,128)(2,1)S(1)} collective-permute-done((bf16[32,1536]{1,0:T(8,128)(2,1)}, bf16[32,1536]{1,0:T(8,128)(2,1)S(1)}, u32[]{:S(2)}, u32[]{:S(2)}) %collective-permute-start.3) | collective-permute-done | bytes 98336 | tf_op jit(solution)/shard_map/ppermute | solution.py:547
  40.1 5.5 %all-gather.8.cloned.1.call-done = bf16[16,32,1536]{2,1,0:T(8,128)(2,1)} async-done(((bf16[4,32,1536]{2,1,0:T(8,128)(2,1)}), bf16[16,32,1536]{2,1,0:T(8,128)(2,1)}) %all-gather.8.cloned.1.call-update) | async-done | bytes 1572880 | tf_op jit(solution)/shard_map/all_gather | solution.py:584
  51.5 8.5 %collective-permute-done.7 = bf16[4,32,1536]{2,1,0:T(8,128)(2,1)S(1)} collective-permute-done((bf16[4,32,1536]{2,1,0:T(8,128)(2,1)S(1)}, bf16[4,32,1536]{2,1,0:T(8,128)(2,1)S(1)}, u32[]{:S(2)}, u32[]{:S(2)}) %collective-permute-start.7) | collective-permute-done | bytes 393248 | tf_op jit(solution)/shard_map/ppermute | solution.py:547
  60.0 6.6 %collective-permute-done.6 = bf16[4,32,1536]{2,1,0:T(8,128)(2,1)S(1)} collective-permute-done((bf16[4,32,1536]{2,1,0:T(8,128)(2,1)S(1)}, bf16[4,32,1536]{2,1,0:T(8,128)(2,1)S(1)}, u32[]{:S(2)}, u32[]{:S(2)}) %collective-permute-start.6) | collective-permute-done | bytes 393248 | tf_op jit(solution)/shard_map/ppermute | solution.py:547
  71.7 6.8 %pack_weights.1 = (bf16[2,1536,576]{2,1,0:T(8,128)(2,1)}, bf16[2,576,1536]{2,1,0:T(8,128)(2,1)}) custom-call(bf16[3,1536,384]{2,1,0:T(8,128)(2,1)} %w_ref.3), custom_call_target="tpu_custom_call" | custom-call | flops 1000 | bytes 1000 | tf_op jit(solution)/shard_map/pack_weights/pallas_call | solution.py:261
  83.9 4.8 %qkv_other.1 = bf16[512,640]{1,0:T(8,128)(2,1)} custom-call(s32[1]{0:T(128)} %bitcast.5.head_ref, bf16[512,1536]{1,0:T(8,128)(2,1)} %all-gather.6.cloned.1.call-done.x_ref.xa_ref, bf16[2,1536,576]{2,1,0:T(8,128)(2,1)} %get-tuple-element.48.w_ref), custom_call_target="tpu_custom_call" | custom-call | flops 1000 | bytes 1000 | tf_op jit(solution)/shard_map/qkv_other/pallas_call | solution.py:291
  88.8 4.3 %qkv_own.1.qa_ref = bf16[512,640]{1,0:T(8,128)(2,1)} custom-call(s32[1]{0:T(128)} %bitcast.1.head_ref.at_ref, bf16[512,1536]{1,0:T(8,128)(2,1)} %all-gather.6.cloned.1.call-done.x_ref.xa_ref, bf16[2,1536,576]{2,1,0:T(8,128)(2,1)} %get-tuple-element.48.w_ref), custom_call_target="tpu_custom_call" | custom-call | flops 1000 | bytes 1000 | tf_op jit(solution)/shard_map/qkv_own/pallas_call | solution.py:291
  93.9 8.8 %attention.1 = (bf16[512,768]{1,0:T(8,128)(2,1)}, bf16[512,768]{1,0:T(8,128)(2,1)}) custom-call(bf16[512,640]{1,0:T(8,128)(2,1)} %qkv_own.1.qa_ref, bf16[512,640]{1,0:T(8,128)(2,1)} %copy-done.7, bf16[512,256]{1,0:T(8,128)(2,1)} %d_o_own.1.da_ref, bf16[512,256]{1,0:T(8,128)(2,1)} %copy-done.16), custom_call_target="tpu_custom_call" | custom-call | flops 1000 | bytes 1000 | tf_op jit(solution)/shard_map/attention/pallas_call | solution.py:353
  106.3 6.6 %d_term.1 = bf16[512,1536]{1,0:T(8,128)(2,1)} custom-call(s32[2]{0:T(128)} %get-tuple-element.107.head_ref, bf16[512,768]{1,0:T(8,128)(2,1)} %get-tuple-element.52.a_ref.ra_ref, bf16[512,768]{1,0:T(8,128)(2,1)} %copy-done.1, bf16[2,576,1536]{2,1,0:T(8,128)(2,1)} %get-tuple-element.49.w_ref), custom_call_target="tpu_custom_call" | custom-call | flops 1000 | bytes 1000 | tf_op jit(solution)/shard_map/d_term/pallas_call | solution.py:391
  113.0 8.6 %weight_gradients.1 = (bf16[768,384]{1,0:T(8,128)(2,1)}, bf16[768,384]{1,0:T(8,128)(2,1)}, bf16[768,384]{1,0:T(8,128)(2,1)}, bf16[768,384]{1,0:T(8,128)(2,1)}) custom-call(s32[1]{0:T(128)} %bitcast.at_ref, bf16[512,1536]{1,0:T(8,128)(2,1)} %all-gather.6.cloned.1.call-done.x_ref.xa_ref, bf16[512,1536]{1,0:T(8,128)(2,1)} %copy-done.6, ...), custom_call_target="tpu_custom_call" | custom-call | flops 1000 | bytes 1000 | tf_op jit(solution)/shard_map/weight_gradients/pallas_call | solution.py:456
  126.1 12.9 %collective-permute-done.26.refs_3_ = bf16[768,384]{1,0:T(8,128)(2,1)S(1)} collective-permute-done((bf16[768,384]{1,0:T(8,128)(2,1)}, bf16[768,384]{1,0:T(8,128)(2,1)S(1)}, u32[]{:S(2)}, u32[]{:S(2)}) %collective-permute-start.26) | collective-permute-done | bytes 589856 | tf_op jit(solution)/shard_map/ppermute | solution.py:547
  139.0 8.5 %reduce-scatter.2.cloned.1.call-done = bf16[1,4,32,1536]{3,2,1,0:T(8,128)(2,1)} async-done(((bf16[4,4,32,1536]{3,2,1,0:T(8,128)(2,1)}), bf16[1,4,32,1536]{3,2,1,0:T(8,128)(2,1)}) %reduce-scatter.2.cloned.1.call-update) | async-done | bytes 393232 | tf_op jit(solution)/shard_map/reduce_scatter | solution.py:613
  165.0 3.3 %conv_gradient.1 = (bf16[2,4,32,1536]{3,2,1,0:T(8,128)(2,1)}, bf16[2,4,1,1536]{3,2,1,0:T(2,128)(2,1)}, bf16[2,4,1,1536]{3,2,1,0:T(2,128)(2,1)}) custom-call(s32[2]{0:T(128)} %pad_add_fusion.at_ref, bf16[32,1536]{1,0:T(8,128)(2,1)} %get-tuple-element.103.refs_0_, bf16[32,1536]{1,0:T(8,128)(2,1)} %copy-done.22, bf16[32,1536]{1,0:T(8,128)(2,1)} %copy-done.21, ...), custom_call_target="tpu_custom_call" | custom-call | flops 1000 | bytes 1000 | tf_op jit(solution)/shard_map/conv_gradient/pallas_call | solution.py:167
  170.2 3.9 %collective-permute-start.17 = (bf16[2,4,1,1536]{3,2,1,0:T(2,128)(2,1)}, bf16[2,4,1,1536]{3,2,1,0:T(2,128)(2,1)S(1)}, u32[]{:S(2)}, u32[]{:S(2)}) collective-permute-start(bf16[2,4,1,1536]{3,2,1,0:T(2,128)(2,1)} %get-tuple-element.58), channel_id=1, source_target_pairs={{1,0},{2,1},{3,2},{4,3},{5,4},{6,5},{7,6},{8,7},{9,8},{10,9},{11,1... | collective-permute-start | bytes 73736 | tf_op jit(solution)/shard_map/ppermute | solution.py:538
  174.5 3.1 %collective-permute-done.17.high_ref = bf16[2,4,1,1536]{3,2,1,0:T(2,128)(2,1)S(1)} collective-permute-done((bf16[2,4,1,1536]{3,2,1,0:T(2,128)(2,1)}, bf16[2,4,1,1536]{3,2,1,0:T(2,128)(2,1)S(1)}, u32[]{:S(2)}, u32[]{:S(2)}) %collective-permute-start.17) | collective-permute-done | bytes 24608 | tf_op jit(solution)/shard_map/ppermute | solution.py:538
  178.2 8.6 %encoder_backward.1 = bf16[256,768]{1,0:T(8,128)(2,1)} custom-call(bf16[2,4,32,1536]{3,2,1,0:T(8,128)(2,1)} %get-tuple-element.68.d_ref, bf16[2,4,1,1536]{3,2,1,0:T(2,128)(2,1)} %copy-done.23, bf16[2,4,1,1536]{3,2,1,0:T(2,128)(2,1)} %copy-done.24, bf16[5,768,1536]{2,1,0:T(8,128)(2,1)} %w_ref.4), custom_call_target="tpu_custom_call" | custom-call | flops 1000 | bytes 1000 | tf_op jit(solution)/shard_map/encoder_backward/pallas_call | solution.py:227
  186.8 6.6 %all-gather.10.cloned.1.call-done = bf16[1536,768]{1,0:T(8,128)(2,1)} async-done(((bf16[384,768]{1,0:T(8,128)(2,1)}), bf16[1536,768]{1,0:T(8,128)(2,1)}) %all-gather.10.cloned.1.call-update) | async-done | bytes 2359312 | tf_op jit(solution)/shard_map/all_gather | solution.py:637
  193.4 5.5 %head_term.1 = (bf16[128,1536]{1,0:T(8,128)(2,1)}, bf16[128,1536]{1,0:T(8,128)(2,1)}, bf16[128,1536]{1,0:T(8,128)(2,1)}, bf16[128,1536]{1,0:T(8,128)(2,1)}) custom-call(s32[2]{0:T(128)} %get-tuple-element.106.head_ref, bf16[512,768]{1,0:T(8,128)(2,1)} %get-tuple-element.52.a_ref.ra_ref, bf16[512,768]{1,0:T(8,128)(2,1)} %copy-done.1, ...), custom_call_target="tpu_custom_call" | custom-call | flops 1000 | bytes 1000 | tf_op jit(solution)/shard_map/head_term/pallas_call | solution.py:391
  201.0 9.9 %collective-permute-done.18.refs_1_ = bf16[128,1536]{1,0:T(8,128)(2,1)S(1)} collective-permute-done((bf16[128,1536]{1,0:T(8,128)(2,1)}, bf16[128,1536]{1,0:T(8,128)(2,1)S(1)}, u32[]{:S(2)}, u32[]{:S(2)}) %collective-permute-start.18) | collective-permute-done | bytes 393248 | tf_op jit(solution)/shard_map/ppermute | solution.py:552
  210.9 24.5 %collective-permute-done.19.refs_2_ = bf16[128,1536]{1,0:T(8,128)(2,1)S(1)} collective-permute-done((bf16[128,1536]{1,0:T(8,128)(2,1)}, bf16[128,1536]{1,0:T(8,128)(2,1)S(1)}, u32[]{:S(2)}, u32[]{:S(2)}) %collective-permute-start.19) | collective-permute-done | bytes 393248 | tf_op jit(solution)/shard_map/ppermute | solution.py:552
  245.5 3.2 %collective-permute-done.22.refs_2_ = bf16[32,1536]{1,0:T(8,128)(2,1)S(1)} collective-permute-done((bf16[32,1536]{1,0:T(8,128)(2,1)S(1)}, bf16[32,1536]{1,0:T(8,128)(2,1)S(1)}, u32[]{:S(2)}, u32[]{:S(2)}) %collective-permute-start.22) | collective-permute-done | bytes 98336 | tf_op jit(solution)/shard_map/ppermute | solution.py:547
  254.9 6.7 %weight_outputs.1 = (f32[3,1536,384]{2,1,0:T(8,128)}, f32[384,1536]{1,0:T(8,128)}) custom-call(s32[1]{0:T(128)} %bitcast.1.head_ref.at_ref, bf16[4,384,768]{2,1,0:T(8,128)(2,1)} %bitcast.50, bf16[4,384,768]{2,1,0:T(8,128)(2,1)} %copy-done.2), custom_call_target="tpu_custom_call" | custom-call | flops 1000 | bytes 1000 | tf_op jit(solution)/shard_map/weight_outputs/pallas_call | solution.py:515
  (132 shorter events, 77.8 us)
Async XLA Ops:
  7.2 38.4 %all-gather.8.cloned.1.call-start = ((), (), s32[]{:S(2)}) async-start(), calls=%async_computation.3 | async-start | bytes 1966080 | tf_op jit(solution)/shard_map/all_gather | solution.py:584
  9.1 74.8 %all-gather.6.cloned.1.call-start = ((), (), s32[]{:S(2)}) async-start(), calls=%async_computation.1 | async-start | bytes 1966080 | tf_op jit(solution)/shard_map/all_gather | solution.py:589
  10.3 8.6 %collective-permute-start.1 = (bf16[2,4,1,768]{3,2,1,0:T(2,128)(2,1)S(1)}, bf16[2,4,1,768]{3,2,1,0:T(2,128)(2,1)S(1)}, u32[]{:S(2)}, u32[]{:S(2)}) collective-permute-start(bf16[2,4,1,768]{3,2,1,0:T(2,128)(2,1)S(1)} %get-tuple-element.104), channel_id=1, source_target_pairs={{1,0},{2,1},{3,2},{4,3},{5,4},{6,5},{7,6},{8,7},{9,8},{10,9},{11,1... | collective-permute-start | bytes 36872 | tf_op jit(solution)/shard_map/ppermute | solution.py:538
  12.6 6.5 %collective-permute-start = (bf16[2,4,1,768]{3,2,1,0:T(2,128)(2,1)S(1)}, bf16[2,4,1,768]{3,2,1,0:T(2,128)(2,1)S(1)}, u32[]{:S(2)}, u32[]{:S(2)}) collective-permute-start(bf16[2,4,1,768]{3,2,1,0:T(2,128)(2,1)S(1)} %get-tuple-element.105), channel_id=1, source_target_pairs={{0,1},{1,2},{2,3},{3,4},{4,5},{5,6},{6,7},{7,8},{8,9},{9,10},{10,1... | collective-permute-start | bytes 36872 | tf_op jit(solution)/shard_map/ppermute | solution.py:538
  31.7 7.5 %collective-permute-start.3 = (bf16[32,1536]{1,0:T(8,128)(2,1)}, bf16[32,1536]{1,0:T(8,128)(2,1)S(1)}, u32[]{:S(2)}, u32[]{:S(2)}) collective-permute-start(bf16[32,1536]{1,0:T(8,128)(2,1)} %get-tuple-element.44), channel_id=1, source_target_pairs={{0,16},{4,20},{8,24},{12,28},{16,0},{20,4},{24,8},{28,12},{1,17},{... | collective-permute-start | bytes 294920 | tf_op jit(solution)/shard_map/ppermute | solution.py:547
  32.2 7.0 %collective-permute-start.4 = (bf16[32,1536]{1,0:T(8,128)(2,1)}, bf16[32,1536]{1,0:T(8,128)(2,1)S(1)}, u32[]{:S(2)}, u32[]{:S(2)}) collective-permute-start(bf16[32,1536]{1,0:T(8,128)(2,1)} %get-tuple-element.45), channel_id=1, source_target_pairs={{0,24},{4,28},{8,0},{12,4},{16,8},{20,12},{24,16},{28,20},{1,25},{... | collective-permute-start | bytes 294920 | tf_op jit(solution)/shard_map/ppermute | solution.py:547
  40.0 107.4 %reduce-scatter.2.cloned.1.call-start = ((), (), s32[]{:S(2)}) async-start(), calls=%async_computation.2 | async-start | bytes 1966080 | tf_op jit(solution)/shard_map/reduce_scatter | solution.py:613
  47.0 13.0 %collective-permute-start.7 = (bf16[4,32,1536]{2,1,0:T(8,128)(2,1)S(1)}, bf16[4,32,1536]{2,1,0:T(8,128)(2,1)S(1)}, u32[]{:S(2)}, u32[]{:S(2)}) collective-permute-start(bf16[4,32,1536]{2,1,0:T(8,128)(2,1)S(1)} %get-tuple-element.93), channel_id=1, source_target_pairs={{0,24},{4,28},{8,0},{12,4},{16,8},{20,12},{24,16},{28,20},{1,25},{... | collective-permute-start | bytes 1179656 | tf_op jit(solution)/shard_map/ppermute | solution.py:547
  47.7 19.0 %collective-permute-start.6 = (bf16[4,32,1536]{2,1,0:T(8,128)(2,1)S(1)}, bf16[4,32,1536]{2,1,0:T(8,128)(2,1)S(1)}, u32[]{:S(2)}, u32[]{:S(2)}) collective-permute-start(bf16[4,32,1536]{2,1,0:T(8,128)(2,1)S(1)} %get-tuple-element.94), channel_id=1, source_target_pairs={{0,16},{4,20},{8,24},{12,28},{16,0},{20,4},{24,8},{28,12},{1,17},{... | collective-permute-start | bytes 1179656 | tf_op jit(solution)/shard_map/ppermute | solution.py:547
  49.2 18.3 %collective-permute-start.5 = (bf16[4,32,1536]{2,1,0:T(8,128)(2,1)S(1)}, bf16[4,32,1536]{2,1,0:T(8,128)(2,1)S(1)}, u32[]{:S(2)}, u32[]{:S(2)}) collective-permute-start(bf16[4,32,1536]{2,1,0:T(8,128)(2,1)S(1)} %get-tuple-element.95), channel_id=1, source_target_pairs={{0,8},{4,12},{8,16},{12,20},{16,24},{20,28},{24,0},{28,4},{1,9},{5... | collective-permute-start | bytes 1179656 | tf_op jit(solution)/shard_map/ppermute | solution.py:547
  67.7 16.1 %collective-permute-start.9 = (bf16[512,1536]{1,0:T(8,128)(2,1)S(1)}, bf16[512,1536]{1,0:T(8,128)(2,1)S(1)}, u32[]{:S(2)}, u32[]{:S(2)}) collective-permute-start(bf16[512,1536]{1,0:T(8,128)(2,1)S(1)} %bitcast.39), channel_id=1, source_target_pairs={{0,4},{4,0},{8,12},{12,8},{16,20},{20,16},{24,28},{28,24},{1,5},{5... | collective-permute-start | bytes 4718600 | tf_op jit(solution)/shard_map/ppermute | solution.py:557
  71.7 12.1 %collective-permute-start.8 = (bf16[512,256]{1,0:T(8,128)(2,1)}, bf16[512,256]{1,0:T(8,128)(2,1)S(1)}, u32[]{:S(2)}, u32[]{:S(2)}) collective-permute-start(bf16[512,256]{1,0:T(8,128)(2,1)} %d_o_other.1), channel_id=1, source_target_pairs={{0,4},{4,0},{8,12},{12,8},{16,20},{20,16},{24,28},{28,24},{1,5},{5... | collective-permute-start | bytes 786440 | tf_op jit(solution)/shard_map/ppermute | solution.py:557
  83.8 9.2 %collective-permute-start.10 = (bf16[512,1536]{1,0:T(8,128)(2,1)}, bf16[512,1536]{1,0:T(8,128)(2,1)S(1)}, u32[]{:S(2)}, u32[]{:S(2)}) collective-permute-start(bf16[512,1536]{1,0:T(8,128)(2,1)} %all-gather.6.cloned.1.call-done.x_ref.xa_ref), channel_id=1, source_target_pairs={{0,4},{4,0},{8,12},{12,8},{16,20},{20,16},{24,28},{28,24},{1,5},{5... | collective-permute-start | bytes 4718600 | tf_op jit(solution)/shard_map/ppermute | solution.py:557
  113.0 80.4 %all-gather.10.cloned.1.call-start = ((), (), s32[]{:S(2)}) async-start(), calls=%async_computation.4 | async-start | bytes 2949120 | tf_op jit(solution)/shard_map/all_gather | solution.py:637
  121.7 17.3 %collective-permute-start.26 = (bf16[768,384]{1,0:T(8,128)(2,1)}, bf16[768,384]{1,0:T(8,128)(2,1)S(1)}, u32[]{:S(2)}, u32[]{:S(2)}) collective-permute-start(bf16[768,384]{1,0:T(8,128)(2,1)} %get-tuple-element.75), channel_id=1, source_target_pairs={{0,24},{4,28},{8,0},{12,4},{16,8},{20,12},{24,16},{28,20},{1,25},{... | collective-permute-start | bytes 1769480 | tf_op jit(solution)/shard_map/ppermute | solution.py:547
  122.3 28.2 %collective-permute-start.25 = (bf16[768,384]{1,0:T(8,128)(2,1)}, bf16[768,384]{1,0:T(8,128)(2,1)S(1)}, u32[]{:S(2)}, u32[]{:S(2)}) collective-permute-start(bf16[768,384]{1,0:T(8,128)(2,1)} %get-tuple-element.73), channel_id=1, source_target_pairs={{0,16},{4,20},{8,24},{12,28},{16,0},{20,4},{24,8},{28,12},{1,17},{... | collective-permute-start | bytes 1769480 | tf_op jit(solution)/shard_map/ppermute | solution.py:547
  123.7 27.4 %collective-permute-start.24 = (bf16[768,384]{1,0:T(8,128)(2,1)}, bf16[768,384]{1,0:T(8,128)(2,1)S(1)}, u32[]{:S(2)}, u32[]{:S(2)}) collective-permute-start(bf16[768,384]{1,0:T(8,128)(2,1)} %get-tuple-element.71), channel_id=1, source_target_pairs={{0,8},{4,12},{8,16},{12,20},{16,24},{20,28},{24,0},{28,4},{1,9},{5... | collective-permute-start | bytes 1769480 | tf_op jit(solution)/shard_map/ppermute | solution.py:547
  168.3 6.2 %collective-permute-start.16 = (bf16[2,4,1,1536]{3,2,1,0:T(2,128)(2,1)}, bf16[2,4,1,1536]{3,2,1,0:T(2,128)(2,1)S(1)}, u32[]{:S(2)}, u32[]{:S(2)}) collective-permute-start(bf16[2,4,1,1536]{3,2,1,0:T(2,128)(2,1)} %get-tuple-element.57), channel_id=1, source_target_pairs={{0,1},{1,2},{2,3},{3,4},{4,5},{5,6},{6,7},{7,8},{8,9},{9,10},{10,1... | collective-permute-start | bytes 73736 | tf_op jit(solution)/shard_map/ppermute | solution.py:538
  170.2 7.4 %collective-permute-start.17 = (bf16[2,4,1,1536]{3,2,1,0:T(2,128)(2,1)}, bf16[2,4,1,1536]{3,2,1,0:T(2,128)(2,1)S(1)}, u32[]{:S(2)}, u32[]{:S(2)}) collective-permute-start(bf16[2,4,1,1536]{3,2,1,0:T(2,128)(2,1)} %get-tuple-element.58), channel_id=1, source_target_pairs={{1,0},{2,1},{3,2},{4,3},{5,4},{6,5},{7,6},{8,7},{9,8},{10,9},{11,1... | collective-permute-start | bytes 73736 | tf_op jit(solution)/shard_map/ppermute | solution.py:538
  193.4 60.1 %collective-permute-start.27 = (bf16[4,384,768]{2,1,0:T(8,128)(2,1)}, bf16[4,384,768]{2,1,0:T(8,128)(2,1)S(1)}, u32[]{:S(2)}, u32[]{:S(2)}) collective-permute-start(bf16[4,384,768]{2,1,0:T(8,128)(2,1)} %bitcast.49), channel_id=1, source_target_pairs={{0,4},{4,0},{8,12},{12,8},{16,20},{20,16},{24,28},{28,24},{1,5},{5... | collective-permute-start | bytes 7077896 | tf_op jit(solution)/shard_map/ppermute | solution.py:557
  198.9 12.0 %collective-permute-start.18 = (bf16[128,1536]{1,0:T(8,128)(2,1)}, bf16[128,1536]{1,0:T(8,128)(2,1)S(1)}, u32[]{:S(2)}, u32[]{:S(2)}) collective-permute-start(bf16[128,1536]{1,0:T(8,128)(2,1)} %get-tuple-element.60), channel_id=1, source_target_pairs={{0,1},{1,2},{2,3},{3,0},{4,5},{5,6},{6,7},{7,4},{8,9},{9,10},{10,1... | collective-permute-start | bytes 1179656 | tf_op jit(solution)/shard_map/ppermute | solution.py:552
  199.0 36.5 %collective-permute-start.19 = (bf16[128,1536]{1,0:T(8,128)(2,1)}, bf16[128,1536]{1,0:T(8,128)(2,1)S(1)}, u32[]{:S(2)}, u32[]{:S(2)}) collective-permute-start(bf16[128,1536]{1,0:T(8,128)(2,1)} %get-tuple-element.63), channel_id=1, source_target_pairs={{0,2},{1,3},{2,0},{3,1},{4,6},{5,7},{6,4},{7,5},{8,10},{9,11},{10,... | collective-permute-start | bytes 1179656 | tf_op jit(solution)/shard_map/ppermute | solution.py:552
  200.4 35.0 %collective-permute-start.20 = (bf16[128,1536]{1,0:T(8,128)(2,1)}, bf16[128,1536]{1,0:T(8,128)(2,1)S(1)}, u32[]{:S(2)}, u32[]{:S(2)}) collective-permute-start(bf16[128,1536]{1,0:T(8,128)(2,1)} %get-tuple-element.66), channel_id=1, source_target_pairs={{0,3},{1,0},{2,1},{3,2},{4,7},{5,4},{6,5},{7,6},{8,11},{9,8},{10,9... | collective-permute-start | bytes 1179656 | tf_op jit(solution)/shard_map/ppermute | solution.py:552
  242.3 6.4 %collective-permute-start.22 = (bf16[32,1536]{1,0:T(8,128)(2,1)S(1)}, bf16[32,1536]{1,0:T(8,128)(2,1)S(1)}, u32[]{:S(2)}, u32[]{:S(2)}) collective-permute-start(bf16[32,1536]{1,0:T(8,128)(2,1)S(1)} %get-tuple-element.97), channel_id=1, source_target_pairs={{0,16},{4,20},{8,24},{12,28},{16,0},{20,4},{24,8},{28,12},{1,17},{... | collective-permute-start | bytes 294920 | tf_op jit(solution)/shard_map/ppermute | solution.py:547
  (36 other events, 186.1 us)
Sparse Core Ops, SparseCore 0:
  9.6 35.9 all-gather.7
  47.7 36.0 all-gather.5
  113.1 34.2 reduce-scatter.1
  154.9 38.4 all-gather.9

commit v5 on v4

--- a/solution.py
+++ b/solution.py
@@ -9,7 +9,7 @@
 
 DH = 192
 KW = 5
-VMEM_LIMIT = 56 * 1024 * 1024
+VMEM_LIMIT = 24 * 1024 * 1024
 COST = pl.CostEstimate(flops=1000, bytes_accessed=1000, transcendentals=0)
 BF = jnp.bfloat16
 F32 = jnp.float32
@@ -407,17 +407,21 @@
     )(place, mine, got, weight)
 
 
-def sum_kernel(*refs):
+def sum_kernel(*refs, count):
+    out_refs = refs[count:]
+    size = out_refs[0].shape[0]
     total = refs[0][...].astype(F32)
-    for ref in refs[1:-1]:
+    for ref in refs[1:count]:
         total = total + ref[...].astype(F32)
-    refs[-1][...] = total.astype(BF)
-
-
-def summed(parts, name):
-    return pl.pallas_call(
-        sum_kernel,
-        out_shape=jax.ShapeDtypeStruct(parts[0].shape, BF),
+    for slot, out_ref in enumerate(out_refs):
+        out_ref[...] = total[slot * size : (slot + 1) * size].astype(BF)
+
+
+def summed(parts, slots, name):
+    rows, width = parts[0].shape
+    return pl.pallas_call(
+        functools.partial(sum_kernel, count=len(parts)),
+        out_shape=[jax.ShapeDtypeStruct((rows // slots, width), BF)] * slots,
         compiler_params=params(),
         cost_estimate=COST,
         name=name,
@@ -580,8 +584,7 @@
     def from_chips(slots):
         return [slots[r] if r == 0 else send_chip(slots[r], -r, heads) for r in range(seqs)]
 
-    grad = jnp.transpose(grad_out, (1, 0, 2))
-    grad_z = lax.all_gather(grad, "head", axis=0, tiled=False)
+    grad_z = lax.all_gather(grad_out, "head", axis=0, tiled=False)
     pairs = jnp.transpose(enc_in.reshape(rows, 2, seqs, enc_in.shape[2]), (1, 2, 0, 3))
     low, high = neighbour_edges(pairs[:, :, :1, :], pairs[:, :, -1:, :])
     skip, slope, normed = encoder(at, pairs, low, high, conv_weight, norm_gain)
@@ -590,7 +593,7 @@
 
     grad_z = after(grad_z, normed_slab)
     grad_slots = [
-        lax.dynamic_index_in_dim(grad_z, (own_seq + r) % seqs, 1, keepdims=False)
+        lax.dynamic_index_in_dim(grad_z, (own_seq + r) % seqs, 2, keepdims=False)
         for r in range(seqs)
     ]
     grad_rows = jnp.stack(to_chips(grad_slots), axis=1).reshape(half, width)
@@ -629,22 +632,24 @@
         turned, result_mine, result_got, w_rows, groups, 3 * DH, 4 * DH, "head_term"
     )
     head_slots = [head_term[0], send_z(head_term[1], 1)]
-    head_slots += [send_z(after(head_term[q], d_normed), q) for q in range(2, groups)]
-    part = [after(p, d_normed) for p in part]
+    part = [after(p, d_normed, head_slots[1]) for p in part]
     d_normed = from_chips([d_normed[r] for r in range(seqs)])
     chunk = weight_sum(part)
     same_head = [[b * heads + h for b in range(seqs)] for h in range(heads)]
     chunks = lax.all_gather(chunk, "seq", axis_index_groups=same_head)
 
+    for q in range(2, groups):
+        head_slots.append(send_z(after(head_term[q], head_slots[1]), q))
+    grad = jnp.transpose(after(grad_out, d_term), (1, 0, 2))
+    d_normed[0] = after(d_normed[0], head_slots[-1])
     d_conv, first, last = conv_gradient(at, d_normed, skip, grad, norm_gain, slope)
     low, high = neighbour_edges(first, last)
-    grad_input = conv_back(d_conv, low, high, conv_weight)
-
-    head_slots = [after(h, low, high) for h in head_slots]
-    head_sum = summed(head_slots, "head_sum").reshape(seqs, rows, width)
-    head_sum = from_chips([head_sum[r] for r in range(seqs)])
-    mixed = mixed_call(at, head_sum, skip)
-    chunks = after(chunks, grad_input)
+    head_sum = summed(head_slots, seqs, "head_sum")
+    grad_input = conv_back(d_conv, after(low, *head_sum), high, conv_weight)
+    head_sum = from_chips(head_sum)
+
+    mixed = mixed_call(at, [after(h, low, high) for h in head_sum], skip)
+    chunks = after(chunks, grad_input, mixed)
     grad_w_qkv, grad_w_out = unpack_weights(head_mine, chunks, swap_heads(chunks))
     grad_input = jnp.transpose(grad_input.reshape(2, seqs, rows, -1), (2, 0, 1, 3))
     return (

time: 270 us -> 229 us (0.85)
  Pallas kernels: 87.2 us -> 51.3 us
  waiting for transfers between devices: 110 us -> 79.5 us
  local copies, waits for them, and re-layouts: 21.5 us -> 41.4 us
  starting transfers between devices: 34.4 us -> 40.8 us
    ppermute x15, waiting for transfers between devices: 46.8 us -> 25.4 us  [send_chip(): lax.ppermute(x, 'seq', [(s, (s + step * heads) % count) for s in range(co...]
    unnamed x61 -> x66, local copies, waits for them, and re-layouts: 15 us -> 35.5 us
    pallas_call x4, Pallas kernels: 14.8 us -> 4.65 us  [head_product(): pl.pallas_call(functools.partial(product_kernel, contract=contract), grid...]
    reduce_scatter x1, waiting for transfers between devices: 8.45 us -> 1.04 us  [unit_body(): lax.psum_scatter(d_term.reshape(groups, seqs, rows, width), 'head', scatt...]
    all_gather x1, waiting for transfers between devices: 6.56 us -> 0.02 us  [unit_body(): chunks = lax.all_gather(chunk, 'seq', axis_index_groups=same_head)]
    pallas_call x1, Pallas kernels: 8.61 us -> 4.33 us  [conv_back(): pl.pallas_call(conv_back_kernel, grid=(KW,), in_specs=[whole(d_conv.shape...]
    ppermute x6, waiting for transfers between devices: 1.49 us -> 5.12 us  [swap_heads(): lax.ppermute(x, 'seq', [(s, s + 1 - 2 * (s % 2)) for s in range(count)])]
    ppermute x3, starting transfers between devices: 2.03 us -> 5.44 us  [send_z(): lax.ppermute(x, 'head', [(z, (z + step) % count) for z in range(count)])]
  transfers between devices with their start and end apart: 32 -> 32, of which waited for: 23 -> 17; matrix products, arithmetic and copies ran while one was open for 4% -> 3% of each run, Pallas kernels for 23% -> 15%
where the time goes in v5:
time: 229 us; the launch traced here: 228 us
  waiting for transfers between devices  79.5 us (35%)
  Pallas kernels  51.3 us (22%)
  local copies, waits for them, and re-layouts  41.4 us (18%)
  starting transfers between devices  40.8 us (18%)
  between operations  14.2 us (6%)
    unnamed x66, local copies, waits for them, and re-layouts  35.5 us
    ppermute x3, waiting for transfers between devices, send_z(): lax.ppermute(x, 'head', [(z, (z + step) % count) for z in range(count)])  35.4 us
    ppermute x15, waiting for transfers between devices, send_chip(): lax.ppermute(x, 'seq', [(s, (s + step * heads) % count) for s in range(co...  25.4 us
    ppermute x15, starting transfers between devices, send_chip(): lax.ppermute(x, 'seq', [(s, (s + step * heads) % count) for s in range(co...  20.6 us
    pallas_call x2, Pallas kernels, pair_term(): pl.pallas_call(functools.partial(term_kernel, first=first, last=last), gr...  8.82 us
    pallas_call x1, Pallas kernels, weight_gradients(): pl.pallas_call(weight_kernel, grid_spec=pltpu.PrefetchScalarGridSpec(num_...  7.67 us
    pallas_call x1, Pallas kernels, attention(): pl.pallas_call(functools.partial(attention_kernel, block=min(256, half)),...  7.36 us
    pallas_call x1, Pallas kernels, encoder(): pl.pallas_call(conv_kernel, grid=(width // tile,), in_specs=[SCALARS, who...  7.09 us
  transfers between devices with their start and end apart: 32, of which 17 were waited for; matrix products, arithmetic and copies ran while one was open for 3% of the time, Pallas kernels for 15%

profile of v5, /device:TPU:26, one launch (start us, length us, event | category | flops | bytes accessed | tf_op | source)
XLA Modules:
  0.0 227.6 jit_solution(7198926538197509906)
XLA Ops:
  11.4 5.0 %collective-permute-start = (bf16[2,4,1,768]{3,2,1,0:T(2,128)(2,1)S(1)}, bf16[2,4,1,768]{3,2,1,0:T(2,128)(2,1)S(1)}, u32[]{:S(2)}, u32[]{:S(2)}) collective-permute-start(bf16[2,4,1,768]{3,2,1,0:T(2,128)(2,1)S(1)} %get-tuple-element.115), channel_id=1, source_target_pairs={{0,1},{1,2},{2,3},{3,4},{4,5},{5,6},{6,7},{7,8},{8,9},{9,10},{10,1... | collective-permute-start | bytes 36872 | tf_op jit(solution)/shard_map/ppermute | solution.py:542
  17.9 4.5 %copy-done = bf16[5,768,1536]{2,1,0:T(8,128)(2,1)S(1)} copy-done((bf16[5,768,1536]{2,1,0:T(8,128)(2,1)S(1)}, bf16[5,768,1536]{2,1,0:T(8,128)(2,1)}, u32[]{:S(2)}) %copy-start) | copy-done | bytes 11796504
  22.5 7.1 %encoder_forward.1 = (bf16[4,32,1536]{2,1,0:T(8,128)(2,1)S(1)}, f32[2,4,32,1536]{3,2,1,0:T(8,128)S(1)}, bf16[32,1536]{1,0:T(8,128)(2,1)S(1)}, bf16[32,1536]{1,0:...) custom-call(s32[2]{0:T(128)S(1)} %pad_add_fusion.at_ref, ...), custom_call_target="tpu_custom_call" | custom-call | flops 1000 | bytes 1000 | tf_op jit(solution)/shard_map/encoder_forward/pallas_call | solution.py:109
  36.4 2.6 %collective-permute-done.3 = bf16[32,1536]{1,0:T(8,128)(2,1)S(1)} collective-permute-done((bf16[32,1536]{1,0:T(8,128)(2,1)S(1)}, bf16[32,1536]{1,0:T(8,128)(2,1)S(1)}, u32[]{:S(2)}, u32[]{:S(2)}) %collective-permute-start.3) | collective-permute-done | bytes 98336 | tf_op jit(solution)/shard_map/ppermute | solution.py:551
  39.9 5.7 %all-gather.8.cloned.1.call-done = bf16[128,4,1536]{2,1,0:T(4,128)(2,1)} async-done(((bf16[32,4,1536]{2,1,0:T(4,128)(2,1)}), bf16[128,4,1536]{2,1,0:T(4,128)(2,1)}) %all-gather.8.cloned.1.call-update) | async-done | bytes 1572880 | tf_op jit(solution)/shard_map/all_gather | solution.py:587
  49.5 2.4 %collective-permute-start.5 = (bf16[4,32,1536]{2,1,0:T(8,128)(2,1)S(1)}, bf16[4,32,1536]{2,1,0:T(8,128)(2,1)S(1)}, u32[]{:S(2)}, u32[]{:S(2)}) collective-permute-start(bf16[4,32,1536]{2,1,0:T(8,128)(2,1)S(1)} %get-tuple-element.109), channel_id=1, source_target_pairs={{0,8},{4,12},{8,16},{12,20},{16,24},{20,28},{24,0},{28,4},{1,9},{5... | collective-permute-start | bytes 1179656 | tf_op jit(solution)/shard_map/ppermute | solution.py:551
  51.9 8.5 %collective-permute-done.7 = bf16[4,32,1536]{2,1,0:T(8,128)(2,1)S(1)} collective-permute-done((bf16[4,32,1536]{2,1,0:T(8,128)(2,1)S(1)}, bf16[4,32,1536]{2,1,0:T(8,128)(2,1)S(1)}, u32[]{:S(2)}, u32[]{:S(2)}) %collective-permute-start.7) | collective-permute-done | bytes 393248 | tf_op jit(solution)/shard_map/ppermute | solution.py:551
  60.4 6.6 %collective-permute-done.6 = bf16[4,32,1536]{2,1,0:T(8,128)(2,1)S(1)} collective-permute-done((bf16[4,32,1536]{2,1,0:T(8,128)(2,1)S(1)}, bf16[4,32,1536]{2,1,0:T(8,128)(2,1)S(1)}, u32[]{:S(2)}, u32[]{:S(2)}) %collective-permute-start.6) | collective-permute-done | bytes 393248 | tf_op jit(solution)/shard_map/ppermute | solution.py:551
  72.7 3.9 %pack_weights.1 = (bf16[2,1536,576]{2,1,0:T(8,128)(2,1)S(1)}, bf16[2,576,1536]{2,1,0:T(8,128)(2,1)S(1)}) custom-call(bf16[3,1536,384]{2,1,0:T(8,128)(2,1)S(1)} %copy-done.12), custom_call_target="tpu_custom_call" | custom-call | flops 1000 | bytes 1000 | tf_op jit(solution)/shard_map/pack_weights/pallas_call | solution.py:261
  91.7 7.4 %attention.1 = (bf16[512,768]{1,0:T(8,128)(2,1)S(1)}, bf16[512,768]{1,0:T(8,128)(2,1)}) custom-call(bf16[512,640]{1,0:T(8,128)(2,1)S(1)} %qkv_own.1.qa_ref, bf16[512,640]{1,0:T(8,128)(2,1)S(1)} %collective-permute-done.11.qb_ref, bf16[512,256]{1,0:T(8,128)(2,1)S(1)} %copy-done.21, bf16[512,256]{1,0:T(8,128)(2,1)S(1)} %copy-done.25), custom_call_target="tpu_custom_call" | custom-call | flops 1000 | bytes 1000 | tf_op jit(solution)/shard_map/attention/pallas_call | solution.py:353
  105.7 4.9 %d_term.1 = bf16[512,1536]{1,0:T(8,128)(2,1)S(1)} custom-call(s32[2]{0:T(128)S(1)} %get-tuple-element.117.head_ref, bf16[512,768]{1,0:T(8,128)(2,1)S(1)} %copy-done.9, bf16[512,768]{1,0:T(8,128)(2,1)} %collective-permute-done.12.b_ref, bf16[2,576,1536]{2,1,0:T(8,128)(2,1)S(1)} %copy-done.14), custom_call_target="tpu_custom_call" | custom-call | flops 1000 | bytes 1000 | tf_op jit(solution)/shard_map/d_term/pallas_call | solution.py:391
  114.6 7.7 %weight_gradients.1 = (bf16[768,384]{1,0:T(8,128)(2,1)S(1)}, bf16[768,384]{1,0:T(8,128)(2,1)}, bf16[768,384]{1,0:T(8,128)(2,1)}, bf16[768,384]{1,0:T(8,128)(2,1)S(1)}) custom-call(s32[1]{0:T(128)} %bitcast.at_ref, bf16[512,1536]{1,0:T(8,128)(2,1)S(1)} %copy-done.5, bf16[512,1536]{1,0:T(8,128)(2,1)S(1)} %copy-done.19, bf16[512,1536]{1,0:T(8,128)(2,1)S(1)} %bitcast.44, ...), custom_call_target="tpu_custom_call" | custom-call | flops 1000 | bytes 1000 | tf_op jit(solution)/shard_map/weight_gradients/pallas_call | solution.py:460
  126.6 3.9 %head_term.1 = (bf16[128,1536]{1,0:T(8,128)(2,1)S(1)}, bf16[128,1536]{1,0:T(8,128)(2,1)S(1)}, bf16[128,1536]{1,0:T(8,128)(2,1)S(1)}, bf16[128,1536]{1,0:T(8,128)(2,1)S(1)}) custom-call(s32[2]{0:T(128)S(1)} %get-tuple-element.116.head_ref, bf16[512,768]{1,0:T(8,128)(2,1)S(1)} %copy-done.10, bf16[512,768]{1,0:T(8,128)(2,1)} %collective-permute-done.12.b_ref, ...), custom_call_target="tpu_custom_call" | custom-call | flops 1000 | bytes 1000 | tf_op jit(solution)/shard_map/head_term/pallas_call | solution.py:391
  132.1 2.6 %collective-permute-start.13 = (bf16[128,1536]{1,0:T(8,128)(2,1)S(1)}, bf16[128,1536]{1,0:T(8,128)(2,1)S(1)}, u32[]{:S(2)}, u32[]{:S(2)}) collective-permute-start(bf16[128,1536]{1,0:T(8,128)(2,1)S(1)} %get-tuple-element.62), channel_id=1, source_target_pairs={{0,1},{1,2},{2,3},{3,0},{4,5},{5,6},{6,7},{7,4},{8,9},{9,10},{10,1... | collective-permute-start | bytes 1179656 | tf_op jit(solution)/shard_map/ppermute | solution.py:556
  134.7 4.7 %collective-permute-done.26.refs_3_ = bf16[768,384]{1,0:T(8,128)(2,1)S(1)} collective-permute-done((bf16[768,384]{1,0:T(8,128)(2,1)S(1)}, bf16[768,384]{1,0:T(8,128)(2,1)S(1)}, u32[]{:S(2)}, u32[]{:S(2)}) %collective-permute-start.26) | collective-permute-done | bytes 589856 | tf_op jit(solution)/shard_map/ppermute | solution.py:551
  139.3 14.2 %collective-permute-done.13.refs_1_ = bf16[128,1536]{1,0:T(8,128)(2,1)S(1)} collective-permute-done((bf16[128,1536]{1,0:T(8,128)(2,1)S(1)}, bf16[128,1536]{1,0:T(8,128)(2,1)S(1)}, u32[]{:S(2)}, u32[]{:S(2)}) %collective-permute-start.13) | collective-permute-done | bytes 393248 | tf_op jit(solution)/shard_map/ppermute | solution.py:556
  164.6 21.2 %collective-permute-done.14.refs_2_ = bf16[128,1536]{1,0:T(8,128)(2,1)S(1)} collective-permute-done((bf16[128,1536]{1,0:T(8,128)(2,1)}, bf16[128,1536]{1,0:T(8,128)(2,1)S(1)}, u32[]{:S(2)}, u32[]{:S(2)}) %collective-permute-start.14) | collective-permute-done | bytes 393248 | tf_op jit(solution)/shard_map/ppermute | solution.py:556
  188.1 2.4 %collective-permute-start.23 = (bf16[32,1536]{1,0:T(8,128)(2,1)S(1)}, bf16[32,1536]{1,0:T(8,128)(2,1)S(1)}, u32[]{:S(2)}, u32[]{:S(2)}) collective-permute-start(bf16[32,1536]{1,0:T(8,128)(2,1)S(1)} %get-tuple-element.79), channel_id=1, source_target_pairs={{0,8},{4,12},{8,16},{12,20},{16,24},{20,28},{24,0},{28,4},{1,9},{5... | collective-permute-start | bytes 294920 | tf_op jit(solution)/shard_map/ppermute | solution.py:551
  193.7 3.9 %collective-permute-start.20 = (bf16[2,4,1,1536]{3,2,1,0:T(2,128)(2,1)S(1)}, bf16[2,4,1,1536]{3,2,1,0:T(2,128)(2,1)S(1)}, u32[]{:S(2)}, u32[]{:S(2)}) collective-permute-start(bf16[2,4,1,1536]{3,2,1,0:T(2,128)(2,1)S(1)} %get-tuple-element.73), channel_id=1, source_target_pairs={{1,0},{2,1},{3,2},{4,3},{5,4},{6,5},{7,6},{8,7},{9,8},{10,9},{11,1... | collective-permute-start | bytes 73736 | tf_op jit(solution)/shard_map/ppermute | solution.py:542
  197.7 3.2 %collective-permute-done.20.high_ref = bf16[2,4,1,1536]{3,2,1,0:T(2,128)(2,1)S(1)} collective-permute-done((bf16[2,4,1,1536]{3,2,1,0:T(2,128)(2,1)S(1)}, bf16[2,4,1,1536]{3,2,1,0:T(2,128)(2,1)S(1)}, u32[]{:S(2)}, u32[]{:S(2)}) %collective-permute-start.20) | collective-permute-done | bytes 24608 | tf_op jit(solution)/shard_map/ppermute | solution.py:542
  201.6 4.3 %copy-done.1 = bf16[5,768,1536]{2,1,0:T(8,128)(2,1)S(1)} copy-done((bf16[5,768,1536]{2,1,0:T(8,128)(2,1)S(1)}, bf16[5,768,1536]{2,1,0:T(8,128)(2,1)}, u32[]{:S(2)}) %copy-start.1) | copy-done | bytes 11796504
  205.9 4.3 %encoder_backward.1 = bf16[256,768]{1,0:T(8,128)(2,1)S(1)} custom-call(bf16[2,4,32,1536]{3,2,1,0:T(8,128)(2,1)S(1)} %get-tuple-element.81.d_ref, bf16[2,4,1,1536]{3,2,1,0:T(2,128)(2,1)S(1)} %collective-permute-done.19.low_ref, bf16[2,4,1,1536]{3,2,1,0:T(2,128)(2,1)S(1)} %collective-permute-done.20.high_ref, bf16[5,768,1536]{2,1,0:T(8,128)(2,1)S(1)} %copy-done.1), custom_call_target="tpu_custom_call" | custom-call | flops 1000 | bytes 1000 | tf_op jit(solution)/shard_map/encoder_backward/pallas_call | solution.py:227
  212.5 2.6 %collective-permute-done.27.other_ref = bf16[4,384,768]{2,1,0:T(8,128)(2,1)S(1)} collective-permute-done((bf16[4,384,768]{2,1,0:T(8,128)(2,1)}, bf16[4,384,768]{2,1,0:T(8,128)(2,1)S(1)}, u32[]{:S(2)}, u32[]{:S(2)}) %collective-permute-start.27) | collective-permute-done | bytes 2359328 | tf_op jit(solution)/shard_map/ppermute | solution.py:561
  216.8 4.3 %weight_outputs.1 = (f32[3,1536,384]{2,1,0:T(8,128)}, f32[384,1536]{1,0:T(8,128)}) custom-call(s32[1]{0:T(128)} %bitcast.1.head_ref.at_ref, bf16[4,384,768]{2,1,0:T(8,128)(2,1)S(1)} %bitcast.50, bf16[4,384,768]{2,1,0:T(8,128)(2,1)S(1)} %collective-permute-done.27.other_ref), custom_call_target="tpu_custom_call" | custom-call | flops 1000 | bytes 1000 | tf_op jit(solution)/shard_map/weight_outputs/pallas_call | solution.py:519
  (139 shorter events, 75.5 us)
Async XLA Ops:
  7.2 38.4 %all-gather.8.cloned.1.call-start = ((), (), s32[]{:S(2)}) async-start(), calls=%async_computation.3 | async-start | bytes 1966080 | tf_op jit(solution)/shard_map/all_gather | solution.py:587
  7.9 75.8 %all-gather.6.cloned.1.call-start = ((), (), s32[]{:S(2)}) async-start(), calls=%async_computation.1 | async-start | bytes 1966080 | tf_op jit(solution)/shard_map/all_gather | solution.py:592
  9.1 8.2 %collective-permute-start.1 = (bf16[2,4,1,768]{3,2,1,0:T(2,128)(2,1)S(1)}, bf16[2,4,1,768]{3,2,1,0:T(2,128)(2,1)S(1)}, u32[]{:S(2)}, u32[]{:S(2)}) collective-permute-start(bf16[2,4,1,768]{3,2,1,0:T(2,128)(2,1)S(1)} %get-tuple-element.114), channel_id=1, source_target_pairs={{1,0},{2,1},{3,2},{4,3},{5,4},{6,5},{7,6},{8,7},{9,8},{10,9},{11,1... | collective-permute-start | bytes 36872 | tf_op jit(solution)/shard_map/ppermute | solution.py:542
  39.8 114.8 %reduce-scatter.2.cloned.1.call-start = ((), (), s32[]{:S(2)}) async-start(), calls=%async_computation.2 | async-start | bytes 1966080 | tf_op jit(solution)/shard_map/reduce_scatter | solution.py:616
  47.4 13.0 %collective-permute-start.7 = (bf16[4,32,1536]{2,1,0:T(8,128)(2,1)S(1)}, bf16[4,32,1536]{2,1,0:T(8,128)(2,1)S(1)}, u32[]{:S(2)}, u32[]{:S(2)}) collective-permute-start(bf16[4,32,1536]{2,1,0:T(8,128)(2,1)S(1)} %get-tuple-element.107), channel_id=1, source_target_pairs={{0,24},{4,28},{8,0},{12,4},{16,8},{20,12},{24,16},{28,20},{1,25},{... | collective-permute-start | bytes 1179656 | tf_op jit(solution)/shard_map/ppermute | solution.py:551
  48.0 19.0 %collective-permute-start.6 = (bf16[4,32,1536]{2,1,0:T(8,128)(2,1)S(1)}, bf16[4,32,1536]{2,1,0:T(8,128)(2,1)S(1)}, u32[]{:S(2)}, u32[]{:S(2)}) collective-permute-start(bf16[4,32,1536]{2,1,0:T(8,128)(2,1)S(1)} %get-tuple-element.108), channel_id=1, source_target_pairs={{0,16},{4,20},{8,24},{12,28},{16,0},{20,4},{24,8},{28,12},{1,17},{... | collective-permute-start | bytes 1179656 | tf_op jit(solution)/shard_map/ppermute | solution.py:551
  49.5 18.4 %collective-permute-start.5 = (bf16[4,32,1536]{2,1,0:T(8,128)(2,1)S(1)}, bf16[4,32,1536]{2,1,0:T(8,128)(2,1)S(1)}, u32[]{:S(2)}, u32[]{:S(2)}) collective-permute-start(bf16[4,32,1536]{2,1,0:T(8,128)(2,1)S(1)} %get-tuple-element.109), channel_id=1, source_target_pairs={{0,8},{4,12},{8,16},{12,20},{16,24},{20,28},{24,0},{28,4},{1,9},{5... | collective-permute-start | bytes 1179656 | tf_op jit(solution)/shard_map/ppermute | solution.py:551
  68.2 16.2 %collective-permute-start.9 = (bf16[512,1536]{1,0:T(8,128)(2,1)S(1)}, bf16[512,1536]{1,0:T(8,128)(2,1)}, u32[]{:S(2)}, u32[]{:S(2)}) collective-permute-start(bf16[512,1536]{1,0:T(8,128)(2,1)S(1)} %bitcast.41), channel_id=1, source_target_pairs={{0,4},{4,0},{8,12},{12,8},{16,20},{20,16},{24,28},{28,24},{1,5},{5... | collective-permute-start | bytes 4718600 | tf_op jit(solution)/shard_map/ppermute | solution.py:561
  70.7 13.0 %collective-permute-start.8 = (bf16[512,256]{1,0:T(8,128)(2,1)}, bf16[512,256]{1,0:T(8,128)(2,1)S(1)}, u32[]{:S(2)}, u32[]{:S(2)}) collective-permute-start(bf16[512,256]{1,0:T(8,128)(2,1)} %d_o_other.1), channel_id=1, source_target_pairs={{0,4},{4,0},{8,12},{12,8},{16,20},{20,16},{24,28},{28,24},{1,5},{5... | collective-permute-start | bytes 786440 | tf_op jit(solution)/shard_map/ppermute | solution.py:561
  84.4 6.9 %collective-permute-start.10 = (bf16[512,1536]{1,0:T(8,128)(2,1)}, bf16[512,1536]{1,0:T(8,128)(2,1)S(1)}, u32[]{:S(2)}, u32[]{:S(2)}) collective-permute-start(bf16[512,1536]{1,0:T(8,128)(2,1)} %all-gather.6.cloned.1.call-done.x_ref.xa_ref), channel_id=1, source_target_pairs={{0,4},{4,0},{8,12},{12,8},{16,20},{20,16},{24,28},{28,24},{1,5},{5... | collective-permute-start | bytes 4718600 | tf_op jit(solution)/shard_map/ppermute | solution.py:561
  111.7 98.5 %all-gather.10.cloned.1.call-start = ((), (), s32[]{:S(2)}) async-start(), calls=%async_computation.4 | async-start | bytes 2949120 | tf_op jit(solution)/shard_map/all_gather | solution.py:639
  122.2 17.1 %collective-permute-start.26 = (bf16[768,384]{1,0:T(8,128)(2,1)S(1)}, bf16[768,384]{1,0:T(8,128)(2,1)S(1)}, u32[]{:S(2)}, u32[]{:S(2)}) collective-permute-start(bf16[768,384]{1,0:T(8,128)(2,1)S(1)} %get-tuple-element.89), channel_id=1, source_target_pairs={{0,24},{4,28},{8,0},{12,4},{16,8},{20,12},{24,16},{28,20},{1,25},{... | collective-permute-start | bytes 1769480 | tf_op jit(solution)/shard_map/ppermute | solution.py:551
  122.8 31.8 %collective-permute-start.25 = (bf16[768,384]{1,0:T(8,128)(2,1)}, bf16[768,384]{1,0:T(8,128)(2,1)S(1)}, u32[]{:S(2)}, u32[]{:S(2)}) collective-permute-start(bf16[768,384]{1,0:T(8,128)(2,1)} %get-tuple-element.87), channel_id=1, source_target_pairs={{0,16},{4,20},{8,24},{12,28},{16,0},{20,4},{24,8},{28,12},{1,17},{... | collective-permute-start | bytes 1769480 | tf_op jit(solution)/shard_map/ppermute | solution.py:551
  124.3 30.3 %collective-permute-start.24 = (bf16[768,384]{1,0:T(8,128)(2,1)}, bf16[768,384]{1,0:T(8,128)(2,1)S(1)}, u32[]{:S(2)}, u32[]{:S(2)}) collective-permute-start(bf16[768,384]{1,0:T(8,128)(2,1)} %get-tuple-element.85), channel_id=1, source_target_pairs={{0,8},{4,12},{8,16},{12,20},{16,24},{20,28},{24,0},{28,4},{1,9},{5... | collective-permute-start | bytes 1769480 | tf_op jit(solution)/shard_map/ppermute | solution.py:551
  132.1 21.5 %collective-permute-start.13 = (bf16[128,1536]{1,0:T(8,128)(2,1)S(1)}, bf16[128,1536]{1,0:T(8,128)(2,1)S(1)}, u32[]{:S(2)}, u32[]{:S(2)}) collective-permute-start(bf16[128,1536]{1,0:T(8,128)(2,1)S(1)} %get-tuple-element.62), channel_id=1, source_target_pairs={{0,1},{1,2},{2,3},{3,0},{4,5},{5,6},{6,7},{7,4},{8,9},{9,10},{10,1... | collective-permute-start | bytes 1179656 | tf_op jit(solution)/shard_map/ppermute | solution.py:556
  156.9 28.9 %collective-permute-start.14 = (bf16[128,1536]{1,0:T(8,128)(2,1)}, bf16[128,1536]{1,0:T(8,128)(2,1)S(1)}, u32[]{:S(2)}, u32[]{:S(2)}) collective-permute-start(bf16[128,1536]{1,0:T(8,128)(2,1)} %copy-done.28), channel_id=1, source_target_pairs={{0,2},{1,3},{2,0},{3,1},{4,6},{5,7},{6,4},{7,5},{8,10},{9,11},{10,... | collective-permute-start | bytes 1179656 | tf_op jit(solution)/shard_map/ppermute | solution.py:556
  158.0 27.8 %collective-permute-start.15 = (bf16[128,1536]{1,0:T(8,128)(2,1)S(1)}, bf16[128,1536]{1,0:T(8,128)(2,1)S(1)}, u32[]{:S(2)}, u32[]{:S(2)}) collective-permute-start(bf16[128,1536]{1,0:T(8,128)(2,1)S(1)} %copy-done.27), channel_id=1, source_target_pairs={{0,3},{1,0},{2,1},{3,2},{4,7},{5,4},{6,5},{7,6},{8,11},{9,8},{10,9... | collective-permute-start | bytes 1179656 | tf_op jit(solution)/shard_map/ppermute | solution.py:556
  160.8 27.3 %collective-permute-start.18 = (bf16[32,1536]{1,0:T(8,128)(2,1)S(1)}, bf16[32,1536]{1,0:T(8,128)(2,1)S(1)}, u32[]{:S(2)}, u32[]{:S(2)}) collective-permute-start(bf16[32,1536]{1,0:T(8,128)(2,1)S(1)} %get-tuple-element.110), channel_id=1, source_target_pairs={{0,8},{4,12},{8,16},{12,20},{16,24},{20,28},{24,0},{28,4},{1,9},{5... | collective-permute-start | bytes 294920 | tf_op jit(solution)/shard_map/ppermute | solution.py:551
  162.6 27.9 %collective-permute-start.17 = (bf16[32,1536]{1,0:T(8,128)(2,1)S(1)}, bf16[32,1536]{1,0:T(8,128)(2,1)S(1)}, u32[]{:S(2)}, u32[]{:S(2)}) collective-permute-start(bf16[32,1536]{1,0:T(8,128)(2,1)S(1)} %get-tuple-element.111), channel_id=1, source_target_pairs={{0,16},{4,20},{8,24},{12,28},{16,0},{20,4},{24,8},{28,12},{1,17},{... | collective-permute-start | bytes 294920 | tf_op jit(solution)/shard_map/ppermute | solution.py:551
  163.2 27.4 %collective-permute-start.16 = (bf16[32,1536]{1,0:T(8,128)(2,1)S(1)}, bf16[32,1536]{1,0:T(8,128)(2,1)S(1)}, u32[]{:S(2)}, u32[]{:S(2)}) collective-permute-start(bf16[32,1536]{1,0:T(8,128)(2,1)S(1)} %get-tuple-element.112), channel_id=1, source_target_pairs={{0,24},{4,28},{8,0},{12,4},{16,8},{20,12},{24,16},{28,20},{1,25},{... | collective-permute-start | bytes 294920 | tf_op jit(solution)/shard_map/ppermute | solution.py:551
  186.0 14.9 %collective-permute-start.21 = (bf16[32,1536]{1,0:T(8,128)(2,1)S(1)}, bf16[32,1536]{1,0:T(8,128)(2,1)S(1)}, u32[]{:S(2)}, u32[]{:S(2)}) collective-permute-start(bf16[32,1536]{1,0:T(8,128)(2,1)S(1)} %get-tuple-element.75), channel_id=1, source_target_pairs={{0,24},{4,28},{8,0},{12,4},{16,8},{20,12},{24,16},{28,20},{1,25},{... | collective-permute-start | bytes 294920 | tf_op jit(solution)/shard_map/ppermute | solution.py:551
  186.6 14.3 %collective-permute-start.22 = (bf16[32,1536]{1,0:T(8,128)(2,1)S(1)}, bf16[32,1536]{1,0:T(8,128)(2,1)S(1)}, u32[]{:S(2)}, u32[]{:S(2)}) collective-permute-start(bf16[32,1536]{1,0:T(8,128)(2,1)S(1)} %get-tuple-element.77), channel_id=1, source_target_pairs={{0,16},{4,20},{8,24},{12,28},{16,0},{20,4},{24,8},{28,12},{1,17},{... | collective-permute-start | bytes 294920 | tf_op jit(solution)/shard_map/ppermute | solution.py:551
  188.1 12.8 %collective-permute-start.23 = (bf16[32,1536]{1,0:T(8,128)(2,1)S(1)}, bf16[32,1536]{1,0:T(8,128)(2,1)S(1)}, u32[]{:S(2)}, u32[]{:S(2)}) collective-permute-start(bf16[32,1536]{1,0:T(8,128)(2,1)S(1)} %get-tuple-element.79), channel_id=1, source_target_pairs={{0,8},{4,12},{8,16},{12,20},{16,24},{20,28},{24,0},{28,4},{1,9},{5... | collective-permute-start | bytes 294920 | tf_op jit(solution)/shard_map/ppermute | solution.py:551
  193.7 7.2 %collective-permute-start.20 = (bf16[2,4,1,1536]{3,2,1,0:T(2,128)(2,1)S(1)}, bf16[2,4,1,1536]{3,2,1,0:T(2,128)(2,1)S(1)}, u32[]{:S(2)}, u32[]{:S(2)}) collective-permute-start(bf16[2,4,1,1536]{3,2,1,0:T(2,128)(2,1)S(1)} %get-tuple-element.73), channel_id=1, source_target_pairs={{1,0},{2,1},{3,2},{4,3},{5,4},{6,5},{7,6},{8,7},{9,8},{10,9},{11,1... | collective-permute-start | bytes 73736 | tf_op jit(solution)/shard_map/ppermute | solution.py:542
  (39 other events, 179.9 us)
Sparse Core Ops, SparseCore 0:
  9.6 35.9 all-gather.7
  47.7 35.9 all-gather.5
  111.9 42.6 reduce-scatter.1
  157.0 43.6 all-gather.9

commit v6 on v4

--- a/solution.py
+++ b/solution.py
@@ -9,7 +9,7 @@
 
 DH = 192
 KW = 5
-VMEM_LIMIT = 56 * 1024 * 1024
+VMEM_LIMIT = 24 * 1024 * 1024
 COST = pl.CostEstimate(flops=1000, bytes_accessed=1000, transcendentals=0)
 BF = jnp.bfloat16
 F32 = jnp.float32
@@ -407,23 +407,6 @@
     )(place, mine, got, weight)
 
 
-def sum_kernel(*refs):
-    total = refs[0][...].astype(F32)
-    for ref in refs[1:-1]:
-        total = total + ref[...].astype(F32)
-    refs[-1][...] = total.astype(BF)
-
-
-def summed(parts, name):
-    return pl.pallas_call(
-        sum_kernel,
-        out_shape=jax.ShapeDtypeStruct(parts[0].shape, BF),
-        compiler_params=params(),
-        cost_estimate=COST,
-        name=name,
-    )(*parts)
-
-
 def weight_kernel(at_ref, xa_ref, xb_ref, ga_ref, gb_ref, ra_ref, rb_ref, *rest):
     del at_ref
     out_refs, turned = rest[:-1], rest[-1]
@@ -470,56 +453,79 @@
 
 
 def weight_sum_kernel(*refs):
-    out_ref = refs[-1]
+    part_refs, out_refs = refs[:-2], refs[-2:]
     split = 3 * DH
-    total = refs[0][...].astype(F32)
-    for ref in refs[1:-1]:
+    total = part_refs[0][...].astype(F32)
+    for ref in part_refs[1:]:
         total = total + ref[...].astype(F32)
-    out_ref[:, :split] = total[:split].T.astype(BF)
-    for part in range(2):
+    turned = total[:split].T.astype(BF)
+    for part, out_ref in enumerate(out_refs):
         rows = slice(part * DH, (part + 1) * DH)
-        out_ref[rows, split:] = total[split:, rows].astype(BF)
+        out_ref[:, :split] = turned[rows]
+        out_ref[:, split:] = total[split:, rows].astype(BF)
 
 
 def weight_sum(parts):
     full, chunk = parts[0].shape
     return pl.pallas_call(
         weight_sum_kernel,
-        out_shape=jax.ShapeDtypeStruct((chunk, full), BF),
+        out_shape=[jax.ShapeDtypeStruct((chunk // 2, full), BF)] * 2,
         compiler_params=params(),
         cost_estimate=COST,
         name="weight_sum",
     )(*parts)
 
 
-def unpack_kernel(at_ref, mine_ref, other_ref, qkv_ref, out_ref):
-    first_head = at_ref[0] == 0
-    mine = mine_ref[0].astype(F32)
-    other = other_ref[0].astype(F32)
-    low = jnp.where(first_head, mine, other)
-    high = jnp.where(first_head, other, mine)
+def unpack_kernel(at_ref, *refs):
+    qkv_ref, out_ref = refs[-2:]
+    step = pl.program_id(0)
     split = 3 * DH
-    for i in range(3):
-        columns = slice(i * DH, (i + 1) * DH)
-        qkv_ref[i] = jnp.concatenate([low[:, columns], high[:, columns]], axis=1)
-    for head, value in enumerate((low, high)):
-        halves = [value[part * DH : (part + 1) * DH, split:] for part in range(2)]
-        out_ref[head * DH : (head + 1) * DH, :] = jnp.concatenate(halves, axis=1)
+    for turn in range(4):
+
+        @pl.when(step == turn)
+        def _():
+            both = []
+            for near_a, near_b, far_a, far_b in (refs[:4], refs[4:8]):
+                first = near_a if turn < 2 else far_a
+                second = near_b if turn % 2 == 0 else far_b
+                both.append((first[...].astype(F32), second[...].astype(F32)))
+            swapped = at_ref[1] != 0
+            for part in range(2):
+                mine, other = both[0][part], both[1][part]
+                low = jnp.where(swapped, other, mine)
+                high = jnp.where(swapped, mine, other)
+                rows = slice(part * DH, (part + 1) * DH)
+                for i in range(3):
+                    columns = slice(i * DH, (i + 1) * DH)
+                    qkv_ref[i, rows, :] = jnp.concatenate(
+                        [low[:, columns], high[:, columns]], axis=1
+                    )
+                out_ref[:DH, rows] = low[:, split:]
+                out_ref[DH:, rows] = high[:, split:]
 
 
 def unpack_weights(at, mine, other):
-    seqs, chunk, full = mine.shape
-    width = chunk * seqs
+    rows, full = mine[0].shape
+    half = rows // 2
+    width = 4 * rows
     local = 2 * DH
-    block = pl.BlockSpec((1, chunk, full), lambda r: (r, 0, 0))
+    specs = [
+        pl.BlockSpec((half, full), lambda j, at: (jnp.minimum(j, 1), 0)),
+        pl.BlockSpec((half, full), lambda j, at: (j // 2, 0)),
+        pl.BlockSpec((half, full), lambda j, at: (jnp.maximum(j - 2, 0), 0)),
+        pl.BlockSpec((half, full), lambda j, at: (j // 2, 0)),
+    ]
     return pl.pallas_call(
         unpack_kernel,
-        grid=(seqs,),
-        in_specs=[SCALARS, block, block],
-        out_specs=[
-            pl.BlockSpec((3, chunk, local), lambda r: (0, r, 0)),
-            pl.BlockSpec((local, chunk), lambda r: (0, r)),
-        ],
+        grid_spec=pltpu.PrefetchScalarGridSpec(
+            num_scalar_prefetch=1,
+            grid=(4,),
+            in_specs=specs * 2,
+            out_specs=[
+                pl.BlockSpec((3, rows, local), lambda j, at: (0, at[0] ^ j, 0)),
+                pl.BlockSpec((local, rows), lambda j, at: (0, at[0] ^ j)),
+            ],
+        ),
         out_shape=[
             jax.ShapeDtypeStruct((3, width, local), F32),
             jax.ShapeDtypeStruct((local, width), F32),
@@ -527,7 +533,7 @@
         compiler_params=params(),
         cost_estimate=COST,
         name="weight_outputs",
-    )(at, mine, other)
+    )(at, *mine, *other)
 
 
 def neighbour_edges(first, last):
@@ -547,9 +553,9 @@
     return lax.ppermute(x, "seq", [(s, (s + step * heads) % count) for s in range(count)])
 
 
-def send_z(x, step):
-    count = lax.axis_size("head")
-    return lax.ppermute(x, "head", [(z, (z + step) % count) for z in range(count)])
+def trade_chip(x, bit, heads):
+    count = lax.axis_size("seq")
+    return lax.ppermute(x, "seq", [(s, s ^ (bit * heads)) for s in range(count)])
 
 
 def swap_heads(x):
@@ -568,7 +574,6 @@
     place = lax.axis_index("seq")
     own_seq = (place // heads).astype(jnp.int32)
     own_head = (place % heads).astype(jnp.int32)
-    own_z = lax.axis_index("head").astype(jnp.int32)
     zero = jnp.zeros((), jnp.int32)
     at = jnp.stack([own_seq, own_head])
     head_mine = own_head.reshape(1)
@@ -580,8 +585,7 @@
     def from_chips(slots):
         return [slots[r] if r == 0 else send_chip(slots[r], -r, heads) for r in range(seqs)]
 
-    grad = jnp.transpose(grad_out, (1, 0, 2))
-    grad_z = lax.all_gather(grad, "head", axis=0, tiled=False)
+    grad_z = lax.all_gather(grad_out, "head", axis=0, tiled=False)
     pairs = jnp.transpose(enc_in.reshape(rows, 2, seqs, enc_in.shape[2]), (1, 2, 0, 3))
     low, high = neighbour_edges(pairs[:, :, :1, :], pairs[:, :, -1:, :])
     skip, slope, normed = encoder(at, pairs, low, high, conv_weight, norm_gain)
@@ -590,7 +594,7 @@
 
     grad_z = after(grad_z, normed_slab)
     grad_slots = [
-        lax.dynamic_index_in_dim(grad_z, (own_seq + r) % seqs, 1, keepdims=False)
+        lax.dynamic_index_in_dim(grad_z, (own_seq + r) % seqs, 2, keepdims=False)
         for r in range(seqs)
     ]
     grad_rows = jnp.stack(to_chips(grad_slots), axis=1).reshape(half, width)
@@ -623,29 +627,35 @@
         result_other,
         seqs,
     )
-    part = to_chips(part)
-    turned = jnp.stack([own_head, own_z])
-    head_term = pair_term(
-        turned, result_mine, result_got, w_rows, groups, 3 * DH, 4 * DH, "head_term"
-    )
-    head_slots = [head_term[0], send_z(head_term[1], 1)]
-    head_slots += [send_z(after(head_term[q], d_normed), q) for q in range(2, groups)]
-    part = [after(p, d_normed) for p in part]
+    (head_term,) = pair_term(
+        plain, result_mine, after(result_got, *part), w_rows, 1, 3 * DH, 4 * DH, "head_term"
+    )
+    head_sum = lax.psum_scatter(
+        head_term.reshape(groups, seqs, rows, width), "head", scatter_dimension=0, tiled=False
+    )
+
+    half_a, half_b = weight_sum([after(p, head_term) for p in to_chips(part)])
+    got_a = trade_chip(half_a, 1, heads)
+    got_b = trade_chip(half_b, 2, heads)
+
     d_normed = from_chips([d_normed[r] for r in range(seqs)])
-    chunk = weight_sum(part)
-    same_head = [[b * heads + h for b in range(seqs)] for h in range(heads)]
-    chunks = lax.all_gather(chunk, "seq", axis_index_groups=same_head)
-
+    grad = jnp.transpose(after(grad_out, d_term), (1, 0, 2))
+    d_normed[0] = after(d_normed[0], half_a)
     d_conv, first, last = conv_gradient(at, d_normed, skip, grad, norm_gain, slope)
     low, high = neighbour_edges(first, last)
-    grad_input = conv_back(d_conv, low, high, conv_weight)
-
-    head_slots = [after(h, low, high) for h in head_slots]
-    head_sum = summed(head_slots, "head_sum").reshape(seqs, rows, width)
+    near_a = jnp.concatenate([half_a, after(got_a, first)], axis=0)
+    near_b = jnp.concatenate([half_b, after(got_b, first)], axis=0)
+    far_a = trade_chip(near_a, 2, heads)
+    far_b = trade_chip(near_b, 1, heads)
+    grad_input = conv_back(d_conv, after(low, near_a, near_b), high, conv_weight)
+    mine = [near_a, near_b, far_a, far_b]
+    other = [swap_heads(after(x, high)) for x in mine[:2]]
+    other += [swap_heads(after(x, grad_input)) for x in mine[2:]]
+    grad_w_qkv, grad_w_out = unpack_weights(at, mine, other)
+
+    head_sum = after(head_sum, grad_input)
     head_sum = from_chips([head_sum[r] for r in range(seqs)])
     mixed = mixed_call(at, head_sum, skip)
-    chunks = after(chunks, grad_input)
-    grad_w_qkv, grad_w_out = unpack_weights(head_mine, chunks, swap_heads(chunks))
     grad_input = jnp.transpose(grad_input.reshape(2, seqs, rows, -1), (2, 0, 1, 3))
     return (
         jnp.transpose(mixed, (1, 0, 2)),
@@ -796,7 +806,7 @@
 def body(enc_in, conv_weight, norm_gain, w_qkv, w_out, grad_out):
     heads = w_qkv.shape[2] // DH
     seqs = enc_in.shape[1]
-    fits = heads == 2 and seqs * heads == lax.axis_size("seq")
+    fits = heads == 2 and seqs == 4 and seqs * heads == lax.axis_size("seq")
     fits = fits and conv_weight.shape[2] == seqs * w_qkv.shape[2]
     chosen = unit_body if fits else gathered_body
     return chosen(enc_in, conv_weight, norm_gain, w_qkv, w_out, grad_out)

time: 270 us -> 224 us (0.83)
  Pallas kernels: 87.2 us -> 47.8 us
  waiting for transfers between devices: 110 us -> 78.4 us
  local copies, waits for them, and re-layouts: 21.5 us -> 40.2 us
  starting transfers between devices: 34.4 us -> 41.7 us
    ppermute x3 -> x4, waiting for transfers between devices: 34.4 us -> 0.01 us  [trade_chip(): return lax.ppermute(x, 'seq', [(s, s ^ bit * heads) for s in range(count)])]
    ppermute x15, waiting for transfers between devices: 46.8 us -> 64.6 us  [send_chip(): lax.ppermute(x, 'seq', [(s, (s + step * heads) % count) for s in range(co...]
    unnamed x61 -> x74, local copies, waits for them, and re-layouts: 15 us -> 31.3 us
    pallas_call x4, Pallas kernels: 14.8 us -> 4.65 us  [head_product(): pl.pallas_call(functools.partial(product_kernel, contract=contract), grid...]
    reduce_scatter x1, waiting for transfers between devices: 8.45 us -> 0.02 us  [unit_body(): lax.psum_scatter(d_term.reshape(groups, seqs, rows, width), 'head', scatt...]
    ppermute x6 -> x9, starting transfers between devices: 0.65 us -> 7.21 us  [swap_heads(): lax.ppermute(x, 'seq', [(s, s + 1 - 2 * (s % 2)) for s in range(count)])]
    all_gather x2 -> x1, waiting for transfers between devices: 12.1 us -> 5.72 us  [unit_body(): grad_z = lax.all_gather(grad_out, 'head', axis=0, tiled=False)]
    pallas_call x3 -> x2, Pallas kernels: 11.9 us -> 6.06 us  [the longest x1 4.88 us: unpack_weights(): pl.pallas_call(unpack_kernel, grid_spec=pltpu.PrefetchScalarGridSpec(num_...]
  transfers between devices with their start and end apart: 32 -> 36, of which waited for: 23 -> 20; matrix products, arithmetic and copies ran while one was open for 4% -> 6% of each run, Pallas kernels for 23% -> 15%
where the time goes in v6:
time: 224 us; the launch traced here: 223 us
  waiting for transfers between devices  78.4 us (35%)
  Pallas kernels  47.8 us (21%)
  starting transfers between devices  41.7 us (19%)
  local copies, waits for them, and re-layouts  40.2 us (18%)
  between operations  14.3 us (6%)
    ppermute x15, waiting for transfers between devices, send_chip(): lax.ppermute(x, 'seq', [(s, (s + step * heads) % count) for s in range(co...  64.6 us
    unnamed x74, local copies, waits for them, and re-layouts  31.3 us
    ppermute x15, starting transfers between devices, send_chip(): lax.ppermute(x, 'seq', [(s, (s + step * heads) % count) for s in range(co...  16.5 us
    ppermute x9, starting transfers between devices, swap_heads(): lax.ppermute(x, 'seq', [(s, s + 1 - 2 * (s % 2)) for s in range(count)])  7.21 us
    pallas_call x1, Pallas kernels, encoder(): pl.pallas_call(conv_kernel, grid=(width // tile,), in_specs=[SCALARS, who...  7.1 us
    pallas_call x2, Pallas kernels, pair_term(): pl.pallas_call(functools.partial(term_kernel, first=first, last=last), gr...  7.01 us
    ppermute x2, starting transfers between devices, neighbour_edges(): lax.ppermute(last, axes, forward)  6.91 us
    pallas_call x1, Pallas kernels, attention(): pl.pallas_call(functools.partial(attention_kernel, block=min(256, half)),...  6.53 us
  transfers between devices with their start and end apart: 36, of which 20 were waited for; matrix products, arithmetic and copies ran while one was open for 6% of the time, Pallas kernels for 15%

profile of v6, /device:TPU:26, one launch (start us, length us, event | category | flops | bytes accessed | tf_op | source)
XLA Modules:
  0.0 222.7 jit_solution(9012038245161482018)
XLA Ops:
  11.4 5.0 %collective-permute-start = (bf16[2,4,1,768]{3,2,1,0:T(2,128)(2,1)S(1)}, bf16[2,4,1,768]{3,2,1,0:T(2,128)(2,1)S(1)}, u32[]{:S(2)}, u32[]{:S(2)}) collective-permute-start(bf16[2,4,1,768]{3,2,1,0:T(2,128)(2,1)S(1)} %get-tuple-element.109), channel_id=1, source_target_pairs={{0,1},{1,2},{2,3},{3,4},{4,5},{5,6},{6,7},{7,8},{8,9},{9,10},{10,1... | collective-permute-start | bytes 36872 | tf_op jit(solution)/shard_map/ppermute | solution.py:544
  17.9 4.5 %copy-done = bf16[5,768,1536]{2,1,0:T(8,128)(2,1)S(1)} copy-done((bf16[5,768,1536]{2,1,0:T(8,128)(2,1)S(1)}, bf16[5,768,1536]{2,1,0:T(8,128)(2,1)}, u32[]{:S(2)}) %copy-start) | copy-done | bytes 11796504
  22.5 7.1 %encoder_forward.1 = (bf16[4,32,1536]{2,1,0:T(8,128)(2,1)S(1)}, f32[2,4,32,1536]{3,2,1,0:T(8,128)S(1)}, bf16[32,1536]{1,0:T(8,128)(2,1)S(1)}, bf16[32,1536]{1,0:...) custom-call(s32[2]{0:T(128)S(1)} %pad_add_fusion.at_ref, ...), custom_call_target="tpu_custom_call" | custom-call | flops 1000 | bytes 1000 | tf_op jit(solution)/shard_map/encoder_forward/pallas_call | solution.py:109
  36.4 2.6 %collective-permute-done.3 = bf16[32,1536]{1,0:T(8,128)(2,1)S(1)} collective-permute-done((bf16[32,1536]{1,0:T(8,128)(2,1)S(1)}, bf16[32,1536]{1,0:T(8,128)(2,1)S(1)}, u32[]{:S(2)}, u32[]{:S(2)}) %collective-permute-start.3) | collective-permute-done | bytes 98336 | tf_op jit(solution)/shard_map/ppermute | solution.py:553
  39.9 5.7 %all-gather.6.cloned.1.call-done = bf16[128,4,1536]{2,1,0:T(4,128)(2,1)} async-done(((bf16[32,4,1536]{2,1,0:T(4,128)(2,1)}), bf16[128,4,1536]{2,1,0:T(4,128)(2,1)}) %all-gather.6.cloned.1.call-update) | async-done | bytes 1572880 | tf_op jit(solution)/shard_map/all_gather | solution.py:588
  49.5 2.4 %collective-permute-start.5 = (bf16[4,32,1536]{2,1,0:T(8,128)(2,1)S(1)}, bf16[4,32,1536]{2,1,0:T(8,128)(2,1)S(1)}, u32[]{:S(2)}, u32[]{:S(2)}) collective-permute-start(bf16[4,32,1536]{2,1,0:T(8,128)(2,1)S(1)} %get-tuple-element.99), channel_id=1, source_target_pairs={{0,8},{4,12},{8,16},{12,20},{16,24},{20,28},{24,0},{28,4},{1,9},{5... | collective-permute-start | bytes 1179656 | tf_op jit(solution)/shard_map/ppermute | solution.py:553
  51.9 8.5 %collective-permute-done.7 = bf16[4,32,1536]{2,1,0:T(8,128)(2,1)S(1)} collective-permute-done((bf16[4,32,1536]{2,1,0:T(8,128)(2,1)S(1)}, bf16[4,32,1536]{2,1,0:T(8,128)(2,1)S(1)}, u32[]{:S(2)}, u32[]{:S(2)}) %collective-permute-start.7) | collective-permute-done | bytes 393248 | tf_op jit(solution)/shard_map/ppermute | solution.py:553
  60.4 6.6 %collective-permute-done.6 = bf16[4,32,1536]{2,1,0:T(8,128)(2,1)S(1)} collective-permute-done((bf16[4,32,1536]{2,1,0:T(8,128)(2,1)S(1)}, bf16[4,32,1536]{2,1,0:T(8,128)(2,1)S(1)}, u32[]{:S(2)}, u32[]{:S(2)}) %collective-permute-start.6) | collective-permute-done | bytes 393248 | tf_op jit(solution)/shard_map/ppermute | solution.py:553
  72.7 3.9 %pack_weights.1 = (bf16[2,1536,576]{2,1,0:T(8,128)(2,1)S(1)}, bf16[2,576,1536]{2,1,0:T(8,128)(2,1)S(1)}) custom-call(bf16[3,1536,384]{2,1,0:T(8,128)(2,1)S(1)} %copy-done.11), custom_call_target="tpu_custom_call" | custom-call | flops 1000 | bytes 1000 | tf_op jit(solution)/shard_map/pack_weights/pallas_call | solution.py:261
  91.7 6.5 %attention.1 = (bf16[512,768]{1,0:T(8,128)(2,1)S(1)}, bf16[512,768]{1,0:T(8,128)(2,1)S(1)}) custom-call(bf16[512,640]{1,0:T(8,128)(2,1)S(1)} %qkv_own.1.qa_ref, bf16[512,640]{1,0:T(8,128)(2,1)S(1)} %collective-permute-done.11.qb_ref, bf16[512,256]{1,0:T(8,128)(2,1)S(1)} %copy-done.21, bf16[512,256]{1,0:T(8,128)(2,1)S(1)} %copy-done.27), custom_call_target="tpu_custom_call" | custom-call | flops 1000 | bytes 1000 | tf_op jit(solution)/shard_map/attention/pallas_call | solution.py:353
  100.6 3.8 %d_term.1 = bf16[512,1536]{1,0:T(8,128)(2,1)S(1)} custom-call(s32[2]{0:T(128)S(1)} %pad_add_fusion.1.head_ref, bf16[512,768]{1,0:T(8,128)(2,1)S(1)} %get-tuple-element.54.ra_ref.a_ref, bf16[512,768]{1,0:T(8,128)(2,1)S(1)} %collective-permute-done.12.b_ref, bf16[2,576,1536]{2,1,0:T(8,128)(2,1)S(1)} %copy-done.13), custom_call_target="tpu_custom_call" | custom-call | flops 1000 | bytes 1000 | tf_op jit(solution)/shard_map/d_term/pallas_call | solution.py:391
  109.6 6.4 %weight_gradients.1 = (bf16[768,384]{1,0:T(8,128)(2,1)S(1)}, bf16[768,384]{1,0:T(8,128)(2,1)S(1)}, bf16[768,384]{1,0:T(8,128)(2,1)S(1)}, bf16[768,384]{1,0:T(8,128)(2,1)S(1)}) custom-call(s32[1]{0:T(128)} %bitcast.at_ref, bf16[512,1536]{1,0:T(8,128)(2,1)S(1)} %copy-done.5, bf16[512,1536]{1,0:T(8,128)(2,1)S(1)} %copy-done.19, bf16[512,1536]{1,0:T(8,128)(2,1)S(1)} %bitcast.51, ...), custom_call_target="tpu_custom_call" | custom-call | flops 1000 | bytes 1000 | tf_op jit(solution)/shard_map/weight_gradients/pallas_call | solution.py:439
  116.0 3.2 %head_term.1 = bf16[512,1536]{1,0:T(8,128)(2,1)} custom-call(s32[2]{0:T(128)S(1)} %pad_add_fusion.1.head_ref, bf16[512,768]{1,0:T(8,128)(2,1)S(1)} %copy-done.9, bf16[512,768]{1,0:T(8,128)(2,1)S(1)} %copy-done.15, bf16[2,192,1536]{2,1,0:T(8,128)(2,1)S(1)} %bitcast.54), custom_call_target="tpu_custom_call" | custom-call | flops 1000 | bytes 1000 | tf_op jit(solution)/shard_map/head_term/pallas_call | solution.py:391
  123.7 12.9 %collective-permute-done.15.refs_3_ = bf16[768,384]{1,0:T(8,128)(2,1)S(1)} collective-permute-done((bf16[768,384]{1,0:T(8,128)(2,1)}, bf16[768,384]{1,0:T(8,128)(2,1)S(1)}, u32[]{:S(2)}, u32[]{:S(2)}) %collective-permute-start.15) | collective-permute-done | bytes 589856 | tf_op jit(solution)/shard_map/ppermute | solution.py:553
  136.6 11.4 %collective-permute-done.14.refs_2_ = bf16[768,384]{1,0:T(8,128)(2,1)S(1)} collective-permute-done((bf16[768,384]{1,0:T(8,128)(2,1)}, bf16[768,384]{1,0:T(8,128)(2,1)S(1)}, u32[]{:S(2)}, u32[]{:S(2)}) %collective-permute-start.14) | collective-permute-done | bytes 589856 | tf_op jit(solution)/shard_map/ppermute | solution.py:553
  158.9 3.3 %collective-permute-done.18.refs_3_ = bf16[32,1536]{1,0:T(8,128)(2,1)S(1)} collective-permute-done((bf16[32,1536]{1,0:T(8,128)(2,1)S(1)}, bf16[32,1536]{1,0:T(8,128)(2,1)S(1)}, u32[]{:S(2)}, u32[]{:S(2)}) %collective-permute-start.18) | collective-permute-done | bytes 98336 | tf_op jit(solution)/shard_map/ppermute | solution.py:553
  171.2 3.9 %collective-permute-start.22 = (bf16[2,4,1,1536]{3,2,1,0:T(2,128)(2,1)S(1)}, bf16[2,4,1,1536]{3,2,1,0:T(2,128)(2,1)S(1)}, u32[]{:S(2)}, u32[]{:S(2)}) collective-permute-start(bf16[2,4,1,1536]{3,2,1,0:T(2,128)(2,1)S(1)} %get-tuple-element.72), channel_id=1, source_target_pairs={{1,0},{2,1},{3,2},{4,3},{5,4},{6,5},{7,6},{8,7},{9,8},{10,9},{11,1... | collective-permute-start | bytes 73736 | tf_op jit(solution)/shard_map/ppermute | solution.py:544
  178.4 4.3 %copy-done.1 = bf16[5,768,1536]{2,1,0:T(8,128)(2,1)S(1)} copy-done((bf16[5,768,1536]{2,1,0:T(8,128)(2,1)S(1)}, bf16[5,768,1536]{2,1,0:T(8,128)(2,1)}, u32[]{:S(2)}) %copy-start.1) | copy-done | bytes 11796504
  182.7 4.3 %encoder_backward.1 = bf16[256,768]{1,0:T(8,128)(2,1)S(1)} custom-call(bf16[2,4,32,1536]{3,2,1,0:T(8,128)(2,1)S(1)} %get-tuple-element.70.d_ref, bf16[2,4,1,1536]{3,2,1,0:T(2,128)(2,1)S(1)} %collective-permute-done.19.low_ref, bf16[2,4,1,1536]{3,2,1,0:T(2,128)(2,1)S(1)} %collective-permute-done.22.high_ref, bf16[5,768,1536]{2,1,0:T(8,128)(2,1)S(1)} %copy-done.1), custom_call_target="tpu_custom_call" | custom-call | flops 1000 | bytes 1000 | tf_op jit(solution)/shard_map/encoder_backward/pallas_call | solution.py:227
  187.1 5.5 %collective-permute-start.28 = (bf16[384,768]{1,0:T(8,128)(2,1)S(1)}, bf16[384,768]{1,0:T(8,128)(2,1)S(1)}, u32[]{:S(2)}, u32[]{:S(2)}) collective-permute-start(bf16[384,768]{1,0:T(8,128)(2,1)S(1)} %constant_dynamic-update-slice_fusion.4.refs_0_), channel_id=1, source_target_pairs={{0,4},{4,0},{8,12},{12,8},{16,20},{20,16},{24,28},{28,24},{1,5},{5... | collective-permute-start | bytes 1769480 | tf_op jit(solution)/shard_map/ppermute | solution.py:563
  194.3 5.1 %collective-permute-done.25.refs_3_ = bf16[32,1536]{1,0:T(8,128)(2,1)S(1)} collective-permute-done((bf16[32,1536]{1,0:T(8,128)(2,1)S(1)}, bf16[32,1536]{1,0:T(8,128)(2,1)S(1)}, u32[]{:S(2)}, u32[]{:S(2)}) %collective-permute-start.25) | collective-permute-done | bytes 98336 | tf_op jit(solution)/shard_map/ppermute | solution.py:553
  199.5 4.6 %collective-permute-done.24.refs_2_ = bf16[32,1536]{1,0:T(8,128)(2,1)S(1)} collective-permute-done((bf16[32,1536]{1,0:T(8,128)(2,1)S(1)}, bf16[32,1536]{1,0:T(8,128)(2,1)S(1)}, u32[]{:S(2)}, u32[]{:S(2)}) %collective-permute-start.24) | collective-permute-done | bytes 98336 | tf_op jit(solution)/shard_map/ppermute | solution.py:553
  205.6 4.0 %collective-permute-done.23.refs_1_ = bf16[32,1536]{1,0:T(8,128)(2,1)S(1)} collective-permute-done((bf16[32,1536]{1,0:T(8,128)(2,1)S(1)}, bf16[32,1536]{1,0:T(8,128)(2,1)S(1)}, u32[]{:S(2)}, u32[]{:S(2)}) %collective-permute-start.23) | collective-permute-done | bytes 98336 | tf_op jit(solution)/shard_map/ppermute | solution.py:553
  211.3 4.9 %weight_outputs.1 = (f32[3,1536,384]{2,1,0:T(8,128)}, f32[384,1536]{1,0:T(8,128)}) custom-call(s32[2]{0:T(128)S(1)} %pad_add_fusion.at_ref, bf16[384,768]{1,0:T(8,128)(2,1)S(1)} %constant_dynamic-update-slice_fusion.4.refs_0_, bf16[384,768]{1,0:T(8,128)(2,1)S(1)} %constant_dynamic-update-slice_fusion.6.refs_1_, ...), custom_call_target="tpu_custom_call" | custom-call | flops 1000 | bytes 1000 | tf_op jit(solution)/shard_map/weight_outputs/pallas_call | solution.py:518
  (157 shorter events, 77.8 us)
Async XLA Ops:
  7.2 38.4 %all-gather.6.cloned.1.call-start = ((), (), s32[]{:S(2)}) async-start(), calls=%async_computation.5 | async-start | bytes 1966080 | tf_op jit(solution)/shard_map/all_gather | solution.py:588
  7.9 75.8 %all-gather.4.cloned.1.call-start = ((), (), s32[]{:S(2)}) async-start(), calls=%async_computation.2 | async-start | bytes 1966080 | tf_op jit(solution)/shard_map/all_gather | solution.py:593
  9.1 8.2 %collective-permute-start.1 = (bf16[2,4,1,768]{3,2,1,0:T(2,128)(2,1)S(1)}, bf16[2,4,1,768]{3,2,1,0:T(2,128)(2,1)S(1)}, u32[]{:S(2)}, u32[]{:S(2)}) collective-permute-start(bf16[2,4,1,768]{3,2,1,0:T(2,128)(2,1)S(1)} %get-tuple-element.108), channel_id=1, source_target_pairs={{1,0},{2,1},{3,2},{4,3},{5,4},{6,5},{7,6},{8,7},{9,8},{10,9},{11,1... | collective-permute-start | bytes 36872 | tf_op jit(solution)/shard_map/ppermute | solution.py:544
  39.8 113.4 %reduce-scatter.5.cloned.1.call-start = ((), (), s32[]{:S(2)}) async-start(), calls=%async_computation.4 | async-start | bytes 1966080 | tf_op jit(solution)/shard_map/reduce_scatter | solution.py:617
  47.4 13.0 %collective-permute-start.7 = (bf16[4,32,1536]{2,1,0:T(8,128)(2,1)S(1)}, bf16[4,32,1536]{2,1,0:T(8,128)(2,1)S(1)}, u32[]{:S(2)}, u32[]{:S(2)}) collective-permute-start(bf16[4,32,1536]{2,1,0:T(8,128)(2,1)S(1)} %get-tuple-element.97), channel_id=1, source_target_pairs={{0,24},{4,28},{8,0},{12,4},{16,8},{20,12},{24,16},{28,20},{1,25},{... | collective-permute-start | bytes 1179656 | tf_op jit(solution)/shard_map/ppermute | solution.py:553
  48.0 19.0 %collective-permute-start.6 = (bf16[4,32,1536]{2,1,0:T(8,128)(2,1)S(1)}, bf16[4,32,1536]{2,1,0:T(8,128)(2,1)S(1)}, u32[]{:S(2)}, u32[]{:S(2)}) collective-permute-start(bf16[4,32,1536]{2,1,0:T(8,128)(2,1)S(1)} %get-tuple-element.98), channel_id=1, source_target_pairs={{0,16},{4,20},{8,24},{12,28},{16,0},{20,4},{24,8},{28,12},{1,17},{... | collective-permute-start | bytes 1179656 | tf_op jit(solution)/shard_map/ppermute | solution.py:553
  49.5 18.4 %collective-permute-start.5 = (bf16[4,32,1536]{2,1,0:T(8,128)(2,1)S(1)}, bf16[4,32,1536]{2,1,0:T(8,128)(2,1)S(1)}, u32[]{:S(2)}, u32[]{:S(2)}) collective-permute-start(bf16[4,32,1536]{2,1,0:T(8,128)(2,1)S(1)} %get-tuple-element.99), channel_id=1, source_target_pairs={{0,8},{4,12},{8,16},{12,20},{16,24},{20,28},{24,0},{28,4},{1,9},{5... | collective-permute-start | bytes 1179656 | tf_op jit(solution)/shard_map/ppermute | solution.py:553
  68.2 16.2 %collective-permute-start.9 = (bf16[512,1536]{1,0:T(8,128)(2,1)S(1)}, bf16[512,1536]{1,0:T(8,128)(2,1)}, u32[]{:S(2)}, u32[]{:S(2)}) collective-permute-start(bf16[512,1536]{1,0:T(8,128)(2,1)S(1)} %bitcast.48), channel_id=1, source_target_pairs={{0,4},{4,0},{8,12},{12,8},{16,20},{20,16},{24,28},{28,24},{1,5},{5... | collective-permute-start | bytes 4718600 | tf_op jit(solution)/shard_map/ppermute | solution.py:563
  70.7 13.0 %collective-permute-start.8 = (bf16[512,256]{1,0:T(8,128)(2,1)}, bf16[512,256]{1,0:T(8,128)(2,1)S(1)}, u32[]{:S(2)}, u32[]{:S(2)}) collective-permute-start(bf16[512,256]{1,0:T(8,128)(2,1)} %d_o_other.1), channel_id=1, source_target_pairs={{0,4},{4,0},{8,12},{12,8},{16,20},{20,16},{24,28},{28,24},{1,5},{5... | collective-permute-start | bytes 786440 | tf_op jit(solution)/shard_map/ppermute | solution.py:563
  105.6 81.5 %reduce-scatter.3.cloned.1.call-start = ((), (), s32[]{:S(2)}) async-start(), calls=%async_computation.3 | async-start | bytes 1966080 | tf_op jit(solution)/shard_map/reduce_scatter | solution.py:633
  119.3 17.4 %collective-permute-start.15 = (bf16[768,384]{1,0:T(8,128)(2,1)}, bf16[768,384]{1,0:T(8,128)(2,1)S(1)}, u32[]{:S(2)}, u32[]{:S(2)}) collective-permute-start(bf16[768,384]{1,0:T(8,128)(2,1)} %copy-done.31), channel_id=1, source_target_pairs={{0,24},{4,28},{8,0},{12,4},{16,8},{20,12},{24,16},{28,20},{1,25},{... | collective-permute-start | bytes 1769480 | tf_op jit(solution)/shard_map/ppermute | solution.py:553
  119.9 28.2 %collective-permute-start.14 = (bf16[768,384]{1,0:T(8,128)(2,1)}, bf16[768,384]{1,0:T(8,128)(2,1)S(1)}, u32[]{:S(2)}, u32[]{:S(2)}) collective-permute-start(bf16[768,384]{1,0:T(8,128)(2,1)} %copy-done.30), channel_id=1, source_target_pairs={{0,16},{4,20},{8,24},{12,28},{16,0},{20,4},{24,8},{28,12},{1,17},{... | collective-permute-start | bytes 1769480 | tf_op jit(solution)/shard_map/ppermute | solution.py:553
  121.4 27.4 %collective-permute-start.13 = (bf16[768,384]{1,0:T(8,128)(2,1)S(1)}, bf16[768,384]{1,0:T(8,128)(2,1)S(1)}, u32[]{:S(2)}, u32[]{:S(2)}) collective-permute-start(bf16[768,384]{1,0:T(8,128)(2,1)S(1)} %copy-done.29), channel_id=1, source_target_pairs={{0,8},{4,12},{8,16},{12,20},{16,24},{20,28},{24,0},{28,4},{1,9},{5... | collective-permute-start | bytes 1769480 | tf_op jit(solution)/shard_map/ppermute | solution.py:553
  149.9 15.3 %collective-permute-start.21 = (bf16[192,768]{1,0:T(8,128)(2,1)}, bf16[192,768]{1,0:T(8,128)(2,1)}, u32[]{:S(2)}, u32[]{:S(2)}) collective-permute-start(bf16[192,768]{1,0:T(8,128)(2,1)} %get-tuple-element.74), channel_id=1, source_target_pairs={{0,16},{4,20},{8,24},{12,28},{16,0},{20,4},{24,8},{28,12},{1,17},{... | collective-permute-start | bytes 884744 | tf_op jit(solution)/shard_map/ppermute | solution.py:558
  150.7 14.5 %collective-permute-start.20 = (bf16[192,768]{1,0:T(8,128)(2,1)}, bf16[192,768]{1,0:T(8,128)(2,1)}, u32[]{:S(2)}, u32[]{:S(2)}) collective-permute-start(bf16[192,768]{1,0:T(8,128)(2,1)} %get-tuple-element.65), channel_id=1, source_target_pairs={{0,8},{4,12},{8,0},{12,4},{16,24},{20,28},{24,16},{28,20},{1,9},{5... | collective-permute-start | bytes 884744 | tf_op jit(solution)/shard_map/ppermute | solution.py:558
  154.3 7.8 %collective-permute-start.18 = (bf16[32,1536]{1,0:T(8,128)(2,1)S(1)}, bf16[32,1536]{1,0:T(8,128)(2,1)S(1)}, u32[]{:S(2)}, u32[]{:S(2)}) collective-permute-start(bf16[32,1536]{1,0:T(8,128)(2,1)S(1)} %get-tuple-element.104), channel_id=1, source_target_pairs={{0,8},{4,12},{8,16},{12,20},{16,24},{20,28},{24,0},{28,4},{1,9},{5... | collective-permute-start | bytes 294920 | tf_op jit(solution)/shard_map/ppermute | solution.py:553
  156.4 7.6 %collective-permute-start.16 = (bf16[32,1536]{1,0:T(8,128)(2,1)S(1)}, bf16[32,1536]{1,0:T(8,128)(2,1)S(1)}, u32[]{:S(2)}, u32[]{:S(2)}) collective-permute-start(bf16[32,1536]{1,0:T(8,128)(2,1)S(1)} %get-tuple-element.106), channel_id=1, source_target_pairs={{0,24},{4,28},{8,0},{12,4},{16,8},{20,12},{24,16},{28,20},{1,25},{... | collective-permute-start | bytes 294920 | tf_op jit(solution)/shard_map/ppermute | solution.py:553
  166.2 26.5 %collective-permute-start.26 = (bf16[384,768]{1,0:T(8,128)(2,1)S(1)}, bf16[384,768]{1,0:T(8,128)(2,1)S(1)}, u32[]{:S(2)}, u32[]{:S(2)}) collective-permute-start(bf16[384,768]{1,0:T(8,128)(2,1)S(1)} %constant_dynamic-update-slice_fusion.4.refs_0_), channel_id=1, source_target_pairs={{0,16},{4,20},{8,24},{12,28},{16,0},{20,4},{24,8},{28,12},{1,17},{... | collective-permute-start | bytes 1769480 | tf_op jit(solution)/shard_map/ppermute | solution.py:558
  167.9 25.3 %collective-permute-start.27 = (bf16[384,768]{1,0:T(8,128)(2,1)S(1)}, bf16[384,768]{1,0:T(8,128)(2,1)S(1)}, u32[]{:S(2)}, u32[]{:S(2)}) collective-permute-start(bf16[384,768]{1,0:T(8,128)(2,1)S(1)} %constant_dynamic-update-slice_fusion.6.refs_1_), channel_id=1, source_target_pairs={{0,8},{4,12},{8,0},{12,4},{16,24},{20,28},{24,16},{28,20},{1,9},{5... | collective-permute-start | bytes 1769480 | tf_op jit(solution)/shard_map/ppermute | solution.py:558
  169.2 7.9 %collective-permute-start.19 = (bf16[2,4,1,1536]{3,2,1,0:T(2,128)(2,1)S(1)}, bf16[2,4,1,1536]{3,2,1,0:T(2,128)(2,1)S(1)}, u32[]{:S(2)}, u32[]{:S(2)}) collective-permute-start(bf16[2,4,1,1536]{3,2,1,0:T(2,128)(2,1)S(1)} %get-tuple-element.71), channel_id=1, source_target_pairs={{0,1},{1,2},{2,3},{3,4},{4,5},{5,6},{6,7},{7,8},{8,9},{9,10},{10,1... | collective-permute-start | bytes 73736 | tf_op jit(solution)/shard_map/ppermute | solution.py:544
  187.1 24.2 %collective-permute-start.28 = (bf16[384,768]{1,0:T(8,128)(2,1)S(1)}, bf16[384,768]{1,0:T(8,128)(2,1)S(1)}, u32[]{:S(2)}, u32[]{:S(2)}) collective-permute-start(bf16[384,768]{1,0:T(8,128)(2,1)S(1)} %constant_dynamic-update-slice_fusion.4.refs_0_), channel_id=1, source_target_pairs={{0,4},{4,0},{8,12},{12,8},{16,20},{20,16},{24,28},{28,24},{1,5},{5... | collective-permute-start | bytes 1769480 | tf_op jit(solution)/shard_map/ppermute | solution.py:563
  192.6 18.7 %collective-permute-start.29 = (bf16[384,768]{1,0:T(8,128)(2,1)S(1)}, bf16[384,768]{1,0:T(8,128)(2,1)S(1)}, u32[]{:S(2)}, u32[]{:S(2)}) collective-permute-start(bf16[384,768]{1,0:T(8,128)(2,1)S(1)} %constant_dynamic-update-slice_fusion.6.refs_1_), channel_id=1, source_target_pairs={{0,4},{4,0},{8,12},{12,8},{16,20},{20,16},{24,28},{28,24},{1,5},{5... | collective-permute-start | bytes 1769480 | tf_op jit(solution)/shard_map/ppermute | solution.py:563
  192.7 18.6 %collective-permute-start.30 = (bf16[384,768]{1,0:T(8,128)(2,1)S(1)}, bf16[384,768]{1,0:T(8,128)(2,1)S(1)}, u32[]{:S(2)}, u32[]{:S(2)}) collective-permute-start(bf16[384,768]{1,0:T(8,128)(2,1)S(1)} %collective-permute-done.26.refs_2_), channel_id=1, source_target_pairs={{0,4},{4,0},{8,12},{12,8},{16,20},{20,16},{24,28},{28,24},{1,5},{5... | collective-permute-start | bytes 1769480 | tf_op jit(solution)/shard_map/ppermute | solution.py:563
  193.1 18.2 %collective-permute-start.31 = (bf16[384,768]{1,0:T(8,128)(2,1)S(1)}, bf16[384,768]{1,0:T(8,128)(2,1)S(1)}, u32[]{:S(2)}, u32[]{:S(2)}) collective-permute-start(bf16[384,768]{1,0:T(8,128)(2,1)S(1)} %collective-permute-done.27.refs_3_), channel_id=1, source_target_pairs={{0,4},{4,0},{8,12},{12,8},{16,20},{20,16},{24,28},{28,24},{1,5},{5... | collective-permute-start | bytes 1769480 | tf_op jit(solution)/shard_map/ppermute | solution.py:563
  (46 other events, 239.0 us)
Sparse Core Ops, SparseCore 0:
  9.6 35.9 all-gather.5
  47.7 35.9 all-gather.3
  105.7 34.2 reduce-scatter.4
  142.8 35.2 reduce-scatter.2

commit v7 on v6

--- a/solution.py
+++ b/solution.py
@@ -13,6 +13,7 @@
 COST = pl.CostEstimate(flops=1000, bytes_accessed=1000, transcendentals=0)
 BF = jnp.bfloat16
 F32 = jnp.float32
+TOKEN = jax.ShapeDtypeStruct((8, 128), F32)
 
 
 def params():
@@ -35,8 +36,8 @@
 SCALARS = pl.BlockSpec(memory_space=pltpu.SMEM)
 
 
-def wrapped(value, size):
-    return jnp.where(value < 0, value + size, jnp.where(value >= size, value - size, value))
+def spare(deps):
+    return [pl.BlockSpec(memory_space=pl.ANY)] * len(deps)
 
 
 def turned_rows(ref, low_ref, high_ref, parity, shift):
@@ -98,7 +99,7 @@
         normed = (wide * inv * gain_ref[...]).astype(BF)
         whole_normed[...] = normed.reshape(whole_normed.shape)
         for slot in range(seqs):
-            normed_refs[slot][...] = whole_normed[wrapped(at_ref[0] + slot, seqs)]
+            normed_refs[slot][...] = whole_normed[at_ref[0] ^ slot]
 
 
 def encoder(at, pairs, low, high, conv_weight, norm_gain):
@@ -139,16 +140,15 @@
     return outs[0], outs[1], list(outs[2:])
 
 
-def d_conv_body(seqs, at_ref, *refs):
-    dn_refs = refs[:seqs]
-    skip_ref, grad_ref, gain_ref, slope_ref, out_ref, first_ref, last_ref = refs[seqs:]
+def d_conv_kernel(at_ref, own_ref, near_ref, far_ref, *refs):
+    skip_ref, grad_ref, gain_ref, slope_ref, out_ref, first_ref, last_ref = refs
     rows = out_ref.shape[2]
-    for slot in range(seqs):
-        b = wrapped(at_ref[0] + slot, seqs)
+    for slot, (ref, place) in enumerate(((own_ref, 0), (near_ref, 0), (far_ref, 0), (far_ref, 1))):
+        b = at_ref[0] ^ slot
         wide = skip_ref[b].astype(F32)
         inv = lax.rsqrt(jnp.mean(wide * wide, axis=-1, keepdims=True) + 1e-06)
         unit = wide * inv
-        scaled = dn_refs[slot][...].astype(F32) * gain_ref[...]
+        scaled = ref[place].astype(F32) * gain_ref[...]
         d_skip = grad_ref[b].astype(F32) + inv * (
             scaled - unit * jnp.mean(scaled * unit, axis=-1, keepdims=True)
         )
@@ -160,25 +160,24 @@
             last_ref[parity, b] = value[rows - 1 :].astype(BF)
 
 
-def conv_gradient(at, d_normed, skip, grad, norm_gain, slope):
-    seqs = len(d_normed)
+def conv_gradient(at, own, near, far, skip, grad, norm_gain, slope):
     vmem = pl.BlockSpec(memory_space=pltpu.VMEM)
     edge = jax.ShapeDtypeStruct(slope.shape[:2] + (1, slope.shape[3]), BF)
     return pl.pallas_call(
-        functools.partial(d_conv_body, seqs),
-        in_specs=[SCALARS] + [vmem] * (seqs + 4),
+        d_conv_kernel,
+        in_specs=[SCALARS] + [vmem] * 7,
         out_specs=[vmem] * 3,
         out_shape=[jax.ShapeDtypeStruct(slope.shape, BF)] + [edge] * 2,
         compiler_params=params(),
         cost_estimate=COST,
         name="conv_gradient",
-    )(at, *d_normed, skip, grad, norm_gain.reshape(1, -1), slope)
+    )(at, own, near, far, skip, grad, norm_gain.reshape(1, -1), slope)
 
 
 def mixed_body(seqs, at_ref, *refs):
     skip_ref, out_ref = refs[seqs:]
     for slot in range(seqs):
-        b = wrapped(at_ref[0] + slot, seqs)
+        b = at_ref[0] ^ slot
         out_ref[b] = (skip_ref[b].astype(F32) + refs[slot][...].astype(F32)).astype(BF)
 
 
@@ -196,7 +195,8 @@
     )(at, *terms, skip)
 
 
-def conv_back_kernel(d_ref, low_ref, high_ref, w_ref, out_ref, turned, acc):
+def conv_back_kernel(d_ref, low_ref, high_ref, w_ref, *rest):
+    out_ref, turned, acc = rest[-3:]
     step = pl.program_id(0)
 
     @pl.when(step == 0)
@@ -220,7 +220,7 @@
                 out_ref[...] = (acc[...] + term).T.astype(BF)
 
 
-def conv_back(d_conv, low, high, conv_weight):
+def conv_back(d_conv, low, high, conv_weight, *deps):
     _, seqs, rows, width = d_conv.shape
     c_in = conv_weight.shape[1]
     flat = 2 * seqs * rows
@@ -232,7 +232,8 @@
             whole(low.shape),
             whole(high.shape),
             pl.BlockSpec((1, c_in, width), lambda k: (k, 0, 0)),
-        ],
+        ]
+        + spare(deps),
         out_specs=whole((flat, c_in)),
         out_shape=jax.ShapeDtypeStruct((flat, c_in), BF),
         scratch_shapes=[
@@ -242,10 +243,11 @@
         compiler_params=params(),
         cost_estimate=COST,
         name="encoder_backward",
-    )(d_conv, low, high, conv_weight)
-
-
-def pack_kernel(w_ref, pack_ref, turned_ref):
+    )(d_conv, low, high, conv_weight, *deps)
+
+
+def pack_kernel(w_ref, pack_ref, turned_ref, token_ref):
+    token_ref[...] = jnp.zeros_like(token_ref)
     for i in range(3):
         for head in range(pack_ref.shape[0]):
             part = w_ref[i, :, head * DH : (head + 1) * DH]
@@ -265,10 +267,12 @@
         out_specs=[
             pl.BlockSpec((heads, tile, 3 * DH), lambda n: (0, n, 0)),
             pl.BlockSpec((heads, 3 * DH, tile), lambda n: (0, 0, n)),
+            pl.BlockSpec(TOKEN.shape, lambda n: (0, 0)),
         ],
         out_shape=[
             jax.ShapeDtypeStruct((heads, width, 3 * DH), BF),
             jax.ShapeDtypeStruct((heads, 3 * DH, width), BF),
+            TOKEN,
         ],
         compiler_params=params(),
         cost_estimate=COST,
@@ -276,15 +280,17 @@
     )(w_qkv)
 
 
-def product_kernel(head_ref, x_ref, w_ref, out_ref, *, contract):
+def product_kernel(head_ref, x_ref, w_ref, *rest, contract):
     del head_ref
+    out_ref, token_ref = rest[-2:]
+    token_ref[...] = jnp.zeros_like(token_ref)
     value = dot(x_ref[...], w_ref[0], contract).astype(BF)
     out_ref[:, : value.shape[1]] = value
     if value.shape[1] < out_ref.shape[1]:
         out_ref[:, value.shape[1] :] = jnp.zeros_like(out_ref[:, value.shape[1] :])
 
 
-def head_product(head, x, weight, contract, name):
+def head_product(head, x, weight, contract, name, *deps):
     columns = weight.shape[2] if contract == NN else weight.shape[1]
     columns += -columns % 128
     rows, width = x.shape
@@ -296,17 +302,22 @@
             in_specs=[
                 pl.BlockSpec((rows, width), lambda i, head: (0, 0)),
                 pl.BlockSpec((1,) + weight.shape[1:], lambda i, head: (head[0], 0, 0)),
+            ]
+            + spare(deps),
+            out_specs=[
+                pl.BlockSpec((rows, columns), lambda i, head: (0, 0)),
+                pl.BlockSpec(TOKEN.shape, lambda i, head: (0, 0)),
             ],
-            out_specs=pl.BlockSpec((rows, columns), lambda i, head: (0, 0)),
         ),
-        out_shape=jax.ShapeDtypeStruct((rows, columns), BF),
+        out_shape=[jax.ShapeDtypeStruct((rows, columns), BF), TOKEN],
         compiler_params=params(),
         cost_estimate=COST,
         name=name,
-    )(head, x, weight)
-
-
-def attention_kernel(qa_ref, qb_ref, da_ref, db_ref, oa_ref, ob_ref, k_all, v_all, dk_acc, dv_acc, *, block):
+    )(head, x, weight, *deps)
+
+
+def attention_kernel(qa_ref, qb_ref, da_ref, db_ref, *rest, block):
+    oa_ref, ob_ref, k_all, v_all, dk_acc, dv_acc = rest[-6:]
     scale = DH ** (-0.5)
     half = qa_ref.shape[0]
     for place, ref in enumerate((qa_ref, qb_ref)):
@@ -347,11 +358,12 @@
         out_ref[:, 2 * DH : 3 * DH] = dv_acc[rows, :].astype(BF)
 
 
-def attention(qkv_a, qkv_b, d_a, d_b):
+def attention(qkv_a, qkv_b, d_a, d_b, *deps):
     half = qkv_a.shape[0]
     shape = jax.ShapeDtypeStruct((half, 4 * DH), BF)
     return pl.pallas_call(
         functools.partial(attention_kernel, block=min(256, half)),
+        in_specs=[pl.BlockSpec(memory_space=pltpu.VMEM)] * 4 + spare(deps),
         out_shape=[shape, shape],
         scratch_shapes=[
             pltpu.VMEM((2 * half, DH), BF),
@@ -362,31 +374,19 @@
         compiler_params=params(),
         cost_estimate=COST,
         name="attention",
-    )(qkv_a, qkv_b, d_a, d_b)
-
-
-def term_kernel(head_ref, a_ref, b_ref, w_ref, *out_refs, first, last):
+    )(qkv_a, qkv_b, d_a, d_b, *deps)
+
+
+def term_kernel(head_ref, a_ref, b_ref, w_ref, *rest, first, last):
     head = head_ref[0]
     total = dot(a_ref[:, first:last], w_ref[head], NN)
     total += dot(b_ref[:, first:last], w_ref[1 - head], NN)
-    count = len(out_refs)
-    size = out_refs[0].shape[0]
-    value = total.astype(BF)
-    if count == 1:
-        out_refs[0][...] = value
-        return
-    for block in range(count):
-        for slot, out_ref in enumerate(out_refs):
-
-            @pl.when(wrapped(block - head_ref[1], count) == slot)
-            def _():
-                out_ref[...] = value[block * size : (block + 1) * size]
-
-
-def pair_term(place, mine, got, weight, slots, first, last, name):
+    rest[-1][...] = total.astype(BF)
+
+
+def pair_term(head, mine, got, weight, first, last, name, *deps):
     half, full = mine.shape
     heads, depth, width = weight.shape
-    size = half // slots
     tile = 512 if width % 512 == 0 else width
     return pl.pallas_call(
         functools.partial(term_kernel, first=first, last=last),
@@ -397,14 +397,15 @@
                 pl.BlockSpec((half, full), lambda n, at: (0, 0)),
                 pl.BlockSpec((half, full), lambda n, at: (0, 0)),
                 pl.BlockSpec((heads, depth, tile), lambda n, at: (0, 0, n)),
-            ],
-            out_specs=[pl.BlockSpec((size, tile), lambda n, at: (0, n))] * slots,
+            ]
+            + spare(deps),
+            out_specs=pl.BlockSpec((half, tile), lambda n, at: (0, n)),
         ),
-        out_shape=[jax.ShapeDtypeStruct((size, width), BF)] * slots,
+        out_shape=jax.ShapeDtypeStruct((half, width), BF),
         compiler_params=params(),
         cost_estimate=COST,
         name=name,
-    )(place, mine, got, weight)
+    )(head, mine, got, weight, *deps)
 
 
 def weight_kernel(at_ref, xa_ref, xb_ref, ga_ref, gb_ref, ra_ref, rb_ref, *rest):
@@ -434,7 +435,7 @@
     half, width = xa.shape
     chunk = width // seqs
     full = ra.shape[1]
-    column = pl.BlockSpec((half, chunk), lambda r, at: (0, lax.rem(r + at[0], seqs)))
+    column = pl.BlockSpec((half, chunk), lambda r, at: (0, r ^ at[0]))
     rest = pl.BlockSpec((half, full), lambda r, at: (0, 0))
     return pl.pallas_call(
         weight_kernel,
@@ -452,8 +453,8 @@
     )(at, xa, xb, ga, gb, ra, rb)
 
 
-def weight_sum_kernel(*refs):
-    part_refs, out_refs = refs[:-2], refs[-2:]
+def weight_sum_kernel(*refs, count):
+    part_refs, out_refs = refs[:count], refs[-2:]
     split = 3 * DH
     total = part_refs[0][...].astype(F32)
     for ref in part_refs[1:]:
@@ -465,15 +466,16 @@
         out_ref[:, split:] = total[split:, rows].astype(BF)
 
 
-def weight_sum(parts):
+def weight_sum(parts, *deps):
     full, chunk = parts[0].shape
     return pl.pallas_call(
-        weight_sum_kernel,
+        functools.partial(weight_sum_kernel, count=len(parts)),
+        in_specs=[pl.BlockSpec(memory_space=pltpu.VMEM)] * len(parts) + spare(deps),
         out_shape=[jax.ShapeDtypeStruct((chunk // 2, full), BF)] * 2,
         compiler_params=params(),
         cost_estimate=COST,
         name="weight_sum",
-    )(*parts)
+    )(*parts, *deps)
 
 
 def unpack_kernel(at_ref, *refs):
@@ -548,11 +550,6 @@
     return lax.optimization_barrier((value,) + others)[0]
 
 
-def send_chip(x, step, heads):
-    count = lax.axis_size("seq")
-    return lax.ppermute(x, "seq", [(s, (s + step * heads) % count) for s in range(count)])
-
-
 def trade_chip(x, bit, heads):
     count = lax.axis_size("seq")
     return lax.ppermute(x, "seq", [(s, s ^ (bit * heads)) for s in range(count)])
@@ -574,49 +571,49 @@
     place = lax.axis_index("seq")
     own_seq = (place // heads).astype(jnp.int32)
     own_head = (place % heads).astype(jnp.int32)
-    zero = jnp.zeros((), jnp.int32)
     at = jnp.stack([own_seq, own_head])
     head_mine = own_head.reshape(1)
     head_other = (1 - own_head).reshape(1)
 
     def to_chips(slots):
-        return [slots[r] if r == 0 else send_chip(slots[r], r, heads) for r in range(seqs)]
-
-    def from_chips(slots):
-        return [slots[r] if r == 0 else send_chip(slots[r], -r, heads) for r in range(seqs)]
+        return [x if j == 0 else trade_chip(x, j, heads) for j, x in enumerate(slots)]
+
+    order = (0, 2, 1, 3)
 
     grad_z = lax.all_gather(grad_out, "head", axis=0, tiled=False)
+
     pairs = jnp.transpose(enc_in.reshape(rows, 2, seqs, enc_in.shape[2]), (1, 2, 0, 3))
     low, high = neighbour_edges(pairs[:, :, :1, :], pairs[:, :, -1:, :])
     skip, slope, normed = encoder(at, pairs, low, high, conv_weight, norm_gain)
-    normed_slab = jnp.concatenate(to_chips(normed), axis=0)
+    normed = to_chips(normed)
+    normed_slab = jnp.concatenate([normed[j] for j in order], axis=0)
     normed_rows = lax.all_gather(normed_slab, "head", axis=0, tiled=True)
 
     grad_z = after(grad_z, normed_slab)
-    grad_slots = [
-        lax.dynamic_index_in_dim(grad_z, (own_seq + r) % seqs, 2, keepdims=False)
-        for r in range(seqs)
-    ]
-    grad_rows = jnp.stack(to_chips(grad_slots), axis=1).reshape(half, width)
-    w_pack, w_turned = pack_weights(after(w_qkv, normed_slab))
+    grad_slots = to_chips(
+        [lax.dynamic_index_in_dim(grad_z, own_seq ^ j, 2, keepdims=False) for j in range(seqs)]
+    )
+    grad_rows = jnp.stack([grad_slots[j] for j in order], axis=1).reshape(half, width)
+    w_pack, w_turned, packed = pack_weights(after(w_qkv, normed_slab))
     w_rows = w_out.reshape(heads, DH, width)
-    d_got = swap_heads(head_product(head_other, grad_rows, w_rows, NT, "d_o_other"))
-    d_mine = head_product(head_mine, grad_rows, w_rows, NT, "d_o_own")
+    d_other, one = head_product(head_other, grad_rows, w_rows, NT, "d_o_other")
+    d_got = swap_heads(d_other)
+    d_mine, two = head_product(head_mine, grad_rows, w_rows, NT, "d_o_own")
     grad_swapped = swap_heads(grad_rows)
-    normed_rows = after(normed_rows, d_got, d_mine, grad_swapped, w_pack, w_turned)
-
-    qkv_got = swap_heads(head_product(head_other, normed_rows, w_pack, NN, "qkv_other"))
+    normed_rows = after(normed_rows, packed, one, two)
+
+    qkv_other, _ = head_product(
+        head_other, normed_rows, w_pack, NN, "qkv_other", d_got, grad_swapped
+    )
+    qkv_got = swap_heads(qkv_other)
     normed_swapped = swap_heads(normed_rows)
-    qkv_mine = head_product(head_mine, normed_rows, w_pack, NN, "qkv_own")
-    qkv_mine = after(qkv_mine, normed_swapped)
-    result_mine, result_other = attention(qkv_mine, qkv_got, d_mine, d_got)
+    qkv_mine, _ = head_product(head_mine, normed_rows, w_pack, NN, "qkv_own")
+    result_mine, result_other = attention(qkv_mine, qkv_got, d_mine, d_got, normed_swapped)
     result_got = swap_heads(result_other)
 
-    plain = jnp.stack([own_head, zero])
-    (d_term,) = pair_term(plain, result_mine, result_got, w_turned, 1, 0, 3 * DH, "d_term")
-    d_normed = lax.psum_scatter(
-        d_term.reshape(groups, seqs, rows, width), "head", scatter_dimension=0, tiled=False
-    )
+    shape = (groups, seqs, rows, width)
+    d_term = pair_term(head_mine, result_mine, result_got, w_turned, 0, 3 * DH, "d_term")
+    d_normed = lax.psum_scatter(d_term.reshape(shape), "head", scatter_dimension=0, tiled=False)
     part = weight_gradients(
         own_seq.reshape(1),
         normed_rows,
@@ -627,34 +624,34 @@
         result_other,
         seqs,
     )
-    (head_term,) = pair_term(
-        plain, result_mine, after(result_got, *part), w_rows, 1, 3 * DH, 4 * DH, "head_term"
-    )
-    head_sum = lax.psum_scatter(
-        head_term.reshape(groups, seqs, rows, width), "head", scatter_dimension=0, tiled=False
-    )
-
-    half_a, half_b = weight_sum([after(p, head_term) for p in to_chips(part)])
+    part = to_chips(part)
+    head_term = pair_term(
+        head_mine, result_mine, result_got, w_rows, 3 * DH, 4 * DH, "head_term", part[1]
+    )
+    head_sum = lax.psum_scatter(head_term.reshape(shape), "head", scatter_dimension=0, tiled=False)
+
+    near = trade_chip(d_normed[2:], 1, heads)
+    far = trade_chip(jnp.stack([d_normed[1], near[1]]), 2, heads)
+    grad = jnp.transpose(after(grad_out, d_term), (1, 0, 2))
+    d_conv, first, last = conv_gradient(at, d_normed, near, far, skip, grad, norm_gain, slope)
+    low, high = neighbour_edges(first, last)
+
+    half_a, half_b = weight_sum(part, far)
     got_a = trade_chip(half_a, 1, heads)
     got_b = trade_chip(half_b, 2, heads)
-
-    d_normed = from_chips([d_normed[r] for r in range(seqs)])
-    grad = jnp.transpose(after(grad_out, d_term), (1, 0, 2))
-    d_normed[0] = after(d_normed[0], half_a)
-    d_conv, first, last = conv_gradient(at, d_normed, skip, grad, norm_gain, slope)
-    low, high = neighbour_edges(first, last)
-    near_a = jnp.concatenate([half_a, after(got_a, first)], axis=0)
-    near_b = jnp.concatenate([half_b, after(got_b, first)], axis=0)
+    near_a = jnp.concatenate([half_a, after(got_a, low, high)], axis=0)
+    near_b = jnp.concatenate([half_b, after(got_b, low, high)], axis=0)
     far_a = trade_chip(near_a, 2, heads)
     far_b = trade_chip(near_b, 1, heads)
-    grad_input = conv_back(d_conv, after(low, near_a, near_b), high, conv_weight)
-    mine = [near_a, near_b, far_a, far_b]
-    other = [swap_heads(after(x, high)) for x in mine[:2]]
-    other += [swap_heads(after(x, grad_input)) for x in mine[2:]]
-    grad_w_qkv, grad_w_out = unpack_weights(at, mine, other)
+    near_other = [swap_heads(near_a), swap_heads(near_b)]
+    grad_input = conv_back(d_conv, low, high, conv_weight, *near_other)
+    far_other = [swap_heads(after(x, grad_input)) for x in (far_a, far_b)]
+    grad_w_qkv, grad_w_out = unpack_weights(
+        at, [near_a, near_b, far_a, far_b], near_other + far_other
+    )
 
     head_sum = after(head_sum, grad_input)
-    head_sum = from_chips([head_sum[r] for r in range(seqs)])
+    head_sum = to_chips([head_sum[order.index(j)] for j in range(seqs)])
     mixed = mixed_call(at, head_sum, skip)
     grad_input = jnp.transpose(grad_input.reshape(2, seqs, rows, -1), (2, 0, 1, 3))
     return (

time: 224 us -> 230 us (1.027)
  waiting for transfers between devices: 78.4 us -> 102 us
  local copies, waits for them, and re-layouts: 40.2 us -> 26.1 us
  starting transfers between devices: 41.7 us -> 36.5 us
    ppermute x4 -> x18, waiting for transfers between devices: 0.01 us -> 66.3 us  [trade_chip(): return lax.ppermute(x, 'seq', [(s, s ^ bit * heads) for s in range(count)])]
    ppermute x15 -> x0, waiting for transfers between devices: 64.6 us -> none  [send_chip(): lax.ppermute(x, 'seq', [(s, (s + step * heads) % count) for s in range(co...]
    ppermute x15 -> x0, starting transfers between devices: 16.5 us -> none  [send_chip(): lax.ppermute(x, 'seq', [(s, (s + step * heads) % count) for s in range(co...]
    ppermute x4 -> x18, starting transfers between devices: 4.34 us -> 17.7 us  [trade_chip(): return lax.ppermute(x, 'seq', [(s, s ^ bit * heads) for s in range(count)])]
    all_gather x1, waiting for transfers between devices: 2.09 us -> 15.4 us  [unit_body(): normed_rows = lax.all_gather(normed_slab, 'head', axis=0, tiled=True)]
    unnamed x74 -> x56, local copies, waits for them, and re-layouts: 31.3 us -> 18.3 us
    reduce_scatter x2, waiting for transfers between devices: 0.04 us -> 4.57 us  [the longest x1 4.57 us: unit_body(): lax.psum_scatter(d_term.reshape(shape), 'head', scatter_dimension=0, tile...]
    ppermute x2, starting transfers between devices: 6.91 us -> 4.22 us  [neighbour_edges(): lax.ppermute(last, axes, forward)]
  transfers between devices with their start and end apart: 36 -> 35, of which waited for: 20 -> 22; matrix products, arithmetic and copies ran while one was open for 6% -> 4% of each run, Pallas kernels for 15% -> 15%
where the time goes in v7:
time: 230 us; the launch traced here: 229 us
  waiting for transfers between devices  102 us (44%)
  Pallas kernels  49.9 us (22%)
  starting transfers between devices  36.5 us (16%)
  local copies, waits for them, and re-layouts  26.1 us (11%)
  between operations  14.2 us (6%)
    ppermute x18, waiting for transfers between devices, trade_chip(): return lax.ppermute(x, 'seq', [(s, s ^ bit * heads) for s in range(count)])  66.3 us
    unnamed x56, local copies, waits for them, and re-layouts  18.3 us
    ppermute x18, starting transfers between devices, trade_chip(): return lax.ppermute(x, 'seq', [(s, s ^ bit * heads) for s in range(count)])  17.7 us
    all_gather x1, waiting for transfers between devices, unit_body(): normed_rows = lax.all_gather(normed_slab, 'head', axis=0, tiled=True)  15.4 us
    ppermute x2, starting transfers between devices, neighbour_edges(): lax.ppermute(first, axes, backward)  7.47 us
    pallas_call x1, Pallas kernels, encoder(): pl.pallas_call(conv_kernel, grid=(width // tile,), in_specs=[SCALARS, who...  7.09 us
    pallas_call x1, Pallas kernels, unpack_weights(): pl.pallas_call(unpack_kernel, grid_spec=pltpu.PrefetchScalarGridSpec(num_...  6.85 us
    ppermute x9, starting transfers between devices, swap_heads(): lax.ppermute(x, 'seq', [(s, s + 1 - 2 * (s % 2)) for s in range(count)])  6.74 us
  transfers between devices with their start and end apart: 35, of which 22 were waited for; matrix products, arithmetic and copies ran while one was open for 4% of the time, Pallas kernels for 15%

profile of v7, /device:TPU:26, one launch (start us, length us, event | category | flops | bytes accessed | tf_op | source)
XLA Modules:
  0.0 228.6 jit_solution(16335491734753033002)
XLA Ops:
  11.0 3.9 %collective-permute-start.1 = (bf16[2,4,1,768]{3,2,1,0:T(2,128)(2,1)S(1)}, bf16[2,4,1,768]{3,2,1,0:T(2,128)(2,1)S(1)}, u32[]{:S(2)}, u32[]{:S(2)}) collective-permute-start(bf16[2,4,1,768]{3,2,1,0:T(2,128)(2,1)S(1)} %get-tuple-element.90), channel_id=1, source_target_pairs={{1,0},{2,1},{3,2},{4,3},{5,4},{6,5},{7,6},{8,7},{9,8},{10,9},{11,1... | collective-permute-start | bytes 36872 | tf_op jit(solution)/shard_map/ppermute | solution.py:546
  17.9 4.5 %copy-done = bf16[5,768,1536]{2,1,0:T(8,128)(2,1)S(1)} copy-done((bf16[5,768,1536]{2,1,0:T(8,128)(2,1)S(1)}, bf16[5,768,1536]{2,1,0:T(8,128)(2,1)}, u32[]{:S(2)}) %copy-start) | copy-done | bytes 11796504
  22.5 7.1 %encoder_forward.1 = (bf16[4,32,1536]{2,1,0:T(8,128)(2,1)S(1)}, f32[2,4,32,1536]{3,2,1,0:T(8,128)S(1)}, bf16[32,1536]{1,0:T(8,128)(2,1)S(1)}, bf16[32,1536]{1,0:...) custom-call(s32[2]{0:T(128)S(1)} %pad_add_fusion.at_ref, ...), custom_call_target="tpu_custom_call" | custom-call | flops 1000 | bytes 1000 | tf_op jit(solution)/shard_map/encoder_forward/pallas_call | solution.py:110
  39.7 5.9 %all-gather.6.cloned.1.call-done = bf16[128,4,1536]{2,1,0:T(4,128)(2,1)} async-done(((bf16[32,4,1536]{2,1,0:T(4,128)(2,1)}), bf16[128,4,1536]{2,1,0:T(4,128)(2,1)}) %all-gather.6.cloned.1.call-update) | async-done | bytes 1572880 | tf_op jit(solution)/shard_map/all_gather | solution.py:583
  51.0 9.4 %collective-permute-done.7 = bf16[4,32,1536]{2,1,0:T(8,128)(2,1)S(1)} collective-permute-done((bf16[4,32,1536]{2,1,0:T(8,128)(2,1)S(1)}, bf16[4,32,1536]{2,1,0:T(8,128)(2,1)S(1)}, u32[]{:S(2)}, u32[]{:S(2)}) %collective-permute-start.7) | collective-permute-done | bytes 393248 | tf_op jit(solution)/shard_map/ppermute | solution.py:555
  60.4 7.5 %collective-permute-done.6 = bf16[4,32,1536]{2,1,0:T(8,128)(2,1)S(1)} collective-permute-done((bf16[4,32,1536]{2,1,0:T(8,128)(2,1)S(1)}, bf16[4,32,1536]{2,1,0:T(8,128)(2,1)S(1)}, u32[]{:S(2)}, u32[]{:S(2)}) %collective-permute-start.6) | collective-permute-done | bytes 393248 | tf_op jit(solution)/shard_map/ppermute | solution.py:555
  68.3 15.4 %all-gather.4.cloned.1.call-done.x_ref.xa_ref = bf16[512,1536]{1,0:T(8,128)(2,1)} async-done(((bf16[128,1536]{1,0:T(8,128)(2,1)}), bf16[512,1536]{1,0:T(8,128)(2,1)}) %all-gather.4.cloned.1.call-update) | async-done | bytes 1572880 | tf_op jit(solution)/shard_map/all_gather | solution.py:590
  87.3 4.5 %pack_weights.1 = (bf16[2,1536,576]{2,1,0:T(8,128)(2,1)S(1)}, bf16[2,576,1536]{2,1,0:T(8,128)(2,1)S(1)}, f32[8,128]{1,0:T(8,128)}) custom-call(bf16[3,1536,384]{2,1,0:T(8,128)(2,1)S(1)} %copy-done.10), custom_call_target="tpu_custom_call" | custom-call | flops 1000 | bytes 1000 | tf_op jit(solution)/shard_map/pack_weights/pallas_call | solution.py:263
  96.9 6.5 %attention.1 = (bf16[512,768]{1,0:T(8,128)(2,1)S(1)}, bf16[512,768]{1,0:T(8,128)(2,1)S(1)}) custom-call(bf16[512,640]{1,0:T(8,128)(2,1)S(1)} %get-tuple-element.43.qa_ref, bf16[512,640]{1,0:T(8,128)(2,1)S(1)} %collective-permute-done.10.qb_ref, bf16[512,256]{1,0:T(8,128)(2,1)S(1)} %get-tuple-element.47.da_ref, ...), custom_call_target="tpu_custom_call" | custom-call | flops 1000 | bytes 1000 | tf_op jit(solution)/shard_map/attention/pallas_call | solution.py:364
  105.8 3.3 %d_term.1 = bf16[512,1536]{1,0:T(8,128)(2,1)S(1)} custom-call(s32[1]{0:T(128)} %bitcast.1.head_ref, bf16[512,768]{1,0:T(8,128)(2,1)S(1)} %get-tuple-element.48.ra_ref.a_ref, bf16[512,768]{1,0:T(8,128)(2,1)S(1)} %collective-permute-done.12.b_ref, bf16[2,576,1536]{2,1,0:T(8,128)(2,1)S(1)} %get-tuple-element.51.w_ref), custom_call_target="tpu_custom_call" | custom-call | flops 1000 | bytes 1000 | tf_op jit(solution)/shard_map/d_term/pallas_call | solution.py:391
  112.8 6.5 %weight_gradients.1 = (bf16[768,384]{1,0:T(8,128)(2,1)S(1)}, bf16[768,384]{1,0:T(8,128)(2,1)S(1)}, bf16[768,384]{1,0:T(8,128)(2,1)S(1)}, bf16[768,384]{1,0:T(8,128)(2,1)S(1)}) custom-call(s32[1]{0:T(128)} %bitcast.at_ref, bf16[512,1536]{1,0:T(8,128)(2,1)S(1)} %copy-done.2, bf16[512,1536]{1,0:T(8,128)(2,1)} %collective-permute-done.11.rest_0_.xb_ref, ...), custom_call_target="tpu_custom_call" | custom-call | flops 1000 | bytes 1000 | tf_op jit(solution)/shard_map/weight_gradients/pallas_call | solution.py:440
  119.9 15.0 %collective-permute-done.13.rest_0_.refs_1_ = bf16[768,384]{1,0:T(8,128)(2,1)S(1)} collective-permute-done((bf16[768,384]{1,0:T(8,128)(2,1)S(1)}, bf16[768,384]{1,0:T(8,128)(2,1)S(1)}, u32[]{:S(2)}, u32[]{:S(2)}) %collective-permute-start.13) | collective-permute-done | bytes 589856 | tf_op jit(solution)/shard_map/ppermute | solution.py:555
  134.9 2.6 %head_term.1 = bf16[512,1536]{1,0:T(8,128)(2,1)} custom-call(s32[1]{0:T(128)} %bitcast.1.head_ref, bf16[512,768]{1,0:T(8,128)(2,1)S(1)} %copy-done.8, bf16[512,768]{1,0:T(8,128)(2,1)S(1)} %copy-done.12, bf16[2,192,1536]{2,1,0:T(8,128)(2,1)S(1)} %bitcast.51, bf16[768,384]{1,0:T(8,128)(2,1)S(1)} %collective-permute-done.13.rest_0_.refs_1_), custom_call_target="tpu_custom_call" | custom-call | flops 1000 | bytes 1000 | tf_op jit(solution)/shard_map/head_term/pallas_call | solution.py:391
  140.1 4.6 %reduce-scatter.5.cloned.1.call-done = bf16[1,4,32,1536]{3,2,1,0:T(8,128)(2,1)} async-done(((bf16[4,4,32,1536]{3,2,1,0:T(8,128)(2,1)}), bf16[1,4,32,1536]{3,2,1,0:T(8,128)(2,1)}) %reduce-scatter.5.cloned.1.call-update) | async-done | bytes 393232 | tf_op jit(solution)/shard_map/reduce_scatter | solution.py:616
  147.2 11.5 %collective-permute-done.14.near_ref = bf16[2,32,1536]{2,1,0:T(8,128)(2,1)S(1)} collective-permute-done((bf16[2,32,1536]{2,1,0:T(8,128)(2,1)S(1)}, bf16[2,32,1536]{2,1,0:T(8,128)(2,1)S(1)}, u32[]{:S(2)}, u32[]{:S(2)}) %collective-permute-start.14) | collective-permute-done | bytes 196640 | tf_op jit(solution)/shard_map/ppermute | solution.py:555
  159.6 7.2 %collective-permute-done.18.refs_2_ = bf16[768,384]{1,0:T(8,128)(2,1)S(1)} collective-permute-done((bf16[768,384]{1,0:T(8,128)(2,1)}, bf16[768,384]{1,0:T(8,128)(2,1)S(1)}, u32[]{:S(2)}, u32[]{:S(2)}) %collective-permute-start.18) | collective-permute-done | bytes 589856 | tf_op jit(solution)/shard_map/ppermute | solution.py:555
  166.8 2.9 %collective-permute-done.15.far_ref.refs_4_ = bf16[2,32,1536]{2,1,0:T(8,128)(2,1)S(1)} collective-permute-done((bf16[2,32,1536]{2,1,0:T(8,128)(2,1)S(1)}, bf16[2,32,1536]{2,1,0:T(8,128)(2,1)S(1)}, u32[]{:S(2)}, u32[]{:S(2)}) %collective-permute-start.15) | collective-permute-done | bytes 196640 | tf_op jit(solution)/shard_map/ppermute | solution.py:555
  175.8 3.5 %collective-permute-start.17 = (bf16[2,4,1,1536]{3,2,1,0:T(2,128)(2,1)S(1)}, bf16[2,4,1,1536]{3,2,1,0:T(2,128)(2,1)S(1)}, u32[]{:S(2)}, u32[]{:S(2)}) collective-permute-start(bf16[2,4,1,1536]{3,2,1,0:T(2,128)(2,1)S(1)} %get-tuple-element.57), channel_id=1, source_target_pairs={{1,0},{2,1},{3,2},{4,3},{5,4},{6,5},{7,6},{8,7},{9,8},{10,9},{11,1... | collective-permute-start | bytes 73736 | tf_op jit(solution)/shard_map/ppermute | solution.py:546
  179.4 2.4 %collective-permute-done.16.low_ref = bf16[2,4,1,1536]{3,2,1,0:T(2,128)(2,1)S(1)} collective-permute-done((bf16[2,4,1,1536]{3,2,1,0:T(2,128)(2,1)S(1)}, bf16[2,4,1,1536]{3,2,1,0:T(2,128)(2,1)S(1)}, u32[]{:S(2)}, u32[]{:S(2)}) %collective-permute-start.16) | collective-permute-done | bytes 24608 | tf_op jit(solution)/shard_map/ppermute | solution.py:546
  183.0 4.9 %collective-permute-start.21 = (bf16[384,768]{1,0:T(8,128)(2,1)S(1)}, bf16[384,768]{1,0:T(8,128)(2,1)S(1)}, u32[]{:S(2)}, u32[]{:S(2)}) collective-permute-start(bf16[384,768]{1,0:T(8,128)(2,1)S(1)} %constant_dynamic-update-slice_fusion.4.refs_0_), channel_id=1, source_target_pairs={{0,4},{4,0},{8,12},{12,8},{16,20},{20,16},{24,28},{28,24},{1,5},{5... | collective-permute-start | bytes 1769480 | tf_op jit(solution)/shard_map/ppermute | solution.py:560
  190.4 4.3 %copy-done.1 = bf16[5,768,1536]{2,1,0:T(8,128)(2,1)S(1)} copy-done((bf16[5,768,1536]{2,1,0:T(8,128)(2,1)S(1)}, bf16[5,768,1536]{2,1,0:T(8,128)(2,1)}, u32[]{:S(2)}) %copy-start.1) | copy-done | bytes 11796504
  194.8 4.3 %encoder_backward.1 = bf16[256,768]{1,0:T(8,128)(2,1)S(1)} custom-call(bf16[2,4,32,1536]{3,2,1,0:T(8,128)(2,1)S(1)} %get-tuple-element.55.d_ref, bf16[2,4,1,1536]{3,2,1,0:T(2,128)(2,1)S(1)} %collective-permute-done.16.low_ref, bf16[2,4,1,1536]{3,2,1,0:T(2,128)(2,1)S(1)} %collective-permute-done.17.high_ref, bf16[5,768,1536]{2,1,0:T(8,128)(2,1)S(1)} %copy-done.1, ...), custom_call_target="tpu_custom_call" | custom-call | flops 1000 | bytes 1000 | tf_op jit(solution)/shard_map/encoder_backward/pallas_call | solution.py:227
  199.1 4.8 %collective-permute-done.27.refs_2_ = bf16[384,768]{1,0:T(8,128)(2,1)} collective-permute-done((bf16[384,768]{1,0:T(8,128)(2,1)S(1)}, bf16[384,768]{1,0:T(8,128)(2,1)}, u32[]{:S(2)}, u32[]{:S(2)}) %collective-permute-start.27) | collective-permute-done | bytes 589856 | tf_op jit(solution)/shard_map/ppermute | solution.py:555
  215.3 6.8 %weight_outputs.1 = (f32[3,1536,384]{2,1,0:T(8,128)}, f32[384,1536]{1,0:T(8,128)}) custom-call(s32[2]{0:T(128)S(1)} %pad_add_fusion.at_ref, bf16[384,768]{1,0:T(8,128)(2,1)S(1)} %constant_dynamic-update-slice_fusion.4.refs_0_, bf16[384,768]{1,0:T(8,128)(2,1)S(1)} %constant_dynamic-update-slice_fusion.6.refs_1_, ...), custom_call_target="tpu_custom_call" | custom-call | flops 1000 | bytes 1000 | tf_op jit(solution)/shard_map/weight_outputs/pallas_call | solution.py:520
  (139 shorter events, 65.0 us)
Async XLA Ops:
  7.2 38.4 %all-gather.6.cloned.1.call-start = ((), (), s32[]{:S(2)}) async-start(), calls=%async_computation.5 | async-start | bytes 1966080 | tf_op jit(solution)/shard_map/all_gather | solution.py:583
  7.9 75.8 %all-gather.4.cloned.1.call-start = ((), (), s32[]{:S(2)}) async-start(), calls=%async_computation.2 | async-start | bytes 1966080 | tf_op jit(solution)/shard_map/all_gather | solution.py:590
  11.0 6.9 %collective-permute-start.1 = (bf16[2,4,1,768]{3,2,1,0:T(2,128)(2,1)S(1)}, bf16[2,4,1,768]{3,2,1,0:T(2,128)(2,1)S(1)}, u32[]{:S(2)}, u32[]{:S(2)}) collective-permute-start(bf16[2,4,1,768]{3,2,1,0:T(2,128)(2,1)S(1)} %get-tuple-element.90), channel_id=1, source_target_pairs={{1,0},{2,1},{3,2},{4,3},{5,4},{6,5},{7,6},{8,7},{9,8},{10,9},{11,1... | collective-permute-start | bytes 36872 | tf_op jit(solution)/shard_map/ppermute | solution.py:546
  39.6 105.0 %reduce-scatter.5.cloned.1.call-start = ((), (), s32[]{:S(2)}) async-start(), calls=%async_computation.4 | async-start | bytes 1966080 | tf_op jit(solution)/shard_map/reduce_scatter | solution.py:616
  47.4 13.0 %collective-permute-start.7 = (bf16[4,32,1536]{2,1,0:T(8,128)(2,1)S(1)}, bf16[4,32,1536]{2,1,0:T(8,128)(2,1)S(1)}, u32[]{:S(2)}, u32[]{:S(2)}) collective-permute-start(bf16[4,32,1536]{2,1,0:T(8,128)(2,1)S(1)} %get-tuple-element.83), channel_id=1, source_target_pairs={{0,24},{4,28},{8,16},{12,20},{16,8},{20,12},{24,0},{28,4},{1,25},{... | collective-permute-start | bytes 1179656 | tf_op jit(solution)/shard_map/ppermute | solution.py:555
  49.4 18.5 %collective-permute-start.6 = (bf16[4,32,1536]{2,1,0:T(8,128)(2,1)S(1)}, bf16[4,32,1536]{2,1,0:T(8,128)(2,1)S(1)}, u32[]{:S(2)}, u32[]{:S(2)}) collective-permute-start(bf16[4,32,1536]{2,1,0:T(8,128)(2,1)S(1)} %get-tuple-element.84), channel_id=1, source_target_pairs={{0,8},{4,12},{8,0},{12,4},{16,24},{20,28},{24,16},{28,20},{1,9},{5... | collective-permute-start | bytes 1179656 | tf_op jit(solution)/shard_map/ppermute | solution.py:555
  50.4 17.5 %collective-permute-start.5 = (bf16[4,32,1536]{2,1,0:T(8,128)(2,1)S(1)}, bf16[4,32,1536]{2,1,0:T(8,128)(2,1)S(1)}, u32[]{:S(2)}, u32[]{:S(2)}) collective-permute-start(bf16[4,32,1536]{2,1,0:T(8,128)(2,1)S(1)} %get-tuple-element.85), channel_id=1, source_target_pairs={{0,16},{4,20},{8,24},{12,28},{16,0},{20,4},{24,8},{28,12},{1,17},{... | collective-permute-start | bytes 1179656 | tf_op jit(solution)/shard_map/ppermute | solution.py:555
  68.2 23.6 %collective-permute-start.9 = (bf16[512,1536]{1,0:T(8,128)(2,1)S(1)}, bf16[512,1536]{1,0:T(8,128)(2,1)}, u32[]{:S(2)}, u32[]{:S(2)}) collective-permute-start(bf16[512,1536]{1,0:T(8,128)(2,1)S(1)} %bitcast.45), channel_id=1, source_target_pairs={{0,4},{4,0},{8,12},{12,8},{16,20},{20,16},{24,28},{28,24},{1,5},{5... | collective-permute-start | bytes 4718600 | tf_op jit(solution)/shard_map/ppermute | solution.py:560
  83.7 13.1 %collective-permute-start.11 = (bf16[512,1536]{1,0:T(8,128)(2,1)}, bf16[512,1536]{1,0:T(8,128)(2,1)}, u32[]{:S(2)}, u32[]{:S(2)}) collective-permute-start(bf16[512,1536]{1,0:T(8,128)(2,1)} %all-gather.4.cloned.1.call-done.x_ref.xa_ref), channel_id=1, source_target_pairs={{0,4},{4,0},{8,12},{12,8},{16,20},{20,16},{24,28},{28,24},{1,5},{5... | collective-permute-start | bytes 4718600 | tf_op jit(solution)/shard_map/ppermute | solution.py:560
  84.8 7.0 %collective-permute-start.8 = (bf16[512,256]{1,0:T(8,128)(2,1)S(1)}, bf16[512,256]{1,0:T(8,128)(2,1)S(1)}, u32[]{:S(2)}, u32[]{:S(2)}) collective-permute-start(bf16[512,256]{1,0:T(8,128)(2,1)S(1)} %get-tuple-element.45), channel_id=1, source_target_pairs={{0,4},{4,0},{8,12},{12,8},{16,20},{20,16},{24,28},{28,24},{1,5},{5... | collective-permute-start | bytes 786440 | tf_op jit(solution)/shard_map/ppermute | solution.py:560
  110.2 94.2 %reduce-scatter.3.cloned.1.call-start = ((), (), s32[]{:S(2)}) async-start(), calls=%async_computation.3 | async-start | bytes 1966080 | tf_op jit(solution)/shard_map/reduce_scatter | solution.py:631
  119.3 15.7 %collective-permute-start.13 = (bf16[768,384]{1,0:T(8,128)(2,1)S(1)}, bf16[768,384]{1,0:T(8,128)(2,1)S(1)}, u32[]{:S(2)}, u32[]{:S(2)}) collective-permute-start(bf16[768,384]{1,0:T(8,128)(2,1)S(1)} %get-tuple-element.50), channel_id=1, source_target_pairs={{0,8},{4,12},{8,0},{12,4},{16,24},{20,28},{24,16},{28,20},{1,9},{5... | collective-permute-start | bytes 1769480 | tf_op jit(solution)/shard_map/ppermute | solution.py:555
  137.6 29.2 %collective-permute-start.18 = (bf16[768,384]{1,0:T(8,128)(2,1)}, bf16[768,384]{1,0:T(8,128)(2,1)S(1)}, u32[]{:S(2)}, u32[]{:S(2)}) collective-permute-start(bf16[768,384]{1,0:T(8,128)(2,1)} %copy-done.22), channel_id=1, source_target_pairs={{0,16},{4,20},{8,24},{12,28},{16,0},{20,4},{24,8},{28,12},{1,17},{... | collective-permute-start | bytes 1769480 | tf_op jit(solution)/shard_map/ppermute | solution.py:555
  139.2 27.6 %collective-permute-start.19 = (bf16[768,384]{1,0:T(8,128)(2,1)S(1)}, bf16[768,384]{1,0:T(8,128)(2,1)S(1)}, u32[]{:S(2)}, u32[]{:S(2)}) collective-permute-start(bf16[768,384]{1,0:T(8,128)(2,1)S(1)} %copy-done.21), channel_id=1, source_target_pairs={{0,24},{4,28},{8,16},{12,20},{16,8},{20,12},{24,0},{28,4},{1,25},{... | collective-permute-start | bytes 1769480 | tf_op jit(solution)/shard_map/ppermute | solution.py:555
  145.6 13.1 %collective-permute-start.14 = (bf16[2,32,1536]{2,1,0:T(8,128)(2,1)S(1)}, bf16[2,32,1536]{2,1,0:T(8,128)(2,1)S(1)}, u32[]{:S(2)}, u32[]{:S(2)}) collective-permute-start(bf16[2,32,1536]{2,1,0:T(8,128)(2,1)S(1)} %slice_bitcast_fusion), channel_id=1, source_target_pairs={{0,8},{4,12},{8,0},{12,4},{16,24},{20,28},{24,16},{28,20},{1,9},{5... | collective-permute-start | bytes 589832 | tf_op jit(solution)/shard_map/ppermute | solution.py:555
  158.7 10.9 %collective-permute-start.15 = (bf16[2,32,1536]{2,1,0:T(8,128)(2,1)S(1)}, bf16[2,32,1536]{2,1,0:T(8,128)(2,1)S(1)}, u32[]{:S(2)}, u32[]{:S(2)}) collective-permute-start(bf16[2,32,1536]{2,1,0:T(8,128)(2,1)S(1)} %pad_maximum_fusion.1), channel_id=1, source_target_pairs={{0,16},{4,20},{8,24},{12,28},{16,0},{20,4},{24,8},{28,12},{1,17},{... | collective-permute-start | bytes 589832 | tf_op jit(solution)/shard_map/ppermute | solution.py:555
  170.0 13.0 %collective-permute-start.20 = (bf16[192,768]{1,0:T(8,128)(2,1)S(1)}, bf16[192,768]{1,0:T(8,128)(2,1)S(1)}, u32[]{:S(2)}, u32[]{:S(2)}) collective-permute-start(bf16[192,768]{1,0:T(8,128)(2,1)S(1)} %get-tuple-element.61), channel_id=1, source_target_pairs={{0,8},{4,12},{8,0},{12,4},{16,24},{20,28},{24,16},{28,20},{1,9},{5... | collective-permute-start | bytes 884744 | tf_op jit(solution)/shard_map/ppermute | solution.py:555
  170.8 17.2 %collective-permute-start.22 = (bf16[192,768]{1,0:T(8,128)(2,1)S(1)}, bf16[192,768]{1,0:T(8,128)(2,1)S(1)}, u32[]{:S(2)}, u32[]{:S(2)}) collective-permute-start(bf16[192,768]{1,0:T(8,128)(2,1)S(1)} %get-tuple-element.63), channel_id=1, source_target_pairs={{0,16},{4,20},{8,24},{12,28},{16,0},{20,4},{24,8},{28,12},{1,17},{... | collective-permute-start | bytes 884744 | tf_op jit(solution)/shard_map/ppermute | solution.py:555
  173.5 8.3 %collective-permute-start.16 = (bf16[2,4,1,1536]{3,2,1,0:T(2,128)(2,1)S(1)}, bf16[2,4,1,1536]{3,2,1,0:T(2,128)(2,1)S(1)}, u32[]{:S(2)}, u32[]{:S(2)}) collective-permute-start(bf16[2,4,1,1536]{3,2,1,0:T(2,128)(2,1)S(1)} %get-tuple-element.56), channel_id=1, source_target_pairs={{0,1},{1,2},{2,3},{3,4},{4,5},{5,6},{6,7},{7,8},{8,9},{9,10},{10,1... | collective-permute-start | bytes 73736 | tf_op jit(solution)/shard_map/ppermute | solution.py:546
  175.8 7.2 %collective-permute-start.17 = (bf16[2,4,1,1536]{3,2,1,0:T(2,128)(2,1)S(1)}, bf16[2,4,1,1536]{3,2,1,0:T(2,128)(2,1)S(1)}, u32[]{:S(2)}, u32[]{:S(2)}) collective-permute-start(bf16[2,4,1,1536]{3,2,1,0:T(2,128)(2,1)S(1)} %get-tuple-element.57), channel_id=1, source_target_pairs={{1,0},{2,1},{3,2},{4,3},{5,4},{6,5},{7,6},{8,7},{9,8},{10,9},{11,1... | collective-permute-start | bytes 73736 | tf_op jit(solution)/shard_map/ppermute | solution.py:546
  188.1 15.8 %collective-permute-start.27 = (bf16[384,768]{1,0:T(8,128)(2,1)S(1)}, bf16[384,768]{1,0:T(8,128)(2,1)}, u32[]{:S(2)}, u32[]{:S(2)}) collective-permute-start(bf16[384,768]{1,0:T(8,128)(2,1)S(1)} %constant_dynamic-update-slice_fusion.4.refs_0_), channel_id=1, source_target_pairs={{0,16},{4,20},{8,24},{12,28},{16,0},{20,4},{24,8},{28,12},{1,17},{... | collective-permute-start | bytes 1769480 | tf_op jit(solution)/shard_map/ppermute | solution.py:555
  188.2 15.8 %collective-permute-start.28 = (bf16[384,768]{1,0:T(8,128)(2,1)S(1)}, bf16[384,768]{1,0:T(8,128)(2,1)}, u32[]{:S(2)}, u32[]{:S(2)}) collective-permute-start(bf16[384,768]{1,0:T(8,128)(2,1)S(1)} %constant_dynamic-update-slice_fusion.6.refs_1_), channel_id=1, source_target_pairs={{0,8},{4,12},{8,0},{12,4},{16,24},{20,28},{24,16},{28,20},{1,9},{5... | collective-permute-start | bytes 1769480 | tf_op jit(solution)/shard_map/ppermute | solution.py:555
  203.9 11.3 %collective-permute-start.29 = (bf16[384,768]{1,0:T(8,128)(2,1)}, bf16[384,768]{1,0:T(8,128)(2,1)}, u32[]{:S(2)}, u32[]{:S(2)}) collective-permute-start(bf16[384,768]{1,0:T(8,128)(2,1)} %collective-permute-done.27.refs_2_), channel_id=1, source_target_pairs={{0,4},{4,0},{8,12},{12,8},{16,20},{20,16},{24,28},{28,24},{1,5},{5... | collective-permute-start | bytes 1769480 | tf_op jit(solution)/shard_map/ppermute | solution.py:560
  203.9 11.3 %collective-permute-start.30 = (bf16[384,768]{1,0:T(8,128)(2,1)}, bf16[384,768]{1,0:T(8,128)(2,1)}, u32[]{:S(2)}, u32[]{:S(2)}) collective-permute-start(bf16[384,768]{1,0:T(8,128)(2,1)} %collective-permute-done.28.refs_3_), channel_id=1, source_target_pairs={{0,4},{4,0},{8,12},{12,8},{16,20},{20,16},{24,28},{28,24},{1,5},{5... | collective-permute-start | bytes 1769480 | tf_op jit(solution)/shard_map/ppermute | solution.py:560
  (36 other events, 289.4 us)
Sparse Core Ops, SparseCore 0:
  9.6 35.9 all-gather.5
  47.7 35.9 all-gather.3
  110.4 34.2 reduce-scatter.4
  147.4 35.3 reduce-scatter.2

commit v8 on v7

--- a/solution.py
+++ b/solution.py
@@ -600,13 +600,13 @@
     d_got = swap_heads(d_other)
     d_mine, two = head_product(head_mine, grad_rows, w_rows, NT, "d_o_own")
     grad_swapped = swap_heads(grad_rows)
-    normed_rows = after(normed_rows, packed, one, two)
-
+    normed_rows, *tokens = lax.optimization_barrier((normed_rows, packed, one, two))
+
+    normed_swapped = swap_heads(normed_rows)
     qkv_other, _ = head_product(
-        head_other, normed_rows, w_pack, NN, "qkv_other", d_got, grad_swapped
+        head_other, normed_rows, w_pack, NN, "qkv_other", d_got, grad_swapped, *tokens
     )
     qkv_got = swap_heads(qkv_other)
-    normed_swapped = swap_heads(normed_rows)
     qkv_mine, _ = head_product(head_mine, normed_rows, w_pack, NN, "qkv_own")
     result_mine, result_other = attention(qkv_mine, qkv_got, d_mine, d_got, normed_swapped)
     result_got = swap_heads(result_other)
@@ -626,7 +626,7 @@
     )
     part = to_chips(part)
     head_term = pair_term(
-        head_mine, result_mine, result_got, w_rows, 3 * DH, 4 * DH, "head_term", part[1]
+        head_mine, result_mine, result_got, w_rows, 3 * DH, 4 * DH, "head_term"
     )
     head_sum = lax.psum_scatter(head_term.reshape(shape), "head", scatter_dimension=0, tiled=False)
 

time: 230 us -> 225 us (0.978)
  waiting for transfers between devices: 102 us -> 82 us
  local copies, waits for them, and re-layouts: 26.1 us -> 40.7 us
    ppermute x18, waiting for transfers between devices: 66.3 us -> 48.6 us  [trade_chip(): return lax.ppermute(x, 'seq', [(s, s ^ bit * heads) for s in range(count)])]
    unnamed x56 -> x68, local copies, waits for them, and re-layouts: 18.3 us -> 33 us
    all_gather x1, waiting for transfers between devices: 15.4 us -> 3.87 us  [unit_body(): normed_rows = lax.all_gather(normed_slab, 'head', axis=0, tiled=True)]
    reduce_scatter x1, waiting for transfers between devices: 4.57 us -> 13.2 us  [unit_body(): lax.psum_scatter(d_term.reshape(shape), 'head', scatter_dimension=0, tile...]
    ppermute x2, starting transfers between devices: 4.22 us -> 7.13 us  [neighbour_edges(): lax.ppermute(last, axes, forward)]
    ppermute x9, waiting for transfers between devices: 3.1 us -> 5.98 us  [swap_heads(): lax.ppermute(x, 'seq', [(s, s + 1 - 2 * (s % 2)) for s in range(count)])]
  transfers between devices with their start and end apart: 35 -> 35, of which waited for: 22 -> 21; matrix products, arithmetic and copies ran while one was open for 4% -> 4% of each run, Pallas kernels for 15% -> 14%
where the time goes in v8:
time: 225 us; the launch traced here: 224 us
  waiting for transfers between devices  82 us (36%)
  Pallas kernels  48.2 us (21%)
  local copies, waits for them, and re-layouts  40.7 us (18%)
  starting transfers between devices  38.1 us (17%)
  between operations  14.2 us (6%)
    ppermute x18, waiting for transfers between devices, trade_chip(): return lax.ppermute(x, 'seq', [(s, s ^ bit * heads) for s in range(count)])  48.6 us
    unnamed x68, local copies, waits for them, and re-layouts  33 us
    ppermute x18, starting transfers between devices, trade_chip(): return lax.ppermute(x, 'seq', [(s, s ^ bit * heads) for s in range(count)])  18.8 us
    reduce_scatter x1, waiting for transfers between devices, unit_body(): lax.psum_scatter(d_term.reshape(shape), 'head', scatter_dimension=0, tile...  13.2 us
    pallas_call x1, Pallas kernels, weight_gradients(): pl.pallas_call(weight_kernel, grid_spec=pltpu.PrefetchScalarGridSpec(num_...  7.44 us
    ppermute x2, starting transfers between devices, neighbour_edges(): lax.ppermute(last, axes, forward)  7.13 us
    pallas_call x1, Pallas kernels, encoder(): pl.pallas_call(conv_kernel, grid=(width // tile,), in_specs=[SCALARS, who...  7.1 us
    pallas_call x1, Pallas kernels, unpack_weights(): pl.pallas_call(unpack_kernel, grid_spec=pltpu.PrefetchScalarGridSpec(num_...  6.85 us
  transfers between devices with their start and end apart: 35, of which 21 were waited for; matrix products, arithmetic and copies ran while one was open for 4% of the time, Pallas kernels for 14%

profile of v8, /device:TPU:26, one launch (start us, length us, event | category | flops | bytes accessed | tf_op | source)
XLA Modules:
  0.0 223.6 jit_solution(3954345619182068244)
XLA Ops:
  9.1 2.4 %collective-permute-start.1 = (bf16[2,4,1,768]{3,2,1,0:T(2,128)(2,1)S(1)}, bf16[2,4,1,768]{3,2,1,0:T(2,128)(2,1)S(1)}, u32[]{:S(2)}, u32[]{:S(2)}) collective-permute-start(bf16[2,4,1,768]{3,2,1,0:T(2,128)(2,1)S(1)} %get-tuple-element.104), channel_id=1, source_target_pairs={{1,0},{2,1},{3,2},{4,3},{5,4},{6,5},{7,6},{8,7},{9,8},{10,9},{11,1... | collective-permute-start | bytes 36872 | tf_op jit(solution)/shard_map/ppermute | solution.py:546
  11.4 5.0 %collective-permute-start = (bf16[2,4,1,768]{3,2,1,0:T(2,128)(2,1)S(1)}, bf16[2,4,1,768]{3,2,1,0:T(2,128)(2,1)S(1)}, u32[]{:S(2)}, u32[]{:S(2)}) collective-permute-start(bf16[2,4,1,768]{3,2,1,0:T(2,128)(2,1)S(1)} %get-tuple-element.105), channel_id=1, source_target_pairs={{0,1},{1,2},{2,3},{3,4},{4,5},{5,6},{6,7},{7,8},{8,9},{9,10},{10,1... | collective-permute-start | bytes 36872 | tf_op jit(solution)/shard_map/ppermute | solution.py:546
  17.9 4.5 %copy-done = bf16[5,768,1536]{2,1,0:T(8,128)(2,1)S(1)} copy-done((bf16[5,768,1536]{2,1,0:T(8,128)(2,1)S(1)}, bf16[5,768,1536]{2,1,0:T(8,128)(2,1)}, u32[]{:S(2)}) %copy-start) | copy-done | bytes 11796504
  22.5 7.1 %encoder_forward.1 = (bf16[4,32,1536]{2,1,0:T(8,128)(2,1)S(1)}, f32[2,4,32,1536]{3,2,1,0:T(8,128)S(1)}, bf16[32,1536]{1,0:T(8,128)(2,1)S(1)}, bf16[32,1536]{1,0:...) custom-call(s32[2]{0:T(128)S(1)} %pad_add_fusion.at_ref, ...), custom_call_target="tpu_custom_call" | custom-call | flops 1000 | bytes 1000 | tf_op jit(solution)/shard_map/encoder_forward/pallas_call | solution.py:110
  35.0 2.2 collective-permute-done.2
  41.3 4.3 %all-gather.6.cloned.1.call-done = bf16[128,4,1536]{2,1,0:T(4,128)(2,1)} async-done(((bf16[32,4,1536]{2,1,0:T(4,128)(2,1)}), bf16[128,4,1536]{2,1,0:T(4,128)(2,1)}) %all-gather.6.cloned.1.call-update) | async-done | bytes 1572880 | tf_op jit(solution)/shard_map/all_gather | solution.py:583
  51.0 9.4 %collective-permute-done.7 = bf16[4,32,1536]{2,1,0:T(8,128)(2,1)S(1)} collective-permute-done((bf16[4,32,1536]{2,1,0:T(8,128)(2,1)S(1)}, bf16[4,32,1536]{2,1,0:T(8,128)(2,1)S(1)}, u32[]{:S(2)}, u32[]{:S(2)}) %collective-permute-start.7) | collective-permute-done | bytes 393248 | tf_op jit(solution)/shard_map/ppermute | solution.py:555
  60.4 7.5 %collective-permute-done.6 = bf16[4,32,1536]{2,1,0:T(8,128)(2,1)S(1)} collective-permute-done((bf16[4,32,1536]{2,1,0:T(8,128)(2,1)S(1)}, bf16[4,32,1536]{2,1,0:T(8,128)(2,1)S(1)}, u32[]{:S(2)}, u32[]{:S(2)}) %collective-permute-start.6) | collective-permute-done | bytes 393248 | tf_op jit(solution)/shard_map/ppermute | solution.py:555
  70.3 3.9 %pack_weights.1 = (bf16[2,1536,576]{2,1,0:T(8,128)(2,1)S(1)}, bf16[2,576,1536]{2,1,0:T(8,128)(2,1)S(1)}, f32[8,128]{1,0:T(8,128)S(1)}) custom-call(bf16[3,1536,384]{2,1,0:T(8,128)(2,1)S(1)} %copy-done.13), custom_call_target="tpu_custom_call" | custom-call | flops 1000 | bytes 1000 | tf_op jit(solution)/shard_map/pack_weights/pallas_call | solution.py:263
  79.8 3.9 %all-gather.4.cloned.1.call-done.x_ref.xa_ref = bf16[512,1536]{1,0:T(8,128)(2,1)} async-done(((bf16[128,1536]{1,0:T(8,128)(2,1)}), bf16[512,1536]{1,0:T(8,128)(2,1)}) %all-gather.4.cloned.1.call-update) | async-done | bytes 1572880 | tf_op jit(solution)/shard_map/all_gather | solution.py:590
  84.2 2.9 %collective-permute-done.8.rest_0_.db_ref = bf16[512,256]{1,0:T(8,128)(2,1)S(1)} collective-permute-done((bf16[512,256]{1,0:T(8,128)(2,1)S(1)}, bf16[512,256]{1,0:T(8,128)(2,1)S(1)}, u32[]{:S(2)}, u32[]{:S(2)}) %collective-permute-start.8) | collective-permute-done | bytes 262176 | tf_op jit(solution)/shard_map/ppermute | solution.py:560
  94.8 6.5 %attention.1 = (bf16[512,768]{1,0:T(8,128)(2,1)S(1)}, bf16[512,768]{1,0:T(8,128)(2,1)S(1)}) custom-call(bf16[512,640]{1,0:T(8,128)(2,1)S(1)} %get-tuple-element.55.qa_ref, bf16[512,640]{1,0:T(8,128)(2,1)S(1)} %collective-permute-done.10.qb_ref, bf16[512,256]{1,0:T(8,128)(2,1)S(1)} %copy-done.28, bf16[512,256]{1,0:T(8,128)(2,1)S(1)} %collective-permute-done.8.rest_0_.db_ref, ...), custom_call_target="tpu_custom_call" | custom-call | flops 1000 | bytes 1000 | tf_op jit(solution)/shard_map/attention/pallas_call | solution.py:364
  103.7 3.3 %d_term.1 = bf16[512,1536]{1,0:T(8,128)(2,1)S(1)} custom-call(s32[1]{0:T(128)} %bitcast.1.head_ref, bf16[512,768]{1,0:T(8,128)(2,1)S(1)} %get-tuple-element.62.a_ref.ra_ref, bf16[512,768]{1,0:T(8,128)(2,1)S(1)} %collective-permute-done.12.b_ref, bf16[2,576,1536]{2,1,0:T(8,128)(2,1)S(1)} %copy-done.15), custom_call_target="tpu_custom_call" | custom-call | flops 1000 | bytes 1000 | tf_op jit(solution)/shard_map/d_term/pallas_call | solution.py:391
  117.6 7.4 %weight_gradients.1 = (bf16[768,384]{1,0:T(8,128)(2,1)S(1)}, bf16[768,384]{1,0:T(8,128)(2,1)}, bf16[768,384]{1,0:T(8,128)(2,1)}, bf16[768,384]{1,0:T(8,128)(2,1)}) custom-call(s32[1]{0:T(128)} %bitcast.at_ref, bf16[512,1536]{1,0:T(8,128)(2,1)S(1)} %copy-done.5, bf16[512,1536]{1,0:T(8,128)(2,1)S(1)} %copy-done.12, bf16[512,1536]{1,0:T(8,128)(2,1)S(1)} %bitcast.48, ...), custom_call_target="tpu_custom_call" | custom-call | flops 1000 | bytes 1000 | tf_op jit(solution)/shard_map/weight_gradients/pallas_call | solution.py:440
  129.4 13.2 %reduce-scatter.5.cloned.1.call-done = bf16[1,4,32,1536]{3,2,1,0:T(8,128)(2,1)} async-done(((bf16[4,4,32,1536]{3,2,1,0:T(8,128)(2,1)}), bf16[1,4,32,1536]{3,2,1,0:T(8,128)(2,1)}) %reduce-scatter.5.cloned.1.call-update) | async-done | bytes 393232 | tf_op jit(solution)/shard_map/reduce_scatter | solution.py:616
  145.1 13.3 %collective-permute-done.13.near_ref = bf16[2,32,1536]{2,1,0:T(8,128)(2,1)S(1)} collective-permute-done((bf16[2,32,1536]{2,1,0:T(8,128)(2,1)S(1)}, bf16[2,32,1536]{2,1,0:T(8,128)(2,1)S(1)}, u32[]{:S(2)}, u32[]{:S(2)}) %collective-permute-start.13) | collective-permute-done | bytes 196640 | tf_op jit(solution)/shard_map/ppermute | solution.py:555
  160.0 4.8 %collective-permute-done.14.far_ref.refs_4_ = bf16[2,32,1536]{2,1,0:T(8,128)(2,1)S(1)} collective-permute-done((bf16[2,32,1536]{2,1,0:T(8,128)(2,1)S(1)}, bf16[2,32,1536]{2,1,0:T(8,128)(2,1)S(1)}, u32[]{:S(2)}, u32[]{:S(2)}) %collective-permute-start.14) | collective-permute-done | bytes 196640 | tf_op jit(solution)/shard_map/ppermute | solution.py:555
  170.7 3.7 %collective-permute-start.16 = (bf16[2,4,1,1536]{3,2,1,0:T(2,128)(2,1)S(1)}, bf16[2,4,1,1536]{3,2,1,0:T(2,128)(2,1)S(1)}, u32[]{:S(2)}, u32[]{:S(2)}) collective-permute-start(bf16[2,4,1,1536]{3,2,1,0:T(2,128)(2,1)S(1)} %get-tuple-element.70), channel_id=1, source_target_pairs={{1,0},{2,1},{3,2},{4,3},{5,4},{6,5},{7,6},{8,7},{9,8},{10,9},{11,1... | collective-permute-start | bytes 73736 | tf_op jit(solution)/shard_map/ppermute | solution.py:546
  174.5 3.1 %collective-permute-done.15.low_ref = bf16[2,4,1,1536]{3,2,1,0:T(2,128)(2,1)S(1)} collective-permute-done((bf16[2,4,1,1536]{3,2,1,0:T(2,128)(2,1)S(1)}, bf16[2,4,1,1536]{3,2,1,0:T(2,128)(2,1)S(1)}, u32[]{:S(2)}, u32[]{:S(2)}) %collective-permute-start.15) | collective-permute-done | bytes 24608 | tf_op jit(solution)/shard_map/ppermute | solution.py:546
  179.2 3.9 %collective-permute-start.23 = (bf16[384,768]{1,0:T(8,128)(2,1)S(1)}, bf16[384,768]{1,0:T(8,128)(2,1)S(1)}, u32[]{:S(2)}, u32[]{:S(2)}) collective-permute-start(bf16[384,768]{1,0:T(8,128)(2,1)S(1)} %constant_dynamic-update-slice_fusion.6.refs_1_), channel_id=1, source_target_pairs={{0,4},{4,0},{8,12},{12,8},{16,20},{20,16},{24,28},{28,24},{1,5},{5... | collective-permute-start | bytes 1769480 | tf_op jit(solution)/shard_map/ppermute | solution.py:560
  185.6 4.3 %copy-done.1 = bf16[5,768,1536]{2,1,0:T(8,128)(2,1)S(1)} copy-done((bf16[5,768,1536]{2,1,0:T(8,128)(2,1)S(1)}, bf16[5,768,1536]{2,1,0:T(8,128)(2,1)}, u32[]{:S(2)}) %copy-start.1) | copy-done | bytes 11796504
  190.0 4.3 %encoder_backward.1 = bf16[256,768]{1,0:T(8,128)(2,1)S(1)} custom-call(bf16[2,4,32,1536]{3,2,1,0:T(8,128)(2,1)S(1)} %get-tuple-element.68.d_ref, bf16[2,4,1,1536]{3,2,1,0:T(2,128)(2,1)S(1)} %collective-permute-done.15.low_ref, bf16[2,4,1,1536]{3,2,1,0:T(2,128)(2,1)S(1)} %collective-permute-done.16.high_ref, bf16[5,768,1536]{2,1,0:T(8,128)(2,1)S(1)} %copy-done.1, ...), custom_call_target="tpu_custom_call" | custom-call | flops 1000 | bytes 1000 | tf_op jit(solution)/shard_map/encoder_backward/pallas_call | solution.py:227
  194.3 4.8 %collective-permute-done.28.refs_3_ = bf16[384,768]{1,0:T(8,128)(2,1)} collective-permute-done((bf16[384,768]{1,0:T(8,128)(2,1)S(1)}, bf16[384,768]{1,0:T(8,128)(2,1)}, u32[]{:S(2)}, u32[]{:S(2)}) %collective-permute-start.28) | collective-permute-done | bytes 589856 | tf_op jit(solution)/shard_map/ppermute | solution.py:555
  210.3 6.8 %weight_outputs.1 = (f32[3,1536,384]{2,1,0:T(8,128)}, f32[384,1536]{1,0:T(8,128)}) custom-call(s32[2]{0:T(128)S(1)} %pad_add_fusion.at_ref, bf16[384,768]{1,0:T(8,128)(2,1)S(1)} %constant_dynamic-update-slice_fusion.4.refs_0_, bf16[384,768]{1,0:T(8,128)(2,1)S(1)} %constant_dynamic-update-slice_fusion.6.refs_1_, ...), custom_call_target="tpu_custom_call" | custom-call | flops 1000 | bytes 1000 | tf_op jit(solution)/shard_map/weight_outputs/pallas_call | solution.py:520
  (151 shorter events, 76.7 us)
Async XLA Ops:
  7.2 38.4 %all-gather.6.cloned.1.call-start = ((), (), s32[]{:S(2)}) async-start(), calls=%async_computation.5 | async-start | bytes 1966080 | tf_op jit(solution)/shard_map/all_gather | solution.py:583
  7.9 75.8 %all-gather.4.cloned.1.call-start = ((), (), s32[]{:S(2)}) async-start(), calls=%async_computation.2 | async-start | bytes 1966080 | tf_op jit(solution)/shard_map/all_gather | solution.py:590
  9.1 8.2 %collective-permute-start.1 = (bf16[2,4,1,768]{3,2,1,0:T(2,128)(2,1)S(1)}, bf16[2,4,1,768]{3,2,1,0:T(2,128)(2,1)S(1)}, u32[]{:S(2)}, u32[]{:S(2)}) collective-permute-start(bf16[2,4,1,768]{3,2,1,0:T(2,128)(2,1)S(1)} %get-tuple-element.104), channel_id=1, source_target_pairs={{1,0},{2,1},{3,2},{4,3},{5,4},{6,5},{7,6},{8,7},{9,8},{10,9},{11,1... | collective-permute-start | bytes 36872 | tf_op jit(solution)/shard_map/ppermute | solution.py:546
  11.4 6.5 %collective-permute-start = (bf16[2,4,1,768]{3,2,1,0:T(2,128)(2,1)S(1)}, bf16[2,4,1,768]{3,2,1,0:T(2,128)(2,1)S(1)}, u32[]{:S(2)}, u32[]{:S(2)}) collective-permute-start(bf16[2,4,1,768]{3,2,1,0:T(2,128)(2,1)S(1)} %get-tuple-element.105), channel_id=1, source_target_pairs={{0,1},{1,2},{2,3},{3,4},{4,5},{5,6},{6,7},{7,8},{8,9},{9,10},{10,1... | collective-permute-start | bytes 36872 | tf_op jit(solution)/shard_map/ppermute | solution.py:546
  33.6 6.9 %collective-permute-start.4 = (bf16[32,1536]{1,0:T(8,128)(2,1)S(1)}, bf16[32,1536]{1,0:T(8,128)(2,1)S(1)}, u32[]{:S(2)}, u32[]{:S(2)}) collective-permute-start(bf16[32,1536]{1,0:T(8,128)(2,1)S(1)} %get-tuple-element.47), channel_id=1, source_target_pairs={{0,24},{4,28},{8,16},{12,20},{16,8},{20,12},{24,0},{28,4},{1,25},{... | collective-permute-start | bytes 294920 | tf_op jit(solution)/shard_map/ppermute | solution.py:555
  41.2 101.4 %reduce-scatter.5.cloned.1.call-start = ((), (), s32[]{:S(2)}) async-start(), calls=%async_computation.4 | async-start | bytes 1966080 | tf_op jit(solution)/shard_map/reduce_scatter | solution.py:616
  47.4 13.0 %collective-permute-start.7 = (bf16[4,32,1536]{2,1,0:T(8,128)(2,1)S(1)}, bf16[4,32,1536]{2,1,0:T(8,128)(2,1)S(1)}, u32[]{:S(2)}, u32[]{:S(2)}) collective-permute-start(bf16[4,32,1536]{2,1,0:T(8,128)(2,1)S(1)} %get-tuple-element.97), channel_id=1, source_target_pairs={{0,24},{4,28},{8,16},{12,20},{16,8},{20,12},{24,0},{28,4},{1,25},{... | collective-permute-start | bytes 1179656 | tf_op jit(solution)/shard_map/ppermute | solution.py:555
  48.9 19.0 %collective-permute-start.6 = (bf16[4,32,1536]{2,1,0:T(8,128)(2,1)S(1)}, bf16[4,32,1536]{2,1,0:T(8,128)(2,1)S(1)}, u32[]{:S(2)}, u32[]{:S(2)}) collective-permute-start(bf16[4,32,1536]{2,1,0:T(8,128)(2,1)S(1)} %get-tuple-element.98), channel_id=1, source_target_pairs={{0,8},{4,12},{8,0},{12,4},{16,24},{20,28},{24,16},{28,20},{1,9},{5... | collective-permute-start | bytes 1179656 | tf_op jit(solution)/shard_map/ppermute | solution.py:555
  50.4 17.5 %collective-permute-start.5 = (bf16[4,32,1536]{2,1,0:T(8,128)(2,1)S(1)}, bf16[4,32,1536]{2,1,0:T(8,128)(2,1)S(1)}, u32[]{:S(2)}, u32[]{:S(2)}) collective-permute-start(bf16[4,32,1536]{2,1,0:T(8,128)(2,1)S(1)} %get-tuple-element.99), channel_id=1, source_target_pairs={{0,16},{4,20},{8,24},{12,28},{16,0},{20,4},{24,8},{28,12},{1,17},{... | collective-permute-start | bytes 1179656 | tf_op jit(solution)/shard_map/ppermute | solution.py:555
  68.2 18.9 %collective-permute-start.9 = (bf16[512,1536]{1,0:T(8,128)(2,1)S(1)}, bf16[512,1536]{1,0:T(8,128)(2,1)}, u32[]{:S(2)}, u32[]{:S(2)}) collective-permute-start(bf16[512,1536]{1,0:T(8,128)(2,1)S(1)} %bitcast.45), channel_id=1, source_target_pairs={{0,4},{4,0},{8,12},{12,8},{16,20},{20,16},{24,28},{28,24},{1,5},{5... | collective-permute-start | bytes 4718600 | tf_op jit(solution)/shard_map/ppermute | solution.py:560
  83.7 11.1 %collective-permute-start.11 = (bf16[512,1536]{1,0:T(8,128)(2,1)}, bf16[512,1536]{1,0:T(8,128)(2,1)S(1)}, u32[]{:S(2)}, u32[]{:S(2)}) collective-permute-start(bf16[512,1536]{1,0:T(8,128)(2,1)} %all-gather.4.cloned.1.call-done.x_ref.xa_ref), channel_id=1, source_target_pairs={{0,4},{4,0},{8,12},{12,8},{16,20},{20,16},{24,28},{28,24},{1,5},{5... | collective-permute-start | bytes 4718600 | tf_op jit(solution)/shard_map/ppermute | solution.py:560
  108.2 91.4 %reduce-scatter.3.cloned.1.call-start = ((), (), s32[]{:S(2)}) async-start(), calls=%async_computation.3 | async-start | bytes 1966080 | tf_op jit(solution)/shard_map/reduce_scatter | solution.py:631
  125.9 34.1 %collective-permute-start.17 = (bf16[768,384]{1,0:T(8,128)(2,1)}, bf16[768,384]{1,0:T(8,128)(2,1)S(1)}, u32[]{:S(2)}, u32[]{:S(2)}) collective-permute-start(bf16[768,384]{1,0:T(8,128)(2,1)} %get-tuple-element.72), channel_id=1, source_target_pairs={{0,8},{4,12},{8,0},{12,4},{16,24},{20,28},{24,16},{28,20},{1,9},{5... | collective-permute-start | bytes 1769480 | tf_op jit(solution)/shard_map/ppermute | solution.py:555
  126.5 33.5 %collective-permute-start.18 = (bf16[768,384]{1,0:T(8,128)(2,1)}, bf16[768,384]{1,0:T(8,128)(2,1)S(1)}, u32[]{:S(2)}, u32[]{:S(2)}) collective-permute-start(bf16[768,384]{1,0:T(8,128)(2,1)} %get-tuple-element.73), channel_id=1, source_target_pairs={{0,16},{4,20},{8,24},{12,28},{16,0},{20,4},{24,8},{28,12},{1,17},{... | collective-permute-start | bytes 1769480 | tf_op jit(solution)/shard_map/ppermute | solution.py:555
  127.9 32.0 %collective-permute-start.19 = (bf16[768,384]{1,0:T(8,128)(2,1)}, bf16[768,384]{1,0:T(8,128)(2,1)S(1)}, u32[]{:S(2)}, u32[]{:S(2)}) collective-permute-start(bf16[768,384]{1,0:T(8,128)(2,1)} %get-tuple-element.74), channel_id=1, source_target_pairs={{0,24},{4,28},{8,16},{12,20},{16,8},{20,12},{24,0},{28,4},{1,25},{... | collective-permute-start | bytes 1769480 | tf_op jit(solution)/shard_map/ppermute | solution.py:555
  143.6 14.9 %collective-permute-start.13 = (bf16[2,32,1536]{2,1,0:T(8,128)(2,1)S(1)}, bf16[2,32,1536]{2,1,0:T(8,128)(2,1)S(1)}, u32[]{:S(2)}, u32[]{:S(2)}) collective-permute-start(bf16[2,32,1536]{2,1,0:T(8,128)(2,1)S(1)} %slice_bitcast_fusion), channel_id=1, source_target_pairs={{0,8},{4,12},{8,0},{12,4},{16,24},{20,28},{24,16},{28,20},{1,9},{5... | collective-permute-start | bytes 589832 | tf_op jit(solution)/shard_map/ppermute | solution.py:555
  165.2 13.9 %collective-permute-start.22 = (bf16[192,768]{1,0:T(8,128)(2,1)S(1)}, bf16[192,768]{1,0:T(8,128)(2,1)S(1)}, u32[]{:S(2)}, u32[]{:S(2)}) collective-permute-start(bf16[192,768]{1,0:T(8,128)(2,1)S(1)} %get-tuple-element.77), channel_id=1, source_target_pairs={{0,16},{4,20},{8,24},{12,28},{16,0},{20,4},{24,8},{28,12},{1,17},{... | collective-permute-start | bytes 884744 | tf_op jit(solution)/shard_map/ppermute | solution.py:555
  166.7 12.4 %collective-permute-start.20 = (bf16[192,768]{1,0:T(8,128)(2,1)S(1)}, bf16[192,768]{1,0:T(8,128)(2,1)S(1)}, u32[]{:S(2)}, u32[]{:S(2)}) collective-permute-start(bf16[192,768]{1,0:T(8,128)(2,1)S(1)} %get-tuple-element.75), channel_id=1, source_target_pairs={{0,8},{4,12},{8,0},{12,4},{16,24},{20,28},{24,16},{28,20},{1,9},{5... | collective-permute-start | bytes 884744 | tf_op jit(solution)/shard_map/ppermute | solution.py:555
  168.6 9.0 %collective-permute-start.15 = (bf16[2,4,1,1536]{3,2,1,0:T(2,128)(2,1)S(1)}, bf16[2,4,1,1536]{3,2,1,0:T(2,128)(2,1)S(1)}, u32[]{:S(2)}, u32[]{:S(2)}) collective-permute-start(bf16[2,4,1,1536]{3,2,1,0:T(2,128)(2,1)S(1)} %get-tuple-element.69), channel_id=1, source_target_pairs={{0,1},{1,2},{2,3},{3,4},{4,5},{5,6},{6,7},{7,8},{8,9},{9,10},{10,1... | collective-permute-start | bytes 73736 | tf_op jit(solution)/shard_map/ppermute | solution.py:546
  170.7 8.4 %collective-permute-start.16 = (bf16[2,4,1,1536]{3,2,1,0:T(2,128)(2,1)S(1)}, bf16[2,4,1,1536]{3,2,1,0:T(2,128)(2,1)S(1)}, u32[]{:S(2)}, u32[]{:S(2)}) collective-permute-start(bf16[2,4,1,1536]{3,2,1,0:T(2,128)(2,1)S(1)} %get-tuple-element.70), channel_id=1, source_target_pairs={{1,0},{2,1},{3,2},{4,3},{5,4},{6,5},{7,6},{8,7},{9,8},{10,9},{11,1... | collective-permute-start | bytes 73736 | tf_op jit(solution)/shard_map/ppermute | solution.py:546
  183.2 15.8 %collective-permute-start.28 = (bf16[384,768]{1,0:T(8,128)(2,1)S(1)}, bf16[384,768]{1,0:T(8,128)(2,1)}, u32[]{:S(2)}, u32[]{:S(2)}) collective-permute-start(bf16[384,768]{1,0:T(8,128)(2,1)S(1)} %constant_dynamic-update-slice_fusion.6.refs_1_), channel_id=1, source_target_pairs={{0,8},{4,12},{8,0},{12,4},{16,24},{20,28},{24,16},{28,20},{1,9},{5... | collective-permute-start | bytes 1769480 | tf_op jit(solution)/shard_map/ppermute | solution.py:555
  183.3 15.8 %collective-permute-start.27 = (bf16[384,768]{1,0:T(8,128)(2,1)S(1)}, bf16[384,768]{1,0:T(8,128)(2,1)}, u32[]{:S(2)}, u32[]{:S(2)}) collective-permute-start(bf16[384,768]{1,0:T(8,128)(2,1)S(1)} %constant_dynamic-update-slice_fusion.4.refs_0_), channel_id=1, source_target_pairs={{0,16},{4,20},{8,24},{12,28},{16,0},{20,4},{24,8},{28,12},{1,17},{... | collective-permute-start | bytes 1769480 | tf_op jit(solution)/shard_map/ppermute | solution.py:555
  199.1 11.2 %collective-permute-start.29 = (bf16[384,768]{1,0:T(8,128)(2,1)}, bf16[384,768]{1,0:T(8,128)(2,1)}, u32[]{:S(2)}, u32[]{:S(2)}) collective-permute-start(bf16[384,768]{1,0:T(8,128)(2,1)} %collective-permute-done.27.refs_2_), channel_id=1, source_target_pairs={{0,4},{4,0},{8,12},{12,8},{16,20},{20,16},{24,28},{28,24},{1,5},{5... | collective-permute-start | bytes 1769480 | tf_op jit(solution)/shard_map/ppermute | solution.py:560
  199.1 11.2 %collective-permute-start.30 = (bf16[384,768]{1,0:T(8,128)(2,1)}, bf16[384,768]{1,0:T(8,128)(2,1)}, u32[]{:S(2)}, u32[]{:S(2)}) collective-permute-start(bf16[384,768]{1,0:T(8,128)(2,1)} %collective-permute-done.28.refs_3_), channel_id=1, source_target_pairs={{0,4},{4,0},{8,12},{12,8},{16,20},{20,16},{24,28},{28,24},{1,5},{5... | collective-permute-start | bytes 1769480 | tf_op jit(solution)/shard_map/ppermute | solution.py:560
  (42 other events, 189.0 us)
Sparse Core Ops, SparseCore 0:
  9.6 35.9 all-gather.5
  47.7 35.9 all-gather.3
  108.3 34.2 reduce-scatter.4
  145.3 35.8 reduce-scatter.2

commit v9 on v8

--- a/solution.py
+++ b/solution.py
@@ -10,14 +10,15 @@
 DH = 192
 KW = 5
 VMEM_LIMIT = 24 * 1024 * 1024
+STREAMING_LIMIT = 56 * 1024 * 1024
 COST = pl.CostEstimate(flops=1000, bytes_accessed=1000, transcendentals=0)
 BF = jnp.bfloat16
 F32 = jnp.float32
 TOKEN = jax.ShapeDtypeStruct((8, 128), F32)
 
 
-def params():
-    return pltpu.CompilerParams(vmem_limit_bytes=VMEM_LIMIT)
+def params(limit=VMEM_LIMIT):
+    return pltpu.CompilerParams(vmem_limit_bytes=limit)
 
 
 def dot(a, b, contract):
@@ -133,7 +134,7 @@
             pltpu.VMEM((seqs * rows, 1), F32),
             pltpu.VMEM(shape, BF),
         ],
-        compiler_params=params(),
+        compiler_params=params(STREAMING_LIMIT),
         cost_estimate=COST,
         name="encoder_forward",
     )(at, pairs, low, high, conv_weight, norm_gain.reshape(1, width))
@@ -141,7 +142,8 @@
 
 
 def d_conv_kernel(at_ref, own_ref, near_ref, far_ref, *refs):
-    skip_ref, grad_ref, gain_ref, slope_ref, out_ref, first_ref, last_ref = refs
+    skip_ref, grad_ref, gain_ref, slope_ref = refs[:4]
+    out_ref, first_ref, last_ref = refs[-3:]
     rows = out_ref.shape[2]
     for slot, (ref, place) in enumerate(((own_ref, 0), (near_ref, 0), (far_ref, 0), (far_ref, 1))):
         b = at_ref[0] ^ slot
@@ -160,18 +162,18 @@
             last_ref[parity, b] = value[rows - 1 :].astype(BF)
 
 
-def conv_gradient(at, own, near, far, skip, grad, norm_gain, slope):
+def conv_gradient(at, own, near, far, skip, grad, norm_gain, slope, *deps):
     vmem = pl.BlockSpec(memory_space=pltpu.VMEM)
     edge = jax.ShapeDtypeStruct(slope.shape[:2] + (1, slope.shape[3]), BF)
     return pl.pallas_call(
         d_conv_kernel,
-        in_specs=[SCALARS] + [vmem] * 7,
+        in_specs=[SCALARS] + [vmem] * 7 + spare(deps),
         out_specs=[vmem] * 3,
         out_shape=[jax.ShapeDtypeStruct(slope.shape, BF)] + [edge] * 2,
         compiler_params=params(),
         cost_estimate=COST,
         name="conv_gradient",
-    )(at, own, near, far, skip, grad, norm_gain.reshape(1, -1), slope)
+    )(at, own, near, far, skip, grad, norm_gain.reshape(1, -1), slope, *deps)
 
 
 def mixed_body(seqs, at_ref, *refs):
@@ -447,7 +449,7 @@
             scratch_shapes=[pltpu.VMEM((full, 2 * half), BF)],
         ),
         out_shape=[jax.ShapeDtypeStruct((full, chunk), BF)] * seqs,
-        compiler_params=params(),
+        compiler_params=params(STREAMING_LIMIT),
         cost_estimate=COST,
         name="weight_gradients",
     )(at, xa, xb, ga, gb, ra, rb)
@@ -600,12 +602,14 @@
     d_got = swap_heads(d_other)
     d_mine, two = head_product(head_mine, grad_rows, w_rows, NT, "d_o_own")
     grad_swapped = swap_heads(grad_rows)
-    normed_rows, *tokens = lax.optimization_barrier((normed_rows, packed, one, two))
+    normed_rows, d_got, d_mine, grad_swapped, w_pack, w_turned, *tokens = (
+        lax.optimization_barrier(
+            (normed_rows, d_got, d_mine, grad_swapped, w_pack, w_turned, packed, one, two)
+        )
+    )
 
     normed_swapped = swap_heads(normed_rows)
-    qkv_other, _ = head_product(
-        head_other, normed_rows, w_pack, NN, "qkv_other", d_got, grad_swapped, *tokens
-    )
+    qkv_other, _ = head_product(head_other, normed_rows, w_pack, NN, "qkv_other", *tokens)
     qkv_got = swap_heads(qkv_other)
     qkv_mine, _ = head_product(head_mine, normed_rows, w_pack, NN, "qkv_own")
     result_mine, result_other = attention(qkv_mine, qkv_got, d_mine, d_got, normed_swapped)
@@ -630,13 +634,16 @@
     )
     head_sum = lax.psum_scatter(head_term.reshape(shape), "head", scatter_dimension=0, tiled=False)
 
-    near = trade_chip(d_normed[2:], 1, heads)
+    leaving = d_normed[2:]
+    near = trade_chip(leaving, 1, heads)
     far = trade_chip(jnp.stack([d_normed[1], near[1]]), 2, heads)
     grad = jnp.transpose(after(grad_out, d_term), (1, 0, 2))
-    d_conv, first, last = conv_gradient(at, d_normed, near, far, skip, grad, norm_gain, slope)
+    half_a, half_b = weight_sum(part, leaving)
+    d_conv, first, last = conv_gradient(
+        at, d_normed, near, far, skip, grad, norm_gain, slope, half_a
+    )
     low, high = neighbour_edges(first, last)
 
-    half_a, half_b = weight_sum(part, far)
     got_a = trade_chip(half_a, 1, heads)
     got_b = trade_chip(half_b, 2, heads)
     near_a = jnp.concatenate([half_a, after(got_a, low, high)], axis=0)

time: 225 us -> 216 us (0.960)
  local copies, waits for them, and re-layouts: 40.7 us -> 29.5 us
  Pallas kernels: 48.2 us -> 53.3 us
  waiting for transfers between devices: 82 us -> 77.4 us
    unnamed x68 -> x62, local copies, waits for them, and re-layouts: 33 us -> 21.1 us
    ppermute x18, waiting for transfers between devices: 48.6 us -> 41.9 us  [trade_chip(): return lax.ppermute(x, 'seq', [(s, s ^ bit * heads) for s in range(count)])]
    reduce_scatter x1, waiting for transfers between devices: 13.2 us -> 19 us  [unit_body(): lax.psum_scatter(d_term.reshape(shape), 'head', scatter_dimension=0, tile...]
    pallas_call x1, Pallas kernels: 7.1 us -> 10.1 us  [encoder(): pl.pallas_call(conv_kernel, grid=(width // tile,), in_specs=[SCALARS, who...]
    ppermute x9, waiting for transfers between devices: 5.98 us -> 3.39 us  [swap_heads(): lax.ppermute(x, 'seq', [(s, s + 1 - 2 * (s % 2)) for s in range(count)])]
  transfers between devices with their start and end apart: 35 -> 35, of which waited for: 21 -> 19; matrix products, arithmetic and copies ran while one was open for 4% -> 5% of each run, Pallas kernels for 14% -> 17%
where the time goes in v9:
time: 216 us; the launch traced here: 214 us
  waiting for transfers between devices  77.4 us (36%)
  Pallas kernels  53.3 us (25%)
  starting transfers between devices  39.1 us (18%)
  local copies, waits for them, and re-layouts  29.5 us (14%)
  between operations  14.2 us (7%)
    ppermute x18, waiting for transfers between devices, trade_chip(): return lax.ppermute(x, 'seq', [(s, s ^ bit * heads) for s in range(count)])  41.9 us
    unnamed x62, local copies, waits for them, and re-layouts  21.1 us
    reduce_scatter x1, waiting for transfers between devices, unit_body(): lax.psum_scatter(d_term.reshape(shape), 'head', scatter_dimension=0, tile...  19 us
    ppermute x18, starting transfers between devices, trade_chip(): return lax.ppermute(x, 'seq', [(s, s ^ bit * heads) for s in range(count)])  18.6 us
    pallas_call x1, Pallas kernels, encoder(): pl.pallas_call(conv_kernel, grid=(width // tile,), in_specs=[SCALARS, who...  10.1 us
    pallas_call x1, Pallas kernels, weight_gradients(): pl.pallas_call(weight_kernel, grid_spec=pltpu.PrefetchScalarGridSpec(num_...  8.86 us
    ppermute x2, starting transfers between devices, neighbour_edges(): lax.ppermute(last, axes, forward)  6.92 us
    ppermute x9, starting transfers between devices, swap_heads(): lax.ppermute(x, 'seq', [(s, s + 1 - 2 * (s % 2)) for s in range(count)])  6.92 us
  transfers between devices with their start and end apart: 35, of which 19 were waited for; matrix products, arithmetic and copies ran while one was open for 5% of the time, Pallas kernels for 17%

profile of v9, /device:TPU:26, one launch (start us, length us, event | category | flops | bytes accessed | tf_op | source)
XLA Modules:
  0.0 214.4 jit_solution(11319300098116954072)
XLA Ops:
  9.1 2.4 %collective-permute-start.1 = (bf16[2,4,1,768]{3,2,1,0:T(2,128)(2,1)S(1)}, bf16[2,4,1,768]{3,2,1,0:T(2,128)(2,1)S(1)}, u32[]{:S(2)}, u32[]{:S(2)}) collective-permute-start(bf16[2,4,1,768]{3,2,1,0:T(2,128)(2,1)S(1)} %get-tuple-element.114), channel_id=1, source_target_pairs={{1,0},{2,1},{3,2},{4,3},{5,4},{6,5},{7,6},{8,7},{9,8},{10,9},{11,1... | collective-permute-start | bytes 36872 | tf_op jit(solution)/shard_map/ppermute | solution.py:548
  11.4 5.0 %collective-permute-start = (bf16[2,4,1,768]{3,2,1,0:T(2,128)(2,1)S(1)}, bf16[2,4,1,768]{3,2,1,0:T(2,128)(2,1)S(1)}, u32[]{:S(2)}, u32[]{:S(2)}) collective-permute-start(bf16[2,4,1,768]{3,2,1,0:T(2,128)(2,1)S(1)} %get-tuple-element.115), channel_id=1, source_target_pairs={{0,1},{1,2},{2,3},{3,4},{4,5},{5,6},{6,7},{7,8},{8,9},{9,10},{10,1... | collective-permute-start | bytes 36872 | tf_op jit(solution)/shard_map/ppermute | solution.py:548
  19.6 10.1 %encoder_forward.1 = (bf16[4,32,1536]{2,1,0:T(8,128)(2,1)}, f32[2,4,32,1536]{3,2,1,0:T(8,128)}, bf16[32,1536]{1,0:T(8,128)(2,1)}, bf16[32,1536]{1,0:T(8,128)(2,1...) custom-call(s32[2]{0:T(128)} %pad_add_fusion.at_ref, bf16[2,4,32,768]{3,2,1,0:T(8,128)(2,1)} %bitcast.59, ...), custom_call_target="tpu_custom_call" | custom-call | flops 1000 | bytes 1000 | tf_op jit(solution)/shard_map/encoder_forward/pallas_call | solution.py:111
  35.0 2.1 collective-permute-done.3
  39.7 5.9 %all-gather.6.cloned.1.call-done = bf16[128,4,1536]{2,1,0:T(4,128)(2,1)} async-done(((bf16[32,4,1536]{2,1,0:T(4,128)(2,1)}), bf16[128,4,1536]{2,1,0:T(4,128)(2,1)}) %all-gather.6.cloned.1.call-update) | async-done | bytes 1572880 | tf_op jit(solution)/shard_map/all_gather | solution.py:585
  51.0 9.4 %collective-permute-done.7 = bf16[4,32,1536]{2,1,0:T(8,128)(2,1)S(1)} collective-permute-done((bf16[4,32,1536]{2,1,0:T(8,128)(2,1)S(1)}, bf16[4,32,1536]{2,1,0:T(8,128)(2,1)S(1)}, u32[]{:S(2)}, u32[]{:S(2)}) %collective-permute-start.7) | collective-permute-done | bytes 393248 | tf_op jit(solution)/shard_map/ppermute | solution.py:557
  60.4 7.5 %collective-permute-done.6 = bf16[4,32,1536]{2,1,0:T(8,128)(2,1)S(1)} collective-permute-done((bf16[4,32,1536]{2,1,0:T(8,128)(2,1)S(1)}, bf16[4,32,1536]{2,1,0:T(8,128)(2,1)S(1)}, u32[]{:S(2)}, u32[]{:S(2)}) %collective-permute-start.6) | collective-permute-done | bytes 393248 | tf_op jit(solution)/shard_map/ppermute | solution.py:557
  72.6 3.9 %pack_weights.1 = (bf16[2,1536,576]{2,1,0:T(8,128)(2,1)S(1)}, bf16[2,576,1536]{2,1,0:T(8,128)(2,1)S(1)}, f32[8,128]{1,0:T(8,128)S(1)}) custom-call(bf16[3,1536,384]{2,1,0:T(8,128)(2,1)S(1)} %copy-done.9), custom_call_target="tpu_custom_call" | custom-call | flops 1000 | bytes 1000 | tf_op jit(solution)/shard_map/pack_weights/pallas_call | solution.py:265
  81.6 2.1 all-gather.4.cloned.1.call-done.x_ref.xa_ref
  83.8 2.1 copy-done.3
  91.7 6.5 %attention.1 = (bf16[512,768]{1,0:T(8,128)(2,1)S(1)}, bf16[512,768]{1,0:T(8,128)(2,1)S(1)}) custom-call(bf16[512,640]{1,0:T(8,128)(2,1)S(1)} %get-tuple-element.64.qa_ref, bf16[512,640]{1,0:T(8,128)(2,1)S(1)} %collective-permute-done.10.qb_ref, bf16[512,256]{1,0:T(8,128)(2,1)S(1)} %copy-done.20, bf16[512,256]{1,0:T(8,128)(2,1)S(1)} %copy-done.18, ...), custom_call_target="tpu_custom_call" | custom-call | flops 1000 | bytes 1000 | tf_op jit(solution)/shard_map/attention/pallas_call | solution.py:366
  98.4 2.1 collective-permute-done.12.b_ref
  100.5 4.1 %d_term.1 = bf16[512,1536]{1,0:T(8,128)(2,1)} custom-call(s32[1]{0:T(128)} %bitcast.1.head_ref, bf16[512,768]{1,0:T(8,128)(2,1)S(1)} %get-tuple-element.71.a_ref.ra_ref, bf16[512,768]{1,0:T(8,128)(2,1)S(1)} %collective-permute-done.12.b_ref, bf16[2,576,1536]{2,1,0:T(8,128)(2,1)S(1)} %copy-done.11), custom_call_target="tpu_custom_call" | custom-call | flops 1000 | bytes 1000 | tf_op jit(solution)/shard_map/d_term/pallas_call | solution.py:393
  107.7 8.9 %weight_gradients.1 = (bf16[768,384]{1,0:T(8,128)(2,1)}, bf16[768,384]{1,0:T(8,128)(2,1)}, bf16[768,384]{1,0:T(8,128)(2,1)}, bf16[768,384]{1,0:T(8,128)(2,1)}) custom-call(s32[1]{0:T(128)} %bitcast.at_ref, bf16[512,1536]{1,0:T(8,128)(2,1)} %all-gather.4.cloned.1.call-done.x_ref.xa_ref, bf16[512,1536]{1,0:T(8,128)(2,1)} %copy-done.8, ...), custom_call_target="tpu_custom_call" | custom-call | flops 1000 | bytes 1000 | tf_op jit(solution)/shard_map/weight_gradients/pallas_call | solution.py:442
  120.0 19.0 %reduce-scatter.5.cloned.1.call-done = bf16[1,4,32,1536]{3,2,1,0:T(8,128)(2,1)} async-done(((bf16[4,4,32,1536]{3,2,1,0:T(8,128)(2,1)}), bf16[1,4,32,1536]{3,2,1,0:T(8,128)(2,1)}) %reduce-scatter.5.cloned.1.call-update) | async-done | bytes 393232 | tf_op jit(solution)/shard_map/reduce_scatter | solution.py:620
  141.5 7.5 %collective-permute-done.13.near_ref = bf16[2,32,1536]{2,1,0:T(8,128)(2,1)S(1)} collective-permute-done((bf16[2,32,1536]{2,1,0:T(8,128)(2,1)S(1)}, bf16[2,32,1536]{2,1,0:T(8,128)(2,1)S(1)}, u32[]{:S(2)}, u32[]{:S(2)}) %collective-permute-start.13) | collective-permute-done | bytes 196640 | tf_op jit(solution)/shard_map/ppermute | solution.py:557
  152.4 4.6 %collective-permute-done.14.far_ref = bf16[2,32,1536]{2,1,0:T(8,128)(2,1)S(1)} collective-permute-done((bf16[2,32,1536]{2,1,0:T(8,128)(2,1)S(1)}, bf16[2,32,1536]{2,1,0:T(8,128)(2,1)S(1)}, u32[]{:S(2)}, u32[]{:S(2)}) %collective-permute-start.14) | collective-permute-done | bytes 196640 | tf_op jit(solution)/shard_map/ppermute | solution.py:557
  160.1 3.9 %collective-permute-start.19 = (bf16[2,4,1,1536]{3,2,1,0:T(2,128)(2,1)S(1)}, bf16[2,4,1,1536]{3,2,1,0:T(2,128)(2,1)S(1)}, u32[]{:S(2)}, u32[]{:S(2)}) collective-permute-start(bf16[2,4,1,1536]{3,2,1,0:T(2,128)(2,1)S(1)} %get-tuple-element.85), channel_id=1, source_target_pairs={{1,0},{2,1},{3,2},{4,3},{5,4},{6,5},{7,6},{8,7},{9,8},{10,9},{11,1... | collective-permute-start | bytes 73736 | tf_op jit(solution)/shard_map/ppermute | solution.py:548
  164.1 2.5 %collective-permute-done.18.low_ref = bf16[2,4,1,1536]{3,2,1,0:T(2,128)(2,1)S(1)} collective-permute-done((bf16[2,4,1,1536]{3,2,1,0:T(2,128)(2,1)S(1)}, bf16[2,4,1,1536]{3,2,1,0:T(2,128)(2,1)S(1)}, u32[]{:S(2)}, u32[]{:S(2)}) %collective-permute-start.18) | collective-permute-done | bytes 24608 | tf_op jit(solution)/shard_map/ppermute | solution.py:548
  168.6 5.3 %collective-permute-start.23 = (bf16[384,768]{1,0:T(8,128)(2,1)S(1)}, bf16[384,768]{1,0:T(8,128)(2,1)S(1)}, u32[]{:S(2)}, u32[]{:S(2)}) collective-permute-start(bf16[384,768]{1,0:T(8,128)(2,1)S(1)} %constant_dynamic-update-slice_fusion.6.refs_1_), channel_id=1, source_target_pairs={{0,4},{4,0},{8,12},{12,8},{16,20},{20,16},{24,28},{28,24},{1,5},{5... | collective-permute-start | bytes 1769480 | tf_op jit(solution)/shard_map/ppermute | solution.py:562
  176.4 4.4 %copy-done = bf16[5,768,1536]{2,1,0:T(8,128)(2,1)S(1)} copy-done((bf16[5,768,1536]{2,1,0:T(8,128)(2,1)S(1)}, bf16[5,768,1536]{2,1,0:T(8,128)(2,1)}, u32[]{:S(2)}) %copy-start) | copy-done | bytes 11796504
  180.8 4.2 %encoder_backward.1 = bf16[256,768]{1,0:T(8,128)(2,1)S(1)} custom-call(bf16[2,4,32,1536]{3,2,1,0:T(8,128)(2,1)S(1)} %get-tuple-element.83.d_ref, bf16[2,4,1,1536]{3,2,1,0:T(2,128)(2,1)S(1)} %collective-permute-done.18.low_ref, bf16[2,4,1,1536]{3,2,1,0:T(2,128)(2,1)S(1)} %collective-permute-done.19.high_ref, bf16[5,768,1536]{2,1,0:T(8,128)(2,1)S(1)} %copy-done, ...), custom_call_target="tpu_custom_call" | custom-call | flops 1000 | bytes 1000 | tf_op jit(solution)/shard_map/encoder_backward/pallas_call | solution.py:229
  185.0 4.8 %collective-permute-done.28.refs_3_ = bf16[384,768]{1,0:T(8,128)(2,1)} collective-permute-done((bf16[384,768]{1,0:T(8,128)(2,1)S(1)}, bf16[384,768]{1,0:T(8,128)(2,1)}, u32[]{:S(2)}, u32[]{:S(2)}) %collective-permute-start.28) | collective-permute-done | bytes 589856 | tf_op jit(solution)/shard_map/ppermute | solution.py:557
  201.0 6.8 %weight_outputs.1 = (f32[3,1536,384]{2,1,0:T(8,128)}, f32[384,1536]{1,0:T(8,128)}) custom-call(s32[2]{0:T(128)S(1)} %copy-done.22, bf16[384,768]{1,0:T(8,128)(2,1)S(1)} %constant_dynamic-update-slice_fusion.4.refs_0_, bf16[384,768]{1,0:T(8,128)(2,1)S(1)} %constant_dynamic-update-slice_fusion.6.refs_1_, bf16[384,768]{1,0:T(8,128)(2,1)} %collective-permute-done.27.refs_2_, ...), custom_call_target="tpu_custom_call" | custom-call | flops 1000 | bytes 1000 | tf_op jit(solution)/shard_map/weight_outputs/pallas_call | solution.py:522
  (145 shorter events, 65.0 us)
Async XLA Ops:
  7.2 38.4 %all-gather.6.cloned.1.call-start = ((), (), s32[]{:S(2)}) async-start(), calls=%async_computation.5 | async-start | bytes 1966080 | tf_op jit(solution)/shard_map/all_gather | solution.py:585
  7.9 75.8 %all-gather.4.cloned.1.call-start = ((), (), s32[]{:S(2)}) async-start(), calls=%async_computation.2 | async-start | bytes 1966080 | tf_op jit(solution)/shard_map/all_gather | solution.py:592
  9.1 9.3 %collective-permute-start.1 = (bf16[2,4,1,768]{3,2,1,0:T(2,128)(2,1)S(1)}, bf16[2,4,1,768]{3,2,1,0:T(2,128)(2,1)S(1)}, u32[]{:S(2)}, u32[]{:S(2)}) collective-permute-start(bf16[2,4,1,768]{3,2,1,0:T(2,128)(2,1)S(1)} %get-tuple-element.114), channel_id=1, source_target_pairs={{1,0},{2,1},{3,2},{4,3},{5,4},{6,5},{7,6},{8,7},{9,8},{10,9},{11,1... | collective-permute-start | bytes 36872 | tf_op jit(solution)/shard_map/ppermute | solution.py:548
  39.6 99.4 %reduce-scatter.5.cloned.1.call-start = ((), (), s32[]{:S(2)}) async-start(), calls=%async_computation.4 | async-start | bytes 1966080 | tf_op jit(solution)/shard_map/reduce_scatter | solution.py:620
  47.4 13.0 %collective-permute-start.7 = (bf16[4,32,1536]{2,1,0:T(8,128)(2,1)S(1)}, bf16[4,32,1536]{2,1,0:T(8,128)(2,1)S(1)}, u32[]{:S(2)}, u32[]{:S(2)}) collective-permute-start(bf16[4,32,1536]{2,1,0:T(8,128)(2,1)S(1)} %get-tuple-element.107), channel_id=1, source_target_pairs={{0,24},{4,28},{8,16},{12,20},{16,8},{20,12},{24,0},{28,4},{1,25},{... | collective-permute-start | bytes 1179656 | tf_op jit(solution)/shard_map/ppermute | solution.py:557
  48.9 19.0 %collective-permute-start.6 = (bf16[4,32,1536]{2,1,0:T(8,128)(2,1)S(1)}, bf16[4,32,1536]{2,1,0:T(8,128)(2,1)S(1)}, u32[]{:S(2)}, u32[]{:S(2)}) collective-permute-start(bf16[4,32,1536]{2,1,0:T(8,128)(2,1)S(1)} %get-tuple-element.108), channel_id=1, source_target_pairs={{0,8},{4,12},{8,0},{12,4},{16,24},{20,28},{24,16},{28,20},{1,9},{5... | collective-permute-start | bytes 1179656 | tf_op jit(solution)/shard_map/ppermute | solution.py:557
  50.4 17.5 %collective-permute-start.5 = (bf16[4,32,1536]{2,1,0:T(8,128)(2,1)S(1)}, bf16[4,32,1536]{2,1,0:T(8,128)(2,1)S(1)}, u32[]{:S(2)}, u32[]{:S(2)}) collective-permute-start(bf16[4,32,1536]{2,1,0:T(8,128)(2,1)S(1)} %get-tuple-element.109), channel_id=1, source_target_pairs={{0,16},{4,20},{8,24},{12,28},{16,0},{20,4},{24,8},{28,12},{1,17},{... | collective-permute-start | bytes 1179656 | tf_op jit(solution)/shard_map/ppermute | solution.py:557
  68.3 15.4 %collective-permute-start.9 = (bf16[512,1536]{1,0:T(8,128)(2,1)S(1)}, bf16[512,1536]{1,0:T(8,128)(2,1)}, u32[]{:S(2)}, u32[]{:S(2)}) collective-permute-start(bf16[512,1536]{1,0:T(8,128)(2,1)S(1)} %bitcast.45), channel_id=1, source_target_pairs={{0,4},{4,0},{8,12},{12,8},{16,20},{20,16},{24,28},{28,24},{1,5},{5... | collective-permute-start | bytes 4718600 | tf_op jit(solution)/shard_map/ppermute | solution.py:562
  70.5 13.2 %collective-permute-start.8 = (bf16[512,256]{1,0:T(8,128)(2,1)S(1)}, bf16[512,256]{1,0:T(8,128)(2,1)S(1)}, u32[]{:S(2)}, u32[]{:S(2)}) collective-permute-start(bf16[512,256]{1,0:T(8,128)(2,1)S(1)} %get-tuple-element.54), channel_id=1, source_target_pairs={{0,4},{4,0},{8,12},{12,8},{16,20},{20,16},{24,28},{28,24},{1,5},{5... | collective-permute-start | bytes 786440 | tf_op jit(solution)/shard_map/ppermute | solution.py:562
  83.7 7.9 %collective-permute-start.11 = (bf16[512,1536]{1,0:T(8,128)(2,1)}, bf16[512,1536]{1,0:T(8,128)(2,1)S(1)}, u32[]{:S(2)}, u32[]{:S(2)}) collective-permute-start(bf16[512,1536]{1,0:T(8,128)(2,1)} %all-gather.4.cloned.1.call-done.x_ref.xa_ref), channel_id=1, source_target_pairs={{0,4},{4,0},{8,12},{12,8},{16,20},{20,16},{24,28},{28,24},{1,5},{5... | collective-permute-start | bytes 4718600 | tf_op jit(solution)/shard_map/ppermute | solution.py:562
  104.6 85.8 %reduce-scatter.3.cloned.1.call-start = ((), (), s32[]{:S(2)}) async-start(), calls=%async_computation.3 | async-start | bytes 1966080 | tf_op jit(solution)/shard_map/reduce_scatter | solution.py:635
  116.5 34.1 %collective-permute-start.15 = (bf16[768,384]{1,0:T(8,128)(2,1)}, bf16[768,384]{1,0:T(8,128)(2,1)S(1)}, u32[]{:S(2)}, u32[]{:S(2)}) collective-permute-start(bf16[768,384]{1,0:T(8,128)(2,1)} %get-tuple-element.79), channel_id=1, source_target_pairs={{0,8},{4,12},{8,0},{12,4},{16,24},{20,28},{24,16},{28,20},{1,9},{5... | collective-permute-start | bytes 1769480 | tf_op jit(solution)/shard_map/ppermute | solution.py:557
  117.1 33.5 %collective-permute-start.16 = (bf16[768,384]{1,0:T(8,128)(2,1)}, bf16[768,384]{1,0:T(8,128)(2,1)S(1)}, u32[]{:S(2)}, u32[]{:S(2)}) collective-permute-start(bf16[768,384]{1,0:T(8,128)(2,1)} %get-tuple-element.80), channel_id=1, source_target_pairs={{0,16},{4,20},{8,24},{12,28},{16,0},{20,4},{24,8},{28,12},{1,17},{... | collective-permute-start | bytes 1769480 | tf_op jit(solution)/shard_map/ppermute | solution.py:557
  118.6 32.0 %collective-permute-start.17 = (bf16[768,384]{1,0:T(8,128)(2,1)}, bf16[768,384]{1,0:T(8,128)(2,1)S(1)}, u32[]{:S(2)}, u32[]{:S(2)}) collective-permute-start(bf16[768,384]{1,0:T(8,128)(2,1)} %get-tuple-element.81), channel_id=1, source_target_pairs={{0,24},{4,28},{8,16},{12,20},{16,8},{20,12},{24,0},{28,4},{1,25},{... | collective-permute-start | bytes 1769480 | tf_op jit(solution)/shard_map/ppermute | solution.py:557
  140.0 9.1 %collective-permute-start.13 = (bf16[2,32,1536]{2,1,0:T(8,128)(2,1)S(1)}, bf16[2,32,1536]{2,1,0:T(8,128)(2,1)S(1)}, u32[]{:S(2)}, u32[]{:S(2)}) collective-permute-start(bf16[2,32,1536]{2,1,0:T(8,128)(2,1)S(1)} %slice_bitcast_fusion.refs_4_), channel_id=1, source_target_pairs={{0,8},{4,12},{8,0},{12,4},{16,24},{20,28},{24,16},{28,20},{1,9},{5... | collective-permute-start | bytes 589832 | tf_op jit(solution)/shard_map/ppermute | solution.py:557
  149.1 7.9 %collective-permute-start.14 = (bf16[2,32,1536]{2,1,0:T(8,128)(2,1)S(1)}, bf16[2,32,1536]{2,1,0:T(8,128)(2,1)S(1)}, u32[]{:S(2)}, u32[]{:S(2)}) collective-permute-start(bf16[2,32,1536]{2,1,0:T(8,128)(2,1)S(1)} %pad_maximum_fusion.1), channel_id=1, source_target_pairs={{0,16},{4,20},{8,24},{12,28},{16,0},{20,4},{24,8},{28,12},{1,17},{... | collective-permute-start | bytes 589832 | tf_op jit(solution)/shard_map/ppermute | solution.py:557
  151.1 13.0 %collective-permute-start.22 = (bf16[192,768]{1,0:T(8,128)(2,1)S(1)}, bf16[192,768]{1,0:T(8,128)(2,1)S(1)}, u32[]{:S(2)}, u32[]{:S(2)}) collective-permute-start(bf16[192,768]{1,0:T(8,128)(2,1)S(1)} %get-tuple-element.87), channel_id=1, source_target_pairs={{0,16},{4,20},{8,24},{12,28},{16,0},{20,4},{24,8},{28,12},{1,17},{... | collective-permute-start | bytes 884744 | tf_op jit(solution)/shard_map/ppermute | solution.py:557
  151.7 16.8 %collective-permute-start.20 = (bf16[192,768]{1,0:T(8,128)(2,1)S(1)}, bf16[192,768]{1,0:T(8,128)(2,1)S(1)}, u32[]{:S(2)}, u32[]{:S(2)}) collective-permute-start(bf16[192,768]{1,0:T(8,128)(2,1)S(1)} %get-tuple-element.82.refs_4_), channel_id=1, source_target_pairs={{0,8},{4,12},{8,0},{12,4},{16,24},{20,28},{24,16},{28,20},{1,9},{5... | collective-permute-start | bytes 884744 | tf_op jit(solution)/shard_map/ppermute | solution.py:557
  158.2 8.4 %collective-permute-start.18 = (bf16[2,4,1,1536]{3,2,1,0:T(2,128)(2,1)S(1)}, bf16[2,4,1,1536]{3,2,1,0:T(2,128)(2,1)S(1)}, u32[]{:S(2)}, u32[]{:S(2)}) collective-permute-start(bf16[2,4,1,1536]{3,2,1,0:T(2,128)(2,1)S(1)} %get-tuple-element.84), channel_id=1, source_target_pairs={{0,1},{1,2},{2,3},{3,4},{4,5},{5,6},{6,7},{7,8},{8,9},{9,10},{10,1... | collective-permute-start | bytes 73736 | tf_op jit(solution)/shard_map/ppermute | solution.py:548
  160.1 8.4 %collective-permute-start.19 = (bf16[2,4,1,1536]{3,2,1,0:T(2,128)(2,1)S(1)}, bf16[2,4,1,1536]{3,2,1,0:T(2,128)(2,1)S(1)}, u32[]{:S(2)}, u32[]{:S(2)}) collective-permute-start(bf16[2,4,1,1536]{3,2,1,0:T(2,128)(2,1)S(1)} %get-tuple-element.85), channel_id=1, source_target_pairs={{1,0},{2,1},{3,2},{4,3},{5,4},{6,5},{7,6},{8,7},{9,8},{10,9},{11,1... | collective-permute-start | bytes 73736 | tf_op jit(solution)/shard_map/ppermute | solution.py:548
  174.0 15.8 %collective-permute-start.28 = (bf16[384,768]{1,0:T(8,128)(2,1)S(1)}, bf16[384,768]{1,0:T(8,128)(2,1)}, u32[]{:S(2)}, u32[]{:S(2)}) collective-permute-start(bf16[384,768]{1,0:T(8,128)(2,1)S(1)} %constant_dynamic-update-slice_fusion.6.refs_1_), channel_id=1, source_target_pairs={{0,8},{4,12},{8,0},{12,4},{16,24},{20,28},{24,16},{28,20},{1,9},{5... | collective-permute-start | bytes 1769480 | tf_op jit(solution)/shard_map/ppermute | solution.py:557
  174.1 15.8 %collective-permute-start.27 = (bf16[384,768]{1,0:T(8,128)(2,1)S(1)}, bf16[384,768]{1,0:T(8,128)(2,1)}, u32[]{:S(2)}, u32[]{:S(2)}) collective-permute-start(bf16[384,768]{1,0:T(8,128)(2,1)S(1)} %constant_dynamic-update-slice_fusion.4.refs_0_), channel_id=1, source_target_pairs={{0,16},{4,20},{8,24},{12,28},{16,0},{20,4},{24,8},{28,12},{1,17},{... | collective-permute-start | bytes 1769480 | tf_op jit(solution)/shard_map/ppermute | solution.py:557
  189.9 11.2 %collective-permute-start.29 = (bf16[384,768]{1,0:T(8,128)(2,1)}, bf16[384,768]{1,0:T(8,128)(2,1)}, u32[]{:S(2)}, u32[]{:S(2)}) collective-permute-start(bf16[384,768]{1,0:T(8,128)(2,1)} %collective-permute-done.27.refs_2_), channel_id=1, source_target_pairs={{0,4},{4,0},{8,12},{12,8},{16,20},{20,16},{24,28},{28,24},{1,5},{5... | collective-permute-start | bytes 1769480 | tf_op jit(solution)/shard_map/ppermute | solution.py:562
  189.9 11.2 %collective-permute-start.30 = (bf16[384,768]{1,0:T(8,128)(2,1)}, bf16[384,768]{1,0:T(8,128)(2,1)}, u32[]{:S(2)}, u32[]{:S(2)}) collective-permute-start(bf16[384,768]{1,0:T(8,128)(2,1)} %collective-permute-done.28.refs_3_), channel_id=1, source_target_pairs={{0,4},{4,0},{8,12},{12,8},{16,20},{20,16},{24,28},{28,24},{1,5},{5... | collective-permute-start | bytes 1769480 | tf_op jit(solution)/shard_map/ppermute | solution.py:562
  (39 other events, 210.9 us)
Sparse Core Ops, SparseCore 0:
  9.6 35.9 all-gather.5
  47.7 35.9 all-gather.3
  104.7 34.2 reduce-scatter.4
  141.7 36.3 reduce-scatter.2

commit v10 on v9

--- a/solution.py
+++ b/solution.py
@@ -462,10 +462,13 @@
     for ref in part_refs[1:]:
         total = total + ref[...].astype(F32)
     turned = total[:split].T.astype(BF)
+    quarter = DH // 2
     for part, out_ref in enumerate(out_refs):
-        rows = slice(part * DH, (part + 1) * DH)
-        out_ref[:, :split] = turned[rows]
-        out_ref[:, split:] = total[split:, rows].astype(BF)
+        out_ref[:, :split] = turned[part * DH : (part + 1) * DH]
+        first = split + part * quarter
+        piece = total[first : first + quarter].astype(BF)
+        out_ref[:quarter, split:] = piece[:, :DH]
+        out_ref[quarter:, split:] = piece[:, DH:]
 
 
 def weight_sum(parts, *deps):
@@ -481,63 +484,66 @@
 
 
 def unpack_kernel(at_ref, *refs):
-    qkv_ref, out_ref = refs[-2:]
+    qkv_ref, out_ref, token_ref = refs[-3:]
     step = pl.program_id(0)
     split = 3 * DH
-    for turn in range(4):
-
-        @pl.when(step == turn)
+    quarter = DH // 2
+    token_ref[...] = jnp.zeros_like(token_ref)
+    for half in range(2):
+
+        @pl.when(step // 2 == half)
         def _():
-            both = []
-            for near_a, near_b, far_a, far_b in (refs[:4], refs[4:8]):
-                first = near_a if turn < 2 else far_a
-                second = near_b if turn % 2 == 0 else far_b
-                both.append((first[...].astype(F32), second[...].astype(F32)))
+            mine = refs[half][...].astype(F32)
+            other = refs[2 + half][...].astype(F32)
             swapped = at_ref[1] != 0
-            for part in range(2):
-                mine, other = both[0][part], both[1][part]
-                low = jnp.where(swapped, other, mine)
-                high = jnp.where(swapped, mine, other)
-                rows = slice(part * DH, (part + 1) * DH)
-                for i in range(3):
-                    columns = slice(i * DH, (i + 1) * DH)
-                    qkv_ref[i, rows, :] = jnp.concatenate(
-                        [low[:, columns], high[:, columns]], axis=1
-                    )
-                out_ref[:DH, rows] = low[:, split:]
-                out_ref[DH:, rows] = high[:, split:]
-
-
-def unpack_weights(at, mine, other):
+            low = jnp.where(swapped, other, mine)
+            high = jnp.where(swapped, mine, other)
+            for i in range(3):
+                columns = slice(i * DH, (i + 1) * DH)
+                qkv_ref[i] = jnp.concatenate([low[:, columns], high[:, columns]], axis=1)
+            for head, value in enumerate((low, high)):
+                folded = [value[:quarter, split:], value[quarter:, split:]]
+                out_ref[head, 0] = jnp.concatenate(folded, axis=1)
+
+
+def unpack_weights(at, mine, other, far, before=()):
     rows, full = mine[0].shape
     half = rows // 2
     width = 4 * rows
-    local = 2 * DH
+
+    def chunk(t, at):
+        if far:
+            return at[0] ^ jnp.where(t < 2, t + 2, 2 * t - 3)
+        return at[0] ^ jnp.where(t < 2, t, 2 * t - 4)
+
     specs = [
-        pl.BlockSpec((half, full), lambda j, at: (jnp.minimum(j, 1), 0)),
-        pl.BlockSpec((half, full), lambda j, at: (j // 2, 0)),
-        pl.BlockSpec((half, full), lambda j, at: (jnp.maximum(j - 2, 0), 0)),
-        pl.BlockSpec((half, full), lambda j, at: (j // 2, 0)),
+        pl.BlockSpec((half, full), lambda t, at: (jnp.minimum(t, 1), 0)),
+        pl.BlockSpec((half, full), lambda t, at: (jnp.maximum(t - 2, 0), 0)),
     ]
     return pl.pallas_call(
         unpack_kernel,
         grid_spec=pltpu.PrefetchScalarGridSpec(
             num_scalar_prefetch=1,
             grid=(4,),
-            in_specs=specs * 2,
+            in_specs=specs * 2 + spare(before),
             out_specs=[
-                pl.BlockSpec((3, rows, local), lambda j, at: (0, at[0] ^ j, 0)),
-                pl.BlockSpec((local, rows), lambda j, at: (0, at[0] ^ j)),
+                pl.BlockSpec((3, half, 2 * DH), lambda t, at: (0, 2 * chunk(t, at) + t // 2, 0)),
+                pl.BlockSpec(
+                    (2, 1, DH // 2, rows), lambda t, at: (0, t // 2, 0, chunk(t, at))
+                ),
+                pl.BlockSpec(TOKEN.shape, lambda t, at: (0, 0)),
             ],
         ),
         out_shape=[
-            jax.ShapeDtypeStruct((3, width, local), F32),
-            jax.ShapeDtypeStruct((local, width), F32),
+            jax.ShapeDtypeStruct((3, width, 2 * DH), F32),
+            jax.ShapeDtypeStruct((2, 2, DH // 2, width), F32),
+            TOKEN,
         ],
+        input_output_aliases={5 + i: i for i in range(len(before))},
         compiler_params=params(),
         cost_estimate=COST,
-        name="weight_outputs",
-    )(at, *mine, *other)
+        name="weight_outputs_far" if far else "weight_outputs_near",
+    )(at, *mine, *other, *before)
 
 
 def neighbour_edges(first, last):
@@ -646,26 +652,26 @@
 
     got_a = trade_chip(half_a, 1, heads)
     got_b = trade_chip(half_b, 2, heads)
-    near_a = jnp.concatenate([half_a, after(got_a, low, high)], axis=0)
-    near_b = jnp.concatenate([half_b, after(got_b, low, high)], axis=0)
+    near_a = jnp.concatenate([half_a, after(got_a, low)], axis=0)
+    near_b = jnp.concatenate([half_b, after(got_b, low)], axis=0)
     far_a = trade_chip(near_a, 2, heads)
     far_b = trade_chip(near_b, 1, heads)
     near_other = [swap_heads(near_a), swap_heads(near_b)]
-    grad_input = conv_back(d_conv, low, high, conv_weight, *near_other)
-    far_other = [swap_heads(after(x, grad_input)) for x in (far_a, far_b)]
-    grad_w_qkv, grad_w_out = unpack_weights(
-        at, [near_a, near_b, far_a, far_b], near_other + far_other
-    )
+    *outputs, token = unpack_weights(at, [near_a, near_b], near_other, False)
+    grad_input = conv_back(d_conv, low, high, conv_weight, token)
 
     head_sum = after(head_sum, grad_input)
-    head_sum = to_chips([head_sum[order.index(j)] for j in range(seqs)])
+    head_sum = [head_sum[order.index(j)] for j in range(seqs)]
+    far_other = [swap_heads(after(x, *head_sum)) for x in (far_a, far_b)]
+    grad_w_qkv, grad_w_out, _ = unpack_weights(at, [far_a, far_b], far_other, True, outputs)
+    head_sum = to_chips(head_sum)
     mixed = mixed_call(at, head_sum, skip)
     grad_input = jnp.transpose(grad_input.reshape(2, seqs, rows, -1), (2, 0, 1, 3))
     return (
         jnp.transpose(mixed, (1, 0, 2)),
         grad_input.reshape(enc_in.shape),
         grad_w_qkv,
-        grad_w_out,
+        grad_w_out.reshape(local, width),
     )
 
 

time: 216 us -> 211 us (0.977)
  starting transfers between devices: 39.1 us -> 35.2 us
  waiting for transfers between devices: 77.4 us -> 74.4 us
    ppermute x9, starting transfers between devices: 6.92 us -> 3.11 us  [swap_heads(): lax.ppermute(x, 'seq', [(s, s + 1 - 2 * (s % 2)) for s in range(count)])]
    ppermute x18, waiting for transfers between devices: 41.9 us -> 38.2 us  [trade_chip(): return lax.ppermute(x, 'seq', [(s, s ^ bit * heads) for s in range(count)])]
    ppermute x2, waiting for transfers between devices: 2.47 us -> 5.18 us  [neighbour_edges(): lax.ppermute(last, axes, forward)]
    pallas_call x1 -> x2, Pallas kernels: 6.84 us -> 6.82 us  [unpack_weights(): pl.pallas_call(unpack_kernel, grid_spec=pltpu.PrefetchScalarGridSpec(num_...]
  transfers between devices with their start and end apart: 35 -> 35, of which waited for: 19 -> 16; matrix products, arithmetic and copies ran while one was open for 5% -> 5% of each run, Pallas kernels for 17% -> 19%
where the time goes in v10:
time: 211 us; the launch traced here: 207 us
  waiting for transfers between devices  74.4 us (35%)
  Pallas kernels  53.1 us (25%)
  starting transfers between devices  35.2 us (17%)
  local copies, waits for them, and re-layouts  29.5 us (14%)
  between operations  14.3 us (7%)
    ppermute x18, waiting for transfers between devices, trade_chip(): return lax.ppermute(x, 'seq', [(s, s ^ bit * heads) for s in range(count)])  38.2 us
    unnamed x62, local copies, waits for them, and re-layouts  21.1 us
    ppermute x18, starting transfers between devices, trade_chip(): return lax.ppermute(x, 'seq', [(s, s ^ bit * heads) for s in range(count)])  19.8 us
    reduce_scatter x1, waiting for transfers between devices, unit_body(): lax.psum_scatter(d_term.reshape(shape), 'head', scatter_dimension=0, tile...  19.1 us
    pallas_call x1, Pallas kernels, encoder(): pl.pallas_call(conv_kernel, grid=(width // tile,), in_specs=[SCALARS, who...  10.1 us
    pallas_call x1, Pallas kernels, weight_gradients(): pl.pallas_call(weight_kernel, grid_spec=pltpu.PrefetchScalarGridSpec(num_...  8.74 us
    ppermute x2, starting transfers between devices, neighbour_edges(): lax.ppermute(last, axes, forward)  6.92 us
    pallas_call x2, Pallas kernels, unpack_weights(): pl.pallas_call(unpack_kernel, grid_spec=pltpu.PrefetchScalarGridSpec(num_...  6.82 us
  transfers between devices with their start and end apart: 35, of which 16 were waited for; matrix products, arithmetic and copies ran while one was open for 5% of the time, Pallas kernels for 19%

profile of v10, /device:TPU:26, one launch (start us, length us, event | category | flops | bytes accessed | tf_op | source)
XLA Modules:
  0.0 207.3 jit_solution(12983001926342879473)
XLA Ops:
  9.1 2.4 %collective-permute-start.1 = (bf16[2,4,1,768]{3,2,1,0:T(2,128)(2,1)S(1)}, bf16[2,4,1,768]{3,2,1,0:T(2,128)(2,1)S(1)}, u32[]{:S(2)}, u32[]{:S(2)}) collective-permute-start(bf16[2,4,1,768]{3,2,1,0:T(2,128)(2,1)S(1)} %get-tuple-element.120), channel_id=1, source_target_pairs={{1,0},{2,1},{3,2},{4,3},{5,4},{6,5},{7,6},{8,7},{9,8},{10,9},{11,1... | collective-permute-start | bytes 36872 | tf_op jit(solution)/shard_map/ppermute | solution.py:554
  11.4 5.0 %collective-permute-start = (bf16[2,4,1,768]{3,2,1,0:T(2,128)(2,1)S(1)}, bf16[2,4,1,768]{3,2,1,0:T(2,128)(2,1)S(1)}, u32[]{:S(2)}, u32[]{:S(2)}) collective-permute-start(bf16[2,4,1,768]{3,2,1,0:T(2,128)(2,1)S(1)} %get-tuple-element.121), channel_id=1, source_target_pairs={{0,1},{1,2},{2,3},{3,4},{4,5},{5,6},{6,7},{7,8},{8,9},{9,10},{10,1... | collective-permute-start | bytes 36872 | tf_op jit(solution)/shard_map/ppermute | solution.py:554
  19.6 10.1 %encoder_forward.1 = (bf16[4,32,1536]{2,1,0:T(8,128)(2,1)}, f32[2,4,32,1536]{3,2,1,0:T(8,128)}, bf16[32,1536]{1,0:T(8,128)(2,1)}, bf16[32,1536]{1,0:T(8,128)(2,1...) custom-call(s32[2]{0:T(128)} %pad_add_fusion.at_ref, bf16[2,4,32,768]{3,2,1,0:T(8,128)(2,1)} %bitcast.61, ...), custom_call_target="tpu_custom_call" | custom-call | flops 1000 | bytes 1000 | tf_op jit(solution)/shard_map/encoder_forward/pallas_call | solution.py:111
  35.1 2.1 %collective-permute-done.3 = bf16[32,1536]{1,0:T(8,128)(2,1)S(1)} collective-permute-done((bf16[32,1536]{1,0:T(8,128)(2,1)}, bf16[32,1536]{1,0:T(8,128)(2,1)S(1)}, u32[]{:S(2)}, u32[]{:S(2)}) %collective-permute-start.3) | collective-permute-done | bytes 98336 | tf_op jit(solution)/shard_map/ppermute | solution.py:563
  39.8 5.8 %all-gather.6.cloned.1.call-done = bf16[128,4,1536]{2,1,0:T(4,128)(2,1)} async-done(((bf16[32,4,1536]{2,1,0:T(4,128)(2,1)}), bf16[128,4,1536]{2,1,0:T(4,128)(2,1)}) %all-gather.6.cloned.1.call-update) | async-done | bytes 1572880 | tf_op jit(solution)/shard_map/all_gather | solution.py:591
  51.0 9.4 %collective-permute-done.7 = bf16[4,32,1536]{2,1,0:T(8,128)(2,1)S(1)} collective-permute-done((bf16[4,32,1536]{2,1,0:T(8,128)(2,1)S(1)}, bf16[4,32,1536]{2,1,0:T(8,128)(2,1)S(1)}, u32[]{:S(2)}, u32[]{:S(2)}) %collective-permute-start.7) | collective-permute-done | bytes 393248 | tf_op jit(solution)/shard_map/ppermute | solution.py:563
  60.4 7.5 %collective-permute-done.6 = bf16[4,32,1536]{2,1,0:T(8,128)(2,1)S(1)} collective-permute-done((bf16[4,32,1536]{2,1,0:T(8,128)(2,1)S(1)}, bf16[4,32,1536]{2,1,0:T(8,128)(2,1)S(1)}, u32[]{:S(2)}, u32[]{:S(2)}) %collective-permute-start.6) | collective-permute-done | bytes 393248 | tf_op jit(solution)/shard_map/ppermute | solution.py:563
  70.6 2.0 copy-done.9
  72.6 3.9 %pack_weights.1 = (bf16[2,1536,576]{2,1,0:T(8,128)(2,1)S(1)}, bf16[2,576,1536]{2,1,0:T(8,128)(2,1)S(1)}, f32[8,128]{1,0:T(8,128)S(1)}) custom-call(bf16[3,1536,384]{2,1,0:T(8,128)(2,1)S(1)} %copy-done.9), custom_call_target="tpu_custom_call" | custom-call | flops 1000 | bytes 1000 | tf_op jit(solution)/shard_map/pack_weights/pallas_call | solution.py:265
  81.6 2.1 %all-gather.4.cloned.1.call-done.x_ref.xa_ref = bf16[512,1536]{1,0:T(8,128)(2,1)} async-done(((bf16[128,1536]{1,0:T(8,128)(2,1)}), bf16[512,1536]{1,0:T(8,128)(2,1)}) %all-gather.4.cloned.1.call-update) | async-done | bytes 1572880 | tf_op jit(solution)/shard_map/all_gather | solution.py:598
  83.8 2.1 %copy-done.3 = bf16[2,1536,576]{2,1,0:T(8,128)(2,1)S(1)} copy-done((bf16[2,1536,576]{2,1,0:T(8,128)(2,1)S(1)}, bf16[2,1536,576]{2,1,0:T(8,128)(2,1)}, u32[]{:S(2)}) %copy-start.3) | copy-done | bytes 3538968
  91.6 6.5 %attention.1 = (bf16[512,768]{1,0:T(8,128)(2,1)S(1)}, bf16[512,768]{1,0:T(8,128)(2,1)S(1)}) custom-call(bf16[512,640]{1,0:T(8,128)(2,1)S(1)} %get-tuple-element.67.qa_ref, bf16[512,640]{1,0:T(8,128)(2,1)S(1)} %collective-permute-done.10.qb_ref, bf16[512,256]{1,0:T(8,128)(2,1)S(1)} %copy-done.20, bf16[512,256]{1,0:T(8,128)(2,1)S(1)} %copy-done.18, ...), custom_call_target="tpu_custom_call" | custom-call | flops 1000 | bytes 1000 | tf_op jit(solution)/shard_map/attention/pallas_call | solution.py:366
  98.4 2.1 %collective-permute-done.12.b_ref = bf16[512,768]{1,0:T(8,128)(2,1)S(1)} collective-permute-done((bf16[512,768]{1,0:T(8,128)(2,1)S(1)}, bf16[512,768]{1,0:T(8,128)(2,1)S(1)}, u32[]{:S(2)}, u32[]{:S(2)}) %collective-permute-start.12) | collective-permute-done | bytes 786464 | tf_op jit(solution)/shard_map/ppermute | solution.py:568
  100.5 4.0 %d_term.1 = bf16[512,1536]{1,0:T(8,128)(2,1)} custom-call(s32[1]{0:T(128)} %bitcast.1.head_ref, bf16[512,768]{1,0:T(8,128)(2,1)S(1)} %get-tuple-element.74.a_ref.ra_ref, bf16[512,768]{1,0:T(8,128)(2,1)S(1)} %collective-permute-done.12.b_ref, bf16[2,576,1536]{2,1,0:T(8,128)(2,1)S(1)} %copy-done.11), custom_call_target="tpu_custom_call" | custom-call | flops 1000 | bytes 1000 | tf_op jit(solution)/shard_map/d_term/pallas_call | solution.py:393
  107.6 8.7 %weight_gradients.1 = (bf16[768,384]{1,0:T(8,128)(2,1)}, bf16[768,384]{1,0:T(8,128)(2,1)}, bf16[768,384]{1,0:T(8,128)(2,1)}, bf16[768,384]{1,0:T(8,128)(2,1)}) custom-call(s32[1]{0:T(128)} %bitcast.at_ref, bf16[512,1536]{1,0:T(8,128)(2,1)} %all-gather.4.cloned.1.call-done.x_ref.xa_ref, bf16[512,1536]{1,0:T(8,128)(2,1)} %copy-done.8, ...), custom_call_target="tpu_custom_call" | custom-call | flops 1000 | bytes 1000 | tf_op jit(solution)/shard_map/weight_gradients/pallas_call | solution.py:442
  119.8 19.1 %reduce-scatter.5.cloned.1.call-done = bf16[1,4,32,1536]{3,2,1,0:T(8,128)(2,1)} async-done(((bf16[4,4,32,1536]{3,2,1,0:T(8,128)(2,1)}), bf16[1,4,32,1536]{3,2,1,0:T(8,128)(2,1)}) %reduce-scatter.5.cloned.1.call-update) | async-done | bytes 393232 | tf_op jit(solution)/shard_map/reduce_scatter | solution.py:626
  141.5 7.4 %collective-permute-done.13.near_ref = bf16[2,32,1536]{2,1,0:T(8,128)(2,1)S(1)} collective-permute-done((bf16[2,32,1536]{2,1,0:T(8,128)(2,1)S(1)}, bf16[2,32,1536]{2,1,0:T(8,128)(2,1)S(1)}, u32[]{:S(2)}, u32[]{:S(2)}) %collective-permute-start.13) | collective-permute-done | bytes 196640 | tf_op jit(solution)/shard_map/ppermute | solution.py:563
  152.2 4.6 %collective-permute-done.14.far_ref = bf16[2,32,1536]{2,1,0:T(8,128)(2,1)S(1)} collective-permute-done((bf16[2,32,1536]{2,1,0:T(8,128)(2,1)S(1)}, bf16[2,32,1536]{2,1,0:T(8,128)(2,1)S(1)}, u32[]{:S(2)}, u32[]{:S(2)}) %collective-permute-start.14) | collective-permute-done | bytes 196640 | tf_op jit(solution)/shard_map/ppermute | solution.py:563
  161.5 5.2 %collective-permute-done.18.low_ref = bf16[2,4,1,1536]{3,2,1,0:T(2,128)(2,1)S(1)} collective-permute-done((bf16[2,4,1,1536]{3,2,1,0:T(2,128)(2,1)S(1)}, bf16[2,4,1,1536]{3,2,1,0:T(2,128)(2,1)S(1)}, u32[]{:S(2)}, u32[]{:S(2)}) %collective-permute-start.18) | collective-permute-done | bytes 24608 | tf_op jit(solution)/shard_map/ppermute | solution.py:554
  169.6 2.7 %collective-permute-start.19 = (bf16[2,4,1,1536]{3,2,1,0:T(2,128)(2,1)S(1)}, bf16[2,4,1,1536]{3,2,1,0:T(2,128)(2,1)S(1)}, u32[]{:S(2)}, u32[]{:S(2)}) collective-permute-start(bf16[2,4,1,1536]{3,2,1,0:T(2,128)(2,1)S(1)} %get-tuple-element.88), channel_id=1, source_target_pairs={{1,0},{2,1},{3,2},{4,3},{5,4},{6,5},{7,6},{8,7},{9,8},{10,9},{11,1... | collective-permute-start | bytes 73736 | tf_op jit(solution)/shard_map/ppermute | solution.py:554
  172.4 3.4 %weight_outputs_near.1 = (f32[3,1536,384]{2,1,0:T(8,128)}, f32[2,2,96,1536]{3,2,1,0:T(8,128)}, f32[8,128]{1,0:T(8,128)S(1)}) custom-call(s32[2]{0:T(128)S(1)} %copy-done.22, bf16[384,768]{1,0:T(8,128)(2,1)S(1)} %constant_dynamic-update-slice_fusion.4.refs_0_, bf16[384,768]{1,0:T(8,128)(2,1)S(1)} %constant_dynamic-update-slice_fusion.6.refs_1_, ...), custom_call_target="tpu_custom_call" | custom-call | flops 1000 | bytes 1000 | tf_op jit(solution)/shard_map/weight_outputs_near/pallas_call | solution.py:523
  176.9 4.3 %copy-done = bf16[5,768,1536]{2,1,0:T(8,128)(2,1)S(1)} copy-done((bf16[5,768,1536]{2,1,0:T(8,128)(2,1)S(1)}, bf16[5,768,1536]{2,1,0:T(8,128)(2,1)}, u32[]{:S(2)}) %copy-start) | copy-done | bytes 11796504
  181.3 4.2 %encoder_backward.1 = bf16[256,768]{1,0:T(8,128)(2,1)S(1)} custom-call(bf16[2,4,32,1536]{3,2,1,0:T(8,128)(2,1)S(1)} %get-tuple-element.86.d_ref, bf16[2,4,1,1536]{3,2,1,0:T(2,128)(2,1)S(1)} %collective-permute-done.18.low_ref, bf16[2,4,1,1536]{3,2,1,0:T(2,128)(2,1)S(1)} %collective-permute-done.19.high_ref, bf16[5,768,1536]{2,1,0:T(8,128)(2,1)S(1)} %copy-done, ...), custom_call_target="tpu_custom_call" | custom-call | flops 1000 | bytes 1000 | tf_op jit(solution)/shard_map/encoder_backward/pallas_call | solution.py:229
  197.4 3.4 %weight_outputs_far.1 = (f32[3,1536,384]{2,1,0:T(8,128)}, f32[2,2,96,1536]{3,2,1,0:T(8,128)}, f32[8,128]{1,0:T(8,128)}) custom-call(s32[2]{0:T(128)S(1)} %copy-done.22, bf16[384,768]{1,0:T(8,128)(2,1)S(1)} %collective-permute-done.27.refs_0_, bf16[384,768]{1,0:T(8,128)(2,1)S(1)} %collective-permute-done.28.refs_1_, ...), custom_call_target="tpu_custom_call", output_to_operand_aliasing={{0}: (5, {}), {1}: (6, {})} | custom-call | flops 1000 | bytes 1000 | tf_op jit(solution)/shard_map/weight_outputs_far/pallas_call | solution.py:523
  (146 shorter events, 64.7 us)
Async XLA Ops:
  7.2 38.4 %all-gather.6.cloned.1.call-start = ((), (), s32[]{:S(2)}) async-start(), calls=%async_computation.5 | async-start | bytes 1966080 | tf_op jit(solution)/shard_map/all_gather | solution.py:591
  7.9 75.8 %all-gather.4.cloned.1.call-start = ((), (), s32[]{:S(2)}) async-start(), calls=%async_computation.2 | async-start | bytes 1966080 | tf_op jit(solution)/shard_map/all_gather | solution.py:598
  9.1 9.3 %collective-permute-start.1 = (bf16[2,4,1,768]{3,2,1,0:T(2,128)(2,1)S(1)}, bf16[2,4,1,768]{3,2,1,0:T(2,128)(2,1)S(1)}, u32[]{:S(2)}, u32[]{:S(2)}) collective-permute-start(bf16[2,4,1,768]{3,2,1,0:T(2,128)(2,1)S(1)} %get-tuple-element.120), channel_id=1, source_target_pairs={{1,0},{2,1},{3,2},{4,3},{5,4},{6,5},{7,6},{8,7},{9,8},{10,9},{11,1... | collective-permute-start | bytes 36872 | tf_op jit(solution)/shard_map/ppermute | solution.py:554
  39.7 99.2 %reduce-scatter.5.cloned.1.call-start = ((), (), s32[]{:S(2)}) async-start(), calls=%async_computation.4 | async-start | bytes 1966080 | tf_op jit(solution)/shard_map/reduce_scatter | solution.py:626
  47.4 13.0 %collective-permute-start.7 = (bf16[4,32,1536]{2,1,0:T(8,128)(2,1)S(1)}, bf16[4,32,1536]{2,1,0:T(8,128)(2,1)S(1)}, u32[]{:S(2)}, u32[]{:S(2)}) collective-permute-start(bf16[4,32,1536]{2,1,0:T(8,128)(2,1)S(1)} %get-tuple-element.113), channel_id=1, source_target_pairs={{0,24},{4,28},{8,16},{12,20},{16,8},{20,12},{24,0},{28,4},{1,25},{... | collective-permute-start | bytes 1179656 | tf_op jit(solution)/shard_map/ppermute | solution.py:563
  48.9 19.0 %collective-permute-start.6 = (bf16[4,32,1536]{2,1,0:T(8,128)(2,1)S(1)}, bf16[4,32,1536]{2,1,0:T(8,128)(2,1)S(1)}, u32[]{:S(2)}, u32[]{:S(2)}) collective-permute-start(bf16[4,32,1536]{2,1,0:T(8,128)(2,1)S(1)} %get-tuple-element.114), channel_id=1, source_target_pairs={{0,8},{4,12},{8,0},{12,4},{16,24},{20,28},{24,16},{28,20},{1,9},{5... | collective-permute-start | bytes 1179656 | tf_op jit(solution)/shard_map/ppermute | solution.py:563
  50.4 17.5 %collective-permute-start.5 = (bf16[4,32,1536]{2,1,0:T(8,128)(2,1)S(1)}, bf16[4,32,1536]{2,1,0:T(8,128)(2,1)S(1)}, u32[]{:S(2)}, u32[]{:S(2)}) collective-permute-start(bf16[4,32,1536]{2,1,0:T(8,128)(2,1)S(1)} %get-tuple-element.115), channel_id=1, source_target_pairs={{0,16},{4,20},{8,24},{12,28},{16,0},{20,4},{24,8},{28,12},{1,17},{... | collective-permute-start | bytes 1179656 | tf_op jit(solution)/shard_map/ppermute | solution.py:563
  68.3 15.5 %collective-permute-start.9 = (bf16[512,1536]{1,0:T(8,128)(2,1)S(1)}, bf16[512,1536]{1,0:T(8,128)(2,1)}, u32[]{:S(2)}, u32[]{:S(2)}) collective-permute-start(bf16[512,1536]{1,0:T(8,128)(2,1)S(1)} %bitcast.46), channel_id=1, source_target_pairs={{0,4},{4,0},{8,12},{12,8},{16,20},{20,16},{24,28},{28,24},{1,5},{5... | collective-permute-start | bytes 4718600 | tf_op jit(solution)/shard_map/ppermute | solution.py:568
  70.5 13.2 %collective-permute-start.8 = (bf16[512,256]{1,0:T(8,128)(2,1)S(1)}, bf16[512,256]{1,0:T(8,128)(2,1)S(1)}, u32[]{:S(2)}, u32[]{:S(2)}) collective-permute-start(bf16[512,256]{1,0:T(8,128)(2,1)S(1)} %get-tuple-element.57), channel_id=1, source_target_pairs={{0,4},{4,0},{8,12},{12,8},{16,20},{20,16},{24,28},{28,24},{1,5},{5... | collective-permute-start | bytes 786440 | tf_op jit(solution)/shard_map/ppermute | solution.py:568
  83.7 7.9 %collective-permute-start.11 = (bf16[512,1536]{1,0:T(8,128)(2,1)}, bf16[512,1536]{1,0:T(8,128)(2,1)S(1)}, u32[]{:S(2)}, u32[]{:S(2)}) collective-permute-start(bf16[512,1536]{1,0:T(8,128)(2,1)} %all-gather.4.cloned.1.call-done.x_ref.xa_ref), channel_id=1, source_target_pairs={{0,4},{4,0},{8,12},{12,8},{16,20},{20,16},{24,28},{28,24},{1,5},{5... | collective-permute-start | bytes 4718600 | tf_op jit(solution)/shard_map/ppermute | solution.py:568
  104.5 81.0 %reduce-scatter.3.cloned.1.call-start = ((), (), s32[]{:S(2)}) async-start(), calls=%async_computation.3 | async-start | bytes 1966080 | tf_op jit(solution)/shard_map/reduce_scatter | solution.py:641
  116.3 34.1 %collective-permute-start.15 = (bf16[768,384]{1,0:T(8,128)(2,1)}, bf16[768,384]{1,0:T(8,128)(2,1)S(1)}, u32[]{:S(2)}, u32[]{:S(2)}) collective-permute-start(bf16[768,384]{1,0:T(8,128)(2,1)} %get-tuple-element.82), channel_id=1, source_target_pairs={{0,8},{4,12},{8,0},{12,4},{16,24},{20,28},{24,16},{28,20},{1,9},{5... | collective-permute-start | bytes 1769480 | tf_op jit(solution)/shard_map/ppermute | solution.py:563
  116.9 33.5 %collective-permute-start.16 = (bf16[768,384]{1,0:T(8,128)(2,1)}, bf16[768,384]{1,0:T(8,128)(2,1)S(1)}, u32[]{:S(2)}, u32[]{:S(2)}) collective-permute-start(bf16[768,384]{1,0:T(8,128)(2,1)} %get-tuple-element.83), channel_id=1, source_target_pairs={{0,16},{4,20},{8,24},{12,28},{16,0},{20,4},{24,8},{28,12},{1,17},{... | collective-permute-start | bytes 1769480 | tf_op jit(solution)/shard_map/ppermute | solution.py:563
  118.4 32.0 %collective-permute-start.17 = (bf16[768,384]{1,0:T(8,128)(2,1)}, bf16[768,384]{1,0:T(8,128)(2,1)S(1)}, u32[]{:S(2)}, u32[]{:S(2)}) collective-permute-start(bf16[768,384]{1,0:T(8,128)(2,1)} %get-tuple-element.84), channel_id=1, source_target_pairs={{0,24},{4,28},{8,16},{12,20},{16,8},{20,12},{24,0},{28,4},{1,25},{... | collective-permute-start | bytes 1769480 | tf_op jit(solution)/shard_map/ppermute | solution.py:563
  139.9 9.0 %collective-permute-start.13 = (bf16[2,32,1536]{2,1,0:T(8,128)(2,1)S(1)}, bf16[2,32,1536]{2,1,0:T(8,128)(2,1)S(1)}, u32[]{:S(2)}, u32[]{:S(2)}) collective-permute-start(bf16[2,32,1536]{2,1,0:T(8,128)(2,1)S(1)} %slice_bitcast_fusion.refs_4_), channel_id=1, source_target_pairs={{0,8},{4,12},{8,0},{12,4},{16,24},{20,28},{24,16},{28,20},{1,9},{5... | collective-permute-start | bytes 589832 | tf_op jit(solution)/shard_map/ppermute | solution.py:563
  148.9 7.9 %collective-permute-start.14 = (bf16[2,32,1536]{2,1,0:T(8,128)(2,1)S(1)}, bf16[2,32,1536]{2,1,0:T(8,128)(2,1)S(1)}, u32[]{:S(2)}, u32[]{:S(2)}) collective-permute-start(bf16[2,32,1536]{2,1,0:T(8,128)(2,1)S(1)} %pad_maximum_fusion.1), channel_id=1, source_target_pairs={{0,16},{4,20},{8,24},{12,28},{16,0},{20,4},{24,8},{28,12},{1,17},{... | collective-permute-start | bytes 589832 | tf_op jit(solution)/shard_map/ppermute | solution.py:563
  150.9 10.6 %collective-permute-start.21 = (bf16[192,768]{1,0:T(8,128)(2,1)S(1)}, bf16[192,768]{1,0:T(8,128)(2,1)S(1)}, u32[]{:S(2)}, u32[]{:S(2)}) collective-permute-start(bf16[192,768]{1,0:T(8,128)(2,1)S(1)} %get-tuple-element.90), channel_id=1, source_target_pairs={{0,16},{4,20},{8,24},{12,28},{16,0},{20,4},{24,8},{28,12},{1,17},{... | collective-permute-start | bytes 884744 | tf_op jit(solution)/shard_map/ppermute | solution.py:563
  151.6 15.1 %collective-permute-start.20 = (bf16[192,768]{1,0:T(8,128)(2,1)S(1)}, bf16[192,768]{1,0:T(8,128)(2,1)S(1)}, u32[]{:S(2)}, u32[]{:S(2)}) collective-permute-start(bf16[192,768]{1,0:T(8,128)(2,1)S(1)} %get-tuple-element.85.refs_4_), channel_id=1, source_target_pairs={{0,8},{4,12},{8,0},{12,4},{16,24},{20,28},{24,16},{28,20},{1,9},{5... | collective-permute-start | bytes 884744 | tf_op jit(solution)/shard_map/ppermute | solution.py:563
  158.0 8.7 %collective-permute-start.18 = (bf16[2,4,1,1536]{3,2,1,0:T(2,128)(2,1)S(1)}, bf16[2,4,1,1536]{3,2,1,0:T(2,128)(2,1)S(1)}, u32[]{:S(2)}, u32[]{:S(2)}) collective-permute-start(bf16[2,4,1,1536]{3,2,1,0:T(2,128)(2,1)S(1)} %get-tuple-element.87), channel_id=1, source_target_pairs={{0,1},{1,2},{2,3},{3,4},{4,5},{5,6},{6,7},{7,8},{8,9},{9,10},{10,1... | collective-permute-start | bytes 73736 | tf_op jit(solution)/shard_map/ppermute | solution.py:554
  167.4 19.3 %collective-permute-start.28 = (bf16[384,768]{1,0:T(8,128)(2,1)S(1)}, bf16[384,768]{1,0:T(8,128)(2,1)S(1)}, u32[]{:S(2)}, u32[]{:S(2)}) collective-permute-start(bf16[384,768]{1,0:T(8,128)(2,1)S(1)} %constant_dynamic-update-slice_fusion.6.refs_1_), channel_id=1, source_target_pairs={{0,8},{4,12},{8,0},{12,4},{16,24},{20,28},{24,16},{28,20},{1,9},{5... | collective-permute-start | bytes 1769480 | tf_op jit(solution)/shard_map/ppermute | solution.py:563
  168.3 18.4 %collective-permute-start.27 = (bf16[384,768]{1,0:T(8,128)(2,1)S(1)}, bf16[384,768]{1,0:T(8,128)(2,1)S(1)}, u32[]{:S(2)}, u32[]{:S(2)}) collective-permute-start(bf16[384,768]{1,0:T(8,128)(2,1)S(1)} %constant_dynamic-update-slice_fusion.4.refs_0_), channel_id=1, source_target_pairs={{0,16},{4,20},{8,24},{12,28},{16,0},{20,4},{24,8},{28,12},{1,17},{... | collective-permute-start | bytes 1769480 | tf_op jit(solution)/shard_map/ppermute | solution.py:563
  169.6 7.3 %collective-permute-start.19 = (bf16[2,4,1,1536]{3,2,1,0:T(2,128)(2,1)S(1)}, bf16[2,4,1,1536]{3,2,1,0:T(2,128)(2,1)S(1)}, u32[]{:S(2)}, u32[]{:S(2)}) collective-permute-start(bf16[2,4,1,1536]{3,2,1,0:T(2,128)(2,1)S(1)} %get-tuple-element.88), channel_id=1, source_target_pairs={{1,0},{2,1},{3,2},{4,3},{5,4},{6,5},{7,6},{8,7},{9,8},{10,9},{11,1... | collective-permute-start | bytes 73736 | tf_op jit(solution)/shard_map/ppermute | solution.py:554
  186.7 10.7 %collective-permute-start.29 = (bf16[384,768]{1,0:T(8,128)(2,1)S(1)}, bf16[384,768]{1,0:T(8,128)(2,1)S(1)}, u32[]{:S(2)}, u32[]{:S(2)}) collective-permute-start(bf16[384,768]{1,0:T(8,128)(2,1)S(1)} %collective-permute-done.27.refs_0_), channel_id=1, source_target_pairs={{0,4},{4,0},{8,12},{12,8},{16,20},{20,16},{24,28},{28,24},{1,5},{5... | collective-permute-start | bytes 1769480 | tf_op jit(solution)/shard_map/ppermute | solution.py:568
  188.1 9.3 %collective-permute-start.30 = (bf16[384,768]{1,0:T(8,128)(2,1)S(1)}, bf16[384,768]{1,0:T(8,128)(2,1)S(1)}, u32[]{:S(2)}, u32[]{:S(2)}) collective-permute-start(bf16[384,768]{1,0:T(8,128)(2,1)S(1)} %collective-permute-done.28.refs_1_), channel_id=1, source_target_pairs={{0,4},{4,0},{8,12},{12,8},{16,20},{20,16},{24,28},{28,24},{1,5},{5... | collective-permute-start | bytes 1769480 | tf_op jit(solution)/shard_map/ppermute | solution.py:568
  (39 other events, 214.6 us)
Sparse Core Ops, SparseCore 0:
  9.6 35.9 all-gather.5
  47.7 35.9 all-gather.3
  104.7 34.2 reduce-scatter.4
  141.1 35.3 reduce-scatter.2

commit v11 on v10

--- a/solution.py
+++ b/solution.py
@@ -195,6 +195,21 @@
         cost_estimate=COST,
         name="mixed_sum",
     )(at, *terms, skip)
+
+
+def marker_kernel(*refs):
+    refs[-1][...] = jnp.zeros_like(refs[-1])
+
+
+def marker(*deps):
+    return pl.pallas_call(
+        marker_kernel,
+        in_specs=spare(deps),
+        out_shape=TOKEN,
+        compiler_params=params(),
+        cost_estimate=COST,
+        name="marker",
+    )(*deps)
 
 
 def conv_back_kernel(d_ref, low_ref, high_ref, w_ref, *rest):
@@ -649,16 +664,17 @@
         at, d_normed, near, far, skip, grad, norm_gain, slope, half_a
     )
     low, high = neighbour_edges(first, last)
+    low, high, at_hand = lax.optimization_barrier((low, high, marker(conv_weight, first)))
 
     got_a = trade_chip(half_a, 1, heads)
     got_b = trade_chip(half_b, 2, heads)
-    near_a = jnp.concatenate([half_a, after(got_a, low)], axis=0)
-    near_b = jnp.concatenate([half_b, after(got_b, low)], axis=0)
+    near_a = jnp.concatenate([half_a, after(got_a, low, high)], axis=0)
+    near_b = jnp.concatenate([half_b, after(got_b, low, high)], axis=0)
     far_a = trade_chip(near_a, 2, heads)
     far_b = trade_chip(near_b, 1, heads)
     near_other = [swap_heads(near_a), swap_heads(near_b)]
     *outputs, token = unpack_weights(at, [near_a, near_b], near_other, False)
-    grad_input = conv_back(d_conv, low, high, conv_weight, token)
+    grad_input = conv_back(d_conv, low, high, conv_weight, token, at_hand)
 
     head_sum = after(head_sum, grad_input)
     head_sum = [head_sum[order.index(j)] for j in range(seqs)]

time: 211 us -> 216 us (1.024)
  waiting for transfers between devices: 74.4 us -> 67.2 us
  Pallas kernels: 53.1 us -> 58 us
  local copies, waits for them, and re-layouts: 29.5 us -> 33.5 us
  starting transfers between devices: 35.2 us -> 39 us
    ppermute x2, waiting for transfers between devices: 5.18 us -> 0.01 us  [neighbour_edges(): lax.ppermute(last, axes, forward)]
    ppermute x9, starting transfers between devices: 3.11 us -> 6.87 us  [swap_heads(): lax.ppermute(x, 'seq', [(s, s + 1 - 2 * (s % 2)) for s in range(count)])]
    pallas_call x2, Pallas kernels: 6.82 us -> 9.96 us  [unpack_weights(): pl.pallas_call(unpack_kernel, grid_spec=pltpu.PrefetchScalarGridSpec(num_...]
    ppermute x18, waiting for transfers between devices: 38.2 us -> 35.6 us  [trade_chip(): return lax.ppermute(x, 'seq', [(s, s ^ bit * heads) for s in range(count)])]
    unnamed x62 -> x64, local copies, waits for them, and re-layouts: 21.1 us -> 22.5 us
  transfers between devices with their start and end apart: 35 -> 35, of which waited for: 16 -> 16; matrix products, arithmetic and copies ran while one was open for 5% -> 7% of each run, Pallas kernels for 19% -> 20%
where the time goes in v11:
time: 216 us; the launch traced here: 213 us
  waiting for transfers between devices  67.2 us (31%)
  Pallas kernels  58 us (27%)
  starting transfers between devices  39 us (18%)
  local copies, waits for them, and re-layouts  33.5 us (16%)
  between operations  14.2 us (7%)
    ppermute x18, waiting for transfers between devices, trade_chip(): return lax.ppermute(x, 'seq', [(s, s ^ bit * heads) for s in range(count)])  35.6 us
    unnamed x64, local copies, waits for them, and re-layouts  22.5 us
    reduce_scatter x1, waiting for transfers between devices, unit_body(): lax.psum_scatter(d_term.reshape(shape), 'head', scatter_dimension=0, tile...  19 us
    ppermute x18, starting transfers between devices, trade_chip(): return lax.ppermute(x, 'seq', [(s, s ^ bit * heads) for s in range(count)])  18.6 us
    pallas_call x1, Pallas kernels, encoder(): pl.pallas_call(conv_kernel, grid=(width // tile,), in_specs=[SCALARS, who...  10.1 us
    pallas_call x2, Pallas kernels, unpack_weights(): pl.pallas_call(unpack_kernel, grid_spec=pltpu.PrefetchScalarGridSpec(num_...  9.96 us
    pallas_call x1, Pallas kernels, weight_gradients(): pl.pallas_call(weight_kernel, grid_spec=pltpu.PrefetchScalarGridSpec(num_...  8.81 us
    ppermute x2, starting transfers between devices, neighbour_edges(): lax.ppermute(last, axes, forward)  6.92 us
  transfers between devices with their start and end apart: 35, of which 16 were waited for; matrix products, arithmetic and copies ran while one was open for 7% of the time, Pallas kernels for 20%

profile of v11, /device:TPU:26, one launch (start us, length us, event | category | flops | bytes accessed | tf_op | source)
XLA Modules:
  0.0 212.8 jit_solution(3026644844956630999)
XLA Ops:
  9.1 2.4 %collective-permute-start.1 = (bf16[2,4,1,768]{3,2,1,0:T(2,128)(2,1)S(1)}, bf16[2,4,1,768]{3,2,1,0:T(2,128)(2,1)S(1)}, u32[]{:S(2)}, u32[]{:S(2)}) collective-permute-start(bf16[2,4,1,768]{3,2,1,0:T(2,128)(2,1)S(1)} %get-tuple-element.126), channel_id=1, source_target_pairs={{1,0},{2,1},{3,2},{4,3},{5,4},{6,5},{7,6},{8,7},{9,8},{10,9},{11,1... | collective-permute-start | bytes 36872 | tf_op jit(solution)/shard_map/ppermute | solution.py:569
  11.4 5.0 %collective-permute-start = (bf16[2,4,1,768]{3,2,1,0:T(2,128)(2,1)S(1)}, bf16[2,4,1,768]{3,2,1,0:T(2,128)(2,1)S(1)}, u32[]{:S(2)}, u32[]{:S(2)}) collective-permute-start(bf16[2,4,1,768]{3,2,1,0:T(2,128)(2,1)S(1)} %get-tuple-element.127), channel_id=1, source_target_pairs={{0,1},{1,2},{2,3},{3,4},{4,5},{5,6},{6,7},{7,8},{8,9},{9,10},{10,1... | collective-permute-start | bytes 36872 | tf_op jit(solution)/shard_map/ppermute | solution.py:569
  19.6 10.1 %encoder_forward.1 = (bf16[4,32,1536]{2,1,0:T(8,128)(2,1)}, f32[2,4,32,1536]{3,2,1,0:T(8,128)}, bf16[32,1536]{1,0:T(8,128)(2,1)}, bf16[32,1536]{1,0:T(8,128)(2,1...) custom-call(s32[2]{0:T(128)} %pad_add_fusion.at_ref, bf16[2,4,32,768]{3,2,1,0:T(8,128)(2,1)} %bitcast.63, ...), custom_call_target="tpu_custom_call" | custom-call | flops 1000 | bytes 1000 | tf_op jit(solution)/shard_map/encoder_forward/pallas_call | solution.py:111
  35.0 2.1 collective-permute-done.3
  39.7 5.9 %all-gather.6.cloned.1.call-done = bf16[128,4,1536]{2,1,0:T(4,128)(2,1)} async-done(((bf16[32,4,1536]{2,1,0:T(4,128)(2,1)}), bf16[128,4,1536]{2,1,0:T(4,128)(2,1)}) %all-gather.6.cloned.1.call-update) | async-done | bytes 1572880 | tf_op jit(solution)/shard_map/all_gather | solution.py:606
  51.0 9.4 %collective-permute-done.7 = bf16[4,32,1536]{2,1,0:T(8,128)(2,1)S(1)} collective-permute-done((bf16[4,32,1536]{2,1,0:T(8,128)(2,1)S(1)}, bf16[4,32,1536]{2,1,0:T(8,128)(2,1)S(1)}, u32[]{:S(2)}, u32[]{:S(2)}) %collective-permute-start.7) | collective-permute-done | bytes 393248 | tf_op jit(solution)/shard_map/ppermute | solution.py:578
  60.4 7.5 %collective-permute-done.6 = bf16[4,32,1536]{2,1,0:T(8,128)(2,1)S(1)} collective-permute-done((bf16[4,32,1536]{2,1,0:T(8,128)(2,1)S(1)}, bf16[4,32,1536]{2,1,0:T(8,128)(2,1)S(1)}, u32[]{:S(2)}, u32[]{:S(2)}) %collective-permute-start.6) | collective-permute-done | bytes 393248 | tf_op jit(solution)/shard_map/ppermute | solution.py:578
  72.6 3.9 %pack_weights.1 = (bf16[2,1536,576]{2,1,0:T(8,128)(2,1)S(1)}, bf16[2,576,1536]{2,1,0:T(8,128)(2,1)S(1)}, f32[8,128]{1,0:T(8,128)S(1)}) custom-call(bf16[3,1536,384]{2,1,0:T(8,128)(2,1)S(1)} %copy-done.9), custom_call_target="tpu_custom_call" | custom-call | flops 1000 | bytes 1000 | tf_op jit(solution)/shard_map/pack_weights/pallas_call | solution.py:280
  80.9 2.8 %all-gather.4.cloned.1.call-done.x_ref.xa_ref = bf16[512,1536]{1,0:T(8,128)(2,1)} async-done(((bf16[128,1536]{1,0:T(8,128)(2,1)}), bf16[512,1536]{1,0:T(8,128)(2,1)}) %all-gather.4.cloned.1.call-update) | async-done | bytes 1572880 | tf_op jit(solution)/shard_map/all_gather | solution.py:613
  83.7 2.1 copy-done.3
  91.5 6.5 %attention.1 = (bf16[512,768]{1,0:T(8,128)(2,1)S(1)}, bf16[512,768]{1,0:T(8,128)(2,1)S(1)}) custom-call(bf16[512,640]{1,0:T(8,128)(2,1)S(1)} %get-tuple-element.70.qa_ref, bf16[512,640]{1,0:T(8,128)(2,1)S(1)} %collective-permute-done.10.qb_ref, bf16[512,256]{1,0:T(8,128)(2,1)S(1)} %get-tuple-element.75.da_ref, ...), custom_call_target="tpu_custom_call" | custom-call | flops 1000 | bytes 1000 | tf_op jit(solution)/shard_map/attention/pallas_call | solution.py:381
  98.3 2.1 collective-permute-done.12.b_ref
  100.4 4.0 %d_term.1 = bf16[512,1536]{1,0:T(8,128)(2,1)} custom-call(s32[1]{0:T(128)} %bitcast.1.head_ref, bf16[512,768]{1,0:T(8,128)(2,1)S(1)} %get-tuple-element.77.a_ref.ra_ref, bf16[512,768]{1,0:T(8,128)(2,1)S(1)} %collective-permute-done.12.b_ref, bf16[2,576,1536]{2,1,0:T(8,128)(2,1)S(1)} %copy-done.11), custom_call_target="tpu_custom_call" | custom-call | flops 1000 | bytes 1000 | tf_op jit(solution)/shard_map/d_term/pallas_call | solution.py:408
  107.5 8.8 %weight_gradients.1 = (bf16[768,384]{1,0:T(8,128)(2,1)}, bf16[768,384]{1,0:T(8,128)(2,1)}, bf16[768,384]{1,0:T(8,128)(2,1)}, bf16[768,384]{1,0:T(8,128)(2,1)}) custom-call(s32[1]{0:T(128)} %bitcast.at_ref, bf16[512,1536]{1,0:T(8,128)(2,1)} %all-gather.4.cloned.1.call-done.x_ref.xa_ref, bf16[512,1536]{1,0:T(8,128)(2,1)} %copy-done.8, ...), custom_call_target="tpu_custom_call" | custom-call | flops 1000 | bytes 1000 | tf_op jit(solution)/shard_map/weight_gradients/pallas_call | solution.py:457
  119.8 19.0 %reduce-scatter.5.cloned.1.call-done = bf16[1,4,32,1536]{3,2,1,0:T(8,128)(2,1)} async-done(((bf16[4,4,32,1536]{3,2,1,0:T(8,128)(2,1)}), bf16[1,4,32,1536]{3,2,1,0:T(8,128)(2,1)}) %reduce-scatter.5.cloned.1.call-update) | async-done | bytes 393232 | tf_op jit(solution)/shard_map/reduce_scatter | solution.py:641
  141.5 7.4 %collective-permute-done.13.near_ref = bf16[2,32,1536]{2,1,0:T(8,128)(2,1)S(1)} collective-permute-done((bf16[2,32,1536]{2,1,0:T(8,128)(2,1)S(1)}, bf16[2,32,1536]{2,1,0:T(8,128)(2,1)S(1)}, u32[]{:S(2)}, u32[]{:S(2)}) %collective-permute-start.13) | collective-permute-done | bytes 196640 | tf_op jit(solution)/shard_map/ppermute | solution.py:578
  159.2 3.9 %collective-permute-start.19 = (bf16[2,4,1,1536]{3,2,1,0:T(2,128)(2,1)S(1)}, bf16[2,4,1,1536]{3,2,1,0:T(2,128)(2,1)S(1)}, u32[]{:S(2)}, u32[]{:S(2)}) collective-permute-start(bf16[2,4,1,1536]{3,2,1,0:T(2,128)(2,1)S(1)} %get-tuple-element.91.refs_1_), channel_id=1, source_target_pairs={{1,0},{2,1},{3,2},{4,3},{5,4},{6,5},{7,6},{8,7},{9,8},{10,9},{11,1... | collective-permute-start | bytes 73736 | tf_op jit(solution)/shard_map/ppermute | solution.py:569
  163.8 4.4 %copy-done = bf16[5,768,1536]{2,1,0:T(8,128)(2,1)S(1)} copy-done((bf16[5,768,1536]{2,1,0:T(8,128)(2,1)S(1)}, bf16[5,768,1536]{2,1,0:T(8,128)(2,1)}, u32[]{:S(2)}) %copy-start) | copy-done | bytes 11796504
  169.0 5.4 %collective-permute-start.23 = (bf16[384,768]{1,0:T(8,128)(2,1)}, bf16[384,768]{1,0:T(8,128)(2,1)S(1)}, u32[]{:S(2)}, u32[]{:S(2)}) collective-permute-start(bf16[384,768]{1,0:T(8,128)(2,1)} %constant_dynamic-update-slice_fusion.6.refs_1_), channel_id=1, source_target_pairs={{0,4},{4,0},{8,12},{12,8},{16,20},{20,16},{24,28},{28,24},{1,5},{5... | collective-permute-start | bytes 1769480 | tf_op jit(solution)/shard_map/ppermute | solution.py:583
  177.3 5.0 %weight_outputs_near.1 = (f32[3,1536,384]{2,1,0:T(8,128)}, f32[2,2,96,1536]{3,2,1,0:T(8,128)}, f32[8,128]{1,0:T(8,128)S(1)}) custom-call(s32[2]{0:T(128)S(1)} %copy-done.20, bf16[384,768]{1,0:T(8,128)(2,1)} %constant_dynamic-update-slice_fusion.4.refs_0_, bf16[384,768]{1,0:T(8,128)(2,1)} %constant_dynamic-update-slice_fusion.6.refs_1_, ...), custom_call_target="tpu_custom_call" | custom-call | flops 1000 | bytes 1000 | tf_op jit(solution)/shard_map/weight_outputs_near/pallas_call | solution.py:538
  182.4 4.3 %encoder_backward.1 = bf16[256,768]{1,0:T(8,128)(2,1)S(1)} custom-call(bf16[2,4,32,1536]{3,2,1,0:T(8,128)(2,1)S(1)} %get-tuple-element.89.d_ref, bf16[2,4,1,1536]{3,2,1,0:T(2,128)(2,1)S(1)} %collective-permute-done.18.low_ref, bf16[2,4,1,1536]{3,2,1,0:T(2,128)(2,1)S(1)} %collective-permute-done.19.high_ref, bf16[5,768,1536]{2,1,0:T(8,128)(2,1)S(1)} %bitcast.47, ...), custom_call_target="tpu_custom_call" | custom-call | flops 1000 | bytes 1000 | tf_op jit(solution)/shard_map/encoder_backward/pallas_call | solution.py:244
  188.5 2.6 %collective-permute-done.28.refs_1_ = bf16[384,768]{1,0:T(8,128)(2,1)} collective-permute-done((bf16[384,768]{1,0:T(8,128)(2,1)}, bf16[384,768]{1,0:T(8,128)(2,1)}, u32[]{:S(2)}, u32[]{:S(2)}) %collective-permute-start.28) | collective-permute-done | bytes 589856 | tf_op jit(solution)/shard_map/ppermute | solution.py:578
  195.2 2.0 copy.25
  201.2 5.0 %weight_outputs_far.1 = (f32[3,1536,384]{2,1,0:T(8,128)}, f32[2,2,96,1536]{3,2,1,0:T(8,128)}, f32[8,128]{1,0:T(8,128)}) custom-call(s32[2]{0:T(128)S(1)} %copy-done.20, bf16[384,768]{1,0:T(8,128)(2,1)} %collective-permute-done.27.refs_0_, bf16[384,768]{1,0:T(8,128)(2,1)} %collective-permute-done.28.refs_1_, ...), custom_call_target="tpu_custom_call", output_to_operand_aliasing={{0}: (5, {}), {1}: (6, {})} | custom-call | flops 1000 | bytes 1000 | tf_op jit(solution)/shard_map/weight_outputs_far/pallas_call | solution.py:538
  (150 shorter events, 66.7 us)
Async XLA Ops:
  7.2 38.4 %all-gather.6.cloned.1.call-start = ((), (), s32[]{:S(2)}) async-start(), calls=%async_computation.5 | async-start | bytes 1966080 | tf_op jit(solution)/shard_map/all_gather | solution.py:606
  7.9 75.8 %all-gather.4.cloned.1.call-start = ((), (), s32[]{:S(2)}) async-start(), calls=%async_computation.2 | async-start | bytes 1966080 | tf_op jit(solution)/shard_map/all_gather | solution.py:613
  9.1 9.3 %collective-permute-start.1 = (bf16[2,4,1,768]{3,2,1,0:T(2,128)(2,1)S(1)}, bf16[2,4,1,768]{3,2,1,0:T(2,128)(2,1)S(1)}, u32[]{:S(2)}, u32[]{:S(2)}) collective-permute-start(bf16[2,4,1,768]{3,2,1,0:T(2,128)(2,1)S(1)} %get-tuple-element.126), channel_id=1, source_target_pairs={{1,0},{2,1},{3,2},{4,3},{5,4},{6,5},{7,6},{8,7},{9,8},{10,9},{11,1... | collective-permute-start | bytes 36872 | tf_op jit(solution)/shard_map/ppermute | solution.py:569
  39.6 99.2 %reduce-scatter.5.cloned.1.call-start = ((), (), s32[]{:S(2)}) async-start(), calls=%async_computation.4 | async-start | bytes 1966080 | tf_op jit(solution)/shard_map/reduce_scatter | solution.py:641
  47.4 13.0 %collective-permute-start.7 = (bf16[4,32,1536]{2,1,0:T(8,128)(2,1)S(1)}, bf16[4,32,1536]{2,1,0:T(8,128)(2,1)S(1)}, u32[]{:S(2)}, u32[]{:S(2)}) collective-permute-start(bf16[4,32,1536]{2,1,0:T(8,128)(2,1)S(1)} %get-tuple-element.119), channel_id=1, source_target_pairs={{0,24},{4,28},{8,16},{12,20},{16,8},{20,12},{24,0},{28,4},{1,25},{... | collective-permute-start | bytes 1179656 | tf_op jit(solution)/shard_map/ppermute | solution.py:578
  48.9 19.0 %collective-permute-start.6 = (bf16[4,32,1536]{2,1,0:T(8,128)(2,1)S(1)}, bf16[4,32,1536]{2,1,0:T(8,128)(2,1)S(1)}, u32[]{:S(2)}, u32[]{:S(2)}) collective-permute-start(bf16[4,32,1536]{2,1,0:T(8,128)(2,1)S(1)} %get-tuple-element.120), channel_id=1, source_target_pairs={{0,8},{4,12},{8,0},{12,4},{16,24},{20,28},{24,16},{28,20},{1,9},{5... | collective-permute-start | bytes 1179656 | tf_op jit(solution)/shard_map/ppermute | solution.py:578
  50.4 17.5 %collective-permute-start.5 = (bf16[4,32,1536]{2,1,0:T(8,128)(2,1)S(1)}, bf16[4,32,1536]{2,1,0:T(8,128)(2,1)S(1)}, u32[]{:S(2)}, u32[]{:S(2)}) collective-permute-start(bf16[4,32,1536]{2,1,0:T(8,128)(2,1)S(1)} %get-tuple-element.121), channel_id=1, source_target_pairs={{0,16},{4,20},{8,24},{12,28},{16,0},{20,4},{24,8},{28,12},{1,17},{... | collective-permute-start | bytes 1179656 | tf_op jit(solution)/shard_map/ppermute | solution.py:578
  68.3 15.5 %collective-permute-start.9 = (bf16[512,1536]{1,0:T(8,128)(2,1)S(1)}, bf16[512,1536]{1,0:T(8,128)(2,1)}, u32[]{:S(2)}, u32[]{:S(2)}) collective-permute-start(bf16[512,1536]{1,0:T(8,128)(2,1)S(1)} %bitcast.48), channel_id=1, source_target_pairs={{0,4},{4,0},{8,12},{12,8},{16,20},{20,16},{24,28},{28,24},{1,5},{5... | collective-permute-start | bytes 4718600 | tf_op jit(solution)/shard_map/ppermute | solution.py:583
  70.5 13.2 %collective-permute-start.8 = (bf16[512,256]{1,0:T(8,128)(2,1)S(1)}, bf16[512,256]{1,0:T(8,128)(2,1)S(1)}, u32[]{:S(2)}, u32[]{:S(2)}) collective-permute-start(bf16[512,256]{1,0:T(8,128)(2,1)S(1)} %get-tuple-element.60), channel_id=1, source_target_pairs={{0,4},{4,0},{8,12},{12,8},{16,20},{20,16},{24,28},{28,24},{1,5},{5... | collective-permute-start | bytes 786440 | tf_op jit(solution)/shard_map/ppermute | solution.py:583
  83.7 7.8 %collective-permute-start.11 = (bf16[512,1536]{1,0:T(8,128)(2,1)}, bf16[512,1536]{1,0:T(8,128)(2,1)S(1)}, u32[]{:S(2)}, u32[]{:S(2)}) collective-permute-start(bf16[512,1536]{1,0:T(8,128)(2,1)} %all-gather.4.cloned.1.call-done.x_ref.xa_ref), channel_id=1, source_target_pairs={{0,4},{4,0},{8,12},{12,8},{16,20},{20,16},{24,28},{28,24},{1,5},{5... | collective-permute-start | bytes 4718600 | tf_op jit(solution)/shard_map/ppermute | solution.py:583
  104.5 83.0 %reduce-scatter.3.cloned.1.call-start = ((), (), s32[]{:S(2)}) async-start(), calls=%async_computation.3 | async-start | bytes 1966080 | tf_op jit(solution)/shard_map/reduce_scatter | solution.py:656
  116.4 34.1 %collective-permute-start.15 = (bf16[768,384]{1,0:T(8,128)(2,1)}, bf16[768,384]{1,0:T(8,128)(2,1)}, u32[]{:S(2)}, u32[]{:S(2)}) collective-permute-start(bf16[768,384]{1,0:T(8,128)(2,1)} %get-tuple-element.85), channel_id=1, source_target_pairs={{0,8},{4,12},{8,0},{12,4},{16,24},{20,28},{24,16},{28,20},{1,9},{5... | collective-permute-start | bytes 1769480 | tf_op jit(solution)/shard_map/ppermute | solution.py:578
  116.9 33.5 %collective-permute-start.16 = (bf16[768,384]{1,0:T(8,128)(2,1)}, bf16[768,384]{1,0:T(8,128)(2,1)}, u32[]{:S(2)}, u32[]{:S(2)}) collective-permute-start(bf16[768,384]{1,0:T(8,128)(2,1)} %get-tuple-element.86), channel_id=1, source_target_pairs={{0,16},{4,20},{8,24},{12,28},{16,0},{20,4},{24,8},{28,12},{1,17},{... | collective-permute-start | bytes 1769480 | tf_op jit(solution)/shard_map/ppermute | solution.py:578
  118.4 32.1 %collective-permute-start.17 = (bf16[768,384]{1,0:T(8,128)(2,1)}, bf16[768,384]{1,0:T(8,128)(2,1)}, u32[]{:S(2)}, u32[]{:S(2)}) collective-permute-start(bf16[768,384]{1,0:T(8,128)(2,1)} %get-tuple-element.87), channel_id=1, source_target_pairs={{0,24},{4,28},{8,16},{12,20},{16,8},{20,12},{24,0},{28,4},{1,25},{... | collective-permute-start | bytes 1769480 | tf_op jit(solution)/shard_map/ppermute | solution.py:578
  139.9 9.0 %collective-permute-start.13 = (bf16[2,32,1536]{2,1,0:T(8,128)(2,1)S(1)}, bf16[2,32,1536]{2,1,0:T(8,128)(2,1)S(1)}, u32[]{:S(2)}, u32[]{:S(2)}) collective-permute-start(bf16[2,32,1536]{2,1,0:T(8,128)(2,1)S(1)} %slice_bitcast_fusion.refs_4_), channel_id=1, source_target_pairs={{0,8},{4,12},{8,0},{12,4},{16,24},{20,28},{24,16},{28,20},{1,9},{5... | collective-permute-start | bytes 589832 | tf_op jit(solution)/shard_map/ppermute | solution.py:578
  152.5 15.8 %collective-permute-start.21 = (bf16[192,768]{1,0:T(8,128)(2,1)S(1)}, bf16[192,768]{1,0:T(8,128)(2,1)S(1)}, u32[]{:S(2)}, u32[]{:S(2)}) collective-permute-start(bf16[192,768]{1,0:T(8,128)(2,1)S(1)} %get-tuple-element.95), channel_id=1, source_target_pairs={{0,16},{4,20},{8,24},{12,28},{16,0},{20,4},{24,8},{28,12},{1,17},{... | collective-permute-start | bytes 884744 | tf_op jit(solution)/shard_map/ppermute | solution.py:578
  153.1 15.1 %collective-permute-start.20 = (bf16[192,768]{1,0:T(8,128)(2,1)S(1)}, bf16[192,768]{1,0:T(8,128)(2,1)S(1)}, u32[]{:S(2)}, u32[]{:S(2)}) collective-permute-start(bf16[192,768]{1,0:T(8,128)(2,1)S(1)} %get-tuple-element.88.refs_4_), channel_id=1, source_target_pairs={{0,8},{4,12},{8,0},{12,4},{16,24},{20,28},{24,16},{28,20},{1,9},{5... | collective-permute-start | bytes 884744 | tf_op jit(solution)/shard_map/ppermute | solution.py:578
  157.2 11.0 %collective-permute-start.18 = (bf16[2,4,1,1536]{3,2,1,0:T(2,128)(2,1)S(1)}, bf16[2,4,1,1536]{3,2,1,0:T(2,128)(2,1)S(1)}, u32[]{:S(2)}, u32[]{:S(2)}) collective-permute-start(bf16[2,4,1,1536]{3,2,1,0:T(2,128)(2,1)S(1)} %get-tuple-element.90), channel_id=1, source_target_pairs={{0,1},{1,2},{2,3},{3,4},{4,5},{5,6},{6,7},{7,8},{8,9},{9,10},{10,1... | collective-permute-start | bytes 73736 | tf_op jit(solution)/shard_map/ppermute | solution.py:569
  159.2 9.1 %collective-permute-start.19 = (bf16[2,4,1,1536]{3,2,1,0:T(2,128)(2,1)S(1)}, bf16[2,4,1,1536]{3,2,1,0:T(2,128)(2,1)S(1)}, u32[]{:S(2)}, u32[]{:S(2)}) collective-permute-start(bf16[2,4,1,1536]{3,2,1,0:T(2,128)(2,1)S(1)} %get-tuple-element.91.refs_1_), channel_id=1, source_target_pairs={{1,0},{2,1},{3,2},{4,3},{5,4},{6,5},{7,6},{8,7},{9,8},{10,9},{11,1... | collective-permute-start | bytes 73736 | tf_op jit(solution)/shard_map/ppermute | solution.py:569
  169.0 7.3 %collective-permute-start.23 = (bf16[384,768]{1,0:T(8,128)(2,1)}, bf16[384,768]{1,0:T(8,128)(2,1)S(1)}, u32[]{:S(2)}, u32[]{:S(2)}) collective-permute-start(bf16[384,768]{1,0:T(8,128)(2,1)} %constant_dynamic-update-slice_fusion.6.refs_1_), channel_id=1, source_target_pairs={{0,4},{4,0},{8,12},{12,8},{16,20},{20,16},{24,28},{28,24},{1,5},{5... | collective-permute-start | bytes 1769480 | tf_op jit(solution)/shard_map/ppermute | solution.py:583
  175.1 16.1 %collective-permute-start.28 = (bf16[384,768]{1,0:T(8,128)(2,1)}, bf16[384,768]{1,0:T(8,128)(2,1)}, u32[]{:S(2)}, u32[]{:S(2)}) collective-permute-start(bf16[384,768]{1,0:T(8,128)(2,1)} %constant_dynamic-update-slice_fusion.6.refs_1_), channel_id=1, source_target_pairs={{0,8},{4,12},{8,0},{12,4},{16,24},{20,28},{24,16},{28,20},{1,9},{5... | collective-permute-start | bytes 1769480 | tf_op jit(solution)/shard_map/ppermute | solution.py:578
  175.1 16.1 %collective-permute-start.27 = (bf16[384,768]{1,0:T(8,128)(2,1)}, bf16[384,768]{1,0:T(8,128)(2,1)}, u32[]{:S(2)}, u32[]{:S(2)}) collective-permute-start(bf16[384,768]{1,0:T(8,128)(2,1)} %constant_dynamic-update-slice_fusion.4.refs_0_), channel_id=1, source_target_pairs={{0,16},{4,20},{8,24},{12,28},{16,0},{20,4},{24,8},{28,12},{1,17},{... | collective-permute-start | bytes 1769480 | tf_op jit(solution)/shard_map/ppermute | solution.py:578
  191.2 10.0 %collective-permute-start.29 = (bf16[384,768]{1,0:T(8,128)(2,1)}, bf16[384,768]{1,0:T(8,128)(2,1)S(1)}, u32[]{:S(2)}, u32[]{:S(2)}) collective-permute-start(bf16[384,768]{1,0:T(8,128)(2,1)} %collective-permute-done.27.refs_0_), channel_id=1, source_target_pairs={{0,4},{4,0},{8,12},{12,8},{16,20},{20,16},{24,28},{28,24},{1,5},{5... | collective-permute-start | bytes 1769480 | tf_op jit(solution)/shard_map/ppermute | solution.py:583
  191.2 10.0 %collective-permute-start.30 = (bf16[384,768]{1,0:T(8,128)(2,1)}, bf16[384,768]{1,0:T(8,128)(2,1)S(1)}, u32[]{:S(2)}, u32[]{:S(2)}) collective-permute-start(bf16[384,768]{1,0:T(8,128)(2,1)} %collective-permute-done.28.refs_1_), channel_id=1, source_target_pairs={{0,4},{4,0},{8,12},{12,8},{16,20},{20,16},{24,28},{28,24},{1,5},{5... | collective-permute-start | bytes 1769480 | tf_op jit(solution)/shard_map/ppermute | solution.py:583
  (40 other events, 324.3 us)
Sparse Core Ops, SparseCore 0:
  9.6 35.9 all-gather.5
  47.7 35.9 all-gather.3
  104.6 34.2 reduce-scatter.4
  141.0 36.3 reduce-scatter.2

commit v12 on v11

--- a/solution.py
+++ b/solution.py
@@ -10,6 +10,7 @@
 DH = 192
 KW = 5
 VMEM_LIMIT = 24 * 1024 * 1024
+SMALL_LIMIT = 16 * 1024 * 1024
 STREAMING_LIMIT = 56 * 1024 * 1024
 COST = pl.CostEstimate(flops=1000, bytes_accessed=1000, transcendentals=0)
 BF = jnp.bfloat16
@@ -170,31 +171,31 @@
         in_specs=[SCALARS] + [vmem] * 7 + spare(deps),
         out_specs=[vmem] * 3,
         out_shape=[jax.ShapeDtypeStruct(slope.shape, BF)] + [edge] * 2,
-        compiler_params=params(),
+        compiler_params=params(SMALL_LIMIT),
         cost_estimate=COST,
         name="conv_gradient",
     )(at, own, near, far, skip, grad, norm_gain.reshape(1, -1), slope, *deps)
 
 
 def mixed_body(seqs, at_ref, *refs):
-    skip_ref, out_ref = refs[seqs:]
+    skip_ref, out_ref = refs[seqs], refs[-1]
     for slot in range(seqs):
         b = at_ref[0] ^ slot
         out_ref[b] = (skip_ref[b].astype(F32) + refs[slot][...].astype(F32)).astype(BF)
 
 
-def mixed_call(at, terms, skip):
+def mixed_call(at, terms, skip, *deps):
     seqs = len(terms)
     vmem = pl.BlockSpec(memory_space=pltpu.VMEM)
     return pl.pallas_call(
         functools.partial(mixed_body, seqs),
-        in_specs=[SCALARS] + [vmem] * (seqs + 1),
+        in_specs=[SCALARS] + [vmem] * (seqs + 1) + spare(deps),
         out_specs=vmem,
         out_shape=jax.ShapeDtypeStruct(skip.shape, BF),
-        compiler_params=params(),
+        compiler_params=params(SMALL_LIMIT),
         cost_estimate=COST,
         name="mixed_sum",
-    )(at, *terms, skip)
+    )(at, *terms, skip, *deps)
 
 
 def marker_kernel(*refs):
@@ -206,7 +207,7 @@
         marker_kernel,
         in_specs=spare(deps),
         out_shape=TOKEN,
-        compiler_params=params(),
+        compiler_params=params(SMALL_LIMIT),
         cost_estimate=COST,
         name="marker",
     )(*deps)
@@ -492,7 +493,7 @@
         functools.partial(weight_sum_kernel, count=len(parts)),
         in_specs=[pl.BlockSpec(memory_space=pltpu.VMEM)] * len(parts) + spare(deps),
         out_shape=[jax.ShapeDtypeStruct((chunk // 2, full), BF)] * 2,
-        compiler_params=params(),
+        compiler_params=params(SMALL_LIMIT),
         cost_estimate=COST,
         name="weight_sum",
     )(*parts, *deps)
@@ -555,7 +556,7 @@
             TOKEN,
         ],
         input_output_aliases={5 + i: i for i in range(len(before))},
-        compiler_params=params(),
+        compiler_params=params(SMALL_LIMIT),
         cost_estimate=COST,
         name="weight_outputs_far" if far else "weight_outputs_near",
     )(at, *mine, *other, *before)
@@ -674,14 +675,14 @@
     far_b = trade_chip(near_b, 1, heads)
     near_other = [swap_heads(near_a), swap_heads(near_b)]
     *outputs, token = unpack_weights(at, [near_a, near_b], near_other, False)
-    grad_input = conv_back(d_conv, low, high, conv_weight, token, at_hand)
+    grad_input = conv_back(d_conv, low, high, conv_weight, at_hand, *near_other)
 
     head_sum = after(head_sum, grad_input)
     head_sum = [head_sum[order.index(j)] for j in range(seqs)]
     far_other = [swap_heads(after(x, *head_sum)) for x in (far_a, far_b)]
     grad_w_qkv, grad_w_out, _ = unpack_weights(at, [far_a, far_b], far_other, True, outputs)
     head_sum = to_chips(head_sum)
-    mixed = mixed_call(at, head_sum, skip)
+    mixed = mixed_call(at, head_sum, skip, token)
     grad_input = jnp.transpose(grad_input.reshape(2, seqs, rows, -1), (2, 0, 1, 3))
     return (
         jnp.transpose(mixed, (1, 0, 2)),

time: 216 us -> 220 us (1.019)
  local copies, waits for them, and re-layouts: 33.5 us -> 36.2 us
    unnamed x64 -> x74, local copies, waits for them, and re-layouts: 22.5 us -> 26.3 us
  transfers between devices with their start and end apart: 35 -> 35, of which waited for: 16 -> 13; matrix products, arithmetic and copies ran while one was open for 7% -> 7% of each run, Pallas kernels for 20% -> 20%
where the time goes in v12:
time: 220 us; the launch traced here: 217 us
  waiting for transfers between devices  68.4 us (31%)
  Pallas kernels  58 us (26%)
  starting transfers between devices  39 us (18%)
  local copies, waits for them, and re-layouts  36.2 us (16%)
  between operations  14.2 us (6%)
    ppermute x18, waiting for transfers between devices, trade_chip(): return lax.ppermute(x, 'seq', [(s, s ^ bit * heads) for s in range(count)])  36.7 us
    unnamed x74, local copies, waits for them, and re-layouts  26.3 us
    reduce_scatter x1, waiting for transfers between devices, unit_body(): lax.psum_scatter(d_term.reshape(shape), 'head', scatter_dimension=0, tile...  19 us
    ppermute x18, starting transfers between devices, trade_chip(): return lax.ppermute(x, 'seq', [(s, s ^ bit * heads) for s in range(count)])  18.5 us
    pallas_call x1, Pallas kernels, encoder(): pl.pallas_call(conv_kernel, grid=(width // tile,), in_specs=[SCALARS, who...  10.1 us
    pallas_call x2, Pallas kernels, unpack_weights(): pl.pallas_call(unpack_kernel, grid_spec=pltpu.PrefetchScalarGridSpec(num_...  9.96 us
    pallas_call x1, Pallas kernels, weight_gradients(): pl.pallas_call(weight_kernel, grid_spec=pltpu.PrefetchScalarGridSpec(num_...  8.83 us
    ppermute x2, starting transfers between devices, neighbour_edges(): lax.ppermute(last, axes, forward)  6.92 us
  transfers between devices with their start and end apart: 35, of which 13 were waited for; matrix products, arithmetic and copies ran while one was open for 7% of the time, Pallas kernels for 20%

profile of v12, /device:TPU:26, one launch (start us, length us, event | category | flops | bytes accessed | tf_op | source)
XLA Modules:
  0.0 216.7 jit_solution(6215920283152182027)
XLA Ops:
  9.1 2.4 %collective-permute-start.1 = (bf16[2,4,1,768]{3,2,1,0:T(2,128)(2,1)S(1)}, bf16[2,4,1,768]{3,2,1,0:T(2,128)(2,1)S(1)}, u32[]{:S(2)}, u32[]{:S(2)}) collective-permute-start(bf16[2,4,1,768]{3,2,1,0:T(2,128)(2,1)S(1)} %get-tuple-element.126), channel_id=1, source_target_pairs={{1,0},{2,1},{3,2},{4,3},{5,4},{6,5},{7,6},{8,7},{9,8},{10,9},{11,1... | collective-permute-start | bytes 36872 | tf_op jit(solution)/shard_map/ppermute | solution.py:570
  11.4 5.0 %collective-permute-start = (bf16[2,4,1,768]{3,2,1,0:T(2,128)(2,1)S(1)}, bf16[2,4,1,768]{3,2,1,0:T(2,128)(2,1)S(1)}, u32[]{:S(2)}, u32[]{:S(2)}) collective-permute-start(bf16[2,4,1,768]{3,2,1,0:T(2,128)(2,1)S(1)} %get-tuple-element.127), channel_id=1, source_target_pairs={{0,1},{1,2},{2,3},{3,4},{4,5},{5,6},{6,7},{7,8},{8,9},{9,10},{10,1... | collective-permute-start | bytes 36872 | tf_op jit(solution)/shard_map/ppermute | solution.py:570
  19.6 10.1 %encoder_forward.1 = (bf16[4,32,1536]{2,1,0:T(8,128)(2,1)}, f32[2,4,32,1536]{3,2,1,0:T(8,128)}, bf16[32,1536]{1,0:T(8,128)(2,1)}, bf16[32,1536]{1,0:T(8,128)(2,1...) custom-call(s32[2]{0:T(128)} %pad_add_fusion.at_ref, bf16[2,4,32,768]{3,2,1,0:T(8,128)(2,1)} %bitcast.63, ...), custom_call_target="tpu_custom_call" | custom-call | flops 1000 | bytes 1000 | tf_op jit(solution)/shard_map/encoder_forward/pallas_call | solution.py:112
  35.0 2.1 collective-permute-done.3
  39.7 5.8 %all-gather.6.cloned.1.call-done = bf16[128,4,1536]{2,1,0:T(4,128)(2,1)} async-done(((bf16[32,4,1536]{2,1,0:T(4,128)(2,1)}), bf16[128,4,1536]{2,1,0:T(4,128)(2,1)}) %all-gather.6.cloned.1.call-update) | async-done | bytes 1572880 | tf_op jit(solution)/shard_map/all_gather | solution.py:607
  51.0 9.4 %collective-permute-done.7 = bf16[4,32,1536]{2,1,0:T(8,128)(2,1)S(1)} collective-permute-done((bf16[4,32,1536]{2,1,0:T(8,128)(2,1)S(1)}, bf16[4,32,1536]{2,1,0:T(8,128)(2,1)S(1)}, u32[]{:S(2)}, u32[]{:S(2)}) %collective-permute-start.7) | collective-permute-done | bytes 393248 | tf_op jit(solution)/shard_map/ppermute | solution.py:579
  60.4 7.5 %collective-permute-done.6 = bf16[4,32,1536]{2,1,0:T(8,128)(2,1)S(1)} collective-permute-done((bf16[4,32,1536]{2,1,0:T(8,128)(2,1)S(1)}, bf16[4,32,1536]{2,1,0:T(8,128)(2,1)S(1)}, u32[]{:S(2)}, u32[]{:S(2)}) %collective-permute-start.6) | collective-permute-done | bytes 393248 | tf_op jit(solution)/shard_map/ppermute | solution.py:579
  70.6 2.0 copy-done.9
  72.6 3.9 %pack_weights.1 = (bf16[2,1536,576]{2,1,0:T(8,128)(2,1)S(1)}, bf16[2,576,1536]{2,1,0:T(8,128)(2,1)S(1)}, f32[8,128]{1,0:T(8,128)S(1)}) custom-call(bf16[3,1536,384]{2,1,0:T(8,128)(2,1)S(1)} %copy-done.9), custom_call_target="tpu_custom_call" | custom-call | flops 1000 | bytes 1000 | tf_op jit(solution)/shard_map/pack_weights/pallas_call | solution.py:281
  80.9 2.8 %all-gather.4.cloned.1.call-done.x_ref.xa_ref = bf16[512,1536]{1,0:T(8,128)(2,1)} async-done(((bf16[128,1536]{1,0:T(8,128)(2,1)}), bf16[512,1536]{1,0:T(8,128)(2,1)}) %all-gather.4.cloned.1.call-update) | async-done | bytes 1572880 | tf_op jit(solution)/shard_map/all_gather | solution.py:614
  83.7 2.1 copy-done.3
  91.5 6.5 %attention.1 = (bf16[512,768]{1,0:T(8,128)(2,1)S(1)}, bf16[512,768]{1,0:T(8,128)(2,1)S(1)}) custom-call(bf16[512,640]{1,0:T(8,128)(2,1)S(1)} %get-tuple-element.70.qa_ref, bf16[512,640]{1,0:T(8,128)(2,1)S(1)} %collective-permute-done.10.qb_ref, bf16[512,256]{1,0:T(8,128)(2,1)S(1)} %get-tuple-element.75.da_ref, ...), custom_call_target="tpu_custom_call" | custom-call | flops 1000 | bytes 1000 | tf_op jit(solution)/shard_map/attention/pallas_call | solution.py:382
  98.3 2.1 collective-permute-done.12.b_ref
  100.4 4.0 %d_term.1 = bf16[512,1536]{1,0:T(8,128)(2,1)} custom-call(s32[1]{0:T(128)} %bitcast.1.head_ref, bf16[512,768]{1,0:T(8,128)(2,1)S(1)} %get-tuple-element.77.a_ref.ra_ref, bf16[512,768]{1,0:T(8,128)(2,1)S(1)} %collective-permute-done.12.b_ref, bf16[2,576,1536]{2,1,0:T(8,128)(2,1)S(1)} %copy-done.11), custom_call_target="tpu_custom_call" | custom-call | flops 1000 | bytes 1000 | tf_op jit(solution)/shard_map/d_term/pallas_call | solution.py:409
  107.6 8.8 %weight_gradients.1 = (bf16[768,384]{1,0:T(8,128)(2,1)}, bf16[768,384]{1,0:T(8,128)(2,1)}, bf16[768,384]{1,0:T(8,128)(2,1)}, bf16[768,384]{1,0:T(8,128)(2,1)}) custom-call(s32[1]{0:T(128)} %bitcast.at_ref, bf16[512,1536]{1,0:T(8,128)(2,1)} %all-gather.4.cloned.1.call-done.x_ref.xa_ref, bf16[512,1536]{1,0:T(8,128)(2,1)} %copy-done.8, ...), custom_call_target="tpu_custom_call" | custom-call | flops 1000 | bytes 1000 | tf_op jit(solution)/shard_map/weight_gradients/pallas_call | solution.py:458
  119.9 19.0 %reduce-scatter.5.cloned.1.call-done = bf16[1,4,32,1536]{3,2,1,0:T(8,128)(2,1)} async-done(((bf16[4,4,32,1536]{3,2,1,0:T(8,128)(2,1)}), bf16[1,4,32,1536]{3,2,1,0:T(8,128)(2,1)}) %reduce-scatter.5.cloned.1.call-update) | async-done | bytes 393232 | tf_op jit(solution)/shard_map/reduce_scatter | solution.py:642
  141.5 7.4 %collective-permute-done.13.near_ref = bf16[2,32,1536]{2,1,0:T(8,128)(2,1)S(1)} collective-permute-done((bf16[2,32,1536]{2,1,0:T(8,128)(2,1)S(1)}, bf16[2,32,1536]{2,1,0:T(8,128)(2,1)S(1)}, u32[]{:S(2)}, u32[]{:S(2)}) %collective-permute-start.13) | collective-permute-done | bytes 196640 | tf_op jit(solution)/shard_map/ppermute | solution.py:579
  159.2 3.9 %collective-permute-start.19 = (bf16[2,4,1,1536]{3,2,1,0:T(2,128)(2,1)S(1)}, bf16[2,4,1,1536]{3,2,1,0:T(2,128)(2,1)S(1)}, u32[]{:S(2)}, u32[]{:S(2)}) collective-permute-start(bf16[2,4,1,1536]{3,2,1,0:T(2,128)(2,1)S(1)} %get-tuple-element.91.refs_1_), channel_id=1, source_target_pairs={{1,0},{2,1},{3,2},{4,3},{5,4},{6,5},{7,6},{8,7},{9,8},{10,9},{11,1... | collective-permute-start | bytes 73736 | tf_op jit(solution)/shard_map/ppermute | solution.py:570
  163.9 4.4 %copy-done = bf16[5,768,1536]{2,1,0:T(8,128)(2,1)S(1)} copy-done((bf16[5,768,1536]{2,1,0:T(8,128)(2,1)S(1)}, bf16[5,768,1536]{2,1,0:T(8,128)(2,1)}, u32[]{:S(2)}) %copy-start) | copy-done | bytes 11796504
  169.0 5.4 %collective-permute-start.23 = (bf16[384,768]{1,0:T(8,128)(2,1)}, bf16[384,768]{1,0:T(8,128)(2,1)S(1)}, u32[]{:S(2)}, u32[]{:S(2)}) collective-permute-start(bf16[384,768]{1,0:T(8,128)(2,1)} %constant_dynamic-update-slice_fusion.6.refs_1_), channel_id=1, source_target_pairs={{0,4},{4,0},{8,12},{12,8},{16,20},{20,16},{24,28},{28,24},{1,5},{5... | collective-permute-start | bytes 1769480 | tf_op jit(solution)/shard_map/ppermute | solution.py:584
  177.4 4.3 %encoder_backward.1 = bf16[256,768]{1,0:T(8,128)(2,1)S(1)} custom-call(bf16[2,4,32,1536]{3,2,1,0:T(8,128)(2,1)S(1)} %get-tuple-element.89.d_ref, bf16[2,4,1,1536]{3,2,1,0:T(2,128)(2,1)S(1)} %collective-permute-done.18.low_ref, bf16[2,4,1,1536]{3,2,1,0:T(2,128)(2,1)S(1)} %collective-permute-done.19.high_ref, bf16[5,768,1536]{2,1,0:T(8,128)(2,1)S(1)} %bitcast.47, ...), custom_call_target="tpu_custom_call" | custom-call | flops 1000 | bytes 1000 | tf_op jit(solution)/shard_map/encoder_backward/pallas_call | solution.py:245
  185.2 6.0 %collective-permute-done.28.refs_1_ = bf16[384,768]{1,0:T(8,128)(2,1)} collective-permute-done((bf16[384,768]{1,0:T(8,128)(2,1)}, bf16[384,768]{1,0:T(8,128)(2,1)}, u32[]{:S(2)}, u32[]{:S(2)}) %collective-permute-start.28) | collective-permute-done | bytes 589856 | tf_op jit(solution)/shard_map/ppermute | solution.py:579
  197.4 5.0 %weight_outputs_near.1 = (f32[3,1536,384]{2,1,0:T(8,128)}, f32[2,2,96,1536]{3,2,1,0:T(8,128)}, f32[8,128]{1,0:T(8,128)S(1)}) custom-call(s32[2]{0:T(128)S(1)} %copy-done.25, bf16[384,768]{1,0:T(8,128)(2,1)} %constant_dynamic-update-slice_fusion.4.refs_0_, bf16[384,768]{1,0:T(8,128)(2,1)} %constant_dynamic-update-slice_fusion.6.refs_1_, ...), custom_call_target="tpu_custom_call" | custom-call | flops 1000 | bytes 1000 | tf_op jit(solution)/shard_map/weight_outputs_near/pallas_call | solution.py:539
  205.1 5.0 %weight_outputs_far.1 = (f32[3,1536,384]{2,1,0:T(8,128)}, f32[2,2,96,1536]{3,2,1,0:T(8,128)}, f32[8,128]{1,0:T(8,128)}) custom-call(s32[2]{0:T(128)S(1)} %copy-done.25, bf16[384,768]{1,0:T(8,128)(2,1)} %collective-permute-done.27.refs_0_, bf16[384,768]{1,0:T(8,128)(2,1)} %collective-permute-done.28.refs_1_, ...), custom_call_target="tpu_custom_call", output_to_operand_aliasing={{0}: (5, {}), {1}: (6, {})} | custom-call | flops 1000 | bytes 1000 | tf_op jit(solution)/shard_map/weight_outputs_far/pallas_call | solution.py:539
  (160 shorter events, 67.2 us)
Async XLA Ops:
  7.2 38.4 %all-gather.6.cloned.1.call-start = ((), (), s32[]{:S(2)}) async-start(), calls=%async_computation.5 | async-start | bytes 1966080 | tf_op jit(solution)/shard_map/all_gather | solution.py:607
  7.9 75.8 %all-gather.4.cloned.1.call-start = ((), (), s32[]{:S(2)}) async-start(), calls=%async_computation.2 | async-start | bytes 1966080 | tf_op jit(solution)/shard_map/all_gather | solution.py:614
  9.1 9.3 %collective-permute-start.1 = (bf16[2,4,1,768]{3,2,1,0:T(2,128)(2,1)S(1)}, bf16[2,4,1,768]{3,2,1,0:T(2,128)(2,1)S(1)}, u32[]{:S(2)}, u32[]{:S(2)}) collective-permute-start(bf16[2,4,1,768]{3,2,1,0:T(2,128)(2,1)S(1)} %get-tuple-element.126), channel_id=1, source_target_pairs={{1,0},{2,1},{3,2},{4,3},{5,4},{6,5},{7,6},{8,7},{9,8},{10,9},{11,1... | collective-permute-start | bytes 36872 | tf_op jit(solution)/shard_map/ppermute | solution.py:570
  39.7 99.2 %reduce-scatter.5.cloned.1.call-start = ((), (), s32[]{:S(2)}) async-start(), calls=%async_computation.4 | async-start | bytes 1966080 | tf_op jit(solution)/shard_map/reduce_scatter | solution.py:642
  47.4 13.0 %collective-permute-start.7 = (bf16[4,32,1536]{2,1,0:T(8,128)(2,1)S(1)}, bf16[4,32,1536]{2,1,0:T(8,128)(2,1)S(1)}, u32[]{:S(2)}, u32[]{:S(2)}) collective-permute-start(bf16[4,32,1536]{2,1,0:T(8,128)(2,1)S(1)} %get-tuple-element.119), channel_id=1, source_target_pairs={{0,24},{4,28},{8,16},{12,20},{16,8},{20,12},{24,0},{28,4},{1,25},{... | collective-permute-start | bytes 1179656 | tf_op jit(solution)/shard_map/ppermute | solution.py:579
  48.9 19.0 %collective-permute-start.6 = (bf16[4,32,1536]{2,1,0:T(8,128)(2,1)S(1)}, bf16[4,32,1536]{2,1,0:T(8,128)(2,1)S(1)}, u32[]{:S(2)}, u32[]{:S(2)}) collective-permute-start(bf16[4,32,1536]{2,1,0:T(8,128)(2,1)S(1)} %get-tuple-element.120), channel_id=1, source_target_pairs={{0,8},{4,12},{8,0},{12,4},{16,24},{20,28},{24,16},{28,20},{1,9},{5... | collective-permute-start | bytes 1179656 | tf_op jit(solution)/shard_map/ppermute | solution.py:579
  50.4 17.5 %collective-permute-start.5 = (bf16[4,32,1536]{2,1,0:T(8,128)(2,1)S(1)}, bf16[4,32,1536]{2,1,0:T(8,128)(2,1)S(1)}, u32[]{:S(2)}, u32[]{:S(2)}) collective-permute-start(bf16[4,32,1536]{2,1,0:T(8,128)(2,1)S(1)} %get-tuple-element.121), channel_id=1, source_target_pairs={{0,16},{4,20},{8,24},{12,28},{16,0},{20,4},{24,8},{28,12},{1,17},{... | collective-permute-start | bytes 1179656 | tf_op jit(solution)/shard_map/ppermute | solution.py:579
  68.3 15.5 %collective-permute-start.9 = (bf16[512,1536]{1,0:T(8,128)(2,1)S(1)}, bf16[512,1536]{1,0:T(8,128)(2,1)}, u32[]{:S(2)}, u32[]{:S(2)}) collective-permute-start(bf16[512,1536]{1,0:T(8,128)(2,1)S(1)} %bitcast.48), channel_id=1, source_target_pairs={{0,4},{4,0},{8,12},{12,8},{16,20},{20,16},{24,28},{28,24},{1,5},{5... | collective-permute-start | bytes 4718600 | tf_op jit(solution)/shard_map/ppermute | solution.py:584
  70.5 13.2 %collective-permute-start.8 = (bf16[512,256]{1,0:T(8,128)(2,1)S(1)}, bf16[512,256]{1,0:T(8,128)(2,1)S(1)}, u32[]{:S(2)}, u32[]{:S(2)}) collective-permute-start(bf16[512,256]{1,0:T(8,128)(2,1)S(1)} %get-tuple-element.60), channel_id=1, source_target_pairs={{0,4},{4,0},{8,12},{12,8},{16,20},{20,16},{24,28},{28,24},{1,5},{5... | collective-permute-start | bytes 786440 | tf_op jit(solution)/shard_map/ppermute | solution.py:584
  104.5 79.6 %reduce-scatter.3.cloned.1.call-start = ((), (), s32[]{:S(2)}) async-start(), calls=%async_computation.3 | async-start | bytes 1966080 | tf_op jit(solution)/shard_map/reduce_scatter | solution.py:657
  116.4 34.1 %collective-permute-start.15 = (bf16[768,384]{1,0:T(8,128)(2,1)}, bf16[768,384]{1,0:T(8,128)(2,1)}, u32[]{:S(2)}, u32[]{:S(2)}) collective-permute-start(bf16[768,384]{1,0:T(8,128)(2,1)} %get-tuple-element.85), channel_id=1, source_target_pairs={{0,8},{4,12},{8,0},{12,4},{16,24},{20,28},{24,16},{28,20},{1,9},{5... | collective-permute-start | bytes 1769480 | tf_op jit(solution)/shard_map/ppermute | solution.py:579
  117.0 33.5 %collective-permute-start.16 = (bf16[768,384]{1,0:T(8,128)(2,1)}, bf16[768,384]{1,0:T(8,128)(2,1)}, u32[]{:S(2)}, u32[]{:S(2)}) collective-permute-start(bf16[768,384]{1,0:T(8,128)(2,1)} %get-tuple-element.86), channel_id=1, source_target_pairs={{0,16},{4,20},{8,24},{12,28},{16,0},{20,4},{24,8},{28,12},{1,17},{... | collective-permute-start | bytes 1769480 | tf_op jit(solution)/shard_map/ppermute | solution.py:579
  118.4 32.1 %collective-permute-start.17 = (bf16[768,384]{1,0:T(8,128)(2,1)}, bf16[768,384]{1,0:T(8,128)(2,1)}, u32[]{:S(2)}, u32[]{:S(2)}) collective-permute-start(bf16[768,384]{1,0:T(8,128)(2,1)} %get-tuple-element.87), channel_id=1, source_target_pairs={{0,24},{4,28},{8,16},{12,20},{16,8},{20,12},{24,0},{28,4},{1,25},{... | collective-permute-start | bytes 1769480 | tf_op jit(solution)/shard_map/ppermute | solution.py:579
  139.9 9.0 %collective-permute-start.13 = (bf16[2,32,1536]{2,1,0:T(8,128)(2,1)S(1)}, bf16[2,32,1536]{2,1,0:T(8,128)(2,1)S(1)}, u32[]{:S(2)}, u32[]{:S(2)}) collective-permute-start(bf16[2,32,1536]{2,1,0:T(8,128)(2,1)S(1)} %slice_bitcast_fusion.refs_4_), channel_id=1, source_target_pairs={{0,8},{4,12},{8,0},{12,4},{16,24},{20,28},{24,16},{28,20},{1,9},{5... | collective-permute-start | bytes 589832 | tf_op jit(solution)/shard_map/ppermute | solution.py:579
  152.5 15.8 %collective-permute-start.22 = (bf16[192,768]{1,0:T(8,128)(2,1)S(1)}, bf16[192,768]{1,0:T(8,128)(2,1)S(1)}, u32[]{:S(2)}, u32[]{:S(2)}) collective-permute-start(bf16[192,768]{1,0:T(8,128)(2,1)S(1)} %get-tuple-element.96), channel_id=1, source_target_pairs={{0,16},{4,20},{8,24},{12,28},{16,0},{20,4},{24,8},{28,12},{1,17},{... | collective-permute-start | bytes 884744 | tf_op jit(solution)/shard_map/ppermute | solution.py:579
  153.2 15.1 %collective-permute-start.20 = (bf16[192,768]{1,0:T(8,128)(2,1)S(1)}, bf16[192,768]{1,0:T(8,128)(2,1)S(1)}, u32[]{:S(2)}, u32[]{:S(2)}) collective-permute-start(bf16[192,768]{1,0:T(8,128)(2,1)S(1)} %get-tuple-element.88.refs_4_), channel_id=1, source_target_pairs={{0,8},{4,12},{8,0},{12,4},{16,24},{20,28},{24,16},{28,20},{1,9},{5... | collective-permute-start | bytes 884744 | tf_op jit(solution)/shard_map/ppermute | solution.py:579
  157.3 11.0 %collective-permute-start.18 = (bf16[2,4,1,1536]{3,2,1,0:T(2,128)(2,1)S(1)}, bf16[2,4,1,1536]{3,2,1,0:T(2,128)(2,1)S(1)}, u32[]{:S(2)}, u32[]{:S(2)}) collective-permute-start(bf16[2,4,1,1536]{3,2,1,0:T(2,128)(2,1)S(1)} %get-tuple-element.90), channel_id=1, source_target_pairs={{0,1},{1,2},{2,3},{3,4},{4,5},{5,6},{6,7},{7,8},{8,9},{9,10},{10,1... | collective-permute-start | bytes 73736 | tf_op jit(solution)/shard_map/ppermute | solution.py:570
  159.2 9.1 %collective-permute-start.19 = (bf16[2,4,1,1536]{3,2,1,0:T(2,128)(2,1)S(1)}, bf16[2,4,1,1536]{3,2,1,0:T(2,128)(2,1)S(1)}, u32[]{:S(2)}, u32[]{:S(2)}) collective-permute-start(bf16[2,4,1,1536]{3,2,1,0:T(2,128)(2,1)S(1)} %get-tuple-element.91.refs_1_), channel_id=1, source_target_pairs={{1,0},{2,1},{3,2},{4,3},{5,4},{6,5},{7,6},{8,7},{9,8},{10,9},{11,1... | collective-permute-start | bytes 73736 | tf_op jit(solution)/shard_map/ppermute | solution.py:570
  175.2 16.1 %collective-permute-start.28 = (bf16[384,768]{1,0:T(8,128)(2,1)}, bf16[384,768]{1,0:T(8,128)(2,1)}, u32[]{:S(2)}, u32[]{:S(2)}) collective-permute-start(bf16[384,768]{1,0:T(8,128)(2,1)} %constant_dynamic-update-slice_fusion.6.refs_1_), channel_id=1, source_target_pairs={{0,8},{4,12},{8,0},{12,4},{16,24},{20,28},{24,16},{28,20},{1,9},{5... | collective-permute-start | bytes 1769480 | tf_op jit(solution)/shard_map/ppermute | solution.py:579
  175.2 16.1 %collective-permute-start.27 = (bf16[384,768]{1,0:T(8,128)(2,1)}, bf16[384,768]{1,0:T(8,128)(2,1)}, u32[]{:S(2)}, u32[]{:S(2)}) collective-permute-start(bf16[384,768]{1,0:T(8,128)(2,1)} %constant_dynamic-update-slice_fusion.4.refs_0_), channel_id=1, source_target_pairs={{0,16},{4,20},{8,24},{12,28},{16,0},{20,4},{24,8},{28,12},{1,17},{... | collective-permute-start | bytes 1769480 | tf_op jit(solution)/shard_map/ppermute | solution.py:579
  191.2 13.9 %collective-permute-start.29 = (bf16[384,768]{1,0:T(8,128)(2,1)}, bf16[384,768]{1,0:T(8,128)(2,1)S(1)}, u32[]{:S(2)}, u32[]{:S(2)}) collective-permute-start(bf16[384,768]{1,0:T(8,128)(2,1)} %collective-permute-done.27.refs_0_), channel_id=1, source_target_pairs={{0,4},{4,0},{8,12},{12,8},{16,20},{20,16},{24,28},{28,24},{1,5},{5... | collective-permute-start | bytes 1769480 | tf_op jit(solution)/shard_map/ppermute | solution.py:584
  191.3 13.9 %collective-permute-start.30 = (bf16[384,768]{1,0:T(8,128)(2,1)}, bf16[384,768]{1,0:T(8,128)(2,1)S(1)}, u32[]{:S(2)}, u32[]{:S(2)}) collective-permute-start(bf16[384,768]{1,0:T(8,128)(2,1)} %collective-permute-done.28.refs_1_), channel_id=1, source_target_pairs={{0,4},{4,0},{8,12},{12,8},{16,20},{20,16},{24,28},{28,24},{1,5},{5... | collective-permute-start | bytes 1769480 | tf_op jit(solution)/shard_map/ppermute | solution.py:584
  191.8 11.7 %collective-permute-start.26 = (bf16[32,1536]{1,0:T(8,128)(2,1)S(1)}, bf16[32,1536]{1,0:T(8,128)(2,1)S(1)}, u32[]{:S(2)}, u32[]{:S(2)}) collective-permute-start(bf16[32,1536]{1,0:T(8,128)(2,1)S(1)} %get-tuple-element.122), channel_id=1, source_target_pairs={{0,24},{4,28},{8,16},{12,20},{16,8},{20,12},{24,0},{28,4},{1,25},{... | collective-permute-start | bytes 294920 | tf_op jit(solution)/shard_map/ppermute | solution.py:579
  193.2 10.2 %collective-permute-start.25 = (bf16[32,1536]{1,0:T(8,128)(2,1)S(1)}, bf16[32,1536]{1,0:T(8,128)(2,1)S(1)}, u32[]{:S(2)}, u32[]{:S(2)}) collective-permute-start(bf16[32,1536]{1,0:T(8,128)(2,1)S(1)} %get-tuple-element.123), channel_id=1, source_target_pairs={{0,16},{4,20},{8,24},{12,28},{16,0},{20,4},{24,8},{28,12},{1,17},{... | collective-permute-start | bytes 294920 | tf_op jit(solution)/shard_map/ppermute | solution.py:579
  (45 other events, 331.8 us)
Sparse Core Ops, SparseCore 0:
  9.6 35.9 all-gather.5
  47.7 35.9 all-gather.3
  104.6 34.2 reduce-scatter.4
  141.6 36.3 reduce-scatter.2

commit v13 on v10

--- a/solution.py
+++ b/solution.py
@@ -410,6 +410,38 @@
     )(head, mine, got, weight, *deps)
 
 
+def part_kernel(head_ref, x_ref, w_ref, *rest, last):
+    del head_ref
+    total = dot(x_ref[:, :last], w_ref[0], NN)
+    if len(rest) > 1:
+        total += rest[0][...]
+    rest[-1][...] = total.astype(rest[-1].dtype)
+
+
+def term_part(head, x, weight, last, name, *before):
+    half, full = x.shape
+    _, depth, width = weight.shape
+    tile = 512 if width % 512 == 0 else width
+    column = pl.BlockSpec((half, tile), lambda n, at: (0, n))
+    return pl.pallas_call(
+        functools.partial(part_kernel, last=last),
+        grid_spec=pltpu.PrefetchScalarGridSpec(
+            num_scalar_prefetch=1,
+            grid=(width // tile,),
+            in_specs=[
+                pl.BlockSpec((half, full), lambda n, at: (0, 0)),
+                pl.BlockSpec((1, depth, tile), lambda n, at: (at[0], 0, n)),
+            ]
+            + [column] * len(before),
+            out_specs=column,
+        ),
+        out_shape=jax.ShapeDtypeStruct((half, width), BF if before else F32),
+        compiler_params=params(),
+        cost_estimate=COST,
+        name=name,
+    )(head, x, weight, *before)
+
+
 def weight_kernel(at_ref, xa_ref, xb_ref, ga_ref, gb_ref, ra_ref, rb_ref, *rest):
     del at_ref
     out_refs, turned = rest[:-1], rest[-1]
@@ -425,12 +457,17 @@
     a, b = slice(0, half), slice(half, 2 * half)
     qkv = dot(turned[:split, a], xa_ref[...], NN) + dot(turned[:split, b], xb_ref[...], NN)
     out = dot(turned[split:, a], ga_ref[...], NN) + dot(turned[split:, b], gb_ref[...], NN)
-    for slot, out_ref in enumerate(out_refs):
+    keep_a, send_a, keep_b, send_b = out_refs
+    rows = keep_a.shape[1]
+    for slot in range(4):
 
         @pl.when(step == slot)
         def _():
-            out_ref[:split, :] = qkv.astype(BF)
-            out_ref[split:, :] = out.astype(BF)
+            first = keep_a if slot % 2 == 0 else send_a
+            second = keep_b if slot < 2 else send_b
+            first[slot // 2] = qkv[:rows].astype(BF)
+            second[slot % 2, : split - rows] = qkv[rows:].astype(BF)
+            second[slot % 2, split - rows :] = out.astype(BF)
 
 
 def weight_gradients(at, xa, xb, ga, gb, ra, rb, seqs):
@@ -445,22 +482,39 @@
             num_scalar_prefetch=1,
             grid=(seqs,),
             in_specs=[column] * 4 + [rest] * 2,
-            out_specs=[pl.BlockSpec((full, chunk), lambda r, at: (0, 0))] * seqs,
+            out_specs=[pl.BlockSpec((2, full // 2, chunk), lambda r, at: (0, 0, 0))] * 4,
             scratch_shapes=[pltpu.VMEM((full, 2 * half), BF)],
         ),
-        out_shape=[jax.ShapeDtypeStruct((full, chunk), BF)] * seqs,
+        out_shape=[jax.ShapeDtypeStruct((2, full // 2, chunk), BF)] * 4,
         compiler_params=params(STREAMING_LIMIT),
         cost_estimate=COST,
         name="weight_gradients",
     )(at, xa, xb, ga, gb, ra, rb)
 
 
-def weight_sum_kernel(*refs, count):
-    part_refs, out_refs = refs[:count], refs[-2:]
+def turn_kernel(keep_a, got_a, keep_b, got_b, out_a, out_b):
+    for keep, got, out in ((keep_a, got_a, out_a), (keep_b, got_b, out_b)):
+        out[...] = (keep[1].astype(F32) + got[1].astype(F32)).astype(BF)
+
+
+def weight_turn(keep_a, got_a, keep_b, got_b):
+    shape = jax.ShapeDtypeStruct(keep_a.shape[1:], BF)
+    return pl.pallas_call(
+        turn_kernel,
+        out_shape=[shape, shape],
+        compiler_params=params(),
+        cost_estimate=COST,
+        name="weight_turn",
+    )(keep_a, got_a, keep_b, got_b)
+
+
+def weight_sum_kernel(keep_a, got_a, last_a, keep_b, got_b, last_b, *out_refs):
     split = 3 * DH
-    total = part_refs[0][...].astype(F32)
-    for ref in part_refs[1:]:
-        total = total + ref[...].astype(F32)
+    parts = [
+        keep[0].astype(F32) + got[0].astype(F32) + last[...].astype(F32)
+        for keep, got, last in ((keep_a, got_a, last_a), (keep_b, got_b, last_b))
+    ]
+    total = jnp.concatenate(parts, axis=0)
     turned = total[:split].T.astype(BF)
     quarter = DH // 2
     for part, out_ref in enumerate(out_refs):
@@ -471,16 +525,15 @@
         out_ref[quarter:, split:] = piece[:, DH:]
 
 
-def weight_sum(parts, *deps):
-    full, chunk = parts[0].shape
-    return pl.pallas_call(
-        functools.partial(weight_sum_kernel, count=len(parts)),
-        in_specs=[pl.BlockSpec(memory_space=pltpu.VMEM)] * len(parts) + spare(deps),
-        out_shape=[jax.ShapeDtypeStruct((chunk // 2, full), BF)] * 2,
+def weight_sum(*parts):
+    _, rows, chunk = parts[0].shape
+    return pl.pallas_call(
+        weight_sum_kernel,
+        out_shape=[jax.ShapeDtypeStruct((chunk // 2, 2 * rows), BF)] * 2,
         compiler_params=params(),
         cost_estimate=COST,
         name="weight_sum",
-    )(*parts, *deps)
+    )(*parts)
 
 
 def unpack_kernel(at_ref, *refs):
@@ -622,9 +675,10 @@
     result_got = swap_heads(result_other)
 
     shape = (groups, seqs, rows, width)
-    d_term = pair_term(head_mine, result_mine, result_got, w_turned, 0, 3 * DH, "d_term")
+    d_own = term_part(head_mine, result_mine, w_turned, 3 * DH, "d_term_own")
+    d_term = term_part(head_other, result_got, w_turned, 3 * DH, "d_term", d_own)
     d_normed = lax.psum_scatter(d_term.reshape(shape), "head", scatter_dimension=0, tiled=False)
-    part = weight_gradients(
+    keep_a, send_a, keep_b, send_b = weight_gradients(
         own_seq.reshape(1),
         normed_rows,
         normed_swapped,
@@ -634,30 +688,33 @@
         result_other,
         seqs,
     )
-    part = to_chips(part)
+    got_a, got_b = trade_chip(send_a, 1, heads), trade_chip(send_b, 2, heads)
+    turn_a, turn_b = weight_turn(keep_a, got_a, keep_b, got_b)
+    last_a, last_b = trade_chip(turn_a, 2, heads), trade_chip(turn_b, 1, heads)
+    half_a, half_b = weight_sum(keep_a, got_a, last_a, keep_b, got_b, last_b)
     head_term = pair_term(
         head_mine, result_mine, result_got, w_rows, 3 * DH, 4 * DH, "head_term"
     )
     head_sum = lax.psum_scatter(head_term.reshape(shape), "head", scatter_dimension=0, tiled=False)
 
+    d_normed = after(d_normed, last_a, last_b)
     leaving = d_normed[2:]
+    got_a, got_b = trade_chip(half_a, 1, heads), trade_chip(half_b, 2, heads)
+    near_a = jnp.concatenate([half_a, after(got_a, leaving)], axis=0)
+    near_b = jnp.concatenate([half_b, after(got_b, leaving)], axis=0)
+    far_a = trade_chip(near_a, 2, heads)
+    far_b = trade_chip(near_b, 1, heads)
+    near_other = [swap_heads(near_a), swap_heads(near_b)]
+
     near = trade_chip(leaving, 1, heads)
     far = trade_chip(jnp.stack([d_normed[1], near[1]]), 2, heads)
     grad = jnp.transpose(after(grad_out, d_term), (1, 0, 2))
-    half_a, half_b = weight_sum(part, leaving)
     d_conv, first, last = conv_gradient(
-        at, d_normed, near, far, skip, grad, norm_gain, slope, half_a
+        at, d_normed, near, far, skip, grad, norm_gain, slope, near_a, near_b
     )
     low, high = neighbour_edges(first, last)
-
-    got_a = trade_chip(half_a, 1, heads)
-    got_b = trade_chip(half_b, 2, heads)
-    near_a = jnp.concatenate([half_a, after(got_a, low)], axis=0)
-    near_b = jnp.concatenate([half_b, after(got_b, low)], axis=0)
-    far_a = trade_chip(near_a, 2, heads)
-    far_b = trade_chip(near_b, 1, heads)
-    near_other = [swap_heads(near_a), swap_heads(near_b)]
     *outputs, token = unpack_weights(at, [near_a, near_b], near_other, False)
+    low, high, token = lax.optimization_barrier((low, high, token))
     grad_input = conv_back(d_conv, low, high, conv_weight, token)
 
     head_sum = after(head_sum, grad_input)

time: 211 us -> 213 us (level)
  waiting for transfers between devices: 74.4 us -> 66 us
  starting transfers between devices: 35.2 us -> 42 us
    reduce_scatter x1, waiting for transfers between devices: 19.1 us -> 0.02 us  [unit_body(): lax.psum_scatter(d_term.reshape(shape), 'head', scatter_dimension=0, tile...]
    ppermute x18 -> x19, waiting for transfers between devices: 38.2 us -> 56.1 us  [trade_chip(): return lax.ppermute(x, 'seq', [(s, s ^ bit * heads) for s in range(count)])]
    ppermute x2, waiting for transfers between devices: 5.18 us -> 0.01 us  [neighbour_edges(): lax.ppermute(last, axes, forward)]
    pallas_call x1 -> x4, Pallas kernels: 0.4 us -> 5.52 us  [the longest x2 5.05 us: term_part(): pl.pallas_call(functools.partial(part_kernel, last=last), grid_spec=pltpu...]
    pallas_call x2 -> x1, Pallas kernels: 5.65 us -> 1.64 us  [pair_term(): pl.pallas_call(functools.partial(term_kernel, first=first, last=last), gr...]
    ppermute x9, starting transfers between devices: 3.11 us -> 6.63 us  [swap_heads(): lax.ppermute(x, 'seq', [(s, s + 1 - 2 * (s % 2)) for s in range(count)])]
    unnamed x62 -> x64, local copies, waits for them, and re-layouts: 21.1 us -> 23.8 us
    ppermute x18 -> x19, starting transfers between devices: 19.8 us -> 21.8 us  [trade_chip(): return lax.ppermute(x, 'seq', [(s, s ^ bit * heads) for s in range(count)])]
  transfers between devices with their start and end apart: 35 -> 36, of which waited for: 16 -> 18; matrix products, arithmetic and copies ran while one was open for 5% -> 5% of each run, Pallas kernels for 19% -> 20%
where the time goes in v13:
time: 213 us; the launch traced here: 209 us
  waiting for transfers between devices  66 us (31%)
  Pallas kernels  54.3 us (25%)
  starting transfers between devices  42 us (20%)
  local copies, waits for them, and re-layouts  31.5 us (15%)
  between operations  14.3 us (7%)
    ppermute x19, waiting for transfers between devices, trade_chip(): return lax.ppermute(x, 'seq', [(s, s ^ bit * heads) for s in range(count)])  56.1 us
    unnamed x64, local copies, waits for them, and re-layouts  23.8 us
    ppermute x19, starting transfers between devices, trade_chip(): return lax.ppermute(x, 'seq', [(s, s ^ bit * heads) for s in range(count)])  21.8 us
    pallas_call x1, Pallas kernels, encoder(): pl.pallas_call(conv_kernel, grid=(width // tile,), in_specs=[SCALARS, who...  10.1 us
    pallas_call x1, Pallas kernels, weight_gradients(): pl.pallas_call(weight_kernel, grid_spec=pltpu.PrefetchScalarGridSpec(num_...  8.74 us
    ppermute x2, starting transfers between devices, neighbour_edges(): lax.ppermute(last, axes, forward)  6.92 us
    pallas_call x2, Pallas kernels, unpack_weights(): pl.pallas_call(unpack_kernel, grid_spec=pltpu.PrefetchScalarGridSpec(num_...  6.83 us
    ppermute x9, starting transfers between devices, swap_heads(): lax.ppermute(x, 'seq', [(s, s + 1 - 2 * (s % 2)) for s in range(count)])  6.63 us
  transfers between devices with their start and end apart: 36, of which 18 were waited for; matrix products, arithmetic and copies ran while one was open for 5% of the time, Pallas kernels for 20%

profile of v13, /device:TPU:26, one launch (start us, length us, event | category | flops | bytes accessed | tf_op | source)
XLA Modules:
  0.0 208.9 jit_solution(17093133920634508999)
XLA Ops:
  9.1 2.4 %collective-permute-start.1 = (bf16[2,4,1,768]{3,2,1,0:T(2,128)(2,1)S(1)}, bf16[2,4,1,768]{3,2,1,0:T(2,128)(2,1)S(1)}, u32[]{:S(2)}, u32[]{:S(2)}) collective-permute-start(bf16[2,4,1,768]{3,2,1,0:T(2,128)(2,1)S(1)} %get-tuple-element.132), channel_id=1, source_target_pairs={{1,0},{2,1},{3,2},{4,3},{5,4},{6,5},{7,6},{8,7},{9,8},{10,9},{11,1... | collective-permute-start | bytes 36872 | tf_op jit(solution)/shard_map/ppermute | solution.py:607
  11.4 5.0 %collective-permute-start = (bf16[2,4,1,768]{3,2,1,0:T(2,128)(2,1)S(1)}, bf16[2,4,1,768]{3,2,1,0:T(2,128)(2,1)S(1)}, u32[]{:S(2)}, u32[]{:S(2)}) collective-permute-start(bf16[2,4,1,768]{3,2,1,0:T(2,128)(2,1)S(1)} %get-tuple-element.133), channel_id=1, source_target_pairs={{0,1},{1,2},{2,3},{3,4},{4,5},{5,6},{6,7},{7,8},{8,9},{9,10},{10,1... | collective-permute-start | bytes 36872 | tf_op jit(solution)/shard_map/ppermute | solution.py:607
  19.6 10.1 %encoder_forward.1 = (bf16[4,32,1536]{2,1,0:T(8,128)(2,1)}, f32[2,4,32,1536]{3,2,1,0:T(8,128)}, bf16[32,1536]{1,0:T(8,128)(2,1)}, bf16[32,1536]{1,0:T(8,128)(2,1...) custom-call(s32[2]{0:T(128)} %pad_add_fusion.at_ref, bf16[2,4,32,768]{3,2,1,0:T(8,128)(2,1)} %bitcast.59, ...), custom_call_target="tpu_custom_call" | custom-call | flops 1000 | bytes 1000 | tf_op jit(solution)/shard_map/encoder_forward/pallas_call | solution.py:111
  35.0 2.1 %collective-permute-done.3 = bf16[32,1536]{1,0:T(8,128)(2,1)S(1)} collective-permute-done((bf16[32,1536]{1,0:T(8,128)(2,1)}, bf16[32,1536]{1,0:T(8,128)(2,1)S(1)}, u32[]{:S(2)}, u32[]{:S(2)}) %collective-permute-start.3) | collective-permute-done | bytes 98336 | tf_op jit(solution)/shard_map/ppermute | solution.py:616
  39.7 5.9 %all-gather.6.cloned.1.call-done = bf16[128,4,1536]{2,1,0:T(4,128)(2,1)} async-done(((bf16[32,4,1536]{2,1,0:T(4,128)(2,1)}), bf16[128,4,1536]{2,1,0:T(4,128)(2,1)}) %all-gather.6.cloned.1.call-update) | async-done | bytes 1572880 | tf_op jit(solution)/shard_map/all_gather | solution.py:644
  51.0 9.4 %collective-permute-done.7 = bf16[4,32,1536]{2,1,0:T(8,128)(2,1)S(1)} collective-permute-done((bf16[4,32,1536]{2,1,0:T(8,128)(2,1)S(1)}, bf16[4,32,1536]{2,1,0:T(8,128)(2,1)S(1)}, u32[]{:S(2)}, u32[]{:S(2)}) %collective-permute-start.7) | collective-permute-done | bytes 393248 | tf_op jit(solution)/shard_map/ppermute | solution.py:616
  60.4 7.5 %collective-permute-done.6 = bf16[4,32,1536]{2,1,0:T(8,128)(2,1)S(1)} collective-permute-done((bf16[4,32,1536]{2,1,0:T(8,128)(2,1)S(1)}, bf16[4,32,1536]{2,1,0:T(8,128)(2,1)S(1)}, u32[]{:S(2)}, u32[]{:S(2)}) %collective-permute-start.6) | collective-permute-done | bytes 393248 | tf_op jit(solution)/shard_map/ppermute | solution.py:616
  72.6 3.9 %pack_weights.1 = (bf16[2,1536,576]{2,1,0:T(8,128)(2,1)S(1)}, bf16[2,576,1536]{2,1,0:T(8,128)(2,1)S(1)}, f32[8,128]{1,0:T(8,128)S(1)}) custom-call(bf16[3,1536,384]{2,1,0:T(8,128)(2,1)S(1)} %copy-done.11), custom_call_target="tpu_custom_call" | custom-call | flops 1000 | bytes 1000 | tf_op jit(solution)/shard_map/pack_weights/pallas_call | solution.py:265
  81.5 2.2 %all-gather.4.cloned.1.call-done.x_ref.xa_ref = bf16[512,1536]{1,0:T(8,128)(2,1)} async-done(((bf16[128,1536]{1,0:T(8,128)(2,1)}), bf16[512,1536]{1,0:T(8,128)(2,1)}) %all-gather.4.cloned.1.call-update) | async-done | bytes 1572880 | tf_op jit(solution)/shard_map/all_gather | solution.py:651
  92.3 6.5 %attention.1 = (bf16[512,768]{1,0:T(8,128)(2,1)S(1)}, bf16[512,768]{1,0:T(8,128)(2,1)S(1)}) custom-call(bf16[512,640]{1,0:T(8,128)(2,1)S(1)} %get-tuple-element.73.qa_ref, bf16[512,640]{1,0:T(8,128)(2,1)S(1)} %collective-permute-done.10.qb_ref, bf16[512,256]{1,0:T(8,128)(2,1)S(1)} %copy-done.21, bf16[512,256]{1,0:T(8,128)(2,1)S(1)} %copy-done.19, ...), custom_call_target="tpu_custom_call" | custom-call | flops 1000 | bytes 1000 | tf_op jit(solution)/shard_map/attention/pallas_call | solution.py:366
  101.2 3.0 %d_term.1 = bf16[512,1536]{1,0:T(8,128)(2,1)} custom-call(s32[1]{0:T(128)} %bitcast.4.head_ref, bf16[512,768]{1,0:T(8,128)(2,1)S(1)} %collective-permute-done.12.b_ref.x_ref, bf16[2,576,1536]{2,1,0:T(8,128)(2,1)S(1)} %copy-done.5, f32[512,1536]{1,0:T(8,128)S(1)} %d_term_own.1.rest_0_), custom_call_target="tpu_custom_call" | custom-call | flops 1000 | bytes 1000 | tf_op jit(solution)/shard_map/d_term/pallas_call | solution.py:426
  107.2 8.7 %weight_gradients.1 = (bf16[2,384,384]{2,1,0:T(8,128)(2,1)}, bf16[2,384,384]{2,1,0:T(8,128)(2,1)}, bf16[2,384,384]{2,1,0:T(8,128)(2,1)}, bf16[2,384,384]{2,1,0:T(8,128)(2,1)}) custom-call(s32[1]{0:T(128)} %bitcast.at_ref, bf16[512,1536]{1,0:T(8,128)(2,1)} %all-gather.4.cloned.1.call-done.x_ref.xa_ref, bf16[512,1536]{1,0:T(8,128)(2,1)} %copy-done.10, ...), custom_call_target="tpu_custom_call" | custom-call | flops 1000 | bytes 1000 | tf_op jit(solution)/shard_map/weight_gradients/pallas_call | solution.py:479
  118.0 13.7 %collective-permute-done.13.got_a = bf16[2,384,384]{2,1,0:T(8,128)(2,1)S(1)} collective-permute-done((bf16[2,384,384]{2,1,0:T(8,128)(2,1)}, bf16[2,384,384]{2,1,0:T(8,128)(2,1)S(1)}, u32[]{:S(2)}, u32[]{:S(2)}) %collective-permute-start.13) | collective-permute-done | bytes 589856 | tf_op jit(solution)/shard_map/ppermute | solution.py:616
  137.3 5.3 %collective-permute-done.15.last_a = bf16[384,384]{1,0:T(8,128)(2,1)S(1)} collective-permute-done((bf16[384,384]{1,0:T(8,128)(2,1)S(1)}, bf16[384,384]{1,0:T(8,128)(2,1)S(1)}, u32[]{:S(2)}, u32[]{:S(2)}) %collective-permute-start.15) | collective-permute-done | bytes 294944 | tf_op jit(solution)/shard_map/ppermute | solution.py:616
  148.1 3.1 %collective-permute-done.20 = bf16[192,768]{1,0:T(8,128)(2,1)S(1)} collective-permute-done((bf16[192,768]{1,0:T(8,128)(2,1)S(1)}, bf16[192,768]{1,0:T(8,128)(2,1)S(1)}, u32[]{:S(2)}, u32[]{:S(2)}) %collective-permute-start.20) | collective-permute-done | bytes 294944 | tf_op jit(solution)/shard_map/ppermute | solution.py:616
  151.2 2.4 %collective-permute-done.19 = bf16[192,768]{1,0:T(8,128)(2,1)S(1)} collective-permute-done((bf16[192,768]{1,0:T(8,128)(2,1)S(1)}, bf16[192,768]{1,0:T(8,128)(2,1)S(1)}, u32[]{:S(2)}, u32[]{:S(2)}) %collective-permute-start.19) | collective-permute-done | bytes 294944 | tf_op jit(solution)/shard_map/ppermute | solution.py:616
  159.3 4.3 %collective-permute-done.18.far_ref = bf16[2,32,1536]{2,1,0:T(8,128)(2,1)S(1)} collective-permute-done((bf16[2,32,1536]{2,1,0:T(8,128)(2,1)S(1)}, bf16[2,32,1536]{2,1,0:T(8,128)(2,1)S(1)}, u32[]{:S(2)}, u32[]{:S(2)}) %collective-permute-start.18) | collective-permute-done | bytes 196640 | tf_op jit(solution)/shard_map/ppermute | solution.py:616
  166.7 3.9 %collective-permute-start.22 = (bf16[2,4,1,1536]{3,2,1,0:T(2,128)(2,1)S(1)}, bf16[2,4,1,1536]{3,2,1,0:T(2,128)(2,1)S(1)}, u32[]{:S(2)}, u32[]{:S(2)}) collective-permute-start(bf16[2,4,1,1536]{3,2,1,0:T(2,128)(2,1)S(1)} %get-tuple-element.100), channel_id=1, source_target_pairs={{1,0},{2,1},{3,2},{4,3},{5,4},{6,5},{7,6},{8,7},{9,8},{10,9},{11,1... | collective-permute-start | bytes 73736 | tf_op jit(solution)/shard_map/ppermute | solution.py:607
  170.6 3.4 %weight_outputs_near.1 = (f32[3,1536,384]{2,1,0:T(8,128)}, f32[2,2,96,1536]{3,2,1,0:T(8,128)}, f32[8,128]{1,0:T(8,128)S(1)}) custom-call(s32[2]{0:T(128)S(1)} %copy-done.23, bf16[384,768]{1,0:T(8,128)(2,1)S(1)} %constant_dynamic-update-slice_fusion.4.refs_4_.refs_0_, bf16[384,768]{1,0:T(8,128)(2,1)S(1)} %constant_dynamic-update-slice_fusion.6.refs_5_.refs_1_, ...), custom_call_target="tpu_custom_call" | custom-call | flops 1000 | bytes 1000 | tf_op jit(solution)/shard_map/weight_outputs_near/pallas_call | solution.py:576
  175.2 4.4 %copy-done = bf16[5,768,1536]{2,1,0:T(8,128)(2,1)S(1)} copy-done((bf16[5,768,1536]{2,1,0:T(8,128)(2,1)S(1)}, bf16[5,768,1536]{2,1,0:T(8,128)(2,1)}, u32[]{:S(2)}) %copy-start) | copy-done | bytes 11796504
  179.6 4.2 %encoder_backward.1 = bf16[256,768]{1,0:T(8,128)(2,1)S(1)} custom-call(bf16[2,4,32,1536]{3,2,1,0:T(8,128)(2,1)S(1)} %get-tuple-element.98.d_ref, bf16[2,4,1,1536]{3,2,1,0:T(2,128)(2,1)S(1)} %collective-permute-done.21.low_ref, bf16[2,4,1,1536]{3,2,1,0:T(2,128)(2,1)S(1)} %collective-permute-done.22.high_ref, bf16[5,768,1536]{2,1,0:T(8,128)(2,1)S(1)} %copy-done, ...), custom_call_target="tpu_custom_call" | custom-call | flops 1000 | bytes 1000 | tf_op jit(solution)/shard_map/encoder_backward/pallas_call | solution.py:229
  184.9 5.0 %collective-permute-start.30 = (bf16[384,768]{1,0:T(8,128)(2,1)S(1)}, bf16[384,768]{1,0:T(8,128)(2,1)S(1)}, u32[]{:S(2)}, u32[]{:S(2)}) collective-permute-start(bf16[384,768]{1,0:T(8,128)(2,1)S(1)} %collective-permute-done.28.refs_0_), channel_id=1, source_target_pairs={{0,4},{4,0},{8,12},{12,8},{16,20},{20,16},{24,28},{28,24},{1,5},{5... | collective-permute-start | bytes 1769480 | tf_op jit(solution)/shard_map/ppermute | solution.py:621
  190.2 3.2 %collective-permute-start.25 = (bf16[32,1536]{1,0:T(8,128)(2,1)S(1)}, bf16[32,1536]{1,0:T(8,128)(2,1)S(1)}, u32[]{:S(2)}, u32[]{:S(2)}) collective-permute-start(bf16[32,1536]{1,0:T(8,128)(2,1)S(1)} %get-tuple-element.130), channel_id=1, source_target_pairs={{0,8},{4,12},{8,0},{12,4},{16,24},{20,28},{24,16},{28,20},{1,9},{5... | collective-permute-start | bytes 294920 | tf_op jit(solution)/shard_map/ppermute | solution.py:616
  198.9 3.4 %weight_outputs_far.1 = (f32[3,1536,384]{2,1,0:T(8,128)}, f32[2,2,96,1536]{3,2,1,0:T(8,128)}, f32[8,128]{1,0:T(8,128)}) custom-call(s32[2]{0:T(128)S(1)} %copy-done.23, bf16[384,768]{1,0:T(8,128)(2,1)S(1)} %collective-permute-done.28.refs_0_, bf16[384,768]{1,0:T(8,128)(2,1)S(1)} %collective-permute-done.29.refs_1_, ...), custom_call_target="tpu_custom_call", output_to_operand_aliasing={{0}: (5, {}), {1}: (6, {})} | custom-call | flops 1000 | bytes 1000 | tf_op jit(solution)/shard_map/weight_outputs_far/pallas_call | solution.py:576
  (152 shorter events, 71.5 us)
Async XLA Ops:
  7.2 38.4 %all-gather.6.cloned.1.call-start = ((), (), s32[]{:S(2)}) async-start(), calls=%async_computation.5 | async-start | bytes 1966080 | tf_op jit(solution)/shard_map/all_gather | solution.py:644
  7.9 75.8 %all-gather.4.cloned.1.call-start = ((), (), s32[]{:S(2)}) async-start(), calls=%async_computation.2 | async-start | bytes 1966080 | tf_op jit(solution)/shard_map/all_gather | solution.py:651
  9.1 9.3 %collective-permute-start.1 = (bf16[2,4,1,768]{3,2,1,0:T(2,128)(2,1)S(1)}, bf16[2,4,1,768]{3,2,1,0:T(2,128)(2,1)S(1)}, u32[]{:S(2)}, u32[]{:S(2)}) collective-permute-start(bf16[2,4,1,768]{3,2,1,0:T(2,128)(2,1)S(1)} %get-tuple-element.132), channel_id=1, source_target_pairs={{1,0},{2,1},{3,2},{4,3},{5,4},{6,5},{7,6},{8,7},{9,8},{10,9},{11,1... | collective-permute-start | bytes 36872 | tf_op jit(solution)/shard_map/ppermute | solution.py:607
  39.7 106.6 %reduce-scatter.5.cloned.1.call-start = ((), (), s32[]{:S(2)}) async-start(), calls=%async_computation.4 | async-start | bytes 1966080 | tf_op jit(solution)/shard_map/reduce_scatter | solution.py:680
  47.4 13.0 %collective-permute-start.7 = (bf16[4,32,1536]{2,1,0:T(8,128)(2,1)S(1)}, bf16[4,32,1536]{2,1,0:T(8,128)(2,1)S(1)}, u32[]{:S(2)}, u32[]{:S(2)}) collective-permute-start(bf16[4,32,1536]{2,1,0:T(8,128)(2,1)S(1)} %get-tuple-element.125), channel_id=1, source_target_pairs={{0,24},{4,28},{8,16},{12,20},{16,8},{20,12},{24,0},{28,4},{1,25},{... | collective-permute-start | bytes 1179656 | tf_op jit(solution)/shard_map/ppermute | solution.py:616
  48.9 19.0 %collective-permute-start.6 = (bf16[4,32,1536]{2,1,0:T(8,128)(2,1)S(1)}, bf16[4,32,1536]{2,1,0:T(8,128)(2,1)S(1)}, u32[]{:S(2)}, u32[]{:S(2)}) collective-permute-start(bf16[4,32,1536]{2,1,0:T(8,128)(2,1)S(1)} %get-tuple-element.126), channel_id=1, source_target_pairs={{0,8},{4,12},{8,0},{12,4},{16,24},{20,28},{24,16},{28,20},{1,9},{5... | collective-permute-start | bytes 1179656 | tf_op jit(solution)/shard_map/ppermute | solution.py:616
  50.4 17.5 %collective-permute-start.5 = (bf16[4,32,1536]{2,1,0:T(8,128)(2,1)S(1)}, bf16[4,32,1536]{2,1,0:T(8,128)(2,1)S(1)}, u32[]{:S(2)}, u32[]{:S(2)}) collective-permute-start(bf16[4,32,1536]{2,1,0:T(8,128)(2,1)S(1)} %get-tuple-element.127), channel_id=1, source_target_pairs={{0,16},{4,20},{8,24},{12,28},{16,0},{20,4},{24,8},{28,12},{1,17},{... | collective-permute-start | bytes 1179656 | tf_op jit(solution)/shard_map/ppermute | solution.py:616
  68.3 16.1 %collective-permute-start.9 = (bf16[512,1536]{1,0:T(8,128)(2,1)S(1)}, bf16[512,1536]{1,0:T(8,128)(2,1)}, u32[]{:S(2)}, u32[]{:S(2)}) collective-permute-start(bf16[512,1536]{1,0:T(8,128)(2,1)S(1)} %bitcast.42), channel_id=1, source_target_pairs={{0,4},{4,0},{8,12},{12,8},{16,20},{20,16},{24,28},{28,24},{1,5},{5... | collective-permute-start | bytes 4718600 | tf_op jit(solution)/shard_map/ppermute | solution.py:621
  70.5 13.2 %collective-permute-start.8 = (bf16[512,256]{1,0:T(8,128)(2,1)S(1)}, bf16[512,256]{1,0:T(8,128)(2,1)S(1)}, u32[]{:S(2)}, u32[]{:S(2)}) collective-permute-start(bf16[512,256]{1,0:T(8,128)(2,1)S(1)} %get-tuple-element.63), channel_id=1, source_target_pairs={{0,4},{4,0},{8,12},{12,8},{16,20},{20,16},{24,28},{28,24},{1,5},{5... | collective-permute-start | bytes 786440 | tf_op jit(solution)/shard_map/ppermute | solution.py:621
  104.2 79.7 %reduce-scatter.3.cloned.1.call-start = ((), (), s32[]{:S(2)}) async-start(), calls=%async_computation.3 | async-start | bytes 1966080 | tf_op jit(solution)/shard_map/reduce_scatter | solution.py:698
  116.0 15.7 %collective-permute-start.13 = (bf16[2,384,384]{2,1,0:T(8,128)(2,1)}, bf16[2,384,384]{2,1,0:T(8,128)(2,1)S(1)}, u32[]{:S(2)}, u32[]{:S(2)}) collective-permute-start(bf16[2,384,384]{2,1,0:T(8,128)(2,1)} %get-tuple-element.85), channel_id=1, source_target_pairs={{0,8},{4,12},{8,0},{12,4},{16,24},{20,28},{24,16},{28,20},{1,9},{5... | collective-permute-start | bytes 1769480 | tf_op jit(solution)/shard_map/ppermute | solution.py:616
  116.5 15.5 %collective-permute-start.14 = (bf16[2,384,384]{2,1,0:T(8,128)(2,1)}, bf16[2,384,384]{2,1,0:T(8,128)(2,1)S(1)}, u32[]{:S(2)}, u32[]{:S(2)}) collective-permute-start(bf16[2,384,384]{2,1,0:T(8,128)(2,1)} %get-tuple-element.87), channel_id=1, source_target_pairs={{0,16},{4,20},{8,24},{12,28},{16,0},{20,4},{24,8},{28,12},{1,17},{... | collective-permute-start | bytes 1769480 | tf_op jit(solution)/shard_map/ppermute | solution.py:616
  134.3 8.3 %collective-permute-start.15 = (bf16[384,384]{1,0:T(8,128)(2,1)S(1)}, bf16[384,384]{1,0:T(8,128)(2,1)S(1)}, u32[]{:S(2)}, u32[]{:S(2)}) collective-permute-start(bf16[384,384]{1,0:T(8,128)(2,1)S(1)} %get-tuple-element.88), channel_id=1, source_target_pairs={{0,16},{4,20},{8,24},{12,28},{16,0},{20,4},{24,8},{28,12},{1,17},{... | collective-permute-start | bytes 884744 | tf_op jit(solution)/shard_map/ppermute | solution.py:616
  135.8 7.9 %collective-permute-start.16 = (bf16[384,384]{1,0:T(8,128)(2,1)S(1)}, bf16[384,384]{1,0:T(8,128)(2,1)S(1)}, u32[]{:S(2)}, u32[]{:S(2)}) collective-permute-start(bf16[384,384]{1,0:T(8,128)(2,1)S(1)} %get-tuple-element.89), channel_id=1, source_target_pairs={{0,8},{4,12},{8,0},{12,4},{16,24},{20,28},{24,16},{28,20},{1,9},{5... | collective-permute-start | bytes 884744 | tf_op jit(solution)/shard_map/ppermute | solution.py:616
  144.7 8.9 %collective-permute-start.19 = (bf16[192,768]{1,0:T(8,128)(2,1)S(1)}, bf16[192,768]{1,0:T(8,128)(2,1)S(1)}, u32[]{:S(2)}, u32[]{:S(2)}) collective-permute-start(bf16[192,768]{1,0:T(8,128)(2,1)S(1)} %get-tuple-element.94), channel_id=1, source_target_pairs={{0,8},{4,12},{8,0},{12,4},{16,24},{20,28},{24,16},{28,20},{1,9},{5... | collective-permute-start | bytes 884744 | tf_op jit(solution)/shard_map/ppermute | solution.py:616
  147.4 8.3 %collective-permute-start.17 = (bf16[2,32,1536]{2,1,0:T(8,128)(2,1)S(1)}, bf16[2,32,1536]{2,1,0:T(8,128)(2,1)S(1)}, u32[]{:S(2)}, u32[]{:S(2)}) collective-permute-start(bf16[2,32,1536]{2,1,0:T(8,128)(2,1)S(1)} %slice.29), channel_id=1, source_target_pairs={{0,8},{4,12},{8,0},{12,4},{16,24},{20,28},{24,16},{28,20},{1,9},{5... | collective-permute-start | bytes 589832 | tf_op jit(solution)/shard_map/ppermute | solution.py:616
  153.6 13.1 %collective-permute-start.23 = (bf16[384,768]{1,0:T(8,128)(2,1)S(1)}, bf16[384,768]{1,0:T(8,128)(2,1)S(1)}, u32[]{:S(2)}, u32[]{:S(2)}) collective-permute-start(bf16[384,768]{1,0:T(8,128)(2,1)S(1)} %constant_dynamic-update-slice_fusion.4.refs_4_.refs_0_), channel_id=1, source_target_pairs={{0,4},{4,0},{8,12},{12,8},{16,20},{20,16},{24,28},{28,24},{1,5},{5... | collective-permute-start | bytes 1769480 | tf_op jit(solution)/shard_map/ppermute | solution.py:621
  153.7 16.9 %collective-permute-start.24 = (bf16[384,768]{1,0:T(8,128)(2,1)S(1)}, bf16[384,768]{1,0:T(8,128)(2,1)S(1)}, u32[]{:S(2)}, u32[]{:S(2)}) collective-permute-start(bf16[384,768]{1,0:T(8,128)(2,1)S(1)} %constant_dynamic-update-slice_fusion.6.refs_5_.refs_1_), channel_id=1, source_target_pairs={{0,4},{4,0},{8,12},{12,8},{16,20},{20,16},{24,28},{28,24},{1,5},{5... | collective-permute-start | bytes 1769480 | tf_op jit(solution)/shard_map/ppermute | solution.py:621
  157.2 27.7 %collective-permute-start.29 = (bf16[384,768]{1,0:T(8,128)(2,1)S(1)}, bf16[384,768]{1,0:T(8,128)(2,1)S(1)}, u32[]{:S(2)}, u32[]{:S(2)}) collective-permute-start(bf16[384,768]{1,0:T(8,128)(2,1)S(1)} %constant_dynamic-update-slice_fusion.6.refs_5_.refs_1_), channel_id=1, source_target_pairs={{0,8},{4,12},{8,0},{12,4},{16,24},{20,28},{24,16},{28,20},{1,9},{5... | collective-permute-start | bytes 1769480 | tf_op jit(solution)/shard_map/ppermute | solution.py:616
  158.6 26.3 %collective-permute-start.28 = (bf16[384,768]{1,0:T(8,128)(2,1)S(1)}, bf16[384,768]{1,0:T(8,128)(2,1)S(1)}, u32[]{:S(2)}, u32[]{:S(2)}) collective-permute-start(bf16[384,768]{1,0:T(8,128)(2,1)S(1)} %constant_dynamic-update-slice_fusion.4.refs_4_.refs_0_), channel_id=1, source_target_pairs={{0,16},{4,20},{8,24},{12,28},{16,0},{20,4},{24,8},{28,12},{1,17},{... | collective-permute-start | bytes 1769480 | tf_op jit(solution)/shard_map/ppermute | solution.py:616
  164.7 9.3 %collective-permute-start.21 = (bf16[2,4,1,1536]{3,2,1,0:T(2,128)(2,1)S(1)}, bf16[2,4,1,1536]{3,2,1,0:T(2,128)(2,1)S(1)}, u32[]{:S(2)}, u32[]{:S(2)}) collective-permute-start(bf16[2,4,1,1536]{3,2,1,0:T(2,128)(2,1)S(1)} %get-tuple-element.99), channel_id=1, source_target_pairs={{0,1},{1,2},{2,3},{3,4},{4,5},{5,6},{6,7},{7,8},{8,9},{9,10},{10,1... | collective-permute-start | bytes 73736 | tf_op jit(solution)/shard_map/ppermute | solution.py:607
  166.7 8.5 %collective-permute-start.22 = (bf16[2,4,1,1536]{3,2,1,0:T(2,128)(2,1)S(1)}, bf16[2,4,1,1536]{3,2,1,0:T(2,128)(2,1)S(1)}, u32[]{:S(2)}, u32[]{:S(2)}) collective-permute-start(bf16[2,4,1,1536]{3,2,1,0:T(2,128)(2,1)S(1)} %get-tuple-element.100), channel_id=1, source_target_pairs={{1,0},{2,1},{3,2},{4,3},{5,4},{6,5},{7,6},{8,7},{9,8},{10,9},{11,1... | collective-permute-start | bytes 73736 | tf_op jit(solution)/shard_map/ppermute | solution.py:607
  184.9 14.0 %collective-permute-start.30 = (bf16[384,768]{1,0:T(8,128)(2,1)S(1)}, bf16[384,768]{1,0:T(8,128)(2,1)S(1)}, u32[]{:S(2)}, u32[]{:S(2)}) collective-permute-start(bf16[384,768]{1,0:T(8,128)(2,1)S(1)} %collective-permute-done.28.refs_0_), channel_id=1, source_target_pairs={{0,4},{4,0},{8,12},{12,8},{16,20},{20,16},{24,28},{28,24},{1,5},{5... | collective-permute-start | bytes 1769480 | tf_op jit(solution)/shard_map/ppermute | solution.py:621
  189.9 9.0 %collective-permute-start.31 = (bf16[384,768]{1,0:T(8,128)(2,1)S(1)}, bf16[384,768]{1,0:T(8,128)(2,1)S(1)}, u32[]{:S(2)}, u32[]{:S(2)}) collective-permute-start(bf16[384,768]{1,0:T(8,128)(2,1)S(1)} %collective-permute-done.29.refs_1_), channel_id=1, source_target_pairs={{0,4},{4,0},{8,12},{12,8},{16,20},{20,16},{24,28},{28,24},{1,5},{5... | collective-permute-start | bytes 1769480 | tf_op jit(solution)/shard_map/ppermute | solution.py:621
  (41 other events, 231.5 us)
Sparse Core Ops, SparseCore 0:
  9.6 35.9 all-gather.5
  47.7 35.9 all-gather.3
  104.3 34.2 reduce-scatter.4
  140.8 35.8 reduce-scatter.2

commit v14 on v13

--- a/solution.py
+++ b/solution.py
@@ -177,24 +177,39 @@
 
 
 def mixed_body(seqs, at_ref, *refs):
-    skip_ref, out_ref = refs[seqs:]
+    skip_ref, out_ref = refs[seqs], refs[-1]
     for slot in range(seqs):
         b = at_ref[0] ^ slot
         out_ref[b] = (skip_ref[b].astype(F32) + refs[slot][...].astype(F32)).astype(BF)
 
 
-def mixed_call(at, terms, skip):
+def mixed_call(at, terms, skip, *deps):
     seqs = len(terms)
     vmem = pl.BlockSpec(memory_space=pltpu.VMEM)
     return pl.pallas_call(
         functools.partial(mixed_body, seqs),
-        in_specs=[SCALARS] + [vmem] * (seqs + 1),
+        in_specs=[SCALARS] + [vmem] * (seqs + 1) + spare(deps),
         out_specs=vmem,
         out_shape=jax.ShapeDtypeStruct(skip.shape, BF),
         compiler_params=params(),
         cost_estimate=COST,
         name="mixed_sum",
-    )(at, *terms, skip)
+    )(at, *terms, skip, *deps)
+
+
+def marker_kernel(*refs):
+    refs[-1][...] = jnp.zeros_like(refs[-1])
+
+
+def marker(*deps):
+    return pl.pallas_call(
+        marker_kernel,
+        in_specs=spare(deps),
+        out_shape=TOKEN,
+        compiler_params=params(),
+        cost_estimate=COST,
+        name="marker",
+    )(*deps)
 
 
 def conv_back_kernel(d_ref, low_ref, high_ref, w_ref, *rest):
@@ -492,23 +507,26 @@
     )(at, xa, xb, ga, gb, ra, rb)
 
 
-def turn_kernel(keep_a, got_a, keep_b, got_b, out_a, out_b):
+def turn_kernel(keep_a, got_a, keep_b, got_b, *rest):
+    out_a, out_b = rest[-2:]
     for keep, got, out in ((keep_a, got_a, out_a), (keep_b, got_b, out_b)):
         out[...] = (keep[1].astype(F32) + got[1].astype(F32)).astype(BF)
 
 
-def weight_turn(keep_a, got_a, keep_b, got_b):
+def weight_turn(keep_a, got_a, keep_b, got_b, *deps):
     shape = jax.ShapeDtypeStruct(keep_a.shape[1:], BF)
     return pl.pallas_call(
         turn_kernel,
+        in_specs=[pl.BlockSpec(memory_space=pltpu.VMEM)] * 4 + spare(deps),
         out_shape=[shape, shape],
         compiler_params=params(),
         cost_estimate=COST,
         name="weight_turn",
-    )(keep_a, got_a, keep_b, got_b)
-
-
-def weight_sum_kernel(keep_a, got_a, last_a, keep_b, got_b, last_b, *out_refs):
+    )(keep_a, got_a, keep_b, got_b, *deps)
+
+
+def weight_sum_kernel(keep_a, got_a, last_a, keep_b, got_b, last_b, *rest):
+    out_refs = rest[-2:]
     split = 3 * DH
     parts = [
         keep[0].astype(F32) + got[0].astype(F32) + last[...].astype(F32)
@@ -525,15 +543,16 @@
         out_ref[quarter:, split:] = piece[:, DH:]
 
 
-def weight_sum(*parts):
-    _, rows, chunk = parts[0].shape
+def weight_sum(keep_a, got_a, last_a, keep_b, got_b, last_b, *deps):
+    _, rows, chunk = keep_a.shape
     return pl.pallas_call(
         weight_sum_kernel,
+        in_specs=[pl.BlockSpec(memory_space=pltpu.VMEM)] * 6 + spare(deps),
         out_shape=[jax.ShapeDtypeStruct((chunk // 2, 2 * rows), BF)] * 2,
         compiler_params=params(),
         cost_estimate=COST,
         name="weight_sum",
-    )(*parts)
+    )(keep_a, got_a, last_a, keep_b, got_b, last_b, *deps)
 
 
 def unpack_kernel(at_ref, *refs):
@@ -559,7 +578,7 @@
                 out_ref[head, 0] = jnp.concatenate(folded, axis=1)
 
 
-def unpack_weights(at, mine, other, far, before=()):
+def unpack_weights(at, mine, other, far, before=(), *deps):
     rows, full = mine[0].shape
     half = rows // 2
     width = 4 * rows
@@ -578,7 +597,7 @@
         grid_spec=pltpu.PrefetchScalarGridSpec(
             num_scalar_prefetch=1,
             grid=(4,),
-            in_specs=specs * 2 + spare(before),
+            in_specs=specs * 2 + spare(tuple(before) + deps),
             out_specs=[
                 pl.BlockSpec((3, half, 2 * DH), lambda t, at: (0, 2 * chunk(t, at) + t // 2, 0)),
                 pl.BlockSpec(
@@ -596,7 +615,7 @@
         compiler_params=params(),
         cost_estimate=COST,
         name="weight_outputs_far" if far else "weight_outputs_near",
-    )(at, *mine, *other, *before)
+    )(at, *mine, *other, *before, *deps)
 
 
 def neighbour_edges(first, last):
@@ -689,40 +708,41 @@
         seqs,
     )
     got_a, got_b = trade_chip(send_a, 1, heads), trade_chip(send_b, 2, heads)
-    turn_a, turn_b = weight_turn(keep_a, got_a, keep_b, got_b)
-    last_a, last_b = trade_chip(turn_a, 2, heads), trade_chip(turn_b, 1, heads)
-    half_a, half_b = weight_sum(keep_a, got_a, last_a, keep_b, got_b, last_b)
     head_term = pair_term(
         head_mine, result_mine, result_got, w_rows, 3 * DH, 4 * DH, "head_term"
     )
     head_sum = lax.psum_scatter(head_term.reshape(shape), "head", scatter_dimension=0, tiled=False)
-
-    d_normed = after(d_normed, last_a, last_b)
+    turn_a, turn_b = weight_turn(keep_a, got_a, keep_b, got_b, head_term)
+    last_a, last_b = trade_chip(turn_a, 2, heads), trade_chip(turn_b, 1, heads)
+
+    d_normed = after(d_normed, turn_a, turn_b)
     leaving = d_normed[2:]
+    near = trade_chip(leaving, 1, heads)
+    far = trade_chip(jnp.stack([d_normed[1], near[1]]), 2, heads)
+    half_a, half_b = weight_sum(keep_a, got_a, last_a, keep_b, got_b, last_b, leaving)
+    grad = jnp.transpose(after(grad_out, d_term), (1, 0, 2))
+    d_conv, first, last = conv_gradient(
+        at, d_normed, near, far, skip, grad, norm_gain, slope, half_a
+    )
+    low, high = neighbour_edges(first, last)
+    low, high, at_hand = lax.optimization_barrier((low, high, marker(conv_weight, first)))
+
     got_a, got_b = trade_chip(half_a, 1, heads), trade_chip(half_b, 2, heads)
-    near_a = jnp.concatenate([half_a, after(got_a, leaving)], axis=0)
-    near_b = jnp.concatenate([half_b, after(got_b, leaving)], axis=0)
+    near_a = jnp.concatenate([half_a, after(got_a, low)], axis=0)
+    near_b = jnp.concatenate([half_b, after(got_b, high)], axis=0)
     far_a = trade_chip(near_a, 2, heads)
     far_b = trade_chip(near_b, 1, heads)
     near_other = [swap_heads(near_a), swap_heads(near_b)]
-
-    near = trade_chip(leaving, 1, heads)
-    far = trade_chip(jnp.stack([d_normed[1], near[1]]), 2, heads)
-    grad = jnp.transpose(after(grad_out, d_term), (1, 0, 2))
-    d_conv, first, last = conv_gradient(
-        at, d_normed, near, far, skip, grad, norm_gain, slope, near_a, near_b
-    )
-    low, high = neighbour_edges(first, last)
-    *outputs, token = unpack_weights(at, [near_a, near_b], near_other, False)
-    low, high, token = lax.optimization_barrier((low, high, token))
-    grad_input = conv_back(d_conv, low, high, conv_weight, token)
-
-    head_sum = after(head_sum, grad_input)
-    head_sum = [head_sum[order.index(j)] for j in range(seqs)]
-    far_other = [swap_heads(after(x, *head_sum)) for x in (far_a, far_b)]
+    grad_input = conv_back(d_conv, low, high, conv_weight, at_hand, *near_other)
+    *outputs, token = unpack_weights(
+        at, [near_a, near_b], near_other, False, (), grad_input
+    )
+
+    head_sum = after(head_sum, grad_input, token)
+    head_sum = to_chips([head_sum[order.index(j)] for j in range(seqs)])
+    far_other = [swap_heads(after(x, *head_sum[1:])) for x in (far_a, far_b)]
     grad_w_qkv, grad_w_out, _ = unpack_weights(at, [far_a, far_b], far_other, True, outputs)
-    head_sum = to_chips(head_sum)
-    mixed = mixed_call(at, head_sum, skip)
+    mixed = mixed_call(at, head_sum, skip, token)
     grad_input = jnp.transpose(grad_input.reshape(2, seqs, rows, -1), (2, 0, 1, 3))
     return (
         jnp.transpose(mixed, (1, 0, 2)),

time: 213 us -> 209 us (0.981)
  waiting for transfers between devices: 66 us -> 63.4 us
    ppermute x19, waiting for transfers between devices: 56.1 us -> 47.9 us  [trade_chip(): return lax.ppermute(x, 'seq', [(s, s ^ bit * heads) for s in range(count)])]
    reduce_scatter x1, waiting for transfers between devices: 0.02 us -> 4.3 us  [unit_body(): lax.psum_scatter(d_term.reshape(shape), 'head', scatter_dimension=0, tile...]
    unnamed x64 -> x66, local copies, waits for them, and re-layouts: 23.8 us -> 22.7 us
  transfers between devices with their start and end apart: 36 -> 36, of which waited for: 18 -> 20; matrix products, arithmetic and copies ran while one was open for 5% -> 5% of each run, Pallas kernels for 20% -> 21%
where the time goes in v14:
time: 209 us; the launch traced here: 206 us
  waiting for transfers between devices  63.4 us (30%)
  Pallas kernels  56.4 us (27%)
  starting transfers between devices  40.2 us (19%)
  local copies, waits for them, and re-layouts  31.1 us (15%)
  between operations  14.3 us (7%)
    ppermute x19, waiting for transfers between devices, trade_chip(): return lax.ppermute(x, 'seq', [(s, s ^ bit * heads) for s in range(count)])  47.9 us
    unnamed x66, local copies, waits for them, and re-layouts  22.7 us
    ppermute x19, starting transfers between devices, trade_chip(): return lax.ppermute(x, 'seq', [(s, s ^ bit * heads) for s in range(count)])  20.3 us
    pallas_call x1, Pallas kernels, encoder(): pl.pallas_call(conv_kernel, grid=(width // tile,), in_specs=[SCALARS, who...  10.1 us
    pallas_call x1, Pallas kernels, weight_gradients(): pl.pallas_call(weight_kernel, grid_spec=pltpu.PrefetchScalarGridSpec(num_...  8.83 us
    pallas_call x2, Pallas kernels, unpack_weights(): pl.pallas_call(unpack_kernel, grid_spec=pltpu.PrefetchScalarGridSpec(num_...  7.75 us
    ppermute x2, starting transfers between devices, neighbour_edges(): lax.ppermute(last, axes, forward)  7.12 us
    pallas_call x1, Pallas kernels, attention(): pl.pallas_call(functools.partial(attention_kernel, block=min(256, half)),...  6.47 us
  transfers between devices with their start and end apart: 36, of which 20 were waited for; matrix products, arithmetic and copies ran while one was open for 5% of the time, Pallas kernels for 21%

profile of v14, /device:TPU:26, one launch (start us, length us, event | category | flops | bytes accessed | tf_op | source)
XLA Modules:
  0.0 206.2 jit_solution(15013564310423257091)
XLA Ops:
  9.1 2.4 %collective-permute-start.1 = (bf16[2,4,1,768]{3,2,1,0:T(2,128)(2,1)S(1)}, bf16[2,4,1,768]{3,2,1,0:T(2,128)(2,1)S(1)}, u32[]{:S(2)}, u32[]{:S(2)}) collective-permute-start(bf16[2,4,1,768]{3,2,1,0:T(2,128)(2,1)S(1)} %get-tuple-element.132), channel_id=1, source_target_pairs={{1,0},{2,1},{3,2},{4,3},{5,4},{6,5},{7,6},{8,7},{9,8},{10,9},{11,1... | collective-permute-start | bytes 36872 | tf_op jit(solution)/shard_map/ppermute | solution.py:626
  11.4 5.0 %collective-permute-start = (bf16[2,4,1,768]{3,2,1,0:T(2,128)(2,1)S(1)}, bf16[2,4,1,768]{3,2,1,0:T(2,128)(2,1)S(1)}, u32[]{:S(2)}, u32[]{:S(2)}) collective-permute-start(bf16[2,4,1,768]{3,2,1,0:T(2,128)(2,1)S(1)} %get-tuple-element.133), channel_id=1, source_target_pairs={{0,1},{1,2},{2,3},{3,4},{4,5},{5,6},{6,7},{7,8},{8,9},{9,10},{10,1... | collective-permute-start | bytes 36872 | tf_op jit(solution)/shard_map/ppermute | solution.py:626
  19.5 10.1 %encoder_forward.1 = (bf16[4,32,1536]{2,1,0:T(8,128)(2,1)}, f32[2,4,32,1536]{3,2,1,0:T(8,128)}, bf16[32,1536]{1,0:T(8,128)(2,1)}, bf16[32,1536]{1,0:T(8,128)(2,1...) custom-call(s32[2]{0:T(128)} %pad_add_fusion.at_ref, bf16[2,4,32,768]{3,2,1,0:T(8,128)(2,1)} %bitcast.58, ...), custom_call_target="tpu_custom_call" | custom-call | flops 1000 | bytes 1000 | tf_op jit(solution)/shard_map/encoder_forward/pallas_call | solution.py:111
  39.7 5.9 %all-gather.6.cloned.1.call-done = bf16[128,4,1536]{2,1,0:T(4,128)(2,1)} async-done(((bf16[32,4,1536]{2,1,0:T(4,128)(2,1)}), bf16[128,4,1536]{2,1,0:T(4,128)(2,1)}) %all-gather.6.cloned.1.call-update) | async-done | bytes 1572880 | tf_op jit(solution)/shard_map/all_gather | solution.py:663
  51.0 9.4 %collective-permute-done.7 = bf16[4,32,1536]{2,1,0:T(8,128)(2,1)S(1)} collective-permute-done((bf16[4,32,1536]{2,1,0:T(8,128)(2,1)S(1)}, bf16[4,32,1536]{2,1,0:T(8,128)(2,1)S(1)}, u32[]{:S(2)}, u32[]{:S(2)}) %collective-permute-start.7) | collective-permute-done | bytes 393248 | tf_op jit(solution)/shard_map/ppermute | solution.py:635
  60.4 7.5 %collective-permute-done.6 = bf16[4,32,1536]{2,1,0:T(8,128)(2,1)S(1)} collective-permute-done((bf16[4,32,1536]{2,1,0:T(8,128)(2,1)S(1)}, bf16[4,32,1536]{2,1,0:T(8,128)(2,1)S(1)}, u32[]{:S(2)}, u32[]{:S(2)}) %collective-permute-start.6) | collective-permute-done | bytes 393248 | tf_op jit(solution)/shard_map/ppermute | solution.py:635
  72.6 3.9 %pack_weights.1 = (bf16[2,1536,576]{2,1,0:T(8,128)(2,1)S(1)}, bf16[2,576,1536]{2,1,0:T(8,128)(2,1)S(1)}, f32[8,128]{1,0:T(8,128)S(1)}) custom-call(bf16[3,1536,384]{2,1,0:T(8,128)(2,1)S(1)} %copy-done.10), custom_call_target="tpu_custom_call" | custom-call | flops 1000 | bytes 1000 | tf_op jit(solution)/shard_map/pack_weights/pallas_call | solution.py:280
  81.5 2.2 %all-gather.4.cloned.1.call-done.x_ref.xa_ref = bf16[512,1536]{1,0:T(8,128)(2,1)} async-done(((bf16[128,1536]{1,0:T(8,128)(2,1)}), bf16[512,1536]{1,0:T(8,128)(2,1)}) %all-gather.4.cloned.1.call-update) | async-done | bytes 1572880 | tf_op jit(solution)/shard_map/all_gather | solution.py:670
  92.3 6.5 %attention.1 = (bf16[512,768]{1,0:T(8,128)(2,1)S(1)}, bf16[512,768]{1,0:T(8,128)(2,1)S(1)}) custom-call(bf16[512,640]{1,0:T(8,128)(2,1)S(1)} %get-tuple-element.73.qa_ref, bf16[512,640]{1,0:T(8,128)(2,1)S(1)} %collective-permute-done.10.qb_ref, bf16[512,256]{1,0:T(8,128)(2,1)S(1)} %copy-done.22, bf16[512,256]{1,0:T(8,128)(2,1)S(1)} %copy-done.20, ...), custom_call_target="tpu_custom_call" | custom-call | flops 1000 | bytes 1000 | tf_op jit(solution)/shard_map/attention/pallas_call | solution.py:381
  101.2 3.1 %d_term.1 = bf16[512,1536]{1,0:T(8,128)(2,1)} custom-call(s32[1]{0:T(128)} %bitcast.4.head_ref, bf16[512,768]{1,0:T(8,128)(2,1)S(1)} %collective-permute-done.12.b_ref.x_ref, bf16[2,576,1536]{2,1,0:T(8,128)(2,1)S(1)} %copy-done.5, f32[512,1536]{1,0:T(8,128)S(1)} %d_term_own.1.rest_0_), custom_call_target="tpu_custom_call" | custom-call | flops 1000 | bytes 1000 | tf_op jit(solution)/shard_map/d_term/pallas_call | solution.py:441
  104.5 2.7 %head_term.1.rest_0_ = bf16[512,1536]{1,0:T(8,128)(2,1)} custom-call(s32[1]{0:T(128)} %bitcast.1.head_ref, bf16[512,768]{1,0:T(8,128)(2,1)S(1)} %get-tuple-element.80.a_ref.x_ref.ra_ref, bf16[512,768]{1,0:T(8,128)(2,1)S(1)} %collective-permute-done.12.b_ref.x_ref, bf16[2,192,1536]{2,1,0:T(8,128)(2,1)S(1)} %bitcast.48), custom_call_target="tpu_custom_call" | custom-call | flops 1000 | bytes 1000 | tf_op jit(solution)/shard_map/head_term/pallas_call | solution.py:408
  107.2 8.8 %weight_gradients.1 = (bf16[2,384,384]{2,1,0:T(8,128)(2,1)}, bf16[2,384,384]{2,1,0:T(8,128)(2,1)}, bf16[2,384,384]{2,1,0:T(8,128)(2,1)}, bf16[2,384,384]{2,1,0:T(8,128)(2,1)}) custom-call(s32[1]{0:T(128)} %bitcast.at_ref, bf16[512,1536]{1,0:T(8,128)(2,1)} %all-gather.4.cloned.1.call-done.x_ref.xa_ref, bf16[512,1536]{1,0:T(8,128)(2,1)} %copy-done.9, ...), custom_call_target="tpu_custom_call" | custom-call | flops 1000 | bytes 1000 | tf_op jit(solution)/shard_map/weight_gradients/pallas_call | solution.py:494
  118.1 13.7 %collective-permute-done.13.got_a = bf16[2,384,384]{2,1,0:T(8,128)(2,1)S(1)} collective-permute-done((bf16[2,384,384]{2,1,0:T(8,128)(2,1)}, bf16[2,384,384]{2,1,0:T(8,128)(2,1)S(1)}, u32[]{:S(2)}, u32[]{:S(2)}) %collective-permute-start.13) | collective-permute-done | bytes 589856 | tf_op jit(solution)/shard_map/ppermute | solution.py:635
  134.4 4.3 %reduce-scatter.5.cloned.1.call-done = bf16[1,4,32,1536]{3,2,1,0:T(8,128)(2,1)} async-done(((bf16[4,4,32,1536]{3,2,1,0:T(8,128)(2,1)}), bf16[1,4,32,1536]{3,2,1,0:T(8,128)(2,1)}) %reduce-scatter.5.cloned.1.call-update) | async-done | bytes 393232 | tf_op jit(solution)/shard_map/reduce_scatter | solution.py:699
  144.1 3.4 %collective-permute-done.15.near_ref = bf16[2,32,1536]{2,1,0:T(8,128)(2,1)S(1)} collective-permute-done((bf16[2,32,1536]{2,1,0:T(8,128)(2,1)S(1)}, bf16[2,32,1536]{2,1,0:T(8,128)(2,1)S(1)}, u32[]{:S(2)}, u32[]{:S(2)}) %collective-permute-start.15) | collective-permute-done | bytes 196640 | tf_op jit(solution)/shard_map/ppermute | solution.py:635
  149.3 3.4 %collective-permute-done.18.last_b = bf16[384,384]{1,0:T(8,128)(2,1)S(1)} collective-permute-done((bf16[384,384]{1,0:T(8,128)(2,1)S(1)}, bf16[384,384]{1,0:T(8,128)(2,1)S(1)}, u32[]{:S(2)}, u32[]{:S(2)}) %collective-permute-start.18) | collective-permute-done | bytes 294944 | tf_op jit(solution)/shard_map/ppermute | solution.py:635
  158.5 3.7 %collective-permute-start.20 = (bf16[2,4,1,1536]{3,2,1,0:T(2,128)(2,1)S(1)}, bf16[2,4,1,1536]{3,2,1,0:T(2,128)(2,1)S(1)}, u32[]{:S(2)}, u32[]{:S(2)}) collective-permute-start(bf16[2,4,1,1536]{3,2,1,0:T(2,128)(2,1)S(1)} %get-tuple-element.97.refs_1_), channel_id=1, source_target_pairs={{1,0},{2,1},{3,2},{4,3},{5,4},{6,5},{7,6},{8,7},{9,8},{10,9},{11,1... | collective-permute-start | bytes 73736 | tf_op jit(solution)/shard_map/ppermute | solution.py:626
  162.3 4.4 %copy-done = bf16[5,768,1536]{2,1,0:T(8,128)(2,1)S(1)} copy-done((bf16[5,768,1536]{2,1,0:T(8,128)(2,1)S(1)}, bf16[5,768,1536]{2,1,0:T(8,128)(2,1)}, u32[]{:S(2)}) %copy-start) | copy-done | bytes 11796504
  167.1 4.9 %collective-permute-start.24 = (bf16[384,768]{1,0:T(8,128)(2,1)S(1)}, bf16[384,768]{1,0:T(8,128)(2,1)S(1)}, u32[]{:S(2)}, u32[]{:S(2)}) collective-permute-start(bf16[384,768]{1,0:T(8,128)(2,1)S(1)} %constant_dynamic-update-slice_fusion.6.refs_1_), channel_id=1, source_target_pairs={{0,4},{4,0},{8,12},{12,8},{16,20},{20,16},{24,28},{28,24},{1,5},{5... | collective-permute-start | bytes 1769480 | tf_op jit(solution)/shard_map/ppermute | solution.py:640
  174.4 4.2 %encoder_backward.1.refs_4_ = bf16[256,768]{1,0:T(8,128)(2,1)S(1)} custom-call(bf16[2,4,32,1536]{3,2,1,0:T(8,128)(2,1)S(1)} %get-tuple-element.95.d_ref, bf16[2,4,1,1536]{3,2,1,0:T(2,128)(2,1)S(1)} %collective-permute-done.19.low_ref, bf16[2,4,1,1536]{3,2,1,0:T(2,128)(2,1)S(1)} %collective-permute-done.20.high_ref, bf16[5,768,1536]{2,1,0:T(8,128)(2,1)S(1)} %copy-done, ...), custom_call_target="tpu_custom_call" | custom-call | flops 1000 | bytes 1000 | tf_op jit(solution)/shard_map/encoder_backward/pallas_call | solution.py:244
  178.7 3.4 %weight_outputs_near.1 = (f32[3,1536,384]{2,1,0:T(8,128)}, f32[2,2,96,1536]{3,2,1,0:T(8,128)}, f32[8,128]{1,0:T(8,128)S(1)}) custom-call(s32[2]{0:T(128)S(1)} %copy-done.24, bf16[384,768]{1,0:T(8,128)(2,1)S(1)} %constant_dynamic-update-slice_fusion.4.refs_0_, bf16[384,768]{1,0:T(8,128)(2,1)S(1)} %constant_dynamic-update-slice_fusion.6.refs_1_, ...), custom_call_target="tpu_custom_call" | custom-call | flops 1000 | bytes 1000 | tf_op jit(solution)/shard_map/weight_outputs_near/pallas_call | solution.py:595
  184.4 2.3 %collective-permute-start.25 = (bf16[32,1536]{1,0:T(8,128)(2,1)S(1)}, bf16[32,1536]{1,0:T(8,128)(2,1)S(1)}, u32[]{:S(2)}, u32[]{:S(2)}) collective-permute-start(bf16[32,1536]{1,0:T(8,128)(2,1)S(1)} %get-tuple-element.130), channel_id=1, source_target_pairs={{0,8},{4,12},{8,0},{12,4},{16,24},{20,28},{24,16},{28,20},{1,9},{5... | collective-permute-start | bytes 294920 | tf_op jit(solution)/shard_map/ppermute | solution.py:635
  189.8 2.2 %collective-permute-done.26.refs_2_ = bf16[32,1536]{1,0:T(8,128)(2,1)S(1)} collective-permute-done((bf16[32,1536]{1,0:T(8,128)(2,1)S(1)}, bf16[32,1536]{1,0:T(8,128)(2,1)S(1)}, u32[]{:S(2)}, u32[]{:S(2)}) %collective-permute-start.26) | collective-permute-done | bytes 98336 | tf_op jit(solution)/shard_map/ppermute | solution.py:635
  195.3 4.3 %weight_outputs_far.1 = (f32[3,1536,384]{2,1,0:T(8,128)}, f32[2,2,96,1536]{3,2,1,0:T(8,128)}, f32[8,128]{1,0:T(8,128)}) custom-call(s32[2]{0:T(128)S(1)} %copy-done.24, bf16[384,768]{1,0:T(8,128)(2,1)} %collective-permute-done.28.refs_0_, bf16[384,768]{1,0:T(8,128)(2,1)S(1)} %collective-permute-done.29.refs_1_, ...), custom_call_target="tpu_custom_call", output_to_operand_aliasing={{0}: (5, {}), {1}: (6, {})} | custom-call | flops 1000 | bytes 1000 | tf_op jit(solution)/shard_map/weight_outputs_far/pallas_call | solution.py:595
  (155 shorter events, 70.2 us)
Async XLA Ops:
  7.2 38.4 %all-gather.6.cloned.1.call-start = ((), (), s32[]{:S(2)}) async-start(), calls=%async_computation.5 | async-start | bytes 1966080 | tf_op jit(solution)/shard_map/all_gather | solution.py:663
  7.9 75.8 %all-gather.4.cloned.1.call-start = ((), (), s32[]{:S(2)}) async-start(), calls=%async_computation.2 | async-start | bytes 1966080 | tf_op jit(solution)/shard_map/all_gather | solution.py:670
  9.1 9.3 %collective-permute-start.1 = (bf16[2,4,1,768]{3,2,1,0:T(2,128)(2,1)S(1)}, bf16[2,4,1,768]{3,2,1,0:T(2,128)(2,1)S(1)}, u32[]{:S(2)}, u32[]{:S(2)}) collective-permute-start(bf16[2,4,1,768]{3,2,1,0:T(2,128)(2,1)S(1)} %get-tuple-element.132), channel_id=1, source_target_pairs={{1,0},{2,1},{3,2},{4,3},{5,4},{6,5},{7,6},{8,7},{9,8},{10,9},{11,1... | collective-permute-start | bytes 36872 | tf_op jit(solution)/shard_map/ppermute | solution.py:626
  39.6 99.1 %reduce-scatter.5.cloned.1.call-start = ((), (), s32[]{:S(2)}) async-start(), calls=%async_computation.4 | async-start | bytes 1966080 | tf_op jit(solution)/shard_map/reduce_scatter | solution.py:699
  47.4 13.0 %collective-permute-start.7 = (bf16[4,32,1536]{2,1,0:T(8,128)(2,1)S(1)}, bf16[4,32,1536]{2,1,0:T(8,128)(2,1)S(1)}, u32[]{:S(2)}, u32[]{:S(2)}) collective-permute-start(bf16[4,32,1536]{2,1,0:T(8,128)(2,1)S(1)} %get-tuple-element.125), channel_id=1, source_target_pairs={{0,24},{4,28},{8,16},{12,20},{16,8},{20,12},{24,0},{28,4},{1,25},{... | collective-permute-start | bytes 1179656 | tf_op jit(solution)/shard_map/ppermute | solution.py:635
  48.9 19.0 %collective-permute-start.6 = (bf16[4,32,1536]{2,1,0:T(8,128)(2,1)S(1)}, bf16[4,32,1536]{2,1,0:T(8,128)(2,1)S(1)}, u32[]{:S(2)}, u32[]{:S(2)}) collective-permute-start(bf16[4,32,1536]{2,1,0:T(8,128)(2,1)S(1)} %get-tuple-element.126), channel_id=1, source_target_pairs={{0,8},{4,12},{8,0},{12,4},{16,24},{20,28},{24,16},{28,20},{1,9},{5... | collective-permute-start | bytes 1179656 | tf_op jit(solution)/shard_map/ppermute | solution.py:635
  50.4 17.5 %collective-permute-start.5 = (bf16[4,32,1536]{2,1,0:T(8,128)(2,1)S(1)}, bf16[4,32,1536]{2,1,0:T(8,128)(2,1)S(1)}, u32[]{:S(2)}, u32[]{:S(2)}) collective-permute-start(bf16[4,32,1536]{2,1,0:T(8,128)(2,1)S(1)} %get-tuple-element.127), channel_id=1, source_target_pairs={{0,16},{4,20},{8,24},{12,28},{16,0},{20,4},{24,8},{28,12},{1,17},{... | collective-permute-start | bytes 1179656 | tf_op jit(solution)/shard_map/ppermute | solution.py:635
  68.3 16.1 %collective-permute-start.9 = (bf16[512,1536]{1,0:T(8,128)(2,1)S(1)}, bf16[512,1536]{1,0:T(8,128)(2,1)}, u32[]{:S(2)}, u32[]{:S(2)}) collective-permute-start(bf16[512,1536]{1,0:T(8,128)(2,1)S(1)} %bitcast.42), channel_id=1, source_target_pairs={{0,4},{4,0},{8,12},{12,8},{16,20},{20,16},{24,28},{28,24},{1,5},{5... | collective-permute-start | bytes 4718600 | tf_op jit(solution)/shard_map/ppermute | solution.py:640
  70.5 13.2 %collective-permute-start.8 = (bf16[512,256]{1,0:T(8,128)(2,1)S(1)}, bf16[512,256]{1,0:T(8,128)(2,1)S(1)}, u32[]{:S(2)}, u32[]{:S(2)}) collective-permute-start(bf16[512,256]{1,0:T(8,128)(2,1)S(1)} %get-tuple-element.63), channel_id=1, source_target_pairs={{0,4},{4,0},{8,12},{12,8},{16,20},{20,16},{24,28},{28,24},{1,5},{5... | collective-permute-start | bytes 786440 | tf_op jit(solution)/shard_map/ppermute | solution.py:640
  84.4 7.9 %collective-permute-start.11 = (bf16[512,1536]{1,0:T(8,128)(2,1)}, bf16[512,1536]{1,0:T(8,128)(2,1)S(1)}, u32[]{:S(2)}, u32[]{:S(2)}) collective-permute-start(bf16[512,1536]{1,0:T(8,128)(2,1)} %all-gather.4.cloned.1.call-done.x_ref.xa_ref), channel_id=1, source_target_pairs={{0,4},{4,0},{8,12},{12,8},{16,20},{20,16},{24,28},{28,24},{1,5},{5... | collective-permute-start | bytes 4718600 | tf_op jit(solution)/shard_map/ppermute | solution.py:640
  104.3 77.8 %reduce-scatter.3.cloned.1.call-start = ((), (), s32[]{:S(2)}) async-start(), calls=%async_computation.3 | async-start | bytes 1966080 | tf_op jit(solution)/shard_map/reduce_scatter | solution.py:714
  116.1 15.7 %collective-permute-start.13 = (bf16[2,384,384]{2,1,0:T(8,128)(2,1)}, bf16[2,384,384]{2,1,0:T(8,128)(2,1)S(1)}, u32[]{:S(2)}, u32[]{:S(2)}) collective-permute-start(bf16[2,384,384]{2,1,0:T(8,128)(2,1)} %get-tuple-element.85), channel_id=1, source_target_pairs={{0,8},{4,12},{8,0},{12,4},{16,24},{20,28},{24,16},{28,20},{1,9},{5... | collective-permute-start | bytes 1769480 | tf_op jit(solution)/shard_map/ppermute | solution.py:635
  116.6 15.5 %collective-permute-start.14 = (bf16[2,384,384]{2,1,0:T(8,128)(2,1)}, bf16[2,384,384]{2,1,0:T(8,128)(2,1)S(1)}, u32[]{:S(2)}, u32[]{:S(2)}) collective-permute-start(bf16[2,384,384]{2,1,0:T(8,128)(2,1)} %get-tuple-element.87), channel_id=1, source_target_pairs={{0,16},{4,20},{8,24},{12,28},{16,0},{20,4},{24,8},{28,12},{1,17},{... | collective-permute-start | bytes 1769480 | tf_op jit(solution)/shard_map/ppermute | solution.py:635
  139.6 7.9 %collective-permute-start.15 = (bf16[2,32,1536]{2,1,0:T(8,128)(2,1)S(1)}, bf16[2,32,1536]{2,1,0:T(8,128)(2,1)S(1)}, u32[]{:S(2)}, u32[]{:S(2)}) collective-permute-start(bf16[2,32,1536]{2,1,0:T(8,128)(2,1)S(1)} %slice.29.rest_0_), channel_id=1, source_target_pairs={{0,8},{4,12},{8,0},{12,4},{16,24},{20,28},{24,16},{28,20},{1,9},{5... | collective-permute-start | bytes 589832 | tf_op jit(solution)/shard_map/ppermute | solution.py:635
  140.3 9.0 %collective-permute-start.17 = (bf16[384,384]{1,0:T(8,128)(2,1)S(1)}, bf16[384,384]{1,0:T(8,128)(2,1)S(1)}, u32[]{:S(2)}, u32[]{:S(2)}) collective-permute-start(bf16[384,384]{1,0:T(8,128)(2,1)S(1)} %get-tuple-element.88), channel_id=1, source_target_pairs={{0,16},{4,20},{8,24},{12,28},{16,0},{20,4},{24,8},{28,12},{1,17},{... | collective-permute-start | bytes 884744 | tf_op jit(solution)/shard_map/ppermute | solution.py:635
  141.7 10.9 %collective-permute-start.18 = (bf16[384,384]{1,0:T(8,128)(2,1)S(1)}, bf16[384,384]{1,0:T(8,128)(2,1)S(1)}, u32[]{:S(2)}, u32[]{:S(2)}) collective-permute-start(bf16[384,384]{1,0:T(8,128)(2,1)S(1)} %get-tuple-element.89), channel_id=1, source_target_pairs={{0,8},{4,12},{8,0},{12,4},{16,24},{20,28},{24,16},{28,20},{1,9},{5... | collective-permute-start | bytes 884744 | tf_op jit(solution)/shard_map/ppermute | solution.py:635
  147.6 7.6 %collective-permute-start.16 = (bf16[2,32,1536]{2,1,0:T(8,128)(2,1)S(1)}, bf16[2,32,1536]{2,1,0:T(8,128)(2,1)S(1)}, u32[]{:S(2)}, u32[]{:S(2)}) collective-permute-start(bf16[2,32,1536]{2,1,0:T(8,128)(2,1)S(1)} %pad_maximum_fusion.1), channel_id=1, source_target_pairs={{0,16},{4,20},{8,24},{12,28},{16,0},{20,4},{24,8},{28,12},{1,17},{... | collective-permute-start | bytes 589832 | tf_op jit(solution)/shard_map/ppermute | solution.py:635
  153.0 14.1 %collective-permute-start.21 = (bf16[192,768]{1,0:T(8,128)(2,1)S(1)}, bf16[192,768]{1,0:T(8,128)(2,1)S(1)}, u32[]{:S(2)}, u32[]{:S(2)}) collective-permute-start(bf16[192,768]{1,0:T(8,128)(2,1)S(1)} %get-tuple-element.94.refs_4_), channel_id=1, source_target_pairs={{0,8},{4,12},{8,0},{12,4},{16,24},{20,28},{24,16},{28,20},{1,9},{5... | collective-permute-start | bytes 884744 | tf_op jit(solution)/shard_map/ppermute | solution.py:635
  153.6 13.4 %collective-permute-start.23 = (bf16[192,768]{1,0:T(8,128)(2,1)S(1)}, bf16[192,768]{1,0:T(8,128)(2,1)S(1)}, u32[]{:S(2)}, u32[]{:S(2)}) collective-permute-start(bf16[192,768]{1,0:T(8,128)(2,1)S(1)} %get-tuple-element.102), channel_id=1, source_target_pairs={{0,16},{4,20},{8,24},{12,28},{16,0},{20,4},{24,8},{28,12},{1,17},{... | collective-permute-start | bytes 884744 | tf_op jit(solution)/shard_map/ppermute | solution.py:635
  156.4 10.3 %collective-permute-start.19 = (bf16[2,4,1,1536]{3,2,1,0:T(2,128)(2,1)S(1)}, bf16[2,4,1,1536]{3,2,1,0:T(2,128)(2,1)S(1)}, u32[]{:S(2)}, u32[]{:S(2)}) collective-permute-start(bf16[2,4,1,1536]{3,2,1,0:T(2,128)(2,1)S(1)} %get-tuple-element.96), channel_id=1, source_target_pairs={{0,1},{1,2},{2,3},{3,4},{4,5},{5,6},{6,7},{7,8},{8,9},{9,10},{10,1... | collective-permute-start | bytes 73736 | tf_op jit(solution)/shard_map/ppermute | solution.py:626
  158.5 8.5 %collective-permute-start.20 = (bf16[2,4,1,1536]{3,2,1,0:T(2,128)(2,1)S(1)}, bf16[2,4,1,1536]{3,2,1,0:T(2,128)(2,1)S(1)}, u32[]{:S(2)}, u32[]{:S(2)}) collective-permute-start(bf16[2,4,1,1536]{3,2,1,0:T(2,128)(2,1)S(1)} %get-tuple-element.97.refs_1_), channel_id=1, source_target_pairs={{1,0},{2,1},{3,2},{4,3},{5,4},{6,5},{7,6},{8,7},{9,8},{10,9},{11,1... | collective-permute-start | bytes 73736 | tf_op jit(solution)/shard_map/ppermute | solution.py:626
  172.1 16.2 %collective-permute-start.29 = (bf16[384,768]{1,0:T(8,128)(2,1)S(1)}, bf16[384,768]{1,0:T(8,128)(2,1)S(1)}, u32[]{:S(2)}, u32[]{:S(2)}) collective-permute-start(bf16[384,768]{1,0:T(8,128)(2,1)S(1)} %constant_dynamic-update-slice_fusion.6.refs_1_), channel_id=1, source_target_pairs={{0,8},{4,12},{8,0},{12,4},{16,24},{20,28},{24,16},{28,20},{1,9},{5... | collective-permute-start | bytes 1769480 | tf_op jit(solution)/shard_map/ppermute | solution.py:635
  172.1 19.9 %collective-permute-start.28 = (bf16[384,768]{1,0:T(8,128)(2,1)S(1)}, bf16[384,768]{1,0:T(8,128)(2,1)}, u32[]{:S(2)}, u32[]{:S(2)}) collective-permute-start(bf16[384,768]{1,0:T(8,128)(2,1)S(1)} %constant_dynamic-update-slice_fusion.4.refs_0_), channel_id=1, source_target_pairs={{0,16},{4,20},{8,24},{12,28},{16,0},{20,4},{24,8},{28,12},{1,17},{... | collective-permute-start | bytes 1769480 | tf_op jit(solution)/shard_map/ppermute | solution.py:635
  184.4 7.6 %collective-permute-start.25 = (bf16[32,1536]{1,0:T(8,128)(2,1)S(1)}, bf16[32,1536]{1,0:T(8,128)(2,1)S(1)}, u32[]{:S(2)}, u32[]{:S(2)}) collective-permute-start(bf16[32,1536]{1,0:T(8,128)(2,1)S(1)} %get-tuple-element.130), channel_id=1, source_target_pairs={{0,8},{4,12},{8,0},{12,4},{16,24},{20,28},{24,16},{28,20},{1,9},{5... | collective-permute-start | bytes 294920 | tf_op jit(solution)/shard_map/ppermute | solution.py:635
  (42 other events, 208.5 us)
Sparse Core Ops, SparseCore 0:
  9.6 35.9 all-gather.5
  47.7 35.9 all-gather.3
  104.4 34.2 reduce-scatter.4
  140.9 36.3 reduce-scatter.2

commit v15 on v14

--- a/solution.py
+++ b/solution.py
@@ -331,6 +331,66 @@
         cost_estimate=COST,
         name=name,
     )(head, x, weight, *deps)
+
+
+def split_product_kernel(head_ref, xa_ref, xb_ref, w_ref, *rest):
+    del head_ref
+    out_ref = rest[-1]
+    cut = xa_ref.shape[1]
+    value = dot(xa_ref[...], w_ref[0, :cut], NN) + dot(xb_ref[...], w_ref[0, cut:], NN)
+    out_ref[:, : value.shape[1]] = value.astype(BF)
+    out_ref[:, value.shape[1] :] = jnp.zeros_like(out_ref[:, value.shape[1] :])
+
+
+def split_product(head, xa, xb, weight, name, *deps):
+    columns = weight.shape[2]
+    columns += -columns % 128
+    rows = xa.shape[0]
+    return pl.pallas_call(
+        split_product_kernel,
+        grid_spec=pltpu.PrefetchScalarGridSpec(
+            num_scalar_prefetch=1,
+            grid=(1,),
+            in_specs=[
+                pl.BlockSpec(xa.shape, lambda i, head: (0, 0)),
+                pl.BlockSpec(xb.shape, lambda i, head: (0, 0)),
+                pl.BlockSpec((1,) + weight.shape[1:], lambda i, head: (head[0], 0, 0)),
+            ]
+            + spare(deps),
+            out_specs=pl.BlockSpec((rows, columns), lambda i, head: (0, 0)),
+        ),
+        out_shape=jax.ShapeDtypeStruct((rows, columns), BF),
+        compiler_params=params(),
+        cost_estimate=COST,
+        name=name,
+    )(head, xa, xb, weight, *deps)
+
+
+def place_kernel(at_ref, *refs):
+    del at_ref
+    for slot, ref in enumerate(refs[:-1]):
+
+        @pl.when(pl.program_id(0) == slot)
+        def _():
+            refs[-1][...] = ref[...]
+
+
+def placed(at, slots, name):
+    count = len(slots)
+    rows, width = slots[0].shape
+    return pl.pallas_call(
+        place_kernel,
+        grid_spec=pltpu.PrefetchScalarGridSpec(
+            num_scalar_prefetch=1,
+            grid=(count,),
+            in_specs=[pl.BlockSpec((rows, width), lambda q, at: (0, 0))] * count,
+            out_specs=pl.BlockSpec((rows, width), lambda q, at: (q ^ at[0], 0)),
+        ),
+        out_shape=jax.ShapeDtypeStruct((count * rows, width), slots[0].dtype),
+        compiler_params=params(),
+        cost_estimate=COST,
+        name=name,
+    )(at, *slots)
 
 
 def attention_kernel(qa_ref, qb_ref, da_ref, db_ref, *rest, block):
@@ -457,10 +517,14 @@
     )(head, x, weight, *before)
 
 
-def weight_kernel(at_ref, xa_ref, xb_ref, ga_ref, gb_ref, ra_ref, rb_ref, *rest):
-    del at_ref
+def weight_kernel(
+    at_ref, xa_ref, ya_ref, xb_ref, yb_ref, ga_ref, gb_ref, ra_ref, rb_ref, *rest
+):
     out_refs, turned = rest[:-1], rest[-1]
     step = pl.program_id(0)
+    last = (step ^ at_ref[0]) == pl.num_programs(0) - 1
+    xa = jnp.where(last, ya_ref[...], xa_ref[...])
+    xb = jnp.where(last, yb_ref[...], xb_ref[...])
     half = ra_ref.shape[0]
     split = 3 * DH
 
@@ -470,7 +534,7 @@
         turned[:, half:] = rb_ref[...].T
 
     a, b = slice(0, half), slice(half, 2 * half)
-    qkv = dot(turned[:split, a], xa_ref[...], NN) + dot(turned[:split, b], xb_ref[...], NN)
+    qkv = dot(turned[:split, a], xa, NN) + dot(turned[:split, b], xb, NN)
     out = dot(turned[split:, a], ga_ref[...], NN) + dot(turned[split:, b], gb_ref[...], NN)
     keep_a, send_a, keep_b, send_b = out_refs
     rows = keep_a.shape[1]
@@ -485,10 +549,12 @@
             second[slot % 2, split - rows :] = out.astype(BF)
 
 
-def weight_gradients(at, xa, xb, ga, gb, ra, rb, seqs):
-    half, width = xa.shape
+def weight_gradients(at, xa, ya, xb, yb, ga, gb, ra, rb, seqs):
+    half, width = ga.shape
     chunk = width // seqs
     full = ra.shape[1]
+    some = pl.BlockSpec((half, chunk), lambda r, at: (0, jnp.minimum(r ^ at[0], seqs - 2)))
+    only = pl.BlockSpec((half, chunk), lambda r, at: (0, 0))
     column = pl.BlockSpec((half, chunk), lambda r, at: (0, r ^ at[0]))
     rest = pl.BlockSpec((half, full), lambda r, at: (0, 0))
     return pl.pallas_call(
@@ -496,7 +562,7 @@
         grid_spec=pltpu.PrefetchScalarGridSpec(
             num_scalar_prefetch=1,
             grid=(seqs,),
-            in_specs=[column] * 4 + [rest] * 2,
+            in_specs=[some, only] * 2 + [column] * 2 + [rest] * 2,
             out_specs=[pl.BlockSpec((2, full // 2, chunk), lambda r, at: (0, 0, 0))] * 4,
             scratch_shapes=[pltpu.VMEM((full, 2 * half), BF)],
         ),
@@ -504,7 +570,7 @@
         compiler_params=params(STREAMING_LIMIT),
         cost_estimate=COST,
         name="weight_gradients",
-    )(at, xa, xb, ga, gb, ra, rb)
+    )(at, xa, ya, xb, yb, ga, gb, ra, rb)
 
 
 def turn_kernel(keep_a, got_a, keep_b, got_b, *rest):
@@ -635,6 +701,11 @@
     return lax.ppermute(x, "seq", [(s, s ^ (bit * heads)) for s in range(count)])
 
 
+def trade_z(x, bit):
+    count = lax.axis_size("head")
+    return lax.ppermute(x, "head", [(z, z ^ bit) for z in range(count)])
+
+
 def swap_heads(x):
     count = lax.axis_size("seq")
     return lax.ppermute(x, "seq", [(s, s + 1 - 2 * (s % 2)) for s in range(count)])
@@ -664,33 +735,40 @@
 
     pairs = jnp.transpose(enc_in.reshape(rows, 2, seqs, enc_in.shape[2]), (1, 2, 0, 3))
     low, high = neighbour_edges(pairs[:, :, :1, :], pairs[:, :, -1:, :])
+    w_pack, w_turned, packed = pack_weights(w_qkv)
+    low, high, packed = lax.optimization_barrier((low, high, packed))
     skip, slope, normed = encoder(at, pairs, low, high, conv_weight, norm_gain)
     normed = to_chips(normed)
-    normed_slab = jnp.concatenate([normed[j] for j in order], axis=0)
-    normed_rows = lax.all_gather(normed_slab, "head", axis=0, tiled=True)
-
-    grad_z = after(grad_z, normed_slab)
+    edge = width - width // seqs
+    slab_a = jnp.concatenate([normed[j][:, :edge] for j in order], axis=0)
+    slab_b = jnp.concatenate([normed[j][:, edge:] for j in order], axis=0)
+    normed_a = lax.all_gather(slab_a, "head", axis=0, tiled=True)
+    slabs_b = [slab_b if q == 0 else trade_z(slab_b, q) for q in range(groups)]
+    normed_b = placed(lax.axis_index("head").astype(jnp.int32).reshape(1), slabs_b, "normed_last")
+
+    grad_z = after(grad_z, slab_a, *slabs_b[1:])
     grad_slots = to_chips(
         [lax.dynamic_index_in_dim(grad_z, own_seq ^ j, 2, keepdims=False) for j in range(seqs)]
     )
     grad_rows = jnp.stack([grad_slots[j] for j in order], axis=1).reshape(half, width)
-    w_pack, w_turned, packed = pack_weights(after(w_qkv, normed_slab))
     w_rows = w_out.reshape(heads, DH, width)
     d_other, one = head_product(head_other, grad_rows, w_rows, NT, "d_o_other")
     d_got = swap_heads(d_other)
     d_mine, two = head_product(head_mine, grad_rows, w_rows, NT, "d_o_own")
     grad_swapped = swap_heads(grad_rows)
-    normed_rows, d_got, d_mine, grad_swapped, w_pack, w_turned, *tokens = (
+    normed_a, normed_b, d_got, d_mine, grad_swapped, w_pack, w_turned, *tokens = (
         lax.optimization_barrier(
-            (normed_rows, d_got, d_mine, grad_swapped, w_pack, w_turned, packed, one, two)
+            (normed_a, normed_b, d_got, d_mine, grad_swapped, w_pack, w_turned, packed, one, two)
         )
     )
 
-    normed_swapped = swap_heads(normed_rows)
-    qkv_other, _ = head_product(head_other, normed_rows, w_pack, NN, "qkv_other", *tokens)
+    swapped_a, swapped_b = swap_heads(normed_a), swap_heads(normed_b)
+    qkv_other = split_product(head_other, normed_a, normed_b, w_pack, "qkv_other", *tokens)
     qkv_got = swap_heads(qkv_other)
-    qkv_mine, _ = head_product(head_mine, normed_rows, w_pack, NN, "qkv_own")
-    result_mine, result_other = attention(qkv_mine, qkv_got, d_mine, d_got, normed_swapped)
+    qkv_mine = split_product(head_mine, normed_a, normed_b, w_pack, "qkv_own")
+    result_mine, result_other = attention(
+        qkv_mine, qkv_got, d_mine, d_got, swapped_a, swapped_b
+    )
     result_got = swap_heads(result_other)
 
     shape = (groups, seqs, rows, width)
@@ -699,8 +777,10 @@
     d_normed = lax.psum_scatter(d_term.reshape(shape), "head", scatter_dimension=0, tiled=False)
     keep_a, send_a, keep_b, send_b = weight_gradients(
         own_seq.reshape(1),
-        normed_rows,
-        normed_swapped,
+        normed_a,
+        normed_b,
+        swapped_a,
+        swapped_b,
         grad_rows,
         grad_swapped,
         result_mine,
@@ -738,7 +818,7 @@
         at, [near_a, near_b], near_other, False, (), grad_input
     )
 
-    head_sum = after(head_sum, grad_input, token)
+    head_sum = after(head_sum, grad_input)
     head_sum = to_chips([head_sum[order.index(j)] for j in range(seqs)])
     far_other = [swap_heads(after(x, *head_sum[1:])) for x in (far_a, far_b)]
     grad_w_qkv, grad_w_out, _ = unpack_weights(at, [far_a, far_b], far_other, True, outputs)
@@ -893,7 +973,7 @@
 def body(enc_in, conv_weight, norm_gain, w_qkv, w_out, grad_out):
     heads = w_qkv.shape[2] // DH
     seqs = enc_in.shape[1]
-    fits = heads == 2 and seqs == 4 and seqs * heads == lax.axis_size("seq")
+    fits = lax.axis_size("head") == 4 and heads == 2 and seqs == 4 and seqs * heads == lax.axis_size("seq")
     fits = fits and conv_weight.shape[2] == seqs * w_qkv.shape[2]
     chosen = unit_body if fits else gathered_body
     return chosen(enc_in, conv_weight, norm_gain, w_qkv, w_out, grad_out)

time: 209 us -> 220 us (1.053)
  starting transfers between devices: 40.2 us -> 45.1 us
    all_gather x1, waiting for transfers between devices: 5.92 us -> 0.01 us  [unit_body(): grad_z = lax.all_gather(grad_out, 'head', axis=0, tiled=False)]
    ppermute x0 -> x3, starting transfers between devices: none -> 4.44 us  [trade_z(): return lax.ppermute(x, 'head', [(z, z ^ bit) for z in range(count)])]
    ppermute x0 -> x3, waiting for transfers between devices: none -> 3.18 us  [trade_z(): return lax.ppermute(x, 'head', [(z, z ^ bit) for z in range(count)])]
    pallas_call x0 -> x3, Pallas kernels: none -> 3.17 us  [the longest x2 3.03 us: split_product(): pl.pallas_call(split_product_kernel, grid_spec=pltpu.PrefetchScalarGridSp...]
    pallas_call x4 -> x2, Pallas kernels: 4.99 us -> 1.92 us  [head_product(): pl.pallas_call(functools.partial(product_kernel, contract=contract), grid...]
    all_gather x1, waiting for transfers between devices: 2.17 us -> 4.84 us  [unit_body(): normed_a = lax.all_gather(slab_a, 'head', axis=0, tiled=True)]
    ppermute x9 -> x10, starting transfers between devices: 6.4 us -> 6.96 us  [swap_heads(): lax.ppermute(x, 'seq', [(s, s + 1 - 2 * (s % 2)) for s in range(count)])]
    unnamed x66 -> x81, local copies, waits for them, and re-layouts: 22.7 us -> 23 us
  transfers between devices with their start and end apart: 36 -> 40, of which waited for: 20 -> 22; matrix products, arithmetic and copies ran while one was open for 5% -> 5% of each run, Pallas kernels for 21% -> 20%
where the time goes in v15:
time: 220 us; the launch traced here: 217 us
  waiting for transfers between devices  65.5 us (30%)
  Pallas kernels  57.6 us (26%)
  starting transfers between devices  45.1 us (20%)
  local copies, waits for them, and re-layouts  32.4 us (15%)
  between operations  14.4 us (7%)
    ppermute x19, waiting for transfers between devices, trade_chip(): return lax.ppermute(x, 'seq', [(s, s ^ bit * heads) for s in range(count)])  49.7 us
    unnamed x81, local copies, waits for them, and re-layouts  23 us
    ppermute x19, starting transfers between devices, trade_chip(): return lax.ppermute(x, 'seq', [(s, s ^ bit * heads) for s in range(count)])  20 us
    pallas_call x1, Pallas kernels, encoder(): pl.pallas_call(conv_kernel, grid=(width // tile,), in_specs=[SCALARS, who...  10.1 us
    pallas_call x1, Pallas kernels, weight_gradients(): pl.pallas_call(weight_kernel, grid_spec=pltpu.PrefetchScalarGridSpec(num_...  9.29 us
    pallas_call x2, Pallas kernels, unpack_weights(): pl.pallas_call(unpack_kernel, grid_spec=pltpu.PrefetchScalarGridSpec(num_...  8.39 us
    ppermute x2, starting transfers between devices, neighbour_edges(): lax.ppermute(last, axes, forward)  7.12 us
    ppermute x10, starting transfers between devices, swap_heads(): lax.ppermute(x, 'seq', [(s, s + 1 - 2 * (s % 2)) for s in range(count)])  6.96 us
  transfers between devices with their start and end apart: 40, of which 22 were waited for; matrix products, arithmetic and copies ran while one was open for 5% of the time, Pallas kernels for 20%

profile of v15, /device:TPU:26, one launch (start us, length us, event | category | flops | bytes accessed | tf_op | source)
XLA Modules:
  0.0 216.6 jit_solution(4733006890571210039)
XLA Ops:
  11.4 5.0 %collective-permute-start = (bf16[2,4,1,768]{3,2,1,0:T(2,128)(2,1)S(1)}, bf16[2,4,1,768]{3,2,1,0:T(2,128)(2,1)S(1)}, u32[]{:S(2)}, u32[]{:S(2)}) collective-permute-start(bf16[2,4,1,768]{3,2,1,0:T(2,128)(2,1)S(1)} %get-tuple-element.135), channel_id=1, source_target_pairs={{0,1},{1,2},{2,3},{3,4},{4,5},{5,6},{6,7},{7,8},{8,9},{9,10},{10,1... | collective-permute-start | bytes 36872 | tf_op jit(solution)/shard_map/ppermute | solution.py:692
  19.3 3.9 %pack_weights.1 = (bf16[2,1536,576]{2,1,0:T(8,128)(2,1)S(1)}, bf16[2,576,1536]{2,1,0:T(8,128)(2,1)S(1)}, f32[8,128]{1,0:T(8,128)S(1)}) custom-call(bf16[3,1536,384]{2,1,0:T(8,128)(2,1)S(1)} %copy-done.12), custom_call_target="tpu_custom_call" | custom-call | flops 1000 | bytes 1000 | tf_op jit(solution)/shard_map/pack_weights/pallas_call | solution.py:280
  28.1 10.1 %encoder_forward.1 = (bf16[4,32,1536]{2,1,0:T(8,128)(2,1)}, f32[2,4,32,1536]{3,2,1,0:T(8,128)}, bf16[32,1536]{1,0:T(8,128)(2,1)}, bf16[32,1536]{1,0:T(8,128)(2,1...) custom-call(s32[2]{0:T(128)} %pad_add_fusion.at_ref, bf16[2,4,32,768]{3,2,1,0:T(8,128)(2,1)} %bitcast.59, ...), custom_call_target="tpu_custom_call" | custom-call | flops 1000 | bytes 1000 | tf_op jit(solution)/shard_map/encoder_forward/pallas_call | solution.py:111
  47.7 4.3 %collective-permute-start.5 = (bf16[128,384]{1,0:T(8,128)(2,1)S(1)}, bf16[128,384]{1,0:T(8,128)(2,1)S(1)}, u32[]{:S(2)}, u32[]{:S(2)}) collective-permute-start(bf16[128,384]{1,0:T(8,128)(2,1)S(1)} %pad_maximum_fusion.3.refs_0_), channel_id=1, source_target_pairs={{0,1},{1,0},{2,3},{3,2},{4,5},{5,4},{6,7},{7,6},{8,9},{9,8},{10,11... | collective-permute-start | bytes 294920 | tf_op jit(solution)/shard_map/ppermute | solution.py:706
  55.1 2.5 %collective-permute-done.6.refs_2_ = bf16[128,384]{1,0:T(8,128)(2,1)S(1)} collective-permute-done((bf16[128,384]{1,0:T(8,128)(2,1)S(1)}, bf16[128,384]{1,0:T(8,128)(2,1)S(1)}, u32[]{:S(2)}, u32[]{:S(2)}) %collective-permute-start.6) | collective-permute-done | bytes 98336 | tf_op jit(solution)/shard_map/ppermute | solution.py:706
  62.0 9.3 %collective-permute-done.10 = bf16[4,32,1536]{2,1,0:T(8,128)(2,1)S(1)} collective-permute-done((bf16[4,32,1536]{2,1,0:T(8,128)(2,1)S(1)}, bf16[4,32,1536]{2,1,0:T(8,128)(2,1)S(1)}, u32[]{:S(2)}, u32[]{:S(2)}) %collective-permute-start.10) | collective-permute-done | bytes 393248 | tf_op jit(solution)/shard_map/ppermute | solution.py:701
  71.2 4.8 %collective-permute-done.9 = bf16[4,32,1536]{2,1,0:T(8,128)(2,1)S(1)} collective-permute-done((bf16[4,32,1536]{2,1,0:T(8,128)(2,1)S(1)}, bf16[4,32,1536]{2,1,0:T(8,128)(2,1)S(1)}, u32[]{:S(2)}, u32[]{:S(2)}) %collective-permute-start.9) | collective-permute-done | bytes 393248 | tf_op jit(solution)/shard_map/ppermute | solution.py:701
  85.7 4.8 %all-gather.4.cloned.1.call-done.xa_ref = bf16[512,1152]{1,0:T(8,128)(2,1)} async-done(((bf16[128,1152]{1,0:T(8,128)(2,1)}), bf16[512,1152]{1,0:T(8,128)(2,1)}) %all-gather.4.cloned.1.call-update) | async-done | bytes 1179664 | tf_op jit(solution)/shard_map/all_gather | solution.py:745
  98.4 6.5 %attention.1 = (bf16[512,768]{1,0:T(8,128)(2,1)S(1)}, bf16[512,768]{1,0:T(8,128)(2,1)S(1)}) custom-call(bf16[512,640]{1,0:T(8,128)(2,1)S(1)} %qkv_own.1.qa_ref, bf16[512,640]{1,0:T(8,128)(2,1)S(1)} %collective-permute-done.13.qb_ref, bf16[512,256]{1,0:T(8,128)(2,1)S(1)} %copy-done.25, bf16[512,256]{1,0:T(8,128)(2,1)S(1)} %copy-done.23, ...), custom_call_target="tpu_custom_call" | custom-call | flops 1000 | bytes 1000 | tf_op jit(solution)/shard_map/attention/pallas_call | solution.py:441
  107.5 3.1 %d_term.1 = bf16[512,1536]{1,0:T(8,128)(2,1)} custom-call(s32[1]{0:T(128)} %bitcast.5.head_ref, bf16[512,768]{1,0:T(8,128)(2,1)S(1)} %collective-permute-done.16.b_ref.x_ref, bf16[2,576,1536]{2,1,0:T(8,128)(2,1)S(1)} %copy-done.5, f32[512,1536]{1,0:T(8,128)S(1)} %d_term_own.1.rest_0_), custom_call_target="tpu_custom_call" | custom-call | flops 1000 | bytes 1000 | tf_op jit(solution)/shard_map/d_term/pallas_call | solution.py:501
  110.9 2.6 %head_term.1.rest_0_ = bf16[512,1536]{1,0:T(8,128)(2,1)} custom-call(s32[1]{0:T(128)} %bitcast.1.head_ref, bf16[512,768]{1,0:T(8,128)(2,1)S(1)} %get-tuple-element.82.a_ref.x_ref.ra_ref, bf16[512,768]{1,0:T(8,128)(2,1)S(1)} %collective-permute-done.16.b_ref.x_ref, bf16[2,192,1536]{2,1,0:T(8,128)(2,1)S(1)} %bitcast.49), custom_call_target="tpu_custom_call" | custom-call | flops 1000 | bytes 1000 | tf_op jit(solution)/shard_map/head_term/pallas_call | solution.py:468
  113.6 9.3 %weight_gradients.1 = (bf16[2,384,384]{2,1,0:T(8,128)(2,1)}, bf16[2,384,384]{2,1,0:T(8,128)(2,1)}, bf16[2,384,384]{2,1,0:T(8,128)(2,1)}, bf16[2,384,384]{2,1,0:T(8,128)(2,1)}) custom-call(s32[1]{0:T(128)} %bitcast.at_ref, bf16[512,1152]{1,0:T(8,128)(2,1)} %all-gather.4.cloned.1.call-done.xa_ref, bf16[512,384]{1,0:T(8,128)(2,1)} %copy-done.10, ...), custom_call_target="tpu_custom_call" | custom-call | flops 1000 | bytes 1000 | tf_op jit(solution)/shard_map/weight_gradients/pallas_call | solution.py:560
  124.8 13.6 %collective-permute-done.17.got_a = bf16[2,384,384]{2,1,0:T(8,128)(2,1)S(1)} collective-permute-done((bf16[2,384,384]{2,1,0:T(8,128)(2,1)}, bf16[2,384,384]{2,1,0:T(8,128)(2,1)S(1)}, u32[]{:S(2)}, u32[]{:S(2)}) %collective-permute-start.17) | collective-permute-done | bytes 589856 | tf_op jit(solution)/shard_map/ppermute | solution.py:701
  141.1 4.0 %reduce-scatter.5.cloned.1.call-done = bf16[1,4,32,1536]{3,2,1,0:T(8,128)(2,1)} async-done(((bf16[4,4,32,1536]{3,2,1,0:T(8,128)(2,1)}), bf16[1,4,32,1536]{3,2,1,0:T(8,128)(2,1)}) %reduce-scatter.5.cloned.1.call-update) | async-done | bytes 393232 | tf_op jit(solution)/shard_map/reduce_scatter | solution.py:777
  150.5 3.4 %collective-permute-done.19.near_ref = bf16[2,32,1536]{2,1,0:T(8,128)(2,1)S(1)} collective-permute-done((bf16[2,32,1536]{2,1,0:T(8,128)(2,1)S(1)}, bf16[2,32,1536]{2,1,0:T(8,128)(2,1)S(1)}, u32[]{:S(2)}, u32[]{:S(2)}) %collective-permute-start.19) | collective-permute-done | bytes 196640 | tf_op jit(solution)/shard_map/ppermute | solution.py:701
  155.7 3.4 %collective-permute-done.22.last_b = bf16[384,384]{1,0:T(8,128)(2,1)S(1)} collective-permute-done((bf16[384,384]{1,0:T(8,128)(2,1)S(1)}, bf16[384,384]{1,0:T(8,128)(2,1)S(1)}, u32[]{:S(2)}, u32[]{:S(2)}) %collective-permute-start.22) | collective-permute-done | bytes 294944 | tf_op jit(solution)/shard_map/ppermute | solution.py:701
  164.9 3.7 %collective-permute-start.24 = (bf16[2,4,1,1536]{3,2,1,0:T(2,128)(2,1)S(1)}, bf16[2,4,1,1536]{3,2,1,0:T(2,128)(2,1)S(1)}, u32[]{:S(2)}, u32[]{:S(2)}) collective-permute-start(bf16[2,4,1,1536]{3,2,1,0:T(2,128)(2,1)S(1)} %get-tuple-element.99.refs_1_), channel_id=1, source_target_pairs={{1,0},{2,1},{3,2},{4,3},{5,4},{6,5},{7,6},{8,7},{9,8},{10,9},{11,1... | collective-permute-start | bytes 73736 | tf_op jit(solution)/shard_map/ppermute | solution.py:692
  168.7 4.4 %copy-done = bf16[5,768,1536]{2,1,0:T(8,128)(2,1)S(1)} copy-done((bf16[5,768,1536]{2,1,0:T(8,128)(2,1)S(1)}, bf16[5,768,1536]{2,1,0:T(8,128)(2,1)}, u32[]{:S(2)}) %copy-start) | copy-done | bytes 11796504
  173.4 4.9 %collective-permute-start.28 = (bf16[384,768]{1,0:T(8,128)(2,1)S(1)}, bf16[384,768]{1,0:T(8,128)(2,1)S(1)}, u32[]{:S(2)}, u32[]{:S(2)}) collective-permute-start(bf16[384,768]{1,0:T(8,128)(2,1)S(1)} %constant_dynamic-update-slice_fusion.2.refs_1_), channel_id=1, source_target_pairs={{0,4},{4,0},{8,12},{12,8},{16,20},{20,16},{24,28},{28,24},{1,5},{5... | collective-permute-start | bytes 1769480 | tf_op jit(solution)/shard_map/ppermute | solution.py:711
  180.8 4.2 %encoder_backward.1.refs_4_ = bf16[256,768]{1,0:T(8,128)(2,1)S(1)} custom-call(bf16[2,4,32,1536]{3,2,1,0:T(8,128)(2,1)S(1)} %get-tuple-element.97.d_ref, bf16[2,4,1,1536]{3,2,1,0:T(2,128)(2,1)S(1)} %collective-permute-done.23.low_ref, bf16[2,4,1,1536]{3,2,1,0:T(2,128)(2,1)S(1)} %collective-permute-done.24.high_ref, bf16[5,768,1536]{2,1,0:T(8,128)(2,1)S(1)} %copy-done, ...), custom_call_target="tpu_custom_call" | custom-call | flops 1000 | bytes 1000 | tf_op jit(solution)/shard_map/encoder_backward/pallas_call | solution.py:244
  189.7 5.0 %collective-permute-done.33.refs_1_ = bf16[384,768]{1,0:T(8,128)(2,1)} collective-permute-done((bf16[384,768]{1,0:T(8,128)(2,1)S(1)}, bf16[384,768]{1,0:T(8,128)(2,1)}, u32[]{:S(2)}, u32[]{:S(2)}) %collective-permute-start.33) | collective-permute-done | bytes 589856 | tf_op jit(solution)/shard_map/ppermute | solution.py:701
  194.7 3.6 %collective-permute-done.30.refs_2_ = bf16[32,1536]{1,0:T(8,128)(2,1)S(1)} collective-permute-done((bf16[32,1536]{1,0:T(8,128)(2,1)S(1)}, bf16[32,1536]{1,0:T(8,128)(2,1)S(1)}, u32[]{:S(2)}, u32[]{:S(2)}) %collective-permute-start.30) | collective-permute-done | bytes 98336 | tf_op jit(solution)/shard_map/ppermute | solution.py:701
  198.9 3.4 %weight_outputs_near.1 = (f32[3,1536,384]{2,1,0:T(8,128)}, f32[2,2,96,1536]{3,2,1,0:T(8,128)}, f32[8,128]{1,0:T(8,128)S(1)}) custom-call(s32[2]{0:T(128)S(1)} %copy-done.33, bf16[384,768]{1,0:T(8,128)(2,1)S(1)} %constant_dynamic-update-slice_fusion.refs_0_, bf16[384,768]{1,0:T(8,128)(2,1)S(1)} %constant_dynamic-update-slice_fusion.2.refs_1_, ...), custom_call_target="tpu_custom_call" | custom-call | flops 1000 | bytes 1000 | tf_op jit(solution)/shard_map/weight_outputs_near/pallas_call | solution.py:661
  205.1 5.0 %weight_outputs_far.1 = (f32[3,1536,384]{2,1,0:T(8,128)}, f32[2,2,96,1536]{3,2,1,0:T(8,128)}, f32[8,128]{1,0:T(8,128)}) custom-call(s32[2]{0:T(128)S(1)} %copy-done.33, bf16[384,768]{1,0:T(8,128)(2,1)} %collective-permute-done.32.refs_0_, bf16[384,768]{1,0:T(8,128)(2,1)} %collective-permute-done.33.refs_1_, ...), custom_call_target="tpu_custom_call", output_to_operand_aliasing={{0}: (5, {}), {1}: (6, {})} | custom-call | flops 1000 | bytes 1000 | tf_op jit(solution)/shard_map/weight_outputs_far/pallas_call | solution.py:661
  (188 shorter events, 77.2 us)
Async XLA Ops:
  7.2 45.6 %all-gather.6.cloned.1.call-start = ((), (), s32[]{:S(2)}) async-start(), calls=%async_computation.5 | async-start | bytes 1966080 | tf_op jit(solution)/shard_map/all_gather | solution.py:734
  7.9 82.6 %all-gather.4.cloned.1.call-start = ((), (), s32[]{:S(2)}) async-start(), calls=%async_computation.2 | async-start | bytes 1474560 | tf_op jit(solution)/shard_map/all_gather | solution.py:745
  9.1 18.5 %collective-permute-start.1 = (bf16[2,4,1,768]{3,2,1,0:T(2,128)(2,1)S(1)}, bf16[2,4,1,768]{3,2,1,0:T(2,128)(2,1)S(1)}, u32[]{:S(2)}, u32[]{:S(2)}) collective-permute-start(bf16[2,4,1,768]{3,2,1,0:T(2,128)(2,1)S(1)} %get-tuple-element.134), channel_id=1, source_target_pairs={{1,0},{2,1},{3,2},{4,3},{5,4},{6,5},{7,6},{8,7},{9,8},{10,9},{11,1... | collective-permute-start | bytes 36872 | tf_op jit(solution)/shard_map/ppermute | solution.py:692
  11.4 16.1 %collective-permute-start = (bf16[2,4,1,768]{3,2,1,0:T(2,128)(2,1)S(1)}, bf16[2,4,1,768]{3,2,1,0:T(2,128)(2,1)S(1)}, u32[]{:S(2)}, u32[]{:S(2)}) collective-permute-start(bf16[2,4,1,768]{3,2,1,0:T(2,128)(2,1)S(1)} %get-tuple-element.135), channel_id=1, source_target_pairs={{0,1},{1,2},{2,3},{3,4},{4,5},{5,6},{6,7},{7,8},{8,9},{9,10},{10,1... | collective-permute-start | bytes 36872 | tf_op jit(solution)/shard_map/ppermute | solution.py:692
  47.6 10.0 %collective-permute-start.6 = (bf16[128,384]{1,0:T(8,128)(2,1)S(1)}, bf16[128,384]{1,0:T(8,128)(2,1)S(1)}, u32[]{:S(2)}, u32[]{:S(2)}) collective-permute-start(bf16[128,384]{1,0:T(8,128)(2,1)S(1)} %pad_maximum_fusion.3.refs_0_), channel_id=1, source_target_pairs={{0,2},{1,3},{2,0},{3,1},{4,6},{5,7},{6,4},{7,5},{8,10},{9,11},{10,... | collective-permute-start | bytes 294920 | tf_op jit(solution)/shard_map/ppermute | solution.py:706
  47.7 9.9 %collective-permute-start.5 = (bf16[128,384]{1,0:T(8,128)(2,1)S(1)}, bf16[128,384]{1,0:T(8,128)(2,1)S(1)}, u32[]{:S(2)}, u32[]{:S(2)}) collective-permute-start(bf16[128,384]{1,0:T(8,128)(2,1)S(1)} %pad_maximum_fusion.3.refs_0_), channel_id=1, source_target_pairs={{0,1},{1,0},{2,3},{3,2},{4,5},{5,4},{6,7},{7,6},{8,9},{9,8},{10,11... | collective-permute-start | bytes 294920 | tf_op jit(solution)/shard_map/ppermute | solution.py:706
  58.2 13.0 %collective-permute-start.10 = (bf16[4,32,1536]{2,1,0:T(8,128)(2,1)S(1)}, bf16[4,32,1536]{2,1,0:T(8,128)(2,1)S(1)}, u32[]{:S(2)}, u32[]{:S(2)}) collective-permute-start(bf16[4,32,1536]{2,1,0:T(8,128)(2,1)S(1)} %get-tuple-element.127), channel_id=1, source_target_pairs={{0,24},{4,28},{8,16},{12,20},{16,8},{20,12},{24,0},{28,4},{1,25},{... | collective-permute-start | bytes 1179656 | tf_op jit(solution)/shard_map/ppermute | solution.py:701
  59.5 16.6 %collective-permute-start.9 = (bf16[4,32,1536]{2,1,0:T(8,128)(2,1)S(1)}, bf16[4,32,1536]{2,1,0:T(8,128)(2,1)S(1)}, u32[]{:S(2)}, u32[]{:S(2)}) collective-permute-start(bf16[4,32,1536]{2,1,0:T(8,128)(2,1)S(1)} %get-tuple-element.128), channel_id=1, source_target_pairs={{0,8},{4,12},{8,0},{12,4},{16,24},{20,28},{24,16},{28,20},{1,9},{5... | collective-permute-start | bytes 1179656 | tf_op jit(solution)/shard_map/ppermute | solution.py:701
  60.1 18.0 %collective-permute-start.8 = (bf16[4,32,1536]{2,1,0:T(8,128)(2,1)S(1)}, bf16[4,32,1536]{2,1,0:T(8,128)(2,1)S(1)}, u32[]{:S(2)}, u32[]{:S(2)}) collective-permute-start(bf16[4,32,1536]{2,1,0:T(8,128)(2,1)S(1)} %get-tuple-element.129), channel_id=1, source_target_pairs={{0,16},{4,20},{8,24},{12,28},{16,0},{20,4},{24,8},{28,12},{1,17},{... | collective-permute-start | bytes 1179656 | tf_op jit(solution)/shard_map/ppermute | solution.py:701
  61.8 83.3 %reduce-scatter.5.cloned.1.call-start = ((), (), s32[]{:S(2)}) async-start(), calls=%async_computation.4 | async-start | bytes 1966080 | tf_op jit(solution)/shard_map/reduce_scatter | solution.py:777
  78.4 12.1 %collective-permute-start.12 = (bf16[512,1536]{1,0:T(8,128)(2,1)S(1)}, bf16[512,1536]{1,0:T(8,128)(2,1)}, u32[]{:S(2)}, u32[]{:S(2)}) collective-permute-start(bf16[512,1536]{1,0:T(8,128)(2,1)S(1)} %bitcast.43), channel_id=1, source_target_pairs={{0,4},{4,0},{8,12},{12,8},{16,20},{20,16},{24,28},{28,24},{1,5},{5... | collective-permute-start | bytes 4718600 | tf_op jit(solution)/shard_map/ppermute | solution.py:711
  81.4 9.1 %collective-permute-start.11 = (bf16[512,256]{1,0:T(8,128)(2,1)}, bf16[512,256]{1,0:T(8,128)(2,1)S(1)}, u32[]{:S(2)}, u32[]{:S(2)}) collective-permute-start(bf16[512,256]{1,0:T(8,128)(2,1)} %get-tuple-element.67), channel_id=1, source_target_pairs={{0,4},{4,0},{8,12},{12,8},{16,20},{20,16},{24,28},{28,24},{1,5},{5... | collective-permute-start | bytes 786440 | tf_op jit(solution)/shard_map/ppermute | solution.py:711
  110.6 74.4 %reduce-scatter.3.cloned.1.call-start = ((), (), s32[]{:S(2)}) async-start(), calls=%async_computation.3 | async-start | bytes 1966080 | tf_op jit(solution)/shard_map/reduce_scatter | solution.py:794
  122.9 15.6 %collective-permute-start.17 = (bf16[2,384,384]{2,1,0:T(8,128)(2,1)}, bf16[2,384,384]{2,1,0:T(8,128)(2,1)S(1)}, u32[]{:S(2)}, u32[]{:S(2)}) collective-permute-start(bf16[2,384,384]{2,1,0:T(8,128)(2,1)} %get-tuple-element.87), channel_id=1, source_target_pairs={{0,8},{4,12},{8,0},{12,4},{16,24},{20,28},{24,16},{28,20},{1,9},{5... | collective-permute-start | bytes 1769480 | tf_op jit(solution)/shard_map/ppermute | solution.py:701
  123.4 15.3 %collective-permute-start.18 = (bf16[2,384,384]{2,1,0:T(8,128)(2,1)}, bf16[2,384,384]{2,1,0:T(8,128)(2,1)S(1)}, u32[]{:S(2)}, u32[]{:S(2)}) collective-permute-start(bf16[2,384,384]{2,1,0:T(8,128)(2,1)} %get-tuple-element.89), channel_id=1, source_target_pairs={{0,16},{4,20},{8,24},{12,28},{16,0},{20,4},{24,8},{28,12},{1,17},{... | collective-permute-start | bytes 1769480 | tf_op jit(solution)/shard_map/ppermute | solution.py:701
  146.7 9.0 %collective-permute-start.21 = (bf16[384,384]{1,0:T(8,128)(2,1)S(1)}, bf16[384,384]{1,0:T(8,128)(2,1)S(1)}, u32[]{:S(2)}, u32[]{:S(2)}) collective-permute-start(bf16[384,384]{1,0:T(8,128)(2,1)S(1)} %get-tuple-element.90), channel_id=1, source_target_pairs={{0,16},{4,20},{8,24},{12,28},{16,0},{20,4},{24,8},{28,12},{1,17},{... | collective-permute-start | bytes 884744 | tf_op jit(solution)/shard_map/ppermute | solution.py:701
  148.1 10.9 %collective-permute-start.22 = (bf16[384,384]{1,0:T(8,128)(2,1)S(1)}, bf16[384,384]{1,0:T(8,128)(2,1)S(1)}, u32[]{:S(2)}, u32[]{:S(2)}) collective-permute-start(bf16[384,384]{1,0:T(8,128)(2,1)S(1)} %get-tuple-element.91), channel_id=1, source_target_pairs={{0,8},{4,12},{8,0},{12,4},{16,24},{20,28},{24,16},{28,20},{1,9},{5... | collective-permute-start | bytes 884744 | tf_op jit(solution)/shard_map/ppermute | solution.py:701
  159.4 14.0 %collective-permute-start.25 = (bf16[192,768]{1,0:T(8,128)(2,1)S(1)}, bf16[192,768]{1,0:T(8,128)(2,1)S(1)}, u32[]{:S(2)}, u32[]{:S(2)}) collective-permute-start(bf16[192,768]{1,0:T(8,128)(2,1)S(1)} %get-tuple-element.96.refs_4_), channel_id=1, source_target_pairs={{0,8},{4,12},{8,0},{12,4},{16,24},{20,28},{24,16},{28,20},{1,9},{5... | collective-permute-start | bytes 884744 | tf_op jit(solution)/shard_map/ppermute | solution.py:701
  160.0 13.3 %collective-permute-start.27 = (bf16[192,768]{1,0:T(8,128)(2,1)S(1)}, bf16[192,768]{1,0:T(8,128)(2,1)S(1)}, u32[]{:S(2)}, u32[]{:S(2)}) collective-permute-start(bf16[192,768]{1,0:T(8,128)(2,1)S(1)} %get-tuple-element.104), channel_id=1, source_target_pairs={{0,16},{4,20},{8,24},{12,28},{16,0},{20,4},{24,8},{28,12},{1,17},{... | collective-permute-start | bytes 884744 | tf_op jit(solution)/shard_map/ppermute | solution.py:701
  162.8 10.3 %collective-permute-start.23 = (bf16[2,4,1,1536]{3,2,1,0:T(2,128)(2,1)S(1)}, bf16[2,4,1,1536]{3,2,1,0:T(2,128)(2,1)S(1)}, u32[]{:S(2)}, u32[]{:S(2)}) collective-permute-start(bf16[2,4,1,1536]{3,2,1,0:T(2,128)(2,1)S(1)} %get-tuple-element.98), channel_id=1, source_target_pairs={{0,1},{1,2},{2,3},{3,4},{4,5},{5,6},{6,7},{7,8},{8,9},{9,10},{10,1... | collective-permute-start | bytes 73736 | tf_op jit(solution)/shard_map/ppermute | solution.py:692
  178.4 16.3 %collective-permute-start.33 = (bf16[384,768]{1,0:T(8,128)(2,1)S(1)}, bf16[384,768]{1,0:T(8,128)(2,1)}, u32[]{:S(2)}, u32[]{:S(2)}) collective-permute-start(bf16[384,768]{1,0:T(8,128)(2,1)S(1)} %constant_dynamic-update-slice_fusion.2.refs_1_), channel_id=1, source_target_pairs={{0,8},{4,12},{8,0},{12,4},{16,24},{20,28},{24,16},{28,20},{1,9},{5... | collective-permute-start | bytes 1769480 | tf_op jit(solution)/shard_map/ppermute | solution.py:701
  178.5 19.9 %collective-permute-start.32 = (bf16[384,768]{1,0:T(8,128)(2,1)S(1)}, bf16[384,768]{1,0:T(8,128)(2,1)}, u32[]{:S(2)}, u32[]{:S(2)}) collective-permute-start(bf16[384,768]{1,0:T(8,128)(2,1)S(1)} %constant_dynamic-update-slice_fusion.refs_0_), channel_id=1, source_target_pairs={{0,16},{4,20},{8,24},{12,28},{16,0},{20,4},{24,8},{28,12},{1,17},{... | collective-permute-start | bytes 1769480 | tf_op jit(solution)/shard_map/ppermute | solution.py:701
  187.4 11.0 %collective-permute-start.30 = (bf16[32,1536]{1,0:T(8,128)(2,1)S(1)}, bf16[32,1536]{1,0:T(8,128)(2,1)S(1)}, u32[]{:S(2)}, u32[]{:S(2)}) collective-permute-start(bf16[32,1536]{1,0:T(8,128)(2,1)S(1)} %get-tuple-element.131), channel_id=1, source_target_pairs={{0,16},{4,20},{8,24},{12,28},{16,0},{20,4},{24,8},{28,12},{1,17},{... | collective-permute-start | bytes 294920 | tf_op jit(solution)/shard_map/ppermute | solution.py:701
  187.4 11.0 %collective-permute-start.29 = (bf16[32,1536]{1,0:T(8,128)(2,1)S(1)}, bf16[32,1536]{1,0:T(8,128)(2,1)S(1)}, u32[]{:S(2)}, u32[]{:S(2)}) collective-permute-start(bf16[32,1536]{1,0:T(8,128)(2,1)S(1)} %get-tuple-element.132), channel_id=1, source_target_pairs={{0,8},{4,12},{8,0},{12,4},{16,24},{20,28},{24,16},{28,20},{1,9},{5... | collective-permute-start | bytes 294920 | tf_op jit(solution)/shard_map/ppermute | solution.py:701
  (55 other events, 287.1 us)
Sparse Core Ops, SparseCore 0:
  9.6 35.9 all-gather.5
  61.9 28.6 all-gather.3
  110.8 34.2 reduce-scatter.4
  147.8 36.3 reduce-scatter.2

commit v16 on v15

--- a/solution.py
+++ b/solution.py
@@ -735,8 +735,6 @@
 
     pairs = jnp.transpose(enc_in.reshape(rows, 2, seqs, enc_in.shape[2]), (1, 2, 0, 3))
     low, high = neighbour_edges(pairs[:, :, :1, :], pairs[:, :, -1:, :])
-    w_pack, w_turned, packed = pack_weights(w_qkv)
-    low, high, packed = lax.optimization_barrier((low, high, packed))
     skip, slope, normed = encoder(at, pairs, low, high, conv_weight, norm_gain)
     normed = to_chips(normed)
     edge = width - width // seqs
@@ -746,11 +744,12 @@
     slabs_b = [slab_b if q == 0 else trade_z(slab_b, q) for q in range(groups)]
     normed_b = placed(lax.axis_index("head").astype(jnp.int32).reshape(1), slabs_b, "normed_last")
 
-    grad_z = after(grad_z, slab_a, *slabs_b[1:])
+    grad_z = after(grad_z, slab_a)
     grad_slots = to_chips(
         [lax.dynamic_index_in_dim(grad_z, own_seq ^ j, 2, keepdims=False) for j in range(seqs)]
     )
     grad_rows = jnp.stack([grad_slots[j] for j in order], axis=1).reshape(half, width)
+    w_pack, w_turned, packed = pack_weights(after(w_qkv, slab_a))
     w_rows = w_out.reshape(heads, DH, width)
     d_other, one = head_product(head_other, grad_rows, w_rows, NT, "d_o_other")
     d_got = swap_heads(d_other)
@@ -818,7 +817,7 @@
         at, [near_a, near_b], near_other, False, (), grad_input
     )
 
-    head_sum = after(head_sum, grad_input)
+    head_sum = after(head_sum, grad_input, token)
     head_sum = to_chips([head_sum[order.index(j)] for j in range(seqs)])
     far_other = [swap_heads(after(x, *head_sum[1:])) for x in (far_a, far_b)]
     grad_w_qkv, grad_w_out, _ = unpack_weights(at, [far_a, far_b], far_other, True, outputs)

time: 220 us -> 219 us (level)
  local copies, waits for them, and re-layouts: 32.4 us -> 34.9 us
    all_gather x1, waiting for transfers between devices: 0.01 us -> 5.95 us  [unit_body(): grad_z = lax.all_gather(grad_out, 'head', axis=0, tiled=False)]
    all_gather x1, waiting for transfers between devices: 4.84 us -> 0.01 us  [unit_body(): normed_a = lax.all_gather(slab_a, 'head', axis=0, tiled=True)]
    unnamed x81 -> x79, local copies, waits for them, and re-layouts: 23 us -> 24.8 us
  transfers between devices with their start and end apart: 40 -> 40, of which waited for: 22 -> 21; matrix products, arithmetic and copies ran while one was open for 5% -> 5% of each run, Pallas kernels for 20% -> 20%
where the time goes in v16:
time: 219 us; the launch traced here: 216 us
  waiting for transfers between devices  63.5 us (29%)
  Pallas kernels  57.1 us (26%)
  starting transfers between devices  44.7 us (20%)
  local copies, waits for them, and re-layouts  34.9 us (16%)
  between operations  14.3 us (7%)
    ppermute x19, waiting for transfers between devices, trade_chip(): return lax.ppermute(x, 'seq', [(s, s ^ bit * heads) for s in range(count)])  47.6 us
    unnamed x79, local copies, waits for them, and re-layouts  24.8 us
    ppermute x19, starting transfers between devices, trade_chip(): return lax.ppermute(x, 'seq', [(s, s ^ bit * heads) for s in range(count)])  20.1 us
    pallas_call x1, Pallas kernels, encoder(): pl.pallas_call(conv_kernel, grid=(width // tile,), in_specs=[SCALARS, who...  10.1 us
    pallas_call x1, Pallas kernels, weight_gradients(): pl.pallas_call(weight_kernel, grid_spec=pltpu.PrefetchScalarGridSpec(num_...  9.23 us
    pallas_call x2, Pallas kernels, unpack_weights(): pl.pallas_call(unpack_kernel, grid_spec=pltpu.PrefetchScalarGridSpec(num_...  7.75 us
    ppermute x2, starting transfers between devices, neighbour_edges(): lax.ppermute(last, axes, forward)  7.16 us
    ppermute x10, starting transfers between devices, swap_heads(): lax.ppermute(x, 'seq', [(s, s + 1 - 2 * (s % 2)) for s in range(count)])  6.75 us
  transfers between devices with their start and end apart: 40, of which 21 were waited for; matrix products, arithmetic and copies ran while one was open for 5% of the time, Pallas kernels for 20%

profile of v16, /device:TPU:26, one launch (start us, length us, event | category | flops | bytes accessed | tf_op | source)
XLA Modules:
  0.0 216.0 jit_solution(13821328166804827666)
XLA Ops:
  9.1 2.4 %collective-permute-start.1 = (bf16[2,4,1,768]{3,2,1,0:T(2,128)(2,1)S(1)}, bf16[2,4,1,768]{3,2,1,0:T(2,128)(2,1)S(1)}, u32[]{:S(2)}, u32[]{:S(2)}) collective-permute-start(bf16[2,4,1,768]{3,2,1,0:T(2,128)(2,1)S(1)} %get-tuple-element.130), channel_id=1, source_target_pairs={{1,0},{2,1},{3,2},{4,3},{5,4},{6,5},{7,6},{8,7},{9,8},{10,9},{11,1... | collective-permute-start | bytes 36872 | tf_op jit(solution)/shard_map/ppermute | solution.py:692
  11.4 5.0 %collective-permute-start = (bf16[2,4,1,768]{3,2,1,0:T(2,128)(2,1)S(1)}, bf16[2,4,1,768]{3,2,1,0:T(2,128)(2,1)S(1)}, u32[]{:S(2)}, u32[]{:S(2)}) collective-permute-start(bf16[2,4,1,768]{3,2,1,0:T(2,128)(2,1)S(1)} %get-tuple-element.131), channel_id=1, source_target_pairs={{0,1},{1,2},{2,3},{3,4},{4,5},{5,6},{6,7},{7,8},{8,9},{9,10},{10,1... | collective-permute-start | bytes 36872 | tf_op jit(solution)/shard_map/ppermute | solution.py:692
  19.6 10.1 %encoder_forward.1 = (bf16[4,32,1536]{2,1,0:T(8,128)(2,1)}, f32[2,4,32,1536]{3,2,1,0:T(8,128)}, bf16[32,1536]{1,0:T(8,128)(2,1)}, bf16[32,1536]{1,0:T(8,128)(2,1...) custom-call(s32[2]{0:T(128)} %pad_add_fusion.at_ref, bf16[2,4,32,768]{3,2,1,0:T(8,128)(2,1)} %bitcast.59, ...), custom_call_target="tpu_custom_call" | custom-call | flops 1000 | bytes 1000 | tf_op jit(solution)/shard_map/encoder_forward/pallas_call | solution.py:111
  39.6 6.0 %all-gather.6.cloned.1.call-done = bf16[128,4,1536]{2,1,0:T(4,128)(2,1)} async-done(((bf16[32,4,1536]{2,1,0:T(4,128)(2,1)}), bf16[128,4,1536]{2,1,0:T(4,128)(2,1)}) %all-gather.6.cloned.1.call-update) | async-done | bytes 1572880 | tf_op jit(solution)/shard_map/all_gather | solution.py:734
  51.0 9.4 %collective-permute-done.10 = bf16[4,32,1536]{2,1,0:T(8,128)(2,1)S(1)} collective-permute-done((bf16[4,32,1536]{2,1,0:T(8,128)(2,1)S(1)}, bf16[4,32,1536]{2,1,0:T(8,128)(2,1)S(1)}, u32[]{:S(2)}, u32[]{:S(2)}) %collective-permute-start.10) | collective-permute-done | bytes 393248 | tf_op jit(solution)/shard_map/ppermute | solution.py:701
  60.4 7.5 %collective-permute-done.9 = bf16[4,32,1536]{2,1,0:T(8,128)(2,1)S(1)} collective-permute-done((bf16[4,32,1536]{2,1,0:T(8,128)(2,1)S(1)}, bf16[4,32,1536]{2,1,0:T(8,128)(2,1)S(1)}, u32[]{:S(2)}, u32[]{:S(2)}) %collective-permute-start.9) | collective-permute-done | bytes 393248 | tf_op jit(solution)/shard_map/ppermute | solution.py:701
  72.0 2.8 %collective-permute-start.7 = (bf16[128,384]{1,0:T(8,128)(2,1)S(1)}, bf16[128,384]{1,0:T(8,128)(2,1)S(1)}, u32[]{:S(2)}, u32[]{:S(2)}) collective-permute-start(bf16[128,384]{1,0:T(8,128)(2,1)S(1)} %pad_maximum_fusion.3.refs_0_), channel_id=1, source_target_pairs={{0,3},{1,2},{2,1},{3,0},{4,7},{5,6},{6,5},{7,4},{8,11},{9,10},{10,... | collective-permute-start | bytes 294920 | tf_op jit(solution)/shard_map/ppermute | solution.py:706
  78.4 3.9 %pack_weights.1 = (bf16[2,1536,576]{2,1,0:T(8,128)(2,1)S(1)}, bf16[2,576,1536]{2,1,0:T(8,128)(2,1)S(1)}, f32[8,128]{1,0:T(8,128)S(1)}) custom-call(bf16[3,1536,384]{2,1,0:T(8,128)(2,1)S(1)} %copy-done.12), custom_call_target="tpu_custom_call" | custom-call | flops 1000 | bytes 1000 | tf_op jit(solution)/shard_map/pack_weights/pallas_call | solution.py:280
  102.0 6.5 %attention.1 = (bf16[512,768]{1,0:T(8,128)(2,1)S(1)}, bf16[512,768]{1,0:T(8,128)(2,1)S(1)}) custom-call(bf16[512,640]{1,0:T(8,128)(2,1)S(1)} %qkv_own.1.qa_ref, bf16[512,640]{1,0:T(8,128)(2,1)S(1)} %collective-permute-done.13.qb_ref, bf16[512,256]{1,0:T(8,128)(2,1)S(1)} %copy-done.25, bf16[512,256]{1,0:T(8,128)(2,1)S(1)} %copy-done.23, ...), custom_call_target="tpu_custom_call" | custom-call | flops 1000 | bytes 1000 | tf_op jit(solution)/shard_map/attention/pallas_call | solution.py:441
  111.1 3.0 %d_term.1 = bf16[512,1536]{1,0:T(8,128)(2,1)} custom-call(s32[1]{0:T(128)} %bitcast.5.head_ref, bf16[512,768]{1,0:T(8,128)(2,1)S(1)} %collective-permute-done.16.b_ref.x_ref, bf16[2,576,1536]{2,1,0:T(8,128)(2,1)S(1)} %copy-done.5, f32[512,1536]{1,0:T(8,128)S(1)} %d_term_own.1.rest_0_), custom_call_target="tpu_custom_call" | custom-call | flops 1000 | bytes 1000 | tf_op jit(solution)/shard_map/d_term/pallas_call | solution.py:501
  114.2 2.9 %head_term.1.rest_0_ = bf16[512,1536]{1,0:T(8,128)(2,1)} custom-call(s32[1]{0:T(128)} %bitcast.1.head_ref, bf16[512,768]{1,0:T(8,128)(2,1)S(1)} %get-tuple-element.78.a_ref.x_ref.ra_ref, bf16[512,768]{1,0:T(8,128)(2,1)S(1)} %collective-permute-done.16.b_ref.x_ref, bf16[2,192,1536]{2,1,0:T(8,128)(2,1)S(1)} %bitcast.49), custom_call_target="tpu_custom_call" | custom-call | flops 1000 | bytes 1000 | tf_op jit(solution)/shard_map/head_term/pallas_call | solution.py:468
  117.1 9.2 %weight_gradients.1 = (bf16[2,384,384]{2,1,0:T(8,128)(2,1)}, bf16[2,384,384]{2,1,0:T(8,128)(2,1)}, bf16[2,384,384]{2,1,0:T(8,128)(2,1)}, bf16[2,384,384]{2,1,0:T(8,128)(2,1)}) custom-call(s32[1]{0:T(128)} %bitcast.at_ref, bf16[512,1152]{1,0:T(8,128)(2,1)} %all-gather.4.cloned.1.call-done.xa_ref, bf16[512,384]{1,0:T(8,128)(2,1)} %copy-done.10, ...), custom_call_target="tpu_custom_call" | custom-call | flops 1000 | bytes 1000 | tf_op jit(solution)/shard_map/weight_gradients/pallas_call | solution.py:560
  128.3 13.7 %collective-permute-done.17.got_a = bf16[2,384,384]{2,1,0:T(8,128)(2,1)S(1)} collective-permute-done((bf16[2,384,384]{2,1,0:T(8,128)(2,1)}, bf16[2,384,384]{2,1,0:T(8,128)(2,1)S(1)}, u32[]{:S(2)}, u32[]{:S(2)}) %collective-permute-start.17) | collective-permute-done | bytes 589856 | tf_op jit(solution)/shard_map/ppermute | solution.py:701
  144.4 4.1 %reduce-scatter.5.cloned.1.call-done = bf16[1,4,32,1536]{3,2,1,0:T(8,128)(2,1)} async-done(((bf16[4,4,32,1536]{3,2,1,0:T(8,128)(2,1)}), bf16[1,4,32,1536]{3,2,1,0:T(8,128)(2,1)}) %reduce-scatter.5.cloned.1.call-update) | async-done | bytes 393232 | tf_op jit(solution)/shard_map/reduce_scatter | solution.py:776
  154.0 3.4 %collective-permute-done.19.near_ref = bf16[2,32,1536]{2,1,0:T(8,128)(2,1)S(1)} collective-permute-done((bf16[2,32,1536]{2,1,0:T(8,128)(2,1)S(1)}, bf16[2,32,1536]{2,1,0:T(8,128)(2,1)S(1)}, u32[]{:S(2)}, u32[]{:S(2)}) %collective-permute-start.19) | collective-permute-done | bytes 196640 | tf_op jit(solution)/shard_map/ppermute | solution.py:701
  159.1 3.4 %collective-permute-done.22.last_b = bf16[384,384]{1,0:T(8,128)(2,1)S(1)} collective-permute-done((bf16[384,384]{1,0:T(8,128)(2,1)S(1)}, bf16[384,384]{1,0:T(8,128)(2,1)S(1)}, u32[]{:S(2)}, u32[]{:S(2)}) %collective-permute-start.22) | collective-permute-done | bytes 294944 | tf_op jit(solution)/shard_map/ppermute | solution.py:701
  168.4 3.7 %collective-permute-start.24 = (bf16[2,4,1,1536]{3,2,1,0:T(2,128)(2,1)S(1)}, bf16[2,4,1,1536]{3,2,1,0:T(2,128)(2,1)S(1)}, u32[]{:S(2)}, u32[]{:S(2)}) collective-permute-start(bf16[2,4,1,1536]{3,2,1,0:T(2,128)(2,1)S(1)} %get-tuple-element.95.refs_1_), channel_id=1, source_target_pairs={{1,0},{2,1},{3,2},{4,3},{5,4},{6,5},{7,6},{8,7},{9,8},{10,9},{11,1... | collective-permute-start | bytes 73736 | tf_op jit(solution)/shard_map/ppermute | solution.py:692
  172.1 4.4 %copy-done = bf16[5,768,1536]{2,1,0:T(8,128)(2,1)S(1)} copy-done((bf16[5,768,1536]{2,1,0:T(8,128)(2,1)S(1)}, bf16[5,768,1536]{2,1,0:T(8,128)(2,1)}, u32[]{:S(2)}) %copy-start) | copy-done | bytes 11796504
  176.9 4.8 %collective-permute-start.28 = (bf16[384,768]{1,0:T(8,128)(2,1)S(1)}, bf16[384,768]{1,0:T(8,128)(2,1)S(1)}, u32[]{:S(2)}, u32[]{:S(2)}) collective-permute-start(bf16[384,768]{1,0:T(8,128)(2,1)S(1)} %constant_dynamic-update-slice_fusion.2.refs_1_), channel_id=1, source_target_pairs={{0,4},{4,0},{8,12},{12,8},{16,20},{20,16},{24,28},{28,24},{1,5},{5... | collective-permute-start | bytes 1769480 | tf_op jit(solution)/shard_map/ppermute | solution.py:711
  184.3 4.2 %encoder_backward.1.refs_4_ = bf16[256,768]{1,0:T(8,128)(2,1)S(1)} custom-call(bf16[2,4,32,1536]{3,2,1,0:T(8,128)(2,1)S(1)} %get-tuple-element.93.d_ref, bf16[2,4,1,1536]{3,2,1,0:T(2,128)(2,1)S(1)} %collective-permute-done.23.low_ref, bf16[2,4,1,1536]{3,2,1,0:T(2,128)(2,1)S(1)} %collective-permute-done.24.high_ref, bf16[5,768,1536]{2,1,0:T(8,128)(2,1)S(1)} %copy-done, ...), custom_call_target="tpu_custom_call" | custom-call | flops 1000 | bytes 1000 | tf_op jit(solution)/shard_map/encoder_backward/pallas_call | solution.py:244
  188.5 3.4 %weight_outputs_near.1 = (f32[3,1536,384]{2,1,0:T(8,128)}, f32[2,2,96,1536]{3,2,1,0:T(8,128)}, f32[8,128]{1,0:T(8,128)S(1)}) custom-call(s32[2]{0:T(128)S(1)} %copy-done.33, bf16[384,768]{1,0:T(8,128)(2,1)S(1)} %constant_dynamic-update-slice_fusion.refs_0_, bf16[384,768]{1,0:T(8,128)(2,1)S(1)} %constant_dynamic-update-slice_fusion.2.refs_1_, ...), custom_call_target="tpu_custom_call" | custom-call | flops 1000 | bytes 1000 | tf_op jit(solution)/shard_map/weight_outputs_near/pallas_call | solution.py:661
  194.3 2.3 %collective-permute-start.29 = (bf16[32,1536]{1,0:T(8,128)(2,1)S(1)}, bf16[32,1536]{1,0:T(8,128)(2,1)S(1)}, u32[]{:S(2)}, u32[]{:S(2)}) collective-permute-start(bf16[32,1536]{1,0:T(8,128)(2,1)S(1)} %get-tuple-element.128), channel_id=1, source_target_pairs={{0,8},{4,12},{8,0},{12,4},{16,24},{20,28},{24,16},{28,20},{1,9},{5... | collective-permute-start | bytes 294920 | tf_op jit(solution)/shard_map/ppermute | solution.py:701
  199.6 2.2 %collective-permute-done.30.refs_2_ = bf16[32,1536]{1,0:T(8,128)(2,1)S(1)} collective-permute-done((bf16[32,1536]{1,0:T(8,128)(2,1)S(1)}, bf16[32,1536]{1,0:T(8,128)(2,1)S(1)}, u32[]{:S(2)}, u32[]{:S(2)}) %collective-permute-start.30) | collective-permute-done | bytes 98336 | tf_op jit(solution)/shard_map/ppermute | solution.py:701
  205.2 4.3 %weight_outputs_far.1 = (f32[3,1536,384]{2,1,0:T(8,128)}, f32[2,2,96,1536]{3,2,1,0:T(8,128)}, f32[8,128]{1,0:T(8,128)}) custom-call(s32[2]{0:T(128)S(1)} %copy-done.33, bf16[384,768]{1,0:T(8,128)(2,1)} %collective-permute-done.32.refs_0_, bf16[384,768]{1,0:T(8,128)(2,1)S(1)} %collective-permute-done.33.refs_1_, ...), custom_call_target="tpu_custom_call", output_to_operand_aliasing={{0}: (5, {}), {1}: (6, {})} | custom-call | flops 1000 | bytes 1000 | tf_op jit(solution)/shard_map/weight_outputs_far/pallas_call | solution.py:661
  (186 shorter events, 79.2 us)
Async XLA Ops:
  7.2 38.4 %all-gather.6.cloned.1.call-start = ((), (), s32[]{:S(2)}) async-start(), calls=%async_computation.5 | async-start | bytes 1966080 | tf_op jit(solution)/shard_map/all_gather | solution.py:734
  7.9 86.2 %all-gather.4.cloned.1.call-start = ((), (), s32[]{:S(2)}) async-start(), calls=%async_computation.2 | async-start | bytes 1474560 | tf_op jit(solution)/shard_map/all_gather | solution.py:743
  9.1 9.3 %collective-permute-start.1 = (bf16[2,4,1,768]{3,2,1,0:T(2,128)(2,1)S(1)}, bf16[2,4,1,768]{3,2,1,0:T(2,128)(2,1)S(1)}, u32[]{:S(2)}, u32[]{:S(2)}) collective-permute-start(bf16[2,4,1,768]{3,2,1,0:T(2,128)(2,1)S(1)} %get-tuple-element.130), channel_id=1, source_target_pairs={{1,0},{2,1},{3,2},{4,3},{5,4},{6,5},{7,6},{8,7},{9,8},{10,9},{11,1... | collective-permute-start | bytes 36872 | tf_op jit(solution)/shard_map/ppermute | solution.py:692
  47.4 13.0 %collective-permute-start.10 = (bf16[4,32,1536]{2,1,0:T(8,128)(2,1)S(1)}, bf16[4,32,1536]{2,1,0:T(8,128)(2,1)S(1)}, u32[]{:S(2)}, u32[]{:S(2)}) collective-permute-start(bf16[4,32,1536]{2,1,0:T(8,128)(2,1)S(1)} %get-tuple-element.123), channel_id=1, source_target_pairs={{0,24},{4,28},{8,16},{12,20},{16,8},{20,12},{24,0},{28,4},{1,25},{... | collective-permute-start | bytes 1179656 | tf_op jit(solution)/shard_map/ppermute | solution.py:701
  48.9 19.0 %collective-permute-start.9 = (bf16[4,32,1536]{2,1,0:T(8,128)(2,1)S(1)}, bf16[4,32,1536]{2,1,0:T(8,128)(2,1)S(1)}, u32[]{:S(2)}, u32[]{:S(2)}) collective-permute-start(bf16[4,32,1536]{2,1,0:T(8,128)(2,1)S(1)} %get-tuple-element.124), channel_id=1, source_target_pairs={{0,8},{4,12},{8,0},{12,4},{16,24},{20,28},{24,16},{28,20},{1,9},{5... | collective-permute-start | bytes 1179656 | tf_op jit(solution)/shard_map/ppermute | solution.py:701
  50.4 17.5 %collective-permute-start.8 = (bf16[4,32,1536]{2,1,0:T(8,128)(2,1)S(1)}, bf16[4,32,1536]{2,1,0:T(8,128)(2,1)S(1)}, u32[]{:S(2)}, u32[]{:S(2)}) collective-permute-start(bf16[4,32,1536]{2,1,0:T(8,128)(2,1)S(1)} %get-tuple-element.125), channel_id=1, source_target_pairs={{0,16},{4,20},{8,24},{12,28},{16,0},{20,4},{24,8},{28,12},{1,17},{... | collective-permute-start | bytes 1179656 | tf_op jit(solution)/shard_map/ppermute | solution.py:701
  51.0 97.6 %reduce-scatter.5.cloned.1.call-start = ((), (), s32[]{:S(2)}) async-start(), calls=%async_computation.4 | async-start | bytes 1966080 | tf_op jit(solution)/shard_map/reduce_scatter | solution.py:776
  68.3 25.9 %collective-permute-start.12 = (bf16[512,1536]{1,0:T(8,128)(2,1)S(1)}, bf16[512,1536]{1,0:T(8,128)(2,1)}, u32[]{:S(2)}, u32[]{:S(2)}) collective-permute-start(bf16[512,1536]{1,0:T(8,128)(2,1)S(1)} %bitcast.43), channel_id=1, source_target_pairs={{0,4},{4,0},{8,12},{12,8},{16,20},{20,16},{24,28},{28,24},{1,5},{5... | collective-permute-start | bytes 4718600 | tf_op jit(solution)/shard_map/ppermute | solution.py:711
  71.2 23.0 %collective-permute-start.11 = (bf16[512,256]{1,0:T(8,128)(2,1)}, bf16[512,256]{1,0:T(8,128)(2,1)S(1)}, u32[]{:S(2)}, u32[]{:S(2)}) collective-permute-start(bf16[512,256]{1,0:T(8,128)(2,1)} %get-tuple-element.62), channel_id=1, source_target_pairs={{0,4},{4,0},{8,12},{12,8},{16,20},{20,16},{24,28},{28,24},{1,5},{5... | collective-permute-start | bytes 786440 | tf_op jit(solution)/shard_map/ppermute | solution.py:711
  72.0 14.1 %collective-permute-start.7 = (bf16[128,384]{1,0:T(8,128)(2,1)S(1)}, bf16[128,384]{1,0:T(8,128)(2,1)S(1)}, u32[]{:S(2)}, u32[]{:S(2)}) collective-permute-start(bf16[128,384]{1,0:T(8,128)(2,1)S(1)} %pad_maximum_fusion.3.refs_0_), channel_id=1, source_target_pairs={{0,3},{1,2},{2,1},{3,0},{4,7},{5,6},{6,5},{7,4},{8,11},{9,10},{10,... | collective-permute-start | bytes 294920 | tf_op jit(solution)/shard_map/ppermute | solution.py:706
  74.7 13.9 %collective-permute-start.6 = (bf16[128,384]{1,0:T(8,128)(2,1)S(1)}, bf16[128,384]{1,0:T(8,128)(2,1)S(1)}, u32[]{:S(2)}, u32[]{:S(2)}) collective-permute-start(bf16[128,384]{1,0:T(8,128)(2,1)S(1)} %pad_maximum_fusion.3.refs_0_), channel_id=1, source_target_pairs={{0,2},{1,3},{2,0},{3,1},{4,6},{5,7},{6,4},{7,5},{8,10},{9,11},{10,... | collective-permute-start | bytes 294920 | tf_op jit(solution)/shard_map/ppermute | solution.py:706
  74.9 14.5 %collective-permute-start.5 = (bf16[128,384]{1,0:T(8,128)(2,1)S(1)}, bf16[128,384]{1,0:T(8,128)(2,1)S(1)}, u32[]{:S(2)}, u32[]{:S(2)}) collective-permute-start(bf16[128,384]{1,0:T(8,128)(2,1)S(1)} %pad_maximum_fusion.3.refs_0_), channel_id=1, source_target_pairs={{0,1},{1,0},{2,3},{3,2},{4,5},{5,4},{6,7},{7,6},{8,9},{9,8},{10,11... | collective-permute-start | bytes 294920 | tf_op jit(solution)/shard_map/ppermute | solution.py:706
  94.1 7.9 %collective-permute-start.14 = (bf16[512,1152]{1,0:T(8,128)(2,1)}, bf16[512,1152]{1,0:T(8,128)(2,1)S(1)}, u32[]{:S(2)}, u32[]{:S(2)}) collective-permute-start(bf16[512,1152]{1,0:T(8,128)(2,1)} %all-gather.4.cloned.1.call-done.xa_ref), channel_id=1, source_target_pairs={{0,4},{4,0},{8,12},{12,8},{16,20},{20,16},{24,28},{28,24},{1,5},{5... | collective-permute-start | bytes 3538952 | tf_op jit(solution)/shard_map/ppermute | solution.py:711
  114.1 77.8 %reduce-scatter.3.cloned.1.call-start = ((), (), s32[]{:S(2)}) async-start(), calls=%async_computation.3 | async-start | bytes 1966080 | tf_op jit(solution)/shard_map/reduce_scatter | solution.py:793
  126.4 15.6 %collective-permute-start.17 = (bf16[2,384,384]{2,1,0:T(8,128)(2,1)}, bf16[2,384,384]{2,1,0:T(8,128)(2,1)S(1)}, u32[]{:S(2)}, u32[]{:S(2)}) collective-permute-start(bf16[2,384,384]{2,1,0:T(8,128)(2,1)} %get-tuple-element.83), channel_id=1, source_target_pairs={{0,8},{4,12},{8,0},{12,4},{16,24},{20,28},{24,16},{28,20},{1,9},{5... | collective-permute-start | bytes 1769480 | tf_op jit(solution)/shard_map/ppermute | solution.py:701
  126.8 15.3 %collective-permute-start.18 = (bf16[2,384,384]{2,1,0:T(8,128)(2,1)}, bf16[2,384,384]{2,1,0:T(8,128)(2,1)S(1)}, u32[]{:S(2)}, u32[]{:S(2)}) collective-permute-start(bf16[2,384,384]{2,1,0:T(8,128)(2,1)} %get-tuple-element.85), channel_id=1, source_target_pairs={{0,16},{4,20},{8,24},{12,28},{16,0},{20,4},{24,8},{28,12},{1,17},{... | collective-permute-start | bytes 1769480 | tf_op jit(solution)/shard_map/ppermute | solution.py:701
  150.1 9.0 %collective-permute-start.21 = (bf16[384,384]{1,0:T(8,128)(2,1)S(1)}, bf16[384,384]{1,0:T(8,128)(2,1)S(1)}, u32[]{:S(2)}, u32[]{:S(2)}) collective-permute-start(bf16[384,384]{1,0:T(8,128)(2,1)S(1)} %get-tuple-element.86), channel_id=1, source_target_pairs={{0,16},{4,20},{8,24},{12,28},{16,0},{20,4},{24,8},{28,12},{1,17},{... | collective-permute-start | bytes 884744 | tf_op jit(solution)/shard_map/ppermute | solution.py:701
  151.6 10.9 %collective-permute-start.22 = (bf16[384,384]{1,0:T(8,128)(2,1)S(1)}, bf16[384,384]{1,0:T(8,128)(2,1)S(1)}, u32[]{:S(2)}, u32[]{:S(2)}) collective-permute-start(bf16[384,384]{1,0:T(8,128)(2,1)S(1)} %get-tuple-element.87), channel_id=1, source_target_pairs={{0,8},{4,12},{8,0},{12,4},{16,24},{20,28},{24,16},{28,20},{1,9},{5... | collective-permute-start | bytes 884744 | tf_op jit(solution)/shard_map/ppermute | solution.py:701
  162.8 14.1 %collective-permute-start.25 = (bf16[192,768]{1,0:T(8,128)(2,1)S(1)}, bf16[192,768]{1,0:T(8,128)(2,1)S(1)}, u32[]{:S(2)}, u32[]{:S(2)}) collective-permute-start(bf16[192,768]{1,0:T(8,128)(2,1)S(1)} %get-tuple-element.92.refs_4_), channel_id=1, source_target_pairs={{0,8},{4,12},{8,0},{12,4},{16,24},{20,28},{24,16},{28,20},{1,9},{5... | collective-permute-start | bytes 884744 | tf_op jit(solution)/shard_map/ppermute | solution.py:701
  163.4 13.5 %collective-permute-start.27 = (bf16[192,768]{1,0:T(8,128)(2,1)S(1)}, bf16[192,768]{1,0:T(8,128)(2,1)S(1)}, u32[]{:S(2)}, u32[]{:S(2)}) collective-permute-start(bf16[192,768]{1,0:T(8,128)(2,1)S(1)} %get-tuple-element.100), channel_id=1, source_target_pairs={{0,16},{4,20},{8,24},{12,28},{16,0},{20,4},{24,8},{28,12},{1,17},{... | collective-permute-start | bytes 884744 | tf_op jit(solution)/shard_map/ppermute | solution.py:701
  166.2 10.3 %collective-permute-start.23 = (bf16[2,4,1,1536]{3,2,1,0:T(2,128)(2,1)S(1)}, bf16[2,4,1,1536]{3,2,1,0:T(2,128)(2,1)S(1)}, u32[]{:S(2)}, u32[]{:S(2)}) collective-permute-start(bf16[2,4,1,1536]{3,2,1,0:T(2,128)(2,1)S(1)} %get-tuple-element.94), channel_id=1, source_target_pairs={{0,1},{1,2},{2,3},{3,4},{4,5},{5,6},{6,7},{7,8},{8,9},{9,10},{10,1... | collective-permute-start | bytes 73736 | tf_op jit(solution)/shard_map/ppermute | solution.py:692
  168.4 8.5 %collective-permute-start.24 = (bf16[2,4,1,1536]{3,2,1,0:T(2,128)(2,1)S(1)}, bf16[2,4,1,1536]{3,2,1,0:T(2,128)(2,1)S(1)}, u32[]{:S(2)}, u32[]{:S(2)}) collective-permute-start(bf16[2,4,1,1536]{3,2,1,0:T(2,128)(2,1)S(1)} %get-tuple-element.95.refs_1_), channel_id=1, source_target_pairs={{1,0},{2,1},{3,2},{4,3},{5,4},{6,5},{7,6},{8,7},{9,8},{10,9},{11,1... | collective-permute-start | bytes 73736 | tf_op jit(solution)/shard_map/ppermute | solution.py:692
  181.9 16.2 %collective-permute-start.33 = (bf16[384,768]{1,0:T(8,128)(2,1)S(1)}, bf16[384,768]{1,0:T(8,128)(2,1)S(1)}, u32[]{:S(2)}, u32[]{:S(2)}) collective-permute-start(bf16[384,768]{1,0:T(8,128)(2,1)S(1)} %constant_dynamic-update-slice_fusion.2.refs_1_), channel_id=1, source_target_pairs={{0,8},{4,12},{8,0},{12,4},{16,24},{20,28},{24,16},{28,20},{1,9},{5... | collective-permute-start | bytes 1769480 | tf_op jit(solution)/shard_map/ppermute | solution.py:701
  182.0 19.9 %collective-permute-start.32 = (bf16[384,768]{1,0:T(8,128)(2,1)S(1)}, bf16[384,768]{1,0:T(8,128)(2,1)}, u32[]{:S(2)}, u32[]{:S(2)}) collective-permute-start(bf16[384,768]{1,0:T(8,128)(2,1)S(1)} %constant_dynamic-update-slice_fusion.refs_0_), channel_id=1, source_target_pairs={{0,16},{4,20},{8,24},{12,28},{16,0},{20,4},{24,8},{28,12},{1,17},{... | collective-permute-start | bytes 1769480 | tf_op jit(solution)/shard_map/ppermute | solution.py:701
  (54 other events, 275.1 us)
Sparse Core Ops, SparseCore 0:
  9.6 35.9 all-gather.5
  51.1 36.0 all-gather.3
  114.2 34.2 reduce-scatter.4
  150.7 36.3 reduce-scatter.2

commit v17 on v16

--- a/solution.py
+++ b/solution.py
@@ -748,8 +748,9 @@
     grad_slots = to_chips(
         [lax.dynamic_index_in_dim(grad_z, own_seq ^ j, 2, keepdims=False) for j in range(seqs)]
     )
+    w_pack, w_turned, packed = pack_weights(after(w_qkv, slab_a))
+    *grad_slots, packed, normed_b = lax.optimization_barrier((*grad_slots, packed, normed_b))
     grad_rows = jnp.stack([grad_slots[j] for j in order], axis=1).reshape(half, width)
-    w_pack, w_turned, packed = pack_weights(after(w_qkv, slab_a))
     w_rows = w_out.reshape(heads, DH, width)
     d_other, one = head_product(head_other, grad_rows, w_rows, NT, "d_o_other")
     d_got = swap_heads(d_other)

time: 219 us -> 222 us (1.014)
  local copies, waits for them, and re-layouts: 34.9 us -> 30.4 us
  starting transfers between devices: 44.7 us -> 47 us
    ppermute x19, waiting for transfers between devices: 47.6 us -> 30.9 us  [trade_chip(): return lax.ppermute(x, 'seq', [(s, s ^ bit * heads) for s in range(count)])]
    all_gather x1, waiting for transfers between devices: 0.01 us -> 16.1 us  [unit_body(): normed_a = lax.all_gather(slab_a, 'head', axis=0, tiled=True)]
    unnamed x79, local copies, waits for them, and re-layouts: 24.8 us -> 17.1 us
  transfers between devices with their start and end apart: 40 -> 40, of which waited for: 21 -> 20; matrix products, arithmetic and copies ran while one was open for 5% -> 7% of each run, Pallas kernels for 20% -> 20%
where the time goes in v17:
time: 222 us; the launch traced here: 218 us
  waiting for transfers between devices  64.8 us (29%)
  Pallas kernels  58.2 us (26%)
  starting transfers between devices  47 us (21%)
  local copies, waits for them, and re-layouts  30.4 us (14%)
  between operations  14.4 us (6%)
  other arithmetic  3.6 us (2%)
    ppermute x19, waiting for transfers between devices, trade_chip(): return lax.ppermute(x, 'seq', [(s, s ^ bit * heads) for s in range(count)])  30.9 us
    ppermute x19, starting transfers between devices, trade_chip(): return lax.ppermute(x, 'seq', [(s, s ^ bit * heads) for s in range(count)])  20.1 us
    unnamed x79, local copies, waits for them, and re-layouts  17.1 us
    all_gather x1, waiting for transfers between devices, unit_body(): normed_a = lax.all_gather(slab_a, 'head', axis=0, tiled=True)  16.1 us
    pallas_call x1, Pallas kernels, encoder(): pl.pallas_call(conv_kernel, grid=(width // tile,), in_specs=[SCALARS, who...  10.1 us
    pallas_call x1, Pallas kernels, weight_gradients(): pl.pallas_call(weight_kernel, grid_spec=pltpu.PrefetchScalarGridSpec(num_...  9.24 us
    pallas_call x2, Pallas kernels, unpack_weights(): pl.pallas_call(unpack_kernel, grid_spec=pltpu.PrefetchScalarGridSpec(num_...  7.74 us
    ppermute x2, starting transfers between devices, neighbour_edges(): lax.ppermute(last, axes, forward)  7.14 us
  transfers between devices with their start and end apart: 40, of which 20 were waited for; matrix products, arithmetic and copies ran while one was open for 7% of the time, Pallas kernels for 20%

profile of v17, /device:TPU:26, one launch (start us, length us, event | category | flops | bytes accessed | tf_op | source)
XLA Modules:
  0.0 218.5 jit_solution(16219180062213708659)
XLA Ops:
  9.1 2.4 %collective-permute-start.1 = (bf16[2,4,1,768]{3,2,1,0:T(2,128)(2,1)S(1)}, bf16[2,4,1,768]{3,2,1,0:T(2,128)(2,1)S(1)}, u32[]{:S(2)}, u32[]{:S(2)}) collective-permute-start(bf16[2,4,1,768]{3,2,1,0:T(2,128)(2,1)S(1)} %get-tuple-element.142), channel_id=1, source_target_pairs={{1,0},{2,1},{3,2},{4,3},{5,4},{6,5},{7,6},{8,7},{9,8},{10,9},{11,1... | collective-permute-start | bytes 36872 | tf_op jit(solution)/shard_map/ppermute | solution.py:692
  11.4 5.0 %collective-permute-start = (bf16[2,4,1,768]{3,2,1,0:T(2,128)(2,1)S(1)}, bf16[2,4,1,768]{3,2,1,0:T(2,128)(2,1)S(1)}, u32[]{:S(2)}, u32[]{:S(2)}) collective-permute-start(bf16[2,4,1,768]{3,2,1,0:T(2,128)(2,1)S(1)} %get-tuple-element.143), channel_id=1, source_target_pairs={{0,1},{1,2},{2,3},{3,4},{4,5},{5,6},{6,7},{7,8},{8,9},{9,10},{10,1... | collective-permute-start | bytes 36872 | tf_op jit(solution)/shard_map/ppermute | solution.py:692
  19.6 10.1 %encoder_forward.1 = (bf16[4,32,1536]{2,1,0:T(8,128)(2,1)}, f32[2,4,32,1536]{3,2,1,0:T(8,128)}, bf16[32,1536]{1,0:T(8,128)(2,1)}, bf16[32,1536]{1,0:T(8,128)(2,1...) custom-call(s32[2]{0:T(128)} %pad_add_fusion.at_ref, bf16[2,4,32,768]{3,2,1,0:T(8,128)(2,1)} %bitcast.60, ...), custom_call_target="tpu_custom_call" | custom-call | flops 1000 | bytes 1000 | tf_op jit(solution)/shard_map/encoder_forward/pallas_call | solution.py:111
  39.6 5.9 %all-gather.6.cloned.1.call-done = bf16[128,4,1536]{2,1,0:T(4,128)(2,1)} async-done(((bf16[32,4,1536]{2,1,0:T(4,128)(2,1)}), bf16[128,4,1536]{2,1,0:T(4,128)(2,1)}) %all-gather.6.cloned.1.call-update) | async-done | bytes 1572880 | tf_op jit(solution)/shard_map/all_gather | solution.py:734
  55.6 2.8 %collective-permute-start.10 = (bf16[128,384]{1,0:T(8,128)(2,1)}, bf16[128,384]{1,0:T(8,128)(2,1)S(1)}, u32[]{:S(2)}, u32[]{:S(2)}) collective-permute-start(bf16[128,384]{1,0:T(8,128)(2,1)} %pad_maximum_fusion.3.refs_0_), channel_id=1, source_target_pairs={{0,3},{1,2},{2,1},{3,0},{4,7},{5,6},{6,5},{7,4},{8,11},{9,10},{10,... | collective-permute-start | bytes 294920 | tf_op jit(solution)/shard_map/ppermute | solution.py:706
  58.5 4.1 %collective-permute-done.10.refs_3_ = bf16[128,384]{1,0:T(8,128)(2,1)S(1)} collective-permute-done((bf16[128,384]{1,0:T(8,128)(2,1)}, bf16[128,384]{1,0:T(8,128)(2,1)S(1)}, u32[]{:S(2)}, u32[]{:S(2)}) %collective-permute-start.10) | collective-permute-done | bytes 98336 | tf_op jit(solution)/shard_map/ppermute | solution.py:706
  63.2 3.6 %collective-permute-start.8 = (bf16[128,384]{1,0:T(8,128)(2,1)}, bf16[128,384]{1,0:T(8,128)(2,1)}, u32[]{:S(2)}, u32[]{:S(2)}) collective-permute-start(bf16[128,384]{1,0:T(8,128)(2,1)} %pad_maximum_fusion.3.refs_0_), channel_id=1, source_target_pairs={{0,1},{1,0},{2,3},{3,2},{4,5},{5,4},{6,7},{7,6},{8,9},{9,8},{10,11... | collective-permute-start | bytes 294920 | tf_op jit(solution)/shard_map/ppermute | solution.py:706
  67.1 3.9 %pack_weights.1 = (bf16[2,1536,576]{2,1,0:T(8,128)(2,1)S(1)}, bf16[2,576,1536]{2,1,0:T(8,128)(2,1)S(1)}, f32[8,128]{1,0:T(8,128)S(1)}) custom-call(bf16[3,1536,384]{2,1,0:T(8,128)(2,1)S(1)} %copy-done.12), custom_call_target="tpu_custom_call" | custom-call | flops 1000 | bytes 1000 | tf_op jit(solution)/shard_map/pack_weights/pallas_call | solution.py:280
  80.5 16.1 %all-gather.4.cloned.1.call-done.xa_ref = bf16[512,1152]{1,0:T(8,128)(2,1)} async-done(((bf16[128,1152]{1,0:T(8,128)(2,1)}), bf16[512,1152]{1,0:T(8,128)(2,1)}) %all-gather.4.cloned.1.call-update) | async-done | bytes 1179664 | tf_op jit(solution)/shard_map/all_gather | solution.py:743
  104.5 6.5 %attention.1 = (bf16[512,768]{1,0:T(8,128)(2,1)S(1)}, bf16[512,768]{1,0:T(8,128)(2,1)S(1)}) custom-call(bf16[512,640]{1,0:T(8,128)(2,1)S(1)} %qkv_own.1.qa_ref, bf16[512,640]{1,0:T(8,128)(2,1)S(1)} %collective-permute-done.13.qb_ref, bf16[512,256]{1,0:T(8,128)(2,1)S(1)} %copy-done.25, bf16[512,256]{1,0:T(8,128)(2,1)S(1)} %copy-done.23, ...), custom_call_target="tpu_custom_call" | custom-call | flops 1000 | bytes 1000 | tf_op jit(solution)/shard_map/attention/pallas_call | solution.py:441
  113.6 3.0 %d_term.1 = bf16[512,1536]{1,0:T(8,128)(2,1)} custom-call(s32[1]{0:T(128)} %bitcast.10.head_ref, bf16[512,768]{1,0:T(8,128)(2,1)S(1)} %collective-permute-done.16.b_ref.x_ref, bf16[2,576,1536]{2,1,0:T(8,128)(2,1)S(1)} %copy-done.5, f32[512,1536]{1,0:T(8,128)S(1)} %d_term_own.1.rest_0_), custom_call_target="tpu_custom_call" | custom-call | flops 1000 | bytes 1000 | tf_op jit(solution)/shard_map/d_term/pallas_call | solution.py:501
  116.9 2.7 %head_term.1.rest_0_ = bf16[512,1536]{1,0:T(8,128)(2,1)} custom-call(s32[1]{0:T(128)} %bitcast.1.head_ref, bf16[512,768]{1,0:T(8,128)(2,1)S(1)} %get-tuple-element.90.a_ref.x_ref.ra_ref, bf16[512,768]{1,0:T(8,128)(2,1)S(1)} %collective-permute-done.16.b_ref.x_ref, bf16[2,192,1536]{2,1,0:T(8,128)(2,1)S(1)} %bitcast.50), custom_call_target="tpu_custom_call" | custom-call | flops 1000 | bytes 1000 | tf_op jit(solution)/shard_map/head_term/pallas_call | solution.py:468
  119.6 9.2 %weight_gradients.1 = (bf16[2,384,384]{2,1,0:T(8,128)(2,1)}, bf16[2,384,384]{2,1,0:T(8,128)(2,1)}, bf16[2,384,384]{2,1,0:T(8,128)(2,1)}, bf16[2,384,384]{2,1,0:T(8,128)(2,1)}) custom-call(s32[1]{0:T(128)} %bitcast.at_ref, bf16[512,1152]{1,0:T(8,128)(2,1)} %all-gather.4.cloned.1.call-done.xa_ref, bf16[512,384]{1,0:T(8,128)(2,1)} %copy-done.10, ...), custom_call_target="tpu_custom_call" | custom-call | flops 1000 | bytes 1000 | tf_op jit(solution)/shard_map/weight_gradients/pallas_call | solution.py:560
  130.8 13.7 %collective-permute-done.17.got_a = bf16[2,384,384]{2,1,0:T(8,128)(2,1)S(1)} collective-permute-done((bf16[2,384,384]{2,1,0:T(8,128)(2,1)}, bf16[2,384,384]{2,1,0:T(8,128)(2,1)S(1)}, u32[]{:S(2)}, u32[]{:S(2)}) %collective-permute-start.17) | collective-permute-done | bytes 589856 | tf_op jit(solution)/shard_map/ppermute | solution.py:701
  147.1 3.9 %reduce-scatter.5.cloned.1.call-done = bf16[1,4,32,1536]{3,2,1,0:T(8,128)(2,1)} async-done(((bf16[4,4,32,1536]{3,2,1,0:T(8,128)(2,1)}), bf16[1,4,32,1536]{3,2,1,0:T(8,128)(2,1)}) %reduce-scatter.5.cloned.1.call-update) | async-done | bytes 393232 | tf_op jit(solution)/shard_map/reduce_scatter | solution.py:777
  156.4 3.4 %collective-permute-done.19.near_ref = bf16[2,32,1536]{2,1,0:T(8,128)(2,1)S(1)} collective-permute-done((bf16[2,32,1536]{2,1,0:T(8,128)(2,1)S(1)}, bf16[2,32,1536]{2,1,0:T(8,128)(2,1)S(1)}, u32[]{:S(2)}, u32[]{:S(2)}) %collective-permute-start.19) | collective-permute-done | bytes 196640 | tf_op jit(solution)/shard_map/ppermute | solution.py:701
  161.6 3.4 %collective-permute-done.22.last_b = bf16[384,384]{1,0:T(8,128)(2,1)S(1)} collective-permute-done((bf16[384,384]{1,0:T(8,128)(2,1)S(1)}, bf16[384,384]{1,0:T(8,128)(2,1)S(1)}, u32[]{:S(2)}, u32[]{:S(2)}) %collective-permute-start.22) | collective-permute-done | bytes 294944 | tf_op jit(solution)/shard_map/ppermute | solution.py:701
  170.9 3.7 %collective-permute-start.24 = (bf16[2,4,1,1536]{3,2,1,0:T(2,128)(2,1)S(1)}, bf16[2,4,1,1536]{3,2,1,0:T(2,128)(2,1)S(1)}, u32[]{:S(2)}, u32[]{:S(2)}) collective-permute-start(bf16[2,4,1,1536]{3,2,1,0:T(2,128)(2,1)S(1)} %get-tuple-element.107.refs_1_), channel_id=1, source_target_pairs={{1,0},{2,1},{3,2},{4,3},{5,4},{6,5},{7,6},{8,7},{9,8},{10,9},{11,1... | collective-permute-start | bytes 73736 | tf_op jit(solution)/shard_map/ppermute | solution.py:692
  174.6 4.4 %copy-done = bf16[5,768,1536]{2,1,0:T(8,128)(2,1)S(1)} copy-done((bf16[5,768,1536]{2,1,0:T(8,128)(2,1)S(1)}, bf16[5,768,1536]{2,1,0:T(8,128)(2,1)}, u32[]{:S(2)}) %copy-start) | copy-done | bytes 11796504
  179.4 4.8 %collective-permute-start.28 = (bf16[384,768]{1,0:T(8,128)(2,1)S(1)}, bf16[384,768]{1,0:T(8,128)(2,1)S(1)}, u32[]{:S(2)}, u32[]{:S(2)}) collective-permute-start(bf16[384,768]{1,0:T(8,128)(2,1)S(1)} %constant_dynamic-update-slice_fusion.2.refs_1_), channel_id=1, source_target_pairs={{0,4},{4,0},{8,12},{12,8},{16,20},{20,16},{24,28},{28,24},{1,5},{5... | collective-permute-start | bytes 1769480 | tf_op jit(solution)/shard_map/ppermute | solution.py:711
  186.7 4.2 %encoder_backward.1.refs_4_ = bf16[256,768]{1,0:T(8,128)(2,1)S(1)} custom-call(bf16[2,4,32,1536]{3,2,1,0:T(8,128)(2,1)S(1)} %get-tuple-element.105.d_ref, bf16[2,4,1,1536]{3,2,1,0:T(2,128)(2,1)S(1)} %collective-permute-done.23.low_ref, bf16[2,4,1,1536]{3,2,1,0:T(2,128)(2,1)S(1)} %collective-permute-done.24.high_ref, bf16[5,768,1536]{2,1,0:T(8,128)(2,1)S(1)} %copy-done, ...), custom_call_target="tpu_custom_call" | custom-call | flops 1000 | bytes 1000 | tf_op jit(solution)/shard_map/encoder_backward/pallas_call | solution.py:244
  191.0 3.4 %weight_outputs_near.1 = (f32[3,1536,384]{2,1,0:T(8,128)}, f32[2,2,96,1536]{3,2,1,0:T(8,128)}, f32[8,128]{1,0:T(8,128)S(1)}) custom-call(s32[2]{0:T(128)S(1)} %copy-done.29, bf16[384,768]{1,0:T(8,128)(2,1)S(1)} %constant_dynamic-update-slice_fusion.refs_0_, bf16[384,768]{1,0:T(8,128)(2,1)S(1)} %constant_dynamic-update-slice_fusion.2.refs_1_, ...), custom_call_target="tpu_custom_call" | custom-call | flops 1000 | bytes 1000 | tf_op jit(solution)/shard_map/weight_outputs_near/pallas_call | solution.py:661
  196.7 2.3 %collective-permute-start.29 = (bf16[32,1536]{1,0:T(8,128)(2,1)S(1)}, bf16[32,1536]{1,0:T(8,128)(2,1)S(1)}, u32[]{:S(2)}, u32[]{:S(2)}) collective-permute-start(bf16[32,1536]{1,0:T(8,128)(2,1)S(1)} %get-tuple-element.140), channel_id=1, source_target_pairs={{0,8},{4,12},{8,0},{12,4},{16,24},{20,28},{24,16},{28,20},{1,9},{5... | collective-permute-start | bytes 294920 | tf_op jit(solution)/shard_map/ppermute | solution.py:701
  207.6 4.3 %weight_outputs_far.1 = (f32[3,1536,384]{2,1,0:T(8,128)}, f32[2,2,96,1536]{3,2,1,0:T(8,128)}, f32[8,128]{1,0:T(8,128)}) custom-call(s32[2]{0:T(128)S(1)} %copy-done.29, bf16[384,768]{1,0:T(8,128)(2,1)} %collective-permute-done.32.refs_0_, bf16[384,768]{1,0:T(8,128)(2,1)S(1)} %collective-permute-done.33.refs_1_, ...), custom_call_target="tpu_custom_call", output_to_operand_aliasing={{0}: (5, {}), {1}: (6, {})} | custom-call | flops 1000 | bytes 1000 | tf_op jit(solution)/shard_map/weight_outputs_far/pallas_call | solution.py:661
  (186 shorter events, 77.1 us)
Async XLA Ops:
  7.2 38.4 %all-gather.6.cloned.1.call-start = ((), (), s32[]{:S(2)}) async-start(), calls=%async_computation.5 | async-start | bytes 1966080 | tf_op jit(solution)/shard_map/all_gather | solution.py:734
  7.9 88.7 %all-gather.4.cloned.1.call-start = ((), (), s32[]{:S(2)}) async-start(), calls=%async_computation.2 | async-start | bytes 1474560 | tf_op jit(solution)/shard_map/all_gather | solution.py:743
  9.1 9.3 %collective-permute-start.1 = (bf16[2,4,1,768]{3,2,1,0:T(2,128)(2,1)S(1)}, bf16[2,4,1,768]{3,2,1,0:T(2,128)(2,1)S(1)}, u32[]{:S(2)}, u32[]{:S(2)}) collective-permute-start(bf16[2,4,1,768]{3,2,1,0:T(2,128)(2,1)S(1)} %get-tuple-element.142), channel_id=1, source_target_pairs={{1,0},{2,1},{3,2},{4,3},{5,4},{6,5},{7,6},{8,7},{9,8},{10,9},{11,1... | collective-permute-start | bytes 36872 | tf_op jit(solution)/shard_map/ppermute | solution.py:692
  48.5 25.9 %collective-permute-start.7 = (bf16[4,32,1536]{2,1,0:T(8,128)(2,1)}, bf16[4,32,1536]{2,1,0:T(8,128)(2,1)}, u32[]{:S(2)}, u32[]{:S(2)}) collective-permute-start(bf16[4,32,1536]{2,1,0:T(8,128)(2,1)} %get-tuple-element.134), channel_id=1, source_target_pairs={{0,24},{4,28},{8,16},{12,20},{16,8},{20,12},{24,0},{28,4},{1,25},{... | collective-permute-start | bytes 1179656 | tf_op jit(solution)/shard_map/ppermute | solution.py:701
  49.9 24.5 %collective-permute-start.6 = (bf16[4,32,1536]{2,1,0:T(8,128)(2,1)}, bf16[4,32,1536]{2,1,0:T(8,128)(2,1)}, u32[]{:S(2)}, u32[]{:S(2)}) collective-permute-start(bf16[4,32,1536]{2,1,0:T(8,128)(2,1)} %get-tuple-element.135), channel_id=1, source_target_pairs={{0,16},{4,20},{8,24},{12,28},{16,0},{20,4},{24,8},{28,12},{1,17},{... | collective-permute-start | bytes 1179656 | tf_op jit(solution)/shard_map/ppermute | solution.py:701
  50.5 23.9 %collective-permute-start.5 = (bf16[4,32,1536]{2,1,0:T(8,128)(2,1)}, bf16[4,32,1536]{2,1,0:T(8,128)(2,1)}, u32[]{:S(2)}, u32[]{:S(2)}) collective-permute-start(bf16[4,32,1536]{2,1,0:T(8,128)(2,1)} %get-tuple-element.136), channel_id=1, source_target_pairs={{0,8},{4,12},{8,0},{12,4},{16,24},{20,28},{24,16},{28,20},{1,9},{5... | collective-permute-start | bytes 1179656 | tf_op jit(solution)/shard_map/ppermute | solution.py:701
  58.4 14.4 %collective-permute-start.9 = (bf16[128,384]{1,0:T(8,128)(2,1)}, bf16[128,384]{1,0:T(8,128)(2,1)}, u32[]{:S(2)}, u32[]{:S(2)}) collective-permute-start(bf16[128,384]{1,0:T(8,128)(2,1)} %pad_maximum_fusion.3.refs_0_), channel_id=1, source_target_pairs={{0,2},{1,3},{2,0},{3,1},{4,6},{5,7},{6,4},{7,5},{8,10},{9,11},{10,... | collective-permute-start | bytes 294920 | tf_op jit(solution)/shard_map/ppermute | solution.py:706
  63.2 9.6 %collective-permute-start.8 = (bf16[128,384]{1,0:T(8,128)(2,1)}, bf16[128,384]{1,0:T(8,128)(2,1)}, u32[]{:S(2)}, u32[]{:S(2)}) collective-permute-start(bf16[128,384]{1,0:T(8,128)(2,1)} %pad_maximum_fusion.3.refs_0_), channel_id=1, source_target_pairs={{0,1},{1,0},{2,3},{3,2},{4,5},{5,4},{6,7},{7,6},{8,9},{9,8},{10,11... | collective-permute-start | bytes 294920 | tf_op jit(solution)/shard_map/ppermute | solution.py:706
  66.8 84.2 %reduce-scatter.5.cloned.1.call-start = ((), (), s32[]{:S(2)}) async-start(), calls=%async_computation.4 | async-start | bytes 1966080 | tf_op jit(solution)/shard_map/reduce_scatter | solution.py:777
  76.2 20.4 %collective-permute-start.12 = (bf16[512,1536]{1,0:T(8,128)(2,1)S(1)}, bf16[512,1536]{1,0:T(8,128)(2,1)}, u32[]{:S(2)}, u32[]{:S(2)}) collective-permute-start(bf16[512,1536]{1,0:T(8,128)(2,1)S(1)} %bitcast.44), channel_id=1, source_target_pairs={{0,4},{4,0},{8,12},{12,8},{16,20},{20,16},{24,28},{28,24},{1,5},{5... | collective-permute-start | bytes 4718600 | tf_op jit(solution)/shard_map/ppermute | solution.py:711
  79.2 17.4 %collective-permute-start.11 = (bf16[512,256]{1,0:T(8,128)(2,1)}, bf16[512,256]{1,0:T(8,128)(2,1)S(1)}, u32[]{:S(2)}, u32[]{:S(2)}) collective-permute-start(bf16[512,256]{1,0:T(8,128)(2,1)} %get-tuple-element.75), channel_id=1, source_target_pairs={{0,4},{4,0},{8,12},{12,8},{16,20},{20,16},{24,28},{28,24},{1,5},{5... | collective-permute-start | bytes 786440 | tf_op jit(solution)/shard_map/ppermute | solution.py:711
  96.6 7.9 %collective-permute-start.14 = (bf16[512,1152]{1,0:T(8,128)(2,1)}, bf16[512,1152]{1,0:T(8,128)(2,1)S(1)}, u32[]{:S(2)}, u32[]{:S(2)}) collective-permute-start(bf16[512,1152]{1,0:T(8,128)(2,1)} %all-gather.4.cloned.1.call-done.xa_ref), channel_id=1, source_target_pairs={{0,4},{4,0},{8,12},{12,8},{16,20},{20,16},{24,28},{28,24},{1,5},{5... | collective-permute-start | bytes 3538952 | tf_op jit(solution)/shard_map/ppermute | solution.py:711
  116.6 77.8 %reduce-scatter.3.cloned.1.call-start = ((), (), s32[]{:S(2)}) async-start(), calls=%async_computation.3 | async-start | bytes 1966080 | tf_op jit(solution)/shard_map/reduce_scatter | solution.py:794
  128.9 15.6 %collective-permute-start.17 = (bf16[2,384,384]{2,1,0:T(8,128)(2,1)}, bf16[2,384,384]{2,1,0:T(8,128)(2,1)S(1)}, u32[]{:S(2)}, u32[]{:S(2)}) collective-permute-start(bf16[2,384,384]{2,1,0:T(8,128)(2,1)} %get-tuple-element.95), channel_id=1, source_target_pairs={{0,8},{4,12},{8,0},{12,4},{16,24},{20,28},{24,16},{28,20},{1,9},{5... | collective-permute-start | bytes 1769480 | tf_op jit(solution)/shard_map/ppermute | solution.py:701
  129.4 15.3 %collective-permute-start.18 = (bf16[2,384,384]{2,1,0:T(8,128)(2,1)}, bf16[2,384,384]{2,1,0:T(8,128)(2,1)S(1)}, u32[]{:S(2)}, u32[]{:S(2)}) collective-permute-start(bf16[2,384,384]{2,1,0:T(8,128)(2,1)} %get-tuple-element.97), channel_id=1, source_target_pairs={{0,16},{4,20},{8,24},{12,28},{16,0},{20,4},{24,8},{28,12},{1,17},{... | collective-permute-start | bytes 1769480 | tf_op jit(solution)/shard_map/ppermute | solution.py:701
  152.0 7.9 %collective-permute-start.19 = (bf16[2,32,1536]{2,1,0:T(8,128)(2,1)S(1)}, bf16[2,32,1536]{2,1,0:T(8,128)(2,1)S(1)}, u32[]{:S(2)}, u32[]{:S(2)}) collective-permute-start(bf16[2,32,1536]{2,1,0:T(8,128)(2,1)S(1)} %slice.61.rest_0_), channel_id=1, source_target_pairs={{0,8},{4,12},{8,0},{12,4},{16,24},{20,28},{24,16},{28,20},{1,9},{5... | collective-permute-start | bytes 589832 | tf_op jit(solution)/shard_map/ppermute | solution.py:701
  152.6 9.0 %collective-permute-start.21 = (bf16[384,384]{1,0:T(8,128)(2,1)S(1)}, bf16[384,384]{1,0:T(8,128)(2,1)S(1)}, u32[]{:S(2)}, u32[]{:S(2)}) collective-permute-start(bf16[384,384]{1,0:T(8,128)(2,1)S(1)} %get-tuple-element.98), channel_id=1, source_target_pairs={{0,16},{4,20},{8,24},{12,28},{16,0},{20,4},{24,8},{28,12},{1,17},{... | collective-permute-start | bytes 884744 | tf_op jit(solution)/shard_map/ppermute | solution.py:701
  154.1 11.0 %collective-permute-start.22 = (bf16[384,384]{1,0:T(8,128)(2,1)S(1)}, bf16[384,384]{1,0:T(8,128)(2,1)S(1)}, u32[]{:S(2)}, u32[]{:S(2)}) collective-permute-start(bf16[384,384]{1,0:T(8,128)(2,1)S(1)} %get-tuple-element.99), channel_id=1, source_target_pairs={{0,8},{4,12},{8,0},{12,4},{16,24},{20,28},{24,16},{28,20},{1,9},{5... | collective-permute-start | bytes 884744 | tf_op jit(solution)/shard_map/ppermute | solution.py:701
  165.3 14.1 %collective-permute-start.25 = (bf16[192,768]{1,0:T(8,128)(2,1)S(1)}, bf16[192,768]{1,0:T(8,128)(2,1)S(1)}, u32[]{:S(2)}, u32[]{:S(2)}) collective-permute-start(bf16[192,768]{1,0:T(8,128)(2,1)S(1)} %get-tuple-element.104.refs_4_), channel_id=1, source_target_pairs={{0,8},{4,12},{8,0},{12,4},{16,24},{20,28},{24,16},{28,20},{1,9},{5... | collective-permute-start | bytes 884744 | tf_op jit(solution)/shard_map/ppermute | solution.py:701
  166.0 13.4 %collective-permute-start.27 = (bf16[192,768]{1,0:T(8,128)(2,1)S(1)}, bf16[192,768]{1,0:T(8,128)(2,1)S(1)}, u32[]{:S(2)}, u32[]{:S(2)}) collective-permute-start(bf16[192,768]{1,0:T(8,128)(2,1)S(1)} %get-tuple-element.112), channel_id=1, source_target_pairs={{0,16},{4,20},{8,24},{12,28},{16,0},{20,4},{24,8},{28,12},{1,17},{... | collective-permute-start | bytes 884744 | tf_op jit(solution)/shard_map/ppermute | solution.py:701
  168.7 10.3 %collective-permute-start.23 = (bf16[2,4,1,1536]{3,2,1,0:T(2,128)(2,1)S(1)}, bf16[2,4,1,1536]{3,2,1,0:T(2,128)(2,1)S(1)}, u32[]{:S(2)}, u32[]{:S(2)}) collective-permute-start(bf16[2,4,1,1536]{3,2,1,0:T(2,128)(2,1)S(1)} %get-tuple-element.106), channel_id=1, source_target_pairs={{0,1},{1,2},{2,3},{3,4},{4,5},{5,6},{6,7},{7,8},{8,9},{9,10},{10,1... | collective-permute-start | bytes 73736 | tf_op jit(solution)/shard_map/ppermute | solution.py:692
  170.9 8.5 %collective-permute-start.24 = (bf16[2,4,1,1536]{3,2,1,0:T(2,128)(2,1)S(1)}, bf16[2,4,1,1536]{3,2,1,0:T(2,128)(2,1)S(1)}, u32[]{:S(2)}, u32[]{:S(2)}) collective-permute-start(bf16[2,4,1,1536]{3,2,1,0:T(2,128)(2,1)S(1)} %get-tuple-element.107.refs_1_), channel_id=1, source_target_pairs={{1,0},{2,1},{3,2},{4,3},{5,4},{6,5},{7,6},{8,7},{9,8},{10,9},{11,1... | collective-permute-start | bytes 73736 | tf_op jit(solution)/shard_map/ppermute | solution.py:692
  184.4 16.2 %collective-permute-start.33 = (bf16[384,768]{1,0:T(8,128)(2,1)S(1)}, bf16[384,768]{1,0:T(8,128)(2,1)S(1)}, u32[]{:S(2)}, u32[]{:S(2)}) collective-permute-start(bf16[384,768]{1,0:T(8,128)(2,1)S(1)} %constant_dynamic-update-slice_fusion.2.refs_1_), channel_id=1, source_target_pairs={{0,8},{4,12},{8,0},{12,4},{16,24},{20,28},{24,16},{28,20},{1,9},{5... | collective-permute-start | bytes 1769480 | tf_op jit(solution)/shard_map/ppermute | solution.py:701
  184.4 19.9 %collective-permute-start.32 = (bf16[384,768]{1,0:T(8,128)(2,1)S(1)}, bf16[384,768]{1,0:T(8,128)(2,1)}, u32[]{:S(2)}, u32[]{:S(2)}) collective-permute-start(bf16[384,768]{1,0:T(8,128)(2,1)S(1)} %constant_dynamic-update-slice_fusion.refs_0_), channel_id=1, source_target_pairs={{0,16},{4,20},{8,24},{12,28},{16,0},{20,4},{24,8},{28,12},{1,17},{... | collective-permute-start | bytes 1769480 | tf_op jit(solution)/shard_map/ppermute | solution.py:701
  (54 other events, 333.6 us)
Sparse Core Ops, SparseCore 0:
  9.6 35.9 all-gather.5
  66.9 29.6 all-gather.3
  116.7 34.2 reduce-scatter.4
  153.2 36.3 reduce-scatter.2

commit v18 on v14

--- a/solution.py
+++ b/solution.py
@@ -263,38 +263,37 @@
     )(d_conv, low, high, conv_weight, *deps)
 
 
-def pack_kernel(w_ref, pack_ref, turned_ref, token_ref):
+def pack_kernel(at_ref, w_ref, own_ref, other_ref, own_turned, other_turned, token_ref):
     token_ref[...] = jnp.zeros_like(token_ref)
+    first_head = at_ref[1] == 0
     for i in range(3):
-        for head in range(pack_ref.shape[0]):
-            part = w_ref[i, :, head * DH : (head + 1) * DH]
-            columns = slice(i * DH, (i + 1) * DH)
-            pack_ref[head, :, columns] = part
-            turned_ref[head, columns, :] = part.T
-
-
-def pack_weights(w_qkv):
+        low, high = w_ref[i, :, :DH], w_ref[i, :, DH:]
+        columns = slice(i * DH, (i + 1) * DH)
+        own = jnp.where(first_head, low, high)
+        other = jnp.where(first_head, high, low)
+        own_ref[:, columns] = own
+        other_ref[:, columns] = other
+        own_turned[columns, :] = own.T
+        other_turned[columns, :] = other.T
+
+
+def pack_weights(at, w_qkv):
     _, width, local = w_qkv.shape
-    heads = local // DH
     tile = local
+    plain = pl.BlockSpec((tile, 3 * DH), lambda n: (n, 0))
+    turned = pl.BlockSpec((3 * DH, tile), lambda n: (0, n))
     return pl.pallas_call(
         pack_kernel,
         grid=(width // tile,),
-        in_specs=[pl.BlockSpec((3, tile, local), lambda n: (0, n, 0))],
-        out_specs=[
-            pl.BlockSpec((heads, tile, 3 * DH), lambda n: (0, n, 0)),
-            pl.BlockSpec((heads, 3 * DH, tile), lambda n: (0, 0, n)),
-            pl.BlockSpec(TOKEN.shape, lambda n: (0, 0)),
-        ],
-        out_shape=[
-            jax.ShapeDtypeStruct((heads, width, 3 * DH), BF),
-            jax.ShapeDtypeStruct((heads, 3 * DH, width), BF),
-            TOKEN,
-        ],
+        in_specs=[SCALARS, pl.BlockSpec((3, tile, local), lambda n: (0, n, 0))],
+        out_specs=[plain, plain, turned, turned, pl.BlockSpec(TOKEN.shape, lambda n: (0, 0))],
+        out_shape=[jax.ShapeDtypeStruct((width, 3 * DH), BF)] * 2
+        + [jax.ShapeDtypeStruct((3 * DH, width), BF)] * 2
+        + [TOKEN],
         compiler_params=params(),
         cost_estimate=COST,
         name="pack_weights",
-    )(w_qkv)
+    )(at, w_qkv)
 
 
 def product_kernel(head_ref, x_ref, w_ref, *rest, contract):
@@ -674,28 +673,29 @@
         [lax.dynamic_index_in_dim(grad_z, own_seq ^ j, 2, keepdims=False) for j in range(seqs)]
     )
     grad_rows = jnp.stack([grad_slots[j] for j in order], axis=1).reshape(half, width)
-    w_pack, w_turned, packed = pack_weights(after(w_qkv, normed_slab))
+    *weights, packed = pack_weights(at, after(w_qkv, normed_slab))
     w_rows = w_out.reshape(heads, DH, width)
     d_other, one = head_product(head_other, grad_rows, w_rows, NT, "d_o_other")
     d_got = swap_heads(d_other)
     d_mine, two = head_product(head_mine, grad_rows, w_rows, NT, "d_o_own")
     grad_swapped = swap_heads(grad_rows)
-    normed_rows, d_got, d_mine, grad_swapped, w_pack, w_turned, *tokens = (
-        lax.optimization_barrier(
-            (normed_rows, d_got, d_mine, grad_swapped, w_pack, w_turned, packed, one, two)
-        )
-    )
+    normed_rows, d_got, d_mine, grad_swapped, *weights = lax.optimization_barrier(
+        (normed_rows, d_got, d_mine, grad_swapped, *weights, packed, one, two)
+    )
+    w_own, w_other, turned_own, turned_other = [w[None] for w in weights[:4]]
+    tokens = weights[4:]
+    sole = jnp.zeros((1,), jnp.int32)
 
     normed_swapped = swap_heads(normed_rows)
-    qkv_other, _ = head_product(head_other, normed_rows, w_pack, NN, "qkv_other", *tokens)
+    qkv_other, _ = head_product(sole, normed_rows, w_other, NN, "qkv_other", *tokens)
     qkv_got = swap_heads(qkv_other)
-    qkv_mine, _ = head_product(head_mine, normed_rows, w_pack, NN, "qkv_own")
+    qkv_mine, _ = head_product(sole, normed_rows, w_own, NN, "qkv_own")
     result_mine, result_other = attention(qkv_mine, qkv_got, d_mine, d_got, normed_swapped)
     result_got = swap_heads(result_other)
 
     shape = (groups, seqs, rows, width)
-    d_own = term_part(head_mine, result_mine, w_turned, 3 * DH, "d_term_own")
-    d_term = term_part(head_other, result_got, w_turned, 3 * DH, "d_term", d_own)
+    d_own = term_part(sole, result_mine, turned_own, 3 * DH, "d_term_own")
+    d_term = term_part(sole, result_got, turned_other, 3 * DH, "d_term", d_own)
     d_normed = lax.psum_scatter(d_term.reshape(shape), "head", scatter_dimension=0, tiled=False)
     keep_a, send_a, keep_b, send_b = weight_gradients(
         own_seq.reshape(1),

time: 209 us -> 210 us (level)
  Pallas kernels: 56.4 us -> 58.9 us
  waiting for transfers between devices: 63.4 us -> 61.3 us
    pallas_call x1, Pallas kernels: 3.92 us -> 6.35 us  [pack_weights(): pl.pallas_call(pack_kernel, grid=(width // tile,), in_specs=[SCALARS, pl....]
    all_gather x1, waiting for transfers between devices: 2.17 us -> 0.01 us  [unit_body(): normed_rows = lax.all_gather(normed_slab, 'head', axis=0, tiled=True)]
    unnamed x66 -> x76, local copies, waits for them, and re-layouts: 22.7 us -> 23.5 us
  transfers between devices with their start and end apart: 36 -> 36, of which waited for: 20 -> 20; matrix products, arithmetic and copies ran while one was open for 5% -> 5% of each run, Pallas kernels for 21% -> 22%
where the time goes in v18:
time: 210 us; the launch traced here: 207 us
  waiting for transfers between devices  61.3 us (29%)
  Pallas kernels  58.9 us (28%)
  starting transfers between devices  40.1 us (19%)
  local copies, waits for them, and re-layouts  31.9 us (15%)
  between operations  14.3 us (7%)
    ppermute x19, waiting for transfers between devices, trade_chip(): return lax.ppermute(x, 'seq', [(s, s ^ bit * heads) for s in range(count)])  47.8 us
    unnamed x76, local copies, waits for them, and re-layouts  23.5 us
    ppermute x19, starting transfers between devices, trade_chip(): return lax.ppermute(x, 'seq', [(s, s ^ bit * heads) for s in range(count)])  20.2 us
    pallas_call x1, Pallas kernels, encoder(): pl.pallas_call(conv_kernel, grid=(width // tile,), in_specs=[SCALARS, who...  10.1 us
    pallas_call x1, Pallas kernels, weight_gradients(): pl.pallas_call(weight_kernel, grid_spec=pltpu.PrefetchScalarGridSpec(num_...  8.73 us
    pallas_call x2, Pallas kernels, unpack_weights(): pl.pallas_call(unpack_kernel, grid_spec=pltpu.PrefetchScalarGridSpec(num_...  7.75 us
    ppermute x2, starting transfers between devices, neighbour_edges(): lax.ppermute(last, axes, forward)  7.12 us
    ppermute x9, starting transfers between devices, swap_heads(): lax.ppermute(x, 'seq', [(s, s + 1 - 2 * (s % 2)) for s in range(count)])  6.53 us
  transfers between devices with their start and end apart: 36, of which 20 were waited for; matrix products, arithmetic and copies ran while one was open for 5% of the time, Pallas kernels for 22%

profile of v18, /device:TPU:26, one launch (start us, length us, event | category | flops | bytes accessed | tf_op | source)
XLA Modules:
  0.0 207.3 jit_solution(16720441129785967518)
XLA Ops:
  9.1 2.4 %collective-permute-start.1 = (bf16[2,4,1,768]{3,2,1,0:T(2,128)(2,1)S(1)}, bf16[2,4,1,768]{3,2,1,0:T(2,128)(2,1)S(1)}, u32[]{:S(2)}, u32[]{:S(2)}) collective-permute-start(bf16[2,4,1,768]{3,2,1,0:T(2,128)(2,1)S(1)} %get-tuple-element.140), channel_id=1, source_target_pairs={{1,0},{2,1},{3,2},{4,3},{5,4},{6,5},{7,6},{8,7},{9,8},{10,9},{11,1... | collective-permute-start | bytes 36872 | tf_op jit(solution)/shard_map/ppermute | solution.py:625
  11.4 5.0 %collective-permute-start = (bf16[2,4,1,768]{3,2,1,0:T(2,128)(2,1)S(1)}, bf16[2,4,1,768]{3,2,1,0:T(2,128)(2,1)S(1)}, u32[]{:S(2)}, u32[]{:S(2)}) collective-permute-start(bf16[2,4,1,768]{3,2,1,0:T(2,128)(2,1)S(1)} %get-tuple-element.141), channel_id=1, source_target_pairs={{0,1},{1,2},{2,3},{3,4},{4,5},{5,6},{6,7},{7,8},{8,9},{9,10},{10,1... | collective-permute-start | bytes 36872 | tf_op jit(solution)/shard_map/ppermute | solution.py:625
  19.6 10.1 %encoder_forward.1 = (bf16[4,32,1536]{2,1,0:T(8,128)(2,1)}, f32[2,4,32,1536]{3,2,1,0:T(8,128)}, bf16[32,1536]{1,0:T(8,128)(2,1)}, bf16[32,1536]{1,0:T(8,128)(2,1...) custom-call(s32[2]{0:T(128)} %pad_add_fusion.at_ref, bf16[2,4,32,768]{3,2,1,0:T(8,128)(2,1)} %bitcast.66, ...), custom_call_target="tpu_custom_call" | custom-call | flops 1000 | bytes 1000 | tf_op jit(solution)/shard_map/encoder_forward/pallas_call | solution.py:111
  35.0 2.1 %collective-permute-done.3 = bf16[32,1536]{1,0:T(8,128)(2,1)S(1)} collective-permute-done((bf16[32,1536]{1,0:T(8,128)(2,1)}, bf16[32,1536]{1,0:T(8,128)(2,1)S(1)}, u32[]{:S(2)}, u32[]{:S(2)}) %collective-permute-start.3) | collective-permute-done | bytes 98336 | tf_op jit(solution)/shard_map/ppermute | solution.py:634
  39.7 5.9 %all-gather.6.cloned.1.call-done = bf16[128,4,1536]{2,1,0:T(4,128)(2,1)} async-done(((bf16[32,4,1536]{2,1,0:T(4,128)(2,1)}), bf16[128,4,1536]{2,1,0:T(4,128)(2,1)}) %all-gather.6.cloned.1.call-update) | async-done | bytes 1572880 | tf_op jit(solution)/shard_map/all_gather | solution.py:662
  51.0 9.4 %collective-permute-done.7 = bf16[4,32,1536]{2,1,0:T(8,128)(2,1)S(1)} collective-permute-done((bf16[4,32,1536]{2,1,0:T(8,128)(2,1)S(1)}, bf16[4,32,1536]{2,1,0:T(8,128)(2,1)S(1)}, u32[]{:S(2)}, u32[]{:S(2)}) %collective-permute-start.7) | collective-permute-done | bytes 393248 | tf_op jit(solution)/shard_map/ppermute | solution.py:634
  60.4 7.5 %collective-permute-done.6 = bf16[4,32,1536]{2,1,0:T(8,128)(2,1)S(1)} collective-permute-done((bf16[4,32,1536]{2,1,0:T(8,128)(2,1)S(1)}, bf16[4,32,1536]{2,1,0:T(8,128)(2,1)S(1)}, u32[]{:S(2)}, u32[]{:S(2)}) %collective-permute-start.6) | collective-permute-done | bytes 393248 | tf_op jit(solution)/shard_map/ppermute | solution.py:634
  72.6 6.4 %pack_weights.1 = (bf16[1536,576]{1,0:T(8,128)(2,1)S(1)}, bf16[1536,576]{1,0:T(8,128)(2,1)S(1)}, bf16[576,1536]{1,0:T(8,128)(2,1)S(1)}, bf16[576,1536]{1,0:T(8,128)(2,1)S(1)}, f32[8,128]{1,0:T(8,128)S(1)}) custom-call(s32[2]{0:T(128)S(1)} %copy-done.29, bf16[3,1536,384]{2,1,0:T(8,128)(2,1)S(1)} %copy-done.7), custom_call_target="tpu_custom_call" | custom-call | flops 1000 | bytes 1000 | tf_op jit(solution)/shard_map/pack_weights/pallas_call | solution.py:285
  93.4 6.5 %attention.1 = (bf16[512,768]{1,0:T(8,128)(2,1)S(1)}, bf16[512,768]{1,0:T(8,128)(2,1)S(1)}) custom-call(bf16[512,640]{1,0:T(8,128)(2,1)S(1)} %get-tuple-element.79.qa_ref, bf16[512,640]{1,0:T(8,128)(2,1)S(1)} %collective-permute-done.10.qb_ref, bf16[512,256]{1,0:T(8,128)(2,1)S(1)} %copy-done.27, bf16[512,256]{1,0:T(8,128)(2,1)S(1)} %copy-done.25, ...), custom_call_target="tpu_custom_call" | custom-call | flops 1000 | bytes 1000 | tf_op jit(solution)/shard_map/attention/pallas_call | solution.py:380
  102.5 3.0 %d_term.1 = bf16[512,1536]{1,0:T(8,128)(2,1)} custom-call(s32[1]{0:T(128)} %constant.43.clone.1.head_ref, bf16[512,768]{1,0:T(8,128)(2,1)S(1)} %collective-permute-done.12.b_ref.x_ref, bf16[1,576,1536]{2,1,0:T(8,128)(2,1)S(1)} %bitcast.56, f32[512,1536]{1,0:T(8,128)S(1)} %d_term_own.1.rest_0_), custom_call_target="tpu_custom_call" | custom-call | flops 1000 | bytes 1000 | tf_op jit(solution)/shard_map/d_term/pallas_call | solution.py:440
  105.5 2.9 %head_term.1.rest_0_ = bf16[512,1536]{1,0:T(8,128)(2,1)} custom-call(s32[1]{0:T(128)} %bitcast.1.head_ref, bf16[512,768]{1,0:T(8,128)(2,1)S(1)} %get-tuple-element.87.a_ref.x_ref.ra_ref, bf16[512,768]{1,0:T(8,128)(2,1)S(1)} %collective-permute-done.12.b_ref.x_ref, bf16[2,192,1536]{2,1,0:T(8,128)(2,1)S(1)} %bitcast.52), custom_call_target="tpu_custom_call" | custom-call | flops 1000 | bytes 1000 | tf_op jit(solution)/shard_map/head_term/pallas_call | solution.py:407
  108.5 8.7 %weight_gradients.1 = (bf16[2,384,384]{2,1,0:T(8,128)(2,1)}, bf16[2,384,384]{2,1,0:T(8,128)(2,1)}, bf16[2,384,384]{2,1,0:T(8,128)(2,1)}, bf16[2,384,384]{2,1,0:T(8,128)(2,1)}) custom-call(s32[1]{0:T(128)} %bitcast.at_ref, bf16[512,1536]{1,0:T(8,128)(2,1)} %all-gather.4.cloned.1.call-done.x_ref.xa_ref, bf16[512,1536]{1,0:T(8,128)(2,1)} %copy-done.6, ...), custom_call_target="tpu_custom_call" | custom-call | flops 1000 | bytes 1000 | tf_op jit(solution)/shard_map/weight_gradients/pallas_call | solution.py:493
  119.2 13.7 %collective-permute-done.13.got_a = bf16[2,384,384]{2,1,0:T(8,128)(2,1)S(1)} collective-permute-done((bf16[2,384,384]{2,1,0:T(8,128)(2,1)}, bf16[2,384,384]{2,1,0:T(8,128)(2,1)S(1)}, u32[]{:S(2)}, u32[]{:S(2)}) %collective-permute-start.13) | collective-permute-done | bytes 589856 | tf_op jit(solution)/shard_map/ppermute | solution.py:634
  135.4 4.4 %reduce-scatter.5.cloned.1.call-done = bf16[1,4,32,1536]{3,2,1,0:T(8,128)(2,1)} async-done(((bf16[4,4,32,1536]{3,2,1,0:T(8,128)(2,1)}), bf16[1,4,32,1536]{3,2,1,0:T(8,128)(2,1)}) %reduce-scatter.5.cloned.1.call-update) | async-done | bytes 393232 | tf_op jit(solution)/shard_map/reduce_scatter | solution.py:699
  145.2 3.4 %collective-permute-done.15.near_ref = bf16[2,32,1536]{2,1,0:T(8,128)(2,1)S(1)} collective-permute-done((bf16[2,32,1536]{2,1,0:T(8,128)(2,1)S(1)}, bf16[2,32,1536]{2,1,0:T(8,128)(2,1)S(1)}, u32[]{:S(2)}, u32[]{:S(2)}) %collective-permute-start.15) | collective-permute-done | bytes 196640 | tf_op jit(solution)/shard_map/ppermute | solution.py:634
  150.4 3.3 %collective-permute-done.18.last_b = bf16[384,384]{1,0:T(8,128)(2,1)S(1)} collective-permute-done((bf16[384,384]{1,0:T(8,128)(2,1)S(1)}, bf16[384,384]{1,0:T(8,128)(2,1)S(1)}, u32[]{:S(2)}, u32[]{:S(2)}) %collective-permute-start.18) | collective-permute-done | bytes 294944 | tf_op jit(solution)/shard_map/ppermute | solution.py:634
  159.6 3.7 %collective-permute-start.20 = (bf16[2,4,1,1536]{3,2,1,0:T(2,128)(2,1)S(1)}, bf16[2,4,1,1536]{3,2,1,0:T(2,128)(2,1)S(1)}, u32[]{:S(2)}, u32[]{:S(2)}) collective-permute-start(bf16[2,4,1,1536]{3,2,1,0:T(2,128)(2,1)S(1)} %get-tuple-element.105.refs_1_), channel_id=1, source_target_pairs={{1,0},{2,1},{3,2},{4,3},{5,4},{6,5},{7,6},{8,7},{9,8},{10,9},{11,1... | collective-permute-start | bytes 73736 | tf_op jit(solution)/shard_map/ppermute | solution.py:625
  163.4 4.4 %copy-done = bf16[5,768,1536]{2,1,0:T(8,128)(2,1)S(1)} copy-done((bf16[5,768,1536]{2,1,0:T(8,128)(2,1)S(1)}, bf16[5,768,1536]{2,1,0:T(8,128)(2,1)}, u32[]{:S(2)}) %copy-start) | copy-done | bytes 11796504
  168.2 4.8 %collective-permute-start.22 = (bf16[384,768]{1,0:T(8,128)(2,1)S(1)}, bf16[384,768]{1,0:T(8,128)(2,1)S(1)}, u32[]{:S(2)}, u32[]{:S(2)}) collective-permute-start(bf16[384,768]{1,0:T(8,128)(2,1)S(1)} %constant_dynamic-update-slice_fusion.4.refs_0_), channel_id=1, source_target_pairs={{0,4},{4,0},{8,12},{12,8},{16,20},{20,16},{24,28},{28,24},{1,5},{5... | collective-permute-start | bytes 1769480 | tf_op jit(solution)/shard_map/ppermute | solution.py:639
  175.5 4.2 %encoder_backward.1.refs_4_ = bf16[256,768]{1,0:T(8,128)(2,1)S(1)} custom-call(bf16[2,4,32,1536]{3,2,1,0:T(8,128)(2,1)S(1)} %get-tuple-element.103.d_ref, bf16[2,4,1,1536]{3,2,1,0:T(2,128)(2,1)S(1)} %collective-permute-done.19.low_ref, bf16[2,4,1,1536]{3,2,1,0:T(2,128)(2,1)S(1)} %collective-permute-done.20.high_ref, bf16[5,768,1536]{2,1,0:T(8,128)(2,1)S(1)} %copy-done, ...), custom_call_target="tpu_custom_call" | custom-call | flops 1000 | bytes 1000 | tf_op jit(solution)/shard_map/encoder_backward/pallas_call | solution.py:244
  179.8 3.4 %weight_outputs_near.1 = (f32[3,1536,384]{2,1,0:T(8,128)}, f32[2,2,96,1536]{3,2,1,0:T(8,128)}, f32[8,128]{1,0:T(8,128)S(1)}) custom-call(s32[2]{0:T(128)S(1)} %copy-done.29, bf16[384,768]{1,0:T(8,128)(2,1)S(1)} %constant_dynamic-update-slice_fusion.4.refs_0_, bf16[384,768]{1,0:T(8,128)(2,1)S(1)} %constant_dynamic-update-slice_fusion.6.refs_1_, ...), custom_call_target="tpu_custom_call" | custom-call | flops 1000 | bytes 1000 | tf_op jit(solution)/shard_map/weight_outputs_near/pallas_call | solution.py:594
  185.5 2.3 %collective-permute-start.25 = (bf16[32,1536]{1,0:T(8,128)(2,1)S(1)}, bf16[32,1536]{1,0:T(8,128)(2,1)S(1)}, u32[]{:S(2)}, u32[]{:S(2)}) collective-permute-start(bf16[32,1536]{1,0:T(8,128)(2,1)S(1)} %get-tuple-element.138), channel_id=1, source_target_pairs={{0,8},{4,12},{8,0},{12,4},{16,24},{20,28},{24,16},{28,20},{1,9},{5... | collective-permute-start | bytes 294920 | tf_op jit(solution)/shard_map/ppermute | solution.py:634
  190.9 2.2 %collective-permute-done.26.refs_2_ = bf16[32,1536]{1,0:T(8,128)(2,1)S(1)} collective-permute-done((bf16[32,1536]{1,0:T(8,128)(2,1)S(1)}, bf16[32,1536]{1,0:T(8,128)(2,1)S(1)}, u32[]{:S(2)}, u32[]{:S(2)}) %collective-permute-start.26) | collective-permute-done | bytes 98336 | tf_op jit(solution)/shard_map/ppermute | solution.py:634
  196.4 4.3 %weight_outputs_far.1 = (f32[3,1536,384]{2,1,0:T(8,128)}, f32[2,2,96,1536]{3,2,1,0:T(8,128)}, f32[8,128]{1,0:T(8,128)}) custom-call(s32[2]{0:T(128)S(1)} %copy-done.29, bf16[384,768]{1,0:T(8,128)(2,1)} %collective-permute-done.28.refs_0_, bf16[384,768]{1,0:T(8,128)(2,1)S(1)} %collective-permute-done.29.refs_1_, ...), custom_call_target="tpu_custom_call", output_to_operand_aliasing={{0}: (5, {}), {1}: (6, {})} | custom-call | flops 1000 | bytes 1000 | tf_op jit(solution)/shard_map/weight_outputs_far/pallas_call | solution.py:594
  (165 shorter events, 68.9 us)
Async XLA Ops:
  7.2 38.4 %all-gather.6.cloned.1.call-start = ((), (), s32[]{:S(2)}) async-start(), calls=%async_computation.5 | async-start | bytes 1966080 | tf_op jit(solution)/shard_map/all_gather | solution.py:662
  7.9 77.4 %all-gather.4.cloned.1.call-start = ((), (), s32[]{:S(2)}) async-start(), calls=%async_computation.2 | async-start | bytes 1966080 | tf_op jit(solution)/shard_map/all_gather | solution.py:669
  9.1 9.3 %collective-permute-start.1 = (bf16[2,4,1,768]{3,2,1,0:T(2,128)(2,1)S(1)}, bf16[2,4,1,768]{3,2,1,0:T(2,128)(2,1)S(1)}, u32[]{:S(2)}, u32[]{:S(2)}) collective-permute-start(bf16[2,4,1,768]{3,2,1,0:T(2,128)(2,1)S(1)} %get-tuple-element.140), channel_id=1, source_target_pairs={{1,0},{2,1},{3,2},{4,3},{5,4},{6,5},{7,6},{8,7},{9,8},{10,9},{11,1... | collective-permute-start | bytes 36872 | tf_op jit(solution)/shard_map/ppermute | solution.py:625
  39.7 100.1 %reduce-scatter.5.cloned.1.call-start = ((), (), s32[]{:S(2)}) async-start(), calls=%async_computation.4 | async-start | bytes 1966080 | tf_op jit(solution)/shard_map/reduce_scatter | solution.py:699
  47.4 13.0 %collective-permute-start.7 = (bf16[4,32,1536]{2,1,0:T(8,128)(2,1)S(1)}, bf16[4,32,1536]{2,1,0:T(8,128)(2,1)S(1)}, u32[]{:S(2)}, u32[]{:S(2)}) collective-permute-start(bf16[4,32,1536]{2,1,0:T(8,128)(2,1)S(1)} %get-tuple-element.133), channel_id=1, source_target_pairs={{0,24},{4,28},{8,16},{12,20},{16,8},{20,12},{24,0},{28,4},{1,25},{... | collective-permute-start | bytes 1179656 | tf_op jit(solution)/shard_map/ppermute | solution.py:634
  48.9 19.0 %collective-permute-start.6 = (bf16[4,32,1536]{2,1,0:T(8,128)(2,1)S(1)}, bf16[4,32,1536]{2,1,0:T(8,128)(2,1)S(1)}, u32[]{:S(2)}, u32[]{:S(2)}) collective-permute-start(bf16[4,32,1536]{2,1,0:T(8,128)(2,1)S(1)} %get-tuple-element.134), channel_id=1, source_target_pairs={{0,8},{4,12},{8,0},{12,4},{16,24},{20,28},{24,16},{28,20},{1,9},{5... | collective-permute-start | bytes 1179656 | tf_op jit(solution)/shard_map/ppermute | solution.py:634
  50.4 17.5 %collective-permute-start.5 = (bf16[4,32,1536]{2,1,0:T(8,128)(2,1)S(1)}, bf16[4,32,1536]{2,1,0:T(8,128)(2,1)S(1)}, u32[]{:S(2)}, u32[]{:S(2)}) collective-permute-start(bf16[4,32,1536]{2,1,0:T(8,128)(2,1)S(1)} %get-tuple-element.135), channel_id=1, source_target_pairs={{0,16},{4,20},{8,24},{12,28},{16,0},{20,4},{24,8},{28,12},{1,17},{... | collective-permute-start | bytes 1179656 | tf_op jit(solution)/shard_map/ppermute | solution.py:634
  68.3 17.7 %collective-permute-start.9 = (bf16[512,1536]{1,0:T(8,128)(2,1)S(1)}, bf16[512,1536]{1,0:T(8,128)(2,1)}, u32[]{:S(2)}, u32[]{:S(2)}) collective-permute-start(bf16[512,1536]{1,0:T(8,128)(2,1)S(1)} %bitcast.46), channel_id=1, source_target_pairs={{0,4},{4,0},{8,12},{12,8},{16,20},{20,16},{24,28},{28,24},{1,5},{5... | collective-permute-start | bytes 4718600 | tf_op jit(solution)/shard_map/ppermute | solution.py:639
  70.5 14.7 %collective-permute-start.8 = (bf16[512,256]{1,0:T(8,128)(2,1)S(1)}, bf16[512,256]{1,0:T(8,128)(2,1)S(1)}, u32[]{:S(2)}, u32[]{:S(2)}) collective-permute-start(bf16[512,256]{1,0:T(8,128)(2,1)S(1)} %get-tuple-element.67), channel_id=1, source_target_pairs={{0,4},{4,0},{8,12},{12,8},{16,20},{20,16},{24,28},{28,24},{1,5},{5... | collective-permute-start | bytes 786440 | tf_op jit(solution)/shard_map/ppermute | solution.py:639
  105.5 77.7 %reduce-scatter.3.cloned.1.call-start = ((), (), s32[]{:S(2)}) async-start(), calls=%async_computation.3 | async-start | bytes 1966080 | tf_op jit(solution)/shard_map/reduce_scatter | solution.py:714
  117.2 15.6 %collective-permute-start.13 = (bf16[2,384,384]{2,1,0:T(8,128)(2,1)}, bf16[2,384,384]{2,1,0:T(8,128)(2,1)S(1)}, u32[]{:S(2)}, u32[]{:S(2)}) collective-permute-start(bf16[2,384,384]{2,1,0:T(8,128)(2,1)} %get-tuple-element.93), channel_id=1, source_target_pairs={{0,8},{4,12},{8,0},{12,4},{16,24},{20,28},{24,16},{28,20},{1,9},{5... | collective-permute-start | bytes 1769480 | tf_op jit(solution)/shard_map/ppermute | solution.py:634
  117.8 15.4 %collective-permute-start.14 = (bf16[2,384,384]{2,1,0:T(8,128)(2,1)}, bf16[2,384,384]{2,1,0:T(8,128)(2,1)S(1)}, u32[]{:S(2)}, u32[]{:S(2)}) collective-permute-start(bf16[2,384,384]{2,1,0:T(8,128)(2,1)} %get-tuple-element.95), channel_id=1, source_target_pairs={{0,16},{4,20},{8,24},{12,28},{16,0},{20,4},{24,8},{28,12},{1,17},{... | collective-permute-start | bytes 1769480 | tf_op jit(solution)/shard_map/ppermute | solution.py:634
  140.7 7.9 %collective-permute-start.15 = (bf16[2,32,1536]{2,1,0:T(8,128)(2,1)S(1)}, bf16[2,32,1536]{2,1,0:T(8,128)(2,1)S(1)}, u32[]{:S(2)}, u32[]{:S(2)}) collective-permute-start(bf16[2,32,1536]{2,1,0:T(8,128)(2,1)S(1)} %slice.29.rest_0_), channel_id=1, source_target_pairs={{0,8},{4,12},{8,0},{12,4},{16,24},{20,28},{24,16},{28,20},{1,9},{5... | collective-permute-start | bytes 589832 | tf_op jit(solution)/shard_map/ppermute | solution.py:634
  141.4 9.0 %collective-permute-start.17 = (bf16[384,384]{1,0:T(8,128)(2,1)S(1)}, bf16[384,384]{1,0:T(8,128)(2,1)S(1)}, u32[]{:S(2)}, u32[]{:S(2)}) collective-permute-start(bf16[384,384]{1,0:T(8,128)(2,1)S(1)} %get-tuple-element.96), channel_id=1, source_target_pairs={{0,16},{4,20},{8,24},{12,28},{16,0},{20,4},{24,8},{28,12},{1,17},{... | collective-permute-start | bytes 884744 | tf_op jit(solution)/shard_map/ppermute | solution.py:634
  142.8 10.9 %collective-permute-start.18 = (bf16[384,384]{1,0:T(8,128)(2,1)S(1)}, bf16[384,384]{1,0:T(8,128)(2,1)S(1)}, u32[]{:S(2)}, u32[]{:S(2)}) collective-permute-start(bf16[384,384]{1,0:T(8,128)(2,1)S(1)} %get-tuple-element.97), channel_id=1, source_target_pairs={{0,8},{4,12},{8,0},{12,4},{16,24},{20,28},{24,16},{28,20},{1,9},{5... | collective-permute-start | bytes 884744 | tf_op jit(solution)/shard_map/ppermute | solution.py:634
  148.7 7.6 %collective-permute-start.16 = (bf16[2,32,1536]{2,1,0:T(8,128)(2,1)S(1)}, bf16[2,32,1536]{2,1,0:T(8,128)(2,1)S(1)}, u32[]{:S(2)}, u32[]{:S(2)}) collective-permute-start(bf16[2,32,1536]{2,1,0:T(8,128)(2,1)S(1)} %pad_maximum_fusion.1), channel_id=1, source_target_pairs={{0,16},{4,20},{8,24},{12,28},{16,0},{20,4},{24,8},{28,12},{1,17},{... | collective-permute-start | bytes 589832 | tf_op jit(solution)/shard_map/ppermute | solution.py:634
  154.1 14.0 %collective-permute-start.23 = (bf16[192,768]{1,0:T(8,128)(2,1)S(1)}, bf16[192,768]{1,0:T(8,128)(2,1)S(1)}, u32[]{:S(2)}, u32[]{:S(2)}) collective-permute-start(bf16[192,768]{1,0:T(8,128)(2,1)S(1)} %get-tuple-element.110), channel_id=1, source_target_pairs={{0,16},{4,20},{8,24},{12,28},{16,0},{20,4},{24,8},{28,12},{1,17},{... | collective-permute-start | bytes 884744 | tf_op jit(solution)/shard_map/ppermute | solution.py:634
  155.7 12.5 %collective-permute-start.21 = (bf16[192,768]{1,0:T(8,128)(2,1)S(1)}, bf16[192,768]{1,0:T(8,128)(2,1)S(1)}, u32[]{:S(2)}, u32[]{:S(2)}) collective-permute-start(bf16[192,768]{1,0:T(8,128)(2,1)S(1)} %get-tuple-element.102.refs_4_), channel_id=1, source_target_pairs={{0,8},{4,12},{8,0},{12,4},{16,24},{20,28},{24,16},{28,20},{1,9},{5... | collective-permute-start | bytes 884744 | tf_op jit(solution)/shard_map/ppermute | solution.py:634
  157.5 10.3 %collective-permute-start.19 = (bf16[2,4,1,1536]{3,2,1,0:T(2,128)(2,1)S(1)}, bf16[2,4,1,1536]{3,2,1,0:T(2,128)(2,1)S(1)}, u32[]{:S(2)}, u32[]{:S(2)}) collective-permute-start(bf16[2,4,1,1536]{3,2,1,0:T(2,128)(2,1)S(1)} %get-tuple-element.104), channel_id=1, source_target_pairs={{0,1},{1,2},{2,3},{3,4},{4,5},{5,6},{6,7},{7,8},{8,9},{9,10},{10,1... | collective-permute-start | bytes 73736 | tf_op jit(solution)/shard_map/ppermute | solution.py:625
  159.6 8.5 %collective-permute-start.20 = (bf16[2,4,1,1536]{3,2,1,0:T(2,128)(2,1)S(1)}, bf16[2,4,1,1536]{3,2,1,0:T(2,128)(2,1)S(1)}, u32[]{:S(2)}, u32[]{:S(2)}) collective-permute-start(bf16[2,4,1,1536]{3,2,1,0:T(2,128)(2,1)S(1)} %get-tuple-element.105.refs_1_), channel_id=1, source_target_pairs={{1,0},{2,1},{3,2},{4,3},{5,4},{6,5},{7,6},{8,7},{9,8},{10,9},{11,1... | collective-permute-start | bytes 73736 | tf_op jit(solution)/shard_map/ppermute | solution.py:625
  173.1 16.2 %collective-permute-start.29 = (bf16[384,768]{1,0:T(8,128)(2,1)S(1)}, bf16[384,768]{1,0:T(8,128)(2,1)S(1)}, u32[]{:S(2)}, u32[]{:S(2)}) collective-permute-start(bf16[384,768]{1,0:T(8,128)(2,1)S(1)} %constant_dynamic-update-slice_fusion.6.refs_1_), channel_id=1, source_target_pairs={{0,8},{4,12},{8,0},{12,4},{16,24},{20,28},{24,16},{28,20},{1,9},{5... | collective-permute-start | bytes 1769480 | tf_op jit(solution)/shard_map/ppermute | solution.py:634
  173.2 19.9 %collective-permute-start.28 = (bf16[384,768]{1,0:T(8,128)(2,1)S(1)}, bf16[384,768]{1,0:T(8,128)(2,1)}, u32[]{:S(2)}, u32[]{:S(2)}) collective-permute-start(bf16[384,768]{1,0:T(8,128)(2,1)S(1)} %constant_dynamic-update-slice_fusion.4.refs_0_), channel_id=1, source_target_pairs={{0,16},{4,20},{8,24},{12,28},{16,0},{20,4},{24,8},{28,12},{1,17},{... | collective-permute-start | bytes 1769480 | tf_op jit(solution)/shard_map/ppermute | solution.py:634
  185.5 7.6 %collective-permute-start.26 = (bf16[32,1536]{1,0:T(8,128)(2,1)S(1)}, bf16[32,1536]{1,0:T(8,128)(2,1)S(1)}, u32[]{:S(2)}, u32[]{:S(2)}) collective-permute-start(bf16[32,1536]{1,0:T(8,128)(2,1)S(1)} %get-tuple-element.137), channel_id=1, source_target_pairs={{0,16},{4,20},{8,24},{12,28},{16,0},{20,4},{24,8},{28,12},{1,17},{... | collective-permute-start | bytes 294920 | tf_op jit(solution)/shard_map/ppermute | solution.py:634
  185.5 7.6 %collective-permute-start.25 = (bf16[32,1536]{1,0:T(8,128)(2,1)S(1)}, bf16[32,1536]{1,0:T(8,128)(2,1)S(1)}, u32[]{:S(2)}, u32[]{:S(2)}) collective-permute-start(bf16[32,1536]{1,0:T(8,128)(2,1)S(1)} %get-tuple-element.138), channel_id=1, source_target_pairs={{0,8},{4,12},{8,0},{12,4},{16,24},{20,28},{24,16},{28,20},{1,9},{5... | collective-permute-start | bytes 294920 | tf_op jit(solution)/shard_map/ppermute | solution.py:634
  (47 other events, 210.0 us)
Sparse Core Ops, SparseCore 0:
  9.6 35.9 all-gather.5
  47.7 35.9 all-gather.3
  105.6 34.1 reduce-scatter.4
  142.0 36.3 reduce-scatter.2

commit v19 on v18

--- a/solution.py
+++ b/solution.py
@@ -330,6 +330,33 @@
         cost_estimate=COST,
         name=name,
     )(head, x, weight, *deps)
+
+
+def place_kernel(at_ref, *refs):
+    del at_ref
+    for slot, ref in enumerate(refs[:-1]):
+
+        @pl.when(pl.program_id(0) == slot)
+        def _():
+            refs[-1][0] = ref[...]
+
+
+def placed(at, slots, name):
+    count = len(slots)
+    shape = slots[0].shape
+    return pl.pallas_call(
+        place_kernel,
+        grid_spec=pltpu.PrefetchScalarGridSpec(
+            num_scalar_prefetch=1,
+            grid=(count,),
+            in_specs=[pl.BlockSpec(shape, lambda q, at: (0, 0, 0))] * count,
+            out_specs=pl.BlockSpec((1,) + shape, lambda q, at: (q ^ at[0], 0, 0, 0)),
+        ),
+        out_shape=jax.ShapeDtypeStruct((count,) + shape, slots[0].dtype),
+        compiler_params=params(),
+        cost_estimate=COST,
+        name=name,
+    )(at, *slots)
 
 
 def attention_kernel(qa_ref, qb_ref, da_ref, db_ref, *rest, block):
@@ -634,6 +661,11 @@
     return lax.ppermute(x, "seq", [(s, s ^ (bit * heads)) for s in range(count)])
 
 
+def trade_z(x, bit):
+    count = lax.axis_size("head")
+    return lax.ppermute(x, "head", [(z, z ^ bit) for z in range(count)])
+
+
 def swap_heads(x):
     count = lax.axis_size("seq")
     return lax.ppermute(x, "seq", [(s, s + 1 - 2 * (s % 2)) for s in range(count)])
@@ -659,21 +691,29 @@
 
     order = (0, 2, 1, 3)
 
-    grad_z = lax.all_gather(grad_out, "head", axis=0, tiled=False)
+    edge = width - width // seqs
+    grad_z = lax.all_gather(grad_out[:, :, :edge], "head", axis=0, tiled=False)
 
     pairs = jnp.transpose(enc_in.reshape(rows, 2, seqs, enc_in.shape[2]), (1, 2, 0, 3))
-    low, high = neighbour_edges(pairs[:, :, :1, :], pairs[:, :, -1:, :])
+    ends = (pairs[:, :, :1, :], pairs[:, :, -1:, :])
+    own_part, *ends = lax.optimization_barrier((grad_out[:, :, edge:], *ends))
+    parts = [trade_z(own_part, q) for q in range(1, groups)]
+    low, high = neighbour_edges(*ends)
+    low, high, *parts = lax.optimization_barrier((low, high, *parts))
     skip, slope, normed = encoder(at, pairs, low, high, conv_weight, norm_gain)
     normed = to_chips(normed)
     normed_slab = jnp.concatenate([normed[j] for j in order], axis=0)
     normed_rows = lax.all_gather(normed_slab, "head", axis=0, tiled=True)
 
     grad_z = after(grad_z, normed_slab)
+    own_z = lax.axis_index("head").astype(jnp.int32).reshape(1)
+    grad_z = jnp.concatenate([grad_z, placed(own_z, [own_part, *parts], "grad_last")], axis=3)
     grad_slots = to_chips(
         [lax.dynamic_index_in_dim(grad_z, own_seq ^ j, 2, keepdims=False) for j in range(seqs)]
     )
+    *weights, packed = pack_weights(at, after(w_qkv, normed_slab))
+    *grad_slots, packed = lax.optimization_barrier((*grad_slots, packed))
     grad_rows = jnp.stack([grad_slots[j] for j in order], axis=1).reshape(half, width)
-    *weights, packed = pack_weights(at, after(w_qkv, normed_slab))
     w_rows = w_out.reshape(heads, DH, width)
     d_other, one = head_product(head_other, grad_rows, w_rows, NT, "d_o_other")
     d_got = swap_heads(d_other)
@@ -893,7 +933,7 @@
 def body(enc_in, conv_weight, norm_gain, w_qkv, w_out, grad_out):
     heads = w_qkv.shape[2] // DH
     seqs = enc_in.shape[1]
-    fits = heads == 2 and seqs == 4 and seqs * heads == lax.axis_size("seq")
+    fits = lax.axis_size("head") == 4 and heads == 2 and seqs == 4 and seqs * heads == lax.axis_size("seq")
     fits = fits and conv_weight.shape[2] == seqs * w_qkv.shape[2]
     chosen = unit_body if fits else gathered_body
     return chosen(enc_in, conv_weight, norm_gain, w_qkv, w_out, grad_out)

time: 210 us -> 208 us (level)
  waiting for transfers between devices: 61.3 us -> 58.1 us
  starting transfers between devices: 40.1 us -> 42.8 us
  local copies, waits for them, and re-layouts: 31.9 us -> 29.6 us
    ppermute x19, waiting for transfers between devices: 47.8 us -> 36.6 us  [trade_chip(): return lax.ppermute(x, 'seq', [(s, s ^ bit * heads) for s in range(count)])]
    all_gather x1, waiting for transfers between devices: 0.01 us -> 9.6 us  [unit_body(): normed_rows = lax.all_gather(normed_slab, 'head', axis=0, tiled=True)]
    all_gather x1, waiting for transfers between devices: 5.87 us -> 0.02 us  [unit_body(): grad_z = lax.all_gather(grad_out[:, :, :edge], 'head', axis=0, tiled=False)]
    ppermute x0 -> x3, starting transfers between devices: none -> 4.45 us  [trade_z(): return lax.ppermute(x, 'head', [(z, z ^ bit) for z in range(count)])]
    unnamed x76 -> x79, local copies, waits for them, and re-layouts: 23.5 us -> 19.4 us
    ppermute x2, starting transfers between devices: 7.12 us -> 4.04 us  [neighbour_edges(): lax.ppermute(last, axes, forward)]
    slice x1 -> x3, local copies, waits for them, and re-layouts: 0.04 us -> 2.75 us  [the longest x1 1.78 us: unit_body(): grad_z = lax.all_gather(grad_out[:, :, :edge], 'head', axis=0, tiled=False)]
    ppermute x2, waiting for transfers between devices: 0.36 us -> 2.97 us  [neighbour_edges(): lax.ppermute(first, axes, backward)]
  transfers between devices with their start and end apart: 36 -> 39, of which waited for: 20 -> 21; matrix products, arithmetic and copies ran while one was open for 5% -> 6% of each run, Pallas kernels for 22% -> 22%
where the time goes in v19:
time: 208 us; the launch traced here: 205 us
  Pallas kernels  59.4 us (29%)
  waiting for transfers between devices  58.1 us (28%)
  starting transfers between devices  42.8 us (21%)
  local copies, waits for them, and re-layouts  29.6 us (14%)
  between operations  14.4 us (7%)
    ppermute x19, waiting for transfers between devices, trade_chip(): return lax.ppermute(x, 'seq', [(s, s ^ bit * heads) for s in range(count)])  36.6 us
    ppermute x19, starting transfers between devices, trade_chip(): return lax.ppermute(x, 'seq', [(s, s ^ bit * heads) for s in range(count)])  20.2 us
    unnamed x79, local copies, waits for them, and re-layouts  19.4 us
    pallas_call x1, Pallas kernels, encoder(): pl.pallas_call(conv_kernel, grid=(width // tile,), in_specs=[SCALARS, who...  10.2 us
    all_gather x1, waiting for transfers between devices, unit_body(): normed_rows = lax.all_gather(normed_slab, 'head', axis=0, tiled=True)  9.6 us
    pallas_call x1, Pallas kernels, weight_gradients(): pl.pallas_call(weight_kernel, grid_spec=pltpu.PrefetchScalarGridSpec(num_...  8.86 us
    pallas_call x2, Pallas kernels, unpack_weights(): pl.pallas_call(unpack_kernel, grid_spec=pltpu.PrefetchScalarGridSpec(num_...  7.76 us
    ppermute x2, starting transfers between devices, neighbour_edges(): lax.ppermute(first, axes, backward)  7.63 us
  transfers between devices with their start and end apart: 39, of which 21 were waited for; matrix products, arithmetic and copies ran while one was open for 6% of the time, Pallas kernels for 22%

profile of v19, /device:TPU:26, one launch (start us, length us, event | category | flops | bytes accessed | tf_op | source)
XLA Modules:
  0.0 205.1 jit_solution(12912826151380544920)
XLA Ops:
  13.1 2.5 %collective-permute-start.2 = (bf16[32,4,384]{2,1,0:T(4,128)(2,1)S(1)}, bf16[32,4,384]{2,1,0:T(4,128)(2,1)S(1)}, u32[]{:S(2)}, u32[]{:S(2)}) collective-permute-start(bf16[32,4,384]{2,1,0:T(4,128)(2,1)S(1)} %slice.33.refs_0_), channel_id=1, source_target_pairs={{0,1},{1,0},{2,3},{3,2},{4,5},{5,4},{6,7},{7,6},{8,9},{9,8},{10,11... | collective-permute-start | bytes 294920 | tf_op jit(solution)/shard_map/ppermute | solution.py:666
  17.5 3.9 %collective-permute-start.1 = (bf16[2,4,1,768]{3,2,1,0:T(2,128)(2,1)S(1)}, bf16[2,4,1,768]{3,2,1,0:T(2,128)(2,1)S(1)}, u32[]{:S(2)}, u32[]{:S(2)}) collective-permute-start(bf16[2,4,1,768]{3,2,1,0:T(2,128)(2,1)S(1)} %get-tuple-element.76), channel_id=1, source_target_pairs={{1,0},{2,1},{3,2},{4,3},{5,4},{6,5},{7,6},{8,7},{9,8},{10,9},{11,1... | collective-permute-start | bytes 36872 | tf_op jit(solution)/shard_map/ppermute | solution.py:652
  22.7 2.6 %collective-permute-done.1.high_ref = bf16[2,4,1,768]{3,2,1,0:T(2,128)(2,1)S(1)} collective-permute-done((bf16[2,4,1,768]{3,2,1,0:T(2,128)(2,1)S(1)}, bf16[2,4,1,768]{3,2,1,0:T(2,128)(2,1)S(1)}, u32[]{:S(2)}, u32[]{:S(2)}) %collective-permute-start.1) | collective-permute-done | bytes 12320 | tf_op jit(solution)/shard_map/ppermute | solution.py:652
  25.3 2.3 %collective-permute-done.3.refs_2_ = bf16[32,4,384]{2,1,0:T(4,128)(2,1)S(1)} collective-permute-done((bf16[32,4,384]{2,1,0:T(4,128)(2,1)S(1)}, bf16[32,4,384]{2,1,0:T(4,128)(2,1)S(1)}, u32[]{:S(2)}, u32[]{:S(2)}) %collective-permute-start.3) | collective-permute-done | bytes 98336 | tf_op jit(solution)/shard_map/ppermute | solution.py:666
  27.5 10.2 %encoder_forward.1 = (bf16[4,32,1536]{2,1,0:T(8,128)(2,1)}, f32[2,4,32,1536]{3,2,1,0:T(8,128)}, bf16[32,1536]{1,0:T(8,128)(2,1)}, bf16[32,1536]{1,0:T(8,128)(2,1...) custom-call(s32[2]{0:T(128)} %pad_add_fusion.at_ref, bf16[2,4,32,768]{3,2,1,0:T(8,128)(2,1)} %bitcast.68, ...), custom_call_target="tpu_custom_call" | custom-call | flops 1000 | bytes 1000 | tf_op jit(solution)/shard_map/encoder_forward/pallas_call | solution.py:111
  53.3 6.4 %pack_weights.1 = (bf16[1536,576]{1,0:T(8,128)(2,1)S(1)}, bf16[1536,576]{1,0:T(8,128)(2,1)S(1)}, bf16[576,1536]{1,0:T(8,128)(2,1)S(1)}, bf16[576,1536]{1,0:T(8,128)(2,1)S(1)}, f32[8,128]{1,0:T(8,128)S(1)}) custom-call(s32[2]{0:T(128)S(1)} %copy-done.29, bf16[3,1536,384]{2,1,0:T(8,128)(2,1)S(1)} %copy-done.7), custom_call_target="tpu_custom_call" | custom-call | flops 1000 | bytes 1000 | tf_op jit(solution)/shard_map/pack_weights/pallas_call | solution.py:285
  63.6 5.7 %collective-permute-done.9 = bf16[4,32,1536]{2,1,0:T(8,128)(2,1)S(1)} collective-permute-done((bf16[4,32,1536]{2,1,0:T(8,128)(2,1)S(1)}, bf16[4,32,1536]{2,1,0:T(8,128)(2,1)S(1)}, u32[]{:S(2)}, u32[]{:S(2)}) %collective-permute-start.9) | collective-permute-done | bytes 393248 | tf_op jit(solution)/shard_map/ppermute | solution.py:661
  74.3 9.6 %all-gather.4.cloned.1.call-done.x_ref.xa_ref = bf16[512,1536]{1,0:T(8,128)(2,1)} async-done(((bf16[128,1536]{1,0:T(8,128)(2,1)}), bf16[512,1536]{1,0:T(8,128)(2,1)}) %all-gather.4.cloned.1.call-update) | async-done | bytes 1572880 | tf_op jit(solution)/shard_map/all_gather | solution.py:706
  91.2 6.5 %attention.1 = (bf16[512,768]{1,0:T(8,128)(2,1)S(1)}, bf16[512,768]{1,0:T(8,128)(2,1)S(1)}) custom-call(bf16[512,640]{1,0:T(8,128)(2,1)S(1)} %get-tuple-element.105.qa_ref, bf16[512,640]{1,0:T(8,128)(2,1)S(1)} %collective-permute-done.13.qb_ref, bf16[512,256]{1,0:T(8,128)(2,1)S(1)} %copy-done.27, bf16[512,256]{1,0:T(8,128)(2,1)S(1)} %copy-done.25, ...), custom_call_target="tpu_custom_call" | custom-call | flops 1000 | bytes 1000 | tf_op jit(solution)/shard_map/attention/pallas_call | solution.py:407
  100.1 3.0 %d_term.1 = bf16[512,1536]{1,0:T(8,128)(2,1)} custom-call(s32[1]{0:T(128)} %constant.45.clone.1.head_ref, bf16[512,768]{1,0:T(8,128)(2,1)S(1)} %collective-permute-done.15.b_ref.x_ref, bf16[1,576,1536]{2,1,0:T(8,128)(2,1)S(1)} %bitcast.58, f32[512,1536]{1,0:T(8,128)S(1)} %d_term_own.1.rest_0_), custom_call_target="tpu_custom_call" | custom-call | flops 1000 | bytes 1000 | tf_op jit(solution)/shard_map/d_term/pallas_call | solution.py:467
  103.2 3.0 %head_term.1.rest_0_ = bf16[512,1536]{1,0:T(8,128)(2,1)} custom-call(s32[1]{0:T(128)} %bitcast.1.head_ref, bf16[512,768]{1,0:T(8,128)(2,1)S(1)} %get-tuple-element.113.a_ref.x_ref.ra_ref, bf16[512,768]{1,0:T(8,128)(2,1)S(1)} %collective-permute-done.15.b_ref.x_ref, bf16[2,192,1536]{2,1,0:T(8,128)(2,1)S(1)} %bitcast.54), custom_call_target="tpu_custom_call" | custom-call | flops 1000 | bytes 1000 | tf_op jit(solution)/shard_map/head_term/pallas_call | solution.py:434
  106.2 8.9 %weight_gradients.1 = (bf16[2,384,384]{2,1,0:T(8,128)(2,1)}, bf16[2,384,384]{2,1,0:T(8,128)(2,1)}, bf16[2,384,384]{2,1,0:T(8,128)(2,1)}, bf16[2,384,384]{2,1,0:T(8,128)(2,1)}) custom-call(s32[1]{0:T(128)} %bitcast.at_ref, bf16[512,1536]{1,0:T(8,128)(2,1)} %all-gather.4.cloned.1.call-done.x_ref.xa_ref, bf16[512,1536]{1,0:T(8,128)(2,1)} %copy-done.6, ...), custom_call_target="tpu_custom_call" | custom-call | flops 1000 | bytes 1000 | tf_op jit(solution)/shard_map/weight_gradients/pallas_call | solution.py:520
  117.1 13.7 %collective-permute-done.16.got_a = bf16[2,384,384]{2,1,0:T(8,128)(2,1)S(1)} collective-permute-done((bf16[2,384,384]{2,1,0:T(8,128)(2,1)}, bf16[2,384,384]{2,1,0:T(8,128)(2,1)S(1)}, u32[]{:S(2)}, u32[]{:S(2)}) %collective-permute-start.16) | collective-permute-done | bytes 589856 | tf_op jit(solution)/shard_map/ppermute | solution.py:661
  133.3 4.2 %reduce-scatter.5.cloned.1.call-done = bf16[1,4,32,1536]{3,2,1,0:T(8,128)(2,1)} async-done(((bf16[4,4,32,1536]{3,2,1,0:T(8,128)(2,1)}), bf16[1,4,32,1536]{3,2,1,0:T(8,128)(2,1)}) %reduce-scatter.5.cloned.1.call-update) | async-done | bytes 393232 | tf_op jit(solution)/shard_map/reduce_scatter | solution.py:739
  143.0 3.4 %collective-permute-done.18.near_ref = bf16[2,32,1536]{2,1,0:T(8,128)(2,1)S(1)} collective-permute-done((bf16[2,32,1536]{2,1,0:T(8,128)(2,1)S(1)}, bf16[2,32,1536]{2,1,0:T(8,128)(2,1)S(1)}, u32[]{:S(2)}, u32[]{:S(2)}) %collective-permute-start.18) | collective-permute-done | bytes 196640 | tf_op jit(solution)/shard_map/ppermute | solution.py:661
  148.1 3.4 %collective-permute-done.21.last_b = bf16[384,384]{1,0:T(8,128)(2,1)S(1)} collective-permute-done((bf16[384,384]{1,0:T(8,128)(2,1)S(1)}, bf16[384,384]{1,0:T(8,128)(2,1)S(1)}, u32[]{:S(2)}, u32[]{:S(2)}) %collective-permute-start.21) | collective-permute-done | bytes 294944 | tf_op jit(solution)/shard_map/ppermute | solution.py:661
  155.3 2.1 %collective-permute-start.22 = (bf16[2,4,1,1536]{3,2,1,0:T(2,128)(2,1)S(1)}, bf16[2,4,1,1536]{3,2,1,0:T(2,128)(2,1)S(1)}, u32[]{:S(2)}, u32[]{:S(2)}) collective-permute-start(bf16[2,4,1,1536]{3,2,1,0:T(2,128)(2,1)S(1)} %get-tuple-element.130), channel_id=1, source_target_pairs={{0,1},{1,2},{2,3},{3,4},{4,5},{5,6},{6,7},{7,8},{8,9},{9,10},{10,1... | collective-permute-start | bytes 73736 | tf_op jit(solution)/shard_map/ppermute | solution.py:652
  157.4 3.7 %collective-permute-start.23 = (bf16[2,4,1,1536]{3,2,1,0:T(2,128)(2,1)S(1)}, bf16[2,4,1,1536]{3,2,1,0:T(2,128)(2,1)S(1)}, u32[]{:S(2)}, u32[]{:S(2)}) collective-permute-start(bf16[2,4,1,1536]{3,2,1,0:T(2,128)(2,1)S(1)} %get-tuple-element.131.refs_1_), channel_id=1, source_target_pairs={{1,0},{2,1},{3,2},{4,3},{5,4},{6,5},{7,6},{8,7},{9,8},{10,9},{11,1... | collective-permute-start | bytes 73736 | tf_op jit(solution)/shard_map/ppermute | solution.py:652
  161.2 4.4 %copy-done = bf16[5,768,1536]{2,1,0:T(8,128)(2,1)S(1)} copy-done((bf16[5,768,1536]{2,1,0:T(8,128)(2,1)S(1)}, bf16[5,768,1536]{2,1,0:T(8,128)(2,1)}, u32[]{:S(2)}) %copy-start) | copy-done | bytes 11796504
  166.0 4.8 %collective-permute-start.25 = (bf16[384,768]{1,0:T(8,128)(2,1)S(1)}, bf16[384,768]{1,0:T(8,128)(2,1)S(1)}, u32[]{:S(2)}, u32[]{:S(2)}) collective-permute-start(bf16[384,768]{1,0:T(8,128)(2,1)S(1)} %constant_dynamic-update-slice_fusion.5.refs_0_), channel_id=1, source_target_pairs={{0,4},{4,0},{8,12},{12,8},{16,20},{20,16},{24,28},{28,24},{1,5},{5... | collective-permute-start | bytes 1769480 | tf_op jit(solution)/shard_map/ppermute | solution.py:671
  173.3 4.3 %encoder_backward.1.refs_4_ = bf16[256,768]{1,0:T(8,128)(2,1)S(1)} custom-call(bf16[2,4,32,1536]{3,2,1,0:T(8,128)(2,1)S(1)} %get-tuple-element.129.d_ref, bf16[2,4,1,1536]{3,2,1,0:T(2,128)(2,1)S(1)} %collective-permute-done.22.low_ref, bf16[2,4,1,1536]{3,2,1,0:T(2,128)(2,1)S(1)} %collective-permute-done.23.high_ref, bf16[5,768,1536]{2,1,0:T(8,128)(2,1)S(1)} %copy-done, ...), custom_call_target="tpu_custom_call" | custom-call | flops 1000 | bytes 1000 | tf_op jit(solution)/shard_map/encoder_backward/pallas_call | solution.py:244
  177.7 3.4 %weight_outputs_near.1 = (f32[3,1536,384]{2,1,0:T(8,128)}, f32[2,2,96,1536]{3,2,1,0:T(8,128)}, f32[8,128]{1,0:T(8,128)S(1)}) custom-call(s32[2]{0:T(128)S(1)} %copy-done.29, bf16[384,768]{1,0:T(8,128)(2,1)S(1)} %constant_dynamic-update-slice_fusion.5.refs_0_, bf16[384,768]{1,0:T(8,128)(2,1)S(1)} %constant_dynamic-update-slice_fusion.7.refs_1_, ...), custom_call_target="tpu_custom_call" | custom-call | flops 1000 | bytes 1000 | tf_op jit(solution)/shard_map/weight_outputs_near/pallas_call | solution.py:621
  183.4 2.3 %collective-permute-start.28 = (bf16[32,1536]{1,0:T(8,128)(2,1)S(1)}, bf16[32,1536]{1,0:T(8,128)(2,1)S(1)}, u32[]{:S(2)}, u32[]{:S(2)}) collective-permute-start(bf16[32,1536]{1,0:T(8,128)(2,1)S(1)} %get-tuple-element.164), channel_id=1, source_target_pairs={{0,8},{4,12},{8,0},{12,4},{16,24},{20,28},{24,16},{28,20},{1,9},{5... | collective-permute-start | bytes 294920 | tf_op jit(solution)/shard_map/ppermute | solution.py:661
  194.2 4.3 %weight_outputs_far.1 = (f32[3,1536,384]{2,1,0:T(8,128)}, f32[2,2,96,1536]{3,2,1,0:T(8,128)}, f32[8,128]{1,0:T(8,128)}) custom-call(s32[2]{0:T(128)S(1)} %copy-done.29, bf16[384,768]{1,0:T(8,128)(2,1)} %collective-permute-done.31.refs_0_, bf16[384,768]{1,0:T(8,128)(2,1)S(1)} %collective-permute-done.32.refs_1_, ...), custom_call_target="tpu_custom_call", output_to_operand_aliasing={{0}: (5, {}), {1}: (6, {})} | custom-call | flops 1000 | bytes 1000 | tf_op jit(solution)/shard_map/weight_outputs_far/pallas_call | solution.py:621
  (178 shorter events, 72.1 us)
Async XLA Ops:
  7.2 40.8 %all-gather.6.cloned.1.call-start = ((), (), s32[]{:S(2)}) async-start(), calls=%async_computation.5 | async-start | bytes 1474560 | tf_op jit(solution)/shard_map/all_gather | solution.py:695
  9.0 74.8 %all-gather.4.cloned.1.call-start = ((), (), s32[]{:S(2)}) async-start(), calls=%async_computation.2 | async-start | bytes 1966080 | tf_op jit(solution)/shard_map/all_gather | solution.py:706
  11.1 14.1 %collective-permute-start.4 = (bf16[32,4,384]{2,1,0:T(4,128)(2,1)S(1)}, bf16[32,4,384]{2,1,0:T(4,128)(2,1)S(1)}, u32[]{:S(2)}, u32[]{:S(2)}) collective-permute-start(bf16[32,4,384]{2,1,0:T(4,128)(2,1)S(1)} %slice.33.refs_0_), channel_id=1, source_target_pairs={{0,3},{1,2},{2,1},{3,0},{4,7},{5,6},{6,5},{7,4},{8,11},{9,10},{10,... | collective-permute-start | bytes 294920 | tf_op jit(solution)/shard_map/ppermute | solution.py:666
  11.4 16.1 %collective-permute-start.3 = (bf16[32,4,384]{2,1,0:T(4,128)(2,1)S(1)}, bf16[32,4,384]{2,1,0:T(4,128)(2,1)S(1)}, u32[]{:S(2)}, u32[]{:S(2)}) collective-permute-start(bf16[32,4,384]{2,1,0:T(4,128)(2,1)S(1)} %slice.33.refs_0_), channel_id=1, source_target_pairs={{0,2},{1,3},{2,0},{3,1},{4,6},{5,7},{6,4},{7,5},{8,10},{9,11},{10,... | collective-permute-start | bytes 294920 | tf_op jit(solution)/shard_map/ppermute | solution.py:666
  13.1 14.4 %collective-permute-start.2 = (bf16[32,4,384]{2,1,0:T(4,128)(2,1)S(1)}, bf16[32,4,384]{2,1,0:T(4,128)(2,1)S(1)}, u32[]{:S(2)}, u32[]{:S(2)}) collective-permute-start(bf16[32,4,384]{2,1,0:T(4,128)(2,1)S(1)} %slice.33.refs_0_), channel_id=1, source_target_pairs={{0,1},{1,0},{2,3},{3,2},{4,5},{5,4},{6,7},{7,6},{8,9},{9,8},{10,11... | collective-permute-start | bytes 294920 | tf_op jit(solution)/shard_map/ppermute | solution.py:666
  17.5 7.7 %collective-permute-start.1 = (bf16[2,4,1,768]{3,2,1,0:T(2,128)(2,1)S(1)}, bf16[2,4,1,768]{3,2,1,0:T(2,128)(2,1)S(1)}, u32[]{:S(2)}, u32[]{:S(2)}) collective-permute-start(bf16[2,4,1,768]{3,2,1,0:T(2,128)(2,1)S(1)} %get-tuple-element.76), channel_id=1, source_target_pairs={{1,0},{2,1},{3,2},{4,3},{5,4},{6,5},{7,6},{8,7},{9,8},{10,9},{11,1... | collective-permute-start | bytes 36872 | tf_op jit(solution)/shard_map/ppermute | solution.py:652
  47.9 89.7 %reduce-scatter.5.cloned.1.call-start = ((), (), s32[]{:S(2)}) async-start(), calls=%async_computation.4 | async-start | bytes 1966080 | tf_op jit(solution)/shard_map/reduce_scatter | solution.py:739
  49.8 13.8 %collective-permute-start.10 = (bf16[4,32,1536]{2,1,0:T(8,128)(2,1)S(1)}, bf16[4,32,1536]{2,1,0:T(8,128)(2,1)S(1)}, u32[]{:S(2)}, u32[]{:S(2)}) collective-permute-start(bf16[4,32,1536]{2,1,0:T(8,128)(2,1)S(1)} %get-tuple-element.158), channel_id=1, source_target_pairs={{0,24},{4,28},{8,16},{12,20},{16,8},{20,12},{24,0},{28,4},{1,25},{... | collective-permute-start | bytes 1179656 | tf_op jit(solution)/shard_map/ppermute | solution.py:661
  50.4 18.9 %collective-permute-start.9 = (bf16[4,32,1536]{2,1,0:T(8,128)(2,1)S(1)}, bf16[4,32,1536]{2,1,0:T(8,128)(2,1)S(1)}, u32[]{:S(2)}, u32[]{:S(2)}) collective-permute-start(bf16[4,32,1536]{2,1,0:T(8,128)(2,1)S(1)} %get-tuple-element.159), channel_id=1, source_target_pairs={{0,16},{4,20},{8,24},{12,28},{16,0},{20,4},{24,8},{28,12},{1,17},{... | collective-permute-start | bytes 1179656 | tf_op jit(solution)/shard_map/ppermute | solution.py:661
  51.6 17.8 %collective-permute-start.8 = (bf16[4,32,1536]{2,1,0:T(8,128)(2,1)S(1)}, bf16[4,32,1536]{2,1,0:T(8,128)(2,1)S(1)}, u32[]{:S(2)}, u32[]{:S(2)}) collective-permute-start(bf16[4,32,1536]{2,1,0:T(8,128)(2,1)S(1)} %get-tuple-element.160), channel_id=1, source_target_pairs={{0,8},{4,12},{8,0},{12,4},{16,24},{20,28},{24,16},{28,20},{1,9},{5... | collective-permute-start | bytes 1179656 | tf_op jit(solution)/shard_map/ppermute | solution.py:661
  69.7 14.2 %collective-permute-start.12 = (bf16[512,1536]{1,0:T(8,128)(2,1)S(1)}, bf16[512,1536]{1,0:T(8,128)(2,1)}, u32[]{:S(2)}, u32[]{:S(2)}) collective-permute-start(bf16[512,1536]{1,0:T(8,128)(2,1)S(1)} %bitcast.48), channel_id=1, source_target_pairs={{0,4},{4,0},{8,12},{12,8},{16,20},{20,16},{24,28},{28,24},{1,5},{5... | collective-permute-start | bytes 4718600 | tf_op jit(solution)/shard_map/ppermute | solution.py:671
  103.1 78.0 %reduce-scatter.3.cloned.1.call-start = ((), (), s32[]{:S(2)}) async-start(), calls=%async_computation.3 | async-start | bytes 1966080 | tf_op jit(solution)/shard_map/reduce_scatter | solution.py:754
  115.0 15.7 %collective-permute-start.16 = (bf16[2,384,384]{2,1,0:T(8,128)(2,1)}, bf16[2,384,384]{2,1,0:T(8,128)(2,1)S(1)}, u32[]{:S(2)}, u32[]{:S(2)}) collective-permute-start(bf16[2,384,384]{2,1,0:T(8,128)(2,1)} %get-tuple-element.119), channel_id=1, source_target_pairs={{0,8},{4,12},{8,0},{12,4},{16,24},{20,28},{24,16},{28,20},{1,9},{5... | collective-permute-start | bytes 1769480 | tf_op jit(solution)/shard_map/ppermute | solution.py:661
  115.6 15.4 %collective-permute-start.17 = (bf16[2,384,384]{2,1,0:T(8,128)(2,1)}, bf16[2,384,384]{2,1,0:T(8,128)(2,1)S(1)}, u32[]{:S(2)}, u32[]{:S(2)}) collective-permute-start(bf16[2,384,384]{2,1,0:T(8,128)(2,1)} %get-tuple-element.121), channel_id=1, source_target_pairs={{0,16},{4,20},{8,24},{12,28},{16,0},{20,4},{24,8},{28,12},{1,17},{... | collective-permute-start | bytes 1769480 | tf_op jit(solution)/shard_map/ppermute | solution.py:661
  138.5 7.9 %collective-permute-start.18 = (bf16[2,32,1536]{2,1,0:T(8,128)(2,1)S(1)}, bf16[2,32,1536]{2,1,0:T(8,128)(2,1)S(1)}, u32[]{:S(2)}, u32[]{:S(2)}) collective-permute-start(bf16[2,32,1536]{2,1,0:T(8,128)(2,1)S(1)} %slice.37.rest_0_), channel_id=1, source_target_pairs={{0,8},{4,12},{8,0},{12,4},{16,24},{20,28},{24,16},{28,20},{1,9},{5... | collective-permute-start | bytes 589832 | tf_op jit(solution)/shard_map/ppermute | solution.py:661
  139.1 9.0 %collective-permute-start.20 = (bf16[384,384]{1,0:T(8,128)(2,1)S(1)}, bf16[384,384]{1,0:T(8,128)(2,1)S(1)}, u32[]{:S(2)}, u32[]{:S(2)}) collective-permute-start(bf16[384,384]{1,0:T(8,128)(2,1)S(1)} %get-tuple-element.122), channel_id=1, source_target_pairs={{0,16},{4,20},{8,24},{12,28},{16,0},{20,4},{24,8},{28,12},{1,17},{... | collective-permute-start | bytes 884744 | tf_op jit(solution)/shard_map/ppermute | solution.py:661
  140.6 10.9 %collective-permute-start.21 = (bf16[384,384]{1,0:T(8,128)(2,1)S(1)}, bf16[384,384]{1,0:T(8,128)(2,1)S(1)}, u32[]{:S(2)}, u32[]{:S(2)}) collective-permute-start(bf16[384,384]{1,0:T(8,128)(2,1)S(1)} %get-tuple-element.123), channel_id=1, source_target_pairs={{0,8},{4,12},{8,0},{12,4},{16,24},{20,28},{24,16},{28,20},{1,9},{5... | collective-permute-start | bytes 884744 | tf_op jit(solution)/shard_map/ppermute | solution.py:661
  146.4 7.6 %collective-permute-start.19 = (bf16[2,32,1536]{2,1,0:T(8,128)(2,1)S(1)}, bf16[2,32,1536]{2,1,0:T(8,128)(2,1)S(1)}, u32[]{:S(2)}, u32[]{:S(2)}) collective-permute-start(bf16[2,32,1536]{2,1,0:T(8,128)(2,1)S(1)} %pad_maximum_fusion.1), channel_id=1, source_target_pairs={{0,16},{4,20},{8,24},{12,28},{16,0},{20,4},{24,8},{28,12},{1,17},{... | collective-permute-start | bytes 589832 | tf_op jit(solution)/shard_map/ppermute | solution.py:661
  151.9 14.1 %collective-permute-start.26 = (bf16[192,768]{1,0:T(8,128)(2,1)S(1)}, bf16[192,768]{1,0:T(8,128)(2,1)S(1)}, u32[]{:S(2)}, u32[]{:S(2)}) collective-permute-start(bf16[192,768]{1,0:T(8,128)(2,1)S(1)} %get-tuple-element.136), channel_id=1, source_target_pairs={{0,16},{4,20},{8,24},{12,28},{16,0},{20,4},{24,8},{28,12},{1,17},{... | collective-permute-start | bytes 884744 | tf_op jit(solution)/shard_map/ppermute | solution.py:661
  153.4 12.6 %collective-permute-start.24 = (bf16[192,768]{1,0:T(8,128)(2,1)S(1)}, bf16[192,768]{1,0:T(8,128)(2,1)S(1)}, u32[]{:S(2)}, u32[]{:S(2)}) collective-permute-start(bf16[192,768]{1,0:T(8,128)(2,1)S(1)} %get-tuple-element.128.refs_4_), channel_id=1, source_target_pairs={{0,8},{4,12},{8,0},{12,4},{16,24},{20,28},{24,16},{28,20},{1,9},{5... | collective-permute-start | bytes 884744 | tf_op jit(solution)/shard_map/ppermute | solution.py:661
  155.3 10.3 %collective-permute-start.22 = (bf16[2,4,1,1536]{3,2,1,0:T(2,128)(2,1)S(1)}, bf16[2,4,1,1536]{3,2,1,0:T(2,128)(2,1)S(1)}, u32[]{:S(2)}, u32[]{:S(2)}) collective-permute-start(bf16[2,4,1,1536]{3,2,1,0:T(2,128)(2,1)S(1)} %get-tuple-element.130), channel_id=1, source_target_pairs={{0,1},{1,2},{2,3},{3,4},{4,5},{5,6},{6,7},{7,8},{8,9},{9,10},{10,1... | collective-permute-start | bytes 73736 | tf_op jit(solution)/shard_map/ppermute | solution.py:652
  157.4 8.5 %collective-permute-start.23 = (bf16[2,4,1,1536]{3,2,1,0:T(2,128)(2,1)S(1)}, bf16[2,4,1,1536]{3,2,1,0:T(2,128)(2,1)S(1)}, u32[]{:S(2)}, u32[]{:S(2)}) collective-permute-start(bf16[2,4,1,1536]{3,2,1,0:T(2,128)(2,1)S(1)} %get-tuple-element.131.refs_1_), channel_id=1, source_target_pairs={{1,0},{2,1},{3,2},{4,3},{5,4},{6,5},{7,6},{8,7},{9,8},{10,9},{11,1... | collective-permute-start | bytes 73736 | tf_op jit(solution)/shard_map/ppermute | solution.py:652
  170.9 16.2 %collective-permute-start.32 = (bf16[384,768]{1,0:T(8,128)(2,1)S(1)}, bf16[384,768]{1,0:T(8,128)(2,1)S(1)}, u32[]{:S(2)}, u32[]{:S(2)}) collective-permute-start(bf16[384,768]{1,0:T(8,128)(2,1)S(1)} %constant_dynamic-update-slice_fusion.7.refs_1_), channel_id=1, source_target_pairs={{0,8},{4,12},{8,0},{12,4},{16,24},{20,28},{24,16},{28,20},{1,9},{5... | collective-permute-start | bytes 1769480 | tf_op jit(solution)/shard_map/ppermute | solution.py:661
  171.0 19.9 %collective-permute-start.31 = (bf16[384,768]{1,0:T(8,128)(2,1)S(1)}, bf16[384,768]{1,0:T(8,128)(2,1)}, u32[]{:S(2)}, u32[]{:S(2)}) collective-permute-start(bf16[384,768]{1,0:T(8,128)(2,1)S(1)} %constant_dynamic-update-slice_fusion.5.refs_0_), channel_id=1, source_target_pairs={{0,16},{4,20},{8,24},{12,28},{16,0},{20,4},{24,8},{28,12},{1,17},{... | collective-permute-start | bytes 1769480 | tf_op jit(solution)/shard_map/ppermute | solution.py:661
  (51 other events, 255.5 us)
Sparse Core Ops, SparseCore 0:
  10.2 32.1 all-gather.5
  48.0 35.8 all-gather.3
  103.2 34.2 reduce-scatter.4
  139.7 36.3 reduce-scatter.2

commit v20 on v19

--- a/solution.py
+++ b/solution.py
@@ -695,14 +695,13 @@
     grad_z = lax.all_gather(grad_out[:, :, :edge], "head", axis=0, tiled=False)
 
     pairs = jnp.transpose(enc_in.reshape(rows, 2, seqs, enc_in.shape[2]), (1, 2, 0, 3))
-    ends = (pairs[:, :, :1, :], pairs[:, :, -1:, :])
-    own_part, *ends = lax.optimization_barrier((grad_out[:, :, edge:], *ends))
+    low, high = neighbour_edges(pairs[:, :, :1, :], pairs[:, :, -1:, :])
+    own_part = grad_out[:, :, edge:]
     parts = [trade_z(own_part, q) for q in range(1, groups)]
-    low, high = neighbour_edges(*ends)
-    low, high, *parts = lax.optimization_barrier((low, high, *parts))
     skip, slope, normed = encoder(at, pairs, low, high, conv_weight, norm_gain)
     normed = to_chips(normed)
     normed_slab = jnp.concatenate([normed[j] for j in order], axis=0)
+    normed_slab, *parts = lax.optimization_barrier((normed_slab, *parts))
     normed_rows = lax.all_gather(normed_slab, "head", axis=0, tiled=True)
 
     grad_z = after(grad_z, normed_slab)

time: 208 us -> 208 us (level)
  waiting for transfers between devices: 58.1 us -> 54.9 us
  starting transfers between devices: 42.8 us -> 45.5 us
    ppermute x19, waiting for transfers between devices: 36.6 us -> 32.6 us  [trade_chip(): return lax.ppermute(x, 'seq', [(s, s ^ bit * heads) for s in range(count)])]
    ppermute x3, waiting for transfers between devices: 2.28 us -> 6.15 us  [trade_z(): return lax.ppermute(x, 'head', [(z, z ^ bit) for z in range(count)])]
    ppermute x2, starting transfers between devices: 4.04 us -> 7.1 us  [neighbour_edges(): lax.ppermute(last, axes, forward)]
    ppermute x2, waiting for transfers between devices: 2.97 us -> 0.34 us  [neighbour_edges(): lax.ppermute(first, axes, backward)]
    unnamed x79 -> x74, local copies, waits for them, and re-layouts: 19.4 us -> 18.6 us
  transfers between devices with their start and end apart: 39 -> 39, of which waited for: 21 -> 20; matrix products, arithmetic and copies ran while one was open for 6% -> 6% of each run, Pallas kernels for 22% -> 22%
where the time goes in v20:
time: 208 us; the launch traced here: 205 us
  Pallas kernels  59.5 us (29%)
  waiting for transfers between devices  54.9 us (26%)
  starting transfers between devices  45.5 us (22%)
  local copies, waits for them, and re-layouts  28.8 us (14%)
  between operations  14.3 us (7%)
  other arithmetic  2.55 us (1%)
    ppermute x19, waiting for transfers between devices, trade_chip(): return lax.ppermute(x, 'seq', [(s, s ^ bit * heads) for s in range(count)])  32.6 us
    ppermute x19, starting transfers between devices, trade_chip(): return lax.ppermute(x, 'seq', [(s, s ^ bit * heads) for s in range(count)])  20.2 us
    unnamed x74, local copies, waits for them, and re-layouts  18.6 us
    pallas_call x1, Pallas kernels, encoder(): pl.pallas_call(conv_kernel, grid=(width // tile,), in_specs=[SCALARS, who...  10.1 us
    pallas_call x1, Pallas kernels, weight_gradients(): pl.pallas_call(weight_kernel, grid_spec=pltpu.PrefetchScalarGridSpec(num_...  8.89 us
    all_gather x1, waiting for transfers between devices, unit_body(): normed_rows = lax.all_gather(normed_slab, 'head', axis=0, tiled=True)  8.79 us
    pallas_call x2, Pallas kernels, unpack_weights(): pl.pallas_call(unpack_kernel, grid_spec=pltpu.PrefetchScalarGridSpec(num_...  7.76 us
    ppermute x2, starting transfers between devices, neighbour_edges(): lax.ppermute(last, axes, forward)  7.1 us
  transfers between devices with their start and end apart: 39, of which 20 were waited for; matrix products, arithmetic and copies ran while one was open for 6% of the time, Pallas kernels for 22%

profile of v20, /device:TPU:26, one launch (start us, length us, event | category | flops | bytes accessed | tf_op | source)
XLA Modules:
  0.0 205.5 jit_solution(7726713997263635946)
XLA Ops:
  10.2 2.4 %collective-permute-start.1 = (bf16[2,4,1,768]{3,2,1,0:T(2,128)(2,1)S(1)}, bf16[2,4,1,768]{3,2,1,0:T(2,128)(2,1)S(1)}, u32[]{:S(2)}, u32[]{:S(2)}) collective-permute-start(bf16[2,4,1,768]{3,2,1,0:T(2,128)(2,1)S(1)} %get-tuple-element.158), channel_id=1, source_target_pairs={{1,0},{2,1},{3,2},{4,3},{5,4},{6,5},{7,6},{8,7},{9,8},{10,9},{11,1... | collective-permute-start | bytes 36872 | tf_op jit(solution)/shard_map/ppermute | solution.py:652
  12.6 5.0 %collective-permute-start = (bf16[2,4,1,768]{3,2,1,0:T(2,128)(2,1)S(1)}, bf16[2,4,1,768]{3,2,1,0:T(2,128)(2,1)S(1)}, u32[]{:S(2)}, u32[]{:S(2)}) collective-permute-start(bf16[2,4,1,768]{3,2,1,0:T(2,128)(2,1)S(1)} %get-tuple-element.159), channel_id=1, source_target_pairs={{0,1},{1,2},{2,3},{3,4},{4,5},{5,6},{6,7},{7,8},{8,9},{9,10},{10,1... | collective-permute-start | bytes 36872 | tf_op jit(solution)/shard_map/ppermute | solution.py:652
  20.1 10.1 %encoder_forward.1 = (bf16[4,32,1536]{2,1,0:T(8,128)(2,1)}, f32[2,4,32,1536]{3,2,1,0:T(8,128)}, bf16[32,1536]{1,0:T(8,128)(2,1)}, bf16[32,1536]{1,0:T(8,128)(2,1...) custom-call(s32[2]{0:T(128)} %pad_add_fusion.at_ref, bf16[2,4,32,768]{3,2,1,0:T(8,128)(2,1)} %bitcast.68, ...), custom_call_target="tpu_custom_call" | custom-call | flops 1000 | bytes 1000 | tf_op jit(solution)/shard_map/encoder_forward/pallas_call | solution.py:111
  34.7 4.6 %collective-permute-start.7 = (bf16[32,4,384]{2,1,0:T(4,128)(2,1)S(1)}, bf16[32,4,384]{2,1,0:T(4,128)(2,1)S(1)}, u32[]{:S(2)}, u32[]{:S(2)}) collective-permute-start(bf16[32,4,384]{2,1,0:T(4,128)(2,1)S(1)} %slice.35.refs_0_), channel_id=1, source_target_pairs={{0,3},{1,2},{2,1},{3,0},{4,7},{5,6},{6,5},{7,4},{8,11},{9,10},{10,... | collective-permute-start | bytes 294920 | tf_op jit(solution)/shard_map/ppermute | solution.py:666
  43.0 4.7 %collective-permute-done.6.refs_2_ = bf16[32,4,384]{2,1,0:T(4,128)(2,1)S(1)} collective-permute-done((bf16[32,4,384]{2,1,0:T(4,128)(2,1)S(1)}, bf16[32,4,384]{2,1,0:T(4,128)(2,1)S(1)}, u32[]{:S(2)}, u32[]{:S(2)}) %collective-permute-start.6) | collective-permute-done | bytes 98336 | tf_op jit(solution)/shard_map/ppermute | solution.py:666
  53.6 6.4 %pack_weights.1 = (bf16[1536,576]{1,0:T(8,128)(2,1)S(1)}, bf16[1536,576]{1,0:T(8,128)(2,1)S(1)}, bf16[576,1536]{1,0:T(8,128)(2,1)S(1)}, bf16[576,1536]{1,0:T(8,128)(2,1)S(1)}, f32[8,128]{1,0:T(8,128)S(1)}) custom-call(s32[2]{0:T(128)S(1)} %copy-done.29, bf16[3,1536,384]{2,1,0:T(8,128)(2,1)S(1)} %copy-done.7), custom_call_target="tpu_custom_call" | custom-call | flops 1000 | bytes 1000 | tf_op jit(solution)/shard_map/pack_weights/pallas_call | solution.py:285
  63.9 6.4 %collective-permute-done.9 = bf16[4,32,1536]{2,1,0:T(8,128)(2,1)S(1)} collective-permute-done((bf16[4,32,1536]{2,1,0:T(8,128)(2,1)S(1)}, bf16[4,32,1536]{2,1,0:T(8,128)(2,1)S(1)}, u32[]{:S(2)}, u32[]{:S(2)}) %collective-permute-start.9) | collective-permute-done | bytes 393248 | tf_op jit(solution)/shard_map/ppermute | solution.py:661
  75.3 8.8 %all-gather.4.cloned.1.call-done.x_ref.xa_ref = bf16[512,1536]{1,0:T(8,128)(2,1)} async-done(((bf16[128,1536]{1,0:T(8,128)(2,1)}), bf16[512,1536]{1,0:T(8,128)(2,1)}) %all-gather.4.cloned.1.call-update) | async-done | bytes 1572880 | tf_op jit(solution)/shard_map/all_gather | solution.py:705
  91.4 6.5 %attention.1 = (bf16[512,768]{1,0:T(8,128)(2,1)S(1)}, bf16[512,768]{1,0:T(8,128)(2,1)S(1)}) custom-call(bf16[512,640]{1,0:T(8,128)(2,1)S(1)} %get-tuple-element.97.qa_ref, bf16[512,640]{1,0:T(8,128)(2,1)S(1)} %collective-permute-done.13.qb_ref, bf16[512,256]{1,0:T(8,128)(2,1)S(1)} %copy-done.27, bf16[512,256]{1,0:T(8,128)(2,1)S(1)} %copy-done.25, ...), custom_call_target="tpu_custom_call" | custom-call | flops 1000 | bytes 1000 | tf_op jit(solution)/shard_map/attention/pallas_call | solution.py:407
  100.3 3.2 %d_term.1 = bf16[512,1536]{1,0:T(8,128)(2,1)} custom-call(s32[1]{0:T(128)} %constant.45.clone.1.head_ref, bf16[512,768]{1,0:T(8,128)(2,1)S(1)} %collective-permute-done.15.b_ref.x_ref, bf16[1,576,1536]{2,1,0:T(8,128)(2,1)S(1)} %bitcast.58, f32[512,1536]{1,0:T(8,128)S(1)} %d_term_own.1.rest_0_), custom_call_target="tpu_custom_call" | custom-call | flops 1000 | bytes 1000 | tf_op jit(solution)/shard_map/d_term/pallas_call | solution.py:467
  103.6 2.8 %head_term.1.rest_0_ = bf16[512,1536]{1,0:T(8,128)(2,1)} custom-call(s32[1]{0:T(128)} %bitcast.1.head_ref, bf16[512,768]{1,0:T(8,128)(2,1)S(1)} %get-tuple-element.105.a_ref.x_ref.ra_ref, bf16[512,768]{1,0:T(8,128)(2,1)S(1)} %collective-permute-done.15.b_ref.x_ref, bf16[2,192,1536]{2,1,0:T(8,128)(2,1)S(1)} %bitcast.54), custom_call_target="tpu_custom_call" | custom-call | flops 1000 | bytes 1000 | tf_op jit(solution)/shard_map/head_term/pallas_call | solution.py:434
  106.4 8.9 %weight_gradients.1 = (bf16[2,384,384]{2,1,0:T(8,128)(2,1)}, bf16[2,384,384]{2,1,0:T(8,128)(2,1)}, bf16[2,384,384]{2,1,0:T(8,128)(2,1)}, bf16[2,384,384]{2,1,0:T(8,128)(2,1)}) custom-call(s32[1]{0:T(128)} %bitcast.at_ref, bf16[512,1536]{1,0:T(8,128)(2,1)} %all-gather.4.cloned.1.call-done.x_ref.xa_ref, bf16[512,1536]{1,0:T(8,128)(2,1)} %copy-done.6, ...), custom_call_target="tpu_custom_call" | custom-call | flops 1000 | bytes 1000 | tf_op jit(solution)/shard_map/weight_gradients/pallas_call | solution.py:520
  117.2 13.8 %collective-permute-done.16.got_a = bf16[2,384,384]{2,1,0:T(8,128)(2,1)S(1)} collective-permute-done((bf16[2,384,384]{2,1,0:T(8,128)(2,1)}, bf16[2,384,384]{2,1,0:T(8,128)(2,1)S(1)}, u32[]{:S(2)}, u32[]{:S(2)}) %collective-permute-start.16) | collective-permute-done | bytes 589856 | tf_op jit(solution)/shard_map/ppermute | solution.py:661
  133.6 4.4 %reduce-scatter.5.cloned.1.call-done = bf16[1,4,32,1536]{3,2,1,0:T(8,128)(2,1)} async-done(((bf16[4,4,32,1536]{3,2,1,0:T(8,128)(2,1)}), bf16[1,4,32,1536]{3,2,1,0:T(8,128)(2,1)}) %reduce-scatter.5.cloned.1.call-update) | async-done | bytes 393232 | tf_op jit(solution)/shard_map/reduce_scatter | solution.py:738
  143.4 3.4 %collective-permute-done.18.near_ref = bf16[2,32,1536]{2,1,0:T(8,128)(2,1)S(1)} collective-permute-done((bf16[2,32,1536]{2,1,0:T(8,128)(2,1)S(1)}, bf16[2,32,1536]{2,1,0:T(8,128)(2,1)S(1)}, u32[]{:S(2)}, u32[]{:S(2)}) %collective-permute-start.18) | collective-permute-done | bytes 196640 | tf_op jit(solution)/shard_map/ppermute | solution.py:661
  148.6 3.3 %collective-permute-done.21.last_b = bf16[384,384]{1,0:T(8,128)(2,1)S(1)} collective-permute-done((bf16[384,384]{1,0:T(8,128)(2,1)S(1)}, bf16[384,384]{1,0:T(8,128)(2,1)S(1)}, u32[]{:S(2)}, u32[]{:S(2)}) %collective-permute-start.21) | collective-permute-done | bytes 294944 | tf_op jit(solution)/shard_map/ppermute | solution.py:661
  157.8 3.7 %collective-permute-start.23 = (bf16[2,4,1,1536]{3,2,1,0:T(2,128)(2,1)S(1)}, bf16[2,4,1,1536]{3,2,1,0:T(2,128)(2,1)S(1)}, u32[]{:S(2)}, u32[]{:S(2)}) collective-permute-start(bf16[2,4,1,1536]{3,2,1,0:T(2,128)(2,1)S(1)} %get-tuple-element.123.refs_1_), channel_id=1, source_target_pairs={{1,0},{2,1},{3,2},{4,3},{5,4},{6,5},{7,6},{8,7},{9,8},{10,9},{11,1... | collective-permute-start | bytes 73736 | tf_op jit(solution)/shard_map/ppermute | solution.py:652
  161.6 4.4 %copy-done = bf16[5,768,1536]{2,1,0:T(8,128)(2,1)S(1)} copy-done((bf16[5,768,1536]{2,1,0:T(8,128)(2,1)S(1)}, bf16[5,768,1536]{2,1,0:T(8,128)(2,1)}, u32[]{:S(2)}) %copy-start) | copy-done | bytes 11796504
  166.3 4.9 %collective-permute-start.25 = (bf16[384,768]{1,0:T(8,128)(2,1)S(1)}, bf16[384,768]{1,0:T(8,128)(2,1)S(1)}, u32[]{:S(2)}, u32[]{:S(2)}) collective-permute-start(bf16[384,768]{1,0:T(8,128)(2,1)S(1)} %constant_dynamic-update-slice_fusion.1.refs_0_), channel_id=1, source_target_pairs={{0,4},{4,0},{8,12},{12,8},{16,20},{20,16},{24,28},{28,24},{1,5},{5... | collective-permute-start | bytes 1769480 | tf_op jit(solution)/shard_map/ppermute | solution.py:671
  173.7 4.3 %encoder_backward.1.refs_4_ = bf16[256,768]{1,0:T(8,128)(2,1)S(1)} custom-call(bf16[2,4,32,1536]{3,2,1,0:T(8,128)(2,1)S(1)} %get-tuple-element.121.d_ref, bf16[2,4,1,1536]{3,2,1,0:T(2,128)(2,1)S(1)} %collective-permute-done.22.low_ref, bf16[2,4,1,1536]{3,2,1,0:T(2,128)(2,1)S(1)} %collective-permute-done.23.high_ref, bf16[5,768,1536]{2,1,0:T(8,128)(2,1)S(1)} %copy-done, ...), custom_call_target="tpu_custom_call" | custom-call | flops 1000 | bytes 1000 | tf_op jit(solution)/shard_map/encoder_backward/pallas_call | solution.py:244
  178.0 3.4 %weight_outputs_near.1 = (f32[3,1536,384]{2,1,0:T(8,128)}, f32[2,2,96,1536]{3,2,1,0:T(8,128)}, f32[8,128]{1,0:T(8,128)S(1)}) custom-call(s32[2]{0:T(128)S(1)} %copy-done.29, bf16[384,768]{1,0:T(8,128)(2,1)S(1)} %constant_dynamic-update-slice_fusion.1.refs_0_, bf16[384,768]{1,0:T(8,128)(2,1)S(1)} %constant_dynamic-update-slice_fusion.3.refs_1_, ...), custom_call_target="tpu_custom_call" | custom-call | flops 1000 | bytes 1000 | tf_op jit(solution)/shard_map/weight_outputs_near/pallas_call | solution.py:621
  183.8 2.3 %collective-permute-start.28 = (bf16[32,1536]{1,0:T(8,128)(2,1)S(1)}, bf16[32,1536]{1,0:T(8,128)(2,1)S(1)}, u32[]{:S(2)}, u32[]{:S(2)}) collective-permute-start(bf16[32,1536]{1,0:T(8,128)(2,1)S(1)} %get-tuple-element.156), channel_id=1, source_target_pairs={{0,8},{4,12},{8,0},{12,4},{16,24},{20,28},{24,16},{28,20},{1,9},{5... | collective-permute-start | bytes 294920 | tf_op jit(solution)/shard_map/ppermute | solution.py:661
  189.2 2.1 %collective-permute-done.29.refs_2_ = bf16[32,1536]{1,0:T(8,128)(2,1)S(1)} collective-permute-done((bf16[32,1536]{1,0:T(8,128)(2,1)S(1)}, bf16[32,1536]{1,0:T(8,128)(2,1)S(1)}, u32[]{:S(2)}, u32[]{:S(2)}) %collective-permute-start.29) | collective-permute-done | bytes 98336 | tf_op jit(solution)/shard_map/ppermute | solution.py:661
  194.6 4.3 %weight_outputs_far.1 = (f32[3,1536,384]{2,1,0:T(8,128)}, f32[2,2,96,1536]{3,2,1,0:T(8,128)}, f32[8,128]{1,0:T(8,128)}) custom-call(s32[2]{0:T(128)S(1)} %copy-done.29, bf16[384,768]{1,0:T(8,128)(2,1)} %collective-permute-done.31.refs_0_, bf16[384,768]{1,0:T(8,128)(2,1)S(1)} %collective-permute-done.32.refs_1_, ...), custom_call_target="tpu_custom_call", output_to_operand_aliasing={{0}: (5, {}), {1}: (6, {})} | custom-call | flops 1000 | bytes 1000 | tf_op jit(solution)/shard_map/weight_outputs_far/pallas_call | solution.py:621
  (173 shorter events, 67.0 us)
Async XLA Ops:
  7.2 41.1 %all-gather.6.cloned.1.call-start = ((), (), s32[]{:S(2)}) async-start(), calls=%async_computation.5 | async-start | bytes 1474560 | tf_op jit(solution)/shard_map/all_gather | solution.py:695
  9.0 75.0 %all-gather.4.cloned.1.call-start = ((), (), s32[]{:S(2)}) async-start(), calls=%async_computation.2 | async-start | bytes 1966080 | tf_op jit(solution)/shard_map/all_gather | solution.py:705
  10.2 8.7 %collective-permute-start.1 = (bf16[2,4,1,768]{3,2,1,0:T(2,128)(2,1)S(1)}, bf16[2,4,1,768]{3,2,1,0:T(2,128)(2,1)S(1)}, u32[]{:S(2)}, u32[]{:S(2)}) collective-permute-start(bf16[2,4,1,768]{3,2,1,0:T(2,128)(2,1)S(1)} %get-tuple-element.158), channel_id=1, source_target_pairs={{1,0},{2,1},{3,2},{4,3},{5,4},{6,5},{7,6},{8,7},{9,8},{10,9},{11,1... | collective-permute-start | bytes 36872 | tf_op jit(solution)/shard_map/ppermute | solution.py:652
  30.2 9.1 %collective-permute-start.2 = (bf16[32,1536]{1,0:T(8,128)(2,1)}, bf16[32,1536]{1,0:T(8,128)(2,1)S(1)}, u32[]{:S(2)}, u32[]{:S(2)}) collective-permute-start(bf16[32,1536]{1,0:T(8,128)(2,1)} %get-tuple-element.72), channel_id=1, source_target_pairs={{0,16},{4,20},{8,24},{12,28},{16,0},{20,4},{24,8},{28,12},{1,17},{... | collective-permute-start | bytes 294920 | tf_op jit(solution)/shard_map/ppermute | solution.py:661
  31.8 8.2 %collective-permute-start.3 = (bf16[32,1536]{1,0:T(8,128)(2,1)}, bf16[32,1536]{1,0:T(8,128)(2,1)S(1)}, u32[]{:S(2)}, u32[]{:S(2)}) collective-permute-start(bf16[32,1536]{1,0:T(8,128)(2,1)} %get-tuple-element.73), channel_id=1, source_target_pairs={{0,8},{4,12},{8,0},{12,4},{16,24},{20,28},{24,16},{28,20},{1,9},{5... | collective-permute-start | bytes 294920 | tf_op jit(solution)/shard_map/ppermute | solution.py:661
  34.7 8.3 %collective-permute-start.7 = (bf16[32,4,384]{2,1,0:T(4,128)(2,1)S(1)}, bf16[32,4,384]{2,1,0:T(4,128)(2,1)S(1)}, u32[]{:S(2)}, u32[]{:S(2)}) collective-permute-start(bf16[32,4,384]{2,1,0:T(4,128)(2,1)S(1)} %slice.35.refs_0_), channel_id=1, source_target_pairs={{0,3},{1,2},{2,1},{3,0},{4,7},{5,6},{6,5},{7,4},{8,11},{9,10},{10,... | collective-permute-start | bytes 294920 | tf_op jit(solution)/shard_map/ppermute | solution.py:666
  39.3 8.5 %collective-permute-start.6 = (bf16[32,4,384]{2,1,0:T(4,128)(2,1)S(1)}, bf16[32,4,384]{2,1,0:T(4,128)(2,1)S(1)}, u32[]{:S(2)}, u32[]{:S(2)}) collective-permute-start(bf16[32,4,384]{2,1,0:T(4,128)(2,1)S(1)} %slice.35.refs_0_), channel_id=1, source_target_pairs={{0,2},{1,3},{2,0},{3,1},{4,6},{5,7},{6,4},{7,5},{8,10},{9,11},{10,... | collective-permute-start | bytes 294920 | tf_op jit(solution)/shard_map/ppermute | solution.py:666
  39.3 8.5 %collective-permute-start.5 = (bf16[32,4,384]{2,1,0:T(4,128)(2,1)S(1)}, bf16[32,4,384]{2,1,0:T(4,128)(2,1)S(1)}, u32[]{:S(2)}, u32[]{:S(2)}) collective-permute-start(bf16[32,4,384]{2,1,0:T(4,128)(2,1)S(1)} %slice.35.refs_0_), channel_id=1, source_target_pairs={{0,1},{1,0},{2,3},{3,2},{4,5},{5,4},{6,7},{7,6},{8,9},{9,8},{10,11... | collective-permute-start | bytes 294920 | tf_op jit(solution)/shard_map/ppermute | solution.py:666
  47.8 90.2 %reduce-scatter.5.cloned.1.call-start = ((), (), s32[]{:S(2)}) async-start(), calls=%async_computation.4 | async-start | bytes 1966080 | tf_op jit(solution)/shard_map/reduce_scatter | solution.py:738
  50.1 13.8 %collective-permute-start.10 = (bf16[4,32,1536]{2,1,0:T(8,128)(2,1)S(1)}, bf16[4,32,1536]{2,1,0:T(8,128)(2,1)S(1)}, u32[]{:S(2)}, u32[]{:S(2)}) collective-permute-start(bf16[4,32,1536]{2,1,0:T(8,128)(2,1)S(1)} %get-tuple-element.150), channel_id=1, source_target_pairs={{0,24},{4,28},{8,16},{12,20},{16,8},{20,12},{24,0},{28,4},{1,25},{... | collective-permute-start | bytes 1179656 | tf_op jit(solution)/shard_map/ppermute | solution.py:661
  51.6 18.7 %collective-permute-start.9 = (bf16[4,32,1536]{2,1,0:T(8,128)(2,1)S(1)}, bf16[4,32,1536]{2,1,0:T(8,128)(2,1)S(1)}, u32[]{:S(2)}, u32[]{:S(2)}) collective-permute-start(bf16[4,32,1536]{2,1,0:T(8,128)(2,1)S(1)} %get-tuple-element.151), channel_id=1, source_target_pairs={{0,16},{4,20},{8,24},{12,28},{16,0},{20,4},{24,8},{28,12},{1,17},{... | collective-permute-start | bytes 1179656 | tf_op jit(solution)/shard_map/ppermute | solution.py:661
  51.9 18.4 %collective-permute-start.8 = (bf16[4,32,1536]{2,1,0:T(8,128)(2,1)S(1)}, bf16[4,32,1536]{2,1,0:T(8,128)(2,1)S(1)}, u32[]{:S(2)}, u32[]{:S(2)}) collective-permute-start(bf16[4,32,1536]{2,1,0:T(8,128)(2,1)S(1)} %get-tuple-element.152), channel_id=1, source_target_pairs={{0,8},{4,12},{8,0},{12,4},{16,24},{20,28},{24,16},{28,20},{1,9},{5... | collective-permute-start | bytes 1179656 | tf_op jit(solution)/shard_map/ppermute | solution.py:661
  70.7 13.3 %collective-permute-start.12 = (bf16[512,1536]{1,0:T(8,128)(2,1)S(1)}, bf16[512,1536]{1,0:T(8,128)(2,1)}, u32[]{:S(2)}, u32[]{:S(2)}) collective-permute-start(bf16[512,1536]{1,0:T(8,128)(2,1)S(1)} %bitcast.48), channel_id=1, source_target_pairs={{0,4},{4,0},{8,12},{12,8},{16,20},{20,16},{24,28},{28,24},{1,5},{5... | collective-permute-start | bytes 4718600 | tf_op jit(solution)/shard_map/ppermute | solution.py:671
  103.5 77.9 %reduce-scatter.3.cloned.1.call-start = ((), (), s32[]{:S(2)}) async-start(), calls=%async_computation.3 | async-start | bytes 1966080 | tf_op jit(solution)/shard_map/reduce_scatter | solution.py:753
  115.2 15.8 %collective-permute-start.16 = (bf16[2,384,384]{2,1,0:T(8,128)(2,1)}, bf16[2,384,384]{2,1,0:T(8,128)(2,1)S(1)}, u32[]{:S(2)}, u32[]{:S(2)}) collective-permute-start(bf16[2,384,384]{2,1,0:T(8,128)(2,1)} %get-tuple-element.111), channel_id=1, source_target_pairs={{0,8},{4,12},{8,0},{12,4},{16,24},{20,28},{24,16},{28,20},{1,9},{5... | collective-permute-start | bytes 1769480 | tf_op jit(solution)/shard_map/ppermute | solution.py:661
  115.8 15.5 %collective-permute-start.17 = (bf16[2,384,384]{2,1,0:T(8,128)(2,1)}, bf16[2,384,384]{2,1,0:T(8,128)(2,1)S(1)}, u32[]{:S(2)}, u32[]{:S(2)}) collective-permute-start(bf16[2,384,384]{2,1,0:T(8,128)(2,1)} %get-tuple-element.113), channel_id=1, source_target_pairs={{0,16},{4,20},{8,24},{12,28},{16,0},{20,4},{24,8},{28,12},{1,17},{... | collective-permute-start | bytes 1769480 | tf_op jit(solution)/shard_map/ppermute | solution.py:661
  139.5 9.0 %collective-permute-start.20 = (bf16[384,384]{1,0:T(8,128)(2,1)S(1)}, bf16[384,384]{1,0:T(8,128)(2,1)S(1)}, u32[]{:S(2)}, u32[]{:S(2)}) collective-permute-start(bf16[384,384]{1,0:T(8,128)(2,1)S(1)} %get-tuple-element.114), channel_id=1, source_target_pairs={{0,16},{4,20},{8,24},{12,28},{16,0},{20,4},{24,8},{28,12},{1,17},{... | collective-permute-start | bytes 884744 | tf_op jit(solution)/shard_map/ppermute | solution.py:661
  141.0 10.9 %collective-permute-start.21 = (bf16[384,384]{1,0:T(8,128)(2,1)S(1)}, bf16[384,384]{1,0:T(8,128)(2,1)S(1)}, u32[]{:S(2)}, u32[]{:S(2)}) collective-permute-start(bf16[384,384]{1,0:T(8,128)(2,1)S(1)} %get-tuple-element.115), channel_id=1, source_target_pairs={{0,8},{4,12},{8,0},{12,4},{16,24},{20,28},{24,16},{28,20},{1,9},{5... | collective-permute-start | bytes 884744 | tf_op jit(solution)/shard_map/ppermute | solution.py:661
  152.2 14.0 %collective-permute-start.26 = (bf16[192,768]{1,0:T(8,128)(2,1)S(1)}, bf16[192,768]{1,0:T(8,128)(2,1)S(1)}, u32[]{:S(2)}, u32[]{:S(2)}) collective-permute-start(bf16[192,768]{1,0:T(8,128)(2,1)S(1)} %get-tuple-element.128), channel_id=1, source_target_pairs={{0,16},{4,20},{8,24},{12,28},{16,0},{20,4},{24,8},{28,12},{1,17},{... | collective-permute-start | bytes 884744 | tf_op jit(solution)/shard_map/ppermute | solution.py:661
  153.8 12.5 %collective-permute-start.24 = (bf16[192,768]{1,0:T(8,128)(2,1)S(1)}, bf16[192,768]{1,0:T(8,128)(2,1)S(1)}, u32[]{:S(2)}, u32[]{:S(2)}) collective-permute-start(bf16[192,768]{1,0:T(8,128)(2,1)S(1)} %get-tuple-element.120.refs_4_), channel_id=1, source_target_pairs={{0,8},{4,12},{8,0},{12,4},{16,24},{20,28},{24,16},{28,20},{1,9},{5... | collective-permute-start | bytes 884744 | tf_op jit(solution)/shard_map/ppermute | solution.py:661
  155.7 10.3 %collective-permute-start.22 = (bf16[2,4,1,1536]{3,2,1,0:T(2,128)(2,1)S(1)}, bf16[2,4,1,1536]{3,2,1,0:T(2,128)(2,1)S(1)}, u32[]{:S(2)}, u32[]{:S(2)}) collective-permute-start(bf16[2,4,1,1536]{3,2,1,0:T(2,128)(2,1)S(1)} %get-tuple-element.122), channel_id=1, source_target_pairs={{0,1},{1,2},{2,3},{3,4},{4,5},{5,6},{6,7},{7,8},{8,9},{9,10},{10,1... | collective-permute-start | bytes 73736 | tf_op jit(solution)/shard_map/ppermute | solution.py:652
  157.8 8.5 %collective-permute-start.23 = (bf16[2,4,1,1536]{3,2,1,0:T(2,128)(2,1)S(1)}, bf16[2,4,1,1536]{3,2,1,0:T(2,128)(2,1)S(1)}, u32[]{:S(2)}, u32[]{:S(2)}) collective-permute-start(bf16[2,4,1,1536]{3,2,1,0:T(2,128)(2,1)S(1)} %get-tuple-element.123.refs_1_), channel_id=1, source_target_pairs={{1,0},{2,1},{3,2},{4,3},{5,4},{6,5},{7,6},{8,7},{9,8},{10,9},{11,1... | collective-permute-start | bytes 73736 | tf_op jit(solution)/shard_map/ppermute | solution.py:652
  171.3 16.2 %collective-permute-start.32 = (bf16[384,768]{1,0:T(8,128)(2,1)S(1)}, bf16[384,768]{1,0:T(8,128)(2,1)S(1)}, u32[]{:S(2)}, u32[]{:S(2)}) collective-permute-start(bf16[384,768]{1,0:T(8,128)(2,1)S(1)} %constant_dynamic-update-slice_fusion.3.refs_1_), channel_id=1, source_target_pairs={{0,8},{4,12},{8,0},{12,4},{16,24},{20,28},{24,16},{28,20},{1,9},{5... | collective-permute-start | bytes 1769480 | tf_op jit(solution)/shard_map/ppermute | solution.py:661
  171.4 19.9 %collective-permute-start.31 = (bf16[384,768]{1,0:T(8,128)(2,1)S(1)}, bf16[384,768]{1,0:T(8,128)(2,1)}, u32[]{:S(2)}, u32[]{:S(2)}) collective-permute-start(bf16[384,768]{1,0:T(8,128)(2,1)S(1)} %constant_dynamic-update-slice_fusion.1.refs_0_), channel_id=1, source_target_pairs={{0,16},{4,20},{8,24},{12,28},{16,0},{20,4},{24,8},{28,12},{1,17},{... | collective-permute-start | bytes 1769480 | tf_op jit(solution)/shard_map/ppermute | solution.py:661
  (50 other events, 242.4 us)
Sparse Core Ops, SparseCore 0:
  10.2 35.7 all-gather.5
  48.1 35.9 all-gather.3
  103.6 34.2 reduce-scatter.4
  140.1 36.3 reduce-scatter.2

commit v21 on v20

--- a/solution.py
+++ b/solution.py
@@ -701,7 +701,6 @@
     skip, slope, normed = encoder(at, pairs, low, high, conv_weight, norm_gain)
     normed = to_chips(normed)
     normed_slab = jnp.concatenate([normed[j] for j in order], axis=0)
-    normed_slab, *parts = lax.optimization_barrier((normed_slab, *parts))
     normed_rows = lax.all_gather(normed_slab, "head", axis=0, tiled=True)
 
     grad_z = after(grad_z, normed_slab)

time: 208 us -> 207 us (level)
    ppermute x3, waiting for transfers between devices: 6.15 us -> 0.01 us  [trade_z(): return lax.ppermute(x, 'head', [(z, z ^ bit) for z in range(count)])]
    ppermute x19, waiting for transfers between devices: 32.6 us -> 36.1 us  [trade_chip(): return lax.ppermute(x, 'seq', [(s, s ^ bit * heads) for s in range(count)])]
    unnamed x74 -> x79, local copies, waits for them, and re-layouts: 18.6 us -> 19.8 us
where the time goes in v21:
time: 207 us; the launch traced here: 204 us
  Pallas kernels  59.4 us (29%)
  waiting for transfers between devices  54.5 us (26%)
  starting transfers between devices  44.6 us (22%)
  local copies, waits for them, and re-layouts  30 us (14%)
  between operations  14.3 us (7%)
    ppermute x19, waiting for transfers between devices, trade_chip(): return lax.ppermute(x, 'seq', [(s, s ^ bit * heads) for s in range(count)])  36.1 us
    ppermute x19, starting transfers between devices, trade_chip(): return lax.ppermute(x, 'seq', [(s, s ^ bit * heads) for s in range(count)])  20.2 us
    unnamed x79, local copies, waits for them, and re-layouts  19.8 us
    all_gather x1, waiting for transfers between devices, unit_body(): normed_rows = lax.all_gather(normed_slab, 'head', axis=0, tiled=True)  10.6 us
    pallas_call x1, Pallas kernels, encoder(): pl.pallas_call(conv_kernel, grid=(width // tile,), in_specs=[SCALARS, who...  10.2 us
    pallas_call x1, Pallas kernels, weight_gradients(): pl.pallas_call(weight_kernel, grid_spec=pltpu.PrefetchScalarGridSpec(num_...  8.86 us
    pallas_call x2, Pallas kernels, unpack_weights(): pl.pallas_call(unpack_kernel, grid_spec=pltpu.PrefetchScalarGridSpec(num_...  7.76 us
    ppermute x2, starting transfers between devices, neighbour_edges(): lax.ppermute(last, axes, forward)  7.59 us
  transfers between devices with their start and end apart: 39, of which 20 were waited for; matrix products, arithmetic and copies ran while one was open for 6% of the time, Pallas kernels for 22%

profile of v21, /device:TPU:26, one launch (start us, length us, event | category | flops | bytes accessed | tf_op | source)
XLA Modules:
  0.0 203.7 jit_solution(11662025601000392821)
XLA Ops:
  12.0 2.5 %collective-permute-start.5 = (bf16[32,4,384]{2,1,0:T(4,128)(2,1)S(1)}, bf16[32,4,384]{2,1,0:T(4,128)(2,1)S(1)}, u32[]{:S(2)}, u32[]{:S(2)}) collective-permute-start(bf16[32,4,384]{2,1,0:T(4,128)(2,1)S(1)} %slice.36.refs_0_), channel_id=1, source_target_pairs={{0,1},{1,0},{2,3},{3,2},{4,5},{5,4},{6,7},{7,6},{8,9},{9,8},{10,11... | collective-permute-start | bytes 294920 | tf_op jit(solution)/shard_map/ppermute | solution.py:666
  17.5 5.4 %collective-permute-start = (bf16[2,4,1,768]{3,2,1,0:T(2,128)(2,1)S(1)}, bf16[2,4,1,768]{3,2,1,0:T(2,128)(2,1)S(1)}, u32[]{:S(2)}, u32[]{:S(2)}) collective-permute-start(bf16[2,4,1,768]{3,2,1,0:T(2,128)(2,1)S(1)} %get-tuple-element.151), channel_id=1, source_target_pairs={{0,1},{1,2},{2,3},{3,4},{4,5},{5,6},{6,7},{7,8},{8,9},{9,10},{10,1... | collective-permute-start | bytes 36872 | tf_op jit(solution)/shard_map/ppermute | solution.py:652
  25.6 10.2 %encoder_forward.1 = (bf16[4,32,1536]{2,1,0:T(8,128)(2,1)}, f32[2,4,32,1536]{3,2,1,0:T(8,128)}, bf16[32,1536]{1,0:T(8,128)(2,1)}, bf16[32,1536]{1,0:T(8,128)(2,1...) custom-call(s32[2]{0:T(128)} %pad_add_fusion.at_ref, bf16[2,4,32,768]{3,2,1,0:T(8,128)(2,1)} %bitcast.68, ...), custom_call_target="tpu_custom_call" | custom-call | flops 1000 | bytes 1000 | tf_op jit(solution)/shard_map/encoder_forward/pallas_call | solution.py:111
  50.8 6.4 %pack_weights.1 = (bf16[1536,576]{1,0:T(8,128)(2,1)S(1)}, bf16[1536,576]{1,0:T(8,128)(2,1)S(1)}, bf16[576,1536]{1,0:T(8,128)(2,1)S(1)}, bf16[576,1536]{1,0:T(8,128)(2,1)S(1)}, f32[8,128]{1,0:T(8,128)S(1)}) custom-call(s32[2]{0:T(128)S(1)} %copy-done.29, bf16[3,1536,384]{2,1,0:T(8,128)(2,1)S(1)} %copy-done.7), custom_call_target="tpu_custom_call" | custom-call | flops 1000 | bytes 1000 | tf_op jit(solution)/shard_map/pack_weights/pallas_call | solution.py:285
  61.1 5.9 %collective-permute-done.9 = bf16[4,32,1536]{2,1,0:T(8,128)(2,1)S(1)} collective-permute-done((bf16[4,32,1536]{2,1,0:T(8,128)(2,1)S(1)}, bf16[4,32,1536]{2,1,0:T(8,128)(2,1)S(1)}, u32[]{:S(2)}, u32[]{:S(2)}) %collective-permute-start.9) | collective-permute-done | bytes 393248 | tf_op jit(solution)/shard_map/ppermute | solution.py:661
  71.9 10.6 %all-gather.4.cloned.1.call-done.x_ref.xa_ref = bf16[512,1536]{1,0:T(8,128)(2,1)} async-done(((bf16[128,1536]{1,0:T(8,128)(2,1)}), bf16[512,1536]{1,0:T(8,128)(2,1)}) %all-gather.4.cloned.1.call-update) | async-done | bytes 1572880 | tf_op jit(solution)/shard_map/all_gather | solution.py:704
  89.8 6.5 %attention.1 = (bf16[512,768]{1,0:T(8,128)(2,1)S(1)}, bf16[512,768]{1,0:T(8,128)(2,1)S(1)}) custom-call(bf16[512,640]{1,0:T(8,128)(2,1)S(1)} %get-tuple-element.89.qa_ref, bf16[512,640]{1,0:T(8,128)(2,1)S(1)} %collective-permute-done.13.qb_ref, bf16[512,256]{1,0:T(8,128)(2,1)S(1)} %copy-done.27, bf16[512,256]{1,0:T(8,128)(2,1)S(1)} %copy-done.25, ...), custom_call_target="tpu_custom_call" | custom-call | flops 1000 | bytes 1000 | tf_op jit(solution)/shard_map/attention/pallas_call | solution.py:407
  96.6 2.1 %d_term_own.1.rest_0_ = f32[512,1536]{1,0:T(8,128)S(1)} custom-call(s32[1]{0:T(128)} %constant.45.clone.1.head_ref, bf16[512,768]{1,0:T(8,128)(2,1)S(1)} %get-tuple-element.97.a_ref.x_ref.ra_ref, bf16[1,576,1536]{2,1,0:T(8,128)(2,1)S(1)} %bitcast.59), custom_call_target="tpu_custom_call" | custom-call | flops 1000 | bytes 1000 | tf_op jit(solution)/shard_map/d_term_own/pallas_call | solution.py:467
  98.7 3.0 %d_term.1 = bf16[512,1536]{1,0:T(8,128)(2,1)} custom-call(s32[1]{0:T(128)} %constant.45.clone.1.head_ref, bf16[512,768]{1,0:T(8,128)(2,1)S(1)} %collective-permute-done.15.b_ref.x_ref, bf16[1,576,1536]{2,1,0:T(8,128)(2,1)S(1)} %bitcast.58, f32[512,1536]{1,0:T(8,128)S(1)} %d_term_own.1.rest_0_), custom_call_target="tpu_custom_call" | custom-call | flops 1000 | bytes 1000 | tf_op jit(solution)/shard_map/d_term/pallas_call | solution.py:467
  101.8 3.0 %head_term.1.rest_0_ = bf16[512,1536]{1,0:T(8,128)(2,1)} custom-call(s32[1]{0:T(128)} %bitcast.1.head_ref, bf16[512,768]{1,0:T(8,128)(2,1)S(1)} %get-tuple-element.97.a_ref.x_ref.ra_ref, bf16[512,768]{1,0:T(8,128)(2,1)S(1)} %collective-permute-done.15.b_ref.x_ref, bf16[2,192,1536]{2,1,0:T(8,128)(2,1)S(1)} %bitcast.54), custom_call_target="tpu_custom_call" | custom-call | flops 1000 | bytes 1000 | tf_op jit(solution)/shard_map/head_term/pallas_call | solution.py:434
  104.8 8.9 %weight_gradients.1 = (bf16[2,384,384]{2,1,0:T(8,128)(2,1)}, bf16[2,384,384]{2,1,0:T(8,128)(2,1)}, bf16[2,384,384]{2,1,0:T(8,128)(2,1)}, bf16[2,384,384]{2,1,0:T(8,128)(2,1)}) custom-call(s32[1]{0:T(128)} %bitcast.at_ref, bf16[512,1536]{1,0:T(8,128)(2,1)} %all-gather.4.cloned.1.call-done.x_ref.xa_ref, bf16[512,1536]{1,0:T(8,128)(2,1)} %copy-done.6, ...), custom_call_target="tpu_custom_call" | custom-call | flops 1000 | bytes 1000 | tf_op jit(solution)/shard_map/weight_gradients/pallas_call | solution.py:520
  115.7 13.7 %collective-permute-done.16.got_a = bf16[2,384,384]{2,1,0:T(8,128)(2,1)S(1)} collective-permute-done((bf16[2,384,384]{2,1,0:T(8,128)(2,1)}, bf16[2,384,384]{2,1,0:T(8,128)(2,1)S(1)}, u32[]{:S(2)}, u32[]{:S(2)}) %collective-permute-start.16) | collective-permute-done | bytes 589856 | tf_op jit(solution)/shard_map/ppermute | solution.py:661
  132.0 4.2 %reduce-scatter.5.cloned.1.call-done = bf16[1,4,32,1536]{3,2,1,0:T(8,128)(2,1)} async-done(((bf16[4,4,32,1536]{3,2,1,0:T(8,128)(2,1)}), bf16[1,4,32,1536]{3,2,1,0:T(8,128)(2,1)}) %reduce-scatter.5.cloned.1.call-update) | async-done | bytes 393232 | tf_op jit(solution)/shard_map/reduce_scatter | solution.py:737
  141.6 3.4 %collective-permute-done.18.near_ref = bf16[2,32,1536]{2,1,0:T(8,128)(2,1)S(1)} collective-permute-done((bf16[2,32,1536]{2,1,0:T(8,128)(2,1)S(1)}, bf16[2,32,1536]{2,1,0:T(8,128)(2,1)S(1)}, u32[]{:S(2)}, u32[]{:S(2)}) %collective-permute-start.18) | collective-permute-done | bytes 196640 | tf_op jit(solution)/shard_map/ppermute | solution.py:661
  146.8 3.4 %collective-permute-done.21.last_b = bf16[384,384]{1,0:T(8,128)(2,1)S(1)} collective-permute-done((bf16[384,384]{1,0:T(8,128)(2,1)S(1)}, bf16[384,384]{1,0:T(8,128)(2,1)S(1)}, u32[]{:S(2)}, u32[]{:S(2)}) %collective-permute-start.21) | collective-permute-done | bytes 294944 | tf_op jit(solution)/shard_map/ppermute | solution.py:661
  153.9 2.2 %collective-permute-start.22 = (bf16[2,4,1,1536]{3,2,1,0:T(2,128)(2,1)S(1)}, bf16[2,4,1,1536]{3,2,1,0:T(2,128)(2,1)S(1)}, u32[]{:S(2)}, u32[]{:S(2)}) collective-permute-start(bf16[2,4,1,1536]{3,2,1,0:T(2,128)(2,1)S(1)} %get-tuple-element.114), channel_id=1, source_target_pairs={{0,1},{1,2},{2,3},{3,4},{4,5},{5,6},{6,7},{7,8},{8,9},{9,10},{10,1... | collective-permute-start | bytes 73736 | tf_op jit(solution)/shard_map/ppermute | solution.py:652
  156.1 3.7 %collective-permute-start.23 = (bf16[2,4,1,1536]{3,2,1,0:T(2,128)(2,1)S(1)}, bf16[2,4,1,1536]{3,2,1,0:T(2,128)(2,1)S(1)}, u32[]{:S(2)}, u32[]{:S(2)}) collective-permute-start(bf16[2,4,1,1536]{3,2,1,0:T(2,128)(2,1)S(1)} %get-tuple-element.115.refs_1_), channel_id=1, source_target_pairs={{1,0},{2,1},{3,2},{4,3},{5,4},{6,5},{7,6},{8,7},{9,8},{10,9},{11,1... | collective-permute-start | bytes 73736 | tf_op jit(solution)/shard_map/ppermute | solution.py:652
  159.8 4.4 %copy-done = bf16[5,768,1536]{2,1,0:T(8,128)(2,1)S(1)} copy-done((bf16[5,768,1536]{2,1,0:T(8,128)(2,1)S(1)}, bf16[5,768,1536]{2,1,0:T(8,128)(2,1)}, u32[]{:S(2)}) %copy-start) | copy-done | bytes 11796504
  164.7 4.8 %collective-permute-start.25 = (bf16[384,768]{1,0:T(8,128)(2,1)S(1)}, bf16[384,768]{1,0:T(8,128)(2,1)S(1)}, u32[]{:S(2)}, u32[]{:S(2)}) collective-permute-start(bf16[384,768]{1,0:T(8,128)(2,1)S(1)} %constant_dynamic-update-slice_fusion.5.refs_0_), channel_id=1, source_target_pairs={{0,4},{4,0},{8,12},{12,8},{16,20},{20,16},{24,28},{28,24},{1,5},{5... | collective-permute-start | bytes 1769480 | tf_op jit(solution)/shard_map/ppermute | solution.py:671
  172.0 4.3 %encoder_backward.1.refs_4_ = bf16[256,768]{1,0:T(8,128)(2,1)S(1)} custom-call(bf16[2,4,32,1536]{3,2,1,0:T(8,128)(2,1)S(1)} %get-tuple-element.113.d_ref, bf16[2,4,1,1536]{3,2,1,0:T(2,128)(2,1)S(1)} %collective-permute-done.22.low_ref, bf16[2,4,1,1536]{3,2,1,0:T(2,128)(2,1)S(1)} %collective-permute-done.23.high_ref, bf16[5,768,1536]{2,1,0:T(8,128)(2,1)S(1)} %copy-done, ...), custom_call_target="tpu_custom_call" | custom-call | flops 1000 | bytes 1000 | tf_op jit(solution)/shard_map/encoder_backward/pallas_call | solution.py:244
  176.3 3.4 %weight_outputs_near.1 = (f32[3,1536,384]{2,1,0:T(8,128)}, f32[2,2,96,1536]{3,2,1,0:T(8,128)}, f32[8,128]{1,0:T(8,128)S(1)}) custom-call(s32[2]{0:T(128)S(1)} %copy-done.29, bf16[384,768]{1,0:T(8,128)(2,1)S(1)} %constant_dynamic-update-slice_fusion.5.refs_0_, bf16[384,768]{1,0:T(8,128)(2,1)S(1)} %constant_dynamic-update-slice_fusion.7.refs_1_, ...), custom_call_target="tpu_custom_call" | custom-call | flops 1000 | bytes 1000 | tf_op jit(solution)/shard_map/weight_outputs_near/pallas_call | solution.py:621
  182.1 2.3 %collective-permute-start.28 = (bf16[32,1536]{1,0:T(8,128)(2,1)S(1)}, bf16[32,1536]{1,0:T(8,128)(2,1)S(1)}, u32[]{:S(2)}, u32[]{:S(2)}) collective-permute-start(bf16[32,1536]{1,0:T(8,128)(2,1)S(1)} %get-tuple-element.148), channel_id=1, source_target_pairs={{0,8},{4,12},{8,0},{12,4},{16,24},{20,28},{24,16},{28,20},{1,9},{5... | collective-permute-start | bytes 294920 | tf_op jit(solution)/shard_map/ppermute | solution.py:661
  187.4 2.1 %collective-permute-done.29.refs_2_ = bf16[32,1536]{1,0:T(8,128)(2,1)S(1)} collective-permute-done((bf16[32,1536]{1,0:T(8,128)(2,1)S(1)}, bf16[32,1536]{1,0:T(8,128)(2,1)S(1)}, u32[]{:S(2)}, u32[]{:S(2)}) %collective-permute-start.29) | collective-permute-done | bytes 98336 | tf_op jit(solution)/shard_map/ppermute | solution.py:661
  192.9 4.3 %weight_outputs_far.1 = (f32[3,1536,384]{2,1,0:T(8,128)}, f32[2,2,96,1536]{3,2,1,0:T(8,128)}, f32[8,128]{1,0:T(8,128)}) custom-call(s32[2]{0:T(128)S(1)} %copy-done.29, bf16[384,768]{1,0:T(8,128)(2,1)} %collective-permute-done.31.refs_0_, bf16[384,768]{1,0:T(8,128)(2,1)S(1)} %collective-permute-done.32.refs_1_, ...), custom_call_target="tpu_custom_call", output_to_operand_aliasing={{0}: (5, {}), {1}: (6, {})} | custom-call | flops 1000 | bytes 1000 | tf_op jit(solution)/shard_map/weight_outputs_far/pallas_call | solution.py:621
  (178 shorter events, 68.8 us)
Async XLA Ops:
  7.2 38.3 %all-gather.6.cloned.1.call-start = ((), (), s32[]{:S(2)}) async-start(), calls=%async_computation.5 | async-start | bytes 1474560 | tf_op jit(solution)/shard_map/all_gather | solution.py:695
  9.0 73.5 %all-gather.4.cloned.1.call-start = ((), (), s32[]{:S(2)}) async-start(), calls=%async_computation.2 | async-start | bytes 1966080 | tf_op jit(solution)/shard_map/all_gather | solution.py:704
  10.0 28.5 %collective-permute-start.7 = (bf16[32,4,384]{2,1,0:T(4,128)(2,1)S(1)}, bf16[32,4,384]{2,1,0:T(4,128)(2,1)S(1)}, u32[]{:S(2)}, u32[]{:S(2)}) collective-permute-start(bf16[32,4,384]{2,1,0:T(4,128)(2,1)S(1)} %slice.36.refs_0_), channel_id=1, source_target_pairs={{0,3},{1,2},{2,1},{3,0},{4,7},{5,6},{6,5},{7,4},{8,11},{9,10},{10,... | collective-permute-start | bytes 294920 | tf_op jit(solution)/shard_map/ppermute | solution.py:666
  10.3 30.0 %collective-permute-start.6 = (bf16[32,4,384]{2,1,0:T(4,128)(2,1)S(1)}, bf16[32,4,384]{2,1,0:T(4,128)(2,1)S(1)}, u32[]{:S(2)}, u32[]{:S(2)}) collective-permute-start(bf16[32,4,384]{2,1,0:T(4,128)(2,1)S(1)} %slice.36.refs_0_), channel_id=1, source_target_pairs={{0,2},{1,3},{2,0},{3,1},{4,6},{5,7},{6,4},{7,5},{8,10},{9,11},{10,... | collective-permute-start | bytes 294920 | tf_op jit(solution)/shard_map/ppermute | solution.py:666
  12.0 28.3 %collective-permute-start.5 = (bf16[32,4,384]{2,1,0:T(4,128)(2,1)S(1)}, bf16[32,4,384]{2,1,0:T(4,128)(2,1)S(1)}, u32[]{:S(2)}, u32[]{:S(2)}) collective-permute-start(bf16[32,4,384]{2,1,0:T(4,128)(2,1)S(1)} %slice.36.refs_0_), channel_id=1, source_target_pairs={{0,1},{1,0},{2,3},{3,2},{4,5},{5,4},{6,7},{7,6},{8,9},{9,8},{10,11... | collective-permute-start | bytes 294920 | tf_op jit(solution)/shard_map/ppermute | solution.py:666
  15.6 8.6 %collective-permute-start.1 = (bf16[2,4,1,768]{3,2,1,0:T(2,128)(2,1)S(1)}, bf16[2,4,1,768]{3,2,1,0:T(2,128)(2,1)S(1)}, u32[]{:S(2)}, u32[]{:S(2)}) collective-permute-start(bf16[2,4,1,768]{3,2,1,0:T(2,128)(2,1)S(1)} %get-tuple-element.150), channel_id=1, source_target_pairs={{1,0},{2,1},{3,2},{4,3},{5,4},{6,5},{7,6},{8,7},{9,8},{10,9},{11,1... | collective-permute-start | bytes 36872 | tf_op jit(solution)/shard_map/ppermute | solution.py:652
  45.4 90.8 %reduce-scatter.5.cloned.1.call-start = ((), (), s32[]{:S(2)}) async-start(), calls=%async_computation.4 | async-start | bytes 1966080 | tf_op jit(solution)/shard_map/reduce_scatter | solution.py:737
  47.3 13.8 %collective-permute-start.10 = (bf16[4,32,1536]{2,1,0:T(8,128)(2,1)S(1)}, bf16[4,32,1536]{2,1,0:T(8,128)(2,1)S(1)}, u32[]{:S(2)}, u32[]{:S(2)}) collective-permute-start(bf16[4,32,1536]{2,1,0:T(8,128)(2,1)S(1)} %get-tuple-element.142), channel_id=1, source_target_pairs={{0,24},{4,28},{8,16},{12,20},{16,8},{20,12},{24,0},{28,4},{1,25},{... | collective-permute-start | bytes 1179656 | tf_op jit(solution)/shard_map/ppermute | solution.py:661
  48.9 18.1 %collective-permute-start.9 = (bf16[4,32,1536]{2,1,0:T(8,128)(2,1)S(1)}, bf16[4,32,1536]{2,1,0:T(8,128)(2,1)S(1)}, u32[]{:S(2)}, u32[]{:S(2)}) collective-permute-start(bf16[4,32,1536]{2,1,0:T(8,128)(2,1)S(1)} %get-tuple-element.143), channel_id=1, source_target_pairs={{0,16},{4,20},{8,24},{12,28},{16,0},{20,4},{24,8},{28,12},{1,17},{... | collective-permute-start | bytes 1179656 | tf_op jit(solution)/shard_map/ppermute | solution.py:661
  50.0 16.9 %collective-permute-start.8 = (bf16[4,32,1536]{2,1,0:T(8,128)(2,1)S(1)}, bf16[4,32,1536]{2,1,0:T(8,128)(2,1)S(1)}, u32[]{:S(2)}, u32[]{:S(2)}) collective-permute-start(bf16[4,32,1536]{2,1,0:T(8,128)(2,1)S(1)} %get-tuple-element.144), channel_id=1, source_target_pairs={{0,8},{4,12},{8,0},{12,4},{16,24},{20,28},{24,16},{28,20},{1,9},{5... | collective-permute-start | bytes 1179656 | tf_op jit(solution)/shard_map/ppermute | solution.py:661
  67.3 15.2 %collective-permute-start.12 = (bf16[512,1536]{1,0:T(8,128)(2,1)S(1)}, bf16[512,1536]{1,0:T(8,128)(2,1)}, u32[]{:S(2)}, u32[]{:S(2)}) collective-permute-start(bf16[512,1536]{1,0:T(8,128)(2,1)S(1)} %bitcast.48), channel_id=1, source_target_pairs={{0,4},{4,0},{8,12},{12,8},{16,20},{20,16},{24,28},{28,24},{1,5},{5... | collective-permute-start | bytes 4718600 | tf_op jit(solution)/shard_map/ppermute | solution.py:671
  101.8 78.0 %reduce-scatter.3.cloned.1.call-start = ((), (), s32[]{:S(2)}) async-start(), calls=%async_computation.3 | async-start | bytes 1966080 | tf_op jit(solution)/shard_map/reduce_scatter | solution.py:752
  113.7 15.7 %collective-permute-start.16 = (bf16[2,384,384]{2,1,0:T(8,128)(2,1)}, bf16[2,384,384]{2,1,0:T(8,128)(2,1)S(1)}, u32[]{:S(2)}, u32[]{:S(2)}) collective-permute-start(bf16[2,384,384]{2,1,0:T(8,128)(2,1)} %get-tuple-element.103), channel_id=1, source_target_pairs={{0,8},{4,12},{8,0},{12,4},{16,24},{20,28},{24,16},{28,20},{1,9},{5... | collective-permute-start | bytes 1769480 | tf_op jit(solution)/shard_map/ppermute | solution.py:661
  114.2 15.4 %collective-permute-start.17 = (bf16[2,384,384]{2,1,0:T(8,128)(2,1)}, bf16[2,384,384]{2,1,0:T(8,128)(2,1)S(1)}, u32[]{:S(2)}, u32[]{:S(2)}) collective-permute-start(bf16[2,384,384]{2,1,0:T(8,128)(2,1)} %get-tuple-element.105), channel_id=1, source_target_pairs={{0,16},{4,20},{8,24},{12,28},{16,0},{20,4},{24,8},{28,12},{1,17},{... | collective-permute-start | bytes 1769480 | tf_op jit(solution)/shard_map/ppermute | solution.py:661
  137.2 7.9 %collective-permute-start.18 = (bf16[2,32,1536]{2,1,0:T(8,128)(2,1)S(1)}, bf16[2,32,1536]{2,1,0:T(8,128)(2,1)S(1)}, u32[]{:S(2)}, u32[]{:S(2)}) collective-permute-start(bf16[2,32,1536]{2,1,0:T(8,128)(2,1)S(1)} %slice.37.rest_0_), channel_id=1, source_target_pairs={{0,8},{4,12},{8,0},{12,4},{16,24},{20,28},{24,16},{28,20},{1,9},{5... | collective-permute-start | bytes 589832 | tf_op jit(solution)/shard_map/ppermute | solution.py:661
  137.8 9.0 %collective-permute-start.20 = (bf16[384,384]{1,0:T(8,128)(2,1)S(1)}, bf16[384,384]{1,0:T(8,128)(2,1)S(1)}, u32[]{:S(2)}, u32[]{:S(2)}) collective-permute-start(bf16[384,384]{1,0:T(8,128)(2,1)S(1)} %get-tuple-element.106), channel_id=1, source_target_pairs={{0,16},{4,20},{8,24},{12,28},{16,0},{20,4},{24,8},{28,12},{1,17},{... | collective-permute-start | bytes 884744 | tf_op jit(solution)/shard_map/ppermute | solution.py:661
  139.3 10.9 %collective-permute-start.21 = (bf16[384,384]{1,0:T(8,128)(2,1)S(1)}, bf16[384,384]{1,0:T(8,128)(2,1)S(1)}, u32[]{:S(2)}, u32[]{:S(2)}) collective-permute-start(bf16[384,384]{1,0:T(8,128)(2,1)S(1)} %get-tuple-element.107), channel_id=1, source_target_pairs={{0,8},{4,12},{8,0},{12,4},{16,24},{20,28},{24,16},{28,20},{1,9},{5... | collective-permute-start | bytes 884744 | tf_op jit(solution)/shard_map/ppermute | solution.py:661
  145.1 7.6 %collective-permute-start.19 = (bf16[2,32,1536]{2,1,0:T(8,128)(2,1)S(1)}, bf16[2,32,1536]{2,1,0:T(8,128)(2,1)S(1)}, u32[]{:S(2)}, u32[]{:S(2)}) collective-permute-start(bf16[2,32,1536]{2,1,0:T(8,128)(2,1)S(1)} %pad_maximum_fusion.1), channel_id=1, source_target_pairs={{0,16},{4,20},{8,24},{12,28},{16,0},{20,4},{24,8},{28,12},{1,17},{... | collective-permute-start | bytes 589832 | tf_op jit(solution)/shard_map/ppermute | solution.py:661
  150.5 14.1 %collective-permute-start.26 = (bf16[192,768]{1,0:T(8,128)(2,1)S(1)}, bf16[192,768]{1,0:T(8,128)(2,1)S(1)}, u32[]{:S(2)}, u32[]{:S(2)}) collective-permute-start(bf16[192,768]{1,0:T(8,128)(2,1)S(1)} %get-tuple-element.120), channel_id=1, source_target_pairs={{0,16},{4,20},{8,24},{12,28},{16,0},{20,4},{24,8},{28,12},{1,17},{... | collective-permute-start | bytes 884744 | tf_op jit(solution)/shard_map/ppermute | solution.py:661
  152.1 12.6 %collective-permute-start.24 = (bf16[192,768]{1,0:T(8,128)(2,1)S(1)}, bf16[192,768]{1,0:T(8,128)(2,1)S(1)}, u32[]{:S(2)}, u32[]{:S(2)}) collective-permute-start(bf16[192,768]{1,0:T(8,128)(2,1)S(1)} %get-tuple-element.112.refs_4_), channel_id=1, source_target_pairs={{0,8},{4,12},{8,0},{12,4},{16,24},{20,28},{24,16},{28,20},{1,9},{5... | collective-permute-start | bytes 884744 | tf_op jit(solution)/shard_map/ppermute | solution.py:661
  153.9 10.3 %collective-permute-start.22 = (bf16[2,4,1,1536]{3,2,1,0:T(2,128)(2,1)S(1)}, bf16[2,4,1,1536]{3,2,1,0:T(2,128)(2,1)S(1)}, u32[]{:S(2)}, u32[]{:S(2)}) collective-permute-start(bf16[2,4,1,1536]{3,2,1,0:T(2,128)(2,1)S(1)} %get-tuple-element.114), channel_id=1, source_target_pairs={{0,1},{1,2},{2,3},{3,4},{4,5},{5,6},{6,7},{7,8},{8,9},{9,10},{10,1... | collective-permute-start | bytes 73736 | tf_op jit(solution)/shard_map/ppermute | solution.py:652
  156.1 8.5 %collective-permute-start.23 = (bf16[2,4,1,1536]{3,2,1,0:T(2,128)(2,1)S(1)}, bf16[2,4,1,1536]{3,2,1,0:T(2,128)(2,1)S(1)}, u32[]{:S(2)}, u32[]{:S(2)}) collective-permute-start(bf16[2,4,1,1536]{3,2,1,0:T(2,128)(2,1)S(1)} %get-tuple-element.115.refs_1_), channel_id=1, source_target_pairs={{1,0},{2,1},{3,2},{4,3},{5,4},{6,5},{7,6},{8,7},{9,8},{10,9},{11,1... | collective-permute-start | bytes 73736 | tf_op jit(solution)/shard_map/ppermute | solution.py:652
  169.6 16.2 %collective-permute-start.32 = (bf16[384,768]{1,0:T(8,128)(2,1)S(1)}, bf16[384,768]{1,0:T(8,128)(2,1)S(1)}, u32[]{:S(2)}, u32[]{:S(2)}) collective-permute-start(bf16[384,768]{1,0:T(8,128)(2,1)S(1)} %constant_dynamic-update-slice_fusion.7.refs_1_), channel_id=1, source_target_pairs={{0,8},{4,12},{8,0},{12,4},{16,24},{20,28},{24,16},{28,20},{1,9},{5... | collective-permute-start | bytes 1769480 | tf_op jit(solution)/shard_map/ppermute | solution.py:661
  169.7 19.9 %collective-permute-start.31 = (bf16[384,768]{1,0:T(8,128)(2,1)S(1)}, bf16[384,768]{1,0:T(8,128)(2,1)}, u32[]{:S(2)}, u32[]{:S(2)}) collective-permute-start(bf16[384,768]{1,0:T(8,128)(2,1)S(1)} %constant_dynamic-update-slice_fusion.5.refs_0_), channel_id=1, source_target_pairs={{0,16},{4,20},{8,24},{12,28},{16,0},{20,4},{24,8},{28,12},{1,17},{... | collective-permute-start | bytes 1769480 | tf_op jit(solution)/shard_map/ppermute | solution.py:661
  (51 other events, 243.2 us)
Sparse Core Ops, SparseCore 0:
  10.2 31.0 all-gather.5
  45.5 36.9 all-gather.3
  101.9 34.2 reduce-scatter.4
  138.4 36.3 reduce-scatter.2
